TPU v7x, 32 devices: a whole 2x2x4 slice. The times are simulated.
32 devices in a mesh: seq: 4 (over y, x), fsdp: 8 (over z, core).
Axes of the slice: x: 2, y: 2, z: 4, core: 2. Of those that a mesh axis runs over, the one named last changes fastest.
Arguments:
- tokens: bfloat16 [8, 512, 2048], P('fsdp', 'seq'), may hold values from -6 to 6
- layer_vectors: bfloat16 [8, 512, 256], P('fsdp', 'seq'), may hold values from -6 to 6
- doc_lengths: int32 [8, 3], P('fsdp'), may hold values from 1 to 385, 512 in all within a row
- cotangent: bfloat16 [8, 512, 2048], P('fsdp', 'seq'), may hold values from -6 to 6
- tile_owner: int32 [3712], replicated, may hold values from 0 to 3711, as said below
- tile_master: float32 [3712, 128, 128], P(('seq', 'fsdp'))
- tile_first: float32 [3712, 128, 128], P(('seq', 'fsdp'))
- tile_second: float32 [3712, 128, 128], P(('seq', 'fsdp'))
- left_basis: float32 [3712, 128, 128], P(('seq', 'fsdp')), may hold values from -1 to 1
- right_basis: float32 [3712, 128, 128], P(('seq', 'fsdp')), may hold values from -1 to 1
- small_master: float32 [80, 128, 128], P('seq')
- small_first: float32 [80, 128, 128], P('seq')
- small_second: float32 [80, 128, 128], P('seq')
- small_left: float32 [80, 128, 128], P('seq'), may hold values from -1 to 1
- small_right: float32 [80, 128, 128], P('seq'), may hold values from -1 to 1
- gains: float32 [12800], P('seq'), may hold values from 0.25 to 1.75
- gain_first: float32 [12800], P('seq')
- gain_second: float32 [12800], P('seq')
Outputs:
- output: bfloat16 [8, 512, 2048], P('fsdp', 'seq')
- input_grad: float32 [8, 512, 2048], P('fsdp', 'seq')
- tile_weight_new: float32 [3712, 128, 128], P(('seq', 'fsdp'))
- tile_first_new: float32 [3712, 128, 128], P(('seq', 'fsdp'))
- tile_second_new: float32 [3712, 128, 128], P(('seq', 'fsdp'))
- small_weight_new: float32 [80, 128, 128], P('seq')
- small_first_new: float32 [80, 128, 128], P('seq')
- small_second_new: float32 [80, 128, 128], P('seq')
- gain_new: float32 [12800], P('seq')
- gain_first_new: float32 [12800], P('seq')
- gain_second_new: float32 [12800], P('seq')
Inputs may be any that keep to these rules, and one draw needn't show every extreme that they name: `doc_lengths`: each pack's 3 document lengths sum to 512; one of them is exactly 385. A permutation: slot s of the tile arrays holds tile tile_owner[s] of the weight table.
All inputs are finite; a program needn't handle non-finite values.
Results may differ from a plain program's by a relative error of at most 0.028.
Values may be sent and summed in bfloat16 or wider, within the bound.
No kernel may reach another device: no remote copies, remote signals or barrier semaphores. Data moves between devices by JAX's collectives and lax.ppermute only.
A program may use at most 1.125 GiB of HBM per device.

v0:
```python
import jax
import jax.numpy as jnp
from jax import lax
from jax.sharding import PartitionSpec as P

HEADS = 8
KV_HEADS = 2
HEAD_DIM = 256
FF = 8192
RANK = 64
PLD = 256
STEP = 5


EPS = 1e-06
SCALE = 0.0625
THETA = 1000000.0
ROOT_HALF = 0.7071067811865476
BETA_ONE = 0.5
BETA_TWO = 0.5
ADAM_EPS = 1e-08
RATE_TILE = 0.02
RATE_SMALL = 0.04
RATE_GAIN = 0.3
DECAY = 0.01
NEGATIVE = -1e30
HIGHEST = lax.Precision.HIGHEST


def rms_norm(value, gain):
    return value * lax.rsqrt(jnp.mean(value * value, axis=-1, keepdims=True) + EPS) * gain


def rotary(value, position):
    half = value.shape[-1] // 2
    freq = THETA ** (-2.0 * jnp.arange(half).astype(jnp.float32) / value.shape[-1])
    angle = position.astype(jnp.float32)[:, None] * freq[None, :]
    cosine = jnp.cos(angle)[:, None, :]
    sine = jnp.sin(angle)[:, None, :]
    first = value[..., :half]
    second = value[..., half:]
    return jnp.concatenate(
        [first * cosine - second * sine, second * cosine + first * sine], axis=-1
    )


def documents(lengths, length):
    places = jnp.arange(length)
    ends = jnp.cumsum(lengths)
    passed = places[:, None] >= ends[None, :]
    segment = jnp.sum(passed.astype(jnp.int32), axis=1)
    before = jnp.sum(jnp.where(passed, lengths[None, :], 0), axis=1)
    return (segment, places - before)


def matmul(left, right):
    return jnp.dot(left, right, preferred_element_type=jnp.float32)


def matmul_flip(left, right):
    return lax.dot_general(
        left, right, (((1,), (1,)), ((), ())), preferred_element_type=jnp.float32
    )


def matmul_outer(left, right):
    return lax.dot_general(
        left, right, (((0,), (0,)), ((), ())), preferred_element_type=jnp.float32
    )


def assemble(tiles, row_blocks):
    size = tiles.shape[1]
    column_blocks = tiles.shape[0] // row_blocks
    return (
        tiles.reshape(row_blocks, column_blocks, size, size)
        .transpose(0, 2, 1, 3)
        .reshape(row_blocks * size, column_blocks * size)
    )


def split_tiles(matrix, size):
    row_blocks = matrix.shape[0] // size
    column_blocks = matrix.shape[1] // size
    return (
        matrix.reshape(row_blocks, size, column_blocks, size)
        .transpose(0, 2, 1, 3)
        .reshape(row_blocks * column_blocks, size, size)
    )


def gelu_product(first, second):
    return jax.nn.gelu(first, approximate=True) * second


def rotate_update(grad, master, first, second, left, right, rate):
    turned = jnp.einsum(
        "bki,bkj->bij",
        left,
        jnp.einsum("bkl,blj->bkj", grad, right, precision=HIGHEST),
        precision=HIGHEST,
    )
    first_new = BETA_ONE * first + (1.0 - BETA_ONE) * turned
    second_new = BETA_TWO * second + (1.0 - BETA_TWO) * turned * turned
    correct_one = 1.0 - BETA_ONE**STEP
    correct_two = 1.0 - BETA_TWO**STEP
    direction = first_new / correct_one / (jnp.sqrt(second_new / correct_two) + ADAM_EPS)
    back = jnp.einsum(
        "bik,bkj->bij",
        left,
        jnp.einsum("bkl,bjl->bkj", direction, right, precision=HIGHEST),
        precision=HIGHEST,
    )
    return (master - rate * (back + DECAY * master), first_new, second_new)


def on_device(
    tokens,
    layer_vectors,
    doc_lengths,
    cotangent,
    tile_owner,
    tile_master,
    tile_first,
    tile_second,
    left_basis,
    right_basis,
    small_master,
    small_first,
    small_second,
    small_left,
    small_right,
    gains,
    gain_first,
    gain_second,
):
    tile = tile_master.shape[1]
    width = tokens.shape[2]
    row_blocks = width // tile
    rows = tokens.shape[1]
    group_size = lax.axis_size("seq")
    length = rows * group_size
    per_device = HEADS // group_size
    kv_group = HEADS // KV_HEADS
    picks = [copy * per_device // kv_group for copy in range(group_size)]
    query_width = HEADS * HEAD_DIM
    key_width = KV_HEADS * HEAD_DIM
    out_start = query_width + 2 * key_width
    ffn_start = out_start + query_width
    down_start = ffn_start + 2 * FF
    stream = tokens[0].astype(jnp.float32)
    vectors = layer_vectors[0].astype(jnp.float32)
    segment, position = documents(doc_lengths[0], length)
    local_position = lax.dynamic_slice_in_dim(position, lax.axis_index("seq") * rows, rows)
    gathered = lax.all_gather(tile_master.astype(jnp.bfloat16), ("seq", "fsdp"), axis=0, tiled=True)
    table = assemble(jnp.zeros_like(gathered).at[tile_owner].set(gathered), row_blocks)
    small_got, gain_got = (
        lax.all_gather(small_master.astype(jnp.bfloat16), "seq", axis=0, tiled=True),
        lax.all_gather(gains.astype(jnp.bfloat16), "seq", axis=0, tiled=True),
    )
    small_table = assemble(small_got, row_blocks)
    gain_full = gain_got.astype(jnp.float32)
    gain_in = gain_full[0:width]
    gain_attn = gain_full[width : 2 * width]
    gain_laurel = gain_full[2 * width : 3 * width]
    gain_pre = gain_full[3 * width : 4 * width]
    gain_post = gain_full[4 * width : 5 * width]
    gain_vec = gain_full[5 * width : 6 * width]
    gain_query = gain_full[6 * width : 6 * width + HEAD_DIM]
    gain_key = gain_full[6 * width + HEAD_DIM : 6 * width + 2 * HEAD_DIM]
    w_query = table[:, :query_width]
    w_key = table[:, query_width : query_width + key_width]
    w_value = table[:, query_width + key_width : out_start]
    w_out = table[:, out_start:ffn_start]
    w_gate = table[:, ffn_start : ffn_start + FF]
    w_up = table[:, ffn_start + FF : down_start]
    w_down = table[:, down_start : down_start + FF]
    laurel_left = small_table[:, :RANK]
    laurel_right = small_table[:, RANK : 2 * RANK]
    vector_gate_w = small_table[:, 2 * RANK : 2 * RANK + PLD]
    vector_proj_w = small_table[:, 2 * RANK + PLD :]
    normed, normed_pull = jax.vjp(rms_norm, stream, gain_in)
    normed_low = normed.astype(jnp.bfloat16)
    query_pre = matmul(normed_low, w_query)
    key_pre = matmul(normed_low, w_key)
    value_pre = matmul(normed_low, w_value)

    def shape_heads(query_in, key_in, query_gain, key_gain):
        query_out = rotary(
            rms_norm(query_in.reshape(rows, HEADS, HEAD_DIM), query_gain), local_position
        )
        key_out = rotary(
            rms_norm(key_in.reshape(rows, KV_HEADS, HEAD_DIM), key_gain), local_position
        )
        return (query_out, key_out)

    (query_rot, key_rot), rotary_pull = jax.vjp(
        shape_heads, query_pre, key_pre, gain_query, gain_key
    )
    keys_low = key_rot.astype(jnp.bfloat16)
    values_low = value_pre.astype(jnp.bfloat16).reshape(rows, KV_HEADS, HEAD_DIM)
    key_copies = jnp.stack([keys_low[:, pick] for pick in picks], axis=1)
    value_copies = jnp.stack([values_low[:, pick] for pick in picks], axis=1)
    query_heads, key_heads, value_heads = (
        lax.all_to_all(
            query_rot.astype(jnp.bfloat16), "seq", split_axis=1, concat_axis=0, tiled=True
        ),
        lax.all_to_all(key_copies, "seq", split_axis=1, concat_axis=0, tiled=True),
        lax.all_to_all(value_copies, "seq", split_axis=1, concat_axis=0, tiled=True),
    )
    key_single = key_heads[:, 0, :]
    value_single = value_heads[:, 0, :]
    block = min(512, length)
    count = length // block
    places = jnp.arange(length)
    starts = jnp.arange(count) * block
    query_blocks = query_heads.reshape(count, block, per_device, HEAD_DIM)

    def score_block(query, first):
        row_places = first + jnp.arange(block)
        allow = (segment[:, None] == segment[None, :]) & (places[None, :] <= row_places[:, None])
        raw = (
            jnp.einsum("qhd,kd->qhk", query, key_single, preferred_element_type=jnp.float32) * SCALE
        )
        return jnp.where(allow[:, None, :], raw, NEGATIVE)

    def forward_block(args):
        query, first = args
        scores = score_block(query, first)
        highest = jnp.max(scores, axis=-1, keepdims=True)
        powers = jnp.exp(scores - highest)
        totals = jnp.sum(powers, axis=-1, keepdims=True)
        prob_low = (powers / totals).astype(jnp.bfloat16)
        attended_block = jnp.einsum(
            "qhk,kd->qhd", prob_low, value_single, preferred_element_type=jnp.float32
        )
        return (attended_block.astype(jnp.bfloat16), (highest + jnp.log(totals))[..., 0])

    attended_blocks, log_totals = lax.map(forward_block, (query_blocks, starts))
    attended_heads = attended_blocks.reshape(length, per_device, HEAD_DIM)
    attended_tokens = lax.all_to_all(attended_heads, "seq", split_axis=0, concat_axis=1, tiled=True)
    attended_low = attended_tokens.reshape(rows, query_width)
    attn_pre = matmul_flip(attended_low, w_out)
    attn_normed, attn_pull = jax.vjp(rms_norm, attn_pre, gain_attn)
    first_sum = stream + attn_normed
    left_pre = matmul(normed_low, laurel_left)
    left_low = left_pre.astype(jnp.bfloat16)
    right_pre = matmul_flip(left_low, laurel_right)
    laurel_normed, laurel_pull = jax.vjp(rms_norm, right_pre, gain_laurel)
    second_sum = (first_sum + normed + laurel_normed) * ROOT_HALF
    feed_normed, feed_pull = jax.vjp(rms_norm, second_sum, gain_pre)
    feed_low = feed_normed.astype(jnp.bfloat16)
    gate_pre = matmul(feed_low, w_gate)
    up_pre = matmul(feed_low, w_up)
    hidden, hidden_pull = jax.vjp(gelu_product, gate_pre, up_pre)
    hidden_low = hidden.astype(jnp.bfloat16)
    down_pre = matmul_flip(hidden_low, w_down)
    down_normed, down_pull = jax.vjp(rms_norm, down_pre, gain_post)
    third_sum = second_sum + down_normed
    third_low = third_sum.astype(jnp.bfloat16)
    vector_pre = matmul(third_low, vector_gate_w)
    vector_gated, vector_pull = jax.vjp(lambda inner: gelu_product(inner, vectors), vector_pre)
    vector_low = vector_gated.astype(jnp.bfloat16)
    proj_pre = matmul_flip(vector_low, vector_proj_w)
    proj_normed, proj_pull = jax.vjp(rms_norm, proj_pre, gain_vec)
    result = third_sum + proj_normed
    output = result.astype(jnp.bfloat16)[None]
    grad_out = cotangent[0].astype(jnp.float32)
    grad_proj, grad_gain_vec = proj_pull(grad_out)
    proj_grad_low = grad_proj.astype(jnp.bfloat16)
    (grad_vector_pre,) = vector_pull(matmul(proj_grad_low, vector_proj_w))
    vector_grad_low = grad_vector_pre.astype(jnp.bfloat16)
    grad_third = grad_out + matmul_flip(vector_grad_low, vector_gate_w)
    grad_down, grad_gain_post = down_pull(grad_third)
    down_grad_low = grad_down.astype(jnp.bfloat16)
    grad_gate, grad_up = hidden_pull(matmul(down_grad_low, w_down))
    gate_grad_low = grad_gate.astype(jnp.bfloat16)
    up_grad_low = grad_up.astype(jnp.bfloat16)
    grad_feed = matmul_flip(gate_grad_low, w_gate) + matmul_flip(up_grad_low, w_up)
    grad_second_norm, grad_gain_pre = feed_pull(grad_feed)
    half_grad = (grad_third + grad_second_norm) * ROOT_HALF
    grad_right, grad_gain_laurel = laurel_pull(half_grad)
    right_grad_low = grad_right.astype(jnp.bfloat16)
    left_grad_low = matmul(right_grad_low, laurel_right).astype(jnp.bfloat16)
    grad_attn, grad_gain_attn = attn_pull(half_grad)
    attn_grad_low = grad_attn.astype(jnp.bfloat16)
    grad_attended = matmul(attn_grad_low, w_out).astype(jnp.bfloat16).reshape(rows, HEADS, HEAD_DIM)
    grad_attended_heads = lax.all_to_all(
        grad_attended, "seq", split_axis=1, concat_axis=0, tiled=True
    )
    grad_blocks = grad_attended_heads.reshape(count, block, per_device, HEAD_DIM)

    def backward_block(carry, args):
        key_sum, value_sum = carry
        query, grad_block, log_block, first = args
        scores = score_block(query, first)
        prob = jnp.exp(scores - log_block[..., None])
        value_sum = value_sum + jnp.einsum(
            "qhk,qhd->kd", prob.astype(jnp.bfloat16), grad_block, preferred_element_type=jnp.float32
        )
        grad_prob = jnp.einsum(
            "qhd,kd->qhk", grad_block, value_single, preferred_element_type=jnp.float32
        )
        inner = jnp.sum(prob * grad_prob, axis=-1, keepdims=True)
        grad_score = (prob * (grad_prob - inner)).astype(jnp.bfloat16)
        grad_query = (
            jnp.einsum("qhk,kd->qhd", grad_score, key_single, preferred_element_type=jnp.float32)
            * SCALE
        )
        key_sum = (
            key_sum
            + jnp.einsum("qhk,qhd->kd", grad_score, query, preferred_element_type=jnp.float32)
            * SCALE
        )
        return ((key_sum, value_sum), grad_query.astype(jnp.bfloat16))

    empty = jnp.zeros((length, HEAD_DIM), jnp.float32)
    (key_sum, value_sum), grad_query_blocks = lax.scan(
        backward_block, (empty, empty), (query_blocks, grad_blocks, log_totals, starts)
    )
    grad_query_heads = grad_query_blocks.reshape(length, per_device, HEAD_DIM)
    back_query, back_key, back_value = (
        lax.all_to_all(grad_query_heads, "seq", split_axis=0, concat_axis=1, tiled=True),
        lax.all_to_all(
            key_sum.astype(jnp.bfloat16)[:, None, :], "seq", split_axis=0, concat_axis=1, tiled=True
        ),
        lax.all_to_all(
            value_sum.astype(jnp.bfloat16)[:, None, :],
            "seq",
            split_axis=0,
            concat_axis=1,
            tiled=True,
        ),
    )
    key_parts = []
    value_parts = []
    for head in range(KV_HEADS):
        key_total = jnp.zeros((rows, HEAD_DIM), jnp.float32)
        value_total = jnp.zeros((rows, HEAD_DIM), jnp.float32)
        for copy in range(group_size):
            if picks[copy] == head:
                key_total = key_total + back_key[:, copy].astype(jnp.float32)
                value_total = value_total + back_value[:, copy].astype(jnp.float32)
        key_parts.append(key_total)
        value_parts.append(value_total)
    grad_key_rot = jnp.stack(key_parts, axis=1)
    grad_value = jnp.stack(value_parts, axis=1).reshape(rows, key_width)
    grad_query_pre, grad_key_pre, grad_gain_query, grad_gain_key = rotary_pull(
        (back_query.astype(jnp.float32), grad_key_rot)
    )
    query_grad_low = grad_query_pre.astype(jnp.bfloat16)
    key_grad_low = grad_key_pre.astype(jnp.bfloat16)
    value_grad_low = grad_value.astype(jnp.bfloat16)
    grad_normed = (
        half_grad
        + matmul_flip(left_grad_low, laurel_left)
        + matmul_flip(query_grad_low, w_query)
        + matmul_flip(key_grad_low, w_key)
        + matmul_flip(value_grad_low, w_value)
    )
    grad_stream_norm, grad_gain_in = normed_pull(grad_normed)
    input_grad = (half_grad + grad_stream_norm)[None]
    column_count = table.shape[1] // tile
    left_stack = jnp.stack([normed_low, attn_grad_low, feed_low, down_grad_low], axis=0)
    left_tiles = (
        left_stack.reshape(4, rows, row_blocks, tile)
        .transpose(0, 2, 1, 3)
        .reshape(4 * row_blocks, rows, tile)
    )
    right_all = jnp.concatenate(
        [
            query_grad_low,
            key_grad_low,
            value_grad_low,
            attended_low,
            gate_grad_low,
            up_grad_low,
            hidden_low,
        ],
        axis=1,
    )
    right_tiles = right_all.reshape(rows, column_count, tile).transpose(1, 0, 2)
    out_block = out_start // tile
    ffn_block = ffn_start // tile
    down_block = down_start // tile
    slot_count = tile_master.shape[0]
    owners = tile_owner.reshape(
        slot_count * lax.axis_size(("seq", "fsdp")) // slot_count, slot_count
    )

    def group_terms(members):
        column = members % column_count
        row_block = members // column_count
        kind = (
            (column >= out_block).astype(jnp.int32)
            + (column >= ffn_block).astype(jnp.int32)
            + (column >= down_block).astype(jnp.int32)
        )
        lefts = left_tiles[kind * row_blocks + row_block]
        rights = right_tiles[column]
        return jnp.einsum("gtk,gtn->gkn", lefts, rights, preferred_element_type=jnp.float32)

    tile_grad = lax.psum_scatter(
        lax.map(group_terms, owners).reshape(
            slot_count * lax.axis_size(("seq", "fsdp")), tile, tile
        ),
        ("seq", "fsdp"),
        scatter_dimension=0,
        tiled=True,
    )
    small_full = jnp.concatenate(
        [
            matmul_outer(normed_low, left_grad_low),
            matmul_outer(right_grad_low, left_low),
            matmul_outer(third_low, vector_grad_low),
            matmul_outer(proj_grad_low, vector_low),
        ],
        axis=1,
    )
    small_tiles_grad = split_tiles(small_full, tile)
    gain_grad = jnp.concatenate(
        [
            grad_gain_in,
            grad_gain_attn,
            grad_gain_laurel,
            grad_gain_pre,
            grad_gain_post,
            grad_gain_vec,
            grad_gain_query,
            grad_gain_key,
        ]
    )
    whole_small, whole_gain = (
        lax.psum(small_tiles_grad.astype(jnp.bfloat16), "fsdp").astype(jnp.float32),
        lax.psum(gain_grad.astype(jnp.bfloat16), "fsdp").astype(jnp.float32),
    )
    small_grad, gain_grad_mine = (
        lax.psum_scatter(
            whole_small.astype(jnp.bfloat16), "seq", scatter_dimension=0, tiled=True
        ).astype(jnp.float32),
        lax.psum_scatter(
            whole_gain.astype(jnp.bfloat16), "seq", scatter_dimension=0, tiled=True
        ).astype(jnp.float32),
    )
    tile_new, tile_first_new, tile_second_new = rotate_update(
        tile_grad, tile_master, tile_first, tile_second, left_basis, right_basis, RATE_TILE
    )
    small_new, small_first_new, small_second_new = rotate_update(
        small_grad, small_master, small_first, small_second, small_left, small_right, RATE_SMALL
    )
    gain_first_new = BETA_ONE * gain_first + (1.0 - BETA_ONE) * gain_grad_mine
    gain_second_new = BETA_TWO * gain_second + (1.0 - BETA_TWO) * gain_grad_mine * gain_grad_mine
    correct_one = 1.0 - BETA_ONE**STEP
    correct_two = 1.0 - BETA_TWO**STEP
    gain_new = gains - RATE_GAIN * (gain_first_new / correct_one) / (
        jnp.sqrt(gain_second_new / correct_two) + ADAM_EPS
    )
    return (
        output,
        input_grad,
        tile_new,
        tile_first_new,
        tile_second_new,
        small_new,
        small_first_new,
        small_second_new,
        gain_new,
        gain_first_new,
        gain_second_new,
    )


def solution(mesh):
    return jax.shard_map(
        on_device,
        mesh=mesh,
        in_specs=(
            P("fsdp", "seq", None),
            P("fsdp", "seq", None),
            P("fsdp", None),
            P("fsdp", "seq", None),
            P(),
            P(("seq", "fsdp"), None, None),
            P(("seq", "fsdp"), None, None),
            P(("seq", "fsdp"), None, None),
            P(("seq", "fsdp"), None, None),
            P(("seq", "fsdp"), None, None),
            P("seq", None, None),
            P("seq", None, None),
            P("seq", None, None),
            P("seq", None, None),
            P("seq", None, None),
            P("seq"),
            P("seq"),
            P("seq"),
        ),
        out_specs=(
            P("fsdp", "seq", None),
            P("fsdp", "seq", None),
            P(("seq", "fsdp"), None, None),
            P(("seq", "fsdp"), None, None),
            P(("seq", "fsdp"), None, None),
            P("seq", None, None),
            P("seq", None, None),
            P("seq", None, None),
            P("seq"),
            P("seq"),
            P("seq"),
        ),
        check_vma=False,
    )
```

profile of v0, /device:TPU:9, one launch (start us, length us, event | category | flops | bytes accessed | tf_op | source)
XLA Modules:
  0.0 5003.4 jit_solution(18311876068246498242)
XLA Ops:
  27.9 23.4 all-gather.6.cloned.1.call-done
  60.9 610.0 %all-gather.4.cloned.1.call-done = bf16[3712,128,128]{2,1,0:T(8,128)(2,1)} async-done(((bf16[116,128,128]{2,1,0:T(8,128)(2,1)}), bf16[3712,128,128]{2,1,0:T(8,128)(2,1)}) %all-gather.4.cloned.1.call-update) | async-done | bytes 121634832 | tf_op jit(solution)/shard_map/all_gather | solution.py:155
  670.9 37.7 broadcast_in_dim.155
  708.5 551.1 %scatter_fusion = bf16[3712,128,128]{2,1,0:T(8,128)(2,1)} fusion(bf16[3712,128,128]{2,1,0:T(8,128)(2,1)} %broadcast_in_dim.155, s32[3712]{0:T(1024)S(1)} %compare_select_fusion.2, bf16[3712,128,128]{2,1,0:T(8,128)(2,1)} %all-gather.4.cloned.1.call-done), kind=kCustom, calls=%fused_computation.2 | custom fusion | bytes 364919296 | tf_op jit(solution)/shard_map/scatter | solution.py:156
  1259.6 124.7 %copy.220 = bf16[16,128,232,128]{3,2,1,0:T(8,128)(2,1)} copy(bf16[16,128,232,128]{3,1,2,0:T(8,128)(2,1)} %bitcast.12) | data formatting | bytes 243269632 | tf_op jit(solution)/shard_map/transpose | solution.py:77
  1384.3 79.7 %copy.294 = bf16[256,8,232,128]{3,1,2,0:T(8,128)(2,1)} copy(bf16[256,8,232,128]{3,2,1,0:T(8,128)(2,1)} %bitcast.93) | data formatting | bytes 243269632
  1467.0 8.4 slice_bitcast_fusion
  1484.6 12.4 copy.221
  1553.5 15.1 fusion.17
  1568.6 17.6 multiply_convert_fusion.1
  1586.2 16.8 multiply_reduce_fusion.12
  1611.4 17.2 fusion.40
  1628.6 17.3 fusion.11
  1645.9 20.1 multiply_reduce_fusion.3
  1766.9 582.0 %while.8 = (s32[]{:T(128)}, f32[32,116,128,128]{3,2,1,0:T(8,128)}, s32[32,116]{1,0:T(8,128)}, bf16[64,128,128]{2,1,0:T(8,128)(2,1)S(1)}, bf16[232,128,128]{2,1,0:T(8,128)(2,1)}, /*index=5*/s32[]{:T(128)}) while((s32[]{:T(128)}, f32[32,116,128,128]{3,2,1,0:T(8,128)}, s32[32,116]{1,0:T(8,128)}, bf16[64,128,128]{2,1,0:T(8,128)(2,1)S(1)}, ...), condition=%wide.region_24.25_spmd, body=%wide.region_23.24_spmd.sunk | while | flops 486544800 | bytes 30422124 | solution.py:404
  1941.1 7.8 bitcast_dynamic-update-slice_fusion.2
  1995.7 7.8 bitcast_dynamic-update-slice_fusion.2
  2195.6 7.8 bitcast_dynamic-update-slice_fusion.2
  2322.9 7.8 bitcast_dynamic-update-slice_fusion.2
  2351.6 8.8 copy.251
  2364.7 9.2 copy.241
  2374.0 8.8 copy.247
  2398.5 12.7 all-reduce.5
  2411.3 24.7 psum.17
  2463.6 2430.4 %reduce-scatter.8.cloned.1.call-done = f32[116,128,128]{2,1,0:T(8,128)} async-done(((f32[3712,128,128]{2,1,0:T(8,128)}), f32[116,128,128]{2,1,0:T(8,128)}) %reduce-scatter.8.cloned.1.call-update) | async-done | bytes 7602192
  4894.0 17.7 fusion.169
  4911.7 18.1 multiply_add_fusion
  4929.8 8.7 copy.261
  4938.5 17.9 fusion.22
  4956.4 8.7 copy.262
  4965.1 22.5 fusion.21
  4987.6 8.7 copy.260
  (607 shorter events, 807.1 us)
Async XLA Ops:
  7.2 2434.8 %copy-start = (f32[20,128,128]{2,1,0:T(8,128)S(1)}, f32[20,128,128]{2,1,0:T(8,128)}, u32[]{:S(2)}) copy-start(f32[20,128,128]{2,1,0:T(8,128)} %param.33) | copy-start | bytes 3932164
  7.2 44.2 all-gather.6.cloned.1.call-start
  9.6 661.2 %all-gather.4.cloned.1.call-start = ((), (), s32[]{:S(2)}) async-start(), calls=%async_computation.10 | async-start | bytes 125435904 | tf_op jit(solution)/shard_map/all_gather | solution.py:155
  22.8 35.6 copy-start.73
  23.4 35.0 copy-start.38
  1484.6 25.0 copy-start.21
  1484.6 25.0 copy-start.62
  1505.2 11.3 all-to-all-start
  1516.5 7.9 all-to-all-start.1
  1524.5 8.3 all-to-all-start.2
  1535.7 8.9 all-to-all-start.3
  1611.4 17.2 copy-start.22
  1628.6 17.3 copy-start.25
  1628.6 17.3 copy-start.92
  1645.9 20.2 copy-start.96
  1645.9 20.2 copy-start.45
  1645.9 20.2 copy-start.47
  1645.9 20.2 copy-start.78
  1645.9 20.2 copy-start.81
  1645.9 20.2 copy-start.94
  1679.5 17.6 all-to-all-start.4
  1683.7 83.1 %reduce-scatter.6.cloned.1.call-start = ((), (), s32[]{:S(2)}) async-start(), calls=%async_computation.12 | async-start | bytes 3276800 | tf_op jit(solution)/shard_map/reduce_scatter | solution.py:438
  1708.5 16.4 all-to-all-start.7
  1723.6 17.4 copy-start.63
  1724.9 8.3 all-to-all-start.6
  1733.3 15.1 all-to-all-start.5
  1737.5 701.8 %all-reduce.8.cloned.1.call-start = ((), (), s32[]{:S(2)}) async-start(), calls=%async_computation.13 | async-start | bytes 1310720 | tf_op jit(solution)/shard_map/psum | solution.py:434
  1766.8 3127.2 %reduce-scatter.8.cloned.1.call-start = ((), (), s32[]{:S(2)}) async-start(), calls=%async_computation.14 | async-start | bytes 250871808
  2392.0 44.0 copy-start.90
  2392.0 44.0 copy-start.57
  2392.0 44.0 copy-start.71
  2392.0 44.0 copy-start.72
  (82 other events, 543.8 us)
Sparse Core Ops, SparseCore 0:
  10.4 40.8 all-gather.5
  54.8 616.0 all-gather.3
  1693.7 50.6 reduce-scatter.5
  1767.0 63.8 all-reduce.7
  2349.0 2544.9 reduce-scatter.7
where the time goes:
time: 5030 us; the launch traced here: 5000 us
  waiting for transfers between devices  3080 us (61%)
  local copies, waits for them, and re-layouts  1240 us (25%)
  matrix products  503 us (10%)
  other arithmetic  89.8 us (2%)
    unnamed x6, waiting for transfers between devices  2430 us
    all_gather x1, waiting for transfers between devices, on_device(): lax.all_gather(tile_master.astype(jnp.bfloat16), ('seq', 'fsdp'), axis=0,...  610 us
    scatter x1, local copies, waits for them, and re-layouts, on_device(): jnp.zeros_like(gathered).at[tile_owner].set(gathered)  551 us
    dot_general x32, matrix products, group_terms(): jnp.einsum('gtk,gtn->gkn', lefts, rights, preferred_element_type=jnp.floa...  246 us
    gather x32, local copies, waits for them, and re-layouts, group_terms(): rights = right_tiles[column]  196 us
    unnamed x243, local copies, waits for them, and re-layouts  175 us
    transpose x1, local copies, waits for them, and re-layouts, assemble(): return tiles.reshape(row_blocks, column_blocks, size, size).transpose(0,...  125 us
  transfers between devices with their start and end apart: 13, of which 8 were waited for; matrix products, arithmetic and copies ran while one was open for 15% of the time, Pallas kernels for 0%

commit v1 on v0

v1 whole, which is shorter than its diff:
```python
import math

import jax
import jax.numpy as jnp
from jax import lax
from jax.experimental import pallas as pl
from jax.experimental.pallas import tpu as pltpu
from jax.sharding import PartitionSpec as P

HEADS = 8
KV_HEADS = 2
HEAD_DIM = 256
FF = 8192
RANK = 64
PLD = 256
STEP = 5


EPS = 1e-06
SCALE = 0.0625
THETA = 1000000.0
ROOT_HALF = 0.7071067811865476
BETA_ONE = 0.5
BETA_TWO = 0.5
ADAM_EPS = 1e-08
RATE_TILE = 0.02
RATE_SMALL = 0.04
RATE_GAIN = 0.3
DECAY = 0.01
NEGATIVE = -1e30
HIGHEST = lax.Precision.HIGHEST


def rms_norm(value, gain):
    return value * lax.rsqrt(jnp.mean(value * value, axis=-1, keepdims=True) + EPS) * gain


def rotary(value, position):
    half = value.shape[-1] // 2
    freq = THETA ** (-2.0 * jnp.arange(half).astype(jnp.float32) / value.shape[-1])
    angle = position.astype(jnp.float32)[:, None] * freq[None, :]
    cosine = jnp.cos(angle)[:, None, :]
    sine = jnp.sin(angle)[:, None, :]
    first = value[..., :half]
    second = value[..., half:]
    return jnp.concatenate(
        [first * cosine - second * sine, second * cosine + first * sine], axis=-1
    )


def documents(lengths, length):
    places = jnp.arange(length)
    ends = jnp.cumsum(lengths)
    passed = places[:, None] >= ends[None, :]
    segment = jnp.sum(passed.astype(jnp.int32), axis=1)
    before = jnp.sum(jnp.where(passed, lengths[None, :], 0), axis=1)
    return (segment, places - before)


def matmul(left, right):
    return jnp.dot(left, right, preferred_element_type=jnp.float32)


def matmul_flip(left, right):
    return lax.dot_general(
        left, right, (((1,), (1,)), ((), ())), preferred_element_type=jnp.float32
    )


def matmul_outer(left, right):
    return lax.dot_general(
        left, right, (((0,), (0,)), ((), ())), preferred_element_type=jnp.float32
    )


def assemble(tiles, row_blocks):
    size = tiles.shape[1]
    column_blocks = tiles.shape[0] // row_blocks
    return (
        tiles.reshape(row_blocks, column_blocks, size, size)
        .transpose(0, 2, 1, 3)
        .reshape(row_blocks * size, column_blocks * size)
    )


def split_tiles(matrix, size):
    row_blocks = matrix.shape[0] // size
    column_blocks = matrix.shape[1] // size
    return (
        matrix.reshape(row_blocks, size, column_blocks, size)
        .transpose(0, 2, 1, 3)
        .reshape(row_blocks * column_blocks, size, size)
    )


def gelu_product(first, second):
    return jax.nn.gelu(first, approximate=True) * second


def rotate_update(grad, master, first, second, left, right, rate):
    turned = jnp.einsum(
        "bki,bkj->bij",
        left,
        jnp.einsum("bkl,blj->bkj", grad, right, precision=HIGHEST),
        precision=HIGHEST,
    )
    first_new = BETA_ONE * first + (1.0 - BETA_ONE) * turned
    second_new = BETA_TWO * second + (1.0 - BETA_TWO) * turned * turned
    correct_one = 1.0 - BETA_ONE**STEP
    correct_two = 1.0 - BETA_TWO**STEP
    direction = first_new / correct_one / (jnp.sqrt(second_new / correct_two) + ADAM_EPS)
    back = jnp.einsum(
        "bik,bkj->bij",
        left,
        jnp.einsum("bkl,bjl->bkj", direction, right, precision=HIGHEST),
        precision=HIGHEST,
    )
    return (master - rate * (back + DECAY * master), first_new, second_new)


def room(count, share):
    mean = count * share
    return math.ceil(mean + 3.6 * math.sqrt(mean * (1.0 - share)) + 3.0)


def count_earlier(group, valid):
    size = group.shape[-1]
    order = jnp.arange(size)
    same = (group[..., :, None] == group[..., None, :]) & valid[..., None, :]
    same = same & (order[None, :] < order[:, None])
    return jnp.sum(same.astype(jnp.int32), axis=-1)


def pick(match, value):
    return jnp.sum(jnp.where(match, value, 0), axis=-1)


def tile_kernel_call(kernel, index, arrays, out_shape):
    return pl.pallas_call(
        kernel,
        out_shape=out_shape,
        in_specs=[pl.BlockSpec(memory_space=pltpu.SMEM)]
        + [pl.BlockSpec(memory_space=pl.ANY)] * len(arrays),
        out_specs=jax.tree.map(lambda _: pl.BlockSpec(memory_space=pl.ANY), out_shape),
        scratch_shapes=[pltpu.SemaphoreType.DMA],
    )(index, *arrays)


def gather_tiles(arrays, index):
    tile = arrays[0].shape[-1]
    count = index.shape[0]

    def kernel(index_ref, *refs):
        sources, out, sem = refs[:-2], refs[-2], refs[-1]

        def step(i, carry):
            place = index_ref[i]
            start = 0
            for ref in sources:
                size = ref.shape[0]

                @pl.when((place >= start) & (place < start + size))
                def _(ref=ref, start=start):
                    pltpu.make_async_copy(ref.at[place - start], out.at[i], sem).start()

                start = start + size
            return carry

        lax.fori_loop(0, count, step, 0)
        pltpu.make_async_copy(out, out, sem).wait()

    total = sum(array.shape[0] for array in arrays)
    index = jnp.clip(index, 0, total - 1)
    out_shape = jax.ShapeDtypeStruct((count, tile, tile), arrays[0].dtype)
    return tile_kernel_call(kernel, index, arrays, out_shape)


def join_tiles(tiles, index, row_blocks, first_columns, second_columns):
    tile = tiles.shape[-1]
    first_count = row_blocks * first_columns

    def kernel(index_ref, source, first, second, sem):
        for out, start, columns in ((first, 0, first_columns), (second, first_count, second_columns)):

            def step(row, carry, out=out, start=start, columns=columns):
                for column in range(columns):
                    place = index_ref[start + row * columns + column]
                    pltpu.make_async_copy(
                        source.at[place],
                        out.at[pl.ds(row * tile, tile), pl.ds(column * tile, tile)],
                        sem,
                    ).start()
                return carry

            lax.fori_loop(0, row_blocks, step, 0)
        pltpu.make_async_copy(first, first, sem).wait()
        pltpu.make_async_copy(second, second, sem).wait()

    index = jnp.clip(index, 0, tiles.shape[0] - 1)
    out_shape = (
        jax.ShapeDtypeStruct((row_blocks * tile, first_columns * tile), tiles.dtype),
        jax.ShapeDtypeStruct((row_blocks * tile, second_columns * tile), tiles.dtype),
    )
    return tile_kernel_call(kernel, index, [tiles], out_shape)


def cut_tiles(first, second, index, tile):
    row_blocks = first.shape[0] // tile
    first_columns = first.shape[1] // tile
    second_columns = second.shape[1] // tile
    first_count = row_blocks * first_columns
    count = index.shape[0]

    def kernel(index_ref, first_ref, second_ref, out, sem):
        def step(i, carry):
            place = index_ref[i]

            def send(ref, local, columns):
                row = pl.multiple_of((local // columns) * tile, tile)
                column = pl.multiple_of((local % columns) * tile, tile)
                pltpu.make_async_copy(
                    ref.at[pl.ds(row, tile), pl.ds(column, tile)], out.at[i], sem
                ).start()

            @pl.when(place < first_count)
            def _():
                send(first_ref, place, first_columns)

            @pl.when(place >= first_count)
            def _():
                send(second_ref, place - first_count, second_columns)

            return carry

        lax.fori_loop(0, count, step, 0)
        pltpu.make_async_copy(out, out, sem).wait()

    index = jnp.clip(index, 0, first_count + row_blocks * second_columns - 1)
    out_shape = jax.ShapeDtypeStruct((count, tile, tile), first.dtype)
    return tile_kernel_call(kernel, index, [first, second], out_shape)


def seq_swap(value, flip):
    size = lax.axis_size("seq")
    return lax.ppermute(value, "seq", [(i, i ^ flip) for i in range(size)])


def core_swap(value):
    size = lax.axis_size("fsdp")
    return lax.ppermute(value, "fsdp", [(i, i ^ 1) for i in range(size)])


def chip_shift(value, offset):
    size = lax.axis_size("fsdp")
    chips = size // 2
    return lax.ppermute(
        value, "fsdp", [(i, (i // 2 + offset) % chips * 2 + i % 2) for i in range(size)]
    )


def seq_gather(value):
    size = lax.axis_size("seq")
    return jnp.concatenate([value] + [seq_swap(value, flip) for flip in range(1, size)], axis=0)


def seq_exchange(value):
    size = lax.axis_size("seq")
    parts = [value[0]] + [seq_swap(value[flip], flip) for flip in range(1, size)]
    return jnp.stack(parts, axis=0)


def seq_sum(value):
    size = lax.axis_size("seq")
    rows = value.shape[0] // size
    parts = value.reshape(size, rows, value.shape[1])
    low = parts.astype(jnp.bfloat16)
    total = parts[0]
    for flip in range(1, size):
        total = total + seq_swap(low[flip], flip).astype(jnp.float32)
    return total


def chip_exchange(value):
    chips = value.shape[0]
    parts = [value[0]] + [chip_shift(value[offset], offset) for offset in range(1, chips)]
    return jnp.stack(parts, axis=0)


def on_device(
    tokens,
    layer_vectors,
    doc_lengths,
    cotangent,
    tile_owner,
    tile_master,
    tile_first,
    tile_second,
    left_basis,
    right_basis,
    small_master,
    small_first,
    small_second,
    small_left,
    small_right,
    gains,
    gain_first,
    gain_second,
):
    bf16 = jnp.bfloat16
    f32 = jnp.float32
    tile = tile_master.shape[1]
    width = tokens.shape[2]
    row_blocks = width // tile
    rows = tokens.shape[1]
    seq_size = lax.axis_size("seq")
    fsdp_size = lax.axis_size("fsdp")
    chips = fsdp_size // 2
    mine = tile_master.shape[0]
    tiles = tile_owner.shape[0]
    length = rows * seq_size
    per_device = HEADS // seq_size
    per_key = seq_size // KV_HEADS
    query_width = HEADS * HEAD_DIM
    key_width = KV_HEADS * HEAD_DIM
    my_seq = lax.axis_index("seq")
    my_fsdp = lax.axis_index("fsdp")
    my_chip = my_fsdp // 2
    my_core = my_fsdp % 2
    flips = jnp.arange(seq_size)
    shifts = jnp.arange(chips)

    query_blocks = query_width // tile
    key_blocks = key_width // tile
    ffn_blocks = FF // tile
    query_each = query_blocks // seq_size
    head_blocks = HEAD_DIM // tile
    ffn_each = ffn_blocks // fsdp_size
    columns = tiles // row_blocks
    attn_first = query_each + head_blocks
    attn_count = row_blocks * (attn_first + query_each)
    ffn_first = 2 * ffn_each
    ffn_count = row_blocks * 3 * ffn_each
    attn_share = (2 * query_blocks + 2 * key_blocks) / columns
    ffn_share = 3 * ffn_blocks / columns
    attn_room = room(mine, attn_share / seq_size)
    attn_hold = room(attn_count, 1.0 / fsdp_size)
    ffn_room = (room(2 * mine, ffn_share / chips) + 1) // 2
    ffn_hold = room(ffn_count, 1.0 / seq_size)

    def tile_places(owner):
        row = owner // columns
        column = owner % columns
        key_at = column - query_blocks
        value_at = key_at - key_blocks
        out_at = value_at - key_blocks
        ffn_at = out_at - query_blocks
        is_attn = ffn_at < 0
        kind = ffn_at // ffn_blocks
        ffn_column = ffn_at % ffn_blocks
        ffn_to = jnp.where(is_attn, -1, ffn_column // ffn_each)
        ffn_local = ffn_column % ffn_each
        ffn_place = jnp.where(
            kind == 2,
            row_blocks * ffn_first + row * ffn_each + ffn_local,
            row * ffn_first + kind * ffn_each + ffn_local,
        )
        attn_to = jnp.where(
            key_at < 0,
            column // query_each,
            jnp.where(
                value_at < 0,
                key_at // head_blocks * per_key,
                jnp.where(
                    out_at < 0,
                    value_at // head_blocks * per_key + per_key - 1,
                    out_at // query_each,
                ),
            ),
        )
        attn_place = jnp.where(
            key_at < 0,
            row * attn_first + column % query_each,
            jnp.where(
                out_at < 0,
                row * attn_first + query_each + key_at % head_blocks,
                row_blocks * attn_first + row * query_each + out_at % query_each,
            ),
        )
        attn_to = jnp.where(is_attn, attn_to, -1)
        return (ffn_to, ffn_place, attn_to, attn_place)

    owners = tile_owner.reshape(seq_size, fsdp_size, mine)
    ffn_to, ffn_place, attn_to, attn_place = tile_places(owners)
    slot_seq = jnp.arange(seq_size)[:, None, None]
    slot_fsdp = jnp.arange(fsdp_size)[None, :, None]
    slot_chip = slot_fsdp // 2
    ffn_chip = jnp.where(ffn_to < 0, -1, ffn_to // 2)
    chip_view = ffn_chip.reshape(seq_size, chips, 2 * mine)
    chip_rank = count_earlier(chip_view, chip_view >= 0).reshape(owners.shape)
    seq_view = ffn_to.reshape(seq_size, fsdp_size * mine)
    ffn_rank = count_earlier(seq_view, seq_view >= 0).reshape(owners.shape)
    attn_rank = count_earlier(attn_to, attn_to >= 0)
    fsdp_view = attn_to.transpose(1, 0, 2).reshape(fsdp_size, seq_size * mine)
    attn_order = (
        count_earlier(fsdp_view, fsdp_view >= 0)
        .reshape(fsdp_size, seq_size, mine)
        .transpose(1, 0, 2)
    )
    fits = jnp.all(
        jnp.where(
            ffn_to < 0,
            (attn_rank < attn_room) & (attn_order < attn_hold),
            (chip_rank < 2 * ffn_room) & (ffn_rank < ffn_hold),
        )
    )
    half = chips * ffn_room
    rank_core = chip_rank // ffn_room
    rank_local = chip_rank % ffn_room
    out_place = (
        jnp.where(rank_core == my_core, 0, half)
        + (my_chip - slot_chip) % chips * ffn_room
        + rank_local
    )
    back_place = (
        jnp.where(rank_core == my_core, 0, half) + (my_chip - ffn_chip) % chips * ffn_room + rank_local
    )
    my_chip_slots = lax.dynamic_slice(
        jnp.stack([ffn_chip, chip_rank]), (0, my_seq, 2 * my_chip, 0), (2, 1, 2, mine)
    ).reshape(2, 2 * mine)
    my_slots = lax.dynamic_slice(
        jnp.stack([ffn_to, attn_to, attn_rank, back_place]),
        (0, my_seq, my_fsdp, 0),
        (4, 1, 1, mine),
    ).reshape(4, mine)
    seq_slots = lax.dynamic_slice(
        jnp.stack([ffn_to, ffn_rank, ffn_place, out_place, chip_rank, jnp.broadcast_to(slot_chip, owners.shape)]),
        (0, my_seq, 0, 0),
        (6, 1, fsdp_size, mine),
    ).reshape(6, fsdp_size * mine)
    fsdp_slots = lax.dynamic_slice(
        jnp.stack([attn_to, attn_order, attn_rank, jnp.broadcast_to(slot_seq, owners.shape)]),
        (0, 0, my_fsdp, 0),
        (4, seq_size, 1, mine),
    ).reshape(4, seq_size * mine)

    local_slots = jnp.arange(mine)
    attn_pack = pick(
        (my_slots[1][None, None, :] == (my_seq ^ flips)[:, None, None])
        & (my_slots[2][None, None, :] == jnp.arange(attn_room)[None, :, None]),
        local_slots,
    )
    attn_keep = pick(
        (fsdp_slots[0][None, :] == my_seq)
        & (fsdp_slots[1][None, :] == jnp.arange(attn_hold)[:, None]),
        (fsdp_slots[3] ^ my_seq) * attn_room + fsdp_slots[2],
    )
    attn_join = pick(
        (attn_to.reshape(1, -1) == my_seq)
        & (attn_place.reshape(1, -1) == jnp.arange(attn_count)[:, None]),
        (slot_fsdp * attn_hold + attn_order).reshape(1, -1),
    )
    ffn_pack = pick(
        (my_chip_slots[0][None, None, :] == ((my_chip + shifts) % chips)[:, None, None])
        & (
            my_chip_slots[1][None, None, :]
            == (my_core * ffn_room + jnp.arange(ffn_room))[None, :, None]
        ),
        jnp.arange(2 * mine) ^ 0,
    )
    ffn_pack = jnp.where(
        ffn_pack // mine == my_core, ffn_pack % mine, mine + ffn_pack % mine
    )
    ffn_keep = pick(
        (seq_slots[0][None, :] == my_fsdp) & (seq_slots[1][None, :] == jnp.arange(ffn_hold)[:, None]),
        seq_slots[3][None, :],
    )
    ffn_join = pick(
        (ffn_to.reshape(1, -1) == my_fsdp)
        & (ffn_place.reshape(1, -1) == jnp.arange(ffn_count)[:, None]),
        (slot_seq * ffn_hold + ffn_rank).reshape(1, -1),
    )
    master_low = tile_master.astype(bf16)
    attn_sent = gather_tiles([master_low], attn_pack.reshape(-1))
    attn_got = seq_exchange(attn_sent.reshape(seq_size, attn_room, tile, tile))
    attn_kept = gather_tiles([attn_got.reshape(-1, tile, tile)], attn_keep)
    attn_all = lax.all_gather(attn_kept, "fsdp", axis=0, tiled=True)
    w_first, w_out = join_tiles(attn_all, attn_join, row_blocks, attn_first, query_each)

    master_other = core_swap(master_low)
    ffn_sent = gather_tiles([master_low, master_other], ffn_pack.reshape(-1))
    ffn_got = chip_exchange(ffn_sent.reshape(chips, ffn_room, tile, tile)).reshape(-1, tile, tile)
    ffn_other = core_swap(ffn_got)
    ffn_kept = gather_tiles([ffn_got, ffn_other], ffn_keep)
    ffn_all = lax.all_gather(ffn_kept, "seq", axis=0, tiled=True)
    w_both, w_down = join_tiles(ffn_all, ffn_join, row_blocks, ffn_first, ffn_each)

    my_columns = jnp.arange(tiles)
    def slow_fetch(_, kept):
        whole = lax.all_gather(master_low, ("seq", "fsdp"), axis=0, tiled=True)
        slots = my_columns.reshape(1, -1)
        attn_slots = pick(
            (attn_to.reshape(1, -1) == my_seq)
            & (attn_place.reshape(1, -1) == jnp.arange(attn_count)[:, None]),
            slots,
        )
        ffn_slots = pick(
            (ffn_to.reshape(1, -1) == my_fsdp)
            & (ffn_place.reshape(1, -1) == jnp.arange(ffn_count)[:, None]),
            slots,
        )
        return join_tiles(whole, attn_slots, row_blocks, attn_first, query_each) + join_tiles(
            whole, ffn_slots, row_blocks, ffn_first, ffn_each
        )

    slow_steps = jnp.where(fits, 0, 1)
    w_first, w_out, w_both, w_down = lax.fori_loop(
        0, slow_steps, slow_fetch, (w_first, w_out, w_both, w_down)
    )

    small_got, gain_got = (
        lax.all_gather(small_master.astype(bf16), "seq", axis=0, tiled=True),
        lax.all_gather(gains.astype(bf16), "seq", axis=0, tiled=True),
    )
    small_table = assemble(small_got, row_blocks)
    gain_full = gain_got.astype(f32)
    gain_in = gain_full[0:width]
    gain_attn = gain_full[width : 2 * width]
    gain_laurel = gain_full[2 * width : 3 * width]
    gain_pre = gain_full[3 * width : 4 * width]
    gain_post = gain_full[4 * width : 5 * width]
    gain_vec = gain_full[5 * width : 6 * width]
    gain_query = gain_full[6 * width : 6 * width + HEAD_DIM]
    gain_key = gain_full[6 * width + HEAD_DIM : 6 * width + 2 * HEAD_DIM]
    laurel_left = small_table[:, :RANK]
    laurel_right = small_table[:, RANK : 2 * RANK]
    vector_gate_w = small_table[:, 2 * RANK : 2 * RANK + PLD]
    vector_proj_w = small_table[:, 2 * RANK + PLD :]

    pack_tokens = seq_gather(tokens[0])
    segment, position = documents(doc_lengths[0], length)
    places = ((my_seq ^ flips)[:, None] * rows + jnp.arange(rows)[None, :]).reshape(-1)

    def reorder(values):
        blocks = values.reshape(seq_size, rows)
        return jnp.concatenate(
            [lax.dynamic_index_in_dim(blocks, my_seq ^ i, 0, False) for i in range(seq_size)]
        )

    pack_segment = reorder(segment)
    pack_position = reorder(position)
    stream = tokens[0].astype(f32)
    vectors = layer_vectors[0].astype(f32)
    normed, normed_pull = jax.vjp(rms_norm, stream, gain_in)
    normed_low = normed.astype(bf16)
    pack_normed = rms_norm(pack_tokens.astype(f32), gain_in).astype(bf16)
    first_pre = matmul(pack_normed, w_first)
    is_key = my_seq % per_key == 0

    def shape_query(query_in, query_gain):
        return rotary(
            rms_norm(query_in.reshape(length, per_device, HEAD_DIM), query_gain), pack_position
        )

    def shape_key(key_in, key_gain):
        return rotary(rms_norm(key_in.reshape(length, 1, HEAD_DIM), key_gain), pack_position)

    query_pre = first_pre[:, : per_device * HEAD_DIM]
    other_pre = first_pre[:, per_device * HEAD_DIM :]
    query_rot, query_pull = jax.vjp(shape_query, query_pre, gain_query)
    key_rot, key_pull = jax.vjp(shape_key, other_pre, gain_key)
    query_heads = query_rot.astype(bf16)
    other_low = jnp.where(is_key, key_rot[:, 0, :], other_pre).astype(bf16)
    partner_low = seq_swap(other_low, 1).reshape(seq_size // 2, 2, rows, HEAD_DIM)
    partner_low = partner_low[:, ::-1].reshape(length, HEAD_DIM)
    key_single = jnp.where(is_key, other_low, partner_low)
    value_single = jnp.where(is_key, partner_low, other_low)

    allow = (pack_segment[:, None] == pack_segment[None, :]) & (
        places[None, :] <= places[:, None]
    )
    raw = (
        jnp.einsum("qhd,kd->qhk", query_heads, key_single, preferred_element_type=f32) * SCALE
    )
    scores = jnp.where(allow[:, None, :], raw, NEGATIVE)
    powers = jnp.exp(scores - jnp.max(scores, axis=-1, keepdims=True))
    prob = powers / jnp.sum(powers, axis=-1, keepdims=True)
    prob_low = prob.astype(bf16)
    attended_low = (
        jnp.einsum("qhk,kd->qhd", prob_low, value_single, preferred_element_type=f32)
        .astype(bf16)
        .reshape(length, per_device * HEAD_DIM)
    )
    attn_pre = seq_sum(matmul_flip(attended_low, w_out))
    attn_normed, attn_pull = jax.vjp(rms_norm, attn_pre, gain_attn)
    first_sum = stream + attn_normed
    left_pre = matmul(normed_low, laurel_left)
    left_low = left_pre.astype(bf16)
    right_pre = matmul_flip(left_low, laurel_right)
    laurel_normed, laurel_pull = jax.vjp(rms_norm, right_pre, gain_laurel)
    second_sum = (first_sum + normed + laurel_normed) * ROOT_HALF
    feed_normed, feed_pull = jax.vjp(rms_norm, second_sum, gain_pre)
    feed_low = lax.all_gather(feed_normed.astype(bf16), "fsdp", axis=0, tiled=True)
    both_pre = matmul(feed_low, w_both)
    ffn_width = w_down.shape[1]
    hidden, hidden_pull = jax.vjp(gelu_product, both_pre[:, :ffn_width], both_pre[:, ffn_width:])
    hidden_low = hidden.astype(bf16)
    down_pre = lax.psum_scatter(
        matmul_flip(hidden_low, w_down).astype(bf16), "fsdp", scatter_dimension=0, tiled=True
    ).astype(f32)
    down_normed, down_pull = jax.vjp(rms_norm, down_pre, gain_post)
    third_sum = second_sum + down_normed
    third_low = third_sum.astype(bf16)
    vector_pre = matmul(third_low, vector_gate_w)
    vector_gated, vector_pull = jax.vjp(lambda inner: gelu_product(inner, vectors), vector_pre)
    vector_low = vector_gated.astype(bf16)
    proj_pre = matmul_flip(vector_low, vector_proj_w)
    proj_normed, proj_pull = jax.vjp(rms_norm, proj_pre, gain_vec)
    result = third_sum + proj_normed
    output = result.astype(bf16)[None]

    grad_out = cotangent[0].astype(f32)
    grad_proj, grad_gain_vec = proj_pull(grad_out)
    proj_grad_low = grad_proj.astype(bf16)
    (grad_vector_pre,) = vector_pull(matmul(proj_grad_low, vector_proj_w))
    vector_grad_low = grad_vector_pre.astype(bf16)
    grad_third = grad_out + matmul_flip(vector_grad_low, vector_gate_w)
    grad_down, grad_gain_post = down_pull(grad_third)
    down_grad_low = lax.all_gather(grad_down.astype(bf16), "fsdp", axis=0, tiled=True)
    grad_gate, grad_up = hidden_pull(matmul(down_grad_low, w_down))
    both_grad_low = jnp.concatenate([grad_gate, grad_up], axis=1).astype(bf16)
    grad_feed = lax.psum_scatter(
        matmul_flip(both_grad_low, w_both).astype(bf16), "fsdp", scatter_dimension=0, tiled=True
    ).astype(f32)
    both_grad_w = matmul_outer(feed_low, both_grad_low).astype(bf16)
    down_grad_w = matmul_outer(down_grad_low, hidden_low).astype(bf16)

    grad_second_norm, grad_gain_pre = feed_pull(grad_feed)
    half_grad = (grad_third + grad_second_norm) * ROOT_HALF
    grad_right, grad_gain_laurel = laurel_pull(half_grad)
    right_grad_low = grad_right.astype(bf16)
    left_grad_low = matmul(right_grad_low, laurel_right).astype(bf16)
    grad_attn, grad_gain_attn = attn_pull(half_grad)
    attn_grad_low = seq_gather(grad_attn.astype(bf16))
    grad_attended = (
        matmul(attn_grad_low, w_out).astype(bf16).reshape(length, per_device, HEAD_DIM)
    )
    out_grad_w = matmul_outer(attn_grad_low, attended_low).astype(bf16)
    value_grad = jnp.einsum("qhk,qhd->kd", prob_low, grad_attended, preferred_element_type=f32)
    grad_prob = jnp.einsum("qhd,kd->qhk", grad_attended, value_single, preferred_element_type=f32)
    inner = jnp.sum(prob * grad_prob, axis=-1, keepdims=True)
    grad_score = (prob * (grad_prob - inner)).astype(bf16)
    grad_query = (
        jnp.einsum("qhk,kd->qhd", grad_score, key_single, preferred_element_type=f32) * SCALE
    ).astype(bf16)
    key_grad = (
        jnp.einsum("qhk,qhd->kd", grad_score, query_heads, preferred_element_type=f32) * SCALE
    ).astype(bf16)
    value_grad = value_grad.astype(bf16)
    partner_grad = seq_swap(jnp.where(is_key, value_grad, key_grad), 1)
    partner_grad = partner_grad.reshape(seq_size // 2, 2, rows, HEAD_DIM)[:, ::-1]
    other_grad = jnp.where(is_key, key_grad, value_grad).astype(f32) + partner_grad.reshape(
        length, HEAD_DIM
    ).astype(f32)
    grad_query_pre, grad_gain_query = query_pull(grad_query.astype(f32))
    grad_key_pre, grad_gain_key = key_pull(other_grad[:, None, :])
    grad_gain_key = jnp.where(is_key, grad_gain_key, 0.0)
    first_grad_low = jnp.concatenate(
        [grad_query_pre, jnp.where(is_key, grad_key_pre, other_grad)], axis=1
    ).astype(bf16)
    first_grad_w = matmul_outer(pack_normed, first_grad_low).astype(bf16)
    grad_normed = (
        half_grad
        + matmul_flip(left_grad_low, laurel_left)
        + seq_sum(matmul_flip(first_grad_low, w_first))
    )
    grad_stream_norm, grad_gain_in = normed_pull(grad_normed)
    input_grad = (half_grad + grad_stream_norm)[None]

    ffn_cut = pick(
        (ffn_to.reshape(seq_size, 1, -1) == my_fsdp)
        & (ffn_rank.reshape(seq_size, 1, -1) == jnp.arange(ffn_hold)[None, :, None]),
        ffn_place.reshape(seq_size, 1, -1),
    )
    ffn_back = pick(
        (seq_slots[5][None, None, :] == ((my_chip + shifts) % chips)[:, None, None])
        & (seq_slots[0][None, None, :] // 2 == my_chip)
        & (seq_slots[0][None, None, :] >= 0)
        & (seq_slots[4][None, None, :] == (my_core * ffn_room + jnp.arange(ffn_room))[None, :, None]),
        jnp.where(seq_slots[0] == my_fsdp, 0, ffn_hold) + seq_slots[1],
    )
    ffn_parts = cut_tiles(both_grad_w, down_grad_w, ffn_cut.reshape(-1), tile)
    ffn_sum = lax.psum_scatter(ffn_parts, "seq", scatter_dimension=0, tiled=True)
    ffn_sum_other = core_swap(ffn_sum)
    ffn_return = gather_tiles([ffn_sum, ffn_sum_other], ffn_back.reshape(-1))
    ffn_returned = chip_exchange(ffn_return.reshape(chips, ffn_room, tile, tile))
    ffn_returned = ffn_returned.reshape(-1, tile, tile)
    ffn_returned_other = core_swap(ffn_returned)

    attn_cut = pick(
        (attn_to.transpose(1, 0, 2).reshape(fsdp_size, 1, -1) == my_seq)
        & (
            attn_order.transpose(1, 0, 2).reshape(fsdp_size, 1, -1)
            == jnp.arange(attn_hold)[None, :, None]
        ),
        attn_place.transpose(1, 0, 2).reshape(fsdp_size, 1, -1),
    )
    attn_back = pick(
        (fsdp_slots[3][None, None, :] == (my_seq ^ flips)[:, None, None])
        & (fsdp_slots[0][None, None, :] == my_seq)
        & (fsdp_slots[2][None, None, :] == jnp.arange(attn_room)[None, :, None]),
        fsdp_slots[1],
    )
    attn_parts = cut_tiles(first_grad_w, out_grad_w, attn_cut.reshape(-1), tile)
    attn_sum = lax.psum_scatter(attn_parts, "fsdp", scatter_dimension=0, tiled=True)
    attn_return = gather_tiles([attn_sum], attn_back.reshape(-1))
    attn_returned = seq_exchange(attn_return.reshape(seq_size, attn_room, tile, tile))
    slot_grad = jnp.where(
        my_slots[0] >= 0,
        my_slots[3],
        2 * half + (my_slots[1] ^ my_seq) * attn_room + my_slots[2],
    )
    tile_grad_low = gather_tiles(
        [ffn_returned, ffn_returned_other, attn_returned.reshape(-1, tile, tile)], slot_grad
    )

    def slow_return(_, kept):
        ffn_parts = split_tiles(both_grad_w, tile), split_tiles(down_grad_w, tile)
        attn_parts = split_tiles(first_grad_w, tile), split_tiles(out_grad_w, tile)
        parts = jnp.concatenate(ffn_parts + attn_parts + (jnp.zeros((1, tile, tile), bf16),))
        index = jnp.where(
            ffn_to == my_fsdp,
            ffn_place,
            jnp.where(attn_to == my_seq, ffn_count + attn_place, ffn_count + attn_count),
        )
        spread = gather_tiles([parts], index.reshape(-1))
        return lax.psum_scatter(spread, ("seq", "fsdp"), scatter_dimension=0, tiled=True)

    tile_grad = lax.fori_loop(0, slow_steps, slow_return, tile_grad_low).astype(f32)

    small_full = jnp.concatenate(
        [
            matmul_outer(normed_low, left_grad_low),
            matmul_outer(right_grad_low, left_low),
            matmul_outer(third_low, vector_grad_low),
            matmul_outer(proj_grad_low, vector_low),
        ],
        axis=1,
    )
    small_tiles_grad = split_tiles(small_full, tile)
    gain_grad = jnp.concatenate(
        [
            grad_gain_in,
            grad_gain_attn,
            grad_gain_laurel,
            grad_gain_pre,
            grad_gain_post,
            grad_gain_vec,
            grad_gain_query,
            grad_gain_key,
        ]
    )
    small_part = lax.psum_scatter(
        small_tiles_grad.astype(bf16), "seq", scatter_dimension=0, tiled=True
    )
    small_grad = lax.psum(small_part, "fsdp").astype(f32)
    whole_gain = lax.psum(gain_grad.astype(bf16), "fsdp")
    gain_grad_mine = lax.psum_scatter(whole_gain, "seq", scatter_dimension=0, tiled=True).astype(f32)
    tile_new, tile_first_new, tile_second_new = rotate_update(
        tile_grad, tile_master, tile_first, tile_second, left_basis, right_basis, RATE_TILE
    )
    small_new, small_first_new, small_second_new = rotate_update(
        small_grad, small_master, small_first, small_second, small_left, small_right, RATE_SMALL
    )
    gain_first_new = BETA_ONE * gain_first + (1.0 - BETA_ONE) * gain_grad_mine
    gain_second_new = BETA_TWO * gain_second + (1.0 - BETA_TWO) * gain_grad_mine * gain_grad_mine
    correct_one = 1.0 - BETA_ONE**STEP
    correct_two = 1.0 - BETA_TWO**STEP
    gain_new = gains - RATE_GAIN * (gain_first_new / correct_one) / (
        jnp.sqrt(gain_second_new / correct_two) + ADAM_EPS
    )
    return (
        output,
        input_grad,
        tile_new,
        tile_first_new,
        tile_second_new,
        small_new,
        small_first_new,
        small_second_new,
        gain_new,
        gain_first_new,
        gain_second_new,
    )


def solution(mesh):
    return jax.shard_map(
        on_device,
        mesh=mesh,
        in_specs=(
            P("fsdp", "seq", None),
            P("fsdp", "seq", None),
            P("fsdp", None),
            P("fsdp", "seq", None),
            P(),
            P(("seq", "fsdp"), None, None),
            P(("seq", "fsdp"), None, None),
            P(("seq", "fsdp"), None, None),
            P(("seq", "fsdp"), None, None),
            P(("seq", "fsdp"), None, None),
            P("seq", None, None),
            P("seq", None, None),
            P("seq", None, None),
            P("seq", None, None),
            P("seq", None, None),
            P("seq"),
            P("seq"),
            P("seq"),
        ),
        out_specs=(
            P("fsdp", "seq", None),
            P("fsdp", "seq", None),
            P(("seq", "fsdp"), None, None),
            P(("seq", "fsdp"), None, None),
            P(("seq", "fsdp"), None, None),
            P("seq", None, None),
            P("seq", None, None),
            P("seq", None, None),
            P("seq"),
            P("seq"),
            P("seq"),
        ),
        check_vma=False,
    )
```

time: 5030 us -> 3150 us (0.63)
  waiting for transfers between devices: 3080 us -> 493 us
  Pallas kernels: 0 us -> 2090 us
  local copies, waits for them, and re-layouts: 1240 us -> 137 us
  matrix products: 503 us -> 202 us
    unnamed x6 -> x12, waiting for transfers between devices: 2430 us -> 0.2 us
    pallas_call x0 -> x11, Pallas kernels: none -> 2090 us  [tile_kernel_call(): pl.pallas_call(kernel, out_shape=out_shape, in_specs=[pl.BlockSpec(memory...]
    scatter x1 -> x0, local copies, waits for them, and re-layouts: 551 us -> none  [on_device(): jnp.zeros_like(gathered).at[tile_owner].set(gathered)]
    all_gather x2 -> x5, waiting for transfers between devices: 633 us -> 94.9 us  [the longest x1 49.3 us: on_device(): lax.all_gather(feed_normed.astype(bf16), 'fsdp', axis=0, tiled=True)]
    ppermute x0 -> x30, waiting for transfers between devices: none -> 307 us  [the longest x6 203 us: chip_shift(): lax.ppermute(value, 'fsdp', [(i, (i // 2 + offset) % chips * 2 + i % 2) f...]
    gather x64 -> x0, local copies, waits for them, and re-layouts: 290 us -> none  [the longest x32 196 us: group_terms(): rights = right_tiles[column]]
    dot_general x38 -> x5, matrix products: 258 us -> 8.22 us  [the longest x1 3.08 us: on_device(): jnp.einsum('qhk,qhd->kd', prob_low, grad_attended, preferred_element_type...]
    transpose x3 -> x2, local copies, waits for them, and re-layouts: 131 us -> 0.01 us  [the longest x1 0.01 us: on_device(): attn_place.transpose(1, 0, 2).reshape(fsdp_size, 1, -1)]
  transfers between devices with their start and end apart: 13 -> 41, of which waited for: 8 -> 25; matrix products, arithmetic and copies ran while one was open for 15% -> 7% of each run, Pallas kernels for 0% -> 51%
where the time goes in v1:
time: 3150 us; the launch traced here: 3140 us
  Pallas kernels  2090 us (66%)
  waiting for transfers between devices  493 us (16%)
  matrix products  202 us (6%)
  local copies, waits for them, and re-layouts  137 us (4%)
  other arithmetic  98.8 us (3%)
  blocking collectives  61.5 us (2%)
  starting transfers between devices  31.8 us (1%)
    pallas_call x11, Pallas kernels, tile_kernel_call(): pl.pallas_call(kernel, out_shape=out_shape, in_specs=[pl.BlockSpec(memory...  2090 us
    ppermute x6, waiting for transfers between devices, chip_shift(): lax.ppermute(value, 'fsdp', [(i, (i // 2 + offset) % chips * 2 + i % 2) f...  203 us
    unnamed x352, local copies, waits for them, and re-layouts  89.6 us
    ppermute x20, waiting for transfers between devices, seq_swap(): return lax.ppermute(value, 'seq', [(i, i ^ flip) for i in range(size)])  88.1 us
  transfers between devices with their start and end apart: 41, of which 25 were waited for; matrix products, arithmetic and copies ran while one was open for 7% of the time, Pallas kernels for 51%

profile of v1, /device:TPU:9, one launch (start us, length us, event | category | flops | bytes accessed | tf_op | source)
XLA Modules:
  0.0 3137.3 jit_solution(7966290934546418597)
XLA Ops:
  34.3 65.3 %shard_map.257 = bf16[64,128,128]{2,1,0:T(8,128)(2,1)} custom-call(s32[64]{0:T(128)} %min.128.index_ref, bf16[116,128,128]{2,1,0:T(8,128)(2,1)} %convert_element_type.219.refs_0_), custom_call_target="tpu_custom_call" | custom-call | tf_op jit(solution)/shard_map/pallas_call | solution.py:139
  130.4 40.5 %shard_map.258 = bf16[39,128,128]{2,1,0:T(8,128)(2,1)} custom-call(s32[39]{0:T(128)} %broadcast_clamp_fusion.10.index_ref, bf16[64,128,128]{2,1,0:T(8,128)(2,1)} %bitcast.366), custom_call_target="tpu_custom_call" | custom-call | tf_op jit(solution)/shard_map/pallas_call | solution.py:139
  179.5 148.7 %shard_map.260 = bf16[148,128,128]{2,1,0:T(8,128)(2,1)} custom-call(s32[148]{0:T(256)} %fusion.256.index_ref, bf16[116,128,128]{2,1,0:T(8,128)(2,1)} %convert_element_type.219.refs_0_, bf16[116,128,128]{2,1,0:T(8,128)(2,1)} %collective-permute-done.6.refs_1_), custom_call_target="tpu_custom_call" | custom-call | tf_op jit(solution)/shard_map/pallas_call | solution.py:139
  335.6 23.9 collective-permute-done.7
  359.5 77.0 %collective-permute-done.8 = bf16[37,128,128]{2,1,0:T(8,128)(2,1)S(1)} collective-permute-done((bf16[37,128,128]{2,1,0:T(8,128)(2,1)S(1)}, bf16[37,128,128]{2,1,0:T(8,128)(2,1)S(1)}, u32[]{:S(2)}, u32[]{:S(2)}) %collective-permute-start.8) | collective-permute-done | bytes 1212448 | tf_op jit(solution)/shard_map/ppermute | solution.py:256
  450.1 130.8 %shard_map.261 = bf16[130,128,128]{2,1,0:T(8,128)(2,1)} custom-call(s32[130]{0:T(256)} %broadcast_clamp_fusion.8.index_ref, bf16[148,128,128]{2,1,0:T(8,128)(2,1)} %bitcast.32.refs_0_, bf16[148,128,128]{2,1,0:T(8,128)(2,1)} %collective-permute-done.10.refs_1_), custom_call_target="tpu_custom_call" | custom-call | tf_op jit(solution)/shard_map/pallas_call | solution.py:139
  585.5 34.6 %all-gather = bf16[4,1,3200]{2,1,0:T(2,128)(2,1)S(1)} all-gather(bf16[1,1,3200]{2,1,0:T(2,128)(2,1)S(1)} %reshape.2501), channel_id=1, replica_groups=mesh['seq'=4,'fsdp'=8] {'seq'}, dimensions={0}, use_global_device_ids=true | all-gather | bytes 32000 | tf_op jit(solution)/shard_map/all_gather | solution.py:522
  644.3 160.6 %shard_map.259 = (bf16[2048,768]{1,0:T(8,128)(2,1)}, bf16[2048,512]{1,0:T(8,128)(2,1)}) custom-call(s32[160]{0:T(256)} %broadcast_clamp_fusion.9.index_ref, bf16[312,128,128]{2,1,0:T(8,128)(2,1)} %all-gather.8.cloned.1.call-done.source), custom_call_target="tpu_custom_call" | custom-call | tf_op jit(solution)/shard_map/pallas_call | solution.py:139
  804.9 383.0 %shard_map.262 = (bf16[2048,2048]{1,0:T(8,128)(2,1)}, bf16[2048,1024]{1,0:T(8,128)(2,1)}) custom-call(s32[384]{0:T(512)} %broadcast_clamp_fusion.6.index_ref, bf16[520,128,128]{2,1,0:T(8,128)(2,1)} %all-gather.10.cloned.1.call-done.source), custom_call_target="tpu_custom_call" | custom-call | tf_op jit(solution)/shard_map/pallas_call | solution.py:139
  1243.0 49.3 %all-gather.14.cloned.1.call-done = bf16[1024,2048]{1,0:T(8,128)(2,1)} async-done(((bf16[128,2048]{1,0:T(8,128)(2,1)}), bf16[1024,2048]{1,0:T(8,128)(2,1)}) %all-gather.14.cloned.1.call-update) | async-done | bytes 4194320 | tf_op jit(solution)/shard_map/all_gather | solution.py:602
  1292.3 12.5 fusion.315
  1316.6 48.4 %reduce-scatter.15.cloned.1.call-done = bf16[128,2048]{1,0:T(8,128)(2,1)} async-done(((bf16[1024,2048]{1,0:T(8,128)(2,1)}), bf16[128,2048]{1,0:T(8,128)(2,1)}) %reduce-scatter.15.cloned.1.call-update) | async-done | bytes 524304 | tf_op jit(solution)/shard_map/reduce_scatter | solution.py:607
  1378.8 45.6 %all-gather.16.cloned.1.call-done = bf16[1024,2048]{1,0:T(8,128)(2,1)} async-done(((bf16[128,2048]{1,0:T(8,128)(2,1)}), bf16[1024,2048]{1,0:T(8,128)(2,1)}) %all-gather.16.cloned.1.call-update) | async-done | bytes 4194320 | tf_op jit(solution)/shard_map/all_gather | solution.py:628
  1424.4 12.1 fusion.20
  1438.5 12.6 convolution_convert_fusion.1
  1456.1 43.4 %reduce-scatter.17.cloned.1.call-done = bf16[128,2048]{1,0:T(8,128)(2,1)} async-done(((bf16[1024,2048]{1,0:T(8,128)(2,1)}), bf16[128,2048]{1,0:T(8,128)(2,1)}) %reduce-scatter.17.cloned.1.call-update) | async-done | bytes 524304 | tf_op jit(solution)/shard_map/reduce_scatter | solution.py:631
  1529.7 11.6 convolution_convert_fusion.first_ref
  1541.4 518.0 %shard_map.263 = bf16[520,128,128]{2,1,0:T(8,128)(2,1)} custom-call(s32[520]{0:T(1024)} %min.142.index_ref, bf16[2048,2048]{1,0:T(8,128)(2,1)} %convolution_convert_fusion.first_ref, bf16[2048,1024]{1,0:T(8,128)(2,1)} %convolution_convert_fusion.2.second_ref), custom_call_target="tpu_custom_call" | custom-call | tf_op jit(solution)/shard_map/pallas_call | solution.py:139
  2064.7 15.5 collective-permute-done.15
  2085.9 16.6 collective-permute-done.17
  2144.9 311.5 %shard_map.265 = bf16[312,128,128]{2,1,0:T(8,128)(2,1)} custom-call(s32[312]{0:T(512)} %min.148.index_ref, bf16[2048,768]{1,0:T(8,128)(2,1)} %convolution_convert_fusion.4.first_ref, bf16[2048,512]{1,0:T(8,128)(2,1)} %convolution_convert_fusion.5.second_ref), custom_call_target="tpu_custom_call" | custom-call | tf_op jit(solution)/shard_map/pallas_call | solution.py:139
  2464.2 148.7 %shard_map.264 = bf16[148,128,128]{2,1,0:T(8,128)(2,1)} custom-call(s32[148]{0:T(256)} %min.139.index_ref, bf16[130,128,128]{2,1,0:T(8,128)(2,1)} %reduce-scatter.23.cloned.1.call-done.refs_0_, bf16[130,128,128]{2,1,0:T(8,128)(2,1)} %collective-permute-done.22.refs_1_), custom_call_target="tpu_custom_call" | custom-call | tf_op jit(solution)/shard_map/pallas_call | solution.py:139
  2624.8 20.5 collective-permute-done.23
  2645.3 76.4 %collective-permute-done.24 = bf16[37,128,128]{2,1,0:T(8,128)(2,1)S(1)} collective-permute-done((bf16[37,128,128]{2,1,0:T(8,128)(2,1)S(1)}, bf16[37,128,128]{2,1,0:T(8,128)(2,1)S(1)}, u32[]{:S(2)}, u32[]{:S(2)}) %collective-permute-start.24) | collective-permute-done | bytes 1212448 | tf_op jit(solution)/shard_map/ppermute | solution.py:256
  2777.7 12.3 all-reduce.6
  2790.1 14.6 psum.16
  2814.1 65.4 %shard_map.266 = bf16[64,128,128]{2,1,0:T(8,128)(2,1)} custom-call(s32[64]{0:T(128)} %min.145.index_ref, bf16[39,128,128]{2,1,0:T(8,128)(2,1)} %reduce-scatter.19.cloned.1.call-done.refs_0_), custom_call_target="tpu_custom_call" | custom-call | tf_op jit(solution)/shard_map/pallas_call | solution.py:139
  2909.8 117.1 %shard_map.267 = bf16[116,128,128]{2,1,0:T(8,128)(2,1)} custom-call(s32[116]{0:T(128)} %fusion.258.index_ref, bf16[148,128,128]{2,1,0:T(8,128)(2,1)} %bitcast.72.refs_0_, bf16[148,128,128]{2,1,0:T(8,128)(2,1)} %collective-permute-done.26.refs_1_, bf16[64,128,128]{2,1,0:T(8,128)(2,1)} %bitcast.365), custom_call_target="tpu_custom_call" | custom-call | tf_op jit(solution)/shard_map/pallas_call | solution.py:139
  3032.1 13.5 fusion.316
  3045.6 18.3 multiply_add_fusion
  3072.6 17.7 fusion.4
  3099.0 22.4 fusion.3
  (681 shorter events, 430.6 us)
Async XLA Ops:
  7.2 628.5 %all-gather.12.cloned.1.call-start = ((), (), s32[]{:S(2)}) async-start(), calls=%async_computation.8 | async-start | bytes 3276800 | tf_op jit(solution)/shard_map/all_gather | solution.py:521
  9.6 634.7 %all-gather.8.cloned.1.call-start = ((), (), s32[]{:S(2)}) async-start(), calls=%async_computation.6 | async-start | bytes 11501568 | tf_op jit(solution)/shard_map/all_gather | solution.py:486
  104.8 22.9 collective-permute-start.5
  171.0 633.9 %all-gather.10.cloned.1.call-start = ((), (), s32[]{:S(2)}) async-start(), calls=%async_computation.7 | async-start | bytes 21299200 | tf_op jit(solution)/shard_map/all_gather | solution.py:494
  331.6 27.9 collective-permute-start.7
  332.9 103.6 %collective-permute-start.8 = (bf16[37,128,128]{2,1,0:T(8,128)(2,1)S(1)}, bf16[37,128,128]{2,1,0:T(8,128)(2,1)S(1)}, u32[]{:S(2)}, u32[]{:S(2)}) collective-permute-start(bf16[37,128,128]{2,1,0:T(8,128)(2,1)S(1)} %get-tuple-element.546), channel_id=1, source_target_pairs={{0,4},{1,5},{2,6},{3,7},{4,0},{5,1},{6,2},{7,3},{8,12},{9,13},{10,... | collective-permute-start | bytes 3637256 | tf_op jit(solution)/shard_map/ppermute | solution.py:256
  334.0 105.0 %collective-permute-start.9 = (bf16[37,128,128]{2,1,0:T(8,128)(2,1)S(1)}, bf16[37,128,128]{2,1,0:T(8,128)(2,1)S(1)}, u32[]{:S(2)}, u32[]{:S(2)}) collective-permute-start(bf16[37,128,128]{2,1,0:T(8,128)(2,1)S(1)} %get-tuple-element.545), channel_id=1, source_target_pairs={{0,6},{1,7},{2,0},{3,1},{4,2},{5,3},{6,4},{7,5},{8,14},{9,15},{10,... | collective-permute-start | bytes 3637256 | tf_op jit(solution)/shard_map/ppermute | solution.py:256
  582.0 51.1 %collective-permute-start = (bf16[128,2048]{1,0:T(8,128)(2,1)S(1)}, bf16[128,2048]{1,0:T(8,128)(2,1)S(1)}, u32[]{:S(2)}, u32[]{:S(2)}) collective-permute-start(bf16[128,2048]{1,0:T(8,128)(2,1)S(1)} %bitcast.356), channel_id=1, source_target_pairs={{0,8},{8,0},{16,24},{24,16},{1,9},{9,1},{17,25},{25,17},{2,10},{10... | collective-permute-start | bytes 1572872 | tf_op jit(solution)/shard_map/ppermute | solution.py:245
  583.0 50.2 %collective-permute-start.1 = (bf16[128,2048]{1,0:T(8,128)(2,1)S(1)}, bf16[128,2048]{1,0:T(8,128)(2,1)S(1)}, u32[]{:S(2)}, u32[]{:S(2)}) collective-permute-start(bf16[128,2048]{1,0:T(8,128)(2,1)S(1)} %bitcast.357), channel_id=1, source_target_pairs={{0,16},{8,24},{16,0},{24,8},{1,17},{9,25},{17,1},{25,9},{2,18},{10... | collective-permute-start | bytes 1572872 | tf_op jit(solution)/shard_map/ppermute | solution.py:245
  583.5 49.7 %collective-permute-start.2 = (bf16[128,2048]{1,0:T(8,128)(2,1)S(1)}, bf16[128,2048]{1,0:T(8,128)(2,1)}, u32[]{:S(2)}, u32[]{:S(2)}) collective-permute-start(bf16[128,2048]{1,0:T(8,128)(2,1)S(1)} %bitcast.358), channel_id=1, source_target_pairs={{0,24},{8,16},{16,8},{24,0},{1,25},{9,17},{17,9},{25,1},{2,26},{10... | collective-permute-start | bytes 1572872 | tf_op jit(solution)/shard_map/ppermute | solution.py:245
  1188.0 104.3 %all-gather.14.cloned.1.call-start = ((), (), s32[]{:S(2)}) async-start(), calls=%async_computation.9 | async-start | bytes 4718592 | tf_op jit(solution)/shard_map/all_gather | solution.py:602
  1220.7 18.9 collective-permute-start.14
  1242.8 122.2 %reduce-scatter.15.cloned.1.call-start = ((), (), s32[]{:S(2)}) async-start(), calls=%async_computation.10 | async-start | bytes 4718592 | tf_op jit(solution)/shard_map/reduce_scatter | solution.py:607
  1316.5 107.9 %all-gather.16.cloned.1.call-start = ((), (), s32[]{:S(2)}) async-start(), calls=%async_computation.11 | async-start | bytes 4718592 | tf_op jit(solution)/shard_map/all_gather | solution.py:628
  1378.5 121.1 %reduce-scatter.17.cloned.1.call-start = ((), (), s32[]{:S(2)}) async-start(), calls=%async_computation.12 | async-start | bytes 4718592 | tf_op jit(solution)/shard_map/reduce_scatter | solution.py:631
  1451.1 688.3 %reduce-scatter.21.cloned.1.call-start = ((), (), s32[]{:S(2)}) async-start(), calls=%async_computation.14 | async-start | bytes 3276800 | tf_op jit(solution)/shard_map/reduce_scatter | solution.py:762
  1516.3 940.2 %reduce-scatter.23.cloned.1.call-start = ((), (), s32[]{:S(2)}) async-start(), calls=%async_computation.16 | async-start | bytes 21299200
  2059.4 748.6 %all-reduce.9.cloned.1.call-start = ((), (), s32[]{:S(2)}) async-start(), calls=%async_computation.15 | async-start | bytes 1310720 | tf_op jit(solution)/shard_map/psum | solution.py:765
  2060.4 19.8 collective-permute-start.15
  2061.6 24.4 collective-permute-start.16
  2062.8 39.8 %collective-permute-start.17 = (bf16[128,2048]{1,0:T(8,128)(2,1)S(1)}, bf16[128,2048]{1,0:T(8,128)(2,1)}, u32[]{:S(2)}, u32[]{:S(2)}) collective-permute-start(bf16[128,2048]{1,0:T(8,128)(2,1)S(1)} %copy-done.61), channel_id=1, source_target_pairs={{0,24},{8,16},{16,8},{24,0},{1,25},{9,17},{17,9},{25,1},{2,26},{10... | collective-permute-start | bytes 1572872 | tf_op jit(solution)/shard_map/ppermute | solution.py:245
  2139.4 674.7 %reduce-scatter.19.cloned.1.call-start = ((), (), s32[]{:S(2)}) async-start(), calls=%async_computation.13 | async-start | bytes 11501568 | tf_op jit(solution)/shard_map/reduce_scatter | solution.py:714
  2616.6 28.7 collective-permute-start.23
  2617.8 103.9 %collective-permute-start.24 = (bf16[37,128,128]{2,1,0:T(8,128)(2,1)S(1)}, bf16[37,128,128]{2,1,0:T(8,128)(2,1)S(1)}, u32[]{:S(2)}, u32[]{:S(2)}) collective-permute-start(bf16[37,128,128]{2,1,0:T(8,128)(2,1)S(1)} %get-tuple-element.542), channel_id=1, source_target_pairs={{0,4},{1,5},{2,6},{3,7},{4,0},{5,1},{6,2},{7,3},{8,12},{9,13},{10,... | collective-permute-start | bytes 3637256 | tf_op jit(solution)/shard_map/ppermute | solution.py:256
  2620.6 103.6 %collective-permute-start.25 = (bf16[37,128,128]{2,1,0:T(8,128)(2,1)S(1)}, bf16[37,128,128]{2,1,0:T(8,128)(2,1)S(1)}, u32[]{:S(2)}, u32[]{:S(2)}) collective-permute-start(bf16[37,128,128]{2,1,0:T(8,128)(2,1)S(1)} %get-tuple-element.541), channel_id=1, source_target_pairs={{0,6},{1,7},{2,0},{3,1},{4,2},{5,3},{6,4},{7,5},{8,14},{9,15},{10,... | collective-permute-start | bytes 3637256 | tf_op jit(solution)/shard_map/ppermute | solution.py:256
  2726.8 183.0 %collective-permute-start.26 = (bf16[148,128,128]{2,1,0:T(8,128)(2,1)}, bf16[148,128,128]{2,1,0:T(8,128)(2,1)}, u32[]{:S(2)}, u32[]{:S(2)}) collective-permute-start(bf16[148,128,128]{2,1,0:T(8,128)(2,1)} %bitcast.72.refs_0_), channel_id=1, source_target_pairs={{0,1},{1,0},{2,3},{3,2},{4,5},{5,4},{6,7},{7,6},{8,9},{9,8},{10,11... | collective-permute-start | bytes 14549000 | tf_op jit(solution)/shard_map/ppermute | solution.py:250
  2729.2 44.5 %collective-permute-start.19 = (bf16[128,2048]{1,0:T(8,128)(2,1)}, bf16[128,2048]{1,0:T(8,128)(2,1)}, u32[]{:S(2)}, u32[]{:S(2)}) collective-permute-start(bf16[128,2048]{1,0:T(8,128)(2,1)} %get-tuple-element.552), channel_id=1, source_target_pairs={{0,8},{8,0},{16,24},{24,16},{1,9},{9,1},{17,25},{25,17},{2,10},{10... | collective-permute-start | bytes 1572872 | tf_op jit(solution)/shard_map/ppermute | solution.py:245
  2730.9 42.8 %collective-permute-start.20 = (bf16[128,2048]{1,0:T(8,128)(2,1)}, bf16[128,2048]{1,0:T(8,128)(2,1)}, u32[]{:S(2)}, u32[]{:S(2)}) collective-permute-start(bf16[128,2048]{1,0:T(8,128)(2,1)} %get-tuple-element.554), channel_id=1, source_target_pairs={{0,16},{8,24},{16,0},{24,8},{1,17},{9,25},{17,1},{25,9},{2,18},{10... | collective-permute-start | bytes 1572872 | tf_op jit(solution)/shard_map/ppermute | solution.py:245
  2731.7 42.0 %collective-permute-start.21 = (bf16[128,2048]{1,0:T(8,128)(2,1)}, bf16[128,2048]{1,0:T(8,128)(2,1)}, u32[]{:S(2)}, u32[]{:S(2)}) collective-permute-start(bf16[128,2048]{1,0:T(8,128)(2,1)} %get-tuple-element.553), channel_id=1, source_target_pairs={{0,24},{8,16},{16,8},{24,0},{1,25},{9,17},{17,9},{25,1},{2,26},{10... | collective-permute-start | bytes 1572872 | tf_op jit(solution)/shard_map/ppermute | solution.py:245
  2882.5 19.5 collective-permute-start.27
  2882.5 19.5 collective-permute-start.28
  2883.1 23.7 collective-permute-start.29
  (171 other events, 7466.5 us)
Sparse Core Ops, SparseCore 0:
  10.4 40.8 all-gather.11
  171.1 96.1 all-gather.7
  581.2 171.3 all-gather.9
  1242.9 49.3 all-gather.13
  1316.6 48.3 reduce-scatter.14
  1378.6 45.6 all-gather.15
  1451.2 48.3 reduce-scatter.16
  1516.4 39.2 reduce-scatter.20
  2059.5 178.4 reduce-scatter.22
  2240.4 54.6 all-reduce.8
  2456.7 105.5 reduce-scatter.18

commit v2 on v1

--- a/solution.py
+++ b/solution.py
@@ -28,7 +28,7 @@
 RATE_GAIN = 0.3
 DECAY = 0.01
 NEGATIVE = -1e30
-HIGHEST = lax.Precision.HIGHEST
+VMEM_BYTES = 32 * 1024 * 1024
 
 
 def rms_norm(value, gain):
@@ -97,27 +97,6 @@
     return jax.nn.gelu(first, approximate=True) * second
 
 
-def rotate_update(grad, master, first, second, left, right, rate):
-    turned = jnp.einsum(
-        "bki,bkj->bij",
-        left,
-        jnp.einsum("bkl,blj->bkj", grad, right, precision=HIGHEST),
-        precision=HIGHEST,
-    )
-    first_new = BETA_ONE * first + (1.0 - BETA_ONE) * turned
-    second_new = BETA_TWO * second + (1.0 - BETA_TWO) * turned * turned
-    correct_one = 1.0 - BETA_ONE**STEP
-    correct_two = 1.0 - BETA_TWO**STEP
-    direction = first_new / correct_one / (jnp.sqrt(second_new / correct_two) + ADAM_EPS)
-    back = jnp.einsum(
-        "bik,bkj->bij",
-        left,
-        jnp.einsum("bkl,bjl->bkj", direction, right, precision=HIGHEST),
-        precision=HIGHEST,
-    )
-    return (master - rate * (back + DECAY * master), first_new, second_new)
-
-
 def room(count, share):
     mean = count * share
     return math.ceil(mean + 3.6 * math.sqrt(mean * (1.0 - share)) + 3.0)
@@ -135,73 +114,103 @@
     return jnp.sum(jnp.where(match, value, 0), axis=-1)
 
 
-def tile_kernel_call(kernel, index, arrays, out_shape):
+def steps_of(count):
+    for steps in range(4, 65):
+        if count % steps == 0 and 16 <= count // steps <= 160:
+            return steps
+    return 2 if count % 2 == 0 else 1
+
+
+def tile_kernel_call(kernel, index, arrays, out_shape, out_specs, steps):
     return pl.pallas_call(
         kernel,
+        grid=(steps,),
         out_shape=out_shape,
         in_specs=[pl.BlockSpec(memory_space=pltpu.SMEM)]
         + [pl.BlockSpec(memory_space=pl.ANY)] * len(arrays),
-        out_specs=jax.tree.map(lambda _: pl.BlockSpec(memory_space=pl.ANY), out_shape),
+        out_specs=out_specs,
         scratch_shapes=[pltpu.SemaphoreType.DMA],
+        compiler_params=pltpu.CompilerParams(vmem_limit_bytes=VMEM_BYTES),
     )(index, *arrays)
+
+
+def start_copy(sources, place, target, sem):
+    start = 0
+    for ref in sources:
+        size = ref.shape[0]
+
+        @pl.when((place >= start) & (place < start + size))
+        def _(ref=ref, start=start):
+            pltpu.make_async_copy(ref.at[place - start], target, sem).start()
+
+        start = start + size
 
 
 def gather_tiles(arrays, index):
     tile = arrays[0].shape[-1]
     count = index.shape[0]
+    steps = steps_of(count)
+    each = count // steps
 
     def kernel(index_ref, *refs):
         sources, out, sem = refs[:-2], refs[-2], refs[-1]
+        base = pl.program_id(0) * each
 
         def step(i, carry):
-            place = index_ref[i]
-            start = 0
-            for ref in sources:
-                size = ref.shape[0]
-
-                @pl.when((place >= start) & (place < start + size))
-                def _(ref=ref, start=start):
-                    pltpu.make_async_copy(ref.at[place - start], out.at[i], sem).start()
-
-                start = start + size
+            start_copy(sources, index_ref[base + i], out.at[i], sem)
             return carry
 
-        lax.fori_loop(0, count, step, 0)
+        lax.fori_loop(0, each, step, 0)
         pltpu.make_async_copy(out, out, sem).wait()
 
     total = sum(array.shape[0] for array in arrays)
-    index = jnp.clip(index, 0, total - 1)
-    out_shape = jax.ShapeDtypeStruct((count, tile, tile), arrays[0].dtype)
-    return tile_kernel_call(kernel, index, arrays, out_shape)
-
-
-def join_tiles(tiles, index, row_blocks, first_columns, second_columns):
-    tile = tiles.shape[-1]
+    return tile_kernel_call(
+        kernel,
+        jnp.clip(index, 0, total - 1),
+        arrays,
+        jax.ShapeDtypeStruct((count, tile, tile), arrays[0].dtype),
+        pl.BlockSpec((each, tile, tile), lambda i: (i, 0, 0)),
+        steps,
+    )
+
+
+def join_tiles(arrays, index, row_blocks, first_columns, second_columns):
+    tile = arrays[0].shape[-1]
     first_count = row_blocks * first_columns
-
-    def kernel(index_ref, source, first, second, sem):
+    steps = 4
+    each = row_blocks // steps
+
+    def kernel(index_ref, *refs):
+        sources, first, second, sem = refs[:-3], refs[-3], refs[-2], refs[-1]
+        base = pl.program_id(0) * each
         for out, start, columns in ((first, 0, first_columns), (second, first_count, second_columns)):
 
-            def step(row, carry, out=out, start=start, columns=columns):
-                for column in range(columns):
-                    place = index_ref[start + row * columns + column]
-                    pltpu.make_async_copy(
-                        source.at[place],
-                        out.at[pl.ds(row * tile, tile), pl.ds(column * tile, tile)],
-                        sem,
-                    ).start()
+            def step(i, carry, out=out, start=start, columns=columns):
+                row = i // columns
+                column = i - row * columns
+                target = out.at[
+                    pl.ds(pl.multiple_of(row * tile, tile), tile),
+                    pl.ds(pl.multiple_of(column * tile, tile), tile),
+                ]
+                start_copy(sources, index_ref[start + base * columns + i], target, sem)
                 return carry
 
-            lax.fori_loop(0, row_blocks, step, 0)
+            lax.fori_loop(0, each * columns, step, 0)
         pltpu.make_async_copy(first, first, sem).wait()
         pltpu.make_async_copy(second, second, sem).wait()
 
-    index = jnp.clip(index, 0, tiles.shape[0] - 1)
-    out_shape = (
-        jax.ShapeDtypeStruct((row_blocks * tile, first_columns * tile), tiles.dtype),
-        jax.ShapeDtypeStruct((row_blocks * tile, second_columns * tile), tiles.dtype),
-    )
-    return tile_kernel_call(kernel, index, [tiles], out_shape)
+    total = sum(array.shape[0] for array in arrays)
+    out_shape = tuple(
+        jax.ShapeDtypeStruct((row_blocks * tile, count * tile), arrays[0].dtype)
+        for count in (first_columns, second_columns)
+    )
+    out_specs = tuple(
+        pl.BlockSpec((each * tile, count * tile), lambda i: (i, 0))
+        for count in (first_columns, second_columns)
+    )
+    return tile_kernel_call(
+        kernel, jnp.clip(index, 0, total - 1), arrays, out_shape, out_specs, steps
+    )
 
 
 def cut_tiles(first, second, index, tile):
@@ -210,10 +219,14 @@
     second_columns = second.shape[1] // tile
     first_count = row_blocks * first_columns
     count = index.shape[0]
+    steps = steps_of(count)
+    each = count // steps
 
     def kernel(index_ref, first_ref, second_ref, out, sem):
+        base = pl.program_id(0) * each
+
         def step(i, carry):
-            place = index_ref[i]
+            place = index_ref[base + i]
 
             def send(ref, local, columns):
                 row = pl.multiple_of((local // columns) * tile, tile)
@@ -232,12 +245,100 @@
 
             return carry
 
-        lax.fori_loop(0, count, step, 0)
+        lax.fori_loop(0, each, step, 0)
         pltpu.make_async_copy(out, out, sem).wait()
 
-    index = jnp.clip(index, 0, first_count + row_blocks * second_columns - 1)
-    out_shape = jax.ShapeDtypeStruct((count, tile, tile), first.dtype)
-    return tile_kernel_call(kernel, index, [first, second], out_shape)
+    return tile_kernel_call(
+        kernel,
+        jnp.clip(index, 0, first_count + row_blocks * second_columns - 1),
+        [first, second],
+        jax.ShapeDtypeStruct((count, tile, tile), first.dtype),
+        pl.BlockSpec((each, tile, tile), lambda i: (i, 0, 0)),
+        steps,
+    )
+
+
+def split_low(value):
+    high = value.astype(jnp.bfloat16)
+    return high, (value - high.astype(jnp.float32)).astype(jnp.bfloat16)
+
+
+def rotate_update(grads, index, master, first, second, left, right, rate):
+    count, tile, _ = master.shape
+    each = 4 if count % 4 == 0 else 1
+    correct_one = 1.0 - BETA_ONE**STEP
+    correct_two = 1.0 - BETA_TWO**STEP
+
+    def product(one, two, dims):
+        return lax.dot_general(one, two, (dims, ((), ())), preferred_element_type=jnp.float32)
+
+    def kernel(index_ref, *refs):
+        sources, refs = refs[: len(grads)], refs[len(grads) :]
+        master_ref, first_ref, second_ref, left_ref, right_ref = refs[:5]
+        master_out, first_out, second_out, held, sem = refs[5:]
+        base = pl.program_id(0) * each
+
+        @pl.when(pl.program_id(0) == 0)
+        def _():
+            def step(i, carry):
+                start_copy(sources, index_ref[i], held.at[i], sem)
+                return carry
+
+            lax.fori_loop(0, count, step, 0)
+            pltpu.make_async_copy(held, held, sem).wait()
+
+        for i in range(each):
+            grad = held[base + i]
+            left_high, left_low = split_low(left_ref[i])
+            right_high, right_low = split_low(right_ref[i])
+            half_turned = product(
+                jnp.concatenate([grad, grad], axis=1),
+                jnp.concatenate([right_high, right_low], axis=0),
+                ((1,), (0,)),
+            )
+            high, low = split_low(half_turned)
+            turned = product(
+                jnp.concatenate([left_high, left_high, left_low], axis=0),
+                jnp.concatenate([high, low, high], axis=0),
+                ((0,), (0,)),
+            )
+            first_new = BETA_ONE * first_ref[i] + (1.0 - BETA_ONE) * turned
+            second_new = BETA_TWO * second_ref[i] + (1.0 - BETA_TWO) * turned * turned
+            direction = first_new / correct_one / (jnp.sqrt(second_new / correct_two) + ADAM_EPS)
+            high, low = split_low(direction)
+            half_back = product(
+                jnp.concatenate([high, low, high], axis=1),
+                jnp.concatenate([right_high, right_high, right_low], axis=1),
+                ((1,), (1,)),
+            )
+            high, low = split_low(half_back)
+            back = product(
+                jnp.concatenate([left_high, left_high, left_low], axis=1),
+                jnp.concatenate([high, low, high], axis=0),
+                ((1,), (0,)),
+            )
+            weight = master_ref[i]
+            master_out[i] = weight - rate * (back + DECAY * weight)
+            first_out[i] = first_new
+            second_out[i] = second_new
+
+    spec = pl.BlockSpec((each, tile, tile), lambda i: (i, 0, 0))
+    shape = jax.ShapeDtypeStruct(master.shape, jnp.float32)
+    total = sum(array.shape[0] for array in grads)
+    return pl.pallas_call(
+        kernel,
+        grid=(count // each,),
+        out_shape=(shape, shape, shape),
+        in_specs=[pl.BlockSpec(memory_space=pltpu.SMEM)]
+        + [pl.BlockSpec(memory_space=pl.ANY)] * len(grads)
+        + [spec] * 5,
+        out_specs=(spec, spec, spec),
+        scratch_shapes=[
+            pltpu.VMEM((count, tile, tile), jnp.bfloat16),
+            pltpu.SemaphoreType.DMA,
+        ],
+        compiler_params=pltpu.CompilerParams(vmem_limit_bytes=VMEM_BYTES),
+    )(jnp.clip(index, 0, total - 1), *grads, master, first, second, left, right)
 
 
 def seq_swap(value, flip):
@@ -263,27 +364,50 @@
     return jnp.concatenate([value] + [seq_swap(value, flip) for flip in range(1, size)], axis=0)
 
 
-def seq_exchange(value):
+def seq_ordered(value):
     size = lax.axis_size("seq")
-    parts = [value[0]] + [seq_swap(value[flip], flip) for flip in range(1, size)]
-    return jnp.stack(parts, axis=0)
-
-
-def seq_sum(value):
+    parts = jnp.stack([value] + [seq_swap(value, flip) for flip in range(1, size)], axis=0)
+    return parts[lax.axis_index("seq") ^ jnp.arange(size)]
+
+
+def seq_exchange(values):
+    return [values[0]] + [seq_swap(values[flip], flip) for flip in range(1, len(values))]
+
+
+def seq_sum(value, wire, ordered=False):
     size = lax.axis_size("seq")
-    rows = value.shape[0] // size
-    parts = value.reshape(size, rows, value.shape[1])
-    low = parts.astype(jnp.bfloat16)
+    parts = value.reshape((size, value.shape[0] // size) + value.shape[1:])
+    if ordered:
+        parts = parts[lax.axis_index("seq") ^ jnp.arange(size)]
     total = parts[0]
     for flip in range(1, size):
-        total = total + seq_swap(low[flip], flip).astype(jnp.float32)
+        total = total + seq_swap(parts[flip].astype(wire), flip).astype(jnp.float32)
     return total
 
 
-def chip_exchange(value):
-    chips = value.shape[0]
-    parts = [value[0]] + [chip_shift(value[offset], offset) for offset in range(1, chips)]
-    return jnp.stack(parts, axis=0)
+def chip_exchange(values):
+    return [values[0]] + [chip_shift(values[offset], offset) for offset in range(1, len(values))]
+
+
+def fsdp_sum(value):
+    size = lax.axis_size("fsdp")
+    chips = size // 2
+    chip = lax.axis_index("fsdp") // 2
+    even = lax.axis_index("fsdp") % 2 == 0
+    shares = value.reshape((chips, 2, value.shape[0] // size) + value.shape[1:])
+    kept = jnp.where(even, shares[:, 0], shares[:, 1])
+    given = jnp.where(even, shares[:, 1], shares[:, 0])
+    kept = kept + core_swap(given.astype(jnp.bfloat16)).astype(jnp.float32)
+    kept = kept[(chip + jnp.arange(chips)) % chips]
+    total = kept[0]
+    for offset in range(1, chips):
+        total = total + chip_shift(kept[offset].astype(jnp.bfloat16), offset).astype(jnp.float32)
+    total = total.astype(jnp.bfloat16)
+    parts = jnp.stack([total] + [chip_shift(total, offset) for offset in range(1, chips)])
+    parts = parts[(chip - jnp.arange(chips)) % chips]
+    other = core_swap(parts)
+    both = jnp.where(even, jnp.stack([parts, other], axis=1), jnp.stack([other, parts], axis=1))
+    return both.reshape(value.shape)
 
 
 def on_device(
@@ -345,7 +469,8 @@
     attn_room = room(mine, attn_share / seq_size)
     attn_hold = room(attn_count, 1.0 / fsdp_size)
     ffn_room = (room(2 * mine, ffn_share / chips) + 1) // 2
-    ffn_hold = room(ffn_count, 1.0 / seq_size)
+    ffn_half = (room(ffn_count, 1.0 / seq_size) + 3) // 4 * 2
+    ffn_hold = 2 * ffn_half
 
     def tile_places(owner):
         row = owner // columns
@@ -465,7 +590,7 @@
             my_chip_slots[1][None, None, :]
             == (my_core * ffn_room + jnp.arange(ffn_room))[None, :, None]
         ),
-        jnp.arange(2 * mine) ^ 0,
+        jnp.arange(2 * mine),
     )
     ffn_pack = jnp.where(
         ffn_pack // mine == my_core, ffn_pack % mine, mine + ffn_pack % mine
@@ -477,21 +602,25 @@
     ffn_join = pick(
         (ffn_to.reshape(1, -1) == my_fsdp)
         & (ffn_place.reshape(1, -1) == jnp.arange(ffn_count)[:, None]),
-        (slot_seq * ffn_hold + ffn_rank).reshape(1, -1),
+        ((slot_seq ^ my_seq) * ffn_hold + ffn_rank).reshape(1, -1),
     )
     master_low = tile_master.astype(bf16)
-    attn_sent = gather_tiles([master_low], attn_pack.reshape(-1))
-    attn_got = seq_exchange(attn_sent.reshape(seq_size, attn_room, tile, tile))
-    attn_kept = gather_tiles([attn_got.reshape(-1, tile, tile)], attn_keep)
+    attn_sent = gather_tiles([master_low], attn_pack.reshape(-1)).reshape(seq_size, attn_room, tile, tile)
+    attn_got = seq_exchange([attn_sent[i] for i in range(seq_size)])
+    attn_kept = gather_tiles(attn_got, attn_keep)
+
+    master_other = core_swap(master_low)
+    ffn_sent = [gather_tiles([master_low, master_other], ffn_pack[i]) for i in range(chips)]
+    ffn_got = chip_exchange(ffn_sent)
+    ffn_other = [core_swap(value) for value in ffn_got]
+    kept_one = gather_tiles(ffn_got + ffn_other, ffn_keep[:ffn_half])
+    kept_two = gather_tiles(ffn_got + ffn_other, ffn_keep[ffn_half:])
     attn_all = lax.all_gather(attn_kept, "fsdp", axis=0, tiled=True)
-    w_first, w_out = join_tiles(attn_all, attn_join, row_blocks, attn_first, query_each)
-
-    master_other = core_swap(master_low)
-    ffn_sent = gather_tiles([master_low, master_other], ffn_pack.reshape(-1))
-    ffn_got = chip_exchange(ffn_sent.reshape(chips, ffn_room, tile, tile)).reshape(-1, tile, tile)
-    ffn_other = core_swap(ffn_got)
-    ffn_kept = gather_tiles([ffn_got, ffn_other], ffn_keep)
-    ffn_all = lax.all_gather(ffn_kept, "seq", axis=0, tiled=True)
+    w_first, w_out = join_tiles([attn_all], attn_join, row_blocks, attn_first, query_each)
+    one_x, two_y = seq_swap(kept_one, 1), seq_swap(kept_two, 2)
+    two_x, one_y = seq_swap(kept_two, 1), seq_swap(kept_one, 2)
+    one_xy, two_xy = seq_swap(one_x, 2), seq_swap(two_y, 1)
+    ffn_all = [kept_one, kept_two, one_x, two_x, one_y, two_y, one_xy, two_xy]
     w_both, w_down = join_tiles(ffn_all, ffn_join, row_blocks, ffn_first, ffn_each)
 
     my_columns = jnp.arange(tiles)
@@ -508,8 +637,8 @@
             & (ffn_place.reshape(1, -1) == jnp.arange(ffn_count)[:, None]),
             slots,
         )
-        return join_tiles(whole, attn_slots, row_blocks, attn_first, query_each) + join_tiles(
-            whole, ffn_slots, row_blocks, ffn_first, ffn_each
+        return join_tiles([whole], attn_slots, row_blocks, attn_first, query_each) + join_tiles(
+            [whole], ffn_slots, row_blocks, ffn_first, ffn_each
         )
 
     slow_steps = jnp.where(fits, 0, 1)
@@ -517,12 +646,9 @@
         0, slow_steps, slow_fetch, (w_first, w_out, w_both, w_down)
     )
 
-    small_got, gain_got = (
-        lax.all_gather(small_master.astype(bf16), "seq", axis=0, tiled=True),
-        lax.all_gather(gains.astype(bf16), "seq", axis=0, tiled=True),
-    )
-    small_table = assemble(small_got, row_blocks)
-    gain_full = gain_got.astype(f32)
+    small_got = seq_ordered(small_master.astype(bf16))
+    small_table = assemble(small_got.reshape((-1,) + small_master.shape[1:]), row_blocks)
+    gain_full = seq_ordered(gains.astype(bf16)).reshape(-1).astype(f32)
     gain_in = gain_full[0:width]
     gain_attn = gain_full[width : 2 * width]
     gain_laurel = gain_full[2 * width : 3 * width]
@@ -590,7 +716,7 @@
         .astype(bf16)
         .reshape(length, per_device * HEAD_DIM)
     )
-    attn_pre = seq_sum(matmul_flip(attended_low, w_out))
+    attn_pre = seq_sum(matmul_flip(attended_low, w_out), bf16)
     attn_normed, attn_pull = jax.vjp(rms_norm, attn_pre, gain_attn)
     first_sum = stream + attn_normed
     left_pre = matmul(normed_low, laurel_left)
@@ -671,15 +797,16 @@
     grad_normed = (
         half_grad
         + matmul_flip(left_grad_low, laurel_left)
-        + seq_sum(matmul_flip(first_grad_low, w_first))
+        + seq_sum(matmul_flip(first_grad_low, w_first), bf16)
     )
     grad_stream_norm, grad_gain_in = normed_pull(grad_normed)
     input_grad = (half_grad + grad_stream_norm)[None]
 
+    flip_to = ffn_to.reshape(seq_size, 1, -1)[my_seq ^ flips]
+    flip_rank = ffn_rank.reshape(seq_size, 1, -1)[my_seq ^ flips]
+    flip_place = ffn_place.reshape(seq_size, 1, -1)[my_seq ^ flips]
     ffn_cut = pick(
-        (ffn_to.reshape(seq_size, 1, -1) == my_fsdp)
-        & (ffn_rank.reshape(seq_size, 1, -1) == jnp.arange(ffn_hold)[None, :, None]),
-        ffn_place.reshape(seq_size, 1, -1),
+        (flip_to == my_fsdp) & (flip_rank == jnp.arange(ffn_hold)[None, :, None]), flip_place
     )
     ffn_back = pick(
         (seq_slots[5][None, None, :] == ((my_chip + shifts) % chips)[:, None, None])
@@ -688,13 +815,21 @@
         & (seq_slots[4][None, None, :] == (my_core * ffn_room + jnp.arange(ffn_room))[None, :, None]),
         jnp.where(seq_slots[0] == my_fsdp, 0, ffn_hold) + seq_slots[1],
     )
-    ffn_parts = cut_tiles(both_grad_w, down_grad_w, ffn_cut.reshape(-1), tile)
-    ffn_sum = lax.psum_scatter(ffn_parts, "seq", scatter_dimension=0, tiled=True)
-    ffn_sum_other = core_swap(ffn_sum)
-    ffn_return = gather_tiles([ffn_sum, ffn_sum_other], ffn_back.reshape(-1))
-    ffn_returned = chip_exchange(ffn_return.reshape(chips, ffn_room, tile, tile))
-    ffn_returned = ffn_returned.reshape(-1, tile, tile)
-    ffn_returned_other = core_swap(ffn_returned)
+
+    def ffn_parts(flips_of, half):
+        index = ffn_cut[:, half * ffn_half : (half + 1) * ffn_half][jnp.array(flips_of)]
+        return cut_tiles(both_grad_w, down_grad_w, index.reshape(-1), tile)
+
+    def added(one, two):
+        return one.astype(f32) + two.astype(f32)
+
+    one_sum = added(ffn_parts([0, 2], 0), seq_swap(ffn_parts([1, 3], 0), 1))
+    two_sum = added(ffn_parts([0, 1], 1), seq_swap(ffn_parts([2, 3], 1), 2))
+    one_sum = added(one_sum[:ffn_half], seq_swap(one_sum[ffn_half:].astype(bf16), 2)).astype(bf16)
+    two_sum = added(two_sum[:ffn_half], seq_swap(two_sum[ffn_half:].astype(bf16), 1)).astype(bf16)
+    ffn_sums = [one_sum, two_sum, core_swap(one_sum), core_swap(two_sum)]
+    ffn_returned = chip_exchange([gather_tiles(ffn_sums, ffn_back[i]) for i in range(chips)])
+    ffn_returned = ffn_returned + [core_swap(value) for value in ffn_returned]
 
     attn_cut = pick(
         (attn_to.transpose(1, 0, 2).reshape(fsdp_size, 1, -1) == my_seq)
@@ -712,21 +847,17 @@
     )
     attn_parts = cut_tiles(first_grad_w, out_grad_w, attn_cut.reshape(-1), tile)
     attn_sum = lax.psum_scatter(attn_parts, "fsdp", scatter_dimension=0, tiled=True)
-    attn_return = gather_tiles([attn_sum], attn_back.reshape(-1))
-    attn_returned = seq_exchange(attn_return.reshape(seq_size, attn_room, tile, tile))
+    attn_returned = seq_exchange([gather_tiles([attn_sum], attn_back[i]) for i in range(seq_size)])
     slot_grad = jnp.where(
         my_slots[0] >= 0,
         my_slots[3],
         2 * half + (my_slots[1] ^ my_seq) * attn_room + my_slots[2],
     )
-    tile_grad_low = gather_tiles(
-        [ffn_returned, ffn_returned_other, attn_returned.reshape(-1, tile, tile)], slot_grad
-    )
 
     def slow_return(_, kept):
-        ffn_parts = split_tiles(both_grad_w, tile), split_tiles(down_grad_w, tile)
-        attn_parts = split_tiles(first_grad_w, tile), split_tiles(out_grad_w, tile)
-        parts = jnp.concatenate(ffn_parts + attn_parts + (jnp.zeros((1, tile, tile), bf16),))
+        own_ffn = split_tiles(both_grad_w, tile), split_tiles(down_grad_w, tile)
+        own_attn = split_tiles(first_grad_w, tile), split_tiles(out_grad_w, tile)
+        parts = jnp.concatenate(own_ffn + own_attn + (jnp.zeros((1, tile, tile), bf16),))
         index = jnp.where(
             ffn_to == my_fsdp,
             ffn_place,
@@ -735,7 +866,11 @@
         spread = gather_tiles([parts], index.reshape(-1))
         return lax.psum_scatter(spread, ("seq", "fsdp"), scatter_dimension=0, tiled=True)
 
-    tile_grad = lax.fori_loop(0, slow_steps, slow_return, tile_grad_low).astype(f32)
+    tile_grads = ffn_returned + attn_returned
+    slow_start = 2 * half + seq_size * attn_room
+    slow_grads = lax.fori_loop(0, slow_steps, slow_return, jnp.zeros((mine, tile, tile), bf16))
+    tile_grads = tile_grads + [slow_grads]
+    slot_grad = jnp.where(fits, slot_grad, slow_start + local_slots)
 
     small_full = jnp.concatenate(
         [
@@ -759,17 +894,25 @@
             grad_gain_key,
         ]
     )
-    small_part = lax.psum_scatter(
-        small_tiles_grad.astype(bf16), "seq", scatter_dimension=0, tiled=True
-    )
-    small_grad = lax.psum(small_part, "fsdp").astype(f32)
-    whole_gain = lax.psum(gain_grad.astype(bf16), "fsdp")
-    gain_grad_mine = lax.psum_scatter(whole_gain, "seq", scatter_dimension=0, tiled=True).astype(f32)
+    small_part = seq_sum(small_tiles_grad, bf16, True)
+    small_grad = fsdp_sum(small_part.reshape(-1, tile)).reshape(small_part.shape)
+    gain_part = seq_sum(gain_grad, f32, True)
+    gain_part = gain_part + core_swap(gain_part)
+    gain_grad_mine = gain_part
+    for offset in range(1, chips):
+        gain_grad_mine = gain_grad_mine + chip_shift(gain_part, offset)
     tile_new, tile_first_new, tile_second_new = rotate_update(
-        tile_grad, tile_master, tile_first, tile_second, left_basis, right_basis, RATE_TILE
+        tile_grads, slot_grad, tile_master, tile_first, tile_second, left_basis, right_basis, RATE_TILE
     )
     small_new, small_first_new, small_second_new = rotate_update(
-        small_grad, small_master, small_first, small_second, small_left, small_right, RATE_SMALL
+        [small_grad],
+        jnp.arange(small_master.shape[0]),
+        small_master,
+        small_first,
+        small_second,
+        small_left,
+        small_right,
+        RATE_SMALL,
     )
     gain_first_new = BETA_ONE * gain_first + (1.0 - BETA_ONE) * gain_grad_mine
     gain_second_new = BETA_TWO * gain_second + (1.0 - BETA_TWO) * gain_grad_mine * gain_grad_mine

time: 3150 us -> 1470 us (0.47)
  Pallas kernels: 2090 us -> 210 us
  waiting for transfers between devices: 493 us -> 818 us
  matrix products: 202 us -> 102 us
  blocking collectives: 61.5 us -> 0 us
  starting transfers between devices: 31.8 us -> 82.8 us
    pallas_call x11 -> x25, Pallas kernels: 2090 us -> 210 us  [the longest x23 125 us: tile_kernel_call(): pl.pallas_call(kernel, grid=(steps,), out_shape=out_shape, in_specs=[pl.B...]
    ppermute x20 -> x42, waiting for transfers between devices: 88.1 us -> 386 us  [seq_swap(): return lax.ppermute(value, 'seq', [(i, i ^ flip) for i in range(size)])]
    dot_general x8 -> x0, matrix products: 86.4 us -> none  [the longest x2 27.7 us: rotate_update(): jnp.einsum('bik,bkj->bij', left, jnp.einsum('bkl,bjl->bkj', direction, ri...]
    unnamed x352 -> x363, local copies, waits for them, and re-layouts: 89.6 us -> 41.7 us
    all_gather x1 -> x0, blocking collectives: 34.6 us -> none  [on_device(): lax.all_gather(gains.astype(bf16), 'seq', axis=0, tiled=True)]
    ppermute x6 -> x15, waiting for transfers between devices: 203 us -> 236 us  [chip_shift(): lax.ppermute(value, 'fsdp', [(i, (i // 2 + offset) % chips * 2 + i % 2) f...]
  transfers between devices with their start and end apart: 41 -> 77, of which waited for: 25 -> 35; matrix products, arithmetic and copies ran while one was open for 7% -> 11% of each run, Pallas kernels for 51% -> 8%
where the time goes in v2:
time: 1470 us; the launch traced here: 1450 us
  waiting for transfers between devices  818 us (56%)
  Pallas kernels  210 us (14%)
  other arithmetic  113 us (8%)
  local copies, waits for them, and re-layouts  106 us (7%)
  matrix products  102 us (7%)
  starting transfers between devices  82.8 us (6%)
  between operations  17.9 us (1%)
    ppermute x42, waiting for transfers between devices, seq_swap(): return lax.ppermute(value, 'seq', [(i, i ^ flip) for i in range(size)])  386 us
    ppermute x15, waiting for transfers between devices, chip_shift(): lax.ppermute(value, 'fsdp', [(i, (i // 2 + offset) % chips * 2 + i % 2) f...  236 us
    pallas_call x23, Pallas kernels, tile_kernel_call(): pl.pallas_call(kernel, grid=(steps,), out_shape=out_shape, in_specs=[pl.B...  125 us
    pallas_call x2, Pallas kernels, rotate_update(): pl.pallas_call(kernel, grid=(count // each,), out_shape=(shape, shape, sh...  85 us
    all_gather x1, waiting for transfers between devices, on_device(): lax.all_gather(feed_normed.astype(bf16), 'fsdp', axis=0, tiled=True)  54.9 us
    reduce_scatter x1, waiting for transfers between devices, on_device(): lax.psum_scatter(matmul_flip(hidden_low, w_down).astype(bf16), 'fsdp', sc...  48.4 us
    reduce_scatter x1, waiting for transfers between devices, on_device(): lax.psum_scatter(matmul_flip(both_grad_low, w_both).astype(bf16), 'fsdp',...  46.4 us
    all_gather x1, waiting for transfers between devices, on_device(): lax.all_gather(grad_down.astype(bf16), 'fsdp', axis=0, tiled=True)  45.5 us
  transfers between devices with their start and end apart: 77, of which 35 were waited for; matrix products, arithmetic and copies ran while one was open for 11% of the time, Pallas kernels for 8%

profile of v2, /device:TPU:9, one launch (start us, length us, event | category | flops | bytes accessed | tf_op | source)
XLA Modules:
  0.0 1449.9 jit_solution(11282212261437186132)
XLA Ops:
  11.1 9.2 convert_reduce_fusion.3
  48.3 12.2 collective-permute-done.7.refs_2_
  96.3 92.1 %collective-permute-done.10.refs_1_ = bf16[37,128,128]{2,1,0:T(8,128)(2,1)S(1)} collective-permute-done((bf16[37,128,128]{2,1,0:T(8,128)(2,1)}, bf16[37,128,128]{2,1,0:T(8,128)(2,1)S(1)}, u32[]{:S(2)}, u32[]{:S(2)}) %collective-permute-start.10) | collective-permute-done | bytes 1212448 | tf_op jit(solution)/shard_map/ppermute | solution.py:357
  189.9 71.1 %collective-permute-done.11.refs_2_ = bf16[37,128,128]{2,1,0:T(8,128)(2,1)S(1)} collective-permute-done((bf16[37,128,128]{2,1,0:T(8,128)(2,1)}, bf16[37,128,128]{2,1,0:T(8,128)(2,1)S(1)}, u32[]{:S(2)}, u32[]{:S(2)}) %collective-permute-start.11) | collective-permute-done | bytes 1212448 | tf_op jit(solution)/shard_map/ppermute | solution.py:357
  278.4 7.9 shard_map.301.refs_1_
  295.9 40.8 %collective-permute-done.2 = bf16[128,2048]{1,0:T(8,128)(2,1)} collective-permute-done((bf16[128,2048]{1,0:T(8,128)(2,1)}, bf16[128,2048]{1,0:T(8,128)(2,1)}, u32[]{:S(2)}, u32[]{:S(2)}) %collective-permute-start.2) | collective-permute-done | bytes 524320 | tf_op jit(solution)/shard_map/ppermute | solution.py:346
  338.6 17.8 %collective-permute-done.1 = bf16[128,2048]{1,0:T(8,128)(2,1)} collective-permute-done((bf16[128,2048]{1,0:T(8,128)(2,1)}, bf16[128,2048]{1,0:T(8,128)(2,1)}, u32[]{:S(2)}, u32[]{:S(2)}) %collective-permute-start.1) | collective-permute-done | bytes 524320 | tf_op jit(solution)/shard_map/ppermute | solution.py:346
  373.5 90.2 %collective-permute-done.27 = bf16[20,128,128]{2,1,0:T(8,128)(2,1)S(1)} collective-permute-done((bf16[20,128,128]{2,1,0:T(8,128)(2,1)}, bf16[20,128,128]{2,1,0:T(8,128)(2,1)S(1)}, u32[]{:S(2)}, u32[]{:S(2)}) %collective-permute-start.27) | collective-permute-done | bytes 655392 | tf_op jit(solution)/shard_map/ppermute | solution.py:346
  468.7 8.6 collective-permute-done.29
  493.2 19.0 %shard_map.302 = (bf16[2048,2048]{1,0:T(8,128)(2,1)}, bf16[2048,1024]{1,0:T(8,128)(2,1)}) custom-call(s32[384]{0:T(512)S(1)} %broadcast_clamp_fusion.3.index_ref, bf16[66,128,128]{2,1,0:T(8,128)(2,1)S(1)} %shard_map.300.refs_0_, bf16[66,128,128]{2,1,0:T(8,128)(2,1)} %shard_map.301.refs_1_, bf16[66,128,128]{2,1,0:T(8,128)(2,1)} %collective-permute-done.17.refs_2_, ...), custom_call_target="tpu_custom_call" | custom-call | tf_op jit(solution)/shard_map/pallas_call | solution.py:125
  551.0 10.2 collective-permute-done.26
  566.1 54.9 %all-gather.7.cloned.1.call-done = bf16[1024,2048]{1,0:T(8,128)(2,1)} async-done(((bf16[128,2048]{1,0:T(8,128)(2,1)}), bf16[1024,2048]{1,0:T(8,128)(2,1)}) %all-gather.7.cloned.1.call-update) | async-done | bytes 4194320 | tf_op jit(solution)/shard_map/all_gather | solution.py:728
  621.0 12.5 fusion.322
  645.2 48.4 %reduce-scatter.11.cloned.1.call-done = bf16[128,2048]{1,0:T(8,128)(2,1)} async-done(((bf16[1024,2048]{1,0:T(8,128)(2,1)}), bf16[128,2048]{1,0:T(8,128)(2,1)}) %reduce-scatter.11.cloned.1.call-update) | async-done | bytes 524304 | tf_op jit(solution)/shard_map/reduce_scatter | solution.py:733
  705.9 45.5 %all-gather.9.cloned.1.call-done = bf16[1024,2048]{1,0:T(8,128)(2,1)} async-done(((bf16[128,2048]{1,0:T(8,128)(2,1)}), bf16[1024,2048]{1,0:T(8,128)(2,1)}) %all-gather.9.cloned.1.call-update) | async-done | bytes 4194320 | tf_op jit(solution)/shard_map/all_gather | solution.py:754
  751.4 12.1 fusion.13
  765.5 12.6 convolution_convert_fusion.1
  780.1 46.4 %reduce-scatter.13.cloned.1.call-done = bf16[128,2048]{1,0:T(8,128)(2,1)} async-done(((bf16[1024,2048]{1,0:T(8,128)(2,1)}), bf16[128,2048]{1,0:T(8,128)(2,1)}) %reduce-scatter.13.cloned.1.call-update) | async-done | bytes 524304 | tf_op jit(solution)/shard_map/reduce_scatter | solution.py:757
  838.4 10.8 collective-permute-done.32
  849.3 10.2 collective-permute-done.31
  887.9 11.6 shard_map.311
  911.5 8.0 convolution_convert_fusion.2.second_ref
  919.5 9.8 convolution_convert_fusion.first_ref
  938.7 12.6 shard_map.306
  961.5 69.3 %collective-permute-done.37 = bf16[132,128,128]{2,1,0:T(8,128)(2,1)} collective-permute-done((bf16[132,128,128]{2,1,0:T(8,128)(2,1)}, bf16[132,128,128]{2,1,0:T(8,128)(2,1)}, u32[]{:S(2)}, u32[]{:S(2)}) %collective-permute-start.37) | collective-permute-done | bytes 4325408 | tf_op jit(solution)/shard_map/ppermute | solution.py:346
  1058.4 35.2 %collective-permute-done.38 = bf16[66,128,128]{2,1,0:T(8,128)(2,1)} collective-permute-done((bf16[66,128,128]{2,1,0:T(8,128)(2,1)}, bf16[66,128,128]{2,1,0:T(8,128)(2,1)}, u32[]{:S(2)}, u32[]{:S(2)}) %collective-permute-start.38) | collective-permute-done | bytes 2162720 | tf_op jit(solution)/shard_map/ppermute | solution.py:346
  1138.6 15.3 %collective-permute-done.55 = bf16[20,128,128]{2,1,0:T(8,128)(2,1)} collective-permute-done((bf16[20,128,128]{2,1,0:T(8,128)(2,1)}, bf16[20,128,128]{2,1,0:T(8,128)(2,1)}, u32[]{:S(2)}, u32[]{:S(2)}) %collective-permute-start.55) | collective-permute-done | bytes 655392 | tf_op jit(solution)/shard_map/ppermute | solution.py:346
  1177.4 11.0 collective-permute-done.36
  1238.2 68.5 %collective-permute-done.69 = f32[3200]{0:T(1024)S(1)} collective-permute-done((f32[3200]{0:T(1024)S(1)}, f32[3200]{0:T(1024)S(1)}, u32[]{:S(2)}, u32[]{:S(2)}) %collective-permute-start.69) | collective-permute-done | bytes 12832 | tf_op jit(solution)/shard_map/ppermute | solution.py:357
  1319.5 13.3 shard_map.317
  1350.7 17.2 %collective-permute-done.51.refs_10_ = bf16[16,128,128]{2,1,0:T(8,128)(2,1)} collective-permute-done((bf16[16,128,128]{2,1,0:T(8,128)(2,1)}, bf16[16,128,128]{2,1,0:T(8,128)(2,1)}, u32[]{:S(2)}, u32[]{:S(2)}) %collective-permute-start.51) | collective-permute-done | bytes 524320 | tf_op jit(solution)/shard_map/ppermute | solution.py:346
  1371.1 71.8 %shard_map.316 = (f32[116,128,128]{2,1,0:T(8,128)}, f32[116,128,128]{2,1,0:T(8,128)}, f32[116,128,128]{2,1,0:T(8,128)}) custom-call(s32[116]{0:T(128)S(1)} %fusion.261.index_ref, bf16[37,128,128]{2,1,0:T(8,128)(2,1)S(1)} %copy-done.15, bf16[37,128,128]{2,1,0:T(8,128)(2,1)} %collective-permute-done.43.refs_1_, ...), custom_call_target="tpu_custom_call" | custom-call | tf_op jit(solution)/shard_map/pallas_call | solution.py:328
  (808 shorter events, 455.8 us)
Async XLA Ops:
  7.2 505.0 %all-gather.5.cloned.1.call-start = ((), (), s32[]{:S(2)}) async-start(), calls=%async_computation.4 | async-start | bytes 11501568 | tf_op jit(solution)/shard_map/all_gather | solution.py:618
  66.3 224.4 %collective-permute-start.5 = (bf16[3200]{0:T(1024)(128)(2,1)}, bf16[3200]{0:T(1024)(128)(2,1)}, u32[]{:S(2)}, u32[]{:S(2)}) collective-permute-start(bf16[3200]{0:T(1024)(128)(2,1)} %convert_element_type.278), channel_id=1, source_target_pairs={{0,24},{8,16},{16,8},{24,0},{1,25},{9,17},{17,9},{25,1},{2,26},{10... | collective-permute-start | bytes 19208 | tf_op jit(solution)/shard_map/ppermute | solution.py:346
  75.8 112.6 %collective-permute-start.10 = (bf16[37,128,128]{2,1,0:T(8,128)(2,1)}, bf16[37,128,128]{2,1,0:T(8,128)(2,1)S(1)}, u32[]{:S(2)}, u32[]{:S(2)}) collective-permute-start(bf16[37,128,128]{2,1,0:T(8,128)(2,1)} %shard_map.297), channel_id=1, source_target_pairs={{0,2},{1,3},{2,4},{3,5},{4,6},{5,7},{6,0},{7,1},{8,10},{9,11},{10,... | collective-permute-start | bytes 3637256 | tf_op jit(solution)/shard_map/ppermute | solution.py:357
  81.1 179.9 %collective-permute-start.11 = (bf16[37,128,128]{2,1,0:T(8,128)(2,1)}, bf16[37,128,128]{2,1,0:T(8,128)(2,1)S(1)}, u32[]{:S(2)}, u32[]{:S(2)}) collective-permute-start(bf16[37,128,128]{2,1,0:T(8,128)(2,1)} %shard_map.298), channel_id=1, source_target_pairs={{0,4},{1,5},{2,6},{3,7},{4,0},{5,1},{6,2},{7,3},{8,12},{9,13},{10,... | collective-permute-start | bytes 3637256 | tf_op jit(solution)/shard_map/ppermute | solution.py:357
  86.0 177.8 %collective-permute-start.12 = (bf16[37,128,128]{2,1,0:T(8,128)(2,1)}, bf16[37,128,128]{2,1,0:T(8,128)(2,1)}, u32[]{:S(2)}, u32[]{:S(2)}) collective-permute-start(bf16[37,128,128]{2,1,0:T(8,128)(2,1)} %shard_map.299), channel_id=1, source_target_pairs={{0,6},{1,7},{2,0},{3,1},{4,2},{5,3},{6,4},{7,5},{8,14},{9,15},{10,... | collective-permute-start | bytes 3637256 | tf_op jit(solution)/shard_map/ppermute | solution.py:357
  96.0 170.4 %collective-permute-start.13 = (bf16[37,128,128]{2,1,0:T(8,128)(2,1)S(1)}, bf16[37,128,128]{2,1,0:T(8,128)(2,1)S(1)}, u32[]{:S(2)}, u32[]{:S(2)}) collective-permute-start(bf16[37,128,128]{2,1,0:T(8,128)(2,1)S(1)} %shard_map.296.refs_0_), channel_id=1, source_target_pairs={{0,1},{1,0},{2,3},{3,2},{4,5},{5,4},{6,7},{7,6},{8,9},{9,8},{10,11... | collective-permute-start | bytes 3637256 | tf_op jit(solution)/shard_map/ppermute | solution.py:351
  188.4 79.2 %collective-permute-start.14 = (bf16[37,128,128]{2,1,0:T(8,128)(2,1)S(1)}, bf16[37,128,128]{2,1,0:T(8,128)(2,1)S(1)}, u32[]{:S(2)}, u32[]{:S(2)}) collective-permute-start(bf16[37,128,128]{2,1,0:T(8,128)(2,1)S(1)} %collective-permute-done.10.refs_1_), channel_id=1, source_target_pairs={{0,1},{1,0},{2,3},{3,2},{4,5},{5,4},{6,7},{7,6},{8,9},{9,8},{10,11... | collective-permute-start | bytes 3637256 | tf_op jit(solution)/shard_map/ppermute | solution.py:351
  276.7 82.2 %collective-permute-start.17 = (bf16[66,128,128]{2,1,0:T(8,128)(2,1)S(1)}, bf16[66,128,128]{2,1,0:T(8,128)(2,1)}, u32[]{:S(2)}, u32[]{:S(2)}) collective-permute-start(bf16[66,128,128]{2,1,0:T(8,128)(2,1)S(1)} %shard_map.300.refs_0_), channel_id=1, source_target_pairs={{0,8},{8,0},{16,24},{24,16},{1,9},{9,1},{17,25},{25,17},{2,10},{10... | collective-permute-start | bytes 6488072 | tf_op jit(solution)/shard_map/ppermute | solution.py:346
  286.3 73.2 %collective-permute-start.20 = (bf16[66,128,128]{2,1,0:T(8,128)(2,1)}, bf16[66,128,128]{2,1,0:T(8,128)(2,1)}, u32[]{:S(2)}, u32[]{:S(2)}) collective-permute-start(bf16[66,128,128]{2,1,0:T(8,128)(2,1)} %shard_map.301.refs_1_), channel_id=1, source_target_pairs={{0,16},{8,24},{16,0},{24,8},{1,17},{9,25},{17,1},{25,9},{2,18},{10... | collective-permute-start | bytes 6488072 | tf_op jit(solution)/shard_map/ppermute | solution.py:346
  293.6 62.8 %collective-permute-start.1 = (bf16[128,2048]{1,0:T(8,128)(2,1)}, bf16[128,2048]{1,0:T(8,128)(2,1)}, u32[]{:S(2)}, u32[]{:S(2)}) collective-permute-start(bf16[128,2048]{1,0:T(8,128)(2,1)} %bitcast.8), channel_id=1, source_target_pairs={{0,16},{8,24},{16,0},{24,8},{1,17},{9,25},{17,1},{25,9},{2,18},{10... | collective-permute-start | bytes 1572872 | tf_op jit(solution)/shard_map/ppermute | solution.py:346
  294.2 62.3 %collective-permute-start = (bf16[128,2048]{1,0:T(8,128)(2,1)}, bf16[128,2048]{1,0:T(8,128)(2,1)}, u32[]{:S(2)}, u32[]{:S(2)}) collective-permute-start(bf16[128,2048]{1,0:T(8,128)(2,1)} %bitcast.8), channel_id=1, source_target_pairs={{0,8},{8,0},{16,24},{24,16},{1,9},{9,1},{17,25},{25,17},{2,10},{10... | collective-permute-start | bytes 1572872 | tf_op jit(solution)/shard_map/ppermute | solution.py:346
  356.4 136.7 %collective-permute-start.19 = (bf16[66,128,128]{2,1,0:T(8,128)(2,1)S(1)}, bf16[66,128,128]{2,1,0:T(8,128)(2,1)}, u32[]{:S(2)}, u32[]{:S(2)}) collective-permute-start(bf16[66,128,128]{2,1,0:T(8,128)(2,1)S(1)} %shard_map.300.refs_0_), channel_id=1, source_target_pairs={{0,16},{8,24},{16,0},{24,8},{1,17},{9,25},{17,1},{25,9},{2,18},{10... | collective-permute-start | bytes 6488072 | tf_op jit(solution)/shard_map/ppermute | solution.py:346
  356.6 136.6 %collective-permute-start.18 = (bf16[66,128,128]{2,1,0:T(8,128)(2,1)}, bf16[66,128,128]{2,1,0:T(8,128)(2,1)}, u32[]{:S(2)}, u32[]{:S(2)}) collective-permute-start(bf16[66,128,128]{2,1,0:T(8,128)(2,1)} %shard_map.301.refs_1_), channel_id=1, source_target_pairs={{0,8},{8,0},{16,24},{24,16},{1,9},{9,1},{17,25},{25,17},{2,10},{10... | collective-permute-start | bytes 6488072 | tf_op jit(solution)/shard_map/ppermute | solution.py:346
  358.9 134.3 %collective-permute-start.21 = (bf16[66,128,128]{2,1,0:T(8,128)(2,1)}, bf16[66,128,128]{2,1,0:T(8,128)(2,1)}, u32[]{:S(2)}, u32[]{:S(2)}) collective-permute-start(bf16[66,128,128]{2,1,0:T(8,128)(2,1)} %collective-permute-done.17.refs_2_), channel_id=1, source_target_pairs={{0,16},{8,24},{16,0},{24,8},{1,17},{9,25},{17,1},{25,9},{2,18},{10... | collective-permute-start | bytes 6488072 | tf_op jit(solution)/shard_map/ppermute | solution.py:346
  359.5 133.7 %collective-permute-start.22 = (bf16[66,128,128]{2,1,0:T(8,128)(2,1)}, bf16[66,128,128]{2,1,0:T(8,128)(2,1)}, u32[]{:S(2)}, u32[]{:S(2)}) collective-permute-start(bf16[66,128,128]{2,1,0:T(8,128)(2,1)} %collective-permute-done.20.refs_5_), channel_id=1, source_target_pairs={{0,8},{8,0},{16,24},{24,16},{1,9},{9,1},{17,25},{25,17},{2,10},{10... | collective-permute-start | bytes 6488072 | tf_op jit(solution)/shard_map/ppermute | solution.py:346
  370.5 93.2 %collective-permute-start.27 = (bf16[20,128,128]{2,1,0:T(8,128)(2,1)}, bf16[20,128,128]{2,1,0:T(8,128)(2,1)S(1)}, u32[]{:S(2)}, u32[]{:S(2)}) collective-permute-start(bf16[20,128,128]{2,1,0:T(8,128)(2,1)} %convert_element_type.296), channel_id=1, source_target_pairs={{0,8},{8,0},{16,24},{24,16},{1,9},{9,1},{17,25},{25,17},{2,10},{10... | collective-permute-start | bytes 1966088 | tf_op jit(solution)/shard_map/ppermute | solution.py:346
  521.8 99.2 %all-gather.7.cloned.1.call-start = ((), (), s32[]{:S(2)}) async-start(), calls=%async_computation.5 | async-start | bytes 4718592 | tf_op jit(solution)/shard_map/all_gather | solution.py:728
  565.8 127.8 %reduce-scatter.11.cloned.1.call-start = ((), (), s32[]{:S(2)}) async-start(), calls=%async_computation.6 | async-start | bytes 4718592 | tf_op jit(solution)/shard_map/reduce_scatter | solution.py:733
  645.2 106.2 %all-gather.9.cloned.1.call-start = ((), (), s32[]{:S(2)}) async-start(), calls=%async_computation.7 | async-start | bytes 4718592 | tf_op jit(solution)/shard_map/all_gather | solution.py:754
  705.6 121.0 %reduce-scatter.13.cloned.1.call-start = ((), (), s32[]{:S(2)}) async-start(), calls=%async_computation.8 | async-start | bytes 4718592 | tf_op jit(solution)/shard_map/reduce_scatter | solution.py:757
  778.1 555.3 %reduce-scatter.15.cloned.1.call-start = ((), (), s32[]{:S(2)}) async-start(), calls=%async_computation.9 | async-start | bytes 11501568 | tf_op jit(solution)/shard_map/reduce_scatter | solution.py:849
  936.1 94.8 %collective-permute-start.37 = (bf16[132,128,128]{2,1,0:T(8,128)(2,1)}, bf16[132,128,128]{2,1,0:T(8,128)(2,1)}, u32[]{:S(2)}, u32[]{:S(2)}) collective-permute-start(bf16[132,128,128]{2,1,0:T(8,128)(2,1)} %shard_map.304), channel_id=1, source_target_pairs={{0,8},{8,0},{16,24},{24,16},{1,9},{9,1},{17,25},{25,17},{2,10},{10... | collective-permute-start | bytes 12976136 | tf_op jit(solution)/shard_map/ppermute | solution.py:346
  951.3 99.0 %collective-permute-start.39 = (bf16[132,128,128]{2,1,0:T(8,128)(2,1)}, bf16[132,128,128]{2,1,0:T(8,128)(2,1)}, u32[]{:S(2)}, u32[]{:S(2)}) collective-permute-start(bf16[132,128,128]{2,1,0:T(8,128)(2,1)} %shard_map.306), channel_id=1, source_target_pairs={{0,16},{8,24},{16,0},{24,8},{1,17},{9,25},{17,1},{25,9},{2,18},{10... | collective-permute-start | bytes 12976136 | tf_op jit(solution)/shard_map/ppermute | solution.py:346
  1042.4 51.1 %collective-permute-start.38 = (bf16[66,128,128]{2,1,0:T(8,128)(2,1)}, bf16[66,128,128]{2,1,0:T(8,128)(2,1)}, u32[]{:S(2)}, u32[]{:S(2)}) collective-permute-start(bf16[66,128,128]{2,1,0:T(8,128)(2,1)} %slice.624), channel_id=1, source_target_pairs={{0,16},{8,24},{16,0},{24,8},{1,17},{9,25},{17,1},{25,9},{2,18},{10... | collective-permute-start | bytes 6488072 | tf_op jit(solution)/shard_map/ppermute | solution.py:346
  1056.1 68.5 %collective-permute-start.40 = (bf16[66,128,128]{2,1,0:T(8,128)(2,1)}, bf16[66,128,128]{2,1,0:T(8,128)(2,1)}, u32[]{:S(2)}, u32[]{:S(2)}) collective-permute-start(bf16[66,128,128]{2,1,0:T(8,128)(2,1)} %slice.623), channel_id=1, source_target_pairs={{0,8},{8,0},{16,24},{24,16},{1,9},{9,1},{17,25},{25,17},{2,10},{10... | collective-permute-start | bytes 6488072 | tf_op jit(solution)/shard_map/ppermute | solution.py:346
  1097.1 67.6 %collective-permute-start.41 = (bf16[66,128,128]{2,1,0:T(8,128)(2,1)S(1)}, bf16[66,128,128]{2,1,0:T(8,128)(2,1)}, u32[]{:S(2)}, u32[]{:S(2)}) collective-permute-start(bf16[66,128,128]{2,1,0:T(8,128)(2,1)S(1)} %fusion.3.refs_0_), channel_id=1, source_target_pairs={{0,1},{1,0},{2,3},{3,2},{4,5},{5,4},{6,7},{7,6},{8,9},{9,8},{10,11... | collective-permute-start | bytes 6488072 | tf_op jit(solution)/shard_map/ppermute | solution.py:351
  1170.6 66.3 %collective-permute-start.43 = (bf16[37,128,128]{2,1,0:T(8,128)(2,1)}, bf16[37,128,128]{2,1,0:T(8,128)(2,1)}, u32[]{:S(2)}, u32[]{:S(2)}) collective-permute-start(bf16[37,128,128]{2,1,0:T(8,128)(2,1)} %shard_map.308), channel_id=1, source_target_pairs={{0,2},{1,3},{2,4},{3,5},{4,6},{5,7},{6,0},{7,1},{8,10},{9,11},{10,... | collective-permute-start | bytes 3637256 | tf_op jit(solution)/shard_map/ppermute | solution.py:357
  1228.8 104.0 %collective-permute-start.44 = (bf16[37,128,128]{2,1,0:T(8,128)(2,1)}, bf16[37,128,128]{2,1,0:T(8,128)(2,1)}, u32[]{:S(2)}, u32[]{:S(2)}) collective-permute-start(bf16[37,128,128]{2,1,0:T(8,128)(2,1)} %copy-done.21), channel_id=1, source_target_pairs={{0,4},{1,5},{2,6},{3,7},{4,0},{5,1},{6,2},{7,3},{8,12},{9,13},{10,... | collective-permute-start | bytes 3637256 | tf_op jit(solution)/shard_map/ppermute | solution.py:357
  1229.1 103.8 %collective-permute-start.45 = (bf16[37,128,128]{2,1,0:T(8,128)(2,1)}, bf16[37,128,128]{2,1,0:T(8,128)(2,1)}, u32[]{:S(2)}, u32[]{:S(2)}) collective-permute-start(bf16[37,128,128]{2,1,0:T(8,128)(2,1)} %copy-done.20), channel_id=1, source_target_pairs={{0,6},{1,7},{2,0},{3,1},{4,2},{5,3},{6,4},{7,5},{8,14},{9,15},{10,... | collective-permute-start | bytes 3637256 | tf_op jit(solution)/shard_map/ppermute | solution.py:357
  1230.8 112.3 %collective-permute-start.46 = (bf16[37,128,128]{2,1,0:T(8,128)(2,1)}, bf16[37,128,128]{2,1,0:T(8,128)(2,1)}, u32[]{:S(2)}, u32[]{:S(2)}) collective-permute-start(bf16[37,128,128]{2,1,0:T(8,128)(2,1)} %copy-done.14), channel_id=1, source_target_pairs={{0,1},{1,0},{2,3},{3,2},{4,5},{5,4},{6,7},{7,6},{8,9},{9,8},{10,11... | collective-permute-start | bytes 3637256 | tf_op jit(solution)/shard_map/ppermute | solution.py:351
  1236.1 70.7 %collective-permute-start.69 = (f32[3200]{0:T(1024)S(1)}, f32[3200]{0:T(1024)S(1)}, u32[]{:S(2)}, u32[]{:S(2)}) collective-permute-start(f32[3200]{0:T(1024)S(1)} %add.1633), channel_id=1, source_target_pairs={{0,4},{1,5},{2,6},{3,7},{4,0},{5,1},{6,2},{7,3},{8,12},{9,13},{10,... | collective-permute-start | bytes 38408 | tf_op jit(solution)/shard_map/ppermute | solution.py:357
  1236.9 106.6 %collective-permute-start.47 = (bf16[37,128,128]{2,1,0:T(8,128)(2,1)}, bf16[37,128,128]{2,1,0:T(8,128)(2,1)}, u32[]{:S(2)}, u32[]{:S(2)}) collective-permute-start(bf16[37,128,128]{2,1,0:T(8,128)(2,1)} %collective-permute-done.43.refs_1_), channel_id=1, source_target_pairs={{0,1},{1,0},{2,3},{3,2},{4,5},{5,4},{6,7},{7,6},{8,9},{9,8},{10,11... | collective-permute-start | bytes 3637256 | tf_op jit(solution)/shard_map/ppermute | solution.py:351
  (220 other events, 4500.2 us)
Sparse Core Ops, SparseCore 0:
  65.1 184.8 all-gather.4
  566.0 54.9 all-gather.6
  645.3 48.3 reduce-scatter.10
  705.7 45.6 all-gather.8
  778.2 48.3 reduce-scatter.12
  905.2 106.1 reduce-scatter.14

commit v3 on v2

--- a/solution.py
+++ b/solution.py
@@ -275,43 +275,54 @@
     def kernel(index_ref, *refs):
         sources, refs = refs[: len(grads)], refs[len(grads) :]
         master_ref, first_ref, second_ref, left_ref, right_ref = refs[:5]
-        master_out, first_out, second_out, held, sem = refs[5:]
-        base = pl.program_id(0) * each
-
-        @pl.when(pl.program_id(0) == 0)
+        master_out, first_out, second_out, held, sems = refs[5:]
+        now = pl.program_id(0)
+
+        @pl.when(now == 0)
         def _():
             def step(i, carry):
-                start_copy(sources, index_ref[i], held.at[i], sem)
+                start_copy(sources, index_ref[i], held.at[i], sems.at[i // each])
                 return carry
 
             lax.fori_loop(0, count, step, 0)
-            pltpu.make_async_copy(held, held, sem).wait()
-
+
+        block = held.at[pl.ds(now * each, each)]
+        pltpu.make_async_copy(block, block, sems.at[now]).wait()
+        lefts, rights, turns = [], [], []
         for i in range(each):
-            grad = held[base + i]
-            left_high, left_low = split_low(left_ref[i])
-            right_high, right_low = split_low(right_ref[i])
+            grad = held[now * each + i]
+            lefts.append(split_low(left_ref[i]))
+            rights.append(split_low(right_ref[i]))
             half_turned = product(
                 jnp.concatenate([grad, grad], axis=1),
-                jnp.concatenate([right_high, right_low], axis=0),
+                jnp.concatenate(rights[i], axis=0),
                 ((1,), (0,)),
             )
-            high, low = split_low(half_turned)
-            turned = product(
+            turns.append(split_low(half_turned))
+        for i in range(each):
+            (left_high, left_low), (high, low) = lefts[i], turns[i]
+            turns[i] = product(
                 jnp.concatenate([left_high, left_high, left_low], axis=0),
                 jnp.concatenate([high, low, high], axis=0),
                 ((0,), (0,)),
             )
-            first_new = BETA_ONE * first_ref[i] + (1.0 - BETA_ONE) * turned
-            second_new = BETA_TWO * second_ref[i] + (1.0 - BETA_TWO) * turned * turned
-            direction = first_new / correct_one / (jnp.sqrt(second_new / correct_two) + ADAM_EPS)
-            high, low = split_low(direction)
+        for i in range(each):
+            right_high, right_low = rights[i]
+            first_new = BETA_ONE * first_ref[i] + (1.0 - BETA_ONE) * turns[i]
+            second_new = BETA_TWO * second_ref[i] + (1.0 - BETA_TWO) * turns[i] * turns[i]
+            first_out[i] = first_new
+            second_out[i] = second_new
+            high, low = split_low(
+                first_new / correct_one / (jnp.sqrt(second_new / correct_two) + ADAM_EPS)
+            )
             half_back = product(
                 jnp.concatenate([high, low, high], axis=1),
                 jnp.concatenate([right_high, right_high, right_low], axis=1),
                 ((1,), (1,)),
             )
-            high, low = split_low(half_back)
+            turns[i] = split_low(half_back)
+        for i in range(each):
+            (left_high, left_low), (high, low) = lefts[i], turns[i]
             back = product(
                 jnp.concatenate([left_high, left_high, left_low], axis=1),
                 jnp.concatenate([high, low, high], axis=0),
@@ -319,8 +330,6 @@
             )
             weight = master_ref[i]
             master_out[i] = weight - rate * (back + DECAY * weight)
-            first_out[i] = first_new
-            second_out[i] = second_new
 
     spec = pl.BlockSpec((each, tile, tile), lambda i: (i, 0, 0))
     shape = jax.ShapeDtypeStruct(master.shape, jnp.float32)
@@ -335,7 +344,7 @@
         out_specs=(spec, spec, spec),
         scratch_shapes=[
             pltpu.VMEM((count, tile, tile), jnp.bfloat16),
-            pltpu.SemaphoreType.DMA,
+            pltpu.SemaphoreType.DMA((count // each,)),
         ],
         compiler_params=pltpu.CompilerParams(vmem_limit_bytes=VMEM_BYTES),
     )(jnp.clip(index, 0, total - 1), *grads, master, first, second, left, right)
@@ -466,8 +475,8 @@
     ffn_count = row_blocks * 3 * ffn_each
     attn_share = (2 * query_blocks + 2 * key_blocks) / columns
     ffn_share = 3 * ffn_blocks / columns
-    attn_room = room(mine, attn_share / seq_size)
-    attn_hold = room(attn_count, 1.0 / fsdp_size)
+    attn_room = (room(2 * mine, attn_share / seq_size) + 1) // 2
+    attn_hold = (room(attn_count, 1.0 / chips) + 1) // 2 + 1
     ffn_room = (room(2 * mine, ffn_share / chips) + 1) // 2
     ffn_half = (room(ffn_count, 1.0 / seq_size) + 3) // 4 * 2
     ffn_hold = 2 * ffn_half
@@ -524,12 +533,20 @@
     chip_rank = count_earlier(chip_view, chip_view >= 0).reshape(owners.shape)
     seq_view = ffn_to.reshape(seq_size, fsdp_size * mine)
     ffn_rank = count_earlier(seq_view, seq_view >= 0).reshape(owners.shape)
-    attn_rank = count_earlier(attn_to, attn_to >= 0)
-    fsdp_view = attn_to.transpose(1, 0, 2).reshape(fsdp_size, seq_size * mine)
+    attn_view = attn_to.reshape(seq_size, chips, 2 * mine)
+    attn_rank = count_earlier(attn_view, attn_view >= 0).reshape(owners.shape)
+    attn_core = (attn_rank + slot_seq) % 2
+    attn_rank = attn_rank // 2
+    attn_key = jnp.where(attn_to < 0, -1, 2 * attn_to + attn_core)
+
+    def by_chip(value):
+        value = value.reshape(seq_size, chips, 2 * mine).transpose(1, 0, 2)
+        return value.reshape(chips, seq_size * 2 * mine)
+
+    attn_key_chip = by_chip(attn_key)
+    attn_order_chip = count_earlier(attn_key_chip, attn_key_chip >= 0)
     attn_order = (
-        count_earlier(fsdp_view, fsdp_view >= 0)
-        .reshape(fsdp_size, seq_size, mine)
-        .transpose(1, 0, 2)
+        attn_order_chip.reshape(chips, seq_size, 2 * mine).transpose(1, 0, 2).reshape(owners.shape)
     )
     fits = jnp.all(
         jnp.where(
@@ -549,51 +566,64 @@
     back_place = (
         jnp.where(rank_core == my_core, 0, half) + (my_chip - ffn_chip) % chips * ffn_room + rank_local
     )
-    my_chip_slots = lax.dynamic_slice(
-        jnp.stack([ffn_chip, chip_rank]), (0, my_seq, 2 * my_chip, 0), (2, 1, 2, mine)
-    ).reshape(2, 2 * mine)
+    attn_back_place = (
+        jnp.where(attn_core == my_core, 0, seq_size * attn_room)
+        + (attn_to ^ my_seq) * attn_room
+        + attn_rank
+    )
+    chip_slots = lax.dynamic_slice(
+        jnp.stack([ffn_chip, chip_rank, attn_key, attn_rank]),
+        (0, my_seq, 2 * my_chip, 0),
+        (4, 1, 2, mine),
+    ).reshape(4, 1, 1, 2 * mine)
     my_slots = lax.dynamic_slice(
-        jnp.stack([ffn_to, attn_to, attn_rank, back_place]),
-        (0, my_seq, my_fsdp, 0),
-        (4, 1, 1, mine),
-    ).reshape(4, mine)
+        jnp.stack([ffn_to, back_place, attn_back_place]), (0, my_seq, my_fsdp, 0), (3, 1, 1, mine)
+    ).reshape(3, mine)
     seq_slots = lax.dynamic_slice(
-        jnp.stack([ffn_to, ffn_rank, ffn_place, out_place, chip_rank, jnp.broadcast_to(slot_chip, owners.shape)]),
+        jnp.stack(
+            [
+                ffn_to,
+                ffn_rank,
+                ffn_place,
+                out_place,
+                chip_rank,
+                jnp.broadcast_to(slot_chip, owners.shape),
+            ]
+        ),
         (0, my_seq, 0, 0),
         (6, 1, fsdp_size, mine),
     ).reshape(6, fsdp_size * mine)
-    fsdp_slots = lax.dynamic_slice(
-        jnp.stack([attn_to, attn_order, attn_rank, jnp.broadcast_to(slot_seq, owners.shape)]),
-        (0, 0, my_fsdp, 0),
-        (4, seq_size, 1, mine),
-    ).reshape(4, seq_size * mine)
+    column_slots = lax.dynamic_slice(
+        jnp.stack([attn_key, attn_order, attn_rank, jnp.broadcast_to(slot_seq, owners.shape)]),
+        (0, 0, 2 * my_chip, 0),
+        (4, seq_size, 2, mine),
+    ).reshape(4, 2 * seq_size * mine)
+    my_key = 2 * my_seq + my_core
 
     local_slots = jnp.arange(mine)
+    both_slots = jnp.arange(2 * mine)
+    both_slots = jnp.where(
+        both_slots // mine == my_core, both_slots % mine, mine + both_slots % mine
+    )
     attn_pack = pick(
-        (my_slots[1][None, None, :] == (my_seq ^ flips)[:, None, None])
-        & (my_slots[2][None, None, :] == jnp.arange(attn_room)[None, :, None]),
-        local_slots,
+        (chip_slots[2] == (2 * (my_seq ^ flips) + my_core)[:, None, None])
+        & (chip_slots[3] == jnp.arange(attn_room)[None, :, None]),
+        both_slots,
     )
     attn_keep = pick(
-        (fsdp_slots[0][None, :] == my_seq)
-        & (fsdp_slots[1][None, :] == jnp.arange(attn_hold)[:, None]),
-        (fsdp_slots[3] ^ my_seq) * attn_room + fsdp_slots[2],
+        (column_slots[0][None, :] == my_key)
+        & (column_slots[1][None, :] == jnp.arange(attn_hold)[:, None]),
+        (column_slots[3] ^ my_seq) * attn_room + column_slots[2],
     )
     attn_join = pick(
         (attn_to.reshape(1, -1) == my_seq)
         & (attn_place.reshape(1, -1) == jnp.arange(attn_count)[:, None]),
-        (slot_fsdp * attn_hold + attn_order).reshape(1, -1),
+        ((2 * slot_chip + attn_core) * attn_hold + attn_order).reshape(1, -1),
     )
     ffn_pack = pick(
-        (my_chip_slots[0][None, None, :] == ((my_chip + shifts) % chips)[:, None, None])
-        & (
-            my_chip_slots[1][None, None, :]
-            == (my_core * ffn_room + jnp.arange(ffn_room))[None, :, None]
-        ),
-        jnp.arange(2 * mine),
-    )
-    ffn_pack = jnp.where(
-        ffn_pack // mine == my_core, ffn_pack % mine, mine + ffn_pack % mine
+        (chip_slots[0] == ((my_chip + shifts) % chips)[:, None, None])
+        & (chip_slots[1] == (my_core * ffn_room + jnp.arange(ffn_room))[None, :, None]),
+        both_slots,
     )
     ffn_keep = pick(
         (seq_slots[0][None, :] == my_fsdp) & (seq_slots[1][None, :] == jnp.arange(ffn_hold)[:, None]),
@@ -602,53 +632,47 @@
     ffn_join = pick(
         (ffn_to.reshape(1, -1) == my_fsdp)
         & (ffn_place.reshape(1, -1) == jnp.arange(ffn_count)[:, None]),
-        ((slot_seq ^ my_seq) * ffn_hold + ffn_rank).reshape(1, -1),
+        (slot_seq * ffn_hold + ffn_rank).reshape(1, -1),
     )
     master_low = tile_master.astype(bf16)
-    attn_sent = gather_tiles([master_low], attn_pack.reshape(-1)).reshape(seq_size, attn_room, tile, tile)
+    masters = [master_low, core_swap(master_low)]
+    attn_sent = gather_tiles(masters, attn_pack.reshape(-1))
+    attn_sent = attn_sent.reshape(seq_size, attn_room, tile, tile)
     attn_got = seq_exchange([attn_sent[i] for i in range(seq_size)])
     attn_kept = gather_tiles(attn_got, attn_keep)
-
-    master_other = core_swap(master_low)
-    ffn_sent = [gather_tiles([master_low, master_other], ffn_pack[i]) for i in range(chips)]
-    ffn_got = chip_exchange(ffn_sent)
+    attn_all = lax.all_gather(attn_kept, "fsdp", axis=0, tiled=True)
+
+    ffn_got = chip_exchange([gather_tiles(masters, ffn_pack[i]) for i in range(chips)])
+    pack_tokens = seq_gather(tokens[0])
+    gain_full = seq_ordered(gains.astype(bf16))
+    small_got = seq_ordered(small_master.astype(bf16))
+    ffn_got, pack_tokens, gain_full, small_got = lax.optimization_barrier(
+        (ffn_got, pack_tokens, gain_full, small_got)
+    )
     ffn_other = [core_swap(value) for value in ffn_got]
-    kept_one = gather_tiles(ffn_got + ffn_other, ffn_keep[:ffn_half])
-    kept_two = gather_tiles(ffn_got + ffn_other, ffn_keep[ffn_half:])
-    attn_all = lax.all_gather(attn_kept, "fsdp", axis=0, tiled=True)
+    ffn_kept = gather_tiles(ffn_got + ffn_other, ffn_keep)
+    ffn_all = lax.all_gather(ffn_kept, "seq", axis=0, tiled=True)
     w_first, w_out = join_tiles([attn_all], attn_join, row_blocks, attn_first, query_each)
-    one_x, two_y = seq_swap(kept_one, 1), seq_swap(kept_two, 2)
-    two_x, one_y = seq_swap(kept_two, 1), seq_swap(kept_one, 2)
-    one_xy, two_xy = seq_swap(one_x, 2), seq_swap(two_y, 1)
-    ffn_all = [kept_one, kept_two, one_x, two_x, one_y, two_y, one_xy, two_xy]
-    w_both, w_down = join_tiles(ffn_all, ffn_join, row_blocks, ffn_first, ffn_each)
-
-    my_columns = jnp.arange(tiles)
-    def slow_fetch(_, kept):
-        whole = lax.all_gather(master_low, ("seq", "fsdp"), axis=0, tiled=True)
-        slots = my_columns.reshape(1, -1)
-        attn_slots = pick(
-            (attn_to.reshape(1, -1) == my_seq)
-            & (attn_place.reshape(1, -1) == jnp.arange(attn_count)[:, None]),
-            slots,
-        )
-        ffn_slots = pick(
-            (ffn_to.reshape(1, -1) == my_fsdp)
-            & (ffn_place.reshape(1, -1) == jnp.arange(ffn_count)[:, None]),
-            slots,
-        )
-        return join_tiles([whole], attn_slots, row_blocks, attn_first, query_each) + join_tiles(
-            [whole], ffn_slots, row_blocks, ffn_first, ffn_each
-        )
+
+    def slow_fetch(to, me, place, columns_of):
+        def fetch(_, kept):
+            whole = lax.all_gather(master_low, ("seq", "fsdp"), axis=0, tiled=True)
+            count = row_blocks * sum(columns_of)
+            index = pick(
+                (to.reshape(1, -1) == me) & (place.reshape(1, -1) == jnp.arange(count)[:, None]),
+                jnp.arange(tiles)[None, :],
+            )
+            return join_tiles([whole], index, row_blocks, *columns_of)
+
+        return fetch
 
     slow_steps = jnp.where(fits, 0, 1)
-    w_first, w_out, w_both, w_down = lax.fori_loop(
-        0, slow_steps, slow_fetch, (w_first, w_out, w_both, w_down)
-    )
-
-    small_got = seq_ordered(small_master.astype(bf16))
+    w_first, w_out = lax.fori_loop(
+        0, slow_steps, slow_fetch(attn_to, my_seq, attn_place, (attn_first, query_each)), (w_first, w_out)
+    )
+
     small_table = assemble(small_got.reshape((-1,) + small_master.shape[1:]), row_blocks)
-    gain_full = seq_ordered(gains.astype(bf16)).reshape(-1).astype(f32)
+    gain_full = gain_full.reshape(-1).astype(f32)
     gain_in = gain_full[0:width]
     gain_attn = gain_full[width : 2 * width]
     gain_laurel = gain_full[2 * width : 3 * width]
@@ -662,7 +686,6 @@
     vector_gate_w = small_table[:, 2 * RANK : 2 * RANK + PLD]
     vector_proj_w = small_table[:, 2 * RANK + PLD :]
 
-    pack_tokens = seq_gather(tokens[0])
     segment, position = documents(doc_lengths[0], length)
     places = ((my_seq ^ flips)[:, None] * rows + jnp.arange(rows)[None, :]).reshape(-1)
 
@@ -725,7 +748,12 @@
     laurel_normed, laurel_pull = jax.vjp(rms_norm, right_pre, gain_laurel)
     second_sum = (first_sum + normed + laurel_normed) * ROOT_HALF
     feed_normed, feed_pull = jax.vjp(rms_norm, second_sum, gain_pre)
-    feed_low = lax.all_gather(feed_normed.astype(bf16), "fsdp", axis=0, tiled=True)
+    ffn_all, feed_own = lax.optimization_barrier((ffn_all, feed_normed.astype(bf16)))
+    feed_low = lax.all_gather(feed_own, "fsdp", axis=0, tiled=True)
+    w_both, w_down = join_tiles([ffn_all], ffn_join, row_blocks, ffn_first, ffn_each)
+    w_both, w_down = lax.fori_loop(
+        0, slow_steps, slow_fetch(ffn_to, my_fsdp, ffn_place, (ffn_first, ffn_each)), (w_both, w_down)
+    )
     both_pre = matmul(feed_low, w_both)
     ffn_width = w_down.shape[1]
     hidden, hidden_pull = jax.vjp(gelu_product, both_pre[:, :ffn_width], both_pre[:, ffn_width:])
@@ -759,6 +787,28 @@
     ).astype(f32)
     both_grad_w = matmul_outer(feed_low, both_grad_low).astype(bf16)
     down_grad_w = matmul_outer(down_grad_low, hidden_low).astype(bf16)
+
+    flip_to = ffn_to.reshape(seq_size, 1, -1)[my_seq ^ flips]
+    flip_rank = ffn_rank.reshape(seq_size, 1, -1)[my_seq ^ flips]
+    flip_place = ffn_place.reshape(seq_size, 1, -1)[my_seq ^ flips]
+    ffn_cut = pick(
+        (flip_to == my_fsdp) & (flip_rank == jnp.arange(ffn_hold)[None, :, None]), flip_place
+    )
+    ffn_back = pick(
+        (seq_slots[5][None, None, :] == ((my_chip + shifts) % chips)[:, None, None])
+        & (seq_slots[0][None, None, :] // 2 == my_chip)
+        & (seq_slots[0][None, None, :] >= 0)
+        & (seq_slots[4][None, None, :] == (my_core * ffn_room + jnp.arange(ffn_room))[None, :, None]),
+        jnp.where(seq_slots[0] == my_fsdp, 0, ffn_hold) + seq_slots[1],
+    )
+
+    def ffn_parts(flips_of, half):
+        index = ffn_cut[:, half * ffn_half : (half + 1) * ffn_half][jnp.array(flips_of)]
+        return cut_tiles(both_grad_w, down_grad_w, index.reshape(-1), tile)
+
+    cut_one, cut_two = ffn_parts([1, 3], 0), ffn_parts([2, 3], 1)
+    cut_one, cut_two, grad_feed = lax.optimization_barrier((cut_one, cut_two, grad_feed))
+    got_one, got_two = seq_swap(cut_one, 1), seq_swap(cut_two, 2)
 
     grad_second_norm, grad_gain_pre = feed_pull(grad_feed)
     half_grad = (grad_third + grad_second_norm) * ROOT_HALF
@@ -802,57 +852,34 @@
     grad_stream_norm, grad_gain_in = normed_pull(grad_normed)
     input_grad = (half_grad + grad_stream_norm)[None]
 
-    flip_to = ffn_to.reshape(seq_size, 1, -1)[my_seq ^ flips]
-    flip_rank = ffn_rank.reshape(seq_size, 1, -1)[my_seq ^ flips]
-    flip_place = ffn_place.reshape(seq_size, 1, -1)[my_seq ^ flips]
-    ffn_cut = pick(
-        (flip_to == my_fsdp) & (flip_rank == jnp.arange(ffn_hold)[None, :, None]), flip_place
-    )
-    ffn_back = pick(
-        (seq_slots[5][None, None, :] == ((my_chip + shifts) % chips)[:, None, None])
-        & (seq_slots[0][None, None, :] // 2 == my_chip)
-        & (seq_slots[0][None, None, :] >= 0)
-        & (seq_slots[4][None, None, :] == (my_core * ffn_room + jnp.arange(ffn_room))[None, :, None]),
-        jnp.where(seq_slots[0] == my_fsdp, 0, ffn_hold) + seq_slots[1],
-    )
-
-    def ffn_parts(flips_of, half):
-        index = ffn_cut[:, half * ffn_half : (half + 1) * ffn_half][jnp.array(flips_of)]
-        return cut_tiles(both_grad_w, down_grad_w, index.reshape(-1), tile)
-
     def added(one, two):
         return one.astype(f32) + two.astype(f32)
 
-    one_sum = added(ffn_parts([0, 2], 0), seq_swap(ffn_parts([1, 3], 0), 1))
-    two_sum = added(ffn_parts([0, 1], 1), seq_swap(ffn_parts([2, 3], 1), 2))
+    one_sum = added(ffn_parts([0, 2], 0), got_one)
+    two_sum = added(ffn_parts([0, 1], 1), got_two)
     one_sum = added(one_sum[:ffn_half], seq_swap(one_sum[ffn_half:].astype(bf16), 2)).astype(bf16)
     two_sum = added(two_sum[:ffn_half], seq_swap(two_sum[ffn_half:].astype(bf16), 1)).astype(bf16)
     ffn_sums = [one_sum, two_sum, core_swap(one_sum), core_swap(two_sum)]
-    ffn_returned = chip_exchange([gather_tiles(ffn_sums, ffn_back[i]) for i in range(chips)])
+    ffn_return = [gather_tiles(ffn_sums, ffn_back[i]) for i in range(chips)]
+    ffn_returned = chip_exchange(ffn_return)
     ffn_returned = ffn_returned + [core_swap(value) for value in ffn_returned]
 
     attn_cut = pick(
-        (attn_to.transpose(1, 0, 2).reshape(fsdp_size, 1, -1) == my_seq)
-        & (
-            attn_order.transpose(1, 0, 2).reshape(fsdp_size, 1, -1)
-            == jnp.arange(attn_hold)[None, :, None]
-        ),
-        attn_place.transpose(1, 0, 2).reshape(fsdp_size, 1, -1),
+        (attn_key_chip[:, None, None, :] == (2 * my_seq + jnp.arange(2))[None, :, None, None])
+        & (attn_order_chip[:, None, None, :] == jnp.arange(attn_hold)[None, None, :, None]),
+        by_chip(attn_place)[:, None, None, :],
     )
     attn_back = pick(
-        (fsdp_slots[3][None, None, :] == (my_seq ^ flips)[:, None, None])
-        & (fsdp_slots[0][None, None, :] == my_seq)
-        & (fsdp_slots[2][None, None, :] == jnp.arange(attn_room)[None, :, None]),
-        fsdp_slots[1],
+        (column_slots[3][None, None, :] == (my_seq ^ flips)[:, None, None])
+        & (column_slots[0][None, None, :] == my_key)
+        & (column_slots[2][None, None, :] == jnp.arange(attn_room)[None, :, None]),
+        column_slots[1],
     )
     attn_parts = cut_tiles(first_grad_w, out_grad_w, attn_cut.reshape(-1), tile)
     attn_sum = lax.psum_scatter(attn_parts, "fsdp", scatter_dimension=0, tiled=True)
     attn_returned = seq_exchange([gather_tiles([attn_sum], attn_back[i]) for i in range(seq_size)])
-    slot_grad = jnp.where(
-        my_slots[0] >= 0,
-        my_slots[3],
-        2 * half + (my_slots[1] ^ my_seq) * attn_room + my_slots[2],
-    )
+    attn_returned = attn_returned + [core_swap(value) for value in attn_returned]
+    slot_grad = jnp.where(my_slots[0] >= 0, my_slots[1], 2 * half + my_slots[2])
 
     def slow_return(_, kept):
         own_ffn = split_tiles(both_grad_w, tile), split_tiles(down_grad_w, tile)
@@ -867,7 +894,7 @@
         return lax.psum_scatter(spread, ("seq", "fsdp"), scatter_dimension=0, tiled=True)
 
     tile_grads = ffn_returned + attn_returned
-    slow_start = 2 * half + seq_size * attn_room
+    slow_start = 2 * half + 2 * seq_size * attn_room
     slow_grads = lax.fori_loop(0, slow_steps, slow_return, jnp.zeros((mine, tile, tile), bf16))
     tile_grads = tile_grads + [slow_grads]
     slot_grad = jnp.where(fits, slot_grad, slow_start + local_slots)

time: 1470 us -> 1270 us (0.86)
  waiting for transfers between devices: 818 us -> 671 us
  Pallas kernels: 210 us -> 146 us
    ppermute x42 -> x36, waiting for transfers between devices: 386 us -> 204 us  [seq_swap(): return lax.ppermute(value, 'seq', [(i, i ^ flip) for i in range(size)])]
    all_gather x1 -> x2, waiting for transfers between devices: 54.9 us -> 143 us  [the longest x1 94.2 us: on_device(): ffn_all = lax.all_gather(ffn_kept, 'seq', axis=0, tiled=True)]
    pallas_call x2, Pallas kernels: 85 us -> 47.3 us  [rotate_update(): pl.pallas_call(kernel, grid=(count // each,), out_shape=(shape, shape, sh...]
    reduce_scatter x1, waiting for transfers between devices: 46.4 us -> 8.84 us  [on_device(): lax.psum_scatter(matmul_flip(both_grad_low, w_both).astype(bf16), 'fsdp',...]
    pallas_call x23 -> x22, Pallas kernels: 125 us -> 98.7 us  [tile_kernel_call(): pl.pallas_call(kernel, grid=(steps,), out_shape=out_shape, in_specs=[pl.B...]
    ppermute x15, waiting for transfers between devices: 236 us -> 214 us  [chip_shift(): lax.ppermute(value, 'fsdp', [(i, (i // 2 + offset) % chips * 2 + i % 2) f...]
    unnamed x363 -> x454, local copies, waits for them, and re-layouts: 41.7 us -> 53.2 us
    ppermute x42 -> x36, starting transfers between devices: 42.9 us -> 33.4 us  [seq_swap(): return lax.ppermute(value, 'seq', [(i, i ^ flip) for i in range(size)])]
  transfers between devices with their start and end apart: 77 -> 76, of which waited for: 35 -> 38; matrix products, arithmetic and copies ran while one was open for 11% -> 17% of each run, Pallas kernels for 8% -> 6%
where the time goes in v3:
time: 1270 us; the launch traced here: 1250 us
  waiting for transfers between devices  671 us (53%)
  Pallas kernels  146 us (11%)
  local copies, waits for them, and re-layouts  117 us (9%)
  other arithmetic  116 us (9%)
  matrix products  102 us (8%)
  starting transfers between devices  79.1 us (6%)
  between operations  20 us (2%)
    ppermute x15, waiting for transfers between devices, chip_shift(): lax.ppermute(value, 'fsdp', [(i, (i // 2 + offset) % chips * 2 + i % 2) f...  214 us
    ppermute x36, waiting for transfers between devices, seq_swap(): return lax.ppermute(value, 'seq', [(i, i ^ flip) for i in range(size)])  204 us
    pallas_call x22, Pallas kernels, tile_kernel_call(): pl.pallas_call(kernel, grid=(steps,), out_shape=out_shape, in_specs=[pl.B...  98.7 us
    all_gather x1, waiting for transfers between devices, on_device(): ffn_all = lax.all_gather(ffn_kept, 'seq', axis=0, tiled=True)  94.2 us
    unnamed x454, local copies, waits for them, and re-layouts  53.2 us
    reduce_scatter x1, waiting for transfers between devices, on_device(): lax.psum_scatter(matmul_flip(hidden_low, w_down).astype(bf16), 'fsdp', sc...  48.4 us
    all_gather x1, waiting for transfers between devices, on_device(): feed_low = lax.all_gather(feed_own, 'fsdp', axis=0, tiled=True)  48.4 us
    pallas_call x2, Pallas kernels, rotate_update(): pl.pallas_call(kernel, grid=(count // each,), out_shape=(shape, shape, sh...  47.3 us
  transfers between devices with their start and end apart: 76, of which 38 were waited for; matrix products, arithmetic and copies ran while one was open for 17% of the time, Pallas kernels for 6%

profile of v3, /device:TPU:9, one launch (start us, length us, event | category | flops | bytes accessed | tf_op | source)
XLA Modules:
  0.0 1251.3 jit_solution(18425091975023045404)
XLA Ops:
  20.8 9.1 convert_reduce_fusion.1
  52.3 9.4 collective-permute-done.15.refs_3_
  130.4 39.9 %collective-permute-done.1.refs_1_ = bf16[37,128,128]{2,1,0:T(8,128)(2,1)} collective-permute-done((bf16[37,128,128]{2,1,0:T(8,128)(2,1)}, bf16[37,128,128]{2,1,0:T(8,128)(2,1)}, u32[]{:S(2)}, u32[]{:S(2)}) %collective-permute-start.1) | collective-permute-done | bytes 1212448 | tf_op jit(solution)/shard_map/ppermute | solution.py:366
  170.3 76.4 %collective-permute-done.2.refs_2_ = bf16[37,128,128]{2,1,0:T(8,128)(2,1)} collective-permute-done((bf16[37,128,128]{2,1,0:T(8,128)(2,1)}, bf16[37,128,128]{2,1,0:T(8,128)(2,1)}, u32[]{:S(2)}, u32[]{:S(2)}) %collective-permute-start.2) | collective-permute-done | bytes 1212448 | tf_op jit(solution)/shard_map/ppermute | solution.py:366
  260.3 10.8 shard_map.300
  314.2 10.5 collective-permute-done.16
  338.1 20.5 %collective-permute-done.19 = bf16[128,2048]{1,0:T(8,128)(2,1)S(1)} collective-permute-done((bf16[128,2048]{1,0:T(8,128)(2,1)S(1)}, bf16[128,2048]{1,0:T(8,128)(2,1)S(1)}, u32[]{:S(2)}, u32[]{:S(2)}) %collective-permute-start.19) | collective-permute-done | bytes 524320 | tf_op jit(solution)/shard_map/ppermute | solution.py:355
  358.6 11.4 collective-permute-done.18
  379.1 94.2 %all-gather.9.cloned.1.call-done.refs_0_ = bf16[528,128,128]{2,1,0:T(8,128)(2,1)} async-done(((bf16[132,128,128]{2,1,0:T(8,128)(2,1)}), bf16[528,128,128]{2,1,0:T(8,128)(2,1)}) %all-gather.9.cloned.1.call-update) | async-done | bytes 17301520 | tf_op jit(solution)/shard_map/all_gather | solution.py:654
  479.2 11.1 shard_map.301
  491.1 48.4 %all-gather.11.cloned.1.call-done = bf16[1024,2048]{1,0:T(8,128)(2,1)} async-done(((bf16[128,2048]{1,0:T(8,128)(2,1)}), bf16[1024,2048]{1,0:T(8,128)(2,1)}) %all-gather.11.cloned.1.call-update) | async-done | bytes 4194320 | tf_op jit(solution)/shard_map/all_gather | solution.py:752
  539.5 12.6 %fusion.353 = f32[1024,2048]{1,0:T(8,128)S(1)} fusion(bf16[1024,2048]{1,0:T(8,128)(2,1)} %all-gather.11.cloned.1.call-done, bf16[2048,2048]{1,0:T(8,128)(2,1)} %get-tuple-element.295), kind=kOutput, calls=%fused_computation.886 | convolution fusion | flops 8589934592 | bytes 20971520 | tf_op jit(solution)/shard_map/dot_general | solution.py:61
  563.5 48.4 %reduce-scatter.11.cloned.1.call-done = bf16[128,2048]{1,0:T(8,128)(2,1)} async-done(((bf16[1024,2048]{1,0:T(8,128)(2,1)}), bf16[128,2048]{1,0:T(8,128)(2,1)}) %reduce-scatter.11.cloned.1.call-update) | async-done | bytes 524304 | tf_op jit(solution)/shard_map/reduce_scatter | solution.py:761
  623.9 45.8 %all-gather.13.cloned.1.call-done = bf16[1024,2048]{1,0:T(8,128)(2,1)} async-done(((bf16[128,2048]{1,0:T(8,128)(2,1)}), bf16[1024,2048]{1,0:T(8,128)(2,1)}) %all-gather.13.cloned.1.call-update) | async-done | bytes 4194320 | tf_op jit(solution)/shard_map/all_gather | solution.py:782
  669.7 12.3 fusion.13
  684.0 12.6 %convolution_convert_fusion.1 = bf16[1024,2048]{1,0:T(8,128)(2,1)} fusion(bf16[2048,2048]{1,0:T(8,128)(2,1)} %get-tuple-element.295, bf16[1024,1024]{1,0:T(8,128)(2,1)S(1)} %get-tuple-element.517, bf16[1024,1024]{1,0:T(8,128)(2,1)S(1)} %get-tuple-element.516), kind=kOutput, calls=%fused_computation.59 | convolution fusion | flops 8600420352 | bytes 16777216 | tf_op jit(solution)/shard_map/dot_general | solution.py:65
  704.1 7.6 convolution_convert_fusion.2.second_ref
  711.8 9.6 convolution_convert_fusion.first_ref
  736.3 8.8 reduce-scatter.13.cloned.1.call-done
  754.6 10.4 collective-permute-done.26
  765.1 10.3 collective-permute-done.25
  800.9 9.9 shard_map.310
  824.3 7.1 shard_map.304
  846.5 6.7 copy.317
  866.3 44.0 %collective-permute-done.31 = bf16[132,128,128]{2,1,0:T(8,128)(2,1)} collective-permute-done((bf16[132,128,128]{2,1,0:T(8,128)(2,1)}, bf16[132,128,128]{2,1,0:T(8,128)(2,1)}, u32[]{:S(2)}, u32[]{:S(2)}) %collective-permute-start.31) | collective-permute-done | bytes 4325408 | tf_op jit(solution)/shard_map/ppermute | solution.py:355
  928.1 11.1 collective-permute-done.52
  955.6 30.0 %collective-permute-done.32 = bf16[66,128,128]{2,1,0:T(8,128)(2,1)} collective-permute-done((bf16[66,128,128]{2,1,0:T(8,128)(2,1)}, bf16[66,128,128]{2,1,0:T(8,128)(2,1)}, u32[]{:S(2)}, u32[]{:S(2)}) %collective-permute-start.32) | collective-permute-done | bytes 2162720 | tf_op jit(solution)/shard_map/ppermute | solution.py:355
  1001.8 9.5 collective-permute-done.30
  1011.6 11.6 collective-permute-done.29
  1052.3 87.5 %collective-permute-done.59 = bf16[320,128]{1,0:T(8,128)(2,1)S(1)} collective-permute-done((bf16[320,128]{1,0:T(8,128)(2,1)S(1)}, bf16[320,128]{1,0:T(8,128)(2,1)S(1)}, u32[]{:S(2)}, u32[]{:S(2)}) %collective-permute-start.59) | collective-permute-done | bytes 81952 | tf_op jit(solution)/shard_map/ppermute | solution.py:366
  1182.3 7.1 shard_map.316
  1203.4 40.2 %shard_map.315 = (f32[116,128,128]{2,1,0:T(8,128)}, f32[116,128,128]{2,1,0:T(8,128)}, f32[116,128,128]{2,1,0:T(8,128)}) custom-call(s32[116]{0:T(128)S(1)} %fusion.289.index_ref, bf16[37,128,128]{2,1,0:T(8,128)(2,1)} %shard_map.306.refs_0_, bf16[37,128,128]{2,1,0:T(8,128)(2,1)} %collective-permute-done.37.refs_1_, ...), custom_call_target="tpu_custom_call" | custom-call | tf_op jit(solution)/shard_map/pallas_call | solution.py:337
  (909 shorter events, 446.5 us)
Async XLA Ops:
  8.0 265.2 %all-gather.7.cloned.1.call-start = ((), (), s32[]{:S(2)}) async-start(), calls=%async_computation.4 | async-start | bytes 9732096 | tf_op jit(solution)/shard_map/all_gather | solution.py:643
  65.6 41.7 %collective-permute-start.6 = (bf16[128,2048]{1,0:T(8,128)(2,1)S(1)}, bf16[128,2048]{1,0:T(8,128)(2,1)}, u32[]{:S(2)}, u32[]{:S(2)}) collective-permute-start(bf16[128,2048]{1,0:T(8,128)(2,1)S(1)} %bitcast.357), channel_id=1, source_target_pairs={{0,24},{8,16},{16,8},{24,0},{1,25},{9,17},{17,9},{25,1},{2,26},{10... | collective-permute-start | bytes 1572872 | tf_op jit(solution)/shard_map/ppermute | solution.py:355
  66.7 41.8 %collective-permute-start.5 = (bf16[128,2048]{1,0:T(8,128)(2,1)S(1)}, bf16[128,2048]{1,0:T(8,128)(2,1)}, u32[]{:S(2)}, u32[]{:S(2)}) collective-permute-start(bf16[128,2048]{1,0:T(8,128)(2,1)S(1)} %bitcast.358), channel_id=1, source_target_pairs={{0,16},{8,24},{16,0},{24,8},{1,17},{9,25},{17,1},{25,9},{2,18},{10... | collective-permute-start | bytes 1572872 | tf_op jit(solution)/shard_map/ppermute | solution.py:355
  67.8 43.0 %collective-permute-start.4 = (bf16[128,2048]{1,0:T(8,128)(2,1)S(1)}, bf16[128,2048]{1,0:T(8,128)(2,1)}, u32[]{:S(2)}, u32[]{:S(2)}) collective-permute-start(bf16[128,2048]{1,0:T(8,128)(2,1)S(1)} %bitcast.359), channel_id=1, source_target_pairs={{0,8},{8,0},{16,24},{24,16},{1,9},{9,1},{17,25},{25,17},{2,10},{10... | collective-permute-start | bytes 1572872 | tf_op jit(solution)/shard_map/ppermute | solution.py:355
  71.0 39.9 %collective-permute-start.12 = (bf16[20,128,128]{2,1,0:T(8,128)(2,1)}, bf16[20,128,128]{2,1,0:T(8,128)(2,1)}, u32[]{:S(2)}, u32[]{:S(2)}) collective-permute-start(bf16[20,128,128]{2,1,0:T(8,128)(2,1)} %convert_element_type.281), channel_id=1, source_target_pairs={{0,24},{8,16},{16,8},{24,0},{1,25},{9,17},{17,9},{25,1},{2,26},{10... | collective-permute-start | bytes 1966088 | tf_op jit(solution)/shard_map/ppermute | solution.py:355
  105.2 65.1 %collective-permute-start.1 = (bf16[37,128,128]{2,1,0:T(8,128)(2,1)}, bf16[37,128,128]{2,1,0:T(8,128)(2,1)}, u32[]{:S(2)}, u32[]{:S(2)}) collective-permute-start(bf16[37,128,128]{2,1,0:T(8,128)(2,1)} %shard_map.294), channel_id=1, source_target_pairs={{0,2},{1,3},{2,4},{3,5},{4,6},{5,7},{6,0},{7,1},{8,10},{9,11},{10,... | collective-permute-start | bytes 3637256 | tf_op jit(solution)/shard_map/ppermute | solution.py:366
  107.3 139.4 %collective-permute-start.2 = (bf16[37,128,128]{2,1,0:T(8,128)(2,1)}, bf16[37,128,128]{2,1,0:T(8,128)(2,1)}, u32[]{:S(2)}, u32[]{:S(2)}) collective-permute-start(bf16[37,128,128]{2,1,0:T(8,128)(2,1)} %shard_map.295), channel_id=1, source_target_pairs={{0,4},{1,5},{2,6},{3,7},{4,0},{5,1},{6,2},{7,3},{8,12},{9,13},{10,... | collective-permute-start | bytes 3637256 | tf_op jit(solution)/shard_map/ppermute | solution.py:366
  108.4 142.4 %collective-permute-start.3 = (bf16[37,128,128]{2,1,0:T(8,128)(2,1)S(1)}, bf16[37,128,128]{2,1,0:T(8,128)(2,1)}, u32[]{:S(2)}, u32[]{:S(2)}) collective-permute-start(bf16[37,128,128]{2,1,0:T(8,128)(2,1)S(1)} %shard_map.296), channel_id=1, source_target_pairs={{0,6},{1,7},{2,0},{3,1},{4,2},{5,3},{6,4},{7,5},{8,14},{9,15},{10,... | collective-permute-start | bytes 3637256 | tf_op jit(solution)/shard_map/ppermute | solution.py:366
  282.4 190.8 %all-gather.9.cloned.1.call-start = ((), (), s32[]{:S(2)}) async-start(), calls=%async_computation.5 | async-start | bytes 21626880 | tf_op jit(solution)/shard_map/all_gather | solution.py:654
  334.3 35.6 %collective-permute-start.18 = (bf16[128,2048]{1,0:T(8,128)(2,1)S(1)}, bf16[128,2048]{1,0:T(8,128)(2,1)S(1)}, u32[]{:S(2)}, u32[]{:S(2)}) collective-permute-start(bf16[128,2048]{1,0:T(8,128)(2,1)S(1)} %get-tuple-element.526), channel_id=1, source_target_pairs={{0,16},{8,24},{16,0},{24,8},{1,17},{9,25},{17,1},{25,9},{2,18},{10... | collective-permute-start | bytes 1572872 | tf_op jit(solution)/shard_map/ppermute | solution.py:355
  335.1 40.4 %collective-permute-start.17 = (bf16[128,2048]{1,0:T(8,128)(2,1)S(1)}, bf16[128,2048]{1,0:T(8,128)(2,1)S(1)}, u32[]{:S(2)}, u32[]{:S(2)}) collective-permute-start(bf16[128,2048]{1,0:T(8,128)(2,1)S(1)} %get-tuple-element.524), channel_id=1, source_target_pairs={{0,8},{8,0},{16,24},{24,16},{1,9},{9,1},{17,25},{25,17},{2,10},{10... | collective-permute-start | bytes 1572872 | tf_op jit(solution)/shard_map/ppermute | solution.py:355
  490.3 49.2 %all-gather.11.cloned.1.call-start = ((), (), s32[]{:S(2)}) async-start(), calls=%async_computation.6 | async-start | bytes 4718592 | tf_op jit(solution)/shard_map/all_gather | solution.py:752
  491.0 120.9 %reduce-scatter.11.cloned.1.call-start = ((), (), s32[]{:S(2)}) async-start(), calls=%async_computation.7 | async-start | bytes 4718592 | tf_op jit(solution)/shard_map/reduce_scatter | solution.py:761
  563.5 106.2 %all-gather.13.cloned.1.call-start = ((), (), s32[]{:S(2)}) async-start(), calls=%async_computation.8 | async-start | bytes 4718592 | tf_op jit(solution)/shard_map/all_gather | solution.py:782
  623.8 121.3 %reduce-scatter.13.cloned.1.call-start = ((), (), s32[]{:S(2)}) async-start(), calls=%async_computation.9 | async-start | bytes 4718592 | tf_op jit(solution)/shard_map/reduce_scatter | solution.py:785
  696.6 473.7 %reduce-scatter.15.cloned.1.call-start = ((), (), s32[]{:S(2)}) async-start(), calls=%async_computation.10 | async-start | bytes 9732096 | tf_op jit(solution)/shard_map/reduce_scatter | solution.py:879
  816.0 94.3 %collective-permute-start.31 = (bf16[132,128,128]{2,1,0:T(8,128)(2,1)}, bf16[132,128,128]{2,1,0:T(8,128)(2,1)}, u32[]{:S(2)}, u32[]{:S(2)}) collective-permute-start(bf16[132,128,128]{2,1,0:T(8,128)(2,1)} %copy-done.15), channel_id=1, source_target_pairs={{0,8},{8,0},{16,24},{24,16},{1,9},{9,1},{17,25},{25,17},{2,10},{10... | collective-permute-start | bytes 12976136 | tf_op jit(solution)/shard_map/ppermute | solution.py:355
  817.4 99.9 %collective-permute-start.33 = (bf16[132,128,128]{2,1,0:T(8,128)(2,1)}, bf16[132,128,128]{2,1,0:T(8,128)(2,1)}, u32[]{:S(2)}, u32[]{:S(2)}) collective-permute-start(bf16[132,128,128]{2,1,0:T(8,128)(2,1)} %copy-done.14), channel_id=1, source_target_pairs={{0,16},{8,24},{16,0},{24,8},{1,17},{9,25},{17,1},{25,9},{2,18},{10... | collective-permute-start | bytes 12976136 | tf_op jit(solution)/shard_map/ppermute | solution.py:355
  863.7 64.4 %collective-permute-start.53 = (bf16[20,128,128]{2,1,0:T(8,128)(2,1)}, bf16[20,128,128]{2,1,0:T(8,128)(2,1)}, u32[]{:S(2)}, u32[]{:S(2)}) collective-permute-start(bf16[20,128,128]{2,1,0:T(8,128)(2,1)} %get-tuple-element.519), channel_id=1, source_target_pairs={{0,24},{8,16},{16,8},{24,0},{1,25},{9,17},{17,9},{25,1},{2,26},{10... | collective-permute-start | bytes 1966088 | tf_op jit(solution)/shard_map/ppermute | solution.py:355
  865.0 74.3 %collective-permute-start.52 = (bf16[20,128,128]{2,1,0:T(8,128)(2,1)}, bf16[20,128,128]{2,1,0:T(8,128)(2,1)}, u32[]{:S(2)}, u32[]{:S(2)}) collective-permute-start(bf16[20,128,128]{2,1,0:T(8,128)(2,1)} %get-tuple-element.520), channel_id=1, source_target_pairs={{0,16},{8,24},{16,0},{24,8},{1,17},{9,25},{17,1},{25,9},{2,18},{10... | collective-permute-start | bytes 1966088 | tf_op jit(solution)/shard_map/ppermute | solution.py:355
  866.1 73.1 %collective-permute-start.51 = (bf16[20,128,128]{2,1,0:T(8,128)(2,1)}, bf16[20,128,128]{2,1,0:T(8,128)(2,1)}, u32[]{:S(2)}, u32[]{:S(2)}) collective-permute-start(bf16[20,128,128]{2,1,0:T(8,128)(2,1)} %get-tuple-element.518), channel_id=1, source_target_pairs={{0,8},{8,0},{16,24},{24,16},{1,9},{9,1},{17,25},{25,17},{2,10},{10... | collective-permute-start | bytes 1966088 | tf_op jit(solution)/shard_map/ppermute | solution.py:355
  916.4 69.2 %collective-permute-start.32 = (bf16[66,128,128]{2,1,0:T(8,128)(2,1)}, bf16[66,128,128]{2,1,0:T(8,128)(2,1)}, u32[]{:S(2)}, u32[]{:S(2)}) collective-permute-start(bf16[66,128,128]{2,1,0:T(8,128)(2,1)} %slice.622), channel_id=1, source_target_pairs={{0,16},{8,24},{16,0},{24,8},{1,17},{9,25},{17,1},{25,9},{2,18},{10... | collective-permute-start | bytes 6488072 | tf_op jit(solution)/shard_map/ppermute | solution.py:355
  926.1 65.6 %collective-permute-start.34 = (bf16[66,128,128]{2,1,0:T(8,128)(2,1)}, bf16[66,128,128]{2,1,0:T(8,128)(2,1)}, u32[]{:S(2)}, u32[]{:S(2)}) collective-permute-start(bf16[66,128,128]{2,1,0:T(8,128)(2,1)} %slice.621), channel_id=1, source_target_pairs={{0,8},{8,0},{16,24},{24,16},{1,9},{9,1},{17,25},{25,17},{2,10},{10... | collective-permute-start | bytes 6488072 | tf_op jit(solution)/shard_map/ppermute | solution.py:355
  951.5 45.7 %collective-permute-start.57 = (bf16[320,128]{1,0:T(8,128)(2,1)S(1)}, bf16[320,128]{1,0:T(8,128)(2,1)S(1)}, u32[]{:S(2)}, u32[]{:S(2)}) collective-permute-start(bf16[320,128]{1,0:T(8,128)(2,1)S(1)} %get-tuple-element.546), channel_id=1, source_target_pairs={{0,6},{1,7},{2,0},{3,1},{4,2},{5,3},{6,4},{7,5},{8,14},{9,15},{10,... | collective-permute-start | bytes 245768 | tf_op jit(solution)/shard_map/ppermute | solution.py:366
  951.8 46.7 %collective-permute-start.56 = (bf16[320,128]{1,0:T(8,128)(2,1)S(1)}, bf16[320,128]{1,0:T(8,128)(2,1)S(1)}, u32[]{:S(2)}, u32[]{:S(2)}) collective-permute-start(bf16[320,128]{1,0:T(8,128)(2,1)S(1)} %get-tuple-element.547), channel_id=1, source_target_pairs={{0,4},{1,5},{2,6},{3,7},{4,0},{5,1},{6,2},{7,3},{8,12},{9,13},{10,... | collective-permute-start | bytes 245768 | tf_op jit(solution)/shard_map/ppermute | solution.py:366
  954.0 45.0 %collective-permute-start.55 = (bf16[320,128]{1,0:T(8,128)(2,1)S(1)}, bf16[320,128]{1,0:T(8,128)(2,1)S(1)}, u32[]{:S(2)}, u32[]{:S(2)}) collective-permute-start(bf16[320,128]{1,0:T(8,128)(2,1)S(1)} %get-tuple-element.545), channel_id=1, source_target_pairs={{0,2},{1,3},{2,4},{3,5},{4,6},{5,7},{6,0},{7,1},{8,10},{9,11},{10,... | collective-permute-start | bytes 245768 | tf_op jit(solution)/shard_map/ppermute | solution.py:366
  989.2 38.5 %collective-permute-start.35 = (bf16[66,128,128]{2,1,0:T(8,128)(2,1)S(1)}, bf16[66,128,128]{2,1,0:T(8,128)(2,1)}, u32[]{:S(2)}, u32[]{:S(2)}) collective-permute-start(bf16[66,128,128]{2,1,0:T(8,128)(2,1)S(1)} %fusion.3.refs_0_), channel_id=1, source_target_pairs={{0,1},{1,0},{2,3},{3,2},{4,5},{5,4},{6,7},{7,6},{8,9},{9,8},{10,11... | collective-permute-start | bytes 6488072 | tf_op jit(solution)/shard_map/ppermute | solution.py:360
  1030.9 132.0 %collective-permute-start.37 = (bf16[37,128,128]{2,1,0:T(8,128)(2,1)}, bf16[37,128,128]{2,1,0:T(8,128)(2,1)}, u32[]{:S(2)}, u32[]{:S(2)}) collective-permute-start(bf16[37,128,128]{2,1,0:T(8,128)(2,1)} %shard_map.307), channel_id=1, source_target_pairs={{0,2},{1,3},{2,4},{3,5},{4,6},{5,7},{6,0},{7,1},{8,10},{9,11},{10,... | collective-permute-start | bytes 3637256 | tf_op jit(solution)/shard_map/ppermute | solution.py:366
  1035.7 127.2 %collective-permute-start.38 = (bf16[37,128,128]{2,1,0:T(8,128)(2,1)}, bf16[37,128,128]{2,1,0:T(8,128)(2,1)}, u32[]{:S(2)}, u32[]{:S(2)}) collective-permute-start(bf16[37,128,128]{2,1,0:T(8,128)(2,1)} %shard_map.308), channel_id=1, source_target_pairs={{0,4},{1,5},{2,6},{3,7},{4,0},{5,1},{6,2},{7,3},{8,12},{9,13},{10,... | collective-permute-start | bytes 3637256 | tf_op jit(solution)/shard_map/ppermute | solution.py:366
  1047.8 128.1 %collective-permute-start.39 = (bf16[37,128,128]{2,1,0:T(8,128)(2,1)}, bf16[37,128,128]{2,1,0:T(8,128)(2,1)}, u32[]{:S(2)}, u32[]{:S(2)}) collective-permute-start(bf16[37,128,128]{2,1,0:T(8,128)(2,1)} %shard_map.309), channel_id=1, source_target_pairs={{0,6},{1,7},{2,0},{3,1},{4,2},{5,3},{6,4},{7,5},{8,14},{9,15},{10,... | collective-permute-start | bytes 3637256 | tf_op jit(solution)/shard_map/ppermute | solution.py:366
  1047.8 129.3 %collective-permute-start.40 = (bf16[37,128,128]{2,1,0:T(8,128)(2,1)}, bf16[37,128,128]{2,1,0:T(8,128)(2,1)}, u32[]{:S(2)}, u32[]{:S(2)}) collective-permute-start(bf16[37,128,128]{2,1,0:T(8,128)(2,1)} %shard_map.306.refs_0_), channel_id=1, source_target_pairs={{0,1},{1,0},{2,3},{3,2},{4,5},{5,4},{6,7},{7,6},{8,9},{9,8},{10,11... | collective-permute-start | bytes 3637256 | tf_op jit(solution)/shard_map/ppermute | solution.py:360
  1051.3 88.6 %collective-permute-start.59 = (bf16[320,128]{1,0:T(8,128)(2,1)S(1)}, bf16[320,128]{1,0:T(8,128)(2,1)S(1)}, u32[]{:S(2)}, u32[]{:S(2)}) collective-permute-start(bf16[320,128]{1,0:T(8,128)(2,1)S(1)} %fusion.117), channel_id=1, source_target_pairs={{0,4},{1,5},{2,6},{3,7},{4,0},{5,1},{6,2},{7,3},{8,12},{9,13},{10,... | collective-permute-start | bytes 245768 | tf_op jit(solution)/shard_map/ppermute | solution.py:366
  (264 other events, 4341.4 us)
Sparse Core Ops, SparseCore 0:
  65.7 119.9 all-gather.6
  493.3 46.1 all-gather.10
  563.6 48.3 reduce-scatter.10
  624.0 45.6 all-gather.12
  696.8 48.3 reduce-scatter.12
  816.1 91.2 reduce-scatter.14
Sparse Core Ops, SparseCore 1:
  285.3 187.9 all-gather.8

commit v4 on v3

--- a/solution.py
+++ b/solution.py
@@ -478,8 +478,7 @@
     attn_room = (room(2 * mine, attn_share / seq_size) + 1) // 2
     attn_hold = (room(attn_count, 1.0 / chips) + 1) // 2 + 1
     ffn_room = (room(2 * mine, ffn_share / chips) + 1) // 2
-    ffn_half = (room(ffn_count, 1.0 / seq_size) + 3) // 4 * 2
-    ffn_hold = 2 * ffn_half
+    ffn_hold = (room(ffn_count, 1.0 / seq_size) + 3) // 4 * 4
 
     def tile_places(owner):
         row = owner // columns
@@ -636,19 +635,20 @@
     )
     master_low = tile_master.astype(bf16)
     masters = [master_low, core_swap(master_low)]
+    ffn_sent = [gather_tiles(masters, ffn_pack[i]) for i in range(chips)]
+    masters, ffn_sent, attn_pack = lax.optimization_barrier((masters, ffn_sent, attn_pack))
+    ffn_got = chip_exchange(ffn_sent)
     attn_sent = gather_tiles(masters, attn_pack.reshape(-1))
     attn_sent = attn_sent.reshape(seq_size, attn_room, tile, tile)
     attn_got = seq_exchange([attn_sent[i] for i in range(seq_size)])
-    attn_kept = gather_tiles(attn_got, attn_keep)
-    attn_all = lax.all_gather(attn_kept, "fsdp", axis=0, tiled=True)
-
-    ffn_got = chip_exchange([gather_tiles(masters, ffn_pack[i]) for i in range(chips)])
     pack_tokens = seq_gather(tokens[0])
     gain_full = seq_ordered(gains.astype(bf16))
     small_got = seq_ordered(small_master.astype(bf16))
-    ffn_got, pack_tokens, gain_full, small_got = lax.optimization_barrier(
-        (ffn_got, pack_tokens, gain_full, small_got)
-    )
+    ffn_got, attn_got, pack_tokens, gain_full, small_got = lax.optimization_barrier(
+        (ffn_got, attn_got, pack_tokens, gain_full, small_got)
+    )
+    attn_kept = gather_tiles(attn_got, attn_keep)
+    attn_all = lax.all_gather(attn_kept, "fsdp", axis=0, tiled=True)
     ffn_other = [core_swap(value) for value in ffn_got]
     ffn_kept = gather_tiles(ffn_got + ffn_other, ffn_keep)
     ffn_all = lax.all_gather(ffn_kept, "seq", axis=0, tiled=True)
@@ -788,27 +788,14 @@
     both_grad_w = matmul_outer(feed_low, both_grad_low).astype(bf16)
     down_grad_w = matmul_outer(down_grad_low, hidden_low).astype(bf16)
 
-    flip_to = ffn_to.reshape(seq_size, 1, -1)[my_seq ^ flips]
-    flip_rank = ffn_rank.reshape(seq_size, 1, -1)[my_seq ^ flips]
-    flip_place = ffn_place.reshape(seq_size, 1, -1)[my_seq ^ flips]
     ffn_cut = pick(
-        (flip_to == my_fsdp) & (flip_rank == jnp.arange(ffn_hold)[None, :, None]), flip_place
-    )
-    ffn_back = pick(
-        (seq_slots[5][None, None, :] == ((my_chip + shifts) % chips)[:, None, None])
-        & (seq_slots[0][None, None, :] // 2 == my_chip)
-        & (seq_slots[0][None, None, :] >= 0)
-        & (seq_slots[4][None, None, :] == (my_core * ffn_room + jnp.arange(ffn_room))[None, :, None]),
-        jnp.where(seq_slots[0] == my_fsdp, 0, ffn_hold) + seq_slots[1],
-    )
-
-    def ffn_parts(flips_of, half):
-        index = ffn_cut[:, half * ffn_half : (half + 1) * ffn_half][jnp.array(flips_of)]
-        return cut_tiles(both_grad_w, down_grad_w, index.reshape(-1), tile)
-
-    cut_one, cut_two = ffn_parts([1, 3], 0), ffn_parts([2, 3], 1)
-    cut_one, cut_two, grad_feed = lax.optimization_barrier((cut_one, cut_two, grad_feed))
-    got_one, got_two = seq_swap(cut_one, 1), seq_swap(cut_two, 2)
+        (ffn_to.reshape(seq_size, 1, -1) == my_fsdp)
+        & (ffn_rank.reshape(seq_size, 1, -1) == jnp.arange(ffn_hold)[None, :, None]),
+        ffn_place.reshape(seq_size, 1, -1),
+    )
+    ffn_parts = cut_tiles(both_grad_w, down_grad_w, ffn_cut.reshape(-1), tile)
+    ffn_parts, grad_feed = lax.optimization_barrier((ffn_parts, grad_feed))
+    ffn_sum = lax.psum_scatter(ffn_parts, "seq", scatter_dimension=0, tiled=True)
 
     grad_second_norm, grad_gain_pre = feed_pull(grad_feed)
     half_grad = (grad_third + grad_second_norm) * ROOT_HALF
@@ -852,53 +839,6 @@
     grad_stream_norm, grad_gain_in = normed_pull(grad_normed)
     input_grad = (half_grad + grad_stream_norm)[None]
 
-    def added(one, two):
-        return one.astype(f32) + two.astype(f32)
-
-    one_sum = added(ffn_parts([0, 2], 0), got_one)
-    two_sum = added(ffn_parts([0, 1], 1), got_two)
-    one_sum = added(one_sum[:ffn_half], seq_swap(one_sum[ffn_half:].astype(bf16), 2)).astype(bf16)
-    two_sum = added(two_sum[:ffn_half], seq_swap(two_sum[ffn_half:].astype(bf16), 1)).astype(bf16)
-    ffn_sums = [one_sum, two_sum, core_swap(one_sum), core_swap(two_sum)]
-    ffn_return = [gather_tiles(ffn_sums, ffn_back[i]) for i in range(chips)]
-    ffn_returned = chip_exchange(ffn_return)
-    ffn_returned = ffn_returned + [core_swap(value) for value in ffn_returned]
-
-    attn_cut = pick(
-        (attn_key_chip[:, None, None, :] == (2 * my_seq + jnp.arange(2))[None, :, None, None])
-        & (attn_order_chip[:, None, None, :] == jnp.arange(attn_hold)[None, None, :, None]),
-        by_chip(attn_place)[:, None, None, :],
-    )
-    attn_back = pick(
-        (column_slots[3][None, None, :] == (my_seq ^ flips)[:, None, None])
-        & (column_slots[0][None, None, :] == my_key)
-        & (column_slots[2][None, None, :] == jnp.arange(attn_room)[None, :, None]),
-        column_slots[1],
-    )
-    attn_parts = cut_tiles(first_grad_w, out_grad_w, attn_cut.reshape(-1), tile)
-    attn_sum = lax.psum_scatter(attn_parts, "fsdp", scatter_dimension=0, tiled=True)
-    attn_returned = seq_exchange([gather_tiles([attn_sum], attn_back[i]) for i in range(seq_size)])
-    attn_returned = attn_returned + [core_swap(value) for value in attn_returned]
-    slot_grad = jnp.where(my_slots[0] >= 0, my_slots[1], 2 * half + my_slots[2])
-
-    def slow_return(_, kept):
-        own_ffn = split_tiles(both_grad_w, tile), split_tiles(down_grad_w, tile)
-        own_attn = split_tiles(first_grad_w, tile), split_tiles(out_grad_w, tile)
-        parts = jnp.concatenate(own_ffn + own_attn + (jnp.zeros((1, tile, tile), bf16),))
-        index = jnp.where(
-            ffn_to == my_fsdp,
-            ffn_place,
-            jnp.where(attn_to == my_seq, ffn_count + attn_place, ffn_count + attn_count),
-        )
-        spread = gather_tiles([parts], index.reshape(-1))
-        return lax.psum_scatter(spread, ("seq", "fsdp"), scatter_dimension=0, tiled=True)
-
-    tile_grads = ffn_returned + attn_returned
-    slow_start = 2 * half + 2 * seq_size * attn_room
-    slow_grads = lax.fori_loop(0, slow_steps, slow_return, jnp.zeros((mine, tile, tile), bf16))
-    tile_grads = tile_grads + [slow_grads]
-    slot_grad = jnp.where(fits, slot_grad, slow_start + local_slots)
-
     small_full = jnp.concatenate(
         [
             matmul_outer(normed_low, left_grad_low),
@@ -928,6 +868,57 @@
     gain_grad_mine = gain_part
     for offset in range(1, chips):
         gain_grad_mine = gain_grad_mine + chip_shift(gain_part, offset)
+
+    ffn_back = pick(
+        (seq_slots[5][None, None, :] == ((my_chip + shifts) % chips)[:, None, None])
+        & (seq_slots[0][None, None, :] // 2 == my_chip)
+        & (seq_slots[0][None, None, :] >= 0)
+        & (seq_slots[4][None, None, :] == (my_core * ffn_room + jnp.arange(ffn_room))[None, :, None]),
+        jnp.where(seq_slots[0] == my_fsdp, 0, ffn_hold) + seq_slots[1],
+    )
+    ffn_sum, small_grad, gain_grad_mine = lax.optimization_barrier(
+        (ffn_sum, small_grad, gain_grad_mine)
+    )
+    ffn_sums = [ffn_sum, core_swap(ffn_sum)]
+    ffn_return = [gather_tiles(ffn_sums, ffn_back[i]) for i in range(chips)]
+    ffn_returned = chip_exchange(ffn_return)
+    ffn_returned = ffn_returned + [core_swap(value) for value in ffn_returned]
+
+    attn_cut = pick(
+        (attn_key_chip[:, None, None, :] == (2 * my_seq + jnp.arange(2))[None, :, None, None])
+        & (attn_order_chip[:, None, None, :] == jnp.arange(attn_hold)[None, None, :, None]),
+        by_chip(attn_place)[:, None, None, :],
+    )
+    attn_back = pick(
+        (column_slots[3][None, None, :] == (my_seq ^ flips)[:, None, None])
+        & (column_slots[0][None, None, :] == my_key)
+        & (column_slots[2][None, None, :] == jnp.arange(attn_room)[None, :, None]),
+        column_slots[1],
+    )
+    attn_parts = cut_tiles(first_grad_w, out_grad_w, attn_cut.reshape(-1), tile)
+    attn_sum = lax.psum_scatter(attn_parts, "fsdp", scatter_dimension=0, tiled=True)
+    attn_returned = seq_exchange([gather_tiles([attn_sum], attn_back[i]) for i in range(seq_size)])
+    attn_returned = attn_returned + [core_swap(value) for value in attn_returned]
+    slot_grad = jnp.where(my_slots[0] >= 0, my_slots[1], 2 * half + my_slots[2])
+
+    def slow_return(_, kept):
+        own_ffn = split_tiles(both_grad_w, tile), split_tiles(down_grad_w, tile)
+        own_attn = split_tiles(first_grad_w, tile), split_tiles(out_grad_w, tile)
+        parts = jnp.concatenate(own_ffn + own_attn + (jnp.zeros((1, tile, tile), bf16),))
+        index = jnp.where(
+            ffn_to == my_fsdp,
+            ffn_place,
+            jnp.where(attn_to == my_seq, ffn_count + attn_place, ffn_count + attn_count),
+        )
+        spread = gather_tiles([parts], index.reshape(-1))
+        return lax.psum_scatter(spread, ("seq", "fsdp"), scatter_dimension=0, tiled=True)
+
+    tile_grads = ffn_returned + attn_returned
+    slow_start = 2 * half + 2 * seq_size * attn_room
+    slow_grads = lax.fori_loop(0, slow_steps, slow_return, jnp.zeros((mine, tile, tile), bf16))
+    tile_grads = tile_grads + [slow_grads]
+    slot_grad = jnp.where(fits, slot_grad, slow_start + local_slots)
+
     tile_new, tile_first_new, tile_second_new = rotate_update(
         tile_grads, slot_grad, tile_master, tile_first, tile_second, left_basis, right_basis, RATE_TILE
     )

time: 1270 us -> 1250 us (0.984)
  waiting for transfers between devices: 671 us -> 690 us
  other arithmetic: 116 us -> 97.6 us
    ppermute x15, waiting for transfers between devices: 214 us -> 135 us  [chip_shift(): lax.ppermute(value, 'fsdp', [(i, (i // 2 + offset) % chips * 2 + i % 2) f...]
    all_gather x1, waiting for transfers between devices: 0.01 us -> 53.2 us  [on_device(): attn_all = lax.all_gather(attn_kept, 'fsdp', axis=0, tiled=True)]
    reduce_scatter x1, waiting for transfers between devices: 0.02 us -> 51.3 us  [on_device(): lax.psum_scatter(attn_parts, 'fsdp', scatter_dimension=0, tiled=True)]
    ppermute x36 -> x32, waiting for transfers between devices: 204 us -> 198 us  [seq_swap(): return lax.ppermute(value, 'seq', [(i, i ^ flip) for i in range(size)])]
    unnamed x454 -> x378, local copies, waits for them, and re-layouts: 53.2 us -> 57.5 us
    ppermute x36 -> x32, starting transfers between devices: 33.4 us -> 31.4 us  [seq_swap(): return lax.ppermute(value, 'seq', [(i, i ^ flip) for i in range(size)])]
    pallas_call x22 -> x19, Pallas kernels: 98.7 us -> 96.8 us  [tile_kernel_call(): pl.pallas_call(kernel, grid=(steps,), out_shape=out_shape, in_specs=[pl.B...]
  transfers between devices with their start and end apart: 76 -> 72, of which waited for: 38 -> 34; matrix products, arithmetic and copies ran while one was open for 17% -> 16% of each run, Pallas kernels for 6% -> 7%
where the time goes in v4:
time: 1250 us; the launch traced here: 1240 us
  waiting for transfers between devices  690 us (55%)
  Pallas kernels  146 us (12%)
  local copies, waits for them, and re-layouts  109 us (9%)
  matrix products  104 us (8%)
  other arithmetic  97.6 us (8%)
  starting transfers between devices  72.7 us (6%)
  between operations  19.6 us (2%)
    ppermute x32, waiting for transfers between devices, seq_swap(): return lax.ppermute(value, 'seq', [(i, i ^ flip) for i in range(size)])  198 us
    ppermute x15, waiting for transfers between devices, chip_shift(): lax.ppermute(value, 'fsdp', [(i, (i // 2 + offset) % chips * 2 + i % 2) f...  135 us
    all_gather x1, waiting for transfers between devices, on_device(): ffn_all = lax.all_gather(ffn_kept, 'seq', axis=0, tiled=True)  100 us
    pallas_call x19, Pallas kernels, tile_kernel_call(): pl.pallas_call(kernel, grid=(steps,), out_shape=out_shape, in_specs=[pl.B...  96.8 us
    unnamed x378, local copies, waits for them, and re-layouts  57.5 us
    all_gather x1, waiting for transfers between devices, on_device(): attn_all = lax.all_gather(attn_kept, 'fsdp', axis=0, tiled=True)  53.2 us
    reduce_scatter x1, waiting for transfers between devices, on_device(): lax.psum_scatter(attn_parts, 'fsdp', scatter_dimension=0, tiled=True)  51.3 us
    pallas_call x2, Pallas kernels, rotate_update(): pl.pallas_call(kernel, grid=(count // each,), out_shape=(shape, shape, sh...  48.9 us
  transfers between devices with their start and end apart: 72, of which 34 were waited for; matrix products, arithmetic and copies ran while one was open for 16% of the time, Pallas kernels for 7%

profile of v4, /device:TPU:9, one launch (start us, length us, event | category | flops | bytes accessed | tf_op | source)
XLA Modules:
  0.0 1238.6 jit_solution(10039684733841373656)
XLA Ops:
  29.5 9.1 convert_reduce_fusion.1
  74.5 8.0 collective-permute-done.13
  85.9 11.6 collective-permute-done.15
  97.7 8.9 collective-permute-done.6.refs_3_
  118.4 56.4 %collective-permute-done.2.refs_2_ = bf16[37,128,128]{2,1,0:T(8,128)(2,1)} collective-permute-done((bf16[37,128,128]{2,1,0:T(8,128)(2,1)}, bf16[37,128,128]{2,1,0:T(8,128)(2,1)}, u32[]{:S(2)}, u32[]{:S(2)}) %collective-permute-start.2) | collective-permute-done | bytes 1212448 | tf_op jit(solution)/shard_map/ppermute | solution.py:366
  194.4 12.0 shard_map.264
  208.5 53.2 %all-gather.7.cloned.1.call-done.refs_0_ = bf16[264,128,128]{2,1,0:T(8,128)(2,1)} async-done(((bf16[33,128,128]{2,1,0:T(8,128)(2,1)}), bf16[264,128,128]{2,1,0:T(8,128)(2,1)}) %all-gather.7.cloned.1.call-update) | async-done | bytes 8650768 | tf_op jit(solution)/shard_map/all_gather | solution.py:651
  295.5 9.7 collective-permute-done.16
  318.1 19.1 %collective-permute-done.17 = bf16[128,2048]{1,0:T(8,128)(2,1)S(1)} collective-permute-done((bf16[128,2048]{1,0:T(8,128)(2,1)S(1)}, bf16[128,2048]{1,0:T(8,128)(2,1)S(1)}, u32[]{:S(2)}, u32[]{:S(2)}) %collective-permute-start.17) | collective-permute-done | bytes 524320 | tf_op jit(solution)/shard_map/ppermute | solution.py:355
  337.2 23.5 %collective-permute-done.19 = bf16[128,2048]{1,0:T(8,128)(2,1)S(1)} collective-permute-done((bf16[128,2048]{1,0:T(8,128)(2,1)S(1)}, bf16[128,2048]{1,0:T(8,128)(2,1)S(1)}, u32[]{:S(2)}, u32[]{:S(2)}) %collective-permute-start.19) | collective-permute-done | bytes 524320 | tf_op jit(solution)/shard_map/ppermute | solution.py:355
  365.2 100.4 %all-gather.9.cloned.1.call-done.refs_0_ = bf16[528,128,128]{2,1,0:T(8,128)(2,1)} async-done(((bf16[132,128,128]{2,1,0:T(8,128)(2,1)}), bf16[528,128,128]{2,1,0:T(8,128)(2,1)}) %all-gather.9.cloned.1.call-update) | async-done | bytes 17301520 | tf_op jit(solution)/shard_map/all_gather | solution.py:654
  471.5 11.1 shard_map.265
  483.4 48.4 %all-gather.11.cloned.1.call-done = bf16[1024,2048]{1,0:T(8,128)(2,1)} async-done(((bf16[128,2048]{1,0:T(8,128)(2,1)}), bf16[1024,2048]{1,0:T(8,128)(2,1)}) %all-gather.11.cloned.1.call-update) | async-done | bytes 4194320 | tf_op jit(solution)/shard_map/all_gather | solution.py:752
  531.8 12.9 %fusion.346 = f32[1024,2048]{1,0:T(8,128)S(1)} fusion(bf16[1024,2048]{1,0:T(8,128)(2,1)} %all-gather.11.cloned.1.call-done, bf16[2048,2048]{1,0:T(8,128)(2,1)} %get-tuple-element.319), kind=kOutput, calls=%fused_computation.847 | convolution fusion | flops 8589934592 | bytes 20971520 | tf_op jit(solution)/shard_map/dot_general | solution.py:61
  556.1 48.4 %reduce-scatter.12.cloned.1.call-done = bf16[128,2048]{1,0:T(8,128)(2,1)} async-done(((bf16[1024,2048]{1,0:T(8,128)(2,1)}), bf16[128,2048]{1,0:T(8,128)(2,1)}) %reduce-scatter.12.cloned.1.call-update) | async-done | bytes 524304 | tf_op jit(solution)/shard_map/reduce_scatter | solution.py:761
  616.6 45.8 %all-gather.13.cloned.1.call-done = bf16[1024,2048]{1,0:T(8,128)(2,1)} async-done(((bf16[128,2048]{1,0:T(8,128)(2,1)}), bf16[1024,2048]{1,0:T(8,128)(2,1)}) %all-gather.13.cloned.1.call-update) | async-done | bytes 4194320 | tf_op jit(solution)/shard_map/all_gather | solution.py:782
  662.4 12.2 fusion.11
  676.6 12.6 %convolution_convert_fusion.1 = bf16[1024,2048]{1,0:T(8,128)(2,1)} fusion(bf16[2048,2048]{1,0:T(8,128)(2,1)} %get-tuple-element.319, bf16[1024,1024]{1,0:T(8,128)(2,1)S(1)} %get-tuple-element.543, bf16[1024,1024]{1,0:T(8,128)(2,1)S(1)} %get-tuple-element.542), kind=kOutput, calls=%fused_computation.44 | convolution fusion | flops 8600420352 | bytes 16777216 | tf_op jit(solution)/shard_map/dot_general | solution.py:65
  700.1 9.6 convolution_convert_fusion.first_ref
  713.1 19.1 %shard_map.266 = bf16[528,128,128]{2,1,0:T(8,128)(2,1)S(1)} custom-call(s32[528]{0:T(1024)S(1)} %min.210.index_ref, bf16[2048,2048]{1,0:T(8,128)(2,1)S(1)} %convolution_convert_fusion.first_ref, bf16[2048,1024]{1,0:T(8,128)(2,1)S(1)} %convolution_convert_fusion.2.second_ref), custom_call_target="tpu_custom_call" | custom-call | tf_op jit(solution)/shard_map/pallas_call | solution.py:125
  752.5 21.6 %collective-permute-done.26 = bf16[128,2048]{1,0:T(8,128)(2,1)} collective-permute-done((bf16[128,2048]{1,0:T(8,128)(2,1)S(1)}, bf16[128,2048]{1,0:T(8,128)(2,1)}, u32[]{:S(2)}, u32[]{:S(2)}) %collective-permute-start.26) | collective-permute-done | bytes 524320 | tf_op jit(solution)/shard_map/ppermute | solution.py:355
  774.1 12.1 collective-permute-done.25
  786.2 10.5 collective-permute-done.24
  816.5 8.1 collective-permute-done.27
  831.3 9.9 shard_map.271
  874.3 19.7 %collective-permute-done.31 = bf16[20,128,128]{2,1,0:T(8,128)(2,1)} collective-permute-done((bf16[20,128,128]{2,1,0:T(8,128)(2,1)}, bf16[20,128,128]{2,1,0:T(8,128)(2,1)}, u32[]{:S(2)}, u32[]{:S(2)}) %collective-permute-start.31) | collective-permute-done | bytes 655392 | tf_op jit(solution)/shard_map/ppermute | solution.py:355
  894.1 28.1 %collective-permute-done.33 = bf16[20,128,128]{2,1,0:T(8,128)(2,1)} collective-permute-done((bf16[20,128,128]{2,1,0:T(8,128)(2,1)}, bf16[20,128,128]{2,1,0:T(8,128)(2,1)}, u32[]{:S(2)}, u32[]{:S(2)}) %collective-permute-start.33) | collective-permute-done | bytes 655392 | tf_op jit(solution)/shard_map/ppermute | solution.py:355
  924.5 7.5 collective-permute-start.34
  962.7 9.2 collective-permute-done.30
  1004.2 51.3 %reduce-scatter.18.cloned.1.call-done.refs_0_ = bf16[33,128,128]{2,1,0:T(8,128)(2,1)} async-done(((bf16[264,128,128]{2,1,0:T(8,128)(2,1)}), bf16[33,128,128]{2,1,0:T(8,128)(2,1)}) %reduce-scatter.18.cloned.1.call-update) | async-done | bytes 1081360 | tf_op jit(solution)/shard_map/reduce_scatter | solution.py:899
  1111.1 64.1 %collective-permute-done.51.refs_2_ = bf16[37,128,128]{2,1,0:T(8,128)(2,1)} collective-permute-done((bf16[37,128,128]{2,1,0:T(8,128)(2,1)}, bf16[37,128,128]{2,1,0:T(8,128)(2,1)}, u32[]{:S(2)}, u32[]{:S(2)}) %collective-permute-start.51) | collective-permute-done | bytes 1212448 | tf_op jit(solution)/shard_map/ppermute | solution.py:366
  1189.0 41.9 %shard_map.276 = (f32[116,128,128]{2,1,0:T(8,128)}, f32[116,128,128]{2,1,0:T(8,128)}, f32[116,128,128]{2,1,0:T(8,128)}) custom-call(s32[116]{0:T(128)S(1)} %fusion.282.index_ref, bf16[37,128,128]{2,1,0:T(8,128)(2,1)} %shard_map.267.refs_0_, bf16[37,128,128]{2,1,0:T(8,128)(2,1)} %collective-permute-done.50.refs_1_, ...), custom_call_target="tpu_custom_call" | custom-call | tf_op jit(solution)/shard_map/pallas_call | solution.py:337
  (797 shorter events, 402.9 us)
Async XLA Ops:
  8.0 253.7 %all-gather.7.cloned.1.call-start = ((), (), s32[]{:S(2)}) async-start(), calls=%async_computation.5 | async-start | bytes 9732096 | tf_op jit(solution)/shard_map/all_gather | solution.py:651
  8.8 34.5 %collective-permute-start.12 = (bf16[3200]{0:T(1024)(128)(2,1)S(1)}, bf16[3200]{0:T(1024)(128)(2,1)S(1)}, u32[]{:S(2)}, u32[]{:S(2)}) collective-permute-start(bf16[3200]{0:T(1024)(128)(2,1)S(1)} %convert_element_type.254), channel_id=1, source_target_pairs={{0,24},{8,16},{16,8},{24,0},{1,25},{9,17},{17,9},{25,1},{2,26},{10... | collective-permute-start | bytes 19208 | tf_op jit(solution)/shard_map/ppermute | solution.py:355
  10.9 33.6 %collective-permute-start.11 = (bf16[3200]{0:T(1024)(128)(2,1)S(1)}, bf16[3200]{0:T(1024)(128)(2,1)S(1)}, u32[]{:S(2)}, u32[]{:S(2)}) collective-permute-start(bf16[3200]{0:T(1024)(128)(2,1)S(1)} %convert_element_type.254), channel_id=1, source_target_pairs={{0,16},{8,24},{16,0},{24,8},{1,17},{9,25},{17,1},{25,9},{2,18},{10... | collective-permute-start | bytes 19208 | tf_op jit(solution)/shard_map/ppermute | solution.py:355
  11.2 34.6 %collective-permute-start.10 = (bf16[3200]{0:T(1024)(128)(2,1)S(1)}, bf16[3200]{0:T(1024)(128)(2,1)S(1)}, u32[]{:S(2)}, u32[]{:S(2)}) collective-permute-start(bf16[3200]{0:T(1024)(128)(2,1)S(1)} %convert_element_type.254), channel_id=1, source_target_pairs={{0,8},{8,0},{16,24},{24,16},{1,9},{9,1},{17,25},{25,17},{2,10},{10... | collective-permute-start | bytes 19208 | tf_op jit(solution)/shard_map/ppermute | solution.py:355
  13.7 58.3 %collective-permute-start.14 = (bf16[20,128,128]{2,1,0:T(8,128)(2,1)}, bf16[20,128,128]{2,1,0:T(8,128)(2,1)}, u32[]{:S(2)}, u32[]{:S(2)}) collective-permute-start(bf16[20,128,128]{2,1,0:T(8,128)(2,1)} %convert_element_type.255), channel_id=1, source_target_pairs={{0,16},{8,24},{16,0},{24,8},{1,17},{9,25},{17,1},{25,9},{2,18},{10... | collective-permute-start | bytes 1966088 | tf_op jit(solution)/shard_map/ppermute | solution.py:355
  46.0 36.5 %collective-permute-start.13 = (bf16[20,128,128]{2,1,0:T(8,128)(2,1)}, bf16[20,128,128]{2,1,0:T(8,128)(2,1)}, u32[]{:S(2)}, u32[]{:S(2)}) collective-permute-start(bf16[20,128,128]{2,1,0:T(8,128)(2,1)} %convert_element_type.255), channel_id=1, source_target_pairs={{0,8},{8,0},{16,24},{24,16},{1,9},{9,1},{17,25},{25,17},{2,10},{10... | collective-permute-start | bytes 1966088 | tf_op jit(solution)/shard_map/ppermute | solution.py:355
  63.2 34.3 %collective-permute-start.15 = (bf16[20,128,128]{2,1,0:T(8,128)(2,1)}, bf16[20,128,128]{2,1,0:T(8,128)(2,1)}, u32[]{:S(2)}, u32[]{:S(2)}) collective-permute-start(bf16[20,128,128]{2,1,0:T(8,128)(2,1)} %convert_element_type.255), channel_id=1, source_target_pairs={{0,24},{8,16},{16,8},{24,0},{1,25},{9,17},{17,9},{25,1},{2,26},{10... | collective-permute-start | bytes 1966088 | tf_op jit(solution)/shard_map/ppermute | solution.py:355
  69.7 48.8 %collective-permute-start.1 = (bf16[37,128,128]{2,1,0:T(8,128)(2,1)}, bf16[37,128,128]{2,1,0:T(8,128)(2,1)}, u32[]{:S(2)}, u32[]{:S(2)}) collective-permute-start(bf16[37,128,128]{2,1,0:T(8,128)(2,1)} %shard_map.258), channel_id=1, source_target_pairs={{0,2},{1,3},{2,4},{3,5},{4,6},{5,7},{6,0},{7,1},{8,10},{9,11},{10,... | collective-permute-start | bytes 3637256 | tf_op jit(solution)/shard_map/ppermute | solution.py:366
  71.0 103.8 %collective-permute-start.2 = (bf16[37,128,128]{2,1,0:T(8,128)(2,1)}, bf16[37,128,128]{2,1,0:T(8,128)(2,1)}, u32[]{:S(2)}, u32[]{:S(2)}) collective-permute-start(bf16[37,128,128]{2,1,0:T(8,128)(2,1)} %shard_map.259), channel_id=1, source_target_pairs={{0,4},{1,5},{2,6},{3,7},{4,0},{5,1},{6,2},{7,3},{8,12},{9,13},{10,... | collective-permute-start | bytes 3637256 | tf_op jit(solution)/shard_map/ppermute | solution.py:366
  72.0 105.4 %collective-permute-start.3 = (bf16[37,128,128]{2,1,0:T(8,128)(2,1)S(1)}, bf16[37,128,128]{2,1,0:T(8,128)(2,1)}, u32[]{:S(2)}, u32[]{:S(2)}) collective-permute-start(bf16[37,128,128]{2,1,0:T(8,128)(2,1)S(1)} %shard_map.260), channel_id=1, source_target_pairs={{0,6},{1,7},{2,0},{3,1},{4,2},{5,3},{6,4},{7,5},{8,14},{9,15},{10,... | collective-permute-start | bytes 3637256 | tf_op jit(solution)/shard_map/ppermute | solution.py:366
  271.1 194.5 %all-gather.9.cloned.1.call-start = ((), (), s32[]{:S(2)}) async-start(), calls=%async_computation.6 | async-start | bytes 21626880 | tf_op jit(solution)/shard_map/all_gather | solution.py:654
  313.9 46.8 %collective-permute-start.19 = (bf16[128,2048]{1,0:T(8,128)(2,1)S(1)}, bf16[128,2048]{1,0:T(8,128)(2,1)S(1)}, u32[]{:S(2)}, u32[]{:S(2)}) collective-permute-start(bf16[128,2048]{1,0:T(8,128)(2,1)S(1)} %get-tuple-element.551), channel_id=1, source_target_pairs={{0,24},{8,16},{16,8},{24,0},{1,25},{9,17},{17,9},{25,1},{2,26},{10... | collective-permute-start | bytes 1572872 | tf_op jit(solution)/shard_map/ppermute | solution.py:355
  315.1 45.6 %collective-permute-start.18 = (bf16[128,2048]{1,0:T(8,128)(2,1)S(1)}, bf16[128,2048]{1,0:T(8,128)(2,1)S(1)}, u32[]{:S(2)}, u32[]{:S(2)}) collective-permute-start(bf16[128,2048]{1,0:T(8,128)(2,1)S(1)} %get-tuple-element.552), channel_id=1, source_target_pairs={{0,16},{8,24},{16,0},{24,8},{1,17},{9,25},{17,1},{25,9},{2,18},{10... | collective-permute-start | bytes 1572872 | tf_op jit(solution)/shard_map/ppermute | solution.py:355
  482.6 49.2 %all-gather.11.cloned.1.call-start = ((), (), s32[]{:S(2)}) async-start(), calls=%async_computation.7 | async-start | bytes 4718592 | tf_op jit(solution)/shard_map/all_gather | solution.py:752
  483.4 121.1 %reduce-scatter.12.cloned.1.call-start = ((), (), s32[]{:S(2)}) async-start(), calls=%async_computation.8 | async-start | bytes 4718592 | tf_op jit(solution)/shard_map/reduce_scatter | solution.py:761
  556.1 106.3 %all-gather.13.cloned.1.call-start = ((), (), s32[]{:S(2)}) async-start(), calls=%async_computation.9 | async-start | bytes 4718592 | tf_op jit(solution)/shard_map/all_gather | solution.py:782
  616.5 121.7 %reduce-scatter.14.cloned.1.call-start = ((), (), s32[]{:S(2)}) async-start(), calls=%async_computation.10 | async-start | bytes 4718592 | tf_op jit(solution)/shard_map/reduce_scatter | solution.py:785
  689.2 307.7 %reduce-scatter.16.cloned.1.call-start = ((), (), s32[]{:S(2)}) async-start(), calls=%async_computation.11 | async-start | bytes 21626880 | tf_op jit(solution)/shard_map/reduce_scatter | solution.py:798
  740.5 315.0 %reduce-scatter.18.cloned.1.call-start = ((), (), s32[]{:S(2)}) async-start(), calls=%async_computation.12 | async-start | bytes 9732096 | tf_op jit(solution)/shard_map/reduce_scatter | solution.py:899
  750.4 35.8 %collective-permute-start.25 = (bf16[128,2048]{1,0:T(8,128)(2,1)S(1)}, bf16[128,2048]{1,0:T(8,128)(2,1)}, u32[]{:S(2)}, u32[]{:S(2)}) collective-permute-start(bf16[128,2048]{1,0:T(8,128)(2,1)S(1)} %get-tuple-element.564), channel_id=1, source_target_pairs={{0,16},{8,24},{16,0},{24,8},{1,17},{9,25},{17,1},{25,9},{2,18},{10... | collective-permute-start | bytes 1572872 | tf_op jit(solution)/shard_map/ppermute | solution.py:355
  750.6 46.0 %collective-permute-start.24 = (bf16[128,2048]{1,0:T(8,128)(2,1)S(1)}, bf16[128,2048]{1,0:T(8,128)(2,1)}, u32[]{:S(2)}, u32[]{:S(2)}) collective-permute-start(bf16[128,2048]{1,0:T(8,128)(2,1)S(1)} %get-tuple-element.564), channel_id=1, source_target_pairs={{0,8},{8,0},{16,24},{24,16},{1,9},{9,1},{17,25},{25,17},{2,10},{10... | collective-permute-start | bytes 1572872 | tf_op jit(solution)/shard_map/ppermute | solution.py:355
  873.0 49.2 %collective-permute-start.33 = (bf16[20,128,128]{2,1,0:T(8,128)(2,1)}, bf16[20,128,128]{2,1,0:T(8,128)(2,1)}, u32[]{:S(2)}, u32[]{:S(2)}) collective-permute-start(bf16[20,128,128]{2,1,0:T(8,128)(2,1)} %get-tuple-element.545), channel_id=1, source_target_pairs={{0,24},{8,16},{16,8},{24,0},{1,25},{9,17},{17,9},{25,1},{2,26},{10... | collective-permute-start | bytes 1966088 | tf_op jit(solution)/shard_map/ppermute | solution.py:355
  873.4 48.8 %collective-permute-start.32 = (bf16[20,128,128]{2,1,0:T(8,128)(2,1)}, bf16[20,128,128]{2,1,0:T(8,128)(2,1)}, u32[]{:S(2)}, u32[]{:S(2)}) collective-permute-start(bf16[20,128,128]{2,1,0:T(8,128)(2,1)} %get-tuple-element.546), channel_id=1, source_target_pairs={{0,16},{8,24},{16,0},{24,8},{1,17},{9,25},{17,1},{25,9},{2,18},{10... | collective-permute-start | bytes 1966088 | tf_op jit(solution)/shard_map/ppermute | solution.py:355
  938.1 33.7 %collective-permute-start.30 = (bf16[128,2048]{1,0:T(8,128)(2,1)}, bf16[128,2048]{1,0:T(8,128)(2,1)}, u32[]{:S(2)}, u32[]{:S(2)}) collective-permute-start(bf16[128,2048]{1,0:T(8,128)(2,1)} %get-tuple-element.548), channel_id=1, source_target_pairs={{0,24},{8,16},{16,8},{24,0},{1,25},{9,17},{17,9},{25,1},{2,26},{10... | collective-permute-start | bytes 1572872 | tf_op jit(solution)/shard_map/ppermute | solution.py:355
  940.2 32.8 %collective-permute-start.29 = (bf16[128,2048]{1,0:T(8,128)(2,1)}, bf16[128,2048]{1,0:T(8,128)(2,1)}, u32[]{:S(2)}, u32[]{:S(2)}) collective-permute-start(bf16[128,2048]{1,0:T(8,128)(2,1)} %get-tuple-element.549), channel_id=1, source_target_pairs={{0,16},{8,24},{16,0},{24,8},{1,17},{9,25},{17,1},{25,9},{2,18},{10... | collective-permute-start | bytes 1572872 | tf_op jit(solution)/shard_map/ppermute | solution.py:355
  997.0 69.8 %collective-permute-start.49 = (bf16[132,128,128]{2,1,0:T(8,128)(2,1)}, bf16[132,128,128]{2,1,0:T(8,128)(2,1)}, u32[]{:S(2)}, u32[]{:S(2)}) collective-permute-start(bf16[132,128,128]{2,1,0:T(8,128)(2,1)} %reduce-scatter.16.cloned.1.call-done.refs_0_), channel_id=1, source_target_pairs={{0,1},{1,0},{2,3},{3,2},{4,5},{5,4},{6,7},{7,6},{8,9},{9,8},{10,11... | collective-permute-start | bytes 12976136 | tf_op jit(solution)/shard_map/ppermute | solution.py:360
  1070.0 40.6 %collective-permute-start.50 = (bf16[37,128,128]{2,1,0:T(8,128)(2,1)}, bf16[37,128,128]{2,1,0:T(8,128)(2,1)}, u32[]{:S(2)}, u32[]{:S(2)}) collective-permute-start(bf16[37,128,128]{2,1,0:T(8,128)(2,1)} %shard_map.268), channel_id=1, source_target_pairs={{0,2},{1,3},{2,4},{3,5},{4,6},{5,7},{6,0},{7,1},{8,10},{9,11},{10,... | collective-permute-start | bytes 3637256 | tf_op jit(solution)/shard_map/ppermute | solution.py:366
  1078.3 96.9 %collective-permute-start.51 = (bf16[37,128,128]{2,1,0:T(8,128)(2,1)}, bf16[37,128,128]{2,1,0:T(8,128)(2,1)}, u32[]{:S(2)}, u32[]{:S(2)}) collective-permute-start(bf16[37,128,128]{2,1,0:T(8,128)(2,1)} %shard_map.269), channel_id=1, source_target_pairs={{0,4},{1,5},{2,6},{3,7},{4,0},{5,1},{6,2},{7,3},{8,12},{9,13},{10,... | collective-permute-start | bytes 3637256 | tf_op jit(solution)/shard_map/ppermute | solution.py:366
  1081.6 98.7 %collective-permute-start.52 = (bf16[37,128,128]{2,1,0:T(8,128)(2,1)}, bf16[37,128,128]{2,1,0:T(8,128)(2,1)}, u32[]{:S(2)}, u32[]{:S(2)}) collective-permute-start(bf16[37,128,128]{2,1,0:T(8,128)(2,1)} %shard_map.270), channel_id=1, source_target_pairs={{0,6},{1,7},{2,0},{3,1},{4,2},{5,3},{6,4},{7,5},{8,14},{9,15},{10,... | collective-permute-start | bytes 3637256 | tf_op jit(solution)/shard_map/ppermute | solution.py:366
  1109.6 74.2 %collective-permute-start.63 = (bf16[13,128,128]{2,1,0:T(8,128)(2,1)}, bf16[13,128,128]{2,1,0:T(8,128)(2,1)}, u32[]{:S(2)}, u32[]{:S(2)}) collective-permute-start(bf16[13,128,128]{2,1,0:T(8,128)(2,1)} %collective-permute-done.59.refs_11_), channel_id=1, source_target_pairs={{0,1},{1,0},{2,3},{3,2},{4,5},{5,4},{6,7},{7,6},{8,9},{9,8},{10,11... | collective-permute-start | bytes 1277960 | tf_op jit(solution)/shard_map/ppermute | solution.py:360
  1110.6 73.3 %collective-permute-start.53 = (bf16[37,128,128]{2,1,0:T(8,128)(2,1)}, bf16[37,128,128]{2,1,0:T(8,128)(2,1)}, u32[]{:S(2)}, u32[]{:S(2)}) collective-permute-start(bf16[37,128,128]{2,1,0:T(8,128)(2,1)} %shard_map.267.refs_0_), channel_id=1, source_target_pairs={{0,1},{1,0},{2,3},{3,2},{4,5},{5,4},{6,7},{7,6},{8,9},{9,8},{10,11... | collective-permute-start | bytes 3637256 | tf_op jit(solution)/shard_map/ppermute | solution.py:360
  1110.7 73.2 %collective-permute-start.54 = (bf16[37,128,128]{2,1,0:T(8,128)(2,1)}, bf16[37,128,128]{2,1,0:T(8,128)(2,1)}, u32[]{:S(2)}, u32[]{:S(2)}) collective-permute-start(bf16[37,128,128]{2,1,0:T(8,128)(2,1)} %collective-permute-done.50.refs_1_), channel_id=1, source_target_pairs={{0,1},{1,0},{2,3},{3,2},{4,5},{5,4},{6,7},{7,6},{8,9},{9,8},{10,11... | collective-permute-start | bytes 3637256 | tf_op jit(solution)/shard_map/ppermute | solution.py:360
  (223 other events, 3555.3 us)
Sparse Core Ops, SparseCore 0:
  180.9 80.8 all-gather.6
  485.7 46.1 all-gather.10
  556.2 48.3 reduce-scatter.11
  616.7 45.6 all-gather.12
  689.3 48.3 reduce-scatter.13
Sparse Core Ops, SparseCore 1:
  274.0 191.5 all-gather.8
  740.6 218.8 reduce-scatter.15
  961.7 93.7 reduce-scatter.17

commit v5 on v4

--- a/solution.py
+++ b/solution.py
@@ -174,75 +174,71 @@
     )
 
 
-def join_tiles(arrays, index, row_blocks, first_columns, second_columns):
+def join_tiles(arrays, index, row_blocks, columns):
     tile = arrays[0].shape[-1]
-    first_count = row_blocks * first_columns
     steps = 4
     each = row_blocks // steps
 
     def kernel(index_ref, *refs):
-        sources, first, second, sem = refs[:-3], refs[-3], refs[-2], refs[-1]
+        sources, outs, sem = refs[: len(arrays)], refs[len(arrays) : -1], refs[-1]
         base = pl.program_id(0) * each
-        for out, start, columns in ((first, 0, first_columns), (second, first_count, second_columns)):
-
-            def step(i, carry, out=out, start=start, columns=columns):
-                row = i // columns
-                column = i - row * columns
+        start = 0
+        for out, width in zip(outs, columns):
+
+            def step(i, carry, out=out, start=start, width=width):
+                row = i // width
+                column = i - row * width
                 target = out.at[
                     pl.ds(pl.multiple_of(row * tile, tile), tile),
                     pl.ds(pl.multiple_of(column * tile, tile), tile),
                 ]
-                start_copy(sources, index_ref[start + base * columns + i], target, sem)
+                start_copy(sources, index_ref[start + base * width + i], target, sem)
                 return carry
 
-            lax.fori_loop(0, each * columns, step, 0)
-        pltpu.make_async_copy(first, first, sem).wait()
-        pltpu.make_async_copy(second, second, sem).wait()
+            lax.fori_loop(0, each * width, step, 0)
+            start = start + row_blocks * width
+        for out in outs:
+            pltpu.make_async_copy(out, out, sem).wait()
 
     total = sum(array.shape[0] for array in arrays)
     out_shape = tuple(
-        jax.ShapeDtypeStruct((row_blocks * tile, count * tile), arrays[0].dtype)
-        for count in (first_columns, second_columns)
-    )
-    out_specs = tuple(
-        pl.BlockSpec((each * tile, count * tile), lambda i: (i, 0))
-        for count in (first_columns, second_columns)
-    )
+        jax.ShapeDtypeStruct((row_blocks * tile, width * tile), arrays[0].dtype)
+        for width in columns
+    )
+    out_specs = tuple(pl.BlockSpec((each * tile, width * tile), lambda i: (i, 0)) for width in columns)
     return tile_kernel_call(
         kernel, jnp.clip(index, 0, total - 1), arrays, out_shape, out_specs, steps
     )
 
 
-def cut_tiles(first, second, index, tile):
-    row_blocks = first.shape[0] // tile
-    first_columns = first.shape[1] // tile
-    second_columns = second.shape[1] // tile
-    first_count = row_blocks * first_columns
+def cut_tiles(matrices, index, tile):
+    row_blocks = matrices[0].shape[0] // tile
+    widths = [matrix.shape[1] // tile for matrix in matrices]
     count = index.shape[0]
     steps = steps_of(count)
     each = count // steps
 
-    def kernel(index_ref, first_ref, second_ref, out, sem):
+    def kernel(index_ref, *refs):
+        sources, out, sem = refs[:-2], refs[-2], refs[-1]
         base = pl.program_id(0) * each
 
         def step(i, carry):
             place = index_ref[base + i]
-
-            def send(ref, local, columns):
-                row = pl.multiple_of((local // columns) * tile, tile)
-                column = pl.multiple_of((local % columns) * tile, tile)
-                pltpu.make_async_copy(
-                    ref.at[pl.ds(row, tile), pl.ds(column, tile)], out.at[i], sem
-                ).start()
-
-            @pl.when(place < first_count)
-            def _():
-                send(first_ref, place, first_columns)
-
-            @pl.when(place >= first_count)
-            def _():
-                send(second_ref, place - first_count, second_columns)
-
+            start = 0
+            for ref, width in zip(sources, widths):
+                size = row_blocks * width
+
+                @pl.when((place >= start) & (place < start + size))
+                def _(ref=ref, start=start, width=width):
+                    row = (place - start) // width
+                    column = place - start - row * width
+                    source = ref.at[
+                        pl.ds(pl.multiple_of(row * tile, tile), tile),
+                        pl.ds(pl.multiple_of(column * tile, tile), tile),
+                    ]
+                    pltpu.make_async_copy(source, out.at[i], sem).start()
+
+                start = start + size
             return carry
 
         lax.fori_loop(0, each, step, 0)
@@ -250,9 +246,9 @@
 
     return tile_kernel_call(
         kernel,
-        jnp.clip(index, 0, first_count + row_blocks * second_columns - 1),
-        [first, second],
-        jax.ShapeDtypeStruct((count, tile, tile), first.dtype),
+        jnp.clip(index, 0, row_blocks * sum(widths) - 1),
+        matrices,
+        jax.ShapeDtypeStruct((count, tile, tile), matrices[0].dtype),
         pl.BlockSpec((each, tile, tile), lambda i: (i, 0, 0)),
         steps,
     )
@@ -398,15 +394,24 @@
     return [values[0]] + [chip_shift(values[offset], offset) for offset in range(1, len(values))]
 
 
-def fsdp_sum(value):
-    size = lax.axis_size("fsdp")
-    chips = size // 2
+def core_pair(value):
+    other = core_swap(value)
+    even = lax.axis_index("fsdp") % 2 == 0
+    return jnp.where(even, jnp.stack([value, other]), jnp.stack([other, value]))
+
+
+def small_sum(value):
+    seq_size = lax.axis_size("seq")
+    chips = lax.axis_size("fsdp") // 2
     chip = lax.axis_index("fsdp") // 2
     even = lax.axis_index("fsdp") % 2 == 0
-    shares = value.reshape((chips, 2, value.shape[0] // size) + value.shape[1:])
-    kept = jnp.where(even, shares[:, 0], shares[:, 1])
-    given = jnp.where(even, shares[:, 1], shares[:, 0])
-    kept = kept + core_swap(given.astype(jnp.bfloat16)).astype(jnp.float32)
+    low = value.astype(jnp.bfloat16)
+    parts = low.reshape((seq_size, 2, low.shape[0] // (2 * seq_size)) + low.shape[1:])
+    kept = jnp.where(even, parts[:, 0], parts[:, 1]).astype(jnp.float32)
+    given = jnp.where(even, parts[:, 1], parts[:, 0])
+    kept = kept + core_swap(given).astype(jnp.float32)
+    kept = seq_sum(kept.reshape((-1,) + low.shape[1:]), jnp.bfloat16, True)
+    kept = kept.reshape((chips, kept.shape[0] // chips) + kept.shape[1:])
     kept = kept[(chip + jnp.arange(chips)) % chips]
     total = kept[0]
     for offset in range(1, chips):
@@ -414,9 +419,7 @@
     total = total.astype(jnp.bfloat16)
     parts = jnp.stack([total] + [chip_shift(total, offset) for offset in range(1, chips)])
     parts = parts[(chip - jnp.arange(chips)) % chips]
-    other = core_swap(parts)
-    both = jnp.where(even, jnp.stack([parts, other], axis=1), jnp.stack([other, parts], axis=1))
-    return both.reshape(value.shape)
+    return core_pair(parts).reshape((value.shape[0] // seq_size,) + value.shape[1:])
 
 
 def on_device(
@@ -477,8 +480,11 @@
     ffn_share = 3 * ffn_blocks / columns
     attn_room = (room(2 * mine, attn_share / seq_size) + 1) // 2
     attn_hold = (room(attn_count, 1.0 / chips) + 1) // 2 + 1
-    ffn_room = (room(2 * mine, ffn_share / chips) + 1) // 2
-    ffn_hold = (room(ffn_count, 1.0 / seq_size) + 3) // 4 * 4
+    ffn_rooms, ffn_holds = [], []
+    both_count = row_blocks * ffn_first
+    for part in (2.0 / 3.0, 1.0 / 3.0):
+        ffn_rooms.append((room(2 * mine, ffn_share * part / chips) + 1) // 2)
+        ffn_holds.append((room(ffn_count * part, 1.0 / seq_size) + 3) // 4 * 4)
 
     def tile_places(owner):
         row = owner // columns
@@ -493,10 +499,9 @@
         ffn_to = jnp.where(is_attn, -1, ffn_column // ffn_each)
         ffn_local = ffn_column % ffn_each
         ffn_place = jnp.where(
-            kind == 2,
-            row_blocks * ffn_first + row * ffn_each + ffn_local,
-            row * ffn_first + kind * ffn_each + ffn_local,
-        )
+            kind == 2, row * ffn_each + ffn_local, row * ffn_first + kind * ffn_each + ffn_local
+        )
+        is_down = (kind == 2).astype(jnp.int32)
         attn_to = jnp.where(
             key_at < 0,
             column // query_each,
@@ -520,17 +525,21 @@
             ),
         )
         attn_to = jnp.where(is_attn, attn_to, -1)
-        return (ffn_to, ffn_place, attn_to, attn_place)
+        return (ffn_to, is_down, ffn_place, attn_to, attn_place)
 
     owners = tile_owner.reshape(seq_size, fsdp_size, mine)
-    ffn_to, ffn_place, attn_to, attn_place = tile_places(owners)
+    ffn_to, is_down, ffn_place, attn_to, attn_place = tile_places(owners)
     slot_seq = jnp.arange(seq_size)[:, None, None]
     slot_fsdp = jnp.arange(fsdp_size)[None, :, None]
     slot_chip = slot_fsdp // 2
     ffn_chip = jnp.where(ffn_to < 0, -1, ffn_to // 2)
-    chip_view = ffn_chip.reshape(seq_size, chips, 2 * mine)
+    ffn_key = jnp.where(ffn_to < 0, -1, 2 * ffn_to + is_down)
+    chip_key = jnp.where(ffn_to < 0, -1, 2 * ffn_chip + is_down)
+    ffn_room = jnp.where(is_down == 1, ffn_rooms[1], ffn_rooms[0])
+    ffn_hold = jnp.where(is_down == 1, ffn_holds[1], ffn_holds[0])
+    chip_view = chip_key.reshape(seq_size, chips, 2 * mine)
     chip_rank = count_earlier(chip_view, chip_view >= 0).reshape(owners.shape)
-    seq_view = ffn_to.reshape(seq_size, fsdp_size * mine)
+    seq_view = ffn_key.reshape(seq_size, fsdp_size * mine)
     ffn_rank = count_earlier(seq_view, seq_view >= 0).reshape(owners.shape)
     attn_view = attn_to.reshape(seq_size, chips, 2 * mine)
     attn_rank = count_earlier(attn_view, attn_view >= 0).reshape(owners.shape)
@@ -554,24 +563,21 @@
             (chip_rank < 2 * ffn_room) & (ffn_rank < ffn_hold),
         )
     )
-    half = chips * ffn_room
-    rank_core = chip_rank // ffn_room
-    rank_local = chip_rank % ffn_room
-    out_place = (
-        jnp.where(rank_core == my_core, 0, half)
-        + (my_chip - slot_chip) % chips * ffn_room
-        + rank_local
-    )
-    back_place = (
-        jnp.where(rank_core == my_core, 0, half) + (my_chip - ffn_chip) % chips * ffn_room + rank_local
-    )
+    rank_core = (chip_rank >= ffn_room).astype(jnp.int32)
+    rank_local = chip_rank - rank_core * ffn_room
+    core_start = jnp.where(rank_core == my_core, 0, chips * ffn_room) + rank_local
+    out_place = core_start + (my_chip - slot_chip) % chips * ffn_room
+    down_start = 2 * chips * ffn_rooms[0]
+    attn_start = down_start + 2 * chips * ffn_rooms[1]
+    back_place = core_start + (my_chip - ffn_chip) % chips * ffn_room + is_down * down_start
     attn_back_place = (
-        jnp.where(attn_core == my_core, 0, seq_size * attn_room)
+        attn_start
+        + jnp.where(attn_core == my_core, 0, seq_size * attn_room)
         + (attn_to ^ my_seq) * attn_room
         + attn_rank
     )
     chip_slots = lax.dynamic_slice(
-        jnp.stack([ffn_chip, chip_rank, attn_key, attn_rank]),
+        jnp.stack([chip_key, chip_rank, attn_key, attn_rank]),
         (0, my_seq, 2 * my_chip, 0),
         (4, 1, 2, mine),
     ).reshape(4, 1, 1, 2 * mine)
@@ -581,9 +587,9 @@
     seq_slots = lax.dynamic_slice(
         jnp.stack(
             [
-                ffn_to,
+                ffn_key,
                 ffn_rank,
-                ffn_place,
+                chip_key,
                 out_place,
                 chip_rank,
                 jnp.broadcast_to(slot_chip, owners.shape),
@@ -619,40 +625,80 @@
         & (attn_place.reshape(1, -1) == jnp.arange(attn_count)[:, None]),
         ((2 * slot_chip + attn_core) * attn_hold + attn_order).reshape(1, -1),
     )
-    ffn_pack = pick(
-        (chip_slots[0] == ((my_chip + shifts) % chips)[:, None, None])
-        & (chip_slots[1] == (my_core * ffn_room + jnp.arange(ffn_room))[None, :, None]),
-        both_slots,
-    )
-    ffn_keep = pick(
-        (seq_slots[0][None, :] == my_fsdp) & (seq_slots[1][None, :] == jnp.arange(ffn_hold)[:, None]),
-        seq_slots[3][None, :],
-    )
-    ffn_join = pick(
-        (ffn_to.reshape(1, -1) == my_fsdp)
-        & (ffn_place.reshape(1, -1) == jnp.arange(ffn_count)[:, None]),
-        (slot_seq * ffn_hold + ffn_rank).reshape(1, -1),
-    )
+    def ffn_tables(kind):
+        room_now, hold_now = ffn_rooms[kind], ffn_holds[kind]
+        ranks = my_core * room_now + jnp.arange(room_now)
+        pack = pick(
+            (chip_slots[0] == (2 * ((my_chip + shifts) % chips) + kind)[:, None, None])
+            & (chip_slots[1] == ranks[None, :, None]),
+            both_slots,
+        )
+        keep = pick(
+            (seq_slots[0][None, :] == 2 * my_fsdp + kind)
+            & (seq_slots[1][None, :] == jnp.arange(hold_now)[:, None]),
+            seq_slots[3][None, :],
+        )
+        half_now = hold_now // 2
+        piece = 2 * (slot_seq ^ my_seq) * half_now + ffn_rank
+        count = both_count if kind == 0 else ffn_count - both_count
+        join = pick(
+            (ffn_key.reshape(1, -1) == 2 * my_fsdp + kind)
+            & (ffn_place.reshape(1, -1) == jnp.arange(count)[:, None]),
+            piece.reshape(1, -1),
+        )
+        cut = pick(
+            (ffn_key.reshape(seq_size, 1, -1) == 2 * my_fsdp + kind)
+            & (ffn_rank.reshape(seq_size, 1, -1) == jnp.arange(hold_now)[None, :, None]),
+            ffn_place.reshape(seq_size, 1, -1),
+        )
+        back = pick(
+            (seq_slots[5][None, None, :] == ((my_chip + shifts) % chips)[:, None, None])
+            & (seq_slots[2][None, None, :] == 2 * my_chip + kind)
+            & (seq_slots[4][None, None, :] == ranks[None, :, None]),
+            jnp.where(seq_slots[0] == 2 * my_fsdp + kind, 0, hold_now) + seq_slots[1],
+        )
+        return (pack, keep, join, cut, back)
+
+    both_pack, both_keep, both_join, both_cut, both_back = ffn_tables(0)
+    down_pack, down_keep, down_join, down_cut, down_back = ffn_tables(1)
+
+    def seq_first(kept):
+        half_now = kept.shape[0] // 2
+        one, two = kept[:half_now], kept[half_now:]
+        return [one, two, seq_swap(one, 1), seq_swap(two, 1), seq_swap(one, 2), seq_swap(two, 2)]
+
+    def seq_second(pieces):
+        return pieces + [seq_swap(pieces[2], 2), seq_swap(pieces[5], 1)]
+
     master_low = tile_master.astype(bf16)
     masters = [master_low, core_swap(master_low)]
-    ffn_sent = [gather_tiles(masters, ffn_pack[i]) for i in range(chips)]
-    masters, ffn_sent, attn_pack = lax.optimization_barrier((masters, ffn_sent, attn_pack))
-    ffn_got = chip_exchange(ffn_sent)
+    both_sent = [gather_tiles(masters, both_pack[i]) for i in range(chips)]
+    masters, both_sent = lax.optimization_barrier((masters, both_sent))
+    both_got = chip_exchange(both_sent)
     attn_sent = gather_tiles(masters, attn_pack.reshape(-1))
     attn_sent = attn_sent.reshape(seq_size, attn_room, tile, tile)
     attn_got = seq_exchange([attn_sent[i] for i in range(seq_size)])
+    down_sent = [gather_tiles(masters, down_pack[i]) for i in range(chips)]
     pack_tokens = seq_gather(tokens[0])
     gain_full = seq_ordered(gains.astype(bf16))
-    small_got = seq_ordered(small_master.astype(bf16))
-    ffn_got, attn_got, pack_tokens, gain_full, small_got = lax.optimization_barrier(
-        (ffn_got, attn_got, pack_tokens, gain_full, small_got)
+    both_got, attn_got, down_sent, pack_tokens, gain_full = lax.optimization_barrier(
+        (both_got, attn_got, down_sent, pack_tokens, gain_full)
     )
     attn_kept = gather_tiles(attn_got, attn_keep)
     attn_all = lax.all_gather(attn_kept, "fsdp", axis=0, tiled=True)
-    ffn_other = [core_swap(value) for value in ffn_got]
-    ffn_kept = gather_tiles(ffn_got + ffn_other, ffn_keep)
-    ffn_all = lax.all_gather(ffn_kept, "seq", axis=0, tiled=True)
-    w_first, w_out = join_tiles([attn_all], attn_join, row_blocks, attn_first, query_each)
+    both_kept = gather_tiles(both_got + [core_swap(value) for value in both_got], both_keep)
+    down_got = chip_exchange(down_sent)
+    down_got = down_got + [core_swap(value) for value in down_got]
+    both_all = seq_second(seq_first(both_kept))
+    small_rows = small_master.shape[0] // 2
+    small_half = lax.dynamic_slice_in_dim(small_master, my_core * small_rows, small_rows)
+    small_got = seq_ordered(small_half.astype(bf16))
+    attn_all, both_all, down_got, small_got = lax.optimization_barrier(
+        (attn_all, both_all, down_got, small_got)
+    )
+    w_first, w_out = join_tiles([attn_all], attn_join, row_blocks, (attn_first, query_each))
+    (w_both,) = join_tiles(both_all, both_join, row_blocks, (ffn_first,))
+    down_pieces = seq_first(gather_tiles(down_got, down_keep))
 
     def slow_fetch(to, me, place, columns_of):
         def fetch(_, kept):
@@ -662,15 +708,18 @@
                 (to.reshape(1, -1) == me) & (place.reshape(1, -1) == jnp.arange(count)[:, None]),
                 jnp.arange(tiles)[None, :],
             )
-            return join_tiles([whole], index, row_blocks, *columns_of)
+            return join_tiles([whole], index, row_blocks, columns_of)
 
         return fetch
 
     slow_steps = jnp.where(fits, 0, 1)
     w_first, w_out = lax.fori_loop(
-        0, slow_steps, slow_fetch(attn_to, my_seq, attn_place, (attn_first, query_each)), (w_first, w_out)
-    )
-
+        0,
+        slow_steps,
+        slow_fetch(attn_to, my_seq, attn_place, (attn_first, query_each)),
+        (w_first, w_out),
+    )
+    small_got = core_pair(small_got).transpose(1, 0, 2, 3, 4)
     small_table = assemble(small_got.reshape((-1,) + small_master.shape[1:]), row_blocks)
     gain_full = gain_full.reshape(-1).astype(f32)
     gain_in = gain_full[0:width]
@@ -748,11 +797,14 @@
     laurel_normed, laurel_pull = jax.vjp(rms_norm, right_pre, gain_laurel)
     second_sum = (first_sum + normed + laurel_normed) * ROOT_HALF
     feed_normed, feed_pull = jax.vjp(rms_norm, second_sum, gain_pre)
-    ffn_all, feed_own = lax.optimization_barrier((ffn_all, feed_normed.astype(bf16)))
+    down_pieces, feed_own = lax.optimization_barrier((down_pieces, feed_normed.astype(bf16)))
     feed_low = lax.all_gather(feed_own, "fsdp", axis=0, tiled=True)
-    w_both, w_down = join_tiles([ffn_all], ffn_join, row_blocks, ffn_first, ffn_each)
-    w_both, w_down = lax.fori_loop(
-        0, slow_steps, slow_fetch(ffn_to, my_fsdp, ffn_place, (ffn_first, ffn_each)), (w_both, w_down)
+    (w_down,) = join_tiles(seq_second(down_pieces), down_join, row_blocks, (ffn_each,))
+    (w_both,) = lax.fori_loop(
+        0, slow_steps, slow_fetch(ffn_key, 2 * my_fsdp, ffn_place, (ffn_first,)), (w_both,)
+    )
+    (w_down,) = lax.fori_loop(
+        0, slow_steps, slow_fetch(ffn_key, 2 * my_fsdp + 1, ffn_place, (ffn_each,)), (w_down,)
     )
     both_pre = matmul(feed_low, w_both)
     ffn_width = w_down.shape[1]
@@ -780,22 +832,45 @@
     grad_third = grad_out + matmul_flip(vector_grad_low, vector_gate_w)
     grad_down, grad_gain_post = down_pull(grad_third)
     down_grad_low = lax.all_gather(grad_down.astype(bf16), "fsdp", axis=0, tiled=True)
+
+    def added(one, two):
+        return one.astype(f32) + two.astype(f32)
+
+    def cut_parts(matrices, cut, flips_of, half):
+        half_now = cut.shape[1] // 2
+        index = cut[my_seq ^ jnp.array(flips_of), half * half_now : (half + 1) * half_now]
+        return cut_tiles(matrices, index.reshape(-1), tile)
+
+    down_grad_w = matmul_outer(down_grad_low, hidden_low).astype(bf16)
+    down_parts = (
+        cut_parts([down_grad_w], down_cut, [1, 3], 0),
+        cut_parts([down_grad_w], down_cut, [2, 3], 1),
+        cut_parts([down_grad_w], down_cut, [0, 2], 0),
+        cut_parts([down_grad_w], down_cut, [0, 1], 1),
+    )
+    down_grad_low, hidden_low, down_parts = lax.optimization_barrier(
+        (down_grad_low, hidden_low, down_parts)
+    )
+    down_one = added(down_parts[2], seq_swap(down_parts[0], 1))
+    down_two = added(down_parts[3], seq_swap(down_parts[1], 2))
     grad_gate, grad_up = hidden_pull(matmul(down_grad_low, w_down))
     both_grad_low = jnp.concatenate([grad_gate, grad_up], axis=1).astype(bf16)
     grad_feed = lax.psum_scatter(
         matmul_flip(both_grad_low, w_both).astype(bf16), "fsdp", scatter_dimension=0, tiled=True
     ).astype(f32)
     both_grad_w = matmul_outer(feed_low, both_grad_low).astype(bf16)
-    down_grad_w = matmul_outer(down_grad_low, hidden_low).astype(bf16)
-
-    ffn_cut = pick(
-        (ffn_to.reshape(seq_size, 1, -1) == my_fsdp)
-        & (ffn_rank.reshape(seq_size, 1, -1) == jnp.arange(ffn_hold)[None, :, None]),
-        ffn_place.reshape(seq_size, 1, -1),
-    )
-    ffn_parts = cut_tiles(both_grad_w, down_grad_w, ffn_cut.reshape(-1), tile)
-    ffn_parts, grad_feed = lax.optimization_barrier((ffn_parts, grad_feed))
-    ffn_sum = lax.psum_scatter(ffn_parts, "seq", scatter_dimension=0, tiled=True)
+    both_parts = cut_tiles([both_grad_w], both_cut.reshape(-1), tile)
+    both_parts, down_one, down_two, grad_feed = lax.optimization_barrier(
+        (both_parts, down_one, down_two, grad_feed)
+    )
+    both_sum = lax.psum_scatter(both_parts, "seq", scatter_dimension=0, tiled=True)
+    down_half = down_one.shape[0] // 2
+    down_one = added(down_one[:down_half], seq_swap(down_one[down_half:].astype(bf16), 2))
+    down_two = added(down_two[:down_half], seq_swap(down_two[down_half:].astype(bf16), 1))
+    down_sums = [down_one.astype(bf16), down_two.astype(bf16)]
+    down_sums = down_sums + [core_swap(value) for value in down_sums]
+    down_returned = chip_exchange([gather_tiles(down_sums, down_back[i]) for i in range(chips)])
+    down_returned = down_returned + [core_swap(value) for value in down_returned]
 
     grad_second_norm, grad_gain_pre = feed_pull(grad_feed)
     half_grad = (grad_third + grad_second_norm) * ROOT_HALF
@@ -848,7 +923,8 @@
         ],
         axis=1,
     )
-    small_tiles_grad = split_tiles(small_full, tile)
+    small_grad = small_sum(split_tiles(small_full, tile).reshape(-1, tile))
+    small_grad = small_grad.reshape(small_master.shape)
     gain_grad = jnp.concatenate(
         [
             grad_gain_in,
@@ -861,60 +937,68 @@
             grad_gain_key,
         ]
     )
-    small_part = seq_sum(small_tiles_grad, bf16, True)
-    small_grad = fsdp_sum(small_part.reshape(-1, tile)).reshape(small_part.shape)
     gain_part = seq_sum(gain_grad, f32, True)
     gain_part = gain_part + core_swap(gain_part)
-    gain_grad_mine = gain_part
+
+    near = (my_chip + shifts) % chips
+    near_key = attn_key_chip[near][:, None, :]
+    near_order = attn_order_chip[near][:, None, :]
+    near_place = by_chip(attn_place)[near][:, None, :]
+
+    def attn_cut(core):
+        index = pick(
+            (near_key == 2 * my_seq + core)
+            & (near_order == jnp.arange(attn_hold)[None, :, None]),
+            near_place,
+        )
+        return cut_tiles([first_grad_w, out_grad_w], index.reshape(-1), tile)
+
+    attn_given, attn_own = attn_cut(1 - my_core), attn_cut(my_core)
+    attn_given, attn_own, small_grad, down_returned = lax.optimization_barrier(
+        (attn_given, attn_own, small_grad, down_returned)
+    )
+    attn_own = added(attn_own, core_swap(attn_given)).reshape(chips, attn_hold, tile, tile)
+    attn_sum = attn_own[0]
     for offset in range(1, chips):
-        gain_grad_mine = gain_grad_mine + chip_shift(gain_part, offset)
-
-    ffn_back = pick(
-        (seq_slots[5][None, None, :] == ((my_chip + shifts) % chips)[:, None, None])
-        & (seq_slots[0][None, None, :] // 2 == my_chip)
-        & (seq_slots[0][None, None, :] >= 0)
-        & (seq_slots[4][None, None, :] == (my_core * ffn_room + jnp.arange(ffn_room))[None, :, None]),
-        jnp.where(seq_slots[0] == my_fsdp, 0, ffn_hold) + seq_slots[1],
-    )
-    ffn_sum, small_grad, gain_grad_mine = lax.optimization_barrier(
-        (ffn_sum, small_grad, gain_grad_mine)
-    )
-    ffn_sums = [ffn_sum, core_swap(ffn_sum)]
-    ffn_return = [gather_tiles(ffn_sums, ffn_back[i]) for i in range(chips)]
-    ffn_returned = chip_exchange(ffn_return)
-    ffn_returned = ffn_returned + [core_swap(value) for value in ffn_returned]
-
-    attn_cut = pick(
-        (attn_key_chip[:, None, None, :] == (2 * my_seq + jnp.arange(2))[None, :, None, None])
-        & (attn_order_chip[:, None, None, :] == jnp.arange(attn_hold)[None, None, :, None]),
-        by_chip(attn_place)[:, None, None, :],
-    )
+        attn_sum = attn_sum + chip_shift(attn_own[offset].astype(bf16), offset).astype(f32)
     attn_back = pick(
         (column_slots[3][None, None, :] == (my_seq ^ flips)[:, None, None])
         & (column_slots[0][None, None, :] == my_key)
         & (column_slots[2][None, None, :] == jnp.arange(attn_room)[None, :, None]),
         column_slots[1],
     )
-    attn_parts = cut_tiles(first_grad_w, out_grad_w, attn_cut.reshape(-1), tile)
-    attn_sum = lax.psum_scatter(attn_parts, "fsdp", scatter_dimension=0, tiled=True)
+    attn_sum = attn_sum.astype(bf16)
     attn_returned = seq_exchange([gather_tiles([attn_sum], attn_back[i]) for i in range(seq_size)])
     attn_returned = attn_returned + [core_swap(value) for value in attn_returned]
-    slot_grad = jnp.where(my_slots[0] >= 0, my_slots[1], 2 * half + my_slots[2])
+
+    both_sums = [both_sum, core_swap(both_sum)]
+    both_return = [gather_tiles(both_sums, both_back[i]) for i in range(chips)]
+    both_return, gain_part = lax.optimization_barrier((both_return, gain_part))
+    both_returned = chip_exchange(both_return)
+    both_returned = both_returned + [core_swap(value) for value in both_returned]
+    gain_grad_mine = gain_part
+    for offset in range(1, chips):
+        gain_grad_mine = gain_grad_mine + chip_shift(gain_part, offset)
+    slot_grad = jnp.where(my_slots[0] >= 0, my_slots[1], my_slots[2])
 
     def slow_return(_, kept):
-        own_ffn = split_tiles(both_grad_w, tile), split_tiles(down_grad_w, tile)
-        own_attn = split_tiles(first_grad_w, tile), split_tiles(out_grad_w, tile)
-        parts = jnp.concatenate(own_ffn + own_attn + (jnp.zeros((1, tile, tile), bf16),))
+        parts = jnp.concatenate(
+            [
+                split_tiles(value, tile)
+                for value in (both_grad_w, down_grad_w, first_grad_w, out_grad_w)
+            ]
+            + [jnp.zeros((1, tile, tile), bf16)]
+        )
         index = jnp.where(
             ffn_to == my_fsdp,
-            ffn_place,
+            is_down * both_count + ffn_place,
             jnp.where(attn_to == my_seq, ffn_count + attn_place, ffn_count + attn_count),
         )
         spread = gather_tiles([parts], index.reshape(-1))
         return lax.psum_scatter(spread, ("seq", "fsdp"), scatter_dimension=0, tiled=True)
 
-    tile_grads = ffn_returned + attn_returned
-    slow_start = 2 * half + 2 * seq_size * attn_room
+    tile_grads = both_returned + down_returned + attn_returned
+    slow_start = attn_start + 2 * seq_size * attn_room
     slow_grads = lax.fori_loop(0, slow_steps, slow_return, jnp.zeros((mine, tile, tile), bf16))
     tile_grads = tile_grads + [slow_grads]
     slot_grad = jnp.where(fits, slot_grad, slow_start + local_slots)

time: 1250 us -> 1350 us (1.080)
  waiting for transfers between devices: 690 us -> 596 us
  starting transfers between devices: 72.7 us -> 132 us
  other arithmetic: 97.6 us -> 147 us
  Pallas kernels: 146 us -> 183 us
  local copies, waits for them, and re-layouts: 109 us -> 141 us
    ppermute x15 -> x24, waiting for transfers between devices: 135 us -> 252 us  [chip_shift(): lax.ppermute(value, 'fsdp', [(i, (i // 2 + offset) % chips * 2 + i % 2) f...]
    all_gather x1 -> x0, waiting for transfers between devices: 100 us -> none  [on_device(): ffn_all = lax.all_gather(ffn_kept, 'seq', axis=0, tiled=True)]
    all_gather x1, waiting for transfers between devices: 53.2 us -> 0.01 us  [on_device(): attn_all = lax.all_gather(attn_kept, 'fsdp', axis=0, tiled=True)]
    reduce_scatter x2 -> x1, waiting for transfers between devices: 51.3 us -> 0.02 us  [on_device(): lax.psum_scatter(both_parts, 'seq', scatter_dimension=0, tiled=True)]
    ppermute x17 -> x29, starting transfers between devices: 18.4 us -> 64 us  [core_swap(): return lax.ppermute(value, 'fsdp', [(i, i ^ 1) for i in range(size)])]
    ppermute x32 -> x48, waiting for transfers between devices: 198 us -> 243 us  [seq_swap(): return lax.ppermute(value, 'seq', [(i, i ^ flip) for i in range(size)])]
    pallas_call x19 -> x34, Pallas kernels: 96.8 us -> 130 us  [tile_kernel_call(): pl.pallas_call(kernel, grid=(steps,), out_shape=out_shape, in_specs=[pl.B...]
    all_gather x1, waiting for transfers between devices: 48.4 us -> 19.1 us  [on_device(): feed_low = lax.all_gather(feed_own, 'fsdp', axis=0, tiled=True)]
  transfers between devices with their start and end apart: 72 -> 107, of which waited for: 34 -> 40; matrix products, arithmetic and copies ran while one was open for 16% -> 21% of each run, Pallas kernels for 7% -> 9%
where the time goes in v5:
time: 1350 us; the launch traced here: 1330 us
  waiting for transfers between devices  596 us (44%)
  Pallas kernels  183 us (14%)
  other arithmetic  147 us (11%)
  local copies, waits for them, and re-layouts  141 us (10%)
  starting transfers between devices  132 us (10%)
  matrix products  113 us (8%)
  between operations  18.6 us (1%)
    ppermute x24, waiting for transfers between devices, chip_shift(): lax.ppermute(value, 'fsdp', [(i, (i // 2 + offset) % chips * 2 + i % 2) f...  252 us
    ppermute x48, waiting for transfers between devices, seq_swap(): return lax.ppermute(value, 'seq', [(i, i ^ flip) for i in range(size)])  243 us
    pallas_call x34, Pallas kernels, tile_kernel_call(): pl.pallas_call(kernel, grid=(steps,), out_shape=out_shape, in_specs=[pl.B...  130 us
    ppermute x29, starting transfers between devices, core_swap(): return lax.ppermute(value, 'fsdp', [(i, i ^ 1) for i in range(size)])  64 us
    unnamed x461, local copies, waits for them, and re-layouts  54.5 us
    pallas_call x2, Pallas kernels, rotate_update(): pl.pallas_call(kernel, grid=(count // each,), out_shape=(shape, shape, sh...  53.1 us
    reduce_scatter x1, waiting for transfers between devices, on_device(): lax.psum_scatter(matmul_flip(hidden_low, w_down).astype(bf16), 'fsdp', sc...  48.4 us
    ppermute x48, starting transfers between devices, seq_swap(): return lax.ppermute(value, 'seq', [(i, i ^ flip) for i in range(size)])  40 us
  transfers between devices with their start and end apart: 107, of which 40 were waited for; matrix products, arithmetic and copies ran while one was open for 21% of the time, Pallas kernels for 9%

profile of v5, /device:TPU:9, one launch (start us, length us, event | category | flops | bytes accessed | tf_op | source)
XLA Modules:
  0.0 1332.1 jit_solution(3603905681499288489)
XLA Ops:
  27.4 9.1 convert_reduce_fusion
  92.7 56.0 %collective-permute-done.2.refs_2_ = bf16[27,128,128]{2,1,0:T(8,128)(2,1)S(1)} collective-permute-done((bf16[27,128,128]{2,1,0:T(8,128)(2,1)}, bf16[27,128,128]{2,1,0:T(8,128)(2,1)S(1)}, u32[]{:S(2)}, u32[]{:S(2)}) %collective-permute-start.2) | collective-permute-done | bytes 884768 | tf_op jit(solution)/shard_map/ppermute | solution.py:362
  172.0 8.8 shard_map.303
  189.1 35.9 %collective-permute-done.32 = bf16[10,128,128]{2,1,0:T(8,128)(2,1)S(1)} collective-permute-done((bf16[10,128,128]{2,1,0:T(8,128)(2,1)}, bf16[10,128,128]{2,1,0:T(8,128)(2,1)S(1)}, u32[]{:S(2)}, u32[]{:S(2)}) %collective-permute-start.32) | collective-permute-done | bytes 327712 | tf_op jit(solution)/shard_map/ppermute | solution.py:351
  228.3 50.3 %collective-permute-done.24.refs_2_ = bf16[17,128,128]{2,1,0:T(8,128)(2,1)} collective-permute-done((bf16[17,128,128]{2,1,0:T(8,128)(2,1)}, bf16[17,128,128]{2,1,0:T(8,128)(2,1)}, u32[]{:S(2)}, u32[]{:S(2)}) %collective-permute-start.24) | collective-permute-done | bytes 557088 | tf_op jit(solution)/shard_map/ppermute | solution.py:362
  300.0 17.3 %collective-permute-done.18.refs_3_ = bf16[46,128,128]{2,1,0:T(8,128)(2,1)} collective-permute-done((bf16[46,128,128]{2,1,0:T(8,128)(2,1)S(1)}, bf16[46,128,128]{2,1,0:T(8,128)(2,1)}, u32[]{:S(2)}, u32[]{:S(2)}) %collective-permute-start.18) | collective-permute-done | bytes 1507360 | tf_op jit(solution)/shard_map/ppermute | solution.py:351
  318.5 31.2 %collective-permute-done.22.refs_7_ = bf16[46,128,128]{2,1,0:T(8,128)(2,1)} collective-permute-done((bf16[46,128,128]{2,1,0:T(8,128)(2,1)}, bf16[46,128,128]{2,1,0:T(8,128)(2,1)}, u32[]{:S(2)}, u32[]{:S(2)}) %collective-permute-start.22) | collective-permute-done | bytes 1507360 | tf_op jit(solution)/shard_map/ppermute | solution.py:351
  403.3 15.5 %shard_map.306 = bf16[2048,2048]{1,0:T(8,128)(2,1)} custom-call(s32[256]{0:T(256)S(1)} %broadcast_clamp_fusion.11.index_ref, bf16[46,128,128]{2,1,0:T(8,128)(2,1)S(1)} %get-tuple-element.440.refs_0_, bf16[46,128,128]{2,1,0:T(8,128)(2,1)S(1)} %get-tuple-element.441.refs_1_, bf16[46,128,128]{2,1,0:T(8,128)(2,1)} %collective-permute-done.17.refs_2_, ...), custom_call_target="tpu_custom_call" | custom-call | tf_op jit(solution)/shard_map/pallas_call | solution.py:125
  441.8 16.7 %collective-permute-done.40.refs_4_ = bf16[28,128,128]{2,1,0:T(8,128)(2,1)S(1)} collective-permute-done((bf16[28,128,128]{2,1,0:T(8,128)(2,1)}, bf16[28,128,128]{2,1,0:T(8,128)(2,1)S(1)}, u32[]{:S(2)}, u32[]{:S(2)}) %collective-permute-start.40) | collective-permute-done | bytes 917536 | tf_op jit(solution)/shard_map/ppermute | solution.py:351
  462.6 19.0 %collective-permute-done.42.refs_6_ = bf16[28,128,128]{2,1,0:T(8,128)(2,1)S(1)} collective-permute-done((bf16[28,128,128]{2,1,0:T(8,128)(2,1)}, bf16[28,128,128]{2,1,0:T(8,128)(2,1)S(1)}, u32[]{:S(2)}, u32[]{:S(2)}) %collective-permute-start.42) | collective-permute-done | bytes 917536 | tf_op jit(solution)/shard_map/ppermute | solution.py:351
  482.8 9.8 shard_map.307
  492.7 19.1 %all-gather.9.cloned.1.call-done = bf16[1024,2048]{1,0:T(8,128)(2,1)} async-done(((bf16[128,2048]{1,0:T(8,128)(2,1)}), bf16[1024,2048]{1,0:T(8,128)(2,1)}) %all-gather.9.cloned.1.call-update) | async-done | bytes 4194320 | tf_op jit(solution)/shard_map/all_gather | solution.py:801
  511.8 12.5 fusion.387
  538.1 48.4 %reduce-scatter.11.cloned.1.call-done = bf16[128,2048]{1,0:T(8,128)(2,1)} async-done(((bf16[1024,2048]{1,0:T(8,128)(2,1)}), bf16[128,2048]{1,0:T(8,128)(2,1)}) %reduce-scatter.11.cloned.1.call-update) | async-done | bytes 524304 | tf_op jit(solution)/shard_map/reduce_scatter | solution.py:813
  615.1 28.6 %all-gather.11.cloned.1.call-done = bf16[1024,2048]{1,0:T(8,128)(2,1)} async-done(((bf16[128,2048]{1,0:T(8,128)(2,1)}), bf16[1024,2048]{1,0:T(8,128)(2,1)}) %all-gather.11.cloned.1.call-update) | async-done | bytes 4194320 | tf_op jit(solution)/shard_map/all_gather | solution.py:834
  664.1 10.7 fusion.10
  676.1 11.8 convolution_convert_fusion.1
  692.8 12.4 convolution_convert_fusion.refs_0_
  708.5 11.9 shard_map.312
  791.6 9.8 collective-permute-done.47
  801.4 10.3 collective-permute-done.46
  832.3 29.9 %collective-permute-done.49 = bf16[512,256]{1,0:T(8,128)(2,1)S(1)} collective-permute-done((bf16[512,256]{1,0:T(8,128)(2,1)S(1)}, bf16[512,256]{1,0:T(8,128)(2,1)S(1)}, u32[]{:S(2)}, u32[]{:S(2)}) %collective-permute-start.49) | collective-permute-done | bytes 262176 | tf_op jit(solution)/shard_map/ppermute | solution.py:351
  888.8 13.8 %collective-permute-done.68 = bf16[1280,128]{1,0:T(8,128)(2,1)S(1)} collective-permute-done((bf16[1280,128]{1,0:T(8,128)(2,1)S(1)}, bf16[1280,128]{1,0:T(8,128)(2,1)S(1)}, u32[]{:S(2)}, u32[]{:S(2)}) %collective-permute-start.68) | collective-permute-done | bytes 327712 | tf_op jit(solution)/shard_map/ppermute | solution.py:351
  930.4 45.5 %collective-permute-done.74 = bf16[320,128]{1,0:T(8,128)(2,1)S(1)} collective-permute-done((bf16[320,128]{1,0:T(8,128)(2,1)S(1)}, bf16[320,128]{1,0:T(8,128)(2,1)S(1)}, u32[]{:S(2)}, u32[]{:S(2)}) %collective-permute-start.74) | collective-permute-done | bytes 81952 | tf_op jit(solution)/shard_map/ppermute | solution.py:362
  1016.6 10.2 collective-permute-done.50
  1026.8 12.2 collective-permute-done.52
  1044.4 9.9 fusion.356
  1082.3 22.9 %collective-permute-done.90 = bf16[33,128,128]{2,1,0:T(8,128)(2,1)} collective-permute-done((bf16[33,128,128]{2,1,0:T(8,128)(2,1)}, bf16[33,128,128]{2,1,0:T(8,128)(2,1)}, u32[]{:S(2)}, u32[]{:S(2)}) %collective-permute-start.90) | collective-permute-done | bytes 1081376 | tf_op jit(solution)/shard_map/ppermute | solution.py:362
  1105.1 44.4 %collective-permute-done.89 = bf16[33,128,128]{2,1,0:T(8,128)(2,1)} collective-permute-done((bf16[33,128,128]{2,1,0:T(8,128)(2,1)}, bf16[33,128,128]{2,1,0:T(8,128)(2,1)}, u32[]{:S(2)}, u32[]{:S(2)}) %collective-permute-start.89) | collective-permute-done | bytes 1081376 | tf_op jit(solution)/shard_map/ppermute | solution.py:362
  1211.2 39.2 %collective-permute-start.62 = (bf16[27,128,128]{2,1,0:T(8,128)(2,1)}, bf16[27,128,128]{2,1,0:T(8,128)(2,1)}, u32[]{:S(2)}, u32[]{:S(2)}) collective-permute-start(bf16[27,128,128]{2,1,0:T(8,128)(2,1)} %collective-permute-done.58.refs_1_), channel_id=1, source_target_pairs={{0,1},{1,0},{2,3},{3,2},{4,5},{5,4},{6,7},{7,6},{8,9},{9,8},{10,11... | collective-permute-start | bytes 2654216 | tf_op jit(solution)/shard_map/ppermute | solution.py:356
  1250.4 16.4 %collective-permute-done.59.refs_2_ = bf16[27,128,128]{2,1,0:T(8,128)(2,1)} collective-permute-done((bf16[27,128,128]{2,1,0:T(8,128)(2,1)}, bf16[27,128,128]{2,1,0:T(8,128)(2,1)}, u32[]{:S(2)}, u32[]{:S(2)}) %collective-permute-start.59) | collective-permute-done | bytes 884768 | tf_op jit(solution)/shard_map/ppermute | solution.py:362
  1278.8 46.1 %shard_map.327 = (f32[116,128,128]{2,1,0:T(8,128)}, f32[116,128,128]{2,1,0:T(8,128)}, f32[116,128,128]{2,1,0:T(8,128)}) custom-call(s32[116]{0:T(128)S(1)} %fusion.311.index_ref, bf16[27,128,128]{2,1,0:T(8,128)(2,1)} %shard_map.313.refs_0_, bf16[27,128,128]{2,1,0:T(8,128)(2,1)} %collective-permute-done.58.refs_1_, ...), custom_call_target="tpu_custom_call" | custom-call | tf_op jit(solution)/shard_map/pallas_call | solution.py:333
  (1045 shorter events, 593.2 us)
Async XLA Ops:
  7.2 343.6 %all-gather.7.cloned.1.call-start = ((), (), s32[]{:S(2)}) async-start(), calls=%async_computation.4 | async-start | bytes 9732096 | tf_op jit(solution)/shard_map/all_gather | solution.py:688
  7.9 51.3 %collective-permute-start.12 = (bf16[3200]{0:T(1024)(128)(2,1)S(1)}, bf16[3200]{0:T(1024)(128)(2,1)S(1)}, u32[]{:S(2)}, u32[]{:S(2)}) collective-permute-start(bf16[3200]{0:T(1024)(128)(2,1)S(1)} %convert_element_type.395), channel_id=1, source_target_pairs={{0,24},{8,16},{16,8},{24,0},{1,25},{9,17},{17,9},{25,1},{2,26},{10... | collective-permute-start | bytes 19208 | tf_op jit(solution)/shard_map/ppermute | solution.py:351
  10.3 61.8 %collective-permute-start.9 = (bf16[128,2048]{1,0:T(8,128)(2,1)}, bf16[128,2048]{1,0:T(8,128)(2,1)}, u32[]{:S(2)}, u32[]{:S(2)}) collective-permute-start(bf16[128,2048]{1,0:T(8,128)(2,1)} %bitcast.8), channel_id=1, source_target_pairs={{0,24},{8,16},{16,8},{24,0},{1,25},{9,17},{17,9},{25,1},{2,26},{10... | collective-permute-start | bytes 1572872 | tf_op jit(solution)/shard_map/ppermute | solution.py:351
  11.6 61.9 %collective-permute-start.8 = (bf16[128,2048]{1,0:T(8,128)(2,1)}, bf16[128,2048]{1,0:T(8,128)(2,1)}, u32[]{:S(2)}, u32[]{:S(2)}) collective-permute-start(bf16[128,2048]{1,0:T(8,128)(2,1)} %bitcast.8), channel_id=1, source_target_pairs={{0,16},{8,24},{16,0},{24,8},{1,17},{9,25},{17,1},{25,9},{2,18},{10... | collective-permute-start | bytes 1572872 | tf_op jit(solution)/shard_map/ppermute | solution.py:351
  72.1 76.5 %collective-permute-start.2 = (bf16[27,128,128]{2,1,0:T(8,128)(2,1)}, bf16[27,128,128]{2,1,0:T(8,128)(2,1)S(1)}, u32[]{:S(2)}, u32[]{:S(2)}) collective-permute-start(bf16[27,128,128]{2,1,0:T(8,128)(2,1)} %shard_map.295), channel_id=1, source_target_pairs={{0,4},{1,5},{2,6},{3,7},{4,0},{5,1},{6,2},{7,3},{8,12},{9,13},{10,... | collective-permute-start | bytes 2654216 | tf_op jit(solution)/shard_map/ppermute | solution.py:362
  73.5 77.4 %collective-permute-start.3 = (bf16[27,128,128]{2,1,0:T(8,128)(2,1)}, bf16[27,128,128]{2,1,0:T(8,128)(2,1)}, u32[]{:S(2)}, u32[]{:S(2)}) collective-permute-start(bf16[27,128,128]{2,1,0:T(8,128)(2,1)} %shard_map.296), channel_id=1, source_target_pairs={{0,6},{1,7},{2,0},{3,1},{4,2},{5,3},{6,4},{7,5},{8,14},{9,15},{10,... | collective-permute-start | bytes 2654216 | tf_op jit(solution)/shard_map/ppermute | solution.py:362
  181.1 104.3 %collective-permute-start.20 = (bf16[46,128,128]{2,1,0:T(8,128)(2,1)S(1)}, bf16[46,128,128]{2,1,0:T(8,128)(2,1)}, u32[]{:S(2)}, u32[]{:S(2)}) collective-permute-start(bf16[46,128,128]{2,1,0:T(8,128)(2,1)S(1)} %get-tuple-element.441.refs_1_), channel_id=1, source_target_pairs={{0,16},{8,24},{16,0},{24,8},{1,17},{9,25},{17,1},{25,9},{2,18},{10... | collective-permute-start | bytes 4521992 | tf_op jit(solution)/shard_map/ppermute | solution.py:351
  183.4 102.3 %collective-permute-start.17 = (bf16[46,128,128]{2,1,0:T(8,128)(2,1)S(1)}, bf16[46,128,128]{2,1,0:T(8,128)(2,1)}, u32[]{:S(2)}, u32[]{:S(2)}) collective-permute-start(bf16[46,128,128]{2,1,0:T(8,128)(2,1)S(1)} %get-tuple-element.440.refs_0_), channel_id=1, source_target_pairs={{0,8},{8,0},{16,24},{24,16},{1,9},{9,1},{17,25},{25,17},{2,10},{10... | collective-permute-start | bytes 4521992 | tf_op jit(solution)/shard_map/ppermute | solution.py:351
  186.8 91.9 %collective-permute-start.24 = (bf16[17,128,128]{2,1,0:T(8,128)(2,1)}, bf16[17,128,128]{2,1,0:T(8,128)(2,1)}, u32[]{:S(2)}, u32[]{:S(2)}) collective-permute-start(bf16[17,128,128]{2,1,0:T(8,128)(2,1)} %copy-done.27), channel_id=1, source_target_pairs={{0,4},{1,5},{2,6},{3,7},{4,0},{5,1},{6,2},{7,3},{8,12},{9,13},{10,... | collective-permute-start | bytes 1671176 | tf_op jit(solution)/shard_map/ppermute | solution.py:362
  225.0 57.7 %collective-permute-start.25 = (bf16[17,128,128]{2,1,0:T(8,128)(2,1)}, bf16[17,128,128]{2,1,0:T(8,128)(2,1)}, u32[]{:S(2)}, u32[]{:S(2)}) collective-permute-start(bf16[17,128,128]{2,1,0:T(8,128)(2,1)} %copy-done.26), channel_id=1, source_target_pairs={{0,6},{1,7},{2,0},{3,1},{4,2},{5,3},{6,4},{7,5},{8,14},{9,15},{10,... | collective-permute-start | bytes 1671176 | tf_op jit(solution)/shard_map/ppermute | solution.py:362
  227.9 56.3 %collective-permute-start.26 = (bf16[17,128,128]{2,1,0:T(8,128)(2,1)}, bf16[17,128,128]{2,1,0:T(8,128)(2,1)}, u32[]{:S(2)}, u32[]{:S(2)}) collective-permute-start(bf16[17,128,128]{2,1,0:T(8,128)(2,1)} %copy-done.11), channel_id=1, source_target_pairs={{0,1},{1,0},{2,3},{3,2},{4,5},{5,4},{6,7},{7,6},{8,9},{9,8},{10,11... | collective-permute-start | bytes 1671176 | tf_op jit(solution)/shard_map/ppermute | solution.py:356
  285.4 64.2 %collective-permute-start.22 = (bf16[46,128,128]{2,1,0:T(8,128)(2,1)}, bf16[46,128,128]{2,1,0:T(8,128)(2,1)}, u32[]{:S(2)}, u32[]{:S(2)}) collective-permute-start(bf16[46,128,128]{2,1,0:T(8,128)(2,1)} %collective-permute-done.20.refs_5_), channel_id=1, source_target_pairs={{0,8},{8,0},{16,24},{24,16},{1,9},{9,1},{17,25},{25,17},{2,10},{10... | collective-permute-start | bytes 4521992 | tf_op jit(solution)/shard_map/ppermute | solution.py:351
  285.7 65.1 %collective-permute-start.21 = (bf16[46,128,128]{2,1,0:T(8,128)(2,1)}, bf16[46,128,128]{2,1,0:T(8,128)(2,1)}, u32[]{:S(2)}, u32[]{:S(2)}) collective-permute-start(bf16[46,128,128]{2,1,0:T(8,128)(2,1)} %collective-permute-done.17.refs_2_), channel_id=1, source_target_pairs={{0,16},{8,24},{16,0},{24,8},{1,17},{9,25},{17,1},{25,9},{2,18},{10... | collective-permute-start | bytes 4521992 | tf_op jit(solution)/shard_map/ppermute | solution.py:351
  366.5 56.8 %collective-permute-start.37 = (bf16[4,10,128,128]{3,2,1,0:T(8,128)(2,1)}, bf16[4,10,128,128]{3,2,1,0:T(8,128)(2,1)}, u32[]{:S(2)}, u32[]{:S(2)}) collective-permute-start(bf16[4,10,128,128]{3,2,1,0:T(8,128)(2,1)} %gather_fusion.1), channel_id=1, source_target_pairs={{0,1},{1,0},{2,3},{3,2},{4,5},{5,4},{6,7},{7,6},{8,9},{9,8},{10,11... | collective-permute-start | bytes 3932168 | tf_op jit(solution)/shard_map/ppermute | solution.py:356
  528.1 58.5 %reduce-scatter.11.cloned.1.call-start = ((), (), s32[]{:S(2)}) async-start(), calls=%async_computation.6 | async-start | bytes 4718592 | tf_op jit(solution)/shard_map/reduce_scatter | solution.py:813
  538.1 105.6 %all-gather.11.cloned.1.call-start = ((), (), s32[]{:S(2)}) async-start(), calls=%async_computation.7 | async-start | bytes 4718592 | tf_op jit(solution)/shard_map/all_gather | solution.py:834
  597.8 142.9 %reduce-scatter.13.cloned.1.call-start = ((), (), s32[]{:S(2)}) async-start(), calls=%async_computation.8 | async-start | bytes 4718592 | tf_op jit(solution)/shard_map/reduce_scatter | solution.py:858
  688.0 354.9 %reduce-scatter.15.cloned.1.call-start = ((), (), s32[]{:S(2)}) async-start(), calls=%async_computation.9 | async-start | bytes 15073280 | tf_op jit(solution)/shard_map/reduce_scatter | solution.py:866
  781.3 94.4 %collective-permute-start.77 = (bf16[28,128,128]{2,1,0:T(8,128)(2,1)}, bf16[28,128,128]{2,1,0:T(8,128)(2,1)}, u32[]{:S(2)}, u32[]{:S(2)}) collective-permute-start(bf16[28,128,128]{2,1,0:T(8,128)(2,1)} %slice.757), channel_id=1, source_target_pairs={{0,8},{8,0},{16,24},{24,16},{1,9},{9,1},{17,25},{25,17},{2,10},{10... | collective-permute-start | bytes 2752520 | tf_op jit(solution)/shard_map/ppermute | solution.py:351
  782.5 98.1 %collective-permute-start.76 = (bf16[28,128,128]{2,1,0:T(8,128)(2,1)}, bf16[28,128,128]{2,1,0:T(8,128)(2,1)}, u32[]{:S(2)}, u32[]{:S(2)}) collective-permute-start(bf16[28,128,128]{2,1,0:T(8,128)(2,1)} %slice.758), channel_id=1, source_target_pairs={{0,16},{8,24},{16,0},{24,8},{1,17},{9,25},{17,1},{25,9},{2,18},{10... | collective-permute-start | bytes 2752520 | tf_op jit(solution)/shard_map/ppermute | solution.py:351
  789.2 77.7 %collective-permute-start.65 = (bf16[4,1280,128]{2,1,0:T(8,128)(2,1)}, bf16[4,1280,128]{2,1,0:T(8,128)(2,1)}, u32[]{:S(2)}, u32[]{:S(2)}) collective-permute-start(bf16[4,1280,128]{2,1,0:T(8,128)(2,1)} %fusion.19), channel_id=1, source_target_pairs={{0,1},{1,0},{2,3},{3,2},{4,5},{5,4},{6,7},{7,6},{8,9},{9,8},{10,11... | collective-permute-start | bytes 3932168 | tf_op jit(solution)/shard_map/ppermute | solution.py:356
  918.1 64.3 %collective-permute-start.80 = (bf16[17,128,128]{2,1,0:T(8,128)(2,1)}, bf16[17,128,128]{2,1,0:T(8,128)(2,1)}, u32[]{:S(2)}, u32[]{:S(2)}) collective-permute-start(bf16[17,128,128]{2,1,0:T(8,128)(2,1)} %shard_map.320), channel_id=1, source_target_pairs={{0,2},{1,3},{2,4},{3,5},{4,6},{5,7},{6,0},{7,1},{8,10},{9,11},{10,... | collective-permute-start | bytes 1671176 | tf_op jit(solution)/shard_map/ppermute | solution.py:362
  923.0 59.4 %collective-permute-start.81 = (bf16[17,128,128]{2,1,0:T(8,128)(2,1)}, bf16[17,128,128]{2,1,0:T(8,128)(2,1)}, u32[]{:S(2)}, u32[]{:S(2)}) collective-permute-start(bf16[17,128,128]{2,1,0:T(8,128)(2,1)} %shard_map.321), channel_id=1, source_target_pairs={{0,4},{1,5},{2,6},{3,7},{4,0},{5,1},{6,2},{7,3},{8,12},{9,13},{10,... | collective-permute-start | bytes 1671176 | tf_op jit(solution)/shard_map/ppermute | solution.py:362
  926.5 56.4 %collective-permute-start.82 = (bf16[17,128,128]{2,1,0:T(8,128)(2,1)}, bf16[17,128,128]{2,1,0:T(8,128)(2,1)}, u32[]{:S(2)}, u32[]{:S(2)}) collective-permute-start(bf16[17,128,128]{2,1,0:T(8,128)(2,1)} %shard_map.322), channel_id=1, source_target_pairs={{0,6},{1,7},{2,0},{3,1},{4,2},{5,3},{6,4},{7,5},{8,14},{9,15},{10,... | collective-permute-start | bytes 1671176 | tf_op jit(solution)/shard_map/ppermute | solution.py:362
  1042.9 122.7 %collective-permute-start.53 = (bf16[92,128,128]{2,1,0:T(8,128)(2,1)}, bf16[92,128,128]{2,1,0:T(8,128)(2,1)S(1)}, u32[]{:S(2)}, u32[]{:S(2)}) collective-permute-start(bf16[92,128,128]{2,1,0:T(8,128)(2,1)} %reduce-scatter.15.cloned.1.call-done.refs_0_), channel_id=1, source_target_pairs={{0,1},{1,0},{2,3},{3,2},{4,5},{5,4},{6,7},{7,6},{8,9},{9,8},{10,11... | collective-permute-start | bytes 9043976 | tf_op jit(solution)/shard_map/ppermute | solution.py:356
  1057.8 91.6 %collective-permute-start.89 = (bf16[33,128,128]{2,1,0:T(8,128)(2,1)}, bf16[33,128,128]{2,1,0:T(8,128)(2,1)}, u32[]{:S(2)}, u32[]{:S(2)}) collective-permute-start(bf16[33,128,128]{2,1,0:T(8,128)(2,1)} %get-tuple-element.904), channel_id=1, source_target_pairs={{0,4},{1,5},{2,6},{3,7},{4,0},{5,1},{6,2},{7,3},{8,12},{9,13},{10,... | collective-permute-start | bytes 3244040 | tf_op jit(solution)/shard_map/ppermute | solution.py:362
  1070.4 93.4 %collective-permute-start.57 = (f32[3200]{0:T(1024)S(1)}, f32[3200]{0:T(1024)S(1)}, u32[]{:S(2)}, u32[]{:S(2)}) collective-permute-start(f32[3200]{0:T(1024)S(1)} %add_add_fusion.9), channel_id=1, source_target_pairs={{0,1},{1,0},{2,3},{3,2},{4,5},{5,4},{6,7},{7,6},{8,9},{9,8},{10,11... | collective-permute-start | bytes 38408 | tf_op jit(solution)/shard_map/ppermute | solution.py:356
  1191.1 75.7 %collective-permute-start.59 = (bf16[27,128,128]{2,1,0:T(8,128)(2,1)}, bf16[27,128,128]{2,1,0:T(8,128)(2,1)}, u32[]{:S(2)}, u32[]{:S(2)}) collective-permute-start(bf16[27,128,128]{2,1,0:T(8,128)(2,1)} %copy-done.24), channel_id=1, source_target_pairs={{0,4},{1,5},{2,6},{3,7},{4,0},{5,1},{6,2},{7,3},{8,12},{9,13},{10,... | collective-permute-start | bytes 2654216 | tf_op jit(solution)/shard_map/ppermute | solution.py:362
  1192.1 77.4 %collective-permute-start.60 = (bf16[27,128,128]{2,1,0:T(8,128)(2,1)}, bf16[27,128,128]{2,1,0:T(8,128)(2,1)}, u32[]{:S(2)}, u32[]{:S(2)}) collective-permute-start(bf16[27,128,128]{2,1,0:T(8,128)(2,1)} %copy-done.23), channel_id=1, source_target_pairs={{0,6},{1,7},{2,0},{3,1},{4,2},{5,3},{6,4},{7,5},{8,14},{9,15},{10,... | collective-permute-start | bytes 2654216 | tf_op jit(solution)/shard_map/ppermute | solution.py:362
  1209.3 63.6 %collective-permute-start.97 = (bf16[13,128,128]{2,1,0:T(8,128)(2,1)}, bf16[13,128,128]{2,1,0:T(8,128)(2,1)}, u32[]{:S(2)}, u32[]{:S(2)}) collective-permute-start(bf16[13,128,128]{2,1,0:T(8,128)(2,1)} %collective-permute-done.93.refs_19_), channel_id=1, source_target_pairs={{0,1},{1,0},{2,3},{3,2},{4,5},{5,4},{6,7},{7,6},{8,9},{9,8},{10,11... | collective-permute-start | bytes 1277960 | tf_op jit(solution)/shard_map/ppermute | solution.py:356
  1209.7 63.2 %collective-permute-start.61 = (bf16[27,128,128]{2,1,0:T(8,128)(2,1)}, bf16[27,128,128]{2,1,0:T(8,128)(2,1)}, u32[]{:S(2)}, u32[]{:S(2)}) collective-permute-start(bf16[27,128,128]{2,1,0:T(8,128)(2,1)} %shard_map.313.refs_0_), channel_id=1, source_target_pairs={{0,1},{1,0},{2,3},{3,2},{4,5},{5,4},{6,7},{7,6},{8,9},{9,8},{10,11... | collective-permute-start | bytes 2654216 | tf_op jit(solution)/shard_map/ppermute | solution.py:356
  1211.2 61.7 %collective-permute-start.62 = (bf16[27,128,128]{2,1,0:T(8,128)(2,1)}, bf16[27,128,128]{2,1,0:T(8,128)(2,1)}, u32[]{:S(2)}, u32[]{:S(2)}) collective-permute-start(bf16[27,128,128]{2,1,0:T(8,128)(2,1)} %collective-permute-done.58.refs_1_), channel_id=1, source_target_pairs={{0,1},{1,0},{2,3},{3,2},{4,5},{5,4},{6,7},{7,6},{8,9},{9,8},{10,11... | collective-permute-start | bytes 2654216 | tf_op jit(solution)/shard_map/ppermute | solution.py:356
  (296 other events, 4345.0 us)
Sparse Core Ops, SparseCore 0:
  154.3 123.5 all-gather.6
  463.5 48.2 all-gather.8
  538.2 48.3 reduce-scatter.10
  598.0 45.6 all-gather.10
  688.1 48.3 reduce-scatter.12
  743.0 178.7 reduce-scatter.14

commit v6 on v4

--- a/solution.py
+++ b/solution.py
@@ -122,9 +122,11 @@
 
 
 def tile_kernel_call(kernel, index, arrays, out_shape, out_specs, steps):
+    moved = sum(math.prod(one.shape) * 2 for one in jax.tree.leaves(out_shape))
     return pl.pallas_call(
         kernel,
         grid=(steps,),
+        cost_estimate=pl.CostEstimate(flops=0, transcendentals=0, bytes_accessed=2 * moved),
         out_shape=out_shape,
         in_specs=[pl.BlockSpec(memory_space=pltpu.SMEM)]
         + [pl.BlockSpec(memory_space=pl.ANY)] * len(arrays),
@@ -174,75 +176,71 @@
     )
 
 
-def join_tiles(arrays, index, row_blocks, first_columns, second_columns):
+def join_tiles(arrays, index, row_blocks, columns):
     tile = arrays[0].shape[-1]
-    first_count = row_blocks * first_columns
     steps = 4
     each = row_blocks // steps
 
     def kernel(index_ref, *refs):
-        sources, first, second, sem = refs[:-3], refs[-3], refs[-2], refs[-1]
+        sources, outs, sem = refs[: len(arrays)], refs[len(arrays) : -1], refs[-1]
         base = pl.program_id(0) * each
-        for out, start, columns in ((first, 0, first_columns), (second, first_count, second_columns)):
-
-            def step(i, carry, out=out, start=start, columns=columns):
-                row = i // columns
-                column = i - row * columns
+        start = 0
+        for out, width in zip(outs, columns):
+
+            def step(i, carry, out=out, start=start, width=width):
+                row = i // width
+                column = i - row * width
                 target = out.at[
                     pl.ds(pl.multiple_of(row * tile, tile), tile),
                     pl.ds(pl.multiple_of(column * tile, tile), tile),
                 ]
-                start_copy(sources, index_ref[start + base * columns + i], target, sem)
+                start_copy(sources, index_ref[start + base * width + i], target, sem)
                 return carry
 
-            lax.fori_loop(0, each * columns, step, 0)
-        pltpu.make_async_copy(first, first, sem).wait()
-        pltpu.make_async_copy(second, second, sem).wait()
+            lax.fori_loop(0, each * width, step, 0)
+            start = start + row_blocks * width
+        for out in outs:
+            pltpu.make_async_copy(out, out, sem).wait()
 
     total = sum(array.shape[0] for array in arrays)
     out_shape = tuple(
-        jax.ShapeDtypeStruct((row_blocks * tile, count * tile), arrays[0].dtype)
-        for count in (first_columns, second_columns)
-    )
-    out_specs = tuple(
-        pl.BlockSpec((each * tile, count * tile), lambda i: (i, 0))
-        for count in (first_columns, second_columns)
-    )
+        jax.ShapeDtypeStruct((row_blocks * tile, width * tile), arrays[0].dtype)
+        for width in columns
+    )
+    out_specs = tuple(pl.BlockSpec((each * tile, width * tile), lambda i: (i, 0)) for width in columns)
     return tile_kernel_call(
         kernel, jnp.clip(index, 0, total - 1), arrays, out_shape, out_specs, steps
     )
 
 
-def cut_tiles(first, second, index, tile):
-    row_blocks = first.shape[0] // tile
-    first_columns = first.shape[1] // tile
-    second_columns = second.shape[1] // tile
-    first_count = row_blocks * first_columns
+def cut_tiles(matrices, index, tile):
+    row_blocks = matrices[0].shape[0] // tile
+    widths = [matrix.shape[1] // tile for matrix in matrices]
     count = index.shape[0]
     steps = steps_of(count)
     each = count // steps
 
-    def kernel(index_ref, first_ref, second_ref, out, sem):
+    def kernel(index_ref, *refs):
+        sources, out, sem = refs[:-2], refs[-2], refs[-1]
         base = pl.program_id(0) * each
 
         def step(i, carry):
             place = index_ref[base + i]
-
-            def send(ref, local, columns):
-                row = pl.multiple_of((local // columns) * tile, tile)
-                column = pl.multiple_of((local % columns) * tile, tile)
-                pltpu.make_async_copy(
-                    ref.at[pl.ds(row, tile), pl.ds(column, tile)], out.at[i], sem
-                ).start()
-
-            @pl.when(place < first_count)
-            def _():
-                send(first_ref, place, first_columns)
-
-            @pl.when(place >= first_count)
-            def _():
-                send(second_ref, place - first_count, second_columns)
-
+            start = 0
+            for ref, width in zip(sources, widths):
+                size = row_blocks * width
+
+                @pl.when((place >= start) & (place < start + size))
+                def _(ref=ref, start=start, width=width):
+                    row = (place - start) // width
+                    column = place - start - row * width
+                    source = ref.at[
+                        pl.ds(pl.multiple_of(row * tile, tile), tile),
+                        pl.ds(pl.multiple_of(column * tile, tile), tile),
+                    ]
+                    pltpu.make_async_copy(source, out.at[i], sem).start()
+
+                start = start + size
             return carry
 
         lax.fori_loop(0, each, step, 0)
@@ -250,9 +248,9 @@
 
     return tile_kernel_call(
         kernel,
-        jnp.clip(index, 0, first_count + row_blocks * second_columns - 1),
-        [first, second],
-        jax.ShapeDtypeStruct((count, tile, tile), first.dtype),
+        jnp.clip(index, 0, row_blocks * sum(widths) - 1),
+        matrices,
+        jax.ShapeDtypeStruct((count, tile, tile), matrices[0].dtype),
         pl.BlockSpec((each, tile, tile), lambda i: (i, 0, 0)),
         steps,
     )
@@ -398,25 +396,28 @@
     return [values[0]] + [chip_shift(values[offset], offset) for offset in range(1, len(values))]
 
 
-def fsdp_sum(value):
-    size = lax.axis_size("fsdp")
-    chips = size // 2
-    chip = lax.axis_index("fsdp") // 2
+def core_pair(value):
+    other = core_swap(value)
     even = lax.axis_index("fsdp") % 2 == 0
-    shares = value.reshape((chips, 2, value.shape[0] // size) + value.shape[1:])
-    kept = jnp.where(even, shares[:, 0], shares[:, 1])
-    given = jnp.where(even, shares[:, 1], shares[:, 0])
-    kept = kept + core_swap(given.astype(jnp.bfloat16)).astype(jnp.float32)
-    kept = kept[(chip + jnp.arange(chips)) % chips]
-    total = kept[0]
-    for offset in range(1, chips):
-        total = total + chip_shift(kept[offset].astype(jnp.bfloat16), offset).astype(jnp.float32)
-    total = total.astype(jnp.bfloat16)
-    parts = jnp.stack([total] + [chip_shift(total, offset) for offset in range(1, chips)])
-    parts = parts[(chip - jnp.arange(chips)) % chips]
-    other = core_swap(parts)
-    both = jnp.where(even, jnp.stack([parts, other], axis=1), jnp.stack([other, parts], axis=1))
-    return both.reshape(value.shape)
+    return jnp.where(even, jnp.stack([value, other]), jnp.stack([other, value]))
+
+
+def small_sum(value):
+    seq_size = lax.axis_size("seq")
+    even = lax.axis_index("fsdp") % 2 == 0
+    low = value.astype(jnp.bfloat16)
+    parts = low.reshape((seq_size, 2, low.shape[0] // (2 * seq_size)) + low.shape[1:])
+    kept = jnp.where(even, parts[:, 0], parts[:, 1]).astype(jnp.float32)
+    given = jnp.where(even, parts[:, 1], parts[:, 0])
+    kept = kept + core_swap(given).astype(jnp.float32)
+    return seq_sum(kept.reshape((-1,) + low.shape[1:]), jnp.bfloat16, True).astype(jnp.bfloat16)
+
+
+def small_all(kept):
+    even = lax.axis_index("fsdp") % 2 == 0
+    empty = jnp.zeros_like(kept)
+    both = jnp.where(even, jnp.stack([kept, empty]), jnp.stack([empty, kept]))
+    return lax.psum(both, "fsdp").reshape((2 * kept.shape[0],) + kept.shape[1:])
 
 
 def on_device(
@@ -479,6 +480,7 @@
     attn_hold = (room(attn_count, 1.0 / chips) + 1) // 2 + 1
     ffn_room = (room(2 * mine, ffn_share / chips) + 1) // 2
     ffn_hold = (room(ffn_count, 1.0 / seq_size) + 3) // 4 * 4
+    ffn_half = ffn_hold // 2
 
     def tile_places(owner):
         row = owner // columns
@@ -617,7 +619,11 @@
     attn_join = pick(
         (attn_to.reshape(1, -1) == my_seq)
         & (attn_place.reshape(1, -1) == jnp.arange(attn_count)[:, None]),
-        ((2 * slot_chip + attn_core) * attn_hold + attn_order).reshape(1, -1),
+        (
+            jnp.where(attn_core == my_core, 0, chips * attn_hold)
+            + (my_chip - slot_chip) % chips * attn_hold
+            + attn_order
+        ).reshape(1, -1),
     )
     ffn_pack = pick(
         (chip_slots[0] == ((my_chip + shifts) % chips)[:, None, None])
@@ -631,7 +637,9 @@
     ffn_join = pick(
         (ffn_to.reshape(1, -1) == my_fsdp)
         & (ffn_place.reshape(1, -1) == jnp.arange(ffn_count)[:, None]),
-        (slot_seq * ffn_hold + ffn_rank).reshape(1, -1),
+        (
+            ffn_rank // ffn_half * (seq_size * ffn_half) + slot_seq * ffn_half + ffn_rank % ffn_half
+        ).reshape(1, -1),
     )
     master_low = tile_master.astype(bf16)
     masters = [master_low, core_swap(master_low)]
@@ -643,16 +651,24 @@
     attn_got = seq_exchange([attn_sent[i] for i in range(seq_size)])
     pack_tokens = seq_gather(tokens[0])
     gain_full = seq_ordered(gains.astype(bf16))
-    small_got = seq_ordered(small_master.astype(bf16))
+    small_rows = small_master.shape[0] // 2
+    small_half = lax.dynamic_slice_in_dim(small_master, my_core * small_rows, small_rows)
+    small_got = core_pair(seq_ordered(small_half.astype(bf16))).transpose(1, 0, 2, 3, 4)
     ffn_got, attn_got, pack_tokens, gain_full, small_got = lax.optimization_barrier(
         (ffn_got, attn_got, pack_tokens, gain_full, small_got)
     )
     attn_kept = gather_tiles(attn_got, attn_keep)
-    attn_all = lax.all_gather(attn_kept, "fsdp", axis=0, tiled=True)
     ffn_other = [core_swap(value) for value in ffn_got]
-    ffn_kept = gather_tiles(ffn_got + ffn_other, ffn_keep)
-    ffn_all = lax.all_gather(ffn_kept, "seq", axis=0, tiled=True)
-    w_first, w_out = join_tiles([attn_all], attn_join, row_blocks, attn_first, query_each)
+    ffn_kept = [
+        gather_tiles(ffn_got + ffn_other, ffn_keep[:ffn_half]),
+        gather_tiles(ffn_got + ffn_other, ffn_keep[ffn_half:]),
+    ]
+    ffn_kept, attn_kept = lax.optimization_barrier((ffn_kept, attn_kept))
+    ffn_all = [lax.all_gather(value, "seq", axis=0, tiled=True) for value in ffn_kept]
+    attn_all = [attn_kept] + [chip_shift(attn_kept, offset) for offset in range(1, chips)]
+    attn_all = attn_all + [core_swap(value) for value in attn_all]
+    attn_all, ffn_all[0] = lax.optimization_barrier((attn_all, ffn_all[0]))
+    w_first, w_out = join_tiles(attn_all, attn_join, row_blocks, (attn_first, query_each))
 
     def slow_fetch(to, me, place, columns_of):
         def fetch(_, kept):
@@ -662,7 +678,7 @@
                 (to.reshape(1, -1) == me) & (place.reshape(1, -1) == jnp.arange(count)[:, None]),
                 jnp.arange(tiles)[None, :],
             )
-            return join_tiles([whole], index, row_blocks, *columns_of)
+            return join_tiles([whole], index, row_blocks, columns_of)
 
         return fetch
 
@@ -748,9 +764,10 @@
     laurel_normed, laurel_pull = jax.vjp(rms_norm, right_pre, gain_laurel)
     second_sum = (first_sum + normed + laurel_normed) * ROOT_HALF
     feed_normed, feed_pull = jax.vjp(rms_norm, second_sum, gain_pre)
-    ffn_all, feed_own = lax.optimization_barrier((ffn_all, feed_normed.astype(bf16)))
+    feed_own = feed_normed.astype(bf16)
+    ffn_all, _ = lax.optimization_barrier((ffn_all, feed_own))
     feed_low = lax.all_gather(feed_own, "fsdp", axis=0, tiled=True)
-    w_both, w_down = join_tiles([ffn_all], ffn_join, row_blocks, ffn_first, ffn_each)
+    w_both, w_down = join_tiles(ffn_all, ffn_join, row_blocks, (ffn_first, ffn_each))
     w_both, w_down = lax.fori_loop(
         0, slow_steps, slow_fetch(ffn_to, my_fsdp, ffn_place, (ffn_first, ffn_each)), (w_both, w_down)
     )
@@ -793,7 +810,7 @@
         & (ffn_rank.reshape(seq_size, 1, -1) == jnp.arange(ffn_hold)[None, :, None]),
         ffn_place.reshape(seq_size, 1, -1),
     )
-    ffn_parts = cut_tiles(both_grad_w, down_grad_w, ffn_cut.reshape(-1), tile)
+    ffn_parts = cut_tiles([both_grad_w, down_grad_w], ffn_cut.reshape(-1), tile)
     ffn_parts, grad_feed = lax.optimization_barrier((ffn_parts, grad_feed))
     ffn_sum = lax.psum_scatter(ffn_parts, "seq", scatter_dimension=0, tiled=True)
 
@@ -848,7 +865,6 @@
         ],
         axis=1,
     )
-    small_tiles_grad = split_tiles(small_full, tile)
     gain_grad = jnp.concatenate(
         [
             grad_gain_in,
@@ -861,14 +877,9 @@
             grad_gain_key,
         ]
     )
-    small_part = seq_sum(small_tiles_grad, bf16, True)
-    small_grad = fsdp_sum(small_part.reshape(-1, tile)).reshape(small_part.shape)
+    small_part = small_sum(split_tiles(small_full, tile).reshape(-1, tile))
     gain_part = seq_sum(gain_grad, f32, True)
     gain_part = gain_part + core_swap(gain_part)
-    gain_grad_mine = gain_part
-    for offset in range(1, chips):
-        gain_grad_mine = gain_grad_mine + chip_shift(gain_part, offset)
-
     ffn_back = pick(
         (seq_slots[5][None, None, :] == ((my_chip + shifts) % chips)[:, None, None])
         & (seq_slots[0][None, None, :] // 2 == my_chip)
@@ -876,27 +887,46 @@
         & (seq_slots[4][None, None, :] == (my_core * ffn_room + jnp.arange(ffn_room))[None, :, None]),
         jnp.where(seq_slots[0] == my_fsdp, 0, ffn_hold) + seq_slots[1],
     )
-    ffn_sum, small_grad, gain_grad_mine = lax.optimization_barrier(
-        (ffn_sum, small_grad, gain_grad_mine)
-    )
-    ffn_sums = [ffn_sum, core_swap(ffn_sum)]
-    ffn_return = [gather_tiles(ffn_sums, ffn_back[i]) for i in range(chips)]
-    ffn_returned = chip_exchange(ffn_return)
-    ffn_returned = ffn_returned + [core_swap(value) for value in ffn_returned]
-
-    attn_cut = pick(
-        (attn_key_chip[:, None, None, :] == (2 * my_seq + jnp.arange(2))[None, :, None, None])
-        & (attn_order_chip[:, None, None, :] == jnp.arange(attn_hold)[None, None, :, None]),
-        by_chip(attn_place)[:, None, None, :],
-    )
+    near = (my_chip + shifts) % chips
+    near_key = attn_key_chip[near][:, None, :]
+    near_order = attn_order_chip[near][:, None, :]
+    near_place = by_chip(attn_place)[near][:, None, :]
+
+    def attn_cut(core):
+        index = pick(
+            (near_key == 2 * my_seq + core)
+            & (near_order == jnp.arange(attn_hold)[None, :, None]),
+            near_place,
+        )
+        return cut_tiles([first_grad_w, out_grad_w], index.reshape(-1), tile)
+
+    attn_given, attn_own = attn_cut(1 - my_core), attn_cut(my_core)
+    def added(one, two):
+        return one.astype(f32) + two.astype(f32)
+
+    attn_own = added(attn_own, core_swap(attn_given)).reshape(chips, attn_hold, tile, tile)
+    attn_sum = attn_own[0]
+    for offset in range(1, chips):
+        attn_sum = attn_sum + chip_shift(attn_own[offset].astype(bf16), offset).astype(f32)
+    attn_sum = attn_sum.astype(bf16)
     attn_back = pick(
         (column_slots[3][None, None, :] == (my_seq ^ flips)[:, None, None])
         & (column_slots[0][None, None, :] == my_key)
         & (column_slots[2][None, None, :] == jnp.arange(attn_room)[None, :, None]),
         column_slots[1],
     )
-    attn_parts = cut_tiles(first_grad_w, out_grad_w, attn_cut.reshape(-1), tile)
-    attn_sum = lax.psum_scatter(attn_parts, "fsdp", scatter_dimension=0, tiled=True)
+    ffn_sum, attn_sum, small_part, gain_part = lax.optimization_barrier(
+        (ffn_sum, attn_sum, small_part, gain_part)
+    )
+    ffn_sums = [ffn_sum, core_swap(ffn_sum)]
+    ffn_return = [gather_tiles(ffn_sums, ffn_back[i]) for i in range(chips)]
+    ffn_return, gain_part, small_part = lax.optimization_barrier((ffn_return, gain_part, small_part))
+    small_grad = small_all(small_part).reshape(small_master.shape)
+    ffn_returned = chip_exchange(ffn_return)
+    ffn_returned = ffn_returned + [core_swap(value) for value in ffn_returned]
+    gain_grad_mine = gain_part
+    for offset in range(1, chips):
+        gain_grad_mine = gain_grad_mine + chip_shift(gain_part, offset)
     attn_returned = seq_exchange([gather_tiles([attn_sum], attn_back[i]) for i in range(seq_size)])
     attn_returned = attn_returned + [core_swap(value) for value in attn_returned]
     slot_grad = jnp.where(my_slots[0] >= 0, my_slots[1], 2 * half + my_slots[2])

time: 1250 us -> 1270 us (1.016); the launches traced: 1240 us -> 1250 us
    ppermute x15, waiting for transfers between devices: 135 us -> 331 us  [chip_shift(): lax.ppermute(value, 'fsdp', [(i, (i // 2 + offset) % chips * 2 + i % 2) f...]
    all_gather x2, waiting for transfers between devices: 154 us -> 18.2 us  [on_device(): lax.all_gather(value, 'seq', axis=0, tiled=True)]
    reduce_scatter x1 -> x0, waiting for transfers between devices: 51.3 us -> none  [on_device(): lax.psum_scatter(attn_parts, 'fsdp', scatter_dimension=0, tiled=True)]
    ppermute x32, waiting for transfers between devices: 198 us -> 171 us  [seq_swap(): return lax.ppermute(value, 'seq', [(i, i ^ flip) for i in range(size)])]
    psum x0 -> x1, waiting for transfers between devices: none -> 23.7 us  [small_all(): return lax.psum(both, 'fsdp').reshape((2 * kept.shape[0],) + kept.shape[1:])]
    pallas_call x19 -> x21, Pallas kernels: 96.8 us -> 110 us  [tile_kernel_call(): pl.pallas_call(kernel, grid=(steps,), cost_estimate=pl.CostEstimate(flops...]
    unnamed x378 -> x422, local copies, waits for them, and re-layouts: 57.5 us -> 53.8 us
  transfers between devices with their start and end apart: 72 -> 77, of which waited for: 34 -> 32; matrix products, arithmetic and copies ran while one was open for 16% -> 16% of each run, Pallas kernels for 7% -> 6%
where the time goes in v6:
time: 1270 us; the launch traced here: 1250 us
  waiting for transfers between devices  694 us (55%)
  Pallas kernels  158 us (12%)
  other arithmetic  103 us (8%)
  local copies, waits for them, and re-layouts  102 us (8%)
  matrix products  99.7 us (8%)
  starting transfers between devices  69.7 us (5%)
  between operations  18.3 us (1%)
    ppermute x15, waiting for transfers between devices, chip_shift(): lax.ppermute(value, 'fsdp', [(i, (i // 2 + offset) % chips * 2 + i % 2) f...  331 us
    ppermute x32, waiting for transfers between devices, seq_swap(): return lax.ppermute(value, 'seq', [(i, i ^ flip) for i in range(size)])  171 us
    pallas_call x21, Pallas kernels, tile_kernel_call(): pl.pallas_call(kernel, grid=(steps,), cost_estimate=pl.CostEstimate(flops...  110 us
    unnamed x422, local copies, waits for them, and re-layouts  53.8 us
    reduce_scatter x1, waiting for transfers between devices, on_device(): lax.psum_scatter(matmul_flip(hidden_low, w_down).astype(bf16), 'fsdp', sc...  48.4 us
    all_gather x1, waiting for transfers between devices, on_device(): feed_low = lax.all_gather(feed_own, 'fsdp', axis=0, tiled=True)  48.3 us
    pallas_call x2, Pallas kernels, rotate_update(): pl.pallas_call(kernel, grid=(count // each,), out_shape=(shape, shape, sh...  48.3 us
    all_gather x1, waiting for transfers between devices, on_device(): lax.all_gather(grad_down.astype(bf16), 'fsdp', axis=0, tiled=True)  45.8 us
  transfers between devices with their start and end apart: 77, of which 32 were waited for; matrix products, arithmetic and copies ran while one was open for 16% of the time, Pallas kernels for 6%

profile of v6, /device:TPU:9, one launch (start us, length us, event | category | flops | bytes accessed | tf_op | source)
XLA Modules:
  0.0 1245.3 jit_solution(17178634871444763381)
XLA Ops:
  27.4 9.1 convert_reduce_fusion
  79.1 8.2 collective-permute-done.4.refs_1_
  98.8 74.9 %collective-permute-done.2.refs_2_ = bf16[37,128,128]{2,1,0:T(8,128)(2,1)} collective-permute-done((bf16[37,128,128]{2,1,0:T(8,128)(2,1)}, bf16[37,128,128]{2,1,0:T(8,128)(2,1)}, u32[]{:S(2)}, u32[]{:S(2)}) %collective-permute-start.2) | collective-permute-done | bytes 1212448 | tf_op jit(solution)/shard_map/ppermute | solution.py:364
  205.2 18.3 %collective-permute-done.21.refs_1_ = bf16[33,128,128]{2,1,0:T(8,128)(2,1)S(1)} collective-permute-done((bf16[33,128,128]{2,1,0:T(8,128)(2,1)S(1)}, bf16[33,128,128]{2,1,0:T(8,128)(2,1)S(1)}, u32[]{:S(2)}, u32[]{:S(2)}) %collective-permute-start.21) | collective-permute-done | bytes 1081376 | tf_op jit(solution)/shard_map/ppermute | solution.py:364
  225.6 65.5 %collective-permute-done.22.refs_2_ = bf16[33,128,128]{2,1,0:T(8,128)(2,1)S(1)} collective-permute-done((bf16[33,128,128]{2,1,0:T(8,128)(2,1)S(1)}, bf16[33,128,128]{2,1,0:T(8,128)(2,1)S(1)}, u32[]{:S(2)}, u32[]{:S(2)}) %collective-permute-start.22) | collective-permute-done | bytes 1081376 | tf_op jit(solution)/shard_map/ppermute | solution.py:364
  299.2 11.9 shard_map.265
  341.8 11.3 collective-permute-done.28
  365.6 19.5 %collective-permute-done.29 = bf16[128,2048]{1,0:T(8,128)(2,1)S(1)} collective-permute-done((bf16[128,2048]{1,0:T(8,128)(2,1)S(1)}, bf16[128,2048]{1,0:T(8,128)(2,1)S(1)}, u32[]{:S(2)}, u32[]{:S(2)}) %collective-permute-start.29) | collective-permute-done | bytes 524320 | tf_op jit(solution)/shard_map/ppermute | solution.py:353
  385.3 22.6 %collective-permute-done.31 = bf16[128,2048]{1,0:T(8,128)(2,1)S(1)} collective-permute-done((bf16[128,2048]{1,0:T(8,128)(2,1)S(1)}, bf16[128,2048]{1,0:T(8,128)(2,1)S(1)}, u32[]{:S(2)}, u32[]{:S(2)}) %collective-permute-start.31) | collective-permute-done | bytes 524320 | tf_op jit(solution)/shard_map/ppermute | solution.py:353
  411.5 18.2 %all-gather.11.cloned.1.call-done.refs_1_ = bf16[264,128,128]{2,1,0:T(8,128)(2,1)} async-done(((bf16[66,128,128]{2,1,0:T(8,128)(2,1)}), bf16[264,128,128]{2,1,0:T(8,128)(2,1)}) %all-gather.11.cloned.1.call-update) | async-done | bytes 8650768 | tf_op jit(solution)/shard_map/all_gather | solution.py:667
  436.7 14.2 %shard_map.266 = (bf16[2048,2048]{1,0:T(8,128)(2,1)}, bf16[2048,1024]{1,0:T(8,128)(2,1)}) custom-call(s32[384]{0:T(512)S(1)} %broadcast_clamp_fusion.6.index_ref, bf16[264,128,128]{2,1,0:T(8,128)(2,1)S(1)} %copy-done.6, bf16[264,128,128]{2,1,0:T(8,128)(2,1)S(1)} %copy-done.7), custom_call_target="tpu_custom_call" | custom-call | bytes 25165824 | tf_op jit(solution)/shard_map/pallas_call | solution.py:126
  451.8 48.3 %all-gather.9.cloned.1.call-done = bf16[1024,2048]{1,0:T(8,128)(2,1)} async-done(((bf16[128,2048]{1,0:T(8,128)(2,1)}), bf16[1024,2048]{1,0:T(8,128)(2,1)}) %all-gather.9.cloned.1.call-update) | async-done | bytes 4194320 | tf_op jit(solution)/shard_map/all_gather | solution.py:769
  500.1 12.7 %fusion.346 = f32[1024,2048]{1,0:T(8,128)S(1)} fusion(bf16[1024,2048]{1,0:T(8,128)(2,1)} %all-gather.9.cloned.1.call-done, bf16[2048,2048]{1,0:T(8,128)(2,1)} %get-tuple-element.350), kind=kOutput, calls=%fused_computation.859 | convolution fusion | flops 8589934592 | bytes 20971520 | tf_op jit(solution)/shard_map/dot_general | solution.py:61
  524.1 48.4 %reduce-scatter.11.cloned.1.call-done = bf16[128,2048]{1,0:T(8,128)(2,1)} async-done(((bf16[1024,2048]{1,0:T(8,128)(2,1)}), bf16[128,2048]{1,0:T(8,128)(2,1)}) %reduce-scatter.11.cloned.1.call-update) | async-done | bytes 524304 | tf_op jit(solution)/shard_map/reduce_scatter | solution.py:778
  582.0 45.8 %all-gather.13.cloned.1.call-done = bf16[1024,2048]{1,0:T(8,128)(2,1)} async-done(((bf16[128,2048]{1,0:T(8,128)(2,1)}), bf16[1024,2048]{1,0:T(8,128)(2,1)}) %all-gather.13.cloned.1.call-update) | async-done | bytes 4194320 | tf_op jit(solution)/shard_map/all_gather | solution.py:799
  627.8 12.4 fusion.11
  642.2 12.6 %convolution_convert_fusion.1 = bf16[1024,2048]{1,0:T(8,128)(2,1)} fusion(bf16[2048,2048]{1,0:T(8,128)(2,1)} %get-tuple-element.350, bf16[1024,1024]{1,0:T(8,128)(2,1)S(1)} %get-tuple-element.570, bf16[1024,1024]{1,0:T(8,128)(2,1)S(1)} %get-tuple-element.569), kind=kOutput, calls=%fused_computation.45 | convolution fusion | flops 8600420352 | bytes 16777216 | tf_op jit(solution)/shard_map/dot_general | solution.py:65
  658.3 7.3 convolution_convert_fusion.2.refs_1_
  665.7 9.6 convolution_convert_fusion.refs_0_
  678.6 19.8 %shard_map.267 = bf16[528,128,128]{2,1,0:T(8,128)(2,1)S(1)} custom-call(s32[528]{0:T(1024)S(1)} %min.221.index_ref, bf16[2048,2048]{1,0:T(8,128)(2,1)S(1)} %convolution_convert_fusion.refs_0_, bf16[2048,1024]{1,0:T(8,128)(2,1)S(1)} %convolution_convert_fusion.2.refs_1_), custom_call_target="tpu_custom_call" | custom-call | bytes 34603008 | tf_op jit(solution)/shard_map/pallas_call | solution.py:126
  724.6 19.7 %collective-permute-done.32 = bf16[128,2048]{1,0:T(8,128)(2,1)S(1)} collective-permute-done((bf16[128,2048]{1,0:T(8,128)(2,1)S(1)}, bf16[128,2048]{1,0:T(8,128)(2,1)S(1)}, u32[]{:S(2)}, u32[]{:S(2)}) %collective-permute-start.32) | collective-permute-done | bytes 524320 | tf_op jit(solution)/shard_map/ppermute | solution.py:353
  745.5 22.1 %collective-permute-done.34 = bf16[128,2048]{1,0:T(8,128)(2,1)S(1)} collective-permute-done((bf16[128,2048]{1,0:T(8,128)(2,1)S(1)}, bf16[128,2048]{1,0:T(8,128)(2,1)S(1)}, u32[]{:S(2)}, u32[]{:S(2)}) %collective-permute-start.34) | collective-permute-done | bytes 524320 | tf_op jit(solution)/shard_map/ppermute | solution.py:353
  784.1 9.6 collective-permute-done.35
  832.4 15.0 %collective-permute-done.36 = bf16[128,2048]{1,0:T(8,128)(2,1)S(1)} collective-permute-done((bf16[128,2048]{1,0:T(8,128)(2,1)S(1)}, bf16[128,2048]{1,0:T(8,128)(2,1)S(1)}, u32[]{:S(2)}, u32[]{:S(2)}) %collective-permute-start.36) | collective-permute-done | bytes 524320 | tf_op jit(solution)/shard_map/ppermute | solution.py:353
  847.4 12.9 %collective-permute-done.38 = bf16[128,2048]{1,0:T(8,128)(2,1)S(1)} collective-permute-done((bf16[128,2048]{1,0:T(8,128)(2,1)S(1)}, bf16[128,2048]{1,0:T(8,128)(2,1)S(1)}, u32[]{:S(2)}, u32[]{:S(2)}) %collective-permute-start.38) | collective-permute-done | bytes 524320 | tf_op jit(solution)/shard_map/ppermute | solution.py:353
  878.2 8.8 fusion.323
  898.9 20.8 %collective-permute-done.45 = bf16[1280,128]{1,0:T(8,128)(2,1)S(1)} collective-permute-done((bf16[1280,128]{1,0:T(8,128)(2,1)S(1)}, bf16[1280,128]{1,0:T(8,128)(2,1)S(1)}, u32[]{:S(2)}, u32[]{:S(2)}) %collective-permute-start.45) | collective-permute-done | bytes 327712 | tf_op jit(solution)/shard_map/ppermute | solution.py:353
  921.8 60.2 %collective-permute-done.41 = bf16[33,128,128]{2,1,0:T(8,128)(2,1)S(1)} collective-permute-done((bf16[33,128,128]{2,1,0:T(8,128)(2,1)S(1)}, bf16[33,128,128]{2,1,0:T(8,128)(2,1)S(1)}, u32[]{:S(2)}, u32[]{:S(2)}) %collective-permute-start.41) | collective-permute-done | bytes 1081376 | tf_op jit(solution)/shard_map/ppermute | solution.py:364
  1034.6 105.1 %collective-permute-done.67 = f32[3200]{0:T(1024)} collective-permute-done((f32[3200]{0:T(1024)S(1)}, f32[3200]{0:T(1024)}, u32[]{:S(2)}, u32[]{:S(2)}) %collective-permute-start.67) | collective-permute-done | bytes 12832 | tf_op jit(solution)/shard_map/ppermute | solution.py:364
  1147.2 23.7 %all-reduce.9.cloned.1.call-done.refs_0_ = bf16[20,128,128]{2,1,0:T(8,128)(2,1)} async-done(((bf16[20,128,128]{2,1,0:T(8,128)(2,1)}), bf16[20,128,128]{2,1,0:T(8,128)(2,1)}) %all-reduce.9.cloned.1.call-update) | async-done | bytes 655376 | tf_op jit(solution)/shard_map/psum | solution.py:420
  1175.9 7.0 shard_map.279
  1197.0 41.2 %shard_map.278 = (f32[116,128,128]{2,1,0:T(8,128)}, f32[116,128,128]{2,1,0:T(8,128)}, f32[116,128,128]{2,1,0:T(8,128)}) custom-call(s32[116]{0:T(128)S(1)} %fusion.284.index_ref, bf16[37,128,128]{2,1,0:T(8,128)(2,1)} %shard_map.270.refs_0_, bf16[37,128,128]{2,1,0:T(8,128)(2,1)} %collective-permute-done.52.refs_1_, ...), custom_call_target="tpu_custom_call" | custom-call | tf_op jit(solution)/shard_map/pallas_call | solution.py:335
  (853 shorter events, 390.2 us)
Async XLA Ops:
  7.2 292.0 %all-gather.7.cloned.1.call-start = ((), (), s32[]{:S(2)}) async-start(), calls=%async_computation.4 | async-start | bytes 10813440 | tf_op jit(solution)/shard_map/all_gather | solution.py:667
  17.1 39.0 %collective-permute-start = (bf16[116,128,128]{2,1,0:T(8,128)(2,1)}, bf16[116,128,128]{2,1,0:T(8,128)(2,1)}, u32[]{:S(2)}, u32[]{:S(2)}) collective-permute-start(bf16[116,128,128]{2,1,0:T(8,128)(2,1)} %convert_element_type.262.refs_0_), channel_id=1, source_target_pairs={{0,1},{1,0},{2,3},{3,2},{4,5},{5,4},{6,7},{7,6},{8,9},{9,8},{10,11... | collective-permute-start | bytes 11403272 | tf_op jit(solution)/shard_map/ppermute | solution.py:358
  43.7 35.3 %collective-permute-start.16 = (bf16[4,10,128,128]{3,2,1,0:T(8,128)(2,1)}, bf16[4,10,128,128]{3,2,1,0:T(8,128)(2,1)}, u32[]{:S(2)}, u32[]{:S(2)}) collective-permute-start(bf16[4,10,128,128]{3,2,1,0:T(8,128)(2,1)} %gather_fusion.1), channel_id=1, source_target_pairs={{0,1},{1,0},{2,3},{3,2},{4,5},{5,4},{6,7},{7,6},{8,9},{9,8},{10,11... | collective-permute-start | bytes 3932168 | tf_op jit(solution)/shard_map/ppermute | solution.py:358
  72.7 101.0 %collective-permute-start.2 = (bf16[37,128,128]{2,1,0:T(8,128)(2,1)}, bf16[37,128,128]{2,1,0:T(8,128)(2,1)}, u32[]{:S(2)}, u32[]{:S(2)}) collective-permute-start(bf16[37,128,128]{2,1,0:T(8,128)(2,1)} %shard_map.259), channel_id=1, source_target_pairs={{0,4},{1,5},{2,6},{3,7},{4,0},{5,1},{6,2},{7,3},{8,12},{9,13},{10,... | collective-permute-start | bytes 3637256 | tf_op jit(solution)/shard_map/ppermute | solution.py:364
  73.7 102.1 %collective-permute-start.3 = (bf16[37,128,128]{2,1,0:T(8,128)(2,1)}, bf16[37,128,128]{2,1,0:T(8,128)(2,1)}, u32[]{:S(2)}, u32[]{:S(2)}) collective-permute-start(bf16[37,128,128]{2,1,0:T(8,128)(2,1)} %shard_map.260), channel_id=1, source_target_pairs={{0,6},{1,7},{2,0},{3,1},{4,2},{5,3},{6,4},{7,5},{8,14},{9,15},{10,... | collective-permute-start | bytes 3637256 | tf_op jit(solution)/shard_map/ppermute | solution.py:364
  198.4 92.6 %collective-permute-start.22 = (bf16[33,128,128]{2,1,0:T(8,128)(2,1)S(1)}, bf16[33,128,128]{2,1,0:T(8,128)(2,1)S(1)}, u32[]{:S(2)}, u32[]{:S(2)}) collective-permute-start(bf16[33,128,128]{2,1,0:T(8,128)(2,1)S(1)} %shard_map.264.refs_0_), channel_id=1, source_target_pairs={{0,4},{1,5},{2,6},{3,7},{4,0},{5,1},{6,2},{7,3},{8,12},{9,13},{10,... | collective-permute-start | bytes 3244040 | tf_op jit(solution)/shard_map/ppermute | solution.py:364
  199.7 93.9 %collective-permute-start.23 = (bf16[33,128,128]{2,1,0:T(8,128)(2,1)S(1)}, bf16[33,128,128]{2,1,0:T(8,128)(2,1)}, u32[]{:S(2)}, u32[]{:S(2)}) collective-permute-start(bf16[33,128,128]{2,1,0:T(8,128)(2,1)S(1)} %shard_map.264.refs_0_), channel_id=1, source_target_pairs={{0,6},{1,7},{2,0},{3,1},{4,2},{5,3},{6,4},{7,5},{8,14},{9,15},{10,... | collective-permute-start | bytes 3244040 | tf_op jit(solution)/shard_map/ppermute | solution.py:364
  203.4 95.7 %collective-permute-start.24 = (bf16[33,128,128]{2,1,0:T(8,128)(2,1)S(1)}, bf16[33,128,128]{2,1,0:T(8,128)(2,1)}, u32[]{:S(2)}, u32[]{:S(2)}) collective-permute-start(bf16[33,128,128]{2,1,0:T(8,128)(2,1)S(1)} %shard_map.264.refs_0_), channel_id=1, source_target_pairs={{0,1},{1,0},{2,3},{3,2},{4,5},{5,4},{6,7},{7,6},{8,9},{9,8},{10,11... | collective-permute-start | bytes 3244040 | tf_op jit(solution)/shard_map/ppermute | solution.py:358
  223.5 75.6 %collective-permute-start.25 = (bf16[33,128,128]{2,1,0:T(8,128)(2,1)S(1)}, bf16[33,128,128]{2,1,0:T(8,128)(2,1)}, u32[]{:S(2)}, u32[]{:S(2)}) collective-permute-start(bf16[33,128,128]{2,1,0:T(8,128)(2,1)S(1)} %collective-permute-done.21.refs_1_), channel_id=1, source_target_pairs={{0,1},{1,0},{2,3},{3,2},{4,5},{5,4},{6,7},{7,6},{8,9},{9,8},{10,11... | collective-permute-start | bytes 3244040 | tf_op jit(solution)/shard_map/ppermute | solution.py:358
  311.3 118.4 %all-gather.11.cloned.1.call-start = ((), (), s32[]{:S(2)}) async-start(), calls=%async_computation.6 | async-start | bytes 10813440 | tf_op jit(solution)/shard_map/all_gather | solution.py:667
  361.8 46.1 %collective-permute-start.31 = (bf16[128,2048]{1,0:T(8,128)(2,1)S(1)}, bf16[128,2048]{1,0:T(8,128)(2,1)S(1)}, u32[]{:S(2)}, u32[]{:S(2)}) collective-permute-start(bf16[128,2048]{1,0:T(8,128)(2,1)S(1)} %get-tuple-element.580), channel_id=1, source_target_pairs={{0,24},{8,16},{16,8},{24,0},{1,25},{9,17},{17,9},{25,1},{2,26},{10... | collective-permute-start | bytes 1572872 | tf_op jit(solution)/shard_map/ppermute | solution.py:353
  451.0 49.1 %all-gather.9.cloned.1.call-start = ((), (), s32[]{:S(2)}) async-start(), calls=%async_computation.5 | async-start | bytes 4718592 | tf_op jit(solution)/shard_map/all_gather | solution.py:769
  451.7 120.8 %reduce-scatter.11.cloned.1.call-start = ((), (), s32[]{:S(2)}) async-start(), calls=%async_computation.7 | async-start | bytes 4718592 | tf_op jit(solution)/shard_map/reduce_scatter | solution.py:778
  524.1 103.7 %all-gather.13.cloned.1.call-start = ((), (), s32[]{:S(2)}) async-start(), calls=%async_computation.8 | async-start | bytes 4718592 | tf_op jit(solution)/shard_map/all_gather | solution.py:799
  581.9 122.5 %reduce-scatter.13.cloned.1.call-start = ((), (), s32[]{:S(2)}) async-start(), calls=%async_computation.9 | async-start | bytes 4718592 | tf_op jit(solution)/shard_map/reduce_scatter | solution.py:802
  654.9 332.4 %reduce-scatter.15.cloned.1.call-start = ((), (), s32[]{:S(2)}) async-start(), calls=%async_computation.10 | async-start | bytes 21626880 | tf_op jit(solution)/shard_map/reduce_scatter | solution.py:815
  706.6 464.3 %all-reduce.9.cloned.1.call-start = ((), (), s32[]{:S(2)}) async-start(), calls=%async_computation.11 | async-start | bytes 1310720 | tf_op jit(solution)/shard_map/psum | solution.py:420
  721.7 45.9 %collective-permute-start.34 = (bf16[128,2048]{1,0:T(8,128)(2,1)S(1)}, bf16[128,2048]{1,0:T(8,128)(2,1)S(1)}, u32[]{:S(2)}, u32[]{:S(2)}) collective-permute-start(bf16[128,2048]{1,0:T(8,128)(2,1)S(1)} %get-tuple-element.596), channel_id=1, source_target_pairs={{0,24},{8,16},{16,8},{24,0},{1,25},{9,17},{17,9},{25,1},{2,26},{10... | collective-permute-start | bytes 1572872 | tf_op jit(solution)/shard_map/ppermute | solution.py:353
  807.9 70.3 %collective-permute-start.39 = (bf16[132,128,128]{2,1,0:T(8,128)(2,1)}, bf16[132,128,128]{2,1,0:T(8,128)(2,1)}, u32[]{:S(2)}, u32[]{:S(2)}) collective-permute-start(bf16[132,128,128]{2,1,0:T(8,128)(2,1)} %shard_map.269), channel_id=1, source_target_pairs={{0,1},{1,0},{2,3},{3,2},{4,5},{5,4},{6,7},{7,6},{8,9},{9,8},{10,11... | collective-permute-start | bytes 12976136 | tf_op jit(solution)/shard_map/ppermute | solution.py:358
  824.4 35.9 %collective-permute-start.38 = (bf16[128,2048]{1,0:T(8,128)(2,1)S(1)}, bf16[128,2048]{1,0:T(8,128)(2,1)S(1)}, u32[]{:S(2)}, u32[]{:S(2)}) collective-permute-start(bf16[128,2048]{1,0:T(8,128)(2,1)S(1)} %get-tuple-element.577), channel_id=1, source_target_pairs={{0,24},{8,16},{16,8},{24,0},{1,25},{9,17},{17,9},{25,1},{2,26},{10... | collective-permute-start | bytes 1572872 | tf_op jit(solution)/shard_map/ppermute | solution.py:353
  826.4 40.4 %collective-permute-start.43 = (bf16[4,1280,128]{2,1,0:T(8,128)(2,1)}, bf16[4,1280,128]{2,1,0:T(8,128)(2,1)}, u32[]{:S(2)}, u32[]{:S(2)}) collective-permute-start(bf16[4,1280,128]{2,1,0:T(8,128)(2,1)} %fusion.19), channel_id=1, source_target_pairs={{0,1},{1,0},{2,3},{3,2},{4,5},{5,4},{6,7},{7,6},{8,9},{9,8},{10,11... | collective-permute-start | bytes 3932168 | tf_op jit(solution)/shard_map/ppermute | solution.py:358
  889.4 32.3 %collective-permute-start.40 = (bf16[33,128,128]{2,1,0:T(8,128)(2,1)S(1)}, bf16[33,128,128]{2,1,0:T(8,128)(2,1)S(1)}, u32[]{:S(2)}, u32[]{:S(2)}) collective-permute-start(bf16[33,128,128]{2,1,0:T(8,128)(2,1)S(1)} %get-tuple-element.573), channel_id=1, source_target_pairs={{0,2},{1,3},{2,4},{3,5},{4,6},{5,7},{6,0},{7,1},{8,10},{9,11},{10,... | collective-permute-start | bytes 3244040 | tf_op jit(solution)/shard_map/ppermute | solution.py:364
  890.7 91.2 %collective-permute-start.41 = (bf16[33,128,128]{2,1,0:T(8,128)(2,1)S(1)}, bf16[33,128,128]{2,1,0:T(8,128)(2,1)S(1)}, u32[]{:S(2)}, u32[]{:S(2)}) collective-permute-start(bf16[33,128,128]{2,1,0:T(8,128)(2,1)S(1)} %get-tuple-element.575), channel_id=1, source_target_pairs={{0,4},{1,5},{2,6},{3,7},{4,0},{5,1},{6,2},{7,3},{8,12},{9,13},{10,... | collective-permute-start | bytes 3244040 | tf_op jit(solution)/shard_map/ppermute | solution.py:364
  891.7 93.9 %collective-permute-start.42 = (bf16[33,128,128]{2,1,0:T(8,128)(2,1)S(1)}, bf16[33,128,128]{2,1,0:T(8,128)(2,1)S(1)}, u32[]{:S(2)}, u32[]{:S(2)}) collective-permute-start(bf16[33,128,128]{2,1,0:T(8,128)(2,1)S(1)} %get-tuple-element.574), channel_id=1, source_target_pairs={{0,6},{1,7},{2,0},{3,1},{4,2},{5,3},{6,4},{7,5},{8,14},{9,15},{10,... | collective-permute-start | bytes 3244040 | tf_op jit(solution)/shard_map/ppermute | solution.py:364
  993.5 33.3 %collective-permute-start.61 = (bf16[13,128,128]{2,1,0:T(8,128)(2,1)}, bf16[13,128,128]{2,1,0:T(8,128)(2,1)}, u32[]{:S(2)}, u32[]{:S(2)}) collective-permute-start(bf16[13,128,128]{2,1,0:T(8,128)(2,1)} %shard_map.277), channel_id=1, source_target_pairs={{0,24},{8,16},{16,8},{24,0},{1,25},{9,17},{17,9},{25,1},{2,26},{10... | collective-permute-start | bytes 1277960 | tf_op jit(solution)/shard_map/ppermute | solution.py:353
  1026.9 158.4 %collective-permute-start.52 = (bf16[37,128,128]{2,1,0:T(8,128)(2,1)}, bf16[37,128,128]{2,1,0:T(8,128)(2,1)}, u32[]{:S(2)}, u32[]{:S(2)}) collective-permute-start(bf16[37,128,128]{2,1,0:T(8,128)(2,1)} %shard_map.271), channel_id=1, source_target_pairs={{0,2},{1,3},{2,4},{3,5},{4,6},{5,7},{6,0},{7,1},{8,10},{9,11},{10,... | collective-permute-start | bytes 3637256 | tf_op jit(solution)/shard_map/ppermute | solution.py:364
  1028.9 156.8 %collective-permute-start.53 = (bf16[37,128,128]{2,1,0:T(8,128)(2,1)}, bf16[37,128,128]{2,1,0:T(8,128)(2,1)}, u32[]{:S(2)}, u32[]{:S(2)}) collective-permute-start(bf16[37,128,128]{2,1,0:T(8,128)(2,1)} %shard_map.272), channel_id=1, source_target_pairs={{0,4},{1,5},{2,6},{3,7},{4,0},{5,1},{6,2},{7,3},{8,12},{9,13},{10,... | collective-permute-start | bytes 3637256 | tf_op jit(solution)/shard_map/ppermute | solution.py:364
  1030.4 155.4 %collective-permute-start.54 = (bf16[37,128,128]{2,1,0:T(8,128)(2,1)}, bf16[37,128,128]{2,1,0:T(8,128)(2,1)}, u32[]{:S(2)}, u32[]{:S(2)}) collective-permute-start(bf16[37,128,128]{2,1,0:T(8,128)(2,1)} %shard_map.273), channel_id=1, source_target_pairs={{0,6},{1,7},{2,0},{3,1},{4,2},{5,3},{6,4},{7,5},{8,14},{9,15},{10,... | collective-permute-start | bytes 3637256 | tf_op jit(solution)/shard_map/ppermute | solution.py:364
  1030.9 108.7 %collective-permute-start.67 = (f32[3200]{0:T(1024)S(1)}, f32[3200]{0:T(1024)}, u32[]{:S(2)}, u32[]{:S(2)}) collective-permute-start(f32[3200]{0:T(1024)S(1)} %add.1845), channel_id=1, source_target_pairs={{0,4},{1,5},{2,6},{3,7},{4,0},{5,1},{6,2},{7,3},{8,12},{9,13},{10,... | collective-permute-start | bytes 38408 | tf_op jit(solution)/shard_map/ppermute | solution.py:364
  1031.8 109.6 %collective-permute-start.68 = (f32[3200]{0:T(1024)S(1)}, f32[3200]{0:T(1024)}, u32[]{:S(2)}, u32[]{:S(2)}) collective-permute-start(f32[3200]{0:T(1024)S(1)} %add.1845), channel_id=1, source_target_pairs={{0,6},{1,7},{2,0},{3,1},{4,2},{5,3},{6,4},{7,5},{8,14},{9,15},{10,... | collective-permute-start | bytes 38408 | tf_op jit(solution)/shard_map/ppermute | solution.py:364
  1139.7 43.3 %collective-permute-start.65 = (bf16[13,128,128]{2,1,0:T(8,128)(2,1)}, bf16[13,128,128]{2,1,0:T(8,128)(2,1)S(1)}, u32[]{:S(2)}, u32[]{:S(2)}) collective-permute-start(bf16[13,128,128]{2,1,0:T(8,128)(2,1)} %collective-permute-done.61.refs_11_), channel_id=1, source_target_pairs={{0,1},{1,0},{2,3},{3,2},{4,5},{5,4},{6,7},{7,6},{8,9},{9,8},{10,11... | collective-permute-start | bytes 1277960 | tf_op jit(solution)/shard_map/ppermute | solution.py:358
  1141.3 43.9 %collective-permute-start.64 = (bf16[13,128,128]{2,1,0:T(8,128)(2,1)}, bf16[13,128,128]{2,1,0:T(8,128)(2,1)S(1)}, u32[]{:S(2)}, u32[]{:S(2)}) collective-permute-start(bf16[13,128,128]{2,1,0:T(8,128)(2,1)} %collective-permute-done.60.refs_10_), channel_id=1, source_target_pairs={{0,1},{1,0},{2,3},{3,2},{4,5},{5,4},{6,7},{7,6},{8,9},{9,8},{10,11... | collective-permute-start | bytes 1277960 | tf_op jit(solution)/shard_map/ppermute | solution.py:358
  (249 other events, 3850.5 us)
Sparse Core Ops, SparseCore 0:
  198.5 89.1 all-gather.6
  314.0 115.7 all-gather.10
  454.0 46.0 all-gather.8
  524.2 48.2 reduce-scatter.10
  582.0 45.6 all-gather.12
  655.0 48.3 reduce-scatter.12
  706.7 215.5 reduce-scatter.14
  1034.7 136.1 all-reduce.8

commit v7 on v6

--- a/solution.py
+++ b/solution.py
@@ -404,20 +404,36 @@
 
 def small_sum(value):
     seq_size = lax.axis_size("seq")
+    chips = lax.axis_size("fsdp") // 2
+    chip = lax.axis_index("fsdp") // 2
     even = lax.axis_index("fsdp") % 2 == 0
     low = value.astype(jnp.bfloat16)
     parts = low.reshape((seq_size, 2, low.shape[0] // (2 * seq_size)) + low.shape[1:])
     kept = jnp.where(even, parts[:, 0], parts[:, 1]).astype(jnp.float32)
     given = jnp.where(even, parts[:, 1], parts[:, 0])
     kept = kept + core_swap(given).astype(jnp.float32)
-    return seq_sum(kept.reshape((-1,) + low.shape[1:]), jnp.bfloat16, True).astype(jnp.bfloat16)
-
-
-def small_all(kept):
-    even = lax.axis_index("fsdp") % 2 == 0
-    empty = jnp.zeros_like(kept)
-    both = jnp.where(even, jnp.stack([kept, empty]), jnp.stack([empty, kept]))
-    return lax.psum(both, "fsdp").reshape((2 * kept.shape[0],) + kept.shape[1:])
+    kept = seq_sum(kept.reshape((-1,) + low.shape[1:]), jnp.bfloat16, True)
+    kept = kept.reshape((chips, kept.shape[0] // chips) + kept.shape[1:])
+    kept = kept[(chip + jnp.arange(chips)) % chips]
+    total = kept[0]
+    for offset in range(1, chips):
+        total = total + chip_shift(kept[offset].astype(jnp.bfloat16), offset).astype(jnp.float32)
+    total = total.astype(jnp.bfloat16)
+    parts = jnp.stack([total] + [chip_shift(total, offset) for offset in range(1, chips)])
+    parts = parts[(chip - jnp.arange(chips)) % chips]
+    return core_pair(parts).reshape((value.shape[0] // seq_size,) + value.shape[1:])
+
+
+def turn(value, cosine, sine):
+    half = value.shape[-1] // 2
+    first, second = value[..., :half], value[..., half:]
+    return jnp.concatenate(
+        [first * cosine - second * sine, second * cosine + first * sine], axis=-1
+    )
+
+
+def added(one, two):
+    return one.astype(jnp.float32) + two.astype(jnp.float32)
 
 
 def on_device(
@@ -479,8 +495,10 @@
     attn_room = (room(2 * mine, attn_share / seq_size) + 1) // 2
     attn_hold = (room(attn_count, 1.0 / chips) + 1) // 2 + 1
     ffn_room = (room(2 * mine, ffn_share / chips) + 1) // 2
-    ffn_hold = (room(ffn_count, 1.0 / seq_size) + 3) // 4 * 4
-    ffn_half = ffn_hold // 2
+    both_count = row_blocks * ffn_first
+    both_hold, down_hold = (
+        (room(count, 1.0 / seq_size) + 3) // 4 * 4 for count in (both_count, ffn_count - both_count)
+    )
 
     def tile_places(owner):
         row = owner // columns
@@ -495,10 +513,9 @@
         ffn_to = jnp.where(is_attn, -1, ffn_column // ffn_each)
         ffn_local = ffn_column % ffn_each
         ffn_place = jnp.where(
-            kind == 2,
-            row_blocks * ffn_first + row * ffn_each + ffn_local,
-            row * ffn_first + kind * ffn_each + ffn_local,
-        )
+            kind == 2, row * ffn_each + ffn_local, row * ffn_first + kind * ffn_each + ffn_local
+        )
+        is_down = (kind == 2).astype(jnp.int32)
         attn_to = jnp.where(
             key_at < 0,
             column // query_each,
@@ -522,17 +539,55 @@
             ),
         )
         attn_to = jnp.where(is_attn, attn_to, -1)
-        return (ffn_to, ffn_place, attn_to, attn_place)
+        return (ffn_to, is_down, ffn_place, attn_to, attn_place)
 
     owners = tile_owner.reshape(seq_size, fsdp_size, mine)
-    ffn_to, ffn_place, attn_to, attn_place = tile_places(owners)
     slot_seq = jnp.arange(seq_size)[:, None, None]
     slot_fsdp = jnp.arange(fsdp_size)[None, :, None]
     slot_chip = slot_fsdp // 2
+    local_slots = jnp.arange(mine)
+    both_slots = jnp.arange(2 * mine)
+    both_slots = jnp.where(
+        both_slots // mine == my_core, both_slots % mine, mine + both_slots % mine
+    )
+
+    ffn_to = tile_places(owners)[0]
     ffn_chip = jnp.where(ffn_to < 0, -1, ffn_to // 2)
     chip_view = ffn_chip.reshape(seq_size, chips, 2 * mine)
     chip_rank = count_earlier(chip_view, chip_view >= 0).reshape(owners.shape)
-    seq_view = ffn_to.reshape(seq_size, fsdp_size * mine)
+    ffn_slots = lax.dynamic_slice(
+        jnp.stack([ffn_chip, chip_rank]), (0, my_seq, 2 * my_chip, 0), (2, 1, 2, mine)
+    ).reshape(2, 1, 1, 2 * mine)
+    ffn_pack = pick(
+        (ffn_slots[0] == ((my_chip + shifts) % chips)[:, None, None])
+        & (ffn_slots[1] == (my_core * ffn_room + jnp.arange(ffn_room))[None, :, None]),
+        both_slots,
+    )
+    master_low = tile_master.astype(bf16)
+    masters = [master_low, core_swap(master_low)]
+    ffn_sent = [gather_tiles(masters, ffn_pack[i]) for i in range(chips)]
+    small_rows = small_master.shape[0] // 2
+    small_half = lax.dynamic_slice_in_dim(small_master, my_core * small_rows, small_rows)
+    masters, ffn_sent, chip_rank, owners, own_tokens, own_gains, small_half = (
+        lax.optimization_barrier(
+            (
+                masters,
+                ffn_sent,
+                chip_rank,
+                owners,
+                tokens[0],
+                gains.astype(bf16),
+                small_half.astype(bf16),
+            )
+        )
+    )
+    ffn_got = chip_exchange(ffn_sent)
+
+    ffn_to, is_down, ffn_place, attn_to, attn_place = tile_places(owners)
+    ffn_chip = jnp.where(ffn_to < 0, -1, ffn_to // 2)
+    ffn_key = jnp.where(ffn_to < 0, -1, 2 * ffn_to + is_down)
+    ffn_hold = jnp.where(is_down == 1, down_hold, both_hold)
+    seq_view = ffn_key.reshape(seq_size, fsdp_size * mine)
     ffn_rank = count_earlier(seq_view, seq_view >= 0).reshape(owners.shape)
     attn_view = attn_to.reshape(seq_size, chips, 2 * mine)
     attn_rank = count_earlier(attn_view, attn_view >= 0).reshape(owners.shape)
@@ -573,19 +628,17 @@
         + attn_rank
     )
     chip_slots = lax.dynamic_slice(
-        jnp.stack([ffn_chip, chip_rank, attn_key, attn_rank]),
-        (0, my_seq, 2 * my_chip, 0),
-        (4, 1, 2, mine),
-    ).reshape(4, 1, 1, 2 * mine)
+        jnp.stack([attn_key, attn_rank]), (0, my_seq, 2 * my_chip, 0), (2, 1, 2, mine)
+    ).reshape(2, 1, 1, 2 * mine)
     my_slots = lax.dynamic_slice(
         jnp.stack([ffn_to, back_place, attn_back_place]), (0, my_seq, my_fsdp, 0), (3, 1, 1, mine)
     ).reshape(3, mine)
     seq_slots = lax.dynamic_slice(
         jnp.stack(
             [
-                ffn_to,
+                ffn_key,
                 ffn_rank,
-                ffn_place,
+                ffn_chip,
                 out_place,
                 chip_rank,
                 jnp.broadcast_to(slot_chip, owners.shape),
@@ -601,20 +654,21 @@
     ).reshape(4, 2 * seq_size * mine)
     my_key = 2 * my_seq + my_core
 
-    local_slots = jnp.arange(mine)
-    both_slots = jnp.arange(2 * mine)
-    both_slots = jnp.where(
-        both_slots // mine == my_core, both_slots % mine, mine + both_slots % mine
-    )
+    attn_message = attn_room + row_blocks * rows // tile + small_rows + -(-own_gains.shape[0] // tile**2)
     attn_pack = pick(
-        (chip_slots[2] == (2 * (my_seq ^ flips) + my_core)[:, None, None])
-        & (chip_slots[3] == jnp.arange(attn_room)[None, :, None]),
+        (chip_slots[0] == (2 * (my_seq ^ flips) + my_core)[:, None, None])
+        & (chip_slots[1] == jnp.arange(attn_room)[None, :, None]),
         both_slots,
     )
     attn_keep = pick(
         (column_slots[0][None, :] == my_key)
         & (column_slots[1][None, :] == jnp.arange(attn_hold)[:, None]),
-        (column_slots[3] ^ my_seq) * attn_room + column_slots[2],
+        jnp.where(
+            column_slots[3] == my_seq,
+            0,
+            attn_room + ((column_slots[3] ^ my_seq) - 1) * attn_message,
+        )
+        + column_slots[2],
     )
     attn_join = pick(
         (attn_to.reshape(1, -1) == my_seq)
@@ -625,71 +679,120 @@
             + attn_order
         ).reshape(1, -1),
     )
-    ffn_pack = pick(
-        (chip_slots[0] == ((my_chip + shifts) % chips)[:, None, None])
-        & (chip_slots[1] == (my_core * ffn_room + jnp.arange(ffn_room))[None, :, None]),
-        both_slots,
-    )
-    ffn_keep = pick(
-        (seq_slots[0][None, :] == my_fsdp) & (seq_slots[1][None, :] == jnp.arange(ffn_hold)[:, None]),
-        seq_slots[3][None, :],
-    )
-    ffn_join = pick(
-        (ffn_to.reshape(1, -1) == my_fsdp)
-        & (ffn_place.reshape(1, -1) == jnp.arange(ffn_count)[:, None]),
-        (
-            ffn_rank // ffn_half * (seq_size * ffn_half) + slot_seq * ffn_half + ffn_rank % ffn_half
-        ).reshape(1, -1),
-    )
-    master_low = tile_master.astype(bf16)
-    masters = [master_low, core_swap(master_low)]
-    ffn_sent = [gather_tiles(masters, ffn_pack[i]) for i in range(chips)]
-    masters, ffn_sent, attn_pack = lax.optimization_barrier((masters, ffn_sent, attn_pack))
-    ffn_got = chip_exchange(ffn_sent)
+    def ffn_tables(kind, hold, count):
+        key = 2 * my_fsdp + kind
+        keep = pick(
+            (seq_slots[0][None, :] == key) & (seq_slots[1][None, :] == jnp.arange(hold)[:, None]),
+            seq_slots[3][None, :],
+        )
+        join = pick(
+            (ffn_key.reshape(1, -1) == key)
+            & (ffn_place.reshape(1, -1) == jnp.arange(count)[:, None]),
+            (slot_seq * hold + ffn_rank).reshape(1, -1),
+        )
+        cut = pick(
+            (ffn_key.reshape(seq_size, 1, -1) == key)
+            & (ffn_rank.reshape(seq_size, 1, -1) == jnp.arange(hold)[None, :, None]),
+            ffn_place.reshape(seq_size, 1, -1),
+        )
+        return (keep, join, cut)
+
+    both_keep, both_join, both_cut = ffn_tables(0, both_hold, both_count)
+    down_keep, down_join, down_cut = ffn_tables(1, down_hold, ffn_count - both_count)
+    ffn_back = pick(
+        (seq_slots[5][None, None, :] == ((my_chip + shifts) % chips)[:, None, None])
+        & (seq_slots[2][None, None, :] == my_chip)
+        & (seq_slots[4][None, None, :] == (my_core * ffn_room + jnp.arange(ffn_room))[None, :, None]),
+        jnp.where(seq_slots[0] % 2 == 1, 2 * both_hold, 0)
+        + jnp.where(
+            seq_slots[0] // 2 == my_fsdp, 0, jnp.where(seq_slots[0] % 2 == 1, down_hold, both_hold)
+        )
+        + seq_slots[1],
+    )
+
     attn_sent = gather_tiles(masters, attn_pack.reshape(-1))
     attn_sent = attn_sent.reshape(seq_size, attn_room, tile, tile)
-    attn_got = seq_exchange([attn_sent[i] for i in range(seq_size)])
-    pack_tokens = seq_gather(tokens[0])
-    gain_full = seq_ordered(gains.astype(bf16))
-    small_rows = small_master.shape[0] // 2
-    small_half = lax.dynamic_slice_in_dim(small_master, my_core * small_rows, small_rows)
-    small_got = core_pair(seq_ordered(small_half.astype(bf16))).transpose(1, 0, 2, 3, 4)
-    ffn_got, attn_got, pack_tokens, gain_full, small_got = lax.optimization_barrier(
-        (ffn_got, attn_got, pack_tokens, gain_full, small_got)
-    )
+    token_tiles = own_tokens.reshape(rows, row_blocks, tile).transpose(1, 0, 2)
+    token_tiles = token_tiles.reshape(-1, tile, tile)
+    gain_rows = own_gains.reshape(-1, tile)
+    gain_tiles = jnp.pad(gain_rows, ((0, -gain_rows.shape[0] % tile), (0, 0))).reshape(-1, tile, tile)
+    common = jnp.concatenate([token_tiles, small_half, gain_tiles])
+    attn_got = [attn_sent[0]] + [
+        seq_swap(jnp.concatenate([attn_sent[flip], common]), flip) for flip in range(1, seq_size)
+    ]
+    segment, position = documents(doc_lengths[0], length)
+    places = ((my_seq ^ flips)[:, None] * rows + jnp.arange(rows)[None, :]).reshape(-1)
+
+    def reorder(values):
+        blocks = values.reshape(seq_size, rows)
+        return jnp.concatenate(
+            [lax.dynamic_index_in_dim(blocks, my_seq ^ i, 0, False) for i in range(seq_size)]
+        )
+
+    pack_segment = reorder(segment)
+    allow = (pack_segment[:, None] == pack_segment[None, :]) & (
+        places[None, :] <= places[:, None]
+    )
+    turns = jnp.arange(HEAD_DIM // 2).astype(f32)
+    angle = reorder(position).astype(f32)[:, None] * (THETA ** (-2.0 * turns / HEAD_DIM))[None, :]
+    cosine, sine = jnp.cos(angle)[:, None, :], jnp.sin(angle)[:, None, :]
+    ready = (allow, cosine, sine, attn_join, both_join)
+    ffn_got, attn_got, common, ready = lax.optimization_barrier((ffn_got, attn_got, common, ready))
+    allow, cosine, sine, attn_join, both_join = ready
+    parts = [common] + [value[attn_room:] for value in attn_got[1:]]
+    token_end = token_tiles.shape[0]
+    small_end = token_end + small_rows
+
+    def seq_order(value):
+        return value[my_seq ^ flips]
+
+    pack_tokens = jnp.concatenate(
+        [
+            part[:token_end].reshape(row_blocks, rows, tile).transpose(1, 0, 2).reshape(rows, width)
+            for part in parts
+        ]
+    )
+    gain_full = seq_order(
+        jnp.stack([part[small_end:].reshape(-1, tile)[: gain_rows.shape[0]] for part in parts])
+    )
+    gain_full = gain_full.reshape(-1).astype(f32)
+    gain_in = gain_full[0:width]
+    small_got = core_pair(seq_order(jnp.stack([part[token_end:small_end] for part in parts])))
+    small_got = small_got.transpose(1, 0, 2, 3, 4)
+    small_table = assemble(small_got.reshape((-1,) + small_master.shape[1:]), row_blocks)
+    pack_normed = rms_norm(pack_tokens.astype(f32), gain_in).astype(bf16)
     attn_kept = gather_tiles(attn_got, attn_keep)
-    ffn_other = [core_swap(value) for value in ffn_got]
-    ffn_kept = [
-        gather_tiles(ffn_got + ffn_other, ffn_keep[:ffn_half]),
-        gather_tiles(ffn_got + ffn_other, ffn_keep[ffn_half:]),
-    ]
-    ffn_kept, attn_kept = lax.optimization_barrier((ffn_kept, attn_kept))
-    ffn_all = [lax.all_gather(value, "seq", axis=0, tiled=True) for value in ffn_kept]
+    ffn_got = ffn_got + [core_swap(value) for value in ffn_got]
+    both_kept, down_kept = gather_tiles(ffn_got, both_keep), gather_tiles(ffn_got, down_keep)
+    both_kept, down_kept, attn_kept = lax.optimization_barrier((both_kept, down_kept, attn_kept))
+    both_all = lax.all_gather(both_kept, "seq", axis=0, tiled=True)
+    down_all = lax.all_gather(down_kept, "seq", axis=0, tiled=True)
     attn_all = [attn_kept] + [chip_shift(attn_kept, offset) for offset in range(1, chips)]
     attn_all = attn_all + [core_swap(value) for value in attn_all]
-    attn_all, ffn_all[0] = lax.optimization_barrier((attn_all, ffn_all[0]))
-    w_first, w_out = join_tiles(attn_all, attn_join, row_blocks, (attn_first, query_each))
-
-    def slow_fetch(to, me, place, columns_of):
-        def fetch(_, kept):
+
+    attn_all, both_all, pack_normed, gain_full = lax.optimization_barrier(
+        (attn_all, both_all, pack_normed, gain_full)
+    )
+    gain_in = gain_full[0:width]
+
+    def fetch(arrays, index, to, me, place, columns_of):
+        def fast():
+            return join_tiles(arrays, index, row_blocks, columns_of)
+
+        def slow():
             whole = lax.all_gather(master_low, ("seq", "fsdp"), axis=0, tiled=True)
             count = row_blocks * sum(columns_of)
-            index = pick(
+            slots = pick(
                 (to.reshape(1, -1) == me) & (place.reshape(1, -1) == jnp.arange(count)[:, None]),
                 jnp.arange(tiles)[None, :],
             )
-            return join_tiles([whole], index, row_blocks, columns_of)
-
-        return fetch
-
-    slow_steps = jnp.where(fits, 0, 1)
-    w_first, w_out = lax.fori_loop(
-        0, slow_steps, slow_fetch(attn_to, my_seq, attn_place, (attn_first, query_each)), (w_first, w_out)
-    )
-
-    small_table = assemble(small_got.reshape((-1,) + small_master.shape[1:]), row_blocks)
-    gain_full = gain_full.reshape(-1).astype(f32)
-    gain_in = gain_full[0:width]
+            return join_tiles([whole], slots, row_blocks, columns_of)
+
+        return lax.cond(fits, fast, slow)
+
+    w_first, w_out = fetch(
+        attn_all, attn_join, attn_to, my_seq, attn_place, (attn_first, query_each)
+    )
     gain_attn = gain_full[width : 2 * width]
     gain_laurel = gain_full[2 * width : 3 * width]
     gain_pre = gain_full[3 * width : 4 * width]
@@ -697,37 +800,19 @@
     gain_vec = gain_full[5 * width : 6 * width]
     gain_query = gain_full[6 * width : 6 * width + HEAD_DIM]
     gain_key = gain_full[6 * width + HEAD_DIM : 6 * width + 2 * HEAD_DIM]
-    laurel_left = small_table[:, :RANK]
-    laurel_right = small_table[:, RANK : 2 * RANK]
-    vector_gate_w = small_table[:, 2 * RANK : 2 * RANK + PLD]
-    vector_proj_w = small_table[:, 2 * RANK + PLD :]
-
-    segment, position = documents(doc_lengths[0], length)
-    places = ((my_seq ^ flips)[:, None] * rows + jnp.arange(rows)[None, :]).reshape(-1)
-
-    def reorder(values):
-        blocks = values.reshape(seq_size, rows)
-        return jnp.concatenate(
-            [lax.dynamic_index_in_dim(blocks, my_seq ^ i, 0, False) for i in range(seq_size)]
-        )
-
-    pack_segment = reorder(segment)
-    pack_position = reorder(position)
-    stream = tokens[0].astype(f32)
+    stream = own_tokens.astype(f32)
     vectors = layer_vectors[0].astype(f32)
     normed, normed_pull = jax.vjp(rms_norm, stream, gain_in)
     normed_low = normed.astype(bf16)
-    pack_normed = rms_norm(pack_tokens.astype(f32), gain_in).astype(bf16)
     first_pre = matmul(pack_normed, w_first)
     is_key = my_seq % per_key == 0
 
     def shape_query(query_in, query_gain):
-        return rotary(
-            rms_norm(query_in.reshape(length, per_device, HEAD_DIM), query_gain), pack_position
-        )
+        value = rms_norm(query_in.reshape(length, per_device, HEAD_DIM), query_gain)
+        return turn(value, cosine, sine)
 
     def shape_key(key_in, key_gain):
-        return rotary(rms_norm(key_in.reshape(length, 1, HEAD_DIM), key_gain), pack_position)
+        return turn(rms_norm(key_in.reshape(length, 1, HEAD_DIM), key_gain), cosine, sine)
 
     query_pre = first_pre[:, : per_device * HEAD_DIM]
     other_pre = first_pre[:, per_device * HEAD_DIM :]
@@ -740,9 +825,6 @@
     key_single = jnp.where(is_key, other_low, partner_low)
     value_single = jnp.where(is_key, partner_low, other_low)
 
-    allow = (pack_segment[:, None] == pack_segment[None, :]) & (
-        places[None, :] <= places[:, None]
-    )
     raw = (
         jnp.einsum("qhd,kd->qhk", query_heads, key_single, preferred_element_type=f32) * SCALE
     )
@@ -755,7 +837,14 @@
         .astype(bf16)
         .reshape(length, per_device * HEAD_DIM)
     )
+    (w_both,) = fetch([both_all], both_join, ffn_key, 2 * my_fsdp, ffn_place, (ffn_first,))
     attn_pre = seq_sum(matmul_flip(attended_low, w_out), bf16)
+    attn_pre, w_both, small_table = lax.optimization_barrier((attn_pre, w_both, small_table))
+    laurel_left = small_table[:, :RANK]
+    laurel_right = small_table[:, RANK : 2 * RANK]
+    vector_gate_w = small_table[:, 2 * RANK : 2 * RANK + PLD]
+    vector_proj_w = small_table[:, 2 * RANK + PLD :]
+
     attn_normed, attn_pull = jax.vjp(rms_norm, attn_pre, gain_attn)
     first_sum = stream + attn_normed
     left_pre = matmul(normed_low, laurel_left)
@@ -765,12 +854,9 @@
     second_sum = (first_sum + normed + laurel_normed) * ROOT_HALF
     feed_normed, feed_pull = jax.vjp(rms_norm, second_sum, gain_pre)
     feed_own = feed_normed.astype(bf16)
-    ffn_all, _ = lax.optimization_barrier((ffn_all, feed_own))
+    down_all, _ = lax.optimization_barrier((down_all, feed_own))
     feed_low = lax.all_gather(feed_own, "fsdp", axis=0, tiled=True)
-    w_both, w_down = join_tiles(ffn_all, ffn_join, row_blocks, (ffn_first, ffn_each))
-    w_both, w_down = lax.fori_loop(
-        0, slow_steps, slow_fetch(ffn_to, my_fsdp, ffn_place, (ffn_first, ffn_each)), (w_both, w_down)
-    )
+    (w_down,) = fetch([down_all], down_join, ffn_key, 2 * my_fsdp + 1, ffn_place, (ffn_each,))
     both_pre = matmul(feed_low, w_both)
     ffn_width = w_down.shape[1]
     hidden, hidden_pull = jax.vjp(gelu_product, both_pre[:, :ffn_width], both_pre[:, ffn_width:])
@@ -799,20 +885,36 @@
     down_grad_low = lax.all_gather(grad_down.astype(bf16), "fsdp", axis=0, tiled=True)
     grad_gate, grad_up = hidden_pull(matmul(down_grad_low, w_down))
     both_grad_low = jnp.concatenate([grad_gate, grad_up], axis=1).astype(bf16)
+
+    def cut_parts(flips_of, half):
+        half_now = down_hold // 2
+        index = down_cut[my_seq ^ jnp.array(flips_of), half * half_now : (half + 1) * half_now]
+        return cut_tiles([down_grad_w], index.reshape(-1), tile)
+
+    early_full = jnp.concatenate(
+        [matmul_outer(third_low, vector_grad_low), matmul_outer(proj_grad_low, vector_low)], axis=1
+    )
+    small_early = small_sum(split_tiles(early_full, tile).reshape(-1, tile))
+    down_grad_w = matmul_outer(down_grad_low, hidden_low).astype(bf16)
+    down_cuts = cut_parts([1, 3], 0), cut_parts([2, 3], 1)
+    both_grad_low, down_cuts, small_early = lax.optimization_barrier(
+        (both_grad_low, down_cuts, small_early)
+    )
     grad_feed = lax.psum_scatter(
         matmul_flip(both_grad_low, w_both).astype(bf16), "fsdp", scatter_dimension=0, tiled=True
     ).astype(f32)
+    down_one = added(cut_parts([0, 2], 0), seq_swap(down_cuts[0], 1))
+    down_two = added(cut_parts([0, 1], 1), seq_swap(down_cuts[1], 2))
     both_grad_w = matmul_outer(feed_low, both_grad_low).astype(bf16)
-    down_grad_w = matmul_outer(down_grad_low, hidden_low).astype(bf16)
-
-    ffn_cut = pick(
-        (ffn_to.reshape(seq_size, 1, -1) == my_fsdp)
-        & (ffn_rank.reshape(seq_size, 1, -1) == jnp.arange(ffn_hold)[None, :, None]),
-        ffn_place.reshape(seq_size, 1, -1),
-    )
-    ffn_parts = cut_tiles([both_grad_w, down_grad_w], ffn_cut.reshape(-1), tile)
-    ffn_parts, grad_feed = lax.optimization_barrier((ffn_parts, grad_feed))
-    ffn_sum = lax.psum_scatter(ffn_parts, "seq", scatter_dimension=0, tiled=True)
+    both_parts = cut_tiles([both_grad_w], both_cut.reshape(-1), tile)
+    both_parts, down_one, down_two, grad_feed = lax.optimization_barrier(
+        (both_parts, down_one, down_two, grad_feed)
+    )
+    both_sum = lax.psum_scatter(both_parts, "seq", scatter_dimension=0, tiled=True)
+    down_half = down_one.shape[0] // 2
+    down_one = added(down_one[:down_half], seq_swap(down_one[down_half:].astype(bf16), 2))
+    down_two = added(down_two[:down_half], seq_swap(down_two[down_half:].astype(bf16), 1))
+    down_sum = jnp.concatenate([down_one, down_two]).astype(bf16)
 
     grad_second_norm, grad_gain_pre = feed_pull(grad_feed)
     half_grad = (grad_third + grad_second_norm) * ROOT_HALF
@@ -848,23 +950,38 @@
         [grad_query_pre, jnp.where(is_key, grad_key_pre, other_grad)], axis=1
     ).astype(bf16)
     first_grad_w = matmul_outer(pack_normed, first_grad_low).astype(bf16)
-    grad_normed = (
-        half_grad
-        + matmul_flip(left_grad_low, laurel_left)
-        + seq_sum(matmul_flip(first_grad_low, w_first), bf16)
-    )
+    near = (my_chip + shifts) % chips
+    near_key = attn_key_chip[near][:, None, :]
+    near_order = attn_order_chip[near][:, None, :]
+    near_place = by_chip(attn_place)[near][:, None, :]
+
+    def attn_cut(core):
+        index = pick(
+            (near_key == 2 * my_seq + core)
+            & (near_order == jnp.arange(attn_hold)[None, :, None]),
+            near_place,
+        )
+        return cut_tiles([first_grad_w, out_grad_w], index.reshape(-1), tile)
+
+    attn_given, attn_own = attn_cut(1 - my_core), attn_cut(my_core)
+    attn_parts = added(attn_own, core_swap(attn_given)).reshape(chips, attn_hold, tile, tile)
+    attn_sum = attn_parts[0]
+    attn_parts = [attn_parts[offset].astype(bf16) for offset in range(1, chips)]
+    normed_sum = seq_sum(matmul_flip(first_grad_low, w_first), bf16)
+    attn_sum, attn_parts, normed_sum = lax.optimization_barrier((attn_sum, attn_parts, normed_sum))
+    for offset in range(1, chips):
+        attn_sum = attn_sum + chip_shift(attn_parts[offset - 1], offset).astype(f32)
+    attn_sum = attn_sum.astype(bf16)
+    attn_back = pick(
+        (column_slots[3][None, None, :] == (my_seq ^ flips)[:, None, None])
+        & (column_slots[0][None, None, :] == my_key)
+        & (column_slots[2][None, None, :] == jnp.arange(attn_room)[None, :, None]),
+        column_slots[1],
+    )
+
+    grad_normed = half_grad + matmul_flip(left_grad_low, laurel_left) + normed_sum
     grad_stream_norm, grad_gain_in = normed_pull(grad_normed)
     input_grad = (half_grad + grad_stream_norm)[None]
-
-    small_full = jnp.concatenate(
-        [
-            matmul_outer(normed_low, left_grad_low),
-            matmul_outer(right_grad_low, left_low),
-            matmul_outer(third_low, vector_grad_low),
-            matmul_outer(proj_grad_low, vector_low),
-        ],
-        axis=1,
-    )
     gain_grad = jnp.concatenate(
         [
             grad_gain_in,
@@ -877,56 +994,35 @@
             grad_gain_key,
         ]
     )
-    small_part = small_sum(split_tiles(small_full, tile).reshape(-1, tile))
-    gain_part = seq_sum(gain_grad, f32, True)
-    gain_part = gain_part + core_swap(gain_part)
-    ffn_back = pick(
-        (seq_slots[5][None, None, :] == ((my_chip + shifts) % chips)[:, None, None])
-        & (seq_slots[0][None, None, :] // 2 == my_chip)
-        & (seq_slots[0][None, None, :] >= 0)
-        & (seq_slots[4][None, None, :] == (my_core * ffn_room + jnp.arange(ffn_room))[None, :, None]),
-        jnp.where(seq_slots[0] == my_fsdp, 0, ffn_hold) + seq_slots[1],
-    )
-    near = (my_chip + shifts) % chips
-    near_key = attn_key_chip[near][:, None, :]
-    near_order = attn_order_chip[near][:, None, :]
-    near_place = by_chip(attn_place)[near][:, None, :]
-
-    def attn_cut(core):
-        index = pick(
-            (near_key == 2 * my_seq + core)
-            & (near_order == jnp.arange(attn_hold)[None, :, None]),
-            near_place,
-        )
-        return cut_tiles([first_grad_w, out_grad_w], index.reshape(-1), tile)
-
-    attn_given, attn_own = attn_cut(1 - my_core), attn_cut(my_core)
-    def added(one, two):
-        return one.astype(f32) + two.astype(f32)
-
-    attn_own = added(attn_own, core_swap(attn_given)).reshape(chips, attn_hold, tile, tile)
-    attn_sum = attn_own[0]
-    for offset in range(1, chips):
-        attn_sum = attn_sum + chip_shift(attn_own[offset].astype(bf16), offset).astype(f32)
-    attn_sum = attn_sum.astype(bf16)
-    attn_back = pick(
-        (column_slots[3][None, None, :] == (my_seq ^ flips)[:, None, None])
-        & (column_slots[0][None, None, :] == my_key)
-        & (column_slots[2][None, None, :] == jnp.arange(attn_room)[None, :, None]),
-        column_slots[1],
-    )
-    ffn_sum, attn_sum, small_part, gain_part = lax.optimization_barrier(
-        (ffn_sum, attn_sum, small_part, gain_part)
-    )
-    ffn_sums = [ffn_sum, core_swap(ffn_sum)]
+    late_full = jnp.concatenate(
+        [matmul_outer(normed_low, left_grad_low), matmul_outer(right_grad_low, left_low)], axis=1
+    )
+    late = jnp.concatenate(
+        [late_full.reshape(seq_size, -1), gain_grad.reshape(seq_size, -1)], axis=1
+    ).reshape(seq_size, -1, tile)
+    late = seq_sum(late.reshape(-1, tile), bf16, True)
+
+    ffn_sums = [both_sum, core_swap(both_sum), down_sum, core_swap(down_sum)]
     ffn_return = [gather_tiles(ffn_sums, ffn_back[i]) for i in range(chips)]
-    ffn_return, gain_part, small_part = lax.optimization_barrier((ffn_return, gain_part, small_part))
-    small_grad = small_all(small_part).reshape(small_master.shape)
+    ffn_return, attn_sum, late, input_grad = lax.optimization_barrier(
+        (ffn_return, attn_sum, late, input_grad)
+    )
     ffn_returned = chip_exchange(ffn_return)
     ffn_returned = ffn_returned + [core_swap(value) for value in ffn_returned]
-    gain_grad_mine = gain_part
+    late = late + core_swap(late.astype(bf16)).astype(f32)
+    late_low = late.astype(bf16)
     for offset in range(1, chips):
-        gain_grad_mine = gain_grad_mine + chip_shift(gain_part, offset)
+        late = late + chip_shift(late_low, offset).astype(f32)
+    late_rows = late_full.shape[0] // seq_size
+    late_tiles = late[:late_rows].reshape(-1, 1, tile, tile)
+    gain_grad_mine = late[late_rows:].reshape(-1)
+    small_grad = jnp.concatenate(
+        [
+            late_tiles.astype(bf16),
+            small_early.reshape(late_tiles.shape[0], -1, tile, tile),
+        ],
+        axis=1,
+    ).reshape(small_master.shape)
     attn_returned = seq_exchange([gather_tiles([attn_sum], attn_back[i]) for i in range(seq_size)])
     attn_returned = attn_returned + [core_swap(value) for value in attn_returned]
     slot_grad = jnp.where(my_slots[0] >= 0, my_slots[1], 2 * half + my_slots[2])
@@ -937,7 +1033,7 @@
         parts = jnp.concatenate(own_ffn + own_attn + (jnp.zeros((1, tile, tile), bf16),))
         index = jnp.where(
             ffn_to == my_fsdp,
-            ffn_place,
+            is_down * both_count + ffn_place,
             jnp.where(attn_to == my_seq, ffn_count + attn_place, ffn_count + attn_count),
         )
         spread = gather_tiles([parts], index.reshape(-1))
@@ -945,6 +1041,7 @@
 
     tile_grads = ffn_returned + attn_returned
     slow_start = 2 * half + 2 * seq_size * attn_room
+    slow_steps = jnp.where(fits, 0, 1)
     slow_grads = lax.fori_loop(0, slow_steps, slow_return, jnp.zeros((mine, tile, tile), bf16))
     tile_grads = tile_grads + [slow_grads]
     slot_grad = jnp.where(fits, slot_grad, slow_start + local_slots)

time: 1270 us -> 1300 us (1.024)
  waiting for transfers between devices: 694 us -> 636 us
  local copies, waits for them, and re-layouts: 102 us -> 158 us
  other arithmetic: 103 us -> 134 us
  Pallas kernels: 158 us -> 175 us
    all_gather x1, waiting for transfers between devices: 45.8 us -> 0.01 us  [on_device(): lax.all_gather(grad_down.astype(bf16), 'fsdp', axis=0, tiled=True)]
    psum x1 -> x0, waiting for transfers between devices: 23.7 us -> none  [small_all(): return lax.psum(both, 'fsdp').reshape((2 * kept.shape[0],) + kept.shape[1:])]
    pallas_call x21 -> x26, Pallas kernels: 110 us -> 127 us  [tile_kernel_call(): pl.pallas_call(kernel, grid=(steps,), cost_estimate=pl.CostEstimate(flops...]
    gather x2 -> x36, local copies, waits for them, and re-layouts: 2.94 us -> 18.6 us  [seq_ordered(): return parts[lax.axis_index('seq') ^ jnp.arange(size)]]
    ppermute x32 -> x27, starting transfers between devices: 31.1 us -> 24.8 us  [seq_swap(): return lax.ppermute(value, 'seq', [(i, i ^ flip) for i in range(size)])]
    ppermute x32 -> x27, waiting for transfers between devices: 171 us -> 175 us  [seq_swap(): return lax.ppermute(value, 'seq', [(i, i ^ flip) for i in range(size)])]
    unnamed x422 -> x421, local copies, waits for them, and re-layouts: 53.8 us -> 52.8 us
    ppermute x15 -> x21, waiting for transfers between devices: 331 us -> 331 us  [chip_shift(): lax.ppermute(value, 'fsdp', [(i, (i // 2 + offset) % chips * 2 + i % 2) f...]
  transfers between devices with their start and end apart: 77 -> 79, of which waited for: 32 -> 43; matrix products, arithmetic and copies ran while one was open for 16% -> 20% of each run, Pallas kernels for 6% -> 4%
where the time goes in v7:
time: 1300 us; the launch traced here: 1280 us
  waiting for transfers between devices  636 us (49%)
  Pallas kernels  175 us (13%)
  local copies, waits for them, and re-layouts  158 us (12%)
  other arithmetic  134 us (10%)
  matrix products  96.2 us (7%)
  starting transfers between devices  64.6 us (5%)
  between operations  18.9 us (1%)
    ppermute x21, waiting for transfers between devices, chip_shift(): lax.ppermute(value, 'fsdp', [(i, (i // 2 + offset) % chips * 2 + i % 2) f...  331 us
    ppermute x27, waiting for transfers between devices, seq_swap(): return lax.ppermute(value, 'seq', [(i, i ^ flip) for i in range(size)])  175 us
    pallas_call x26, Pallas kernels, tile_kernel_call(): pl.pallas_call(kernel, grid=(steps,), cost_estimate=pl.CostEstimate(flops...  127 us
    unnamed x421, local copies, waits for them, and re-layouts  52.8 us
    reduce_scatter x1, waiting for transfers between devices, on_device(): lax.psum_scatter(matmul_flip(hidden_low, w_down).astype(bf16), 'fsdp', sc...  48.4 us
    all_gather x1, waiting for transfers between devices, on_device(): feed_low = lax.all_gather(feed_own, 'fsdp', axis=0, tiled=True)  48.2 us
    pallas_call x2, Pallas kernels, rotate_update(): pl.pallas_call(kernel, grid=(count // each,), out_shape=(shape, shape, sh...  48.2 us
    dot_general x8, matrix products, matmul(): return jnp.dot(left, right, preferred_element_type=jnp.float32)  32.1 us
  transfers between devices with their start and end apart: 79, of which 43 were waited for; matrix products, arithmetic and copies ran while one was open for 20% of the time, Pallas kernels for 4%

profile of v7, /device:TPU:9, one launch (start us, length us, event | category | flops | bytes accessed | tf_op | source)
XLA Modules:
  0.0 1283.2 jit_solution(2259934482546259210)
XLA Ops:
  75.8 69.3 %collective-permute-done.1.refs_1_ = bf16[37,128,128]{2,1,0:T(8,128)(2,1)S(1)} collective-permute-done((bf16[37,128,128]{2,1,0:T(8,128)(2,1)}, bf16[37,128,128]{2,1,0:T(8,128)(2,1)S(1)}, u32[]{:S(2)}, u32[]{:S(2)}) %collective-permute-start.1) | collective-permute-done | bytes 1212448 | tf_op jit(solution)/shard_map/ppermute | solution.py:364
  195.0 9.8 shard_map.298
  213.3 17.1 %collective-permute-done.11 = bf16[33,128,128]{2,1,0:T(8,128)(2,1)} collective-permute-done((bf16[33,128,128]{2,1,0:T(8,128)(2,1)}, bf16[33,128,128]{2,1,0:T(8,128)(2,1)}, u32[]{:S(2)}, u32[]{:S(2)}) %collective-permute-start.11) | collective-permute-done | bytes 1081376 | tf_op jit(solution)/shard_map/ppermute | solution.py:364
  232.3 65.7 %collective-permute-done.12 = bf16[33,128,128]{2,1,0:T(8,128)(2,1)} collective-permute-done((bf16[33,128,128]{2,1,0:T(8,128)(2,1)}, bf16[33,128,128]{2,1,0:T(8,128)(2,1)}, u32[]{:S(2)}, u32[]{:S(2)}) %collective-permute-start.12) | collective-permute-done | bytes 1081376 | tf_op jit(solution)/shard_map/ppermute | solution.py:364
  308.9 14.3 %all-gather.14.cloned.1.call-done = bf16[368,128,128]{2,1,0:T(8,128)(2,1)} async-done(((bf16[92,128,128]{2,1,0:T(8,128)(2,1)}), bf16[368,128,128]{2,1,0:T(8,128)(2,1)}) %all-gather.14.cloned.1.call-update) | async-done | bytes 12058640 | tf_op jit(solution)/shard_map/all_gather | solution.py:768
  323.3 10.8 conditional.4
  323.3 10.7 branch_1_fun.4
  334.1 10.2 conditional.3
  334.1 10.2 branch_1_fun.3
  366.1 11.4 collective-permute-done.18
  400.5 11.6 collective-permute-done.19
  414.6 19.9 %collective-permute-done.21 = bf16[128,2048]{1,0:T(8,128)(2,1)} collective-permute-done((bf16[128,2048]{1,0:T(8,128)(2,1)}, bf16[128,2048]{1,0:T(8,128)(2,1)}, u32[]{:S(2)}, u32[]{:S(2)}) %collective-permute-start.21) | collective-permute-done | bytes 524320 | tf_op jit(solution)/shard_map/ppermute | solution.py:353
  439.8 13.7 %all-gather.18.cloned.1.call-done = bf16[224,128,128]{2,1,0:T(8,128)(2,1)} async-done(((bf16[56,128,128]{2,1,0:T(8,128)(2,1)}), bf16[224,128,128]{2,1,0:T(8,128)(2,1)}) %all-gather.18.cloned.1.call-update) | async-done | bytes 7340048 | tf_op jit(solution)/shard_map/all_gather | solution.py:769
  454.9 10.3 conditional.5
  466.0 48.2 %all-gather.16.cloned.1.call-done = bf16[1024,2048]{1,0:T(8,128)(2,1)} async-done(((bf16[128,2048]{1,0:T(8,128)(2,1)}), bf16[1024,2048]{1,0:T(8,128)(2,1)}) %all-gather.16.cloned.1.call-update) | async-done | bytes 4194320 | tf_op jit(solution)/shard_map/all_gather | solution.py:858
  514.2 12.5 fusion.286
  539.1 48.4 %reduce-scatter.11.cloned.1.call-done = bf16[128,2048]{1,0:T(8,128)(2,1)} async-done(((bf16[1024,2048]{1,0:T(8,128)(2,1)}), bf16[128,2048]{1,0:T(8,128)(2,1)}) %reduce-scatter.11.cloned.1.call-update) | async-done | bytes 524304 | tf_op jit(solution)/shard_map/reduce_scatter | solution.py:864
  673.4 9.7 fusion.13
  685.7 10.5 convolution_convert_fusion.1
  720.5 10.8 convolution_convert_fusion.refs_0_
  734.6 12.1 shard_map.303
  783.6 21.0 %collective-permute-done.40 = bf16[128,2048]{1,0:T(8,128)(2,1)S(1)} collective-permute-done((bf16[128,2048]{1,0:T(8,128)(2,1)}, bf16[128,2048]{1,0:T(8,128)(2,1)S(1)}, u32[]{:S(2)}, u32[]{:S(2)}) %collective-permute-start.40) | collective-permute-done | bytes 524320 | tf_op jit(solution)/shard_map/ppermute | solution.py:353
  804.6 23.7 %collective-permute-done.42 = bf16[128,2048]{1,0:T(8,128)(2,1)} collective-permute-done((bf16[128,2048]{1,0:T(8,128)(2,1)}, bf16[128,2048]{1,0:T(8,128)(2,1)}, u32[]{:S(2)}, u32[]{:S(2)}) %collective-permute-start.42) | collective-permute-done | bytes 524320 | tf_op jit(solution)/shard_map/ppermute | solution.py:353
  844.4 9.5 collective-permute-done.43
  896.3 29.8 %collective-permute-done.37 = bf16[28,128,128]{2,1,0:T(8,128)(2,1)S(1)} collective-permute-done((bf16[28,128,128]{2,1,0:T(8,128)(2,1)S(1)}, bf16[28,128,128]{2,1,0:T(8,128)(2,1)S(1)}, u32[]{:S(2)}, u32[]{:S(2)}) %collective-permute-start.37) | collective-permute-done | bytes 917536 | tf_op jit(solution)/shard_map/ppermute | solution.py:353
  930.9 10.5 collective-permute-done.45
  941.6 12.0 collective-permute-done.47
  994.3 17.9 %collective-permute-done.48 = bf16[33,128,128]{2,1,0:T(8,128)(2,1)S(1)} collective-permute-done((bf16[33,128,128]{2,1,0:T(8,128)(2,1)}, bf16[33,128,128]{2,1,0:T(8,128)(2,1)S(1)}, u32[]{:S(2)}, u32[]{:S(2)}) %collective-permute-start.48) | collective-permute-done | bytes 1081376 | tf_op jit(solution)/shard_map/ppermute | solution.py:364
  1012.2 68.6 %collective-permute-done.49 = bf16[33,128,128]{2,1,0:T(8,128)(2,1)S(1)} collective-permute-done((bf16[33,128,128]{2,1,0:T(8,128)(2,1)}, bf16[33,128,128]{2,1,0:T(8,128)(2,1)S(1)}, u32[]{:S(2)}, u32[]{:S(2)}) %collective-permute-start.49) | collective-permute-done | bytes 1081376 | tf_op jit(solution)/shard_map/ppermute | solution.py:364
  1123.6 51.7 %collective-permute-done.71 = bf16[537,128]{1,0:T(8,128)(2,1)S(1)} collective-permute-done((bf16[537,128]{1,0:T(8,128)(2,1)S(1)}, bf16[537,128]{1,0:T(8,128)(2,1)S(1)}, u32[]{:S(2)}, u32[]{:S(2)}) %collective-permute-start.71) | collective-permute-done | bytes 137504 | tf_op jit(solution)/shard_map/ppermute | solution.py:364
  1209.1 15.5 %collective-permute-done.55.refs_2_ = bf16[37,128,128]{2,1,0:T(8,128)(2,1)} collective-permute-done((bf16[37,128,128]{2,1,0:T(8,128)(2,1)}, bf16[37,128,128]{2,1,0:T(8,128)(2,1)}, u32[]{:S(2)}, u32[]{:S(2)}) %collective-permute-start.55) | collective-permute-done | bytes 1212448 | tf_op jit(solution)/shard_map/ppermute | solution.py:364
  1235.0 41.1 %shard_map.316 = (f32[116,128,128]{2,1,0:T(8,128)}, f32[116,128,128]{2,1,0:T(8,128)}, f32[116,128,128]{2,1,0:T(8,128)}) custom-call(s32[116]{0:T(128)S(1)} %fusion.219.index_ref, bf16[37,128,128]{2,1,0:T(8,128)(2,1)} %shard_map.306.refs_0_, bf16[37,128,128]{2,1,0:T(8,128)(2,1)} %collective-permute-done.54.refs_1_, ...), custom_call_target="tpu_custom_call" | custom-call | tf_op jit(solution)/shard_map/pallas_call | solution.py:335
  (977 shorter events, 571.6 us)
Async XLA Ops:
  7.2 316.1 %all-gather.14.cloned.1.call-start = ((), (), s32[]{:S(2)}) async-start(), calls=%async_computation.7 | async-start | bytes 15073280 | tf_op jit(solution)/shard_map/all_gather | solution.py:768
  62.4 108.8 %collective-permute-start.4 = (bf16[40,128,128]{2,1,0:T(8,128)(2,1)}, bf16[40,128,128]{2,1,0:T(8,128)(2,1)}, u32[]{:S(2)}, u32[]{:S(2)}) collective-permute-start(bf16[40,128,128]{2,1,0:T(8,128)(2,1)} %get-tuple-element.727), channel_id=1, source_target_pairs={{0,8},{8,0},{16,24},{24,16},{1,9},{9,1},{17,25},{25,17},{2,10},{10... | collective-permute-start | bytes 3932168 | tf_op jit(solution)/shard_map/ppermute | solution.py:353
  63.5 107.6 %collective-permute-start.5 = (bf16[40,128,128]{2,1,0:T(8,128)(2,1)}, bf16[40,128,128]{2,1,0:T(8,128)(2,1)}, u32[]{:S(2)}, u32[]{:S(2)}) collective-permute-start(bf16[40,128,128]{2,1,0:T(8,128)(2,1)} %get-tuple-element.726), channel_id=1, source_target_pairs={{0,16},{8,24},{16,0},{24,8},{1,17},{9,25},{17,1},{25,9},{2,18},{10... | collective-permute-start | bytes 3932168 | tf_op jit(solution)/shard_map/ppermute | solution.py:353
  64.9 106.3 %collective-permute-start.6 = (bf16[40,128,128]{2,1,0:T(8,128)(2,1)}, bf16[40,128,128]{2,1,0:T(8,128)(2,1)}, u32[]{:S(2)}, u32[]{:S(2)}) collective-permute-start(bf16[40,128,128]{2,1,0:T(8,128)(2,1)} %get-tuple-element.725), channel_id=1, source_target_pairs={{0,24},{8,16},{16,8},{24,0},{1,25},{9,17},{17,9},{25,1},{2,26},{10... | collective-permute-start | bytes 3932168 | tf_op jit(solution)/shard_map/ppermute | solution.py:353
  65.0 80.0 %collective-permute-start.1 = (bf16[37,128,128]{2,1,0:T(8,128)(2,1)}, bf16[37,128,128]{2,1,0:T(8,128)(2,1)S(1)}, u32[]{:S(2)}, u32[]{:S(2)}) collective-permute-start(bf16[37,128,128]{2,1,0:T(8,128)(2,1)} %shard_map.294), channel_id=1, source_target_pairs={{0,2},{1,3},{2,4},{3,5},{4,6},{5,7},{6,0},{7,1},{8,10},{9,11},{10,... | collective-permute-start | bytes 3637256 | tf_op jit(solution)/shard_map/ppermute | solution.py:364
  66.3 103.7 %collective-permute-start.2 = (bf16[37,128,128]{2,1,0:T(8,128)(2,1)}, bf16[37,128,128]{2,1,0:T(8,128)(2,1)}, u32[]{:S(2)}, u32[]{:S(2)}) collective-permute-start(bf16[37,128,128]{2,1,0:T(8,128)(2,1)} %shard_map.295), channel_id=1, source_target_pairs={{0,4},{1,5},{2,6},{3,7},{4,0},{5,1},{6,2},{7,3},{8,12},{9,13},{10,... | collective-permute-start | bytes 3637256 | tf_op jit(solution)/shard_map/ppermute | solution.py:364
  205.1 92.9 %collective-permute-start.12 = (bf16[33,128,128]{2,1,0:T(8,128)(2,1)}, bf16[33,128,128]{2,1,0:T(8,128)(2,1)}, u32[]{:S(2)}, u32[]{:S(2)}) collective-permute-start(bf16[33,128,128]{2,1,0:T(8,128)(2,1)} %shard_map.300), channel_id=1, source_target_pairs={{0,4},{1,5},{2,6},{3,7},{4,0},{5,1},{6,2},{7,3},{8,12},{9,13},{10,... | collective-permute-start | bytes 3244040 | tf_op jit(solution)/shard_map/ppermute | solution.py:364
  207.0 93.6 %collective-permute-start.13 = (bf16[33,128,128]{2,1,0:T(8,128)(2,1)}, bf16[33,128,128]{2,1,0:T(8,128)(2,1)}, u32[]{:S(2)}, u32[]{:S(2)}) collective-permute-start(bf16[33,128,128]{2,1,0:T(8,128)(2,1)} %shard_map.300), channel_id=1, source_target_pairs={{0,6},{1,7},{2,0},{3,1},{4,2},{5,3},{6,4},{7,5},{8,14},{9,15},{10,... | collective-permute-start | bytes 3244040 | tf_op jit(solution)/shard_map/ppermute | solution.py:364
  213.1 95.8 %collective-permute-start.14 = (bf16[33,128,128]{2,1,0:T(8,128)(2,1)}, bf16[33,128,128]{2,1,0:T(8,128)(2,1)}, u32[]{:S(2)}, u32[]{:S(2)}) collective-permute-start(bf16[33,128,128]{2,1,0:T(8,128)(2,1)} %shard_map.300), channel_id=1, source_target_pairs={{0,1},{1,0},{2,3},{3,2},{4,5},{5,4},{6,7},{7,6},{8,9},{9,8},{10,11... | collective-permute-start | bytes 3244040 | tf_op jit(solution)/shard_map/ppermute | solution.py:358
  230.4 78.6 %collective-permute-start.15 = (bf16[33,128,128]{2,1,0:T(8,128)(2,1)}, bf16[33,128,128]{2,1,0:T(8,128)(2,1)}, u32[]{:S(2)}, u32[]{:S(2)}) collective-permute-start(bf16[33,128,128]{2,1,0:T(8,128)(2,1)} %collective-permute-done.11), channel_id=1, source_target_pairs={{0,1},{1,0},{2,3},{3,2},{4,5},{5,4},{6,7},{7,6},{8,9},{9,8},{10,11... | collective-permute-start | bytes 3244040 | tf_op jit(solution)/shard_map/ppermute | solution.py:358
  344.3 109.3 %all-gather.18.cloned.1.call-start = ((), (), s32[]{:S(2)}) async-start(), calls=%async_computation.9 | async-start | bytes 9175040 | tf_op jit(solution)/shard_map/all_gather | solution.py:769
  389.1 45.4 %collective-permute-start.21 = (bf16[128,2048]{1,0:T(8,128)(2,1)}, bf16[128,2048]{1,0:T(8,128)(2,1)}, u32[]{:S(2)}, u32[]{:S(2)}) collective-permute-start(bf16[128,2048]{1,0:T(8,128)(2,1)} %get-tuple-element.704), channel_id=1, source_target_pairs={{0,24},{8,16},{16,8},{24,0},{1,25},{9,17},{17,9},{25,1},{2,26},{10... | collective-permute-start | bytes 1572872 | tf_op jit(solution)/shard_map/ppermute | solution.py:353
  465.2 49.0 %all-gather.16.cloned.1.call-start = ((), (), s32[]{:S(2)}) async-start(), calls=%async_computation.8 | async-start | bytes 4718592 | tf_op jit(solution)/shard_map/all_gather | solution.py:858
  465.9 121.6 %reduce-scatter.11.cloned.1.call-start = ((), (), s32[]{:S(2)}) async-start(), calls=%async_computation.10 | async-start | bytes 4718592 | tf_op jit(solution)/shard_map/reduce_scatter | solution.py:864
  539.0 120.3 %all-gather.20.cloned.1.call-start = ((), (), s32[]{:S(2)}) async-start(), calls=%async_computation.11 | async-start | bytes 4718592 | tf_op jit(solution)/shard_map/all_gather | solution.py:885
  597.3 169.4 %reduce-scatter.13.cloned.1.call-start = ((), (), s32[]{:S(2)}) async-start(), calls=%async_computation.12 | async-start | bytes 4718592 | tf_op jit(solution)/shard_map/reduce_scatter | solution.py:903
  696.2 275.5 %reduce-scatter.15.cloned.1.call-start = ((), (), s32[]{:S(2)}) async-start(), calls=%async_computation.13 | async-start | bytes 15073280 | tf_op jit(solution)/shard_map/reduce_scatter | solution.py:913
  713.9 44.2 %collective-permute-start.35 = (bf16[56,128,128]{2,1,0:T(8,128)(2,1)}, bf16[56,128,128]{2,1,0:T(8,128)(2,1)}, u32[]{:S(2)}, u32[]{:S(2)}) collective-permute-start(bf16[56,128,128]{2,1,0:T(8,128)(2,1)} %shard_map.302), channel_id=1, source_target_pairs={{0,16},{8,24},{16,0},{24,8},{1,17},{9,25},{17,1},{25,9},{2,18},{10... | collective-permute-start | bytes 5505032 | tf_op jit(solution)/shard_map/ppermute | solution.py:353
  781.0 47.3 %collective-permute-start.42 = (bf16[128,2048]{1,0:T(8,128)(2,1)}, bf16[128,2048]{1,0:T(8,128)(2,1)}, u32[]{:S(2)}, u32[]{:S(2)}) collective-permute-start(bf16[128,2048]{1,0:T(8,128)(2,1)} %get-tuple-element.717), channel_id=1, source_target_pairs={{0,24},{8,16},{16,8},{24,0},{1,25},{9,17},{17,9},{25,1},{2,26},{10... | collective-permute-start | bytes 1572872 | tf_op jit(solution)/shard_map/ppermute | solution.py:353
  866.1 88.8 %collective-permute-start.44 = (bf16[132,128,128]{2,1,0:T(8,128)(2,1)}, bf16[132,128,128]{2,1,0:T(8,128)(2,1)}, u32[]{:S(2)}, u32[]{:S(2)}) collective-permute-start(bf16[132,128,128]{2,1,0:T(8,128)(2,1)} %shard_map.311), channel_id=1, source_target_pairs={{0,1},{1,0},{2,3},{3,2},{4,5},{5,4},{6,7},{7,6},{8,9},{9,8},{10,11... | collective-permute-start | bytes 12976136 | tf_op jit(solution)/shard_map/ppermute | solution.py:358
  888.4 53.0 %collective-permute-start.45 = (bf16[128,2048]{1,0:T(8,128)(2,1)S(1)}, bf16[128,2048]{1,0:T(8,128)(2,1)S(1)}, u32[]{:S(2)}, u32[]{:S(2)}) collective-permute-start(bf16[128,2048]{1,0:T(8,128)(2,1)S(1)} %get-tuple-element.700), channel_id=1, source_target_pairs={{0,8},{8,0},{16,24},{24,16},{1,9},{9,1},{17,25},{25,17},{2,10},{10... | collective-permute-start | bytes 1572872 | tf_op jit(solution)/shard_map/ppermute | solution.py:353
  889.6 52.0 %collective-permute-start.46 = (bf16[128,2048]{1,0:T(8,128)(2,1)S(1)}, bf16[128,2048]{1,0:T(8,128)(2,1)S(1)}, u32[]{:S(2)}, u32[]{:S(2)}) collective-permute-start(bf16[128,2048]{1,0:T(8,128)(2,1)S(1)} %get-tuple-element.702), channel_id=1, source_target_pairs={{0,16},{8,24},{16,0},{24,8},{1,17},{9,25},{17,1},{25,9},{2,18},{10... | collective-permute-start | bytes 1572872 | tf_op jit(solution)/shard_map/ppermute | solution.py:353
  929.5 155.4 %collective-permute-start.39 = (bf16[56,128,128]{2,1,0:T(8,128)(2,1)}, bf16[56,128,128]{2,1,0:T(8,128)(2,1)}, u32[]{:S(2)}, u32[]{:S(2)}) collective-permute-start(bf16[56,128,128]{2,1,0:T(8,128)(2,1)} %pad_maximum_fusion.9.refs_2_), channel_id=1, source_target_pairs={{0,1},{1,0},{2,3},{3,2},{4,5},{5,4},{6,7},{7,6},{8,9},{9,8},{10,11... | collective-permute-start | bytes 5505032 | tf_op jit(solution)/shard_map/ppermute | solution.py:358
  971.8 113.2 %collective-permute-start.36 = (bf16[92,128,128]{2,1,0:T(8,128)(2,1)}, bf16[92,128,128]{2,1,0:T(8,128)(2,1)S(1)}, u32[]{:S(2)}, u32[]{:S(2)}) collective-permute-start(bf16[92,128,128]{2,1,0:T(8,128)(2,1)} %reduce-scatter.15.cloned.1.call-done.refs_0_), channel_id=1, source_target_pairs={{0,1},{1,0},{2,3},{3,2},{4,5},{5,4},{6,7},{7,6},{8,9},{9,8},{10,11... | collective-permute-start | bytes 9043976 | tf_op jit(solution)/shard_map/ppermute | solution.py:358
  989.0 91.8 %collective-permute-start.49 = (bf16[33,128,128]{2,1,0:T(8,128)(2,1)}, bf16[33,128,128]{2,1,0:T(8,128)(2,1)S(1)}, u32[]{:S(2)}, u32[]{:S(2)}) collective-permute-start(bf16[33,128,128]{2,1,0:T(8,128)(2,1)} %get-tuple-element.327), channel_id=1, source_target_pairs={{0,4},{1,5},{2,6},{3,7},{4,0},{5,1},{6,2},{7,3},{8,12},{9,13},{10,... | collective-permute-start | bytes 3244040 | tf_op jit(solution)/shard_map/ppermute | solution.py:364
  990.8 93.4 %collective-permute-start.50 = (bf16[33,128,128]{2,1,0:T(8,128)(2,1)}, bf16[33,128,128]{2,1,0:T(8,128)(2,1)S(1)}, u32[]{:S(2)}, u32[]{:S(2)}) collective-permute-start(bf16[33,128,128]{2,1,0:T(8,128)(2,1)} %get-tuple-element.328), channel_id=1, source_target_pairs={{0,6},{1,7},{2,0},{3,1},{4,2},{5,3},{6,4},{7,5},{8,14},{9,15},{10,... | collective-permute-start | bytes 3244040 | tf_op jit(solution)/shard_map/ppermute | solution.py:364
  1104.4 76.3 %collective-permute-start.63 = (bf16[13,128,128]{2,1,0:T(8,128)(2,1)}, bf16[13,128,128]{2,1,0:T(8,128)(2,1)}, u32[]{:S(2)}, u32[]{:S(2)}) collective-permute-start(bf16[13,128,128]{2,1,0:T(8,128)(2,1)} %shard_map.315), channel_id=1, source_target_pairs={{0,24},{8,16},{16,8},{24,0},{1,25},{9,17},{17,9},{25,1},{2,26},{10... | collective-permute-start | bytes 1277960 | tf_op jit(solution)/shard_map/ppermute | solution.py:353
  1106.5 75.1 %collective-permute-start.62 = (bf16[13,128,128]{2,1,0:T(8,128)(2,1)}, bf16[13,128,128]{2,1,0:T(8,128)(2,1)}, u32[]{:S(2)}, u32[]{:S(2)}) collective-permute-start(bf16[13,128,128]{2,1,0:T(8,128)(2,1)} %shard_map.314), channel_id=1, source_target_pairs={{0,16},{8,24},{16,0},{24,8},{1,17},{9,25},{17,1},{25,9},{2,18},{10... | collective-permute-start | bytes 1277960 | tf_op jit(solution)/shard_map/ppermute | solution.py:353
  1110.3 65.0 %collective-permute-start.71 = (bf16[537,128]{1,0:T(8,128)(2,1)S(1)}, bf16[537,128]{1,0:T(8,128)(2,1)S(1)}, u32[]{:S(2)}, u32[]{:S(2)}) collective-permute-start(bf16[537,128]{1,0:T(8,128)(2,1)S(1)} %fusion.109), channel_id=1, source_target_pairs={{0,6},{1,7},{2,0},{3,1},{4,2},{5,3},{6,4},{7,5},{8,14},{9,15},{10,... | collective-permute-start | bytes 412424 | tf_op jit(solution)/shard_map/ppermute | solution.py:364
  1113.7 95.0 %collective-permute-start.54 = (bf16[37,128,128]{2,1,0:T(8,128)(2,1)}, bf16[37,128,128]{2,1,0:T(8,128)(2,1)}, u32[]{:S(2)}, u32[]{:S(2)}) collective-permute-start(bf16[37,128,128]{2,1,0:T(8,128)(2,1)} %shard_map.307), channel_id=1, source_target_pairs={{0,2},{1,3},{2,4},{3,5},{4,6},{5,7},{6,0},{7,1},{8,10},{9,11},{10,... | collective-permute-start | bytes 3637256 | tf_op jit(solution)/shard_map/ppermute | solution.py:364
  1120.0 104.6 %collective-permute-start.55 = (bf16[37,128,128]{2,1,0:T(8,128)(2,1)}, bf16[37,128,128]{2,1,0:T(8,128)(2,1)}, u32[]{:S(2)}, u32[]{:S(2)}) collective-permute-start(bf16[37,128,128]{2,1,0:T(8,128)(2,1)} %shard_map.308), channel_id=1, source_target_pairs={{0,4},{1,5},{2,6},{3,7},{4,0},{5,1},{6,2},{7,3},{8,12},{9,13},{10,... | collective-permute-start | bytes 3637256 | tf_op jit(solution)/shard_map/ppermute | solution.py:364
  1175.3 52.1 %collective-permute-start.56 = (bf16[37,128,128]{2,1,0:T(8,128)(2,1)}, bf16[37,128,128]{2,1,0:T(8,128)(2,1)}, u32[]{:S(2)}, u32[]{:S(2)}) collective-permute-start(bf16[37,128,128]{2,1,0:T(8,128)(2,1)} %shard_map.309), channel_id=1, source_target_pairs={{0,6},{1,7},{2,0},{3,1},{4,2},{5,3},{6,4},{7,5},{8,14},{9,15},{10,... | collective-permute-start | bytes 3637256 | tf_op jit(solution)/shard_map/ppermute | solution.py:364
  (248 other events, 4747.3 us)
Sparse Core Ops, SparseCore 0:
  204.9 118.2 all-gather.13
  347.0 106.5 all-gather.17
  468.2 45.9 all-gather.15
  539.1 48.3 reduce-scatter.10
  597.5 48.8 all-gather.19
  696.4 48.0 reduce-scatter.12
  769.0 166.7 reduce-scatter.14

commit v8 on v7

--- a/solution.py
+++ b/solution.py
@@ -353,6 +353,12 @@
     return lax.ppermute(value, "seq", [(i, i ^ flip) for i in range(size)])
 
 
+def take_blocks(value, order):
+    return jnp.stack(
+        [lax.dynamic_index_in_dim(value, order[i], 0, False) for i in range(order.shape[0])]
+    )
+
+
 def core_swap(value):
     size = lax.axis_size("fsdp")
     return lax.ppermute(value, "fsdp", [(i, i ^ 1) for i in range(size)])
@@ -374,7 +380,7 @@
 def seq_ordered(value):
     size = lax.axis_size("seq")
     parts = jnp.stack([value] + [seq_swap(value, flip) for flip in range(1, size)], axis=0)
-    return parts[lax.axis_index("seq") ^ jnp.arange(size)]
+    return take_blocks(parts, lax.axis_index("seq") ^ jnp.arange(size))
 
 
 def seq_exchange(values):
@@ -385,7 +391,7 @@
     size = lax.axis_size("seq")
     parts = value.reshape((size, value.shape[0] // size) + value.shape[1:])
     if ordered:
-        parts = parts[lax.axis_index("seq") ^ jnp.arange(size)]
+        parts = take_blocks(parts, lax.axis_index("seq") ^ jnp.arange(size))
     total = parts[0]
     for flip in range(1, size):
         total = total + seq_swap(parts[flip].astype(wire), flip).astype(jnp.float32)
@@ -414,13 +420,13 @@
     kept = kept + core_swap(given).astype(jnp.float32)
     kept = seq_sum(kept.reshape((-1,) + low.shape[1:]), jnp.bfloat16, True)
     kept = kept.reshape((chips, kept.shape[0] // chips) + kept.shape[1:])
-    kept = kept[(chip + jnp.arange(chips)) % chips]
+    kept = take_blocks(kept, (chip + jnp.arange(chips)) % chips)
     total = kept[0]
     for offset in range(1, chips):
         total = total + chip_shift(kept[offset].astype(jnp.bfloat16), offset).astype(jnp.float32)
     total = total.astype(jnp.bfloat16)
     parts = jnp.stack([total] + [chip_shift(total, offset) for offset in range(1, chips)])
-    parts = parts[(chip - jnp.arange(chips)) % chips]
+    parts = take_blocks(parts, (chip - jnp.arange(chips)) % chips)
     return core_pair(parts).reshape((value.shape[0] // seq_size,) + value.shape[1:])
 
 
@@ -496,9 +502,8 @@
     attn_hold = (room(attn_count, 1.0 / chips) + 1) // 2 + 1
     ffn_room = (room(2 * mine, ffn_share / chips) + 1) // 2
     both_count = row_blocks * ffn_first
-    both_hold, down_hold = (
-        (room(count, 1.0 / seq_size) + 3) // 4 * 4 for count in (both_count, ffn_count - both_count)
-    )
+    ffn_hold = (room(ffn_count, 1.0 / seq_size) + 3) // 4 * 4
+    ffn_half = ffn_hold // 2
 
     def tile_places(owner):
         row = owner // columns
@@ -513,9 +518,10 @@
         ffn_to = jnp.where(is_attn, -1, ffn_column // ffn_each)
         ffn_local = ffn_column % ffn_each
         ffn_place = jnp.where(
-            kind == 2, row * ffn_each + ffn_local, row * ffn_first + kind * ffn_each + ffn_local
+            kind == 2,
+            both_count + row * ffn_each + ffn_local,
+            row * ffn_first + kind * ffn_each + ffn_local,
         )
-        is_down = (kind == 2).astype(jnp.int32)
         attn_to = jnp.where(
             key_at < 0,
             column // query_each,
@@ -539,7 +545,7 @@
             ),
         )
         attn_to = jnp.where(is_attn, attn_to, -1)
-        return (ffn_to, is_down, ffn_place, attn_to, attn_place)
+        return (ffn_to, ffn_place, attn_to, attn_place)
 
     owners = tile_owner.reshape(seq_size, fsdp_size, mine)
     slot_seq = jnp.arange(seq_size)[:, None, None]
@@ -583,11 +589,9 @@
     )
     ffn_got = chip_exchange(ffn_sent)
 
-    ffn_to, is_down, ffn_place, attn_to, attn_place = tile_places(owners)
+    ffn_to, ffn_place, attn_to, attn_place = tile_places(owners)
     ffn_chip = jnp.where(ffn_to < 0, -1, ffn_to // 2)
-    ffn_key = jnp.where(ffn_to < 0, -1, 2 * ffn_to + is_down)
-    ffn_hold = jnp.where(is_down == 1, down_hold, both_hold)
-    seq_view = ffn_key.reshape(seq_size, fsdp_size * mine)
+    seq_view = ffn_to.reshape(seq_size, fsdp_size * mine)
     ffn_rank = count_earlier(seq_view, seq_view >= 0).reshape(owners.shape)
     attn_view = attn_to.reshape(seq_size, chips, 2 * mine)
     attn_rank = count_earlier(attn_view, attn_view >= 0).reshape(owners.shape)
@@ -636,7 +640,7 @@
     seq_slots = lax.dynamic_slice(
         jnp.stack(
             [
-                ffn_key,
+                ffn_to,
                 ffn_rank,
                 ffn_chip,
                 out_place,
@@ -679,35 +683,27 @@
             + attn_order
         ).reshape(1, -1),
     )
-    def ffn_tables(kind, hold, count):
-        key = 2 * my_fsdp + kind
-        keep = pick(
-            (seq_slots[0][None, :] == key) & (seq_slots[1][None, :] == jnp.arange(hold)[:, None]),
-            seq_slots[3][None, :],
-        )
-        join = pick(
-            (ffn_key.reshape(1, -1) == key)
-            & (ffn_place.reshape(1, -1) == jnp.arange(count)[:, None]),
-            (slot_seq * hold + ffn_rank).reshape(1, -1),
-        )
-        cut = pick(
-            (ffn_key.reshape(seq_size, 1, -1) == key)
-            & (ffn_rank.reshape(seq_size, 1, -1) == jnp.arange(hold)[None, :, None]),
-            ffn_place.reshape(seq_size, 1, -1),
-        )
-        return (keep, join, cut)
-
-    both_keep, both_join, both_cut = ffn_tables(0, both_hold, both_count)
-    down_keep, down_join, down_cut = ffn_tables(1, down_hold, ffn_count - both_count)
+    ffn_keep = pick(
+        (seq_slots[0][None, :] == my_fsdp) & (seq_slots[1][None, :] == jnp.arange(ffn_hold)[:, None]),
+        seq_slots[3][None, :],
+    )
+    ffn_join = pick(
+        (ffn_to.reshape(1, -1) == my_fsdp)
+        & (ffn_place.reshape(1, -1) == jnp.arange(ffn_count)[:, None]),
+        (
+            ffn_rank // ffn_half * (seq_size * ffn_half) + slot_seq * ffn_half + ffn_rank % ffn_half
+        ).reshape(1, -1),
+    )
+    ffn_cut = pick(
+        (ffn_to.reshape(seq_size, 1, -1) == my_fsdp)
+        & (ffn_rank.reshape(seq_size, 1, -1) == jnp.arange(ffn_hold)[None, :, None]),
+        ffn_place.reshape(seq_size, 1, -1),
+    )
     ffn_back = pick(
         (seq_slots[5][None, None, :] == ((my_chip + shifts) % chips)[:, None, None])
         & (seq_slots[2][None, None, :] == my_chip)
         & (seq_slots[4][None, None, :] == (my_core * ffn_room + jnp.arange(ffn_room))[None, :, None]),
-        jnp.where(seq_slots[0] % 2 == 1, 2 * both_hold, 0)
-        + jnp.where(
-            seq_slots[0] // 2 == my_fsdp, 0, jnp.where(seq_slots[0] % 2 == 1, down_hold, both_hold)
-        )
-        + seq_slots[1],
+        jnp.where(seq_slots[0] == my_fsdp, 0, ffn_hold) + seq_slots[1],
     )
 
     attn_sent = gather_tiles(masters, attn_pack.reshape(-1))
@@ -736,15 +732,15 @@
     turns = jnp.arange(HEAD_DIM // 2).astype(f32)
     angle = reorder(position).astype(f32)[:, None] * (THETA ** (-2.0 * turns / HEAD_DIM))[None, :]
     cosine, sine = jnp.cos(angle)[:, None, :], jnp.sin(angle)[:, None, :]
-    ready = (allow, cosine, sine, attn_join, both_join)
+    ready = (allow, cosine, sine, attn_join, ffn_join)
     ffn_got, attn_got, common, ready = lax.optimization_barrier((ffn_got, attn_got, common, ready))
-    allow, cosine, sine, attn_join, both_join = ready
+    allow, cosine, sine, attn_join, ffn_join = ready
     parts = [common] + [value[attn_room:] for value in attn_got[1:]]
     token_end = token_tiles.shape[0]
     small_end = token_end + small_rows
 
     def seq_order(value):
-        return value[my_seq ^ flips]
+        return take_blocks(value, my_seq ^ flips)
 
     pack_tokens = jnp.concatenate(
         [
@@ -763,15 +759,17 @@
     pack_normed = rms_norm(pack_tokens.astype(f32), gain_in).astype(bf16)
     attn_kept = gather_tiles(attn_got, attn_keep)
     ffn_got = ffn_got + [core_swap(value) for value in ffn_got]
-    both_kept, down_kept = gather_tiles(ffn_got, both_keep), gather_tiles(ffn_got, down_keep)
-    both_kept, down_kept, attn_kept = lax.optimization_barrier((both_kept, down_kept, attn_kept))
-    both_all = lax.all_gather(both_kept, "seq", axis=0, tiled=True)
-    down_all = lax.all_gather(down_kept, "seq", axis=0, tiled=True)
+    ffn_kept = [
+        gather_tiles(ffn_got, ffn_keep[:ffn_half]),
+        gather_tiles(ffn_got, ffn_keep[ffn_half:]),
+    ]
+    ffn_kept, attn_kept = lax.optimization_barrier((ffn_kept, attn_kept))
+    ffn_all = [lax.all_gather(value, "seq", axis=0, tiled=True) for value in ffn_kept]
     attn_all = [attn_kept] + [chip_shift(attn_kept, offset) for offset in range(1, chips)]
     attn_all = attn_all + [core_swap(value) for value in attn_all]
 
-    attn_all, both_all, pack_normed, gain_full = lax.optimization_barrier(
-        (attn_all, both_all, pack_normed, gain_full)
+    attn_all, ffn_all[0], pack_normed, gain_full = lax.optimization_barrier(
+        (attn_all, ffn_all[0], pack_normed, gain_full)
     )
     gain_in = gain_full[0:width]
 
@@ -780,7 +778,13 @@
             return join_tiles(arrays, index, row_blocks, columns_of)
 
         def slow():
-            whole = lax.all_gather(master_low, ("seq", "fsdp"), axis=0, tiled=True)
+            whole = lax.all_to_all(
+                jnp.broadcast_to(master_low[None], (seq_size * fsdp_size,) + master_low.shape),
+                ("seq", "fsdp"),
+                split_axis=0,
+                concat_axis=0,
+                tiled=True,
+            ).reshape(-1, tile, tile)
             count = row_blocks * sum(columns_of)
             slots = pick(
                 (to.reshape(1, -1) == me) & (place.reshape(1, -1) == jnp.arange(count)[:, None]),
@@ -837,9 +841,8 @@
         .astype(bf16)
         .reshape(length, per_device * HEAD_DIM)
     )
-    (w_both,) = fetch([both_all], both_join, ffn_key, 2 * my_fsdp, ffn_place, (ffn_first,))
     attn_pre = seq_sum(matmul_flip(attended_low, w_out), bf16)
-    attn_pre, w_both, small_table = lax.optimization_barrier((attn_pre, w_both, small_table))
+    attn_pre, small_table = lax.optimization_barrier((attn_pre, small_table))
     laurel_left = small_table[:, :RANK]
     laurel_right = small_table[:, RANK : 2 * RANK]
     vector_gate_w = small_table[:, 2 * RANK : 2 * RANK + PLD]
@@ -854,9 +857,11 @@
     second_sum = (first_sum + normed + laurel_normed) * ROOT_HALF
     feed_normed, feed_pull = jax.vjp(rms_norm, second_sum, gain_pre)
     feed_own = feed_normed.astype(bf16)
-    down_all, _ = lax.optimization_barrier((down_all, feed_own))
     feed_low = lax.all_gather(feed_own, "fsdp", axis=0, tiled=True)
-    (w_down,) = fetch([down_all], down_join, ffn_key, 2 * my_fsdp + 1, ffn_place, (ffn_each,))
+    ffn_all, _ = lax.optimization_barrier((ffn_all, feed_own))
+    w_both, w_down = fetch(
+        ffn_all, ffn_join, ffn_to, my_fsdp, ffn_place, (ffn_first, ffn_each)
+    )
     both_pre = matmul(feed_low, w_both)
     ffn_width = w_down.shape[1]
     hidden, hidden_pull = jax.vjp(gelu_product, both_pre[:, :ffn_width], both_pre[:, ffn_width:])
@@ -886,35 +891,24 @@
     grad_gate, grad_up = hidden_pull(matmul(down_grad_low, w_down))
     both_grad_low = jnp.concatenate([grad_gate, grad_up], axis=1).astype(bf16)
 
-    def cut_parts(flips_of, half):
-        half_now = down_hold // 2
-        index = down_cut[my_seq ^ jnp.array(flips_of), half * half_now : (half + 1) * half_now]
-        return cut_tiles([down_grad_w], index.reshape(-1), tile)
-
     early_full = jnp.concatenate(
         [matmul_outer(third_low, vector_grad_low), matmul_outer(proj_grad_low, vector_low)], axis=1
     )
     small_early = small_sum(split_tiles(early_full, tile).reshape(-1, tile))
-    down_grad_w = matmul_outer(down_grad_low, hidden_low).astype(bf16)
-    down_cuts = cut_parts([1, 3], 0), cut_parts([2, 3], 1)
-    both_grad_low, down_cuts, small_early = lax.optimization_barrier(
-        (both_grad_low, down_cuts, small_early)
-    )
+    both_grad_low, small_early = lax.optimization_barrier((both_grad_low, small_early))
     grad_feed = lax.psum_scatter(
         matmul_flip(both_grad_low, w_both).astype(bf16), "fsdp", scatter_dimension=0, tiled=True
     ).astype(f32)
-    down_one = added(cut_parts([0, 2], 0), seq_swap(down_cuts[0], 1))
-    down_two = added(cut_parts([0, 1], 1), seq_swap(down_cuts[1], 2))
     both_grad_w = matmul_outer(feed_low, both_grad_low).astype(bf16)
-    both_parts = cut_tiles([both_grad_w], both_cut.reshape(-1), tile)
-    both_parts, down_one, down_two, grad_feed = lax.optimization_barrier(
-        (both_parts, down_one, down_two, grad_feed)
-    )
-    both_sum = lax.psum_scatter(both_parts, "seq", scatter_dimension=0, tiled=True)
-    down_half = down_one.shape[0] // 2
-    down_one = added(down_one[:down_half], seq_swap(down_one[down_half:].astype(bf16), 2))
-    down_two = added(down_two[:down_half], seq_swap(down_two[down_half:].astype(bf16), 1))
-    down_sum = jnp.concatenate([down_one, down_two]).astype(bf16)
+    down_grad_w = matmul_outer(down_grad_low, hidden_low).astype(bf16)
+    ffn_parts = [
+        cut_tiles([both_grad_w, down_grad_w], index.reshape(-1), tile)
+        for index in (ffn_cut[:, :ffn_half], ffn_cut[:, ffn_half:])
+    ]
+    ffn_parts, grad_feed = lax.optimization_barrier((ffn_parts, grad_feed))
+    ffn_sums = [
+        lax.psum_scatter(value, "seq", scatter_dimension=0, tiled=True) for value in ffn_parts
+    ]
 
     grad_second_norm, grad_gain_pre = feed_pull(grad_feed)
     half_grad = (grad_third + grad_second_norm) * ROOT_HALF
@@ -951,9 +945,9 @@
     ).astype(bf16)
     first_grad_w = matmul_outer(pack_normed, first_grad_low).astype(bf16)
     near = (my_chip + shifts) % chips
-    near_key = attn_key_chip[near][:, None, :]
-    near_order = attn_order_chip[near][:, None, :]
-    near_place = by_chip(attn_place)[near][:, None, :]
+    near_key = take_blocks(attn_key_chip, near)[:, None, :]
+    near_order = take_blocks(attn_order_chip, near)[:, None, :]
+    near_place = take_blocks(by_chip(attn_place), near)[:, None, :]
 
     def attn_cut(core):
         index = pick(
@@ -964,11 +958,15 @@
         return cut_tiles([first_grad_w, out_grad_w], index.reshape(-1), tile)
 
     attn_given, attn_own = attn_cut(1 - my_core), attn_cut(my_core)
+    attn_given, attn_own, ffn_sums[0] = lax.optimization_barrier(
+        (attn_given, attn_own, ffn_sums[0])
+    )
     attn_parts = added(attn_own, core_swap(attn_given)).reshape(chips, attn_hold, tile, tile)
     attn_sum = attn_parts[0]
     attn_parts = [attn_parts[offset].astype(bf16) for offset in range(1, chips)]
-    normed_sum = seq_sum(matmul_flip(first_grad_low, w_first), bf16)
-    attn_sum, attn_parts, normed_sum = lax.optimization_barrier((attn_sum, attn_parts, normed_sum))
+    normed_pre = matmul_flip(first_grad_low, w_first)
+    attn_sum, attn_parts, normed_pre = lax.optimization_barrier((attn_sum, attn_parts, normed_pre))
+    normed_sum = seq_sum(normed_pre, bf16)
     for offset in range(1, chips):
         attn_sum = attn_sum + chip_shift(attn_parts[offset - 1], offset).astype(f32)
     attn_sum = attn_sum.astype(bf16)
@@ -1002,17 +1000,18 @@
     ).reshape(seq_size, -1, tile)
     late = seq_sum(late.reshape(-1, tile), bf16, True)
 
-    ffn_sums = [both_sum, core_swap(both_sum), down_sum, core_swap(down_sum)]
-    ffn_return = [gather_tiles(ffn_sums, ffn_back[i]) for i in range(chips)]
-    ffn_return, attn_sum, late, input_grad = lax.optimization_barrier(
-        (ffn_return, attn_sum, late, input_grad)
-    )
-    ffn_returned = chip_exchange(ffn_return)
-    ffn_returned = ffn_returned + [core_swap(value) for value in ffn_returned]
     late = late + core_swap(late.astype(bf16)).astype(f32)
     late_low = late.astype(bf16)
     for offset in range(1, chips):
         late = late + chip_shift(late_low, offset).astype(f32)
+    ffn_sums, attn_sum, late, input_grad = lax.optimization_barrier(
+        (ffn_sums, attn_sum, late, input_grad)
+    )
+    ffn_sums = ffn_sums + [core_swap(value) for value in ffn_sums]
+    ffn_return = [gather_tiles(ffn_sums, ffn_back[i]) for i in range(chips)]
+    ffn_return, attn_sum = lax.optimization_barrier((ffn_return, attn_sum))
+    ffn_returned = chip_exchange(ffn_return)
+    ffn_returned = ffn_returned + [core_swap(value) for value in ffn_returned]
     late_rows = late_full.shape[0] // seq_size
     late_tiles = late[:late_rows].reshape(-1, 1, tile, tile)
     gain_grad_mine = late[late_rows:].reshape(-1)
@@ -1027,22 +1026,28 @@
     attn_returned = attn_returned + [core_swap(value) for value in attn_returned]
     slot_grad = jnp.where(my_slots[0] >= 0, my_slots[1], 2 * half + my_slots[2])
 
-    def slow_return(_, kept):
+    def slow_return():
         own_ffn = split_tiles(both_grad_w, tile), split_tiles(down_grad_w, tile)
         own_attn = split_tiles(first_grad_w, tile), split_tiles(out_grad_w, tile)
         parts = jnp.concatenate(own_ffn + own_attn + (jnp.zeros((1, tile, tile), bf16),))
         index = jnp.where(
             ffn_to == my_fsdp,
-            is_down * both_count + ffn_place,
+            ffn_place,
             jnp.where(attn_to == my_seq, ffn_count + attn_place, ffn_count + attn_count),
         )
         spread = gather_tiles([parts], index.reshape(-1))
-        return lax.psum_scatter(spread, ("seq", "fsdp"), scatter_dimension=0, tiled=True)
+        spread = lax.all_to_all(
+            spread.reshape((seq_size * fsdp_size, mine, tile, tile)),
+            ("seq", "fsdp"),
+            split_axis=0,
+            concat_axis=0,
+            tiled=True,
+        )
+        return jnp.sum(spread.astype(f32), axis=0).astype(bf16)
 
     tile_grads = ffn_returned + attn_returned
     slow_start = 2 * half + 2 * seq_size * attn_room
-    slow_steps = jnp.where(fits, 0, 1)
-    slow_grads = lax.fori_loop(0, slow_steps, slow_return, jnp.zeros((mine, tile, tile), bf16))
+    slow_grads = lax.cond(fits, lambda: jnp.zeros((mine, tile, tile), bf16), slow_return)
     tile_grads = tile_grads + [slow_grads]
     slot_grad = jnp.where(fits, slot_grad, slow_start + local_slots)
 

time: 1300 us -> 1210 us (0.931)
  waiting for transfers between devices: 636 us -> 504 us
  starting transfers between devices: 64.6 us -> 178 us
  local copies, waits for them, and re-layouts: 158 us -> 120 us
  other arithmetic: 134 us -> 98 us
  between operations: 18.9 us -> 41.3 us
  Pallas kernels: 175 us -> 155 us
    ppermute x24, starting transfers between devices: 17.1 us -> 129 us  [core_swap(): return lax.ppermute(value, 'fsdp', [(i, i ^ 1) for i in range(size)])]
    ppermute x21, waiting for transfers between devices: 331 us -> 241 us  [chip_shift(): lax.ppermute(value, 'fsdp', [(i, (i // 2 + offset) % chips * 2 + i % 2) f...]
    all_gather x2, waiting for transfers between devices: 28 us -> 0.02 us  [on_device(): lax.all_gather(value, 'seq', axis=0, tiled=True)]
    gather x41 -> x0, local copies, waits for them, and re-layouts: 26.9 us -> none
    pallas_call x26 -> x22, Pallas kernels: 127 us -> 105 us  [tile_kernel_call(): pl.pallas_call(kernel, grid=(steps,), cost_estimate=pl.CostEstimate(flops...]
    ppermute x27 -> x23, waiting for transfers between devices: 175 us -> 155 us  [seq_swap(): return lax.ppermute(value, 'seq', [(i, i ^ flip) for i in range(size)])]
    all_gather x1, waiting for transfers between devices: 48.2 us -> 33.5 us  [on_device(): feed_low = lax.all_gather(feed_own, 'fsdp', axis=0, tiled=True)]
    unnamed x421 -> x417, local copies, waits for them, and re-layouts: 52.8 us -> 59.1 us
  transfers between devices with their start and end apart: 79 -> 76, of which waited for: 43 -> 38; matrix products, arithmetic and copies ran while one was open for 20% -> 15% of each run, Pallas kernels for 4% -> 6%
where the time goes in v8:
time: 1210 us; the launch traced here: 1200 us
  waiting for transfers between devices  504 us (42%)
  starting transfers between devices  178 us (15%)
  Pallas kernels  155 us (13%)
  local copies, waits for them, and re-layouts  120 us (10%)
  matrix products  101 us (8%)
  other arithmetic  98 us (8%)
  between operations  41.3 us (3%)
    ppermute x21, waiting for transfers between devices, chip_shift(): lax.ppermute(value, 'fsdp', [(i, (i // 2 + offset) % chips * 2 + i % 2) f...  241 us
    ppermute x23, waiting for transfers between devices, seq_swap(): return lax.ppermute(value, 'seq', [(i, i ^ flip) for i in range(size)])  155 us
    ppermute x24, starting transfers between devices, core_swap(): return lax.ppermute(value, 'fsdp', [(i, i ^ 1) for i in range(size)])  129 us
    pallas_call x22, Pallas kernels, tile_kernel_call(): pl.pallas_call(kernel, grid=(steps,), cost_estimate=pl.CostEstimate(flops...  105 us
    unnamed x417, local copies, waits for them, and re-layouts  59.1 us
    pallas_call x2, Pallas kernels, rotate_update(): pl.pallas_call(kernel, grid=(count // each,), out_shape=(shape, shape, sh...  49.6 us
    reduce_scatter x1, waiting for transfers between devices, on_device(): lax.psum_scatter(matmul_flip(hidden_low, w_down).astype(bf16), 'fsdp', sc...  48.4 us
    dot_general x8, matrix products, matmul_flip(): lax.dot_general(left, right, (((1,), (1,)), ((), ())), preferred_element_...  34.7 us
  transfers between devices with their start and end apart: 76, of which 38 were waited for; matrix products, arithmetic and copies ran while one was open for 15% of the time, Pallas kernels for 6%

profile of v8, /device:TPU:9, one launch (start us, length us, event | category | flops | bytes accessed | tf_op | source)
XLA Modules:
  0.0 1199.7 jit_solution(5236759961207858552)
XLA Ops:
  44.4 9.2 convert_reduce_fusion
  77.2 67.8 %collective-permute-done.1.refs_1_ = bf16[37,128,128]{2,1,0:T(8,128)(2,1)S(1)} collective-permute-done((bf16[37,128,128]{2,1,0:T(8,128)(2,1)}, bf16[37,128,128]{2,1,0:T(8,128)(2,1)S(1)}, u32[]{:S(2)}, u32[]{:S(2)}) %collective-permute-start.1) | collective-permute-done | bytes 1212448 | tf_op jit(solution)/shard_map/ppermute | solution.py:370
  217.7 12.2 %collective-permute-done.13 = bf16[33,128,128]{2,1,0:T(8,128)(2,1)} collective-permute-done((bf16[33,128,128]{2,1,0:T(8,128)(2,1)S(1)}, bf16[33,128,128]{2,1,0:T(8,128)(2,1)}, u32[]{:S(2)}, u32[]{:S(2)}) %collective-permute-start.13) | collective-permute-done | bytes 1081376 | tf_op jit(solution)/shard_map/ppermute | solution.py:370
  229.9 49.3 %collective-permute-start.17 = (bf16[33,128,128]{2,1,0:T(8,128)(2,1)}, bf16[33,128,128]{2,1,0:T(8,128)(2,1)S(1)}, u32[]{:S(2)}, u32[]{:S(2)}) collective-permute-start(bf16[33,128,128]{2,1,0:T(8,128)(2,1)} %collective-permute-done.13), channel_id=1, source_target_pairs={{0,1},{1,0},{2,3},{3,2},{4,5},{5,4},{6,7},{7,6},{8,9},{9,8},{10,11... | collective-permute-start | bytes 3244040 | tf_op jit(solution)/shard_map/ppermute | solution.py:364
  279.2 19.7 %collective-permute-done.11 = bf16[33,128,128]{2,1,0:T(8,128)(2,1)} collective-permute-done((bf16[33,128,128]{2,1,0:T(8,128)(2,1)S(1)}, bf16[33,128,128]{2,1,0:T(8,128)(2,1)}, u32[]{:S(2)}, u32[]{:S(2)}) %collective-permute-start.11) | collective-permute-done | bytes 1081376 | tf_op jit(solution)/shard_map/ppermute | solution.py:370
  307.3 10.7 conditional.3
  307.4 10.4 branch_1_fun.2
  328.1 8.8 collective-permute-done.18
  359.2 13.5 %collective-permute-done.19 = bf16[128,2048]{1,0:T(8,128)(2,1)S(1)} collective-permute-done((bf16[128,2048]{1,0:T(8,128)(2,1)}, bf16[128,2048]{1,0:T(8,128)(2,1)S(1)}, u32[]{:S(2)}, u32[]{:S(2)}) %collective-permute-start.19) | collective-permute-done | bytes 524320 | tf_op jit(solution)/shard_map/ppermute | solution.py:353
  372.7 23.3 %collective-permute-done.21 = bf16[128,2048]{1,0:T(8,128)(2,1)} collective-permute-done((bf16[128,2048]{1,0:T(8,128)(2,1)}, bf16[128,2048]{1,0:T(8,128)(2,1)}, u32[]{:S(2)}, u32[]{:S(2)}) %collective-permute-start.21) | collective-permute-done | bytes 524320 | tf_op jit(solution)/shard_map/ppermute | solution.py:353
  402.8 14.2 %conditional.4 = ((bf16[2048,2048]{1,0:T(8,128)(2,1)}, bf16[2048,1024]{1,0:T(8,128)(2,1)})) conditional(s32[]{:T(128)} %convert_element_type.370, (s32[]{:T(128)}, s32[4,8,116]{2,1,0:T(8,128)S(1)}, s32[4,8,116]{2,1,0:T(8,128)S(1)}, bf16[116,128,128]{2,1,0:T(8,128)(2,1)}) %tuple.236, (s32[384]{0:T(512)S(1)}, bf16[264,128,128]{2,1,0:T(8,128)(2,1)}, ...), branch_computations={%region_26.28_spmd, %region_28.29_spmd} | conditional | flops 5705344 | bytes 515585056 | solution.py:795
  403.0 13.9 %branch_1_fun.3 = (bf16[2048,2048]{1,0:T(8,128)(2,1)}, bf16[2048,1024]{1,0:T(8,128)(2,1)}) custom-call(s32[384]{0:T(512)S(1)} %broadcast_clamp_fusion.3.index_ref, bf16[264,128,128]{2,1,0:T(8,128)(2,1)} %get-tuple-element.81.refs_0_, bf16[264,128,128]{2,1,0:T(8,128)(2,1)} %get-tuple-element.82.refs_1_), custom_call_target="tpu_custom_call" | custom-call | bytes 25165824 | tf_op jit(solution)/shard_map/cond/branch_1_fun/pallas_call | solution.py:126
  417.0 33.5 %all-gather.7.cloned.1.call-done = bf16[1024,2048]{1,0:T(8,128)(2,1)} async-done(((bf16[128,2048]{1,0:T(8,128)(2,1)}), bf16[1024,2048]{1,0:T(8,128)(2,1)}) %all-gather.7.cloned.1.call-update) | async-done | bytes 4194320 | tf_op jit(solution)/shard_map/all_gather | solution.py:860
  450.5 12.5 %fusion.276 = f32[1024,2048]{1,0:T(8,128)S(1)} fusion(bf16[1024,2048]{1,0:T(8,128)(2,1)} %all-gather.7.cloned.1.call-done, bf16[2048,2048]{1,0:T(8,128)(2,1)} %get-tuple-element.225), kind=kOutput, calls=%fused_computation.728 | convolution fusion | flops 8589934592 | bytes 20971520 | tf_op jit(solution)/shard_map/dot_general | solution.py:61
  474.7 48.4 %reduce-scatter.5.cloned.1.call-done = bf16[128,2048]{1,0:T(8,128)(2,1)} async-done(((bf16[1024,2048]{1,0:T(8,128)(2,1)}), bf16[128,2048]{1,0:T(8,128)(2,1)}) %reduce-scatter.5.cloned.1.call-update) | async-done | bytes 524304 | tf_op jit(solution)/shard_map/reduce_scatter | solution.py:869
  592.8 12.1 %fusion.13 = (bf16[1024,1024]{1,0:T(8,128)(2,1)S(1)}, bf16[1024,1024]{1,0:T(8,128)(2,1)S(1)}) fusion(f32[1024,2048]{1,0:T(8,128)} %copy-done.47, bf16[1024,2048]{1,0:T(8,128)(2,1)} %all-gather.11.cloned.1.call-done, bf16[2048,1024]{1,0:T(8,128)(2,1)} %get-tuple-element.226), kind=kOutput, calls=%fused_computation.39 | convolution fusion | flops 4320133120 | bytes 20971520 | tf_op jit(solution)/shard_map/dot_general | solution.py:61
  607.3 12.6 %convolution_convert_fusion.1 = bf16[1024,2048]{1,0:T(8,128)(2,1)} fusion(bf16[1024,2048]{1,0:T(8,128)(2,1)S(1)} %pad_maximum_fusion, bf16[2048,2048]{1,0:T(8,128)(2,1)} %get-tuple-element.225), kind=kOutput, calls=%fused_computation.47 | convolution fusion | flops 8592031744 | bytes 16777216 | tf_op jit(solution)/shard_map/dot_general | solution.py:65
  630.8 9.7 convolution_convert_fusion.refs_0_
  643.8 10.2 shard_map.266
  657.5 10.0 shard_map.265
  684.0 21.5 %collective-permute-done.36 = bf16[128,2048]{1,0:T(8,128)(2,1)S(1)} collective-permute-done((bf16[128,2048]{1,0:T(8,128)(2,1)S(1)}, bf16[128,2048]{1,0:T(8,128)(2,1)S(1)}, u32[]{:S(2)}, u32[]{:S(2)}) %collective-permute-start.36) | collective-permute-done | bytes 524320 | tf_op jit(solution)/shard_map/ppermute | solution.py:353
  705.4 11.6 collective-permute-done.35
  717.0 10.0 collective-permute-done.34
  741.6 10.8 collective-permute-done.37
  775.1 13.0 %reduce-scatter.9.cloned.1.call-done.refs_0_ = bf16[66,128,128]{2,1,0:T(8,128)(2,1)} async-done(((bf16[264,128,128]{2,1,0:T(8,128)(2,1)}), bf16[66,128,128]{2,1,0:T(8,128)(2,1)}) %reduce-scatter.9.cloned.1.call-update) | async-done | bytes 2162704 | tf_op jit(solution)/shard_map/reduce_scatter | solution.py:910
  819.9 16.8 %collective-permute-done.42 = bf16[128,2048]{1,0:T(8,128)(2,1)S(1)} collective-permute-done((bf16[128,2048]{1,0:T(8,128)(2,1)}, bf16[128,2048]{1,0:T(8,128)(2,1)S(1)}, u32[]{:S(2)}, u32[]{:S(2)}) %collective-permute-start.42) | collective-permute-done | bytes 524320 | tf_op jit(solution)/shard_map/ppermute | solution.py:353
  836.7 23.3 %collective-permute-done.44 = bf16[128,2048]{1,0:T(8,128)(2,1)} collective-permute-done((bf16[128,2048]{1,0:T(8,128)(2,1)}, bf16[128,2048]{1,0:T(8,128)(2,1)}, u32[]{:S(2)}, u32[]{:S(2)}) %collective-permute-start.44) | collective-permute-done | bytes 524320 | tf_op jit(solution)/shard_map/ppermute | solution.py:353
  886.3 100.3 %collective-permute-done.51 = bf16[537,128]{1,0:T(8,128)(2,1)S(1)} collective-permute-done((bf16[537,128]{1,0:T(8,128)(2,1)S(1)}, bf16[537,128]{1,0:T(8,128)(2,1)S(1)}, u32[]{:S(2)}, u32[]{:S(2)}) %collective-permute-start.51) | collective-permute-done | bytes 137504 | tf_op jit(solution)/shard_map/ppermute | solution.py:370
  1033.1 9.9 collective-permute-start.64
  1045.6 51.5 %collective-permute-start.58 = (bf16[37,128,128]{2,1,0:T(8,128)(2,1)}, bf16[37,128,128]{2,1,0:T(8,128)(2,1)}, u32[]{:S(2)}, u32[]{:S(2)}) collective-permute-start(bf16[37,128,128]{2,1,0:T(8,128)(2,1)} %collective-permute-done.54.refs_1_), channel_id=1, source_target_pairs={{0,1},{1,0},{2,3},{3,2},{4,5},{5,4},{6,7},{7,6},{8,9},{9,8},{10,11... | collective-permute-start | bytes 3637256 | tf_op jit(solution)/shard_map/ppermute | solution.py:364
  1097.1 21.2 %collective-permute-done.55.refs_2_ = bf16[37,128,128]{2,1,0:T(8,128)(2,1)} collective-permute-done((bf16[37,128,128]{2,1,0:T(8,128)(2,1)S(1)}, bf16[37,128,128]{2,1,0:T(8,128)(2,1)}, u32[]{:S(2)}, u32[]{:S(2)}) %collective-permute-start.55) | collective-permute-done | bytes 1212448 | tf_op jit(solution)/shard_map/ppermute | solution.py:370
  1150.1 42.5 %shard_map.277 = (f32[116,128,128]{2,1,0:T(8,128)}, f32[116,128,128]{2,1,0:T(8,128)}, f32[116,128,128]{2,1,0:T(8,128)}) custom-call(s32[116]{0:T(128)S(1)} %fusion.216.index_ref, bf16[37,128,128]{2,1,0:T(8,128)(2,1)} %shard_map.269.refs_0_, bf16[37,128,128]{2,1,0:T(8,128)(2,1)} %collective-permute-done.54.refs_1_, ...), custom_call_target="tpu_custom_call" | custom-call | tf_op jit(solution)/shard_map/pallas_call | solution.py:335
  (885 shorter events, 451.1 us)
Async XLA Ops:
  7.2 300.1 %all-gather.5.cloned.1.call-start = ((), (), s32[]{:S(2)}) async-start(), calls=%async_computation.7 | async-start | bytes 10813440 | tf_op jit(solution)/shard_map/all_gather | solution.py:767
  64.4 80.6 %collective-permute-start.1 = (bf16[37,128,128]{2,1,0:T(8,128)(2,1)}, bf16[37,128,128]{2,1,0:T(8,128)(2,1)S(1)}, u32[]{:S(2)}, u32[]{:S(2)}) collective-permute-start(bf16[37,128,128]{2,1,0:T(8,128)(2,1)} %copy-done.16), channel_id=1, source_target_pairs={{0,2},{1,3},{2,4},{3,5},{4,6},{5,7},{6,0},{7,1},{8,10},{9,11},{10,... | collective-permute-start | bytes 3637256 | tf_op jit(solution)/shard_map/ppermute | solution.py:370
  66.1 99.8 %collective-permute-start.2 = (bf16[37,128,128]{2,1,0:T(8,128)(2,1)}, bf16[37,128,128]{2,1,0:T(8,128)(2,1)}, u32[]{:S(2)}, u32[]{:S(2)}) collective-permute-start(bf16[37,128,128]{2,1,0:T(8,128)(2,1)} %copy-done.15), channel_id=1, source_target_pairs={{0,4},{1,5},{2,6},{3,7},{4,0},{5,1},{6,2},{7,3},{8,12},{9,13},{10,... | collective-permute-start | bytes 3637256 | tf_op jit(solution)/shard_map/ppermute | solution.py:370
  70.6 96.4 %collective-permute-start.6 = (bf16[40,128,128]{2,1,0:T(8,128)(2,1)}, bf16[40,128,128]{2,1,0:T(8,128)(2,1)}, u32[]{:S(2)}, u32[]{:S(2)}) collective-permute-start(bf16[40,128,128]{2,1,0:T(8,128)(2,1)} %get-tuple-element.417), channel_id=1, source_target_pairs={{0,24},{8,16},{16,8},{24,0},{1,25},{9,17},{17,9},{25,1},{2,26},{10... | collective-permute-start | bytes 3932168 | tf_op jit(solution)/shard_map/ppermute | solution.py:353
  72.8 94.2 %collective-permute-start.5 = (bf16[40,128,128]{2,1,0:T(8,128)(2,1)}, bf16[40,128,128]{2,1,0:T(8,128)(2,1)}, u32[]{:S(2)}, u32[]{:S(2)}) collective-permute-start(bf16[40,128,128]{2,1,0:T(8,128)(2,1)} %get-tuple-element.418), channel_id=1, source_target_pairs={{0,16},{8,24},{16,0},{24,8},{1,17},{9,25},{17,1},{25,9},{2,18},{10... | collective-permute-start | bytes 3932168 | tf_op jit(solution)/shard_map/ppermute | solution.py:353
  72.9 94.2 %collective-permute-start.4 = (bf16[40,128,128]{2,1,0:T(8,128)(2,1)}, bf16[40,128,128]{2,1,0:T(8,128)(2,1)}, u32[]{:S(2)}, u32[]{:S(2)}) collective-permute-start(bf16[40,128,128]{2,1,0:T(8,128)(2,1)} %get-tuple-element.419), channel_id=1, source_target_pairs={{0,8},{8,0},{16,24},{24,16},{1,9},{9,1},{17,25},{25,17},{2,10},{10... | collective-permute-start | bytes 3932168 | tf_op jit(solution)/shard_map/ppermute | solution.py:353
  187.4 215.4 %all-gather.9.cloned.1.call-start = ((), (), s32[]{:S(2)}) async-start(), calls=%async_computation.9 | async-start | bytes 10813440 | tf_op jit(solution)/shard_map/all_gather | solution.py:767
  188.1 262.4 %all-gather.7.cloned.1.call-start = ((), (), s32[]{:S(2)}) async-start(), calls=%async_computation.8 | async-start | bytes 4718592 | tf_op jit(solution)/shard_map/all_gather | solution.py:860
  205.2 74.0 %collective-permute-start.12 = (bf16[33,128,128]{2,1,0:T(8,128)(2,1)S(1)}, bf16[33,128,128]{2,1,0:T(8,128)(2,1)}, u32[]{:S(2)}, u32[]{:S(2)}) collective-permute-start(bf16[33,128,128]{2,1,0:T(8,128)(2,1)S(1)} %copy-done.63), channel_id=1, source_target_pairs={{0,4},{1,5},{2,6},{3,7},{4,0},{5,1},{6,2},{7,3},{8,12},{9,13},{10,... | collective-permute-start | bytes 3244040 | tf_op jit(solution)/shard_map/ppermute | solution.py:370
  206.8 92.2 %collective-permute-start.11 = (bf16[33,128,128]{2,1,0:T(8,128)(2,1)S(1)}, bf16[33,128,128]{2,1,0:T(8,128)(2,1)}, u32[]{:S(2)}, u32[]{:S(2)}) collective-permute-start(bf16[33,128,128]{2,1,0:T(8,128)(2,1)S(1)} %copy-done.63), channel_id=1, source_target_pairs={{0,2},{1,3},{2,4},{3,5},{4,6},{5,7},{6,0},{7,1},{8,10},{9,11},{10,... | collective-permute-start | bytes 3244040 | tf_op jit(solution)/shard_map/ppermute | solution.py:370
  216.0 88.3 %collective-permute-start.14 = (bf16[33,128,128]{2,1,0:T(8,128)(2,1)S(1)}, bf16[33,128,128]{2,1,0:T(8,128)(2,1)S(1)}, u32[]{:S(2)}, u32[]{:S(2)}) collective-permute-start(bf16[33,128,128]{2,1,0:T(8,128)(2,1)S(1)} %copy-done.63), channel_id=1, source_target_pairs={{0,1},{1,0},{2,3},{3,2},{4,5},{5,4},{6,7},{7,6},{8,9},{9,8},{10,11... | collective-permute-start | bytes 3244040 | tf_op jit(solution)/shard_map/ppermute | solution.py:364
  229.9 75.4 %collective-permute-start.17 = (bf16[33,128,128]{2,1,0:T(8,128)(2,1)}, bf16[33,128,128]{2,1,0:T(8,128)(2,1)S(1)}, u32[]{:S(2)}, u32[]{:S(2)}) collective-permute-start(bf16[33,128,128]{2,1,0:T(8,128)(2,1)} %collective-permute-done.13), channel_id=1, source_target_pairs={{0,1},{1,0},{2,3},{3,2},{4,5},{5,4},{6,7},{7,6},{8,9},{9,8},{10,11... | collective-permute-start | bytes 3244040 | tf_op jit(solution)/shard_map/ppermute | solution.py:364
  302.1 48.2 %collective-permute-start.22 = (bf16[4,10,128,128]{3,2,1,0:T(8,128)(2,1)}, bf16[4,10,128,128]{3,2,1,0:T(8,128)(2,1)}, u32[]{:S(2)}, u32[]{:S(2)}) collective-permute-start(bf16[4,10,128,128]{3,2,1,0:T(8,128)(2,1)} %get-tuple-element.401), channel_id=1, source_target_pairs={{0,1},{1,0},{2,3},{3,2},{4,5},{5,4},{6,7},{7,6},{8,9},{9,8},{10,11... | collective-permute-start | bytes 3932168 | tf_op jit(solution)/shard_map/ppermute | solution.py:364
  349.1 46.9 %collective-permute-start.21 = (bf16[128,2048]{1,0:T(8,128)(2,1)}, bf16[128,2048]{1,0:T(8,128)(2,1)}, u32[]{:S(2)}, u32[]{:S(2)}) collective-permute-start(bf16[128,2048]{1,0:T(8,128)(2,1)} %get-tuple-element.390), channel_id=1, source_target_pairs={{0,24},{8,16},{16,8},{24,0},{1,25},{9,17},{17,9},{25,1},{2,26},{10... | collective-permute-start | bytes 1572872 | tf_op jit(solution)/shard_map/ppermute | solution.py:353
  350.1 45.9 %collective-permute-start.20 = (bf16[128,2048]{1,0:T(8,128)(2,1)}, bf16[128,2048]{1,0:T(8,128)(2,1)}, u32[]{:S(2)}, u32[]{:S(2)}) collective-permute-start(bf16[128,2048]{1,0:T(8,128)(2,1)} %get-tuple-element.391), channel_id=1, source_target_pairs={{0,16},{8,24},{16,0},{24,8},{1,17},{9,25},{17,1},{25,9},{2,18},{10... | collective-permute-start | bytes 1572872 | tf_op jit(solution)/shard_map/ppermute | solution.py:353
  402.7 120.4 %reduce-scatter.5.cloned.1.call-start = ((), (), s32[]{:S(2)}) async-start(), calls=%async_computation.10 | async-start | bytes 4718592 | tf_op jit(solution)/shard_map/reduce_scatter | solution.py:869
  474.7 118.1 %all-gather.11.cloned.1.call-start = ((), (), s32[]{:S(2)}) async-start(), calls=%async_computation.11 | async-start | bytes 4718592 | tf_op jit(solution)/shard_map/all_gather | solution.py:890
  531.9 139.0 %reduce-scatter.7.cloned.1.call-start = ((), (), s32[]{:S(2)}) async-start(), calls=%async_computation.12 | async-start | bytes 4718592 | tf_op jit(solution)/shard_map/reduce_scatter | solution.py:899
  619.9 168.2 %reduce-scatter.9.cloned.1.call-start = ((), (), s32[]{:S(2)}) async-start(), calls=%async_computation.13 | async-start | bytes 10813440 | tf_op jit(solution)/shard_map/reduce_scatter | solution.py:910
  673.1 319.8 %reduce-scatter.11.cloned.1.call-start = ((), (), s32[]{:S(2)}) async-start(), calls=%async_computation.14 | async-start | bytes 10813440 | tf_op jit(solution)/shard_map/reduce_scatter | solution.py:910
  812.6 47.4 %collective-permute-start.44 = (bf16[128,2048]{1,0:T(8,128)(2,1)}, bf16[128,2048]{1,0:T(8,128)(2,1)}, u32[]{:S(2)}, u32[]{:S(2)}) collective-permute-start(bf16[128,2048]{1,0:T(8,128)(2,1)} %get-tuple-element.384), channel_id=1, source_target_pairs={{0,24},{8,16},{16,8},{24,0},{1,25},{9,17},{17,9},{25,1},{2,26},{10... | collective-permute-start | bytes 1572872 | tf_op jit(solution)/shard_map/ppermute | solution.py:353
  813.8 46.2 %collective-permute-start.43 = (bf16[128,2048]{1,0:T(8,128)(2,1)}, bf16[128,2048]{1,0:T(8,128)(2,1)}, u32[]{:S(2)}, u32[]{:S(2)}) collective-permute-start(bf16[128,2048]{1,0:T(8,128)(2,1)} %get-tuple-element.385), channel_id=1, source_target_pairs={{0,16},{8,24},{16,0},{24,8},{1,17},{9,25},{17,1},{25,9},{2,18},{10... | collective-permute-start | bytes 1572872 | tf_op jit(solution)/shard_map/ppermute | solution.py:353
  881.1 111.1 %collective-permute-start.39 = (bf16[33,128,128]{2,1,0:T(8,128)(2,1)}, bf16[33,128,128]{2,1,0:T(8,128)(2,1)S(1)}, u32[]{:S(2)}, u32[]{:S(2)}) collective-permute-start(bf16[33,128,128]{2,1,0:T(8,128)(2,1)} %get-tuple-element.235), channel_id=1, source_target_pairs={{0,2},{1,3},{2,4},{3,5},{4,6},{5,7},{6,0},{7,1},{8,10},{9,11},{10,... | collective-permute-start | bytes 3244040 | tf_op jit(solution)/shard_map/ppermute | solution.py:370
  882.3 109.9 %collective-permute-start.40 = (bf16[33,128,128]{2,1,0:T(8,128)(2,1)}, bf16[33,128,128]{2,1,0:T(8,128)(2,1)S(1)}, u32[]{:S(2)}, u32[]{:S(2)}) collective-permute-start(bf16[33,128,128]{2,1,0:T(8,128)(2,1)} %get-tuple-element.236), channel_id=1, source_target_pairs={{0,4},{1,5},{2,6},{3,7},{4,0},{5,1},{6,2},{7,3},{8,12},{9,13},{10,... | collective-permute-start | bytes 3244040 | tf_op jit(solution)/shard_map/ppermute | solution.py:370
  883.5 108.7 %collective-permute-start.41 = (bf16[33,128,128]{2,1,0:T(8,128)(2,1)}, bf16[33,128,128]{2,1,0:T(8,128)(2,1)S(1)}, u32[]{:S(2)}, u32[]{:S(2)}) collective-permute-start(bf16[33,128,128]{2,1,0:T(8,128)(2,1)} %get-tuple-element.237), channel_id=1, source_target_pairs={{0,6},{1,7},{2,0},{3,1},{4,2},{5,3},{6,4},{7,5},{8,14},{9,15},{10,... | collective-permute-start | bytes 3244040 | tf_op jit(solution)/shard_map/ppermute | solution.py:370
  884.8 101.8 %collective-permute-start.51 = (bf16[537,128]{1,0:T(8,128)(2,1)S(1)}, bf16[537,128]{1,0:T(8,128)(2,1)S(1)}, u32[]{:S(2)}, u32[]{:S(2)}) collective-permute-start(bf16[537,128]{1,0:T(8,128)(2,1)S(1)} %fusion.102), channel_id=1, source_target_pairs={{0,6},{1,7},{2,0},{3,1},{4,2},{5,3},{6,4},{7,5},{8,14},{9,15},{10,... | collective-permute-start | bytes 412424 | tf_op jit(solution)/shard_map/ppermute | solution.py:370
  886.0 102.0 %collective-permute-start.50 = (bf16[537,128]{1,0:T(8,128)(2,1)S(1)}, bf16[537,128]{1,0:T(8,128)(2,1)S(1)}, u32[]{:S(2)}, u32[]{:S(2)}) collective-permute-start(bf16[537,128]{1,0:T(8,128)(2,1)S(1)} %fusion.102), channel_id=1, source_target_pairs={{0,4},{1,5},{2,6},{3,7},{4,0},{5,1},{6,2},{7,3},{8,12},{9,13},{10,... | collective-permute-start | bytes 412424 | tf_op jit(solution)/shard_map/ppermute | solution.py:370
  1016.1 102.2 %collective-permute-start.55 = (bf16[37,128,128]{2,1,0:T(8,128)(2,1)S(1)}, bf16[37,128,128]{2,1,0:T(8,128)(2,1)}, u32[]{:S(2)}, u32[]{:S(2)}) collective-permute-start(bf16[37,128,128]{2,1,0:T(8,128)(2,1)S(1)} %shard_map.271), channel_id=1, source_target_pairs={{0,4},{1,5},{2,6},{3,7},{4,0},{5,1},{6,2},{7,3},{8,12},{9,13},{10,... | collective-permute-start | bytes 3637256 | tf_op jit(solution)/shard_map/ppermute | solution.py:370
  1017.4 105.2 %collective-permute-start.56 = (bf16[37,128,128]{2,1,0:T(8,128)(2,1)S(1)}, bf16[37,128,128]{2,1,0:T(8,128)(2,1)}, u32[]{:S(2)}, u32[]{:S(2)}) collective-permute-start(bf16[37,128,128]{2,1,0:T(8,128)(2,1)S(1)} %shard_map.272), channel_id=1, source_target_pairs={{0,6},{1,7},{2,0},{3,1},{4,2},{5,3},{6,4},{7,5},{8,14},{9,15},{10,... | collective-permute-start | bytes 3637256 | tf_op jit(solution)/shard_map/ppermute | solution.py:370
  1043.8 79.3 %collective-permute-start.65 = (bf16[13,128,128]{2,1,0:T(8,128)(2,1)S(1)}, bf16[13,128,128]{2,1,0:T(8,128)(2,1)S(1)}, u32[]{:S(2)}, u32[]{:S(2)}) collective-permute-start(bf16[13,128,128]{2,1,0:T(8,128)(2,1)S(1)} %collective-permute-done.61.refs_9_), channel_id=1, source_target_pairs={{0,1},{1,0},{2,3},{3,2},{4,5},{5,4},{6,7},{7,6},{8,9},{9,8},{10,11... | collective-permute-start | bytes 1277960 | tf_op jit(solution)/shard_map/ppermute | solution.py:364
  1045.3 100.7 %collective-permute-start.57 = (bf16[37,128,128]{2,1,0:T(8,128)(2,1)}, bf16[37,128,128]{2,1,0:T(8,128)(2,1)}, u32[]{:S(2)}, u32[]{:S(2)}) collective-permute-start(bf16[37,128,128]{2,1,0:T(8,128)(2,1)} %shard_map.269.refs_0_), channel_id=1, source_target_pairs={{0,1},{1,0},{2,3},{3,2},{4,5},{5,4},{6,7},{7,6},{8,9},{9,8},{10,11... | collective-permute-start | bytes 3637256 | tf_op jit(solution)/shard_map/ppermute | solution.py:364
  1045.6 100.3 %collective-permute-start.58 = (bf16[37,128,128]{2,1,0:T(8,128)(2,1)}, bf16[37,128,128]{2,1,0:T(8,128)(2,1)}, u32[]{:S(2)}, u32[]{:S(2)}) collective-permute-start(bf16[37,128,128]{2,1,0:T(8,128)(2,1)} %collective-permute-done.54.refs_1_), channel_id=1, source_target_pairs={{0,1},{1,0},{2,3},{3,2},{4,5},{5,4},{6,7},{7,6},{8,9},{9,8},{10,11... | collective-permute-start | bytes 3637256 | tf_op jit(solution)/shard_map/ppermute | solution.py:364
  (245 other events, 3390.1 us)
Sparse Core Ops, SparseCore 0:
  187.5 89.8 all-gather.4
  279.2 122.3 all-gather.8
  403.8 46.6 all-gather.6
  474.8 48.2 reduce-scatter.4
  532.0 52.7 all-gather.10
  620.0 46.9 reduce-scatter.6
  673.2 114.7 reduce-scatter.8
  791.2 111.5 reduce-scatter.10

commit v9 on v8

--- a/solution.py
+++ b/solution.py
@@ -110,6 +110,31 @@
     return jnp.sum(same.astype(jnp.int32), axis=-1)
 
 
+def count_long(keys):
+    groups, size = keys.shape
+
+    def kernel(row_ref, column_ref, out_ref):
+        row = row_ref[0]
+        column = column_ref[0]
+        here = lax.broadcasted_iota(jnp.int32, (size, size), 1)
+        other = lax.broadcasted_iota(jnp.int32, (size, size), 0)
+        earlier = (column == row) & (other < here)
+        out_ref[0] = jnp.sum(earlier.astype(jnp.int32), axis=0, keepdims=True)
+
+    return pl.pallas_call(
+        kernel,
+        grid=(groups,),
+        out_shape=jax.ShapeDtypeStruct((groups, 1, size), jnp.int32),
+        in_specs=[
+            pl.BlockSpec((1, 1, size), lambda i: (i, 0, 0)),
+            pl.BlockSpec((1, size, 1), lambda i: (i, 0, 0)),
+        ],
+        out_specs=pl.BlockSpec((1, 1, size), lambda i: (i, 0, 0)),
+        cost_estimate=pl.CostEstimate(flops=0, transcendentals=0, bytes_accessed=0),
+        compiler_params=pltpu.CompilerParams(vmem_limit_bytes=VMEM_BYTES),
+    )(keys[:, None, :], keys[:, :, None]).reshape(groups, size)
+
+
 def pick(match, value):
     return jnp.sum(jnp.where(match, value, 0), axis=-1)
 
@@ -136,16 +161,20 @@
     )(index, *arrays)
 
 
-def start_copy(sources, place, target, sem):
-    start = 0
-    for ref in sources:
-        size = ref.shape[0]
-
-        @pl.when((place >= start) & (place < start + size))
-        def _(ref=ref, start=start):
-            pltpu.make_async_copy(ref.at[place - start], target, sem).start()
-
-        start = start + size
+def start_copy(sources, place, target, sem, start=0):
+    if len(sources) == 1:
+        pltpu.make_async_copy(sources[0].at[place - start], target, sem).start()
+        return
+    half = len(sources) // 2
+    middle = start + sum(ref.shape[0] for ref in sources[:half])
+
+    @pl.when(place < middle)
+    def _():
+        start_copy(sources[:half], place, target, sem, start)
+
+    @pl.when(place >= middle)
+    def _():
+        start_copy(sources[half:], place, target, sem, middle)
 
 
 def gather_tiles(arrays, index):
@@ -503,7 +532,8 @@
     ffn_room = (room(2 * mine, ffn_share / chips) + 1) // 2
     both_count = row_blocks * ffn_first
     ffn_hold = (room(ffn_count, 1.0 / seq_size) + 3) // 4 * 4
-    ffn_half = ffn_hold // 2
+    ffn_half = ffn_hold * 3 // 7 // 4 * 4
+    ffn_rest = ffn_hold - ffn_half
 
     def tile_places(owner):
         row = owner // columns
@@ -591,20 +621,31 @@
 
     ffn_to, ffn_place, attn_to, attn_place = tile_places(owners)
     ffn_chip = jnp.where(ffn_to < 0, -1, ffn_to // 2)
-    seq_view = ffn_to.reshape(seq_size, fsdp_size * mine)
-    ffn_rank = count_earlier(seq_view, seq_view >= 0).reshape(owners.shape)
     attn_view = attn_to.reshape(seq_size, chips, 2 * mine)
     attn_rank = count_earlier(attn_view, attn_view >= 0).reshape(owners.shape)
     attn_core = (attn_rank + slot_seq) % 2
     attn_rank = attn_rank // 2
     attn_key = jnp.where(attn_to < 0, -1, 2 * attn_to + attn_core)
 
+    chip_slots = lax.dynamic_slice(
+        jnp.stack([attn_key, attn_rank]), (0, my_seq, 2 * my_chip, 0), (2, 1, 2, mine)
+    ).reshape(2, 1, 1, 2 * mine)
+    attn_message = attn_room + row_blocks * rows // tile + small_rows + -(-own_gains.shape[0] // tile**2)
+    attn_pack = pick(
+        (chip_slots[0] == (2 * (my_seq ^ flips) + my_core)[:, None, None])
+        & (chip_slots[1] == jnp.arange(attn_room)[None, :, None]),
+        both_slots,
+    )
+    attn_sent = gather_tiles(masters, attn_pack.reshape(-1))
+    attn_sent = attn_sent.reshape(seq_size, attn_room, tile, tile)
+    seq_view = ffn_to.reshape(seq_size, fsdp_size * mine)
+    ffn_rank = count_long(seq_view).reshape(owners.shape)
     def by_chip(value):
         value = value.reshape(seq_size, chips, 2 * mine).transpose(1, 0, 2)
         return value.reshape(chips, seq_size * 2 * mine)
 
     attn_key_chip = by_chip(attn_key)
-    attn_order_chip = count_earlier(attn_key_chip, attn_key_chip >= 0)
+    attn_order_chip = count_long(attn_key_chip)
     attn_order = (
         attn_order_chip.reshape(chips, seq_size, 2 * mine).transpose(1, 0, 2).reshape(owners.shape)
     )
@@ -631,9 +672,6 @@
         + (attn_to ^ my_seq) * attn_room
         + attn_rank
     )
-    chip_slots = lax.dynamic_slice(
-        jnp.stack([attn_key, attn_rank]), (0, my_seq, 2 * my_chip, 0), (2, 1, 2, mine)
-    ).reshape(2, 1, 1, 2 * mine)
     my_slots = lax.dynamic_slice(
         jnp.stack([ffn_to, back_place, attn_back_place]), (0, my_seq, my_fsdp, 0), (3, 1, 1, mine)
     ).reshape(3, mine)
@@ -658,12 +696,6 @@
     ).reshape(4, 2 * seq_size * mine)
     my_key = 2 * my_seq + my_core
 
-    attn_message = attn_room + row_blocks * rows // tile + small_rows + -(-own_gains.shape[0] // tile**2)
-    attn_pack = pick(
-        (chip_slots[0] == (2 * (my_seq ^ flips) + my_core)[:, None, None])
-        & (chip_slots[1] == jnp.arange(attn_room)[None, :, None]),
-        both_slots,
-    )
     attn_keep = pick(
         (column_slots[0][None, :] == my_key)
         & (column_slots[1][None, :] == jnp.arange(attn_hold)[:, None]),
@@ -691,7 +723,11 @@
         (ffn_to.reshape(1, -1) == my_fsdp)
         & (ffn_place.reshape(1, -1) == jnp.arange(ffn_count)[:, None]),
         (
-            ffn_rank // ffn_half * (seq_size * ffn_half) + slot_seq * ffn_half + ffn_rank % ffn_half
+            jnp.where(
+                ffn_rank < ffn_half,
+                slot_seq * ffn_half + ffn_rank,
+                seq_size * ffn_half + slot_seq * ffn_rest + ffn_rank - ffn_half,
+            )
         ).reshape(1, -1),
     )
     ffn_cut = pick(
@@ -706,8 +742,6 @@
         jnp.where(seq_slots[0] == my_fsdp, 0, ffn_hold) + seq_slots[1],
     )
 
-    attn_sent = gather_tiles(masters, attn_pack.reshape(-1))
-    attn_sent = attn_sent.reshape(seq_size, attn_room, tile, tile)
     token_tiles = own_tokens.reshape(rows, row_blocks, tile).transpose(1, 0, 2)
     token_tiles = token_tiles.reshape(-1, tile, tile)
     gain_rows = own_gains.reshape(-1, tile)
@@ -732,9 +766,6 @@
     turns = jnp.arange(HEAD_DIM // 2).astype(f32)
     angle = reorder(position).astype(f32)[:, None] * (THETA ** (-2.0 * turns / HEAD_DIM))[None, :]
     cosine, sine = jnp.cos(angle)[:, None, :], jnp.sin(angle)[:, None, :]
-    ready = (allow, cosine, sine, attn_join, ffn_join)
-    ffn_got, attn_got, common, ready = lax.optimization_barrier((ffn_got, attn_got, common, ready))
-    allow, cosine, sine, attn_join, ffn_join = ready
     parts = [common] + [value[attn_room:] for value in attn_got[1:]]
     token_end = token_tiles.shape[0]
     small_end = token_end + small_rows
@@ -753,10 +784,14 @@
     )
     gain_full = gain_full.reshape(-1).astype(f32)
     gain_in = gain_full[0:width]
+    pack_normed = rms_norm(pack_tokens.astype(f32), gain_in).astype(bf16)
+    ready = (allow, cosine, sine, ffn_keep, attn_keep, pack_normed, gain_full)
+    ffn_got, attn_got, parts, ready = lax.optimization_barrier((ffn_got, attn_got, parts, ready))
+    allow, cosine, sine, ffn_keep, attn_keep, pack_normed, gain_full = ready
+    gain_in = gain_full[0:width]
     small_got = core_pair(seq_order(jnp.stack([part[token_end:small_end] for part in parts])))
     small_got = small_got.transpose(1, 0, 2, 3, 4)
     small_table = assemble(small_got.reshape((-1,) + small_master.shape[1:]), row_blocks)
-    pack_normed = rms_norm(pack_tokens.astype(f32), gain_in).astype(bf16)
     attn_kept = gather_tiles(attn_got, attn_keep)
     ffn_got = ffn_got + [core_swap(value) for value in ffn_got]
     ffn_kept = [
@@ -768,10 +803,7 @@
     attn_all = [attn_kept] + [chip_shift(attn_kept, offset) for offset in range(1, chips)]
     attn_all = attn_all + [core_swap(value) for value in attn_all]
 
-    attn_all, ffn_all[0], pack_normed, gain_full = lax.optimization_barrier(
-        (attn_all, ffn_all[0], pack_normed, gain_full)
-    )
-    gain_in = gain_full[0:width]
+    attn_all, ffn_all[0] = lax.optimization_barrier((attn_all, ffn_all[0]))
 
     def fetch(arrays, index, to, me, place, columns_of):
         def fast():
@@ -895,10 +927,9 @@
         [matmul_outer(third_low, vector_grad_low), matmul_outer(proj_grad_low, vector_low)], axis=1
     )
     small_early = small_sum(split_tiles(early_full, tile).reshape(-1, tile))
-    both_grad_low, small_early = lax.optimization_barrier((both_grad_low, small_early))
-    grad_feed = lax.psum_scatter(
-        matmul_flip(both_grad_low, w_both).astype(bf16), "fsdp", scatter_dimension=0, tiled=True
-    ).astype(f32)
+    feed_part = matmul_flip(both_grad_low, w_both).astype(bf16)
+    feed_part, small_early = lax.optimization_barrier((feed_part, small_early))
+    grad_feed = lax.psum_scatter(feed_part, "fsdp", scatter_dimension=0, tiled=True).astype(f32)
     both_grad_w = matmul_outer(feed_low, both_grad_low).astype(bf16)
     down_grad_w = matmul_outer(down_grad_low, hidden_low).astype(bf16)
     ffn_parts = [
@@ -964,9 +995,8 @@
     attn_parts = added(attn_own, core_swap(attn_given)).reshape(chips, attn_hold, tile, tile)
     attn_sum = attn_parts[0]
     attn_parts = [attn_parts[offset].astype(bf16) for offset in range(1, chips)]
-    normed_pre = matmul_flip(first_grad_low, w_first)
-    attn_sum, attn_parts, normed_pre = lax.optimization_barrier((attn_sum, attn_parts, normed_pre))
-    normed_sum = seq_sum(normed_pre, bf16)
+    normed_sum = seq_sum(matmul_flip(first_grad_low, w_first), bf16)
+    attn_sum, attn_parts, normed_sum = lax.optimization_barrier((attn_sum, attn_parts, normed_sum))
     for offset in range(1, chips):
         attn_sum = attn_sum + chip_shift(attn_parts[offset - 1], offset).astype(f32)
     attn_sum = attn_sum.astype(bf16)
@@ -1000,18 +1030,15 @@
     ).reshape(seq_size, -1, tile)
     late = seq_sum(late.reshape(-1, tile), bf16, True)
 
-    late = late + core_swap(late.astype(bf16)).astype(f32)
-    late_low = late.astype(bf16)
-    for offset in range(1, chips):
-        late = late + chip_shift(late_low, offset).astype(f32)
+    late = late.astype(bf16)
     ffn_sums, attn_sum, late, input_grad = lax.optimization_barrier(
         (ffn_sums, attn_sum, late, input_grad)
     )
     ffn_sums = ffn_sums + [core_swap(value) for value in ffn_sums]
     ffn_return = [gather_tiles(ffn_sums, ffn_back[i]) for i in range(chips)]
-    ffn_return, attn_sum = lax.optimization_barrier((ffn_return, attn_sum))
+    ffn_return, attn_sum, late = lax.optimization_barrier((ffn_return, attn_sum, late))
+    late = lax.psum(late, "fsdp").astype(f32)
     ffn_returned = chip_exchange(ffn_return)
-    ffn_returned = ffn_returned + [core_swap(value) for value in ffn_returned]
     late_rows = late_full.shape[0] // seq_size
     late_tiles = late[:late_rows].reshape(-1, 1, tile, tile)
     gain_grad_mine = late[late_rows:].reshape(-1)
@@ -1045,15 +1072,8 @@
         )
         return jnp.sum(spread.astype(f32), axis=0).astype(bf16)
 
-    tile_grads = ffn_returned + attn_returned
     slow_start = 2 * half + 2 * seq_size * attn_room
     slow_grads = lax.cond(fits, lambda: jnp.zeros((mine, tile, tile), bf16), slow_return)
-    tile_grads = tile_grads + [slow_grads]
-    slot_grad = jnp.where(fits, slot_grad, slow_start + local_slots)
-
-    tile_new, tile_first_new, tile_second_new = rotate_update(
-        tile_grads, slot_grad, tile_master, tile_first, tile_second, left_basis, right_basis, RATE_TILE
-    )
     small_new, small_first_new, small_second_new = rotate_update(
         [small_grad],
         jnp.arange(small_master.shape[0]),
@@ -1063,6 +1083,16 @@
         small_left,
         small_right,
         RATE_SMALL,
+    )
+    ffn_returned, slow_grads, small_new = lax.optimization_barrier(
+        (ffn_returned, slow_grads, small_new)
+    )
+    ffn_returned = ffn_returned + [core_swap(value) for value in ffn_returned]
+    tile_grads = ffn_returned + attn_returned + [slow_grads]
+    slot_grad = jnp.where(fits, slot_grad, slow_start + local_slots)
+
+    tile_new, tile_first_new, tile_second_new = rotate_update(
+        tile_grads, slot_grad, tile_master, tile_first, tile_second, left_basis, right_basis, RATE_TILE
     )
     gain_first_new = BETA_ONE * gain_first + (1.0 - BETA_ONE) * gain_grad_mine
     gain_second_new = BETA_TWO * gain_second + (1.0 - BETA_TWO) * gain_grad_mine * gain_grad_mine

time: 1210 us -> 1210 us (level)
  starting transfers between devices: 178 us -> 65.9 us
  waiting for transfers between devices: 504 us -> 568 us
  local copies, waits for them, and re-layouts: 120 us -> 154 us
    ppermute x24 -> x23, starting transfers between devices: 129 us -> 15.6 us  [core_swap(): return lax.ppermute(value, 'fsdp', [(i, i ^ 1) for i in range(size)])]
    psum x0 -> x1, waiting for transfers between devices: none -> 104 us  [on_device(): late = lax.psum(late, 'fsdp').astype(f32)]
    ppermute x21 -> x18, waiting for transfers between devices: 241 us -> 180 us  [chip_shift(): lax.ppermute(value, 'fsdp', [(i, (i // 2 + offset) % chips * 2 + i % 2) f...]
    ppermute x23, waiting for transfers between devices: 155 us -> 173 us  [seq_swap(): return lax.ppermute(value, 'seq', [(i, i ^ flip) for i in range(size)])]
    unnamed x417 -> x422, local copies, waits for them, and re-layouts: 59.1 us -> 71 us
    ppermute x21 -> x18, starting transfers between devices: 23.1 us -> 24.6 us  [chip_shift(): lax.ppermute(value, 'fsdp', [(i, (i // 2 + offset) % chips * 2 + i % 2) f...]
  transfers between devices with their start and end apart: 76 -> 73, of which waited for: 38 -> 40; matrix products, arithmetic and copies ran while one was open for 15% -> 18% of each run, Pallas kernels for 6% -> 7%
where the time goes in v9:
time: 1210 us; the launch traced here: 1200 us
  waiting for transfers between devices  568 us (47%)
  Pallas kernels  165 us (14%)
  local copies, waits for them, and re-layouts  154 us (13%)
  other arithmetic  104 us (9%)
  matrix products  97.8 us (8%)
  starting transfers between devices  65.9 us (5%)
  between operations  41.3 us (3%)
    ppermute x18, waiting for transfers between devices, chip_shift(): lax.ppermute(value, 'fsdp', [(i, (i // 2 + offset) % chips * 2 + i % 2) f...  180 us
    ppermute x23, waiting for transfers between devices, seq_swap(): return lax.ppermute(value, 'seq', [(i, i ^ flip) for i in range(size)])  173 us
    pallas_call x22, Pallas kernels, tile_kernel_call(): pl.pallas_call(kernel, grid=(steps,), cost_estimate=pl.CostEstimate(flops...  115 us
    psum x1, waiting for transfers between devices, on_device(): late = lax.psum(late, 'fsdp').astype(f32)  104 us
    unnamed x422, local copies, waits for them, and re-layouts  71 us
    reduce_scatter x1, waiting for transfers between devices, on_device(): lax.psum_scatter(matmul_flip(hidden_low, w_down).astype(bf16), 'fsdp', sc...  48.4 us
    pallas_call x2, Pallas kernels, rotate_update(): pl.pallas_call(kernel, grid=(count // each,), out_shape=(shape, shape, sh...  47.1 us
    dot_general x8, matrix products, matmul(): return jnp.dot(left, right, preferred_element_type=jnp.float32)  35 us
  transfers between devices with their start and end apart: 73, of which 40 were waited for; matrix products, arithmetic and copies ran while one was open for 18% of the time, Pallas kernels for 7%

profile of v9, /device:TPU:9, one launch (start us, length us, event | category | flops | bytes accessed | tf_op | source)
XLA Modules:
  0.0 1196.4 jit_solution(8228421893772909753)
XLA Ops:
  99.7 7.4 collective-permute-done.6.refs_3_
  110.1 20.5 %collective-permute-done.5.refs_2_ = bf16[40,128,128]{2,1,0:T(8,128)(2,1)} collective-permute-done((bf16[40,128,128]{2,1,0:T(8,128)(2,1)}, bf16[40,128,128]{2,1,0:T(8,128)(2,1)}, u32[]{:S(2)}, u32[]{:S(2)}) %collective-permute-start.5) | collective-permute-done | bytes 1310752 | tf_op jit(solution)/shard_map/ppermute | solution.py:382
  200.8 63.1 %collective-permute-done.13 = bf16[33,128,128]{2,1,0:T(8,128)(2,1)} collective-permute-done((bf16[33,128,128]{2,1,0:T(8,128)(2,1)S(1)}, bf16[33,128,128]{2,1,0:T(8,128)(2,1)}, u32[]{:S(2)}, u32[]{:S(2)}) %collective-permute-start.13) | collective-permute-done | bytes 1081376 | tf_op jit(solution)/shard_map/ppermute | solution.py:399
  265.5 20.7 %collective-permute-done.11 = bf16[33,128,128]{2,1,0:T(8,128)(2,1)} collective-permute-done((bf16[33,128,128]{2,1,0:T(8,128)(2,1)S(1)}, bf16[33,128,128]{2,1,0:T(8,128)(2,1)}, u32[]{:S(2)}, u32[]{:S(2)}) %collective-permute-start.11) | collective-permute-done | bytes 1081376 | tf_op jit(solution)/shard_map/ppermute | solution.py:399
  294.8 16.5 %conditional.3 = ((bf16[2048,768]{1,0:T(8,128)(2,1)}, bf16[2048,512]{1,0:T(8,128)(2,1)})) conditional(s32[]{:T(128)} %convert_element_type.348, (s32[]{:T(128)}, s32[4,8,116]{2,1,0:T(8,128)S(1)}, s32[4,8,116]{2,1,0:T(8,128)S(1)}, bf16[116,128,128]{2,1,0:T(8,128)(2,1)}) %tuple.65, (s32[]{:T(128)}, s32[4,8,116]{2,1,0:T(8,128)S(1)}, ...), branch_computations={%region_11.13_spmd, %region_13.15_spmd} | conditional | flops 2438944 | bytes 500902304 | solution.py:827
  300.5 10.7 branch_1_fun.2
  348.5 12.3 %collective-permute-done.19 = bf16[128,2048]{1,0:T(8,128)(2,1)S(1)} collective-permute-done((bf16[128,2048]{1,0:T(8,128)(2,1)}, bf16[128,2048]{1,0:T(8,128)(2,1)S(1)}, u32[]{:S(2)}, u32[]{:S(2)}) %collective-permute-start.19) | collective-permute-done | bytes 524320 | tf_op jit(solution)/shard_map/ppermute | solution.py:382
  360.8 24.5 %collective-permute-done.21 = bf16[128,2048]{1,0:T(8,128)(2,1)} collective-permute-done((bf16[128,2048]{1,0:T(8,128)(2,1)}, bf16[128,2048]{1,0:T(8,128)(2,1)}, u32[]{:S(2)}, u32[]{:S(2)}) %collective-permute-start.21) | collective-permute-done | bytes 524320 | tf_op jit(solution)/shard_map/ppermute | solution.py:382
  391.9 9.9 all-gather.9.cloned.1.call-done
  404.7 19.1 %conditional.4 = ((bf16[2048,2048]{1,0:T(8,128)(2,1)}, bf16[2048,1024]{1,0:T(8,128)(2,1)})) conditional(s32[]{:T(128)} %convert_element_type.348, (s32[]{:T(128)}, s32[4,8,116]{2,1,0:T(8,128)S(1)}, s32[4,8,116]{2,1,0:T(8,128)S(1)}, bf16[116,128,128]{2,1,0:T(8,128)(2,1)}) %tuple.261, (s32[]{:T(128)}, s32[4,8,116]{2,1,0:T(8,128)S(1)}, ...), branch_computations={%region_23.25_spmd, %region_25.27_spmd} | conditional | flops 5723916 | bytes 515585056 | solution.py:827
  409.7 14.1 %branch_1_fun.3 = (bf16[2048,2048]{1,0:T(8,128)(2,1)}, bf16[2048,1024]{1,0:T(8,128)(2,1)}) custom-call(s32[384]{0:T(512)S(1)} %broadcast_clamp_fusion.3.index_ref, bf16[224,128,128]{2,1,0:T(8,128)(2,1)} %get-tuple-element.247.refs_0_, bf16[304,128,128]{2,1,0:T(8,128)(2,1)} %get-tuple-element.248.refs_1_), custom_call_target="tpu_custom_call" | custom-call | bytes 25165824 | tf_op jit(solution)/shard_map/cond/branch_1_fun/pallas_call | solution.py:151
  423.8 28.1 %all-gather.7.cloned.1.call-done = bf16[1024,2048]{1,0:T(8,128)(2,1)} async-done(((bf16[128,2048]{1,0:T(8,128)(2,1)}), bf16[1024,2048]{1,0:T(8,128)(2,1)}) %all-gather.7.cloned.1.call-update) | async-done | bytes 4194320 | tf_op jit(solution)/shard_map/all_gather | solution.py:892
  451.9 12.5 %fusion.287 = f32[1024,2048]{1,0:T(8,128)S(1)} fusion(bf16[1024,2048]{1,0:T(8,128)(2,1)} %all-gather.7.cloned.1.call-done, bf16[2048,2048]{1,0:T(8,128)(2,1)} %get-tuple-element.404), kind=kOutput, calls=%fused_computation.731 | convolution fusion | flops 8589934592 | bytes 20971520 | tf_op jit(solution)/shard_map/dot_general | solution.py:61
  476.2 48.4 %reduce-scatter.5.cloned.1.call-done = bf16[128,2048]{1,0:T(8,128)(2,1)} async-done(((bf16[1024,2048]{1,0:T(8,128)(2,1)}), bf16[128,2048]{1,0:T(8,128)(2,1)}) %reduce-scatter.5.cloned.1.call-update) | async-done | bytes 524304 | tf_op jit(solution)/shard_map/reduce_scatter | solution.py:901
  594.6 12.1 %fusion.20 = (bf16[1024,1024]{1,0:T(8,128)(2,1)S(1)}, bf16[1024,1024]{1,0:T(8,128)(2,1)S(1)}) fusion(f32[1024,2048]{1,0:T(8,128)} %copy-done.53, bf16[1024,2048]{1,0:T(8,128)(2,1)} %all-gather.11.cloned.1.call-done, bf16[2048,1024]{1,0:T(8,128)(2,1)} %get-tuple-element.405), kind=kOutput, calls=%fused_computation.57 | convolution fusion | flops 4320133120 | bytes 20971520 | tf_op jit(solution)/shard_map/dot_general | solution.py:61
  608.7 12.6 %convolution_convert_fusion.1 = bf16[1024,2048]{1,0:T(8,128)(2,1)} fusion(bf16[2048,2048]{1,0:T(8,128)(2,1)} %get-tuple-element.404, bf16[1024,1024]{1,0:T(8,128)(2,1)S(1)} %get-tuple-element.575, bf16[1024,1024]{1,0:T(8,128)(2,1)S(1)} %get-tuple-element.574), kind=kOutput, calls=%fused_computation.64 | convolution fusion | flops 8600420352 | bytes 16777216 | tf_op jit(solution)/shard_map/dot_general | solution.py:65
  624.7 7.5 convolution_convert_fusion.2.refs_1_
  632.2 9.6 convolution_convert_fusion.refs_0_
  645.2 8.8 shard_map.267
  657.0 17.4 %shard_map.268 = bf16[304,128,128]{2,1,0:T(8,128)(2,1)S(1)} custom-call(s32[304]{0:T(512)S(1)} %min.230.index_ref, bf16[2048,2048]{1,0:T(8,128)(2,1)} %copy-done.34, bf16[2048,1024]{1,0:T(8,128)(2,1)} %copy-done.37), custom_call_target="tpu_custom_call" | custom-call | bytes 19922944 | tf_op jit(solution)/shard_map/pallas_call | solution.py:151
  691.5 21.6 %collective-permute-done.36 = bf16[128,2048]{1,0:T(8,128)(2,1)S(1)} collective-permute-done((bf16[128,2048]{1,0:T(8,128)(2,1)}, bf16[128,2048]{1,0:T(8,128)(2,1)S(1)}, u32[]{:S(2)}, u32[]{:S(2)}) %collective-permute-start.36) | collective-permute-done | bytes 524320 | tf_op jit(solution)/shard_map/ppermute | solution.py:382
  713.1 11.6 collective-permute-done.35
  724.7 10.1 collective-permute-done.34
  794.7 17.3 %collective-permute-done.39 = bf16[128,2048]{1,0:T(8,128)(2,1)S(1)} collective-permute-done((bf16[128,2048]{1,0:T(8,128)(2,1)}, bf16[128,2048]{1,0:T(8,128)(2,1)S(1)}, u32[]{:S(2)}, u32[]{:S(2)}) %collective-permute-start.39) | collective-permute-done | bytes 524320 | tf_op jit(solution)/shard_map/ppermute | solution.py:382
  812.1 23.0 %collective-permute-done.41 = bf16[128,2048]{1,0:T(8,128)(2,1)} collective-permute-done((bf16[128,2048]{1,0:T(8,128)(2,1)}, bf16[128,2048]{1,0:T(8,128)(2,1)}, u32[]{:S(2)}, u32[]{:S(2)}) %collective-permute-start.41) | collective-permute-done | bytes 524320 | tf_op jit(solution)/shard_map/ppermute | solution.py:382
  837.0 8.9 fusion.263
  881.2 68.4 %collective-permute-done.43 = bf16[33,128,128]{2,1,0:T(8,128)(2,1)} collective-permute-done((bf16[33,128,128]{2,1,0:T(8,128)(2,1)}, bf16[33,128,128]{2,1,0:T(8,128)(2,1)}, u32[]{:S(2)}, u32[]{:S(2)}) %collective-permute-start.43) | collective-permute-done | bytes 1081376 | tf_op jit(solution)/shard_map/ppermute | solution.py:399
  999.7 9.6 collective-permute-done.50.refs_1_
  1014.7 103.9 %all-reduce.7.cloned.1.call-done = bf16[537,128]{1,0:T(8,128)(2,1)} async-done(((bf16[537,128]{1,0:T(8,128)(2,1)}), bf16[537,128]{1,0:T(8,128)(2,1)}) %all-reduce.7.cloned.1.call-update) | async-done | bytes 137488 | tf_op jit(solution)/shard_map/psum | solution.py:1040
  1128.0 7.0 shard_map.275
  1136.3 7.9 collective-permute-done.62.refs_14_
  1149.5 40.1 %shard_map.280 = (f32[116,128,128]{2,1,0:T(8,128)}, f32[116,128,128]{2,1,0:T(8,128)}, f32[116,128,128]{2,1,0:T(8,128)}) custom-call(s32[116]{0:T(128)S(1)} %fusion.226.index_ref, bf16[37,128,128]{2,1,0:T(8,128)(2,1)S(1)} %copy-done.20, bf16[37,128,128]{2,1,0:T(8,128)(2,1)} %collective-permute-done.50.refs_1_, ...), custom_call_target="tpu_custom_call" | custom-call | tf_op jit(solution)/shard_map/pallas_call | solution.py:364
  (901 shorter events, 487.6 us)
Async XLA Ops:
  7.2 286.9 %all-gather.5.cloned.1.call-start = ((), (), s32[]{:S(2)}) async-start(), calls=%async_computation.7 | async-start | bytes 9175040 | tf_op jit(solution)/shard_map/all_gather | solution.py:802
  57.6 100.0 %collective-permute-start.1 = (bf16[37,128,128]{2,1,0:T(8,128)(2,1)}, bf16[37,128,128]{2,1,0:T(8,128)(2,1)}, u32[]{:S(2)}, u32[]{:S(2)}) collective-permute-start(bf16[37,128,128]{2,1,0:T(8,128)(2,1)} %copy-done.29), channel_id=1, source_target_pairs={{0,2},{1,3},{2,4},{3,5},{4,6},{5,7},{6,0},{7,1},{8,10},{9,11},{10,... | collective-permute-start | bytes 3637256 | tf_op jit(solution)/shard_map/ppermute | solution.py:399
  58.7 100.0 %collective-permute-start.2 = (bf16[37,128,128]{2,1,0:T(8,128)(2,1)}, bf16[37,128,128]{2,1,0:T(8,128)(2,1)}, u32[]{:S(2)}, u32[]{:S(2)}) collective-permute-start(bf16[37,128,128]{2,1,0:T(8,128)(2,1)} %copy-done.28), channel_id=1, source_target_pairs={{0,4},{1,5},{2,6},{3,7},{4,0},{5,1},{6,2},{7,3},{8,12},{9,13},{10,... | collective-permute-start | bytes 3637256 | tf_op jit(solution)/shard_map/ppermute | solution.py:399
  77.5 53.1 %collective-permute-start.5 = (bf16[40,128,128]{2,1,0:T(8,128)(2,1)}, bf16[40,128,128]{2,1,0:T(8,128)(2,1)}, u32[]{:S(2)}, u32[]{:S(2)}) collective-permute-start(bf16[40,128,128]{2,1,0:T(8,128)(2,1)} %get-tuple-element.616), channel_id=1, source_target_pairs={{0,16},{8,24},{16,0},{24,8},{1,17},{9,25},{17,1},{25,9},{2,18},{10... | collective-permute-start | bytes 3932168 | tf_op jit(solution)/shard_map/ppermute | solution.py:382
  77.5 53.8 %collective-permute-start.4 = (bf16[40,128,128]{2,1,0:T(8,128)(2,1)}, bf16[40,128,128]{2,1,0:T(8,128)(2,1)}, u32[]{:S(2)}, u32[]{:S(2)}) collective-permute-start(bf16[40,128,128]{2,1,0:T(8,128)(2,1)} %get-tuple-element.617), channel_id=1, source_target_pairs={{0,8},{8,0},{16,24},{24,16},{1,9},{9,1},{17,25},{25,17},{2,10},{10... | collective-permute-start | bytes 3932168 | tf_op jit(solution)/shard_map/ppermute | solution.py:382
  107.1 53.0 %collective-permute-start.3 = (bf16[37,128,128]{2,1,0:T(8,128)(2,1)}, bf16[37,128,128]{2,1,0:T(8,128)(2,1)}, u32[]{:S(2)}, u32[]{:S(2)}) collective-permute-start(bf16[37,128,128]{2,1,0:T(8,128)(2,1)} %copy-done.27), channel_id=1, source_target_pairs={{0,6},{1,7},{2,0},{3,1},{4,2},{5,3},{6,4},{7,5},{8,14},{9,15},{10,... | collective-permute-start | bytes 3637256 | tf_op jit(solution)/shard_map/ppermute | solution.py:399
  190.8 211.0 %all-gather.9.cloned.1.call-start = ((), (), s32[]{:S(2)}) async-start(), calls=%async_computation.9 | async-start | bytes 12451840 | tf_op jit(solution)/shard_map/all_gather | solution.py:802
  191.6 260.3 %all-gather.7.cloned.1.call-start = ((), (), s32[]{:S(2)}) async-start(), calls=%async_computation.8 | async-start | bytes 4718592 | tf_op jit(solution)/shard_map/all_gather | solution.py:892
  192.2 71.7 %collective-permute-start.13 = (bf16[33,128,128]{2,1,0:T(8,128)(2,1)S(1)}, bf16[33,128,128]{2,1,0:T(8,128)(2,1)}, u32[]{:S(2)}, u32[]{:S(2)}) collective-permute-start(bf16[33,128,128]{2,1,0:T(8,128)(2,1)S(1)} %copy-done.72), channel_id=1, source_target_pairs={{0,6},{1,7},{2,0},{3,1},{4,2},{5,3},{6,4},{7,5},{8,14},{9,15},{10,... | collective-permute-start | bytes 3244040 | tf_op jit(solution)/shard_map/ppermute | solution.py:399
  192.2 73.3 %collective-permute-start.12 = (bf16[33,128,128]{2,1,0:T(8,128)(2,1)S(1)}, bf16[33,128,128]{2,1,0:T(8,128)(2,1)}, u32[]{:S(2)}, u32[]{:S(2)}) collective-permute-start(bf16[33,128,128]{2,1,0:T(8,128)(2,1)S(1)} %copy-done.72), channel_id=1, source_target_pairs={{0,4},{1,5},{2,6},{3,7},{4,0},{5,1},{6,2},{7,3},{8,12},{9,13},{10,... | collective-permute-start | bytes 3244040 | tf_op jit(solution)/shard_map/ppermute | solution.py:399
  193.4 92.7 %collective-permute-start.11 = (bf16[33,128,128]{2,1,0:T(8,128)(2,1)S(1)}, bf16[33,128,128]{2,1,0:T(8,128)(2,1)}, u32[]{:S(2)}, u32[]{:S(2)}) collective-permute-start(bf16[33,128,128]{2,1,0:T(8,128)(2,1)S(1)} %copy-done.72), channel_id=1, source_target_pairs={{0,2},{1,3},{2,4},{3,5},{4,6},{5,7},{6,0},{7,1},{8,10},{9,11},{10,... | collective-permute-start | bytes 3244040 | tf_op jit(solution)/shard_map/ppermute | solution.py:399
  200.7 90.4 %collective-permute-start.14 = (bf16[33,128,128]{2,1,0:T(8,128)(2,1)S(1)}, bf16[33,128,128]{2,1,0:T(8,128)(2,1)S(1)}, u32[]{:S(2)}, u32[]{:S(2)}) collective-permute-start(bf16[33,128,128]{2,1,0:T(8,128)(2,1)S(1)} %copy-done.72), channel_id=1, source_target_pairs={{0,1},{1,0},{2,3},{3,2},{4,5},{5,4},{6,7},{7,6},{8,9},{9,8},{10,11... | collective-permute-start | bytes 3244040 | tf_op jit(solution)/shard_map/ppermute | solution.py:393
  289.2 51.1 %collective-permute-start.22 = (bf16[4,10,128,128]{3,2,1,0:T(8,128)(2,1)}, bf16[4,10,128,128]{3,2,1,0:T(8,128)(2,1)}, u32[]{:S(2)}, u32[]{:S(2)}) collective-permute-start(bf16[4,10,128,128]{3,2,1,0:T(8,128)(2,1)} %get-tuple-element.599), channel_id=1, source_target_pairs={{0,1},{1,0},{2,3},{3,2},{4,5},{5,4},{6,7},{7,6},{8,9},{9,8},{10,11... | collective-permute-start | bytes 3932168 | tf_op jit(solution)/shard_map/ppermute | solution.py:393
  337.4 47.9 %collective-permute-start.21 = (bf16[128,2048]{1,0:T(8,128)(2,1)}, bf16[128,2048]{1,0:T(8,128)(2,1)}, u32[]{:S(2)}, u32[]{:S(2)}) collective-permute-start(bf16[128,2048]{1,0:T(8,128)(2,1)} %get-tuple-element.588), channel_id=1, source_target_pairs={{0,24},{8,16},{16,8},{24,0},{1,25},{9,17},{17,9},{25,1},{2,26},{10... | collective-permute-start | bytes 1572872 | tf_op jit(solution)/shard_map/ppermute | solution.py:382
  339.4 45.9 %collective-permute-start.20 = (bf16[128,2048]{1,0:T(8,128)(2,1)}, bf16[128,2048]{1,0:T(8,128)(2,1)}, u32[]{:S(2)}, u32[]{:S(2)}) collective-permute-start(bf16[128,2048]{1,0:T(8,128)(2,1)} %get-tuple-element.589), channel_id=1, source_target_pairs={{0,16},{8,24},{16,0},{24,8},{1,17},{9,25},{17,1},{25,9},{2,18},{10... | collective-permute-start | bytes 1572872 | tf_op jit(solution)/shard_map/ppermute | solution.py:382
  391.8 132.8 %reduce-scatter.5.cloned.1.call-start = ((), (), s32[]{:S(2)}) async-start(), calls=%async_computation.10 | async-start | bytes 4718592 | tf_op jit(solution)/shard_map/reduce_scatter | solution.py:901
  476.1 118.4 %all-gather.11.cloned.1.call-start = ((), (), s32[]{:S(2)}) async-start(), calls=%async_computation.11 | async-start | bytes 4718592 | tf_op jit(solution)/shard_map/all_gather | solution.py:922
  533.4 144.8 %reduce-scatter.7.cloned.1.call-start = ((), (), s32[]{:S(2)}) async-start(), calls=%async_computation.12 | async-start | bytes 4718592 | tf_op jit(solution)/shard_map/reduce_scatter | solution.py:932
  621.3 159.4 %reduce-scatter.9.cloned.1.call-start = ((), (), s32[]{:S(2)}) async-start(), calls=%async_computation.13 | async-start | bytes 9175040 | tf_op jit(solution)/shard_map/reduce_scatter | solution.py:941
  680.5 276.7 %reduce-scatter.11.cloned.1.call-start = ((), (), s32[]{:S(2)}) async-start(), calls=%async_computation.14 | async-start | bytes 12451840 | tf_op jit(solution)/shard_map/reduce_scatter | solution.py:941
  689.6 45.2 %collective-permute-start.34 = (bf16[128,2048]{1,0:T(8,128)(2,1)}, bf16[128,2048]{1,0:T(8,128)(2,1)}, u32[]{:S(2)}, u32[]{:S(2)}) collective-permute-start(bf16[128,2048]{1,0:T(8,128)(2,1)} %get-tuple-element.610), channel_id=1, source_target_pairs={{0,8},{8,0},{16,24},{24,16},{1,9},{9,1},{17,25},{25,17},{2,10},{10... | collective-permute-start | bytes 1572872 | tf_op jit(solution)/shard_map/ppermute | solution.py:382
  691.5 427.2 %all-reduce.7.cloned.1.call-start = ((), (), s32[]{:S(2)}) async-start(), calls=%async_computation.15 | async-start | bytes 278528 | tf_op jit(solution)/shard_map/psum | solution.py:1040
  780.6 56.4 %collective-permute-start.38 = (bf16[132,128,128]{2,1,0:T(8,128)(2,1)}, bf16[132,128,128]{2,1,0:T(8,128)(2,1)}, u32[]{:S(2)}, u32[]{:S(2)}) collective-permute-start(bf16[132,128,128]{2,1,0:T(8,128)(2,1)} %copy-done.21), channel_id=1, source_target_pairs={{0,1},{1,0},{2,3},{3,2},{4,5},{5,4},{6,7},{7,6},{8,9},{9,8},{10,11... | collective-permute-start | bytes 12976136 | tf_op jit(solution)/shard_map/ppermute | solution.py:393
  789.5 45.5 %collective-permute-start.41 = (bf16[128,2048]{1,0:T(8,128)(2,1)}, bf16[128,2048]{1,0:T(8,128)(2,1)}, u32[]{:S(2)}, u32[]{:S(2)}) collective-permute-start(bf16[128,2048]{1,0:T(8,128)(2,1)} %get-tuple-element.582), channel_id=1, source_target_pairs={{0,24},{8,16},{16,8},{24,0},{1,25},{9,17},{17,9},{25,1},{2,26},{10... | collective-permute-start | bytes 1572872 | tf_op jit(solution)/shard_map/ppermute | solution.py:382
  790.7 44.3 %collective-permute-start.40 = (bf16[128,2048]{1,0:T(8,128)(2,1)}, bf16[128,2048]{1,0:T(8,128)(2,1)}, u32[]{:S(2)}, u32[]{:S(2)}) collective-permute-start(bf16[128,2048]{1,0:T(8,128)(2,1)} %get-tuple-element.583), channel_id=1, source_target_pairs={{0,16},{8,24},{16,0},{24,8},{1,17},{9,25},{17,1},{25,9},{2,18},{10... | collective-permute-start | bytes 1572872 | tf_op jit(solution)/shard_map/ppermute | solution.py:382
  857.9 91.7 %collective-permute-start.43 = (bf16[33,128,128]{2,1,0:T(8,128)(2,1)}, bf16[33,128,128]{2,1,0:T(8,128)(2,1)}, u32[]{:S(2)}, u32[]{:S(2)}) collective-permute-start(bf16[33,128,128]{2,1,0:T(8,128)(2,1)} %get-tuple-element.415), channel_id=1, source_target_pairs={{0,4},{1,5},{2,6},{3,7},{4,0},{5,1},{6,2},{7,3},{8,12},{9,13},{10,... | collective-permute-start | bytes 3244040 | tf_op jit(solution)/shard_map/ppermute | solution.py:399
  859.1 94.2 %collective-permute-start.44 = (bf16[33,128,128]{2,1,0:T(8,128)(2,1)}, bf16[33,128,128]{2,1,0:T(8,128)(2,1)}, u32[]{:S(2)}, u32[]{:S(2)}) collective-permute-start(bf16[33,128,128]{2,1,0:T(8,128)(2,1)} %get-tuple-element.416), channel_id=1, source_target_pairs={{0,6},{1,7},{2,0},{3,1},{4,2},{5,3},{6,4},{7,5},{8,14},{9,15},{10,... | collective-permute-start | bytes 3244040 | tf_op jit(solution)/shard_map/ppermute | solution.py:399
  981.5 138.1 %collective-permute-start.51 = (bf16[37,128,128]{2,1,0:T(8,128)(2,1)}, bf16[37,128,128]{2,1,0:T(8,128)(2,1)}, u32[]{:S(2)}, u32[]{:S(2)}) collective-permute-start(bf16[37,128,128]{2,1,0:T(8,128)(2,1)} %shard_map.273), channel_id=1, source_target_pairs={{0,4},{1,5},{2,6},{3,7},{4,0},{5,1},{6,2},{7,3},{8,12},{9,13},{10,... | collective-permute-start | bytes 3637256 | tf_op jit(solution)/shard_map/ppermute | solution.py:399
  982.4 152.6 %collective-permute-start.52 = (bf16[37,128,128]{2,1,0:T(8,128)(2,1)}, bf16[37,128,128]{2,1,0:T(8,128)(2,1)}, u32[]{:S(2)}, u32[]{:S(2)}) collective-permute-start(bf16[37,128,128]{2,1,0:T(8,128)(2,1)} %shard_map.274), channel_id=1, source_target_pairs={{0,6},{1,7},{2,0},{3,1},{4,2},{5,3},{6,4},{7,5},{8,14},{9,15},{10,... | collective-permute-start | bytes 3637256 | tf_op jit(solution)/shard_map/ppermute | solution.py:399
  990.9 144.2 %collective-permute-start.58 = (bf16[13,128,128]{2,1,0:T(8,128)(2,1)}, bf16[13,128,128]{2,1,0:T(8,128)(2,1)}, u32[]{:S(2)}, u32[]{:S(2)}) collective-permute-start(bf16[13,128,128]{2,1,0:T(8,128)(2,1)} %shard_map.278), channel_id=1, source_target_pairs={{0,16},{8,24},{16,0},{24,8},{1,17},{9,25},{17,1},{25,9},{2,18},{10... | collective-permute-start | bytes 1277960 | tf_op jit(solution)/shard_map/ppermute | solution.py:382
  995.8 139.8 %collective-permute-start.59 = (bf16[13,128,128]{2,1,0:T(8,128)(2,1)}, bf16[13,128,128]{2,1,0:T(8,128)(2,1)}, u32[]{:S(2)}, u32[]{:S(2)}) collective-permute-start(bf16[13,128,128]{2,1,0:T(8,128)(2,1)} %shard_map.279), channel_id=1, source_target_pairs={{0,24},{8,16},{16,8},{24,0},{1,25},{9,17},{17,9},{25,1},{2,26},{10... | collective-permute-start | bytes 1277960 | tf_op jit(solution)/shard_map/ppermute | solution.py:382
  1009.3 126.4 %collective-permute-start.60 = (bf16[13,128,128]{2,1,0:T(8,128)(2,1)}, bf16[13,128,128]{2,1,0:T(8,128)(2,1)}, u32[]{:S(2)}, u32[]{:S(2)}) collective-permute-start(bf16[13,128,128]{2,1,0:T(8,128)(2,1)} %shard_map.276.refs_8_), channel_id=1, source_target_pairs={{0,1},{1,0},{2,3},{3,2},{4,5},{5,4},{6,7},{7,6},{8,9},{9,8},{10,11... | collective-permute-start | bytes 1277960 | tf_op jit(solution)/shard_map/ppermute | solution.py:393
  (246 other events, 3596.1 us)
Sparse Core Ops, SparseCore 0:
  190.9 79.7 all-gather.4
  272.6 129.2 all-gather.8
  404.0 47.8 all-gather.6
  476.3 48.3 reduce-scatter.4
  533.5 52.3 all-gather.10
  621.4 46.9 reduce-scatter.6
  680.6 100.0 reduce-scatter.8
  783.8 124.6 reduce-scatter.10
  1011.7 106.8 all-reduce.6

commit v10 on v9

--- a/solution.py
+++ b/solution.py
@@ -140,8 +140,8 @@
 
 
 def steps_of(count):
-    for steps in range(4, 65):
-        if count % steps == 0 and 16 <= count // steps <= 160:
+    for steps in range(4, 129):
+        if count % steps == 0 and 16 <= count // steps <= 66:
             return steps
     return 2 if count % 2 == 0 else 1
 
@@ -657,6 +657,7 @@
         )
     )
     half = chips * ffn_room
+    rows_late = 2 * RANK * row_blocks // seq_size
     rank_core = chip_rank // ffn_room
     rank_local = chip_rank % ffn_room
     out_place = (
@@ -664,8 +665,12 @@
         + (my_chip - slot_chip) % chips * ffn_room
         + rank_local
     )
+    late_count = -(-(rows_late + own_gains.shape[0] // tile) // (2 * tile))
+    return_size = ffn_room + late_count
     back_place = (
-        jnp.where(rank_core == my_core, 0, half) + (my_chip - ffn_chip) % chips * ffn_room + rank_local
+        jnp.where(rank_core == my_core, 0, chips * return_size)
+        + (my_chip - ffn_chip) % chips * return_size
+        + rank_local
     )
     attn_back_place = (
         jnp.where(attn_core == my_core, 0, seq_size * attn_room)
@@ -803,7 +808,7 @@
     attn_all = [attn_kept] + [chip_shift(attn_kept, offset) for offset in range(1, chips)]
     attn_all = attn_all + [core_swap(value) for value in attn_all]
 
-    attn_all, ffn_all[0] = lax.optimization_barrier((attn_all, ffn_all[0]))
+    attn_all, ffn_all[0], attn_join = lax.optimization_barrier((attn_all, ffn_all[0], attn_join))
 
     def fetch(arrays, index, to, me, place, columns_of):
         def fast():
@@ -874,7 +879,7 @@
         .reshape(length, per_device * HEAD_DIM)
     )
     attn_pre = seq_sum(matmul_flip(attended_low, w_out), bf16)
-    attn_pre, small_table = lax.optimization_barrier((attn_pre, small_table))
+    attn_pre, small_table, ffn_join = lax.optimization_barrier((attn_pre, small_table, ffn_join))
     laurel_left = small_table[:, :RANK]
     laurel_right = small_table[:, RANK : 2 * RANK]
     vector_gate_w = small_table[:, 2 * RANK : 2 * RANK + PLD]
@@ -1031,27 +1036,25 @@
     late = seq_sum(late.reshape(-1, tile), bf16, True)
 
     late = late.astype(bf16)
+    late = added(late, core_swap(late)).astype(bf16)
     ffn_sums, attn_sum, late, input_grad = lax.optimization_barrier(
         (ffn_sums, attn_sum, late, input_grad)
     )
     ffn_sums = ffn_sums + [core_swap(value) for value in ffn_sums]
-    ffn_return = [gather_tiles(ffn_sums, ffn_back[i]) for i in range(chips)]
-    ffn_return, attn_sum, late = lax.optimization_barrier((ffn_return, attn_sum, late))
-    late = lax.psum(late, "fsdp").astype(f32)
+    late = jnp.pad(late, ((0, 2 * late_count * tile - late.shape[0]), (0, 0)))
+    late = late.reshape(2, late_count, tile, tile)
+    late = lax.dynamic_index_in_dim(late, my_core, 0, False)
+    late_index = 2 * ffn_hold + jnp.arange(late_count)
+    ffn_return = [
+        gather_tiles(ffn_sums + [late], jnp.concatenate([ffn_back[i], late_index]))
+        for i in range(chips)
+    ]
+    ffn_return, attn_sum = lax.optimization_barrier((ffn_return, attn_sum))
     ffn_returned = chip_exchange(ffn_return)
-    late_rows = late_full.shape[0] // seq_size
-    late_tiles = late[:late_rows].reshape(-1, 1, tile, tile)
-    gain_grad_mine = late[late_rows:].reshape(-1)
-    small_grad = jnp.concatenate(
-        [
-            late_tiles.astype(bf16),
-            small_early.reshape(late_tiles.shape[0], -1, tile, tile),
-        ],
-        axis=1,
-    ).reshape(small_master.shape)
     attn_returned = seq_exchange([gather_tiles([attn_sum], attn_back[i]) for i in range(seq_size)])
     attn_returned = attn_returned + [core_swap(value) for value in attn_returned]
-    slot_grad = jnp.where(my_slots[0] >= 0, my_slots[1], 2 * half + my_slots[2])
+    back_size = 2 * chips * return_size
+    slot_grad = jnp.where(my_slots[0] >= 0, my_slots[1], back_size + my_slots[2])
 
     def slow_return():
         own_ffn = split_tiles(both_grad_w, tile), split_tiles(down_grad_w, tile)
@@ -1072,8 +1075,28 @@
         )
         return jnp.sum(spread.astype(f32), axis=0).astype(bf16)
 
-    slow_start = 2 * half + 2 * seq_size * attn_room
+    slow_start = back_size + 2 * seq_size * attn_room
     slow_grads = lax.cond(fits, lambda: jnp.zeros((mine, tile, tile), bf16), slow_return)
+    ffn_returned, slow_grads = lax.optimization_barrier((ffn_returned, slow_grads))
+    late = sum(value[ffn_room:].astype(f32) for value in ffn_returned).astype(bf16)
+    late = core_pair(late).reshape(-1, tile).astype(f32)
+    ffn_returned = ffn_returned + [core_swap(value) for value in ffn_returned]
+    tile_grads = ffn_returned + attn_returned + [slow_grads]
+    slot_grad = jnp.where(fits, slot_grad, slow_start + local_slots)
+
+    tile_new, tile_first_new, tile_second_new = rotate_update(
+        tile_grads, slot_grad, tile_master, tile_first, tile_second, left_basis, right_basis, RATE_TILE
+    )
+    late_rows = late_full.shape[0] // seq_size
+    late_tiles = late[:late_rows].reshape(-1, 1, tile, tile)
+    gain_grad_mine = late[late_rows : late_rows + own_gains.shape[0] // tile].reshape(-1)
+    small_grad = jnp.concatenate(
+        [
+            late_tiles.astype(bf16),
+            small_early.reshape(late_tiles.shape[0], -1, tile, tile),
+        ],
+        axis=1,
+    ).reshape(small_master.shape)
     small_new, small_first_new, small_second_new = rotate_update(
         [small_grad],
         jnp.arange(small_master.shape[0]),
@@ -1083,16 +1106,6 @@
         small_left,
         small_right,
         RATE_SMALL,
-    )
-    ffn_returned, slow_grads, small_new = lax.optimization_barrier(
-        (ffn_returned, slow_grads, small_new)
-    )
-    ffn_returned = ffn_returned + [core_swap(value) for value in ffn_returned]
-    tile_grads = ffn_returned + attn_returned + [slow_grads]
-    slot_grad = jnp.where(fits, slot_grad, slow_start + local_slots)
-
-    tile_new, tile_first_new, tile_second_new = rotate_update(
-        tile_grads, slot_grad, tile_master, tile_first, tile_second, left_basis, right_basis, RATE_TILE
     )
     gain_first_new = BETA_ONE * gain_first + (1.0 - BETA_ONE) * gain_grad_mine
     gain_second_new = BETA_TWO * gain_second + (1.0 - BETA_TWO) * gain_grad_mine * gain_grad_mine

time: 1210 us -> 1190 us (0.983)
  starting transfers between devices: 65.9 us -> 113 us
  waiting for transfers between devices: 568 us -> 526 us
  local copies, waits for them, and re-layouts: 154 us -> 136 us
    psum x1 -> x0, waiting for transfers between devices: 104 us -> none  [on_device(): late = lax.psum(late, 'fsdp').astype(f32)]
    ppermute x23 -> x25, starting transfers between devices: 15.6 us -> 67 us  [core_swap(): return lax.ppermute(value, 'fsdp', [(i, i ^ 1) for i in range(size)])]
    ppermute x18, waiting for transfers between devices: 180 us -> 224 us  [chip_shift(): lax.ppermute(value, 'fsdp', [(i, (i // 2 + offset) % chips * 2 + i % 2) f...]
    unnamed x422 -> x460, local copies, waits for them, and re-layouts: 71 us -> 66.7 us
  transfers between devices with their start and end apart: 73 -> 74, of which waited for: 40 -> 39; matrix products, arithmetic and copies ran while one was open for 18% -> 17% of each run, Pallas kernels for 7% -> 8%
where the time goes in v10:
time: 1190 us; the launch traced here: 1170 us
  waiting for transfers between devices  526 us (44%)
  Pallas kernels  164 us (14%)
  local copies, waits for them, and re-layouts  136 us (11%)
  starting transfers between devices  113 us (9%)
  matrix products  96.8 us (8%)
  other arithmetic  93.1 us (8%)
  between operations  41.2 us (3%)
    ppermute x18, waiting for transfers between devices, chip_shift(): lax.ppermute(value, 'fsdp', [(i, (i // 2 + offset) % chips * 2 + i % 2) f...  224 us
    ppermute x23, waiting for transfers between devices, seq_swap(): return lax.ppermute(value, 'seq', [(i, i ^ flip) for i in range(size)])  183 us
    pallas_call x22, Pallas kernels, tile_kernel_call(): pl.pallas_call(kernel, grid=(steps,), cost_estimate=pl.CostEstimate(flops...  114 us
    ppermute x25, starting transfers between devices, core_swap(): return lax.ppermute(value, 'fsdp', [(i, i ^ 1) for i in range(size)])  67 us
    unnamed x460, local copies, waits for them, and re-layouts  66.7 us
    reduce_scatter x1, waiting for transfers between devices, on_device(): lax.psum_scatter(matmul_flip(hidden_low, w_down).astype(bf16), 'fsdp', sc...  48.3 us
    pallas_call x2, Pallas kernels, rotate_update(): pl.pallas_call(kernel, grid=(count // each,), out_shape=(shape, shape, sh...  47.6 us
    dot_general x8, matrix products, matmul(): return jnp.dot(left, right, preferred_element_type=jnp.float32)  33.5 us
  transfers between devices with their start and end apart: 74, of which 39 were waited for; matrix products, arithmetic and copies ran while one was open for 17% of the time, Pallas kernels for 8%

profile of v10, /device:TPU:9, one launch (start us, length us, event | category | flops | bytes accessed | tf_op | source)
XLA Modules:
  0.0 1171.7 jit_solution(17890370611828370020)
XLA Ops:
  81.9 13.9 %collective-permute-done.6.refs_3_ = bf16[40,128,128]{2,1,0:T(8,128)(2,1)} collective-permute-done((bf16[40,128,128]{2,1,0:T(8,128)(2,1)}, bf16[40,128,128]{2,1,0:T(8,128)(2,1)}, u32[]{:S(2)}, u32[]{:S(2)}) %collective-permute-start.6) | collective-permute-done | bytes 1310752 | tf_op jit(solution)/shard_map/ppermute | solution.py:382
  98.2 24.0 %collective-permute-done.5.refs_2_ = bf16[40,128,128]{2,1,0:T(8,128)(2,1)} collective-permute-done((bf16[40,128,128]{2,1,0:T(8,128)(2,1)}, bf16[40,128,128]{2,1,0:T(8,128)(2,1)}, u32[]{:S(2)}, u32[]{:S(2)}) %collective-permute-start.5) | collective-permute-done | bytes 1310752 | tf_op jit(solution)/shard_map/ppermute | solution.py:382
  202.6 15.7 %collective-permute-done.13 = bf16[33,128,128]{2,1,0:T(8,128)(2,1)S(1)} collective-permute-done((bf16[33,128,128]{2,1,0:T(8,128)(2,1)S(1)}, bf16[33,128,128]{2,1,0:T(8,128)(2,1)S(1)}, u32[]{:S(2)}, u32[]{:S(2)}) %collective-permute-start.13) | collective-permute-done | bytes 1081376 | tf_op jit(solution)/shard_map/ppermute | solution.py:399
  218.2 48.3 %collective-permute-start.17 = (bf16[33,128,128]{2,1,0:T(8,128)(2,1)S(1)}, bf16[33,128,128]{2,1,0:T(8,128)(2,1)S(1)}, u32[]{:S(2)}, u32[]{:S(2)}) collective-permute-start(bf16[33,128,128]{2,1,0:T(8,128)(2,1)S(1)} %collective-permute-done.13), channel_id=1, source_target_pairs={{0,1},{1,0},{2,3},{3,2},{4,5},{5,4},{6,7},{7,6},{8,9},{9,8},{10,11... | collective-permute-start | bytes 3244040 | tf_op jit(solution)/shard_map/ppermute | solution.py:393
  266.6 21.3 %collective-permute-done.11 = bf16[33,128,128]{2,1,0:T(8,128)(2,1)S(1)} collective-permute-done((bf16[33,128,128]{2,1,0:T(8,128)(2,1)S(1)}, bf16[33,128,128]{2,1,0:T(8,128)(2,1)S(1)}, u32[]{:S(2)}, u32[]{:S(2)}) %collective-permute-start.11) | collective-permute-done | bytes 1081376 | tf_op jit(solution)/shard_map/ppermute | solution.py:399
  295.1 11.1 conditional.3
  295.1 10.7 branch_1_fun.2
  340.4 13.6 %collective-permute-done.19 = bf16[128,2048]{1,0:T(8,128)(2,1)S(1)} collective-permute-done((bf16[128,2048]{1,0:T(8,128)(2,1)}, bf16[128,2048]{1,0:T(8,128)(2,1)S(1)}, u32[]{:S(2)}, u32[]{:S(2)}) %collective-permute-start.19) | collective-permute-done | bytes 524320 | tf_op jit(solution)/shard_map/ppermute | solution.py:382
  354.0 23.6 %collective-permute-done.21 = bf16[128,2048]{1,0:T(8,128)(2,1)} collective-permute-done((bf16[128,2048]{1,0:T(8,128)(2,1)}, bf16[128,2048]{1,0:T(8,128)(2,1)}, u32[]{:S(2)}, u32[]{:S(2)}) %collective-permute-start.21) | collective-permute-done | bytes 524320 | tf_op jit(solution)/shard_map/ppermute | solution.py:382
  384.2 13.8 %all-gather.9.cloned.1.call-done = bf16[304,128,128]{2,1,0:T(8,128)(2,1)} async-done(((bf16[76,128,128]{2,1,0:T(8,128)(2,1)}), bf16[304,128,128]{2,1,0:T(8,128)(2,1)}) %all-gather.9.cloned.1.call-update) | async-done | bytes 9961488 | tf_op jit(solution)/shard_map/all_gather | solution.py:807
  398.1 14.2 %conditional.4 = ((bf16[2048,2048]{1,0:T(8,128)(2,1)}, bf16[2048,1024]{1,0:T(8,128)(2,1)})) conditional(s32[]{:T(128)} %convert_element_type.377, (s32[]{:T(128)}, s32[4,8,116]{2,1,0:T(8,128)S(1)}, s32[4,8,116]{2,1,0:T(8,128)S(1)}, bf16[116,128,128]{2,1,0:T(8,128)(2,1)}) %tuple.237, (s32[384]{0:T(512)S(1)}, bf16[224,128,128]{2,1,0:T(8,128)(2,1)}, ...), branch_computations={%region_24.26_spmd, %region_26.27_spmd} | conditional | flops 5705344 | bytes 515585056 | solution.py:832
  398.3 14.0 %branch_1_fun.3 = (bf16[2048,2048]{1,0:T(8,128)(2,1)}, bf16[2048,1024]{1,0:T(8,128)(2,1)}) custom-call(s32[384]{0:T(512)S(1)} %broadcast_clamp_fusion.3.index_ref, bf16[224,128,128]{2,1,0:T(8,128)(2,1)} %get-tuple-element.81.refs_0_, bf16[304,128,128]{2,1,0:T(8,128)(2,1)} %get-tuple-element.82.refs_1_), custom_call_target="tpu_custom_call" | custom-call | bytes 25165824 | tf_op jit(solution)/shard_map/cond/branch_1_fun/pallas_call | solution.py:151
  412.3 33.1 %all-gather.7.cloned.1.call-done = bf16[1024,2048]{1,0:T(8,128)(2,1)} async-done(((bf16[128,2048]{1,0:T(8,128)(2,1)}), bf16[1024,2048]{1,0:T(8,128)(2,1)}) %all-gather.7.cloned.1.call-update) | async-done | bytes 4194320 | tf_op jit(solution)/shard_map/all_gather | solution.py:897
  445.4 12.5 %fusion.277 = f32[1024,2048]{1,0:T(8,128)S(1)} fusion(bf16[1024,2048]{1,0:T(8,128)(2,1)} %all-gather.7.cloned.1.call-done, bf16[2048,2048]{1,0:T(8,128)(2,1)} %get-tuple-element.240), kind=kOutput, calls=%fused_computation.726 | convolution fusion | flops 8589934592 | bytes 20971520 | tf_op jit(solution)/shard_map/dot_general | solution.py:61
  469.6 48.3 %reduce-scatter.5.cloned.1.call-done = bf16[128,2048]{1,0:T(8,128)(2,1)} async-done(((bf16[1024,2048]{1,0:T(8,128)(2,1)}), bf16[128,2048]{1,0:T(8,128)(2,1)}) %reduce-scatter.5.cloned.1.call-update) | async-done | bytes 524304 | tf_op jit(solution)/shard_map/reduce_scatter | solution.py:906
  587.4 12.1 %fusion.13 = (bf16[1024,1024]{1,0:T(8,128)(2,1)S(1)}, bf16[1024,1024]{1,0:T(8,128)(2,1)S(1)}) fusion(f32[1024,2048]{1,0:T(8,128)} %copy-done.58, bf16[1024,2048]{1,0:T(8,128)(2,1)} %all-gather.11.cloned.1.call-done, bf16[2048,1024]{1,0:T(8,128)(2,1)} %get-tuple-element.241), kind=kOutput, calls=%fused_computation.37 | convolution fusion | flops 4320133120 | bytes 20971520 | tf_op jit(solution)/shard_map/dot_general | solution.py:61
  601.5 12.6 %convolution_convert_fusion.1 = bf16[1024,2048]{1,0:T(8,128)(2,1)} fusion(bf16[2048,2048]{1,0:T(8,128)(2,1)} %get-tuple-element.240, bf16[1024,1024]{1,0:T(8,128)(2,1)S(1)} %get-tuple-element.383, bf16[1024,1024]{1,0:T(8,128)(2,1)S(1)} %get-tuple-element.382), kind=kOutput, calls=%fused_computation.44 | convolution fusion | flops 8600420352 | bytes 16777216 | tf_op jit(solution)/shard_map/dot_general | solution.py:65
  617.6 7.4 convolution_convert_fusion.2.refs_1_
  625.0 9.6 convolution_convert_fusion.refs_0_
  637.9 8.8 shard_map.267
  649.8 20.6 %shard_map.268 = bf16[304,128,128]{2,1,0:T(8,128)(2,1)S(1)} custom-call(s32[304]{0:T(512)S(1)} %min.224.index_ref, bf16[2048,2048]{1,0:T(8,128)(2,1)} %copy-done.37, bf16[2048,1024]{1,0:T(8,128)(2,1)} %copy-done.40), custom_call_target="tpu_custom_call" | custom-call | bytes 19922944 | tf_op jit(solution)/shard_map/pallas_call | solution.py:151
  687.4 21.6 %collective-permute-done.36 = bf16[128,2048]{1,0:T(8,128)(2,1)S(1)} collective-permute-done((bf16[128,2048]{1,0:T(8,128)(2,1)}, bf16[128,2048]{1,0:T(8,128)(2,1)S(1)}, u32[]{:S(2)}, u32[]{:S(2)}) %collective-permute-start.36) | collective-permute-done | bytes 524320 | tf_op jit(solution)/shard_map/ppermute | solution.py:382
  709.0 11.6 collective-permute-done.35
  720.6 10.1 collective-permute-done.34
  792.4 17.4 %collective-permute-done.39 = bf16[128,2048]{1,0:T(8,128)(2,1)S(1)} collective-permute-done((bf16[128,2048]{1,0:T(8,128)(2,1)}, bf16[128,2048]{1,0:T(8,128)(2,1)S(1)}, u32[]{:S(2)}, u32[]{:S(2)}) %collective-permute-start.39) | collective-permute-done | bytes 524320 | tf_op jit(solution)/shard_map/ppermute | solution.py:382
  809.8 23.0 %collective-permute-done.41 = bf16[128,2048]{1,0:T(8,128)(2,1)} collective-permute-done((bf16[128,2048]{1,0:T(8,128)(2,1)}, bf16[128,2048]{1,0:T(8,128)(2,1)}, u32[]{:S(2)}, u32[]{:S(2)}) %collective-permute-start.41) | collective-permute-done | bytes 524320 | tf_op jit(solution)/shard_map/ppermute | solution.py:382
  834.7 8.9 fusion.252
  874.6 7.3 collective-permute-done.42
  881.9 68.5 %collective-permute-done.43 = bf16[33,128,128]{2,1,0:T(8,128)(2,1)S(1)} collective-permute-done((bf16[33,128,128]{2,1,0:T(8,128)(2,1)}, bf16[33,128,128]{2,1,0:T(8,128)(2,1)S(1)}, u32[]{:S(2)}, u32[]{:S(2)}) %collective-permute-start.43) | collective-permute-done | bytes 1081376 | tf_op jit(solution)/shard_map/ppermute | solution.py:399
  999.5 11.5 collective-permute-done.51.refs_1_
  1014.5 78.7 %collective-permute-done.52.refs_2_ = bf16[40,128,128]{2,1,0:T(8,128)(2,1)S(1)} collective-permute-done((bf16[40,128,128]{2,1,0:T(8,128)(2,1)S(1)}, bf16[40,128,128]{2,1,0:T(8,128)(2,1)S(1)}, u32[]{:S(2)}, u32[]{:S(2)}) %collective-permute-start.52) | collective-permute-done | bytes 1310752 | tf_op jit(solution)/shard_map/ppermute | solution.py:399
  1124.0 40.6 %shard_map.279 = (f32[116,128,128]{2,1,0:T(8,128)}, f32[116,128,128]{2,1,0:T(8,128)}, f32[116,128,128]{2,1,0:T(8,128)}) custom-call(s32[116]{0:T(128)S(1)} %fusion.216.index_ref, bf16[40,128,128]{2,1,0:T(8,128)(2,1)S(1)} %copy-done.10, bf16[40,128,128]{2,1,0:T(8,128)(2,1)S(1)} %copy-done.22, bf16[40,128,128]{2,1,0:T(8,128)(2,1)S(1)} %copy-done.24, ...), custom_call_target="tpu_custom_call" | custom-call | tf_op jit(solution)/shard_map/pallas_call | solution.py:364
  (935 shorter events, 469.9 us)
Async XLA Ops:
  7.2 287.9 %all-gather.5.cloned.1.call-start = ((), (), s32[]{:S(2)}) async-start(), calls=%async_computation.7 | async-start | bytes 9175040 | tf_op jit(solution)/shard_map/all_gather | solution.py:807
  52.1 98.2 %collective-permute-start.1 = (bf16[37,128,128]{2,1,0:T(8,128)(2,1)}, bf16[37,128,128]{2,1,0:T(8,128)(2,1)}, u32[]{:S(2)}, u32[]{:S(2)}) collective-permute-start(bf16[37,128,128]{2,1,0:T(8,128)(2,1)} %copy-done.31), channel_id=1, source_target_pairs={{0,2},{1,3},{2,4},{3,5},{4,6},{5,7},{6,0},{7,1},{8,10},{9,11},{10,... | collective-permute-start | bytes 3637256 | tf_op jit(solution)/shard_map/ppermute | solution.py:399
  53.3 103.0 %collective-permute-start.2 = (bf16[37,128,128]{2,1,0:T(8,128)(2,1)}, bf16[37,128,128]{2,1,0:T(8,128)(2,1)}, u32[]{:S(2)}, u32[]{:S(2)}) collective-permute-start(bf16[37,128,128]{2,1,0:T(8,128)(2,1)} %copy-done.30), channel_id=1, source_target_pairs={{0,4},{1,5},{2,6},{3,7},{4,0},{5,1},{6,2},{7,3},{8,12},{9,13},{10,... | collective-permute-start | bytes 3637256 | tf_op jit(solution)/shard_map/ppermute | solution.py:399
  66.0 56.1 %collective-permute-start.5 = (bf16[40,128,128]{2,1,0:T(8,128)(2,1)}, bf16[40,128,128]{2,1,0:T(8,128)(2,1)}, u32[]{:S(2)}, u32[]{:S(2)}) collective-permute-start(bf16[40,128,128]{2,1,0:T(8,128)(2,1)} %get-tuple-element.424), channel_id=1, source_target_pairs={{0,16},{8,24},{16,0},{24,8},{1,17},{9,25},{17,1},{25,9},{2,18},{10... | collective-permute-start | bytes 3932168 | tf_op jit(solution)/shard_map/ppermute | solution.py:382
  66.4 56.5 %collective-permute-start.4 = (bf16[40,128,128]{2,1,0:T(8,128)(2,1)}, bf16[40,128,128]{2,1,0:T(8,128)(2,1)}, u32[]{:S(2)}, u32[]{:S(2)}) collective-permute-start(bf16[40,128,128]{2,1,0:T(8,128)(2,1)} %get-tuple-element.425), channel_id=1, source_target_pairs={{0,8},{8,0},{16,24},{24,16},{1,9},{9,1},{17,25},{25,17},{2,10},{10... | collective-permute-start | bytes 3932168 | tf_op jit(solution)/shard_map/ppermute | solution.py:382
  95.8 61.8 %collective-permute-start.3 = (bf16[37,128,128]{2,1,0:T(8,128)(2,1)}, bf16[37,128,128]{2,1,0:T(8,128)(2,1)S(1)}, u32[]{:S(2)}, u32[]{:S(2)}) collective-permute-start(bf16[37,128,128]{2,1,0:T(8,128)(2,1)} %copy-done.29), channel_id=1, source_target_pairs={{0,6},{1,7},{2,0},{3,1},{4,2},{5,3},{6,4},{7,5},{8,14},{9,15},{10,... | collective-permute-start | bytes 3637256 | tf_op jit(solution)/shard_map/ppermute | solution.py:399
  188.4 209.7 %all-gather.9.cloned.1.call-start = ((), (), s32[]{:S(2)}) async-start(), calls=%async_computation.9 | async-start | bytes 12451840 | tf_op jit(solution)/shard_map/all_gather | solution.py:807
  189.2 256.2 %all-gather.7.cloned.1.call-start = ((), (), s32[]{:S(2)}) async-start(), calls=%async_computation.8 | async-start | bytes 4718592 | tf_op jit(solution)/shard_map/all_gather | solution.py:897
  193.1 73.4 %collective-permute-start.12 = (bf16[33,128,128]{2,1,0:T(8,128)(2,1)S(1)}, bf16[33,128,128]{2,1,0:T(8,128)(2,1)S(1)}, u32[]{:S(2)}, u32[]{:S(2)}) collective-permute-start(bf16[33,128,128]{2,1,0:T(8,128)(2,1)S(1)} %copy-done.75), channel_id=1, source_target_pairs={{0,4},{1,5},{2,6},{3,7},{4,0},{5,1},{6,2},{7,3},{8,12},{9,13},{10,... | collective-permute-start | bytes 3244040 | tf_op jit(solution)/shard_map/ppermute | solution.py:399
  194.6 93.2 %collective-permute-start.11 = (bf16[33,128,128]{2,1,0:T(8,128)(2,1)S(1)}, bf16[33,128,128]{2,1,0:T(8,128)(2,1)S(1)}, u32[]{:S(2)}, u32[]{:S(2)}) collective-permute-start(bf16[33,128,128]{2,1,0:T(8,128)(2,1)S(1)} %copy-done.75), channel_id=1, source_target_pairs={{0,2},{1,3},{2,4},{3,5},{4,6},{5,7},{6,0},{7,1},{8,10},{9,11},{10,... | collective-permute-start | bytes 3244040 | tf_op jit(solution)/shard_map/ppermute | solution.py:399
  202.1 90.7 %collective-permute-start.14 = (bf16[33,128,128]{2,1,0:T(8,128)(2,1)S(1)}, bf16[33,128,128]{2,1,0:T(8,128)(2,1)S(1)}, u32[]{:S(2)}, u32[]{:S(2)}) collective-permute-start(bf16[33,128,128]{2,1,0:T(8,128)(2,1)S(1)} %copy-done.75), channel_id=1, source_target_pairs={{0,1},{1,0},{2,3},{3,2},{4,5},{5,4},{6,7},{7,6},{8,9},{9,8},{10,11... | collective-permute-start | bytes 3244040 | tf_op jit(solution)/shard_map/ppermute | solution.py:393
  218.2 74.5 %collective-permute-start.17 = (bf16[33,128,128]{2,1,0:T(8,128)(2,1)S(1)}, bf16[33,128,128]{2,1,0:T(8,128)(2,1)S(1)}, u32[]{:S(2)}, u32[]{:S(2)}) collective-permute-start(bf16[33,128,128]{2,1,0:T(8,128)(2,1)S(1)} %collective-permute-done.13), channel_id=1, source_target_pairs={{0,1},{1,0},{2,3},{3,2},{4,5},{5,4},{6,7},{7,6},{8,9},{9,8},{10,11... | collective-permute-start | bytes 3244040 | tf_op jit(solution)/shard_map/ppermute | solution.py:393
  292.4 39.9 %collective-permute-start.22 = (bf16[4,10,128,128]{3,2,1,0:T(8,128)(2,1)}, bf16[4,10,128,128]{3,2,1,0:T(8,128)(2,1)}, u32[]{:S(2)}, u32[]{:S(2)}) collective-permute-start(bf16[4,10,128,128]{3,2,1,0:T(8,128)(2,1)} %get-tuple-element.407), channel_id=1, source_target_pairs={{0,1},{1,0},{2,3},{3,2},{4,5},{5,4},{6,7},{7,6},{8,9},{9,8},{10,11... | collective-permute-start | bytes 3932168 | tf_op jit(solution)/shard_map/ppermute | solution.py:393
  329.9 47.7 %collective-permute-start.21 = (bf16[128,2048]{1,0:T(8,128)(2,1)}, bf16[128,2048]{1,0:T(8,128)(2,1)}, u32[]{:S(2)}, u32[]{:S(2)}) collective-permute-start(bf16[128,2048]{1,0:T(8,128)(2,1)} %get-tuple-element.396), channel_id=1, source_target_pairs={{0,24},{8,16},{16,8},{24,0},{1,25},{9,17},{17,9},{25,1},{2,26},{10... | collective-permute-start | bytes 1572872 | tf_op jit(solution)/shard_map/ppermute | solution.py:382
  331.5 46.1 %collective-permute-start.20 = (bf16[128,2048]{1,0:T(8,128)(2,1)}, bf16[128,2048]{1,0:T(8,128)(2,1)}, u32[]{:S(2)}, u32[]{:S(2)}) collective-permute-start(bf16[128,2048]{1,0:T(8,128)(2,1)} %get-tuple-element.397), channel_id=1, source_target_pairs={{0,16},{8,24},{16,0},{24,8},{1,17},{9,25},{17,1},{25,9},{2,18},{10... | collective-permute-start | bytes 1572872 | tf_op jit(solution)/shard_map/ppermute | solution.py:382
  384.2 133.8 %reduce-scatter.5.cloned.1.call-start = ((), (), s32[]{:S(2)}) async-start(), calls=%async_computation.10 | async-start | bytes 4718592 | tf_op jit(solution)/shard_map/reduce_scatter | solution.py:906
  469.6 117.8 %all-gather.11.cloned.1.call-start = ((), (), s32[]{:S(2)}) async-start(), calls=%async_computation.11 | async-start | bytes 4718592 | tf_op jit(solution)/shard_map/all_gather | solution.py:927
  526.9 147.2 %reduce-scatter.7.cloned.1.call-start = ((), (), s32[]{:S(2)}) async-start(), calls=%async_computation.12 | async-start | bytes 4718592 | tf_op jit(solution)/shard_map/reduce_scatter | solution.py:937
  614.1 164.2 %reduce-scatter.9.cloned.1.call-start = ((), (), s32[]{:S(2)}) async-start(), calls=%async_computation.13 | async-start | bytes 9175040 | tf_op jit(solution)/shard_map/reduce_scatter | solution.py:946
  676.4 280.2 %reduce-scatter.11.cloned.1.call-start = ((), (), s32[]{:S(2)}) async-start(), calls=%async_computation.14 | async-start | bytes 12451840 | tf_op jit(solution)/shard_map/reduce_scatter | solution.py:946
  684.2 36.4 %collective-permute-start.35 = (bf16[128,2048]{1,0:T(8,128)(2,1)}, bf16[128,2048]{1,0:T(8,128)(2,1)}, u32[]{:S(2)}, u32[]{:S(2)}) collective-permute-start(bf16[128,2048]{1,0:T(8,128)(2,1)} %get-tuple-element.418), channel_id=1, source_target_pairs={{0,16},{8,24},{16,0},{24,8},{1,17},{9,25},{17,1},{25,9},{2,18},{10... | collective-permute-start | bytes 1572872 | tf_op jit(solution)/shard_map/ppermute | solution.py:382
  685.2 45.5 %collective-permute-start.34 = (bf16[128,2048]{1,0:T(8,128)(2,1)}, bf16[128,2048]{1,0:T(8,128)(2,1)}, u32[]{:S(2)}, u32[]{:S(2)}) collective-permute-start(bf16[128,2048]{1,0:T(8,128)(2,1)} %get-tuple-element.418), channel_id=1, source_target_pairs={{0,8},{8,0},{16,24},{24,16},{1,9},{9,1},{17,25},{25,17},{2,10},{10... | collective-permute-start | bytes 1572872 | tf_op jit(solution)/shard_map/ppermute | solution.py:382
  778.3 56.4 %collective-permute-start.38 = (bf16[132,128,128]{2,1,0:T(8,128)(2,1)}, bf16[132,128,128]{2,1,0:T(8,128)(2,1)}, u32[]{:S(2)}, u32[]{:S(2)}) collective-permute-start(bf16[132,128,128]{2,1,0:T(8,128)(2,1)} %copy-done.19), channel_id=1, source_target_pairs={{0,1},{1,0},{2,3},{3,2},{4,5},{5,4},{6,7},{7,6},{8,9},{9,8},{10,11... | collective-permute-start | bytes 12976136 | tf_op jit(solution)/shard_map/ppermute | solution.py:393
  787.1 45.6 %collective-permute-start.41 = (bf16[128,2048]{1,0:T(8,128)(2,1)}, bf16[128,2048]{1,0:T(8,128)(2,1)}, u32[]{:S(2)}, u32[]{:S(2)}) collective-permute-start(bf16[128,2048]{1,0:T(8,128)(2,1)} %get-tuple-element.390), channel_id=1, source_target_pairs={{0,24},{8,16},{16,8},{24,0},{1,25},{9,17},{17,9},{25,1},{2,26},{10... | collective-permute-start | bytes 1572872 | tf_op jit(solution)/shard_map/ppermute | solution.py:382
  788.3 44.4 %collective-permute-start.40 = (bf16[128,2048]{1,0:T(8,128)(2,1)}, bf16[128,2048]{1,0:T(8,128)(2,1)}, u32[]{:S(2)}, u32[]{:S(2)}) collective-permute-start(bf16[128,2048]{1,0:T(8,128)(2,1)} %get-tuple-element.391), channel_id=1, source_target_pairs={{0,16},{8,24},{16,0},{24,8},{1,17},{9,25},{17,1},{25,9},{2,18},{10... | collective-permute-start | bytes 1572872 | tf_op jit(solution)/shard_map/ppermute | solution.py:382
  859.6 90.9 %collective-permute-start.43 = (bf16[33,128,128]{2,1,0:T(8,128)(2,1)}, bf16[33,128,128]{2,1,0:T(8,128)(2,1)S(1)}, u32[]{:S(2)}, u32[]{:S(2)}) collective-permute-start(bf16[33,128,128]{2,1,0:T(8,128)(2,1)} %get-tuple-element.251), channel_id=1, source_target_pairs={{0,4},{1,5},{2,6},{3,7},{4,0},{5,1},{6,2},{7,3},{8,12},{9,13},{10,... | collective-permute-start | bytes 3244040 | tf_op jit(solution)/shard_map/ppermute | solution.py:399
  863.9 91.1 %collective-permute-start.44 = (bf16[33,128,128]{2,1,0:T(8,128)(2,1)}, bf16[33,128,128]{2,1,0:T(8,128)(2,1)S(1)}, u32[]{:S(2)}, u32[]{:S(2)}) collective-permute-start(bf16[33,128,128]{2,1,0:T(8,128)(2,1)} %get-tuple-element.252), channel_id=1, source_target_pairs={{0,6},{1,7},{2,0},{3,1},{4,2},{5,3},{6,4},{7,5},{8,14},{9,15},{10,... | collective-permute-start | bytes 3244040 | tf_op jit(solution)/shard_map/ppermute | solution.py:399
  981.7 111.5 %collective-permute-start.52 = (bf16[40,128,128]{2,1,0:T(8,128)(2,1)S(1)}, bf16[40,128,128]{2,1,0:T(8,128)(2,1)S(1)}, u32[]{:S(2)}, u32[]{:S(2)}) collective-permute-start(bf16[40,128,128]{2,1,0:T(8,128)(2,1)S(1)} %shard_map.273), channel_id=1, source_target_pairs={{0,4},{1,5},{2,6},{3,7},{4,0},{5,1},{6,2},{7,3},{8,12},{9,13},{10,... | collective-permute-start | bytes 3932168 | tf_op jit(solution)/shard_map/ppermute | solution.py:399
  982.7 115.4 %collective-permute-start.53 = (bf16[40,128,128]{2,1,0:T(8,128)(2,1)}, bf16[40,128,128]{2,1,0:T(8,128)(2,1)}, u32[]{:S(2)}, u32[]{:S(2)}) collective-permute-start(bf16[40,128,128]{2,1,0:T(8,128)(2,1)} %shard_map.274), channel_id=1, source_target_pairs={{0,6},{1,7},{2,0},{3,1},{4,2},{5,3},{6,4},{7,5},{8,14},{9,15},{10,... | collective-permute-start | bytes 3932168 | tf_op jit(solution)/shard_map/ppermute | solution.py:399
  990.7 108.5 %collective-permute-start.59 = (bf16[13,128,128]{2,1,0:T(8,128)(2,1)}, bf16[13,128,128]{2,1,0:T(8,128)(2,1)}, u32[]{:S(2)}, u32[]{:S(2)}) collective-permute-start(bf16[13,128,128]{2,1,0:T(8,128)(2,1)} %shard_map.277), channel_id=1, source_target_pairs={{0,16},{8,24},{16,0},{24,8},{1,17},{9,25},{17,1},{25,9},{2,18},{10... | collective-permute-start | bytes 1277960 | tf_op jit(solution)/shard_map/ppermute | solution.py:382
  995.4 103.9 %collective-permute-start.60 = (bf16[13,128,128]{2,1,0:T(8,128)(2,1)}, bf16[13,128,128]{2,1,0:T(8,128)(2,1)}, u32[]{:S(2)}, u32[]{:S(2)}) collective-permute-start(bf16[13,128,128]{2,1,0:T(8,128)(2,1)} %shard_map.278), channel_id=1, source_target_pairs={{0,24},{8,16},{16,8},{24,0},{1,25},{9,17},{17,9},{25,1},{2,26},{10... | collective-permute-start | bytes 1277960 | tf_op jit(solution)/shard_map/ppermute | solution.py:382
  1011.0 88.7 %collective-permute-start.61 = (bf16[13,128,128]{2,1,0:T(8,128)(2,1)}, bf16[13,128,128]{2,1,0:T(8,128)(2,1)}, u32[]{:S(2)}, u32[]{:S(2)}) collective-permute-start(bf16[13,128,128]{2,1,0:T(8,128)(2,1)} %shard_map.275.refs_8_), channel_id=1, source_target_pairs={{0,1},{1,0},{2,3},{3,2},{4,5},{5,4},{6,7},{7,6},{8,9},{9,8},{10,11... | collective-permute-start | bytes 1277960 | tf_op jit(solution)/shard_map/ppermute | solution.py:393
  (264 other events, 3409.3 us)
Sparse Core Ops, SparseCore 0:
  188.5 79.2 all-gather.4
  269.7 128.3 all-gather.8
  400.2 45.1 all-gather.6
  469.7 48.2 reduce-scatter.4
  527.0 52.7 all-gather.10
  614.2 47.1 reduce-scatter.6
  676.4 101.8 reduce-scatter.8
  781.4 127.5 reduce-scatter.10

commit v11 on v10

--- a/solution.py
+++ b/solution.py
@@ -439,16 +439,20 @@
 
 def small_sum(value):
     seq_size = lax.axis_size("seq")
-    chips = lax.axis_size("fsdp") // 2
-    chip = lax.axis_index("fsdp") // 2
     even = lax.axis_index("fsdp") % 2 == 0
     low = value.astype(jnp.bfloat16)
     parts = low.reshape((seq_size, 2, low.shape[0] // (2 * seq_size)) + low.shape[1:])
     kept = jnp.where(even, parts[:, 0], parts[:, 1]).astype(jnp.float32)
     given = jnp.where(even, parts[:, 1], parts[:, 0])
     kept = kept + core_swap(given).astype(jnp.float32)
-    kept = seq_sum(kept.reshape((-1,) + low.shape[1:]), jnp.bfloat16, True)
-    kept = kept.reshape((chips, kept.shape[0] // chips) + kept.shape[1:])
+    return seq_sum(kept.reshape((-1,) + low.shape[1:]), jnp.bfloat16, True)
+
+
+def small_all(kept):
+    chips = lax.axis_size("fsdp") // 2
+    chip = lax.axis_index("fsdp") // 2
+    rows = kept.shape[0]
+    kept = kept.reshape((chips, rows // chips) + kept.shape[1:])
     kept = take_blocks(kept, (chip + jnp.arange(chips)) % chips)
     total = kept[0]
     for offset in range(1, chips):
@@ -456,7 +460,7 @@
     total = total.astype(jnp.bfloat16)
     parts = jnp.stack([total] + [chip_shift(total, offset) for offset in range(1, chips)])
     parts = take_blocks(parts, (chip - jnp.arange(chips)) % chips)
-    return core_pair(parts).reshape((value.shape[0] // seq_size,) + value.shape[1:])
+    return core_pair(parts).reshape((2 * rows,) + parts.shape[2:])
 
 
 def turn(value, cosine, sine):
@@ -531,9 +535,9 @@
     attn_hold = (room(attn_count, 1.0 / chips) + 1) // 2 + 1
     ffn_room = (room(2 * mine, ffn_share / chips) + 1) // 2
     both_count = row_blocks * ffn_first
-    ffn_hold = (room(ffn_count, 1.0 / seq_size) + 3) // 4 * 4
-    ffn_half = ffn_hold * 3 // 7 // 4 * 4
-    ffn_rest = ffn_hold - ffn_half
+    both_hold, down_hold = (
+        (room(count, 1.0 / seq_size) + 3) // 4 * 4 for count in (both_count, ffn_count - both_count)
+    )
 
     def tile_places(owner):
         row = owner // columns
@@ -548,10 +552,9 @@
         ffn_to = jnp.where(is_attn, -1, ffn_column // ffn_each)
         ffn_local = ffn_column % ffn_each
         ffn_place = jnp.where(
-            kind == 2,
-            both_count + row * ffn_each + ffn_local,
-            row * ffn_first + kind * ffn_each + ffn_local,
-        )
+            kind == 2, row * ffn_each + ffn_local, row * ffn_first + kind * ffn_each + ffn_local
+        )
+        is_down = (kind == 2).astype(jnp.int32)
         attn_to = jnp.where(
             key_at < 0,
             column // query_each,
@@ -575,7 +578,7 @@
             ),
         )
         attn_to = jnp.where(is_attn, attn_to, -1)
-        return (ffn_to, ffn_place, attn_to, attn_place)
+        return (ffn_to, is_down, ffn_place, attn_to, attn_place)
 
     owners = tile_owner.reshape(seq_size, fsdp_size, mine)
     slot_seq = jnp.arange(seq_size)[:, None, None]
@@ -619,8 +622,10 @@
     )
     ffn_got = chip_exchange(ffn_sent)
 
-    ffn_to, ffn_place, attn_to, attn_place = tile_places(owners)
+    ffn_to, is_down, ffn_place, attn_to, attn_place = tile_places(owners)
     ffn_chip = jnp.where(ffn_to < 0, -1, ffn_to // 2)
+    ffn_key = jnp.where(ffn_to < 0, -1, 2 * ffn_to + is_down)
+    ffn_hold = jnp.where(is_down == 1, down_hold, both_hold)
     attn_view = attn_to.reshape(seq_size, chips, 2 * mine)
     attn_rank = count_earlier(attn_view, attn_view >= 0).reshape(owners.shape)
     attn_core = (attn_rank + slot_seq) % 2
@@ -638,7 +643,7 @@
     )
     attn_sent = gather_tiles(masters, attn_pack.reshape(-1))
     attn_sent = attn_sent.reshape(seq_size, attn_room, tile, tile)
-    seq_view = ffn_to.reshape(seq_size, fsdp_size * mine)
+    seq_view = ffn_key.reshape(seq_size, fsdp_size * mine)
     ffn_rank = count_long(seq_view).reshape(owners.shape)
     def by_chip(value):
         value = value.reshape(seq_size, chips, 2 * mine).transpose(1, 0, 2)
@@ -683,7 +688,7 @@
     seq_slots = lax.dynamic_slice(
         jnp.stack(
             [
-                ffn_to,
+                ffn_key,
                 ffn_rank,
                 ffn_chip,
                 out_place,
@@ -720,31 +725,35 @@
             + attn_order
         ).reshape(1, -1),
     )
-    ffn_keep = pick(
-        (seq_slots[0][None, :] == my_fsdp) & (seq_slots[1][None, :] == jnp.arange(ffn_hold)[:, None]),
-        seq_slots[3][None, :],
-    )
-    ffn_join = pick(
-        (ffn_to.reshape(1, -1) == my_fsdp)
-        & (ffn_place.reshape(1, -1) == jnp.arange(ffn_count)[:, None]),
-        (
-            jnp.where(
-                ffn_rank < ffn_half,
-                slot_seq * ffn_half + ffn_rank,
-                seq_size * ffn_half + slot_seq * ffn_rest + ffn_rank - ffn_half,
-            )
-        ).reshape(1, -1),
-    )
-    ffn_cut = pick(
-        (ffn_to.reshape(seq_size, 1, -1) == my_fsdp)
-        & (ffn_rank.reshape(seq_size, 1, -1) == jnp.arange(ffn_hold)[None, :, None]),
-        ffn_place.reshape(seq_size, 1, -1),
-    )
+    def ffn_tables(kind, hold, count):
+        key = 2 * my_fsdp + kind
+        keep = pick(
+            (seq_slots[0][None, :] == key) & (seq_slots[1][None, :] == jnp.arange(hold)[:, None]),
+            seq_slots[3][None, :],
+        )
+        join = pick(
+            (ffn_key.reshape(1, -1) == key)
+            & (ffn_place.reshape(1, -1) == jnp.arange(count)[:, None]),
+            (slot_seq * hold + ffn_rank).reshape(1, -1),
+        )
+        cut = pick(
+            (ffn_key.reshape(seq_size, 1, -1) == key)
+            & (ffn_rank.reshape(seq_size, 1, -1) == jnp.arange(hold)[None, :, None]),
+            ffn_place.reshape(seq_size, 1, -1),
+        )
+        return (keep, join, cut)
+
+    both_keep, both_join, both_cut = ffn_tables(0, both_hold, both_count)
+    down_keep, down_join, down_cut = ffn_tables(1, down_hold, ffn_count - both_count)
     ffn_back = pick(
         (seq_slots[5][None, None, :] == ((my_chip + shifts) % chips)[:, None, None])
         & (seq_slots[2][None, None, :] == my_chip)
         & (seq_slots[4][None, None, :] == (my_core * ffn_room + jnp.arange(ffn_room))[None, :, None]),
-        jnp.where(seq_slots[0] == my_fsdp, 0, ffn_hold) + seq_slots[1],
+        jnp.where(seq_slots[0] % 2 == 1, 2 * both_hold, 0)
+        + jnp.where(
+            seq_slots[0] // 2 == my_fsdp, 0, jnp.where(seq_slots[0] % 2 == 1, down_hold, both_hold)
+        )
+        + seq_slots[1],
     )
 
     token_tiles = own_tokens.reshape(rows, row_blocks, tile).transpose(1, 0, 2)
@@ -790,25 +799,24 @@
     gain_full = gain_full.reshape(-1).astype(f32)
     gain_in = gain_full[0:width]
     pack_normed = rms_norm(pack_tokens.astype(f32), gain_in).astype(bf16)
-    ready = (allow, cosine, sine, ffn_keep, attn_keep, pack_normed, gain_full)
+    keeps = (both_keep, down_keep, attn_keep)
+    ready = (allow, cosine, sine, keeps, pack_normed, gain_full)
     ffn_got, attn_got, parts, ready = lax.optimization_barrier((ffn_got, attn_got, parts, ready))
-    allow, cosine, sine, ffn_keep, attn_keep, pack_normed, gain_full = ready
+    allow, cosine, sine, (both_keep, down_keep, attn_keep), pack_normed, gain_full = ready
     gain_in = gain_full[0:width]
     small_got = core_pair(seq_order(jnp.stack([part[token_end:small_end] for part in parts])))
     small_got = small_got.transpose(1, 0, 2, 3, 4)
     small_table = assemble(small_got.reshape((-1,) + small_master.shape[1:]), row_blocks)
     attn_kept = gather_tiles(attn_got, attn_keep)
     ffn_got = ffn_got + [core_swap(value) for value in ffn_got]
-    ffn_kept = [
-        gather_tiles(ffn_got, ffn_keep[:ffn_half]),
-        gather_tiles(ffn_got, ffn_keep[ffn_half:]),
-    ]
-    ffn_kept, attn_kept = lax.optimization_barrier((ffn_kept, attn_kept))
-    ffn_all = [lax.all_gather(value, "seq", axis=0, tiled=True) for value in ffn_kept]
+    both_kept, down_kept = gather_tiles(ffn_got, both_keep), gather_tiles(ffn_got, down_keep)
+    both_kept, down_kept, attn_kept = lax.optimization_barrier((both_kept, down_kept, attn_kept))
+    down_all = lax.all_gather(down_kept, "seq", axis=0, tiled=True)
+    both_all = lax.all_gather(both_kept, "seq", axis=0, tiled=True)
     attn_all = [attn_kept] + [chip_shift(attn_kept, offset) for offset in range(1, chips)]
     attn_all = attn_all + [core_swap(value) for value in attn_all]
 
-    attn_all, ffn_all[0], attn_join = lax.optimization_barrier((attn_all, ffn_all[0], attn_join))
+    attn_all, down_all, attn_join = lax.optimization_barrier((attn_all, down_all, attn_join))
 
     def fetch(arrays, index, to, me, place, columns_of):
         def fast():
@@ -879,7 +887,10 @@
         .reshape(length, per_device * HEAD_DIM)
     )
     attn_pre = seq_sum(matmul_flip(attended_low, w_out), bf16)
-    attn_pre, small_table, ffn_join = lax.optimization_barrier((attn_pre, small_table, ffn_join))
+    (w_down,) = fetch([down_all], down_join, ffn_key, 2 * my_fsdp + 1, ffn_place, (ffn_each,))
+    attn_pre, small_table, both_join, w_down = lax.optimization_barrier(
+        (attn_pre, small_table, both_join, w_down)
+    )
     laurel_left = small_table[:, :RANK]
     laurel_right = small_table[:, RANK : 2 * RANK]
     vector_gate_w = small_table[:, 2 * RANK : 2 * RANK + PLD]
@@ -895,10 +906,8 @@
     feed_normed, feed_pull = jax.vjp(rms_norm, second_sum, gain_pre)
     feed_own = feed_normed.astype(bf16)
     feed_low = lax.all_gather(feed_own, "fsdp", axis=0, tiled=True)
-    ffn_all, _ = lax.optimization_barrier((ffn_all, feed_own))
-    w_both, w_down = fetch(
-        ffn_all, ffn_join, ffn_to, my_fsdp, ffn_place, (ffn_first, ffn_each)
-    )
+    both_all, _ = lax.optimization_barrier((both_all, feed_own))
+    (w_both,) = fetch([both_all], both_join, ffn_key, 2 * my_fsdp, ffn_place, (ffn_first,))
     both_pre = matmul(feed_low, w_both)
     ffn_width = w_down.shape[1]
     hidden, hidden_pull = jax.vjp(gelu_product, both_pre[:, :ffn_width], both_pre[:, ffn_width:])
@@ -935,16 +944,35 @@
     feed_part = matmul_flip(both_grad_low, w_both).astype(bf16)
     feed_part, small_early = lax.optimization_barrier((feed_part, small_early))
     grad_feed = lax.psum_scatter(feed_part, "fsdp", scatter_dimension=0, tiled=True).astype(f32)
+
+    def cut_parts(flips_of, half):
+        half_now = down_hold // 2
+        rows_of = [lax.dynamic_index_in_dim(down_cut, my_seq ^ flip, 0, False) for flip in flips_of]
+        index = jnp.stack(rows_of)[:, half * half_now : (half + 1) * half_now]
+        return cut_tiles([down_grad_w], index.reshape(-1), tile)
+
+    down_grad_w = matmul_outer(down_grad_low, hidden_low).astype(bf16)
+    down_cuts = cut_parts([1, 3], 0), cut_parts([2, 3], 1)
+    feed_low, down_cuts = lax.optimization_barrier((feed_low, down_cuts))
+    down_one = added(cut_parts([0, 2], 0), seq_swap(down_cuts[0], 1))
+    down_two = added(cut_parts([0, 1], 1), seq_swap(down_cuts[1], 2))
     both_grad_w = matmul_outer(feed_low, both_grad_low).astype(bf16)
-    down_grad_w = matmul_outer(down_grad_low, hidden_low).astype(bf16)
-    ffn_parts = [
-        cut_tiles([both_grad_w, down_grad_w], index.reshape(-1), tile)
-        for index in (ffn_cut[:, :ffn_half], ffn_cut[:, ffn_half:])
+    both_half = both_hold * 3 // 7 // 4 * 4
+    both_parts = [
+        cut_tiles([both_grad_w], index.reshape(-1), tile)
+        for index in (both_cut[:, :both_half], both_cut[:, both_half:])
     ]
-    ffn_parts, grad_feed = lax.optimization_barrier((ffn_parts, grad_feed))
-    ffn_sums = [
-        lax.psum_scatter(value, "seq", scatter_dimension=0, tiled=True) for value in ffn_parts
+    both_parts, down_one, down_two, grad_feed, small_early = lax.optimization_barrier(
+        (both_parts, down_one, down_two, grad_feed, small_early)
+    )
+    both_sums = [
+        lax.psum_scatter(value, "seq", scatter_dimension=0, tiled=True) for value in both_parts
     ]
+    down_half = down_one.shape[0] // 2
+    down_one = added(down_one[:down_half], seq_swap(down_one[down_half:].astype(bf16), 2))
+    down_two = added(down_two[:down_half], seq_swap(down_two[down_half:].astype(bf16), 1))
+    down_sum = jnp.concatenate([down_one, down_two]).astype(bf16)
+    small_early = small_all(small_early)
 
     grad_second_norm, grad_gain_pre = feed_pull(grad_feed)
     half_grad = (grad_third + grad_second_norm) * ROOT_HALF
@@ -994,17 +1022,19 @@
         return cut_tiles([first_grad_w, out_grad_w], index.reshape(-1), tile)
 
     attn_given, attn_own = attn_cut(1 - my_core), attn_cut(my_core)
-    attn_given, attn_own, ffn_sums[0] = lax.optimization_barrier(
-        (attn_given, attn_own, ffn_sums[0])
+    attn_given, attn_own, small_early, down_sum, both_sums[0] = lax.optimization_barrier(
+        (attn_given, attn_own, small_early, down_sum, both_sums[0])
     )
     attn_parts = added(attn_own, core_swap(attn_given)).reshape(chips, attn_hold, tile, tile)
     attn_sum = attn_parts[0]
     attn_parts = [attn_parts[offset].astype(bf16) for offset in range(1, chips)]
-    normed_sum = seq_sum(matmul_flip(first_grad_low, w_first), bf16)
-    attn_sum, attn_parts, normed_sum = lax.optimization_barrier((attn_sum, attn_parts, normed_sum))
+    normed_pre = matmul_flip(first_grad_low, w_first)
+    attn_sum, attn_parts, normed_pre = lax.optimization_barrier((attn_sum, attn_parts, normed_pre))
+    normed_sum = seq_sum(normed_pre, bf16)
     for offset in range(1, chips):
         attn_sum = attn_sum + chip_shift(attn_parts[offset - 1], offset).astype(f32)
     attn_sum = attn_sum.astype(bf16)
+    attn_sum, normed_sum = lax.optimization_barrier((attn_sum, normed_sum))
     attn_back = pick(
         (column_slots[3][None, None, :] == (my_seq ^ flips)[:, None, None])
         & (column_slots[0][None, None, :] == my_key)
@@ -1037,14 +1067,13 @@
 
     late = late.astype(bf16)
     late = added(late, core_swap(late)).astype(bf16)
-    ffn_sums, attn_sum, late, input_grad = lax.optimization_barrier(
-        (ffn_sums, attn_sum, late, input_grad)
-    )
-    ffn_sums = ffn_sums + [core_swap(value) for value in ffn_sums]
+    both_sums, late, input_grad = lax.optimization_barrier((both_sums, late, input_grad))
+    ffn_sums = both_sums + [core_swap(value) for value in both_sums]
+    ffn_sums = ffn_sums + [down_sum, core_swap(down_sum)]
     late = jnp.pad(late, ((0, 2 * late_count * tile - late.shape[0]), (0, 0)))
     late = late.reshape(2, late_count, tile, tile)
     late = lax.dynamic_index_in_dim(late, my_core, 0, False)
-    late_index = 2 * ffn_hold + jnp.arange(late_count)
+    late_index = 2 * (both_hold + down_hold) + jnp.arange(late_count)
     ffn_return = [
         gather_tiles(ffn_sums + [late], jnp.concatenate([ffn_back[i], late_index]))
         for i in range(chips)
@@ -1062,7 +1091,7 @@
         parts = jnp.concatenate(own_ffn + own_attn + (jnp.zeros((1, tile, tile), bf16),))
         index = jnp.where(
             ffn_to == my_fsdp,
-            ffn_place,
+            is_down * both_count + ffn_place,
             jnp.where(attn_to == my_seq, ffn_count + attn_place, ffn_count + attn_count),
         )
         spread = gather_tiles([parts], index.reshape(-1))

time: 1190 us -> 1220 us (1.025)
  waiting for transfers between devices: 526 us -> 482 us
  local copies, waits for them, and re-layouts: 136 us -> 163 us
  other arithmetic: 93.1 us -> 116 us
  starting transfers between devices: 113 us -> 128 us
    ppermute x18, waiting for transfers between devices: 224 us -> 169 us  [chip_shift(): lax.ppermute(value, 'fsdp', [(i, (i // 2 + offset) % chips * 2 + i % 2) f...]
    all_gather x1, waiting for transfers between devices: 0.01 us -> 17.9 us  [on_device(): lax.all_gather(grad_down.astype(bf16), 'fsdp', axis=0, tiled=True)]
    ppermute x23 -> x27, waiting for transfers between devices: 183 us -> 170 us  [seq_swap(): return lax.ppermute(value, 'seq', [(i, i ^ flip) for i in range(size)])]
    ppermute x25 -> x26, starting transfers between devices: 67 us -> 79.8 us  [core_swap(): return lax.ppermute(value, 'fsdp', [(i, i ^ 1) for i in range(size)])]
    pallas_call x22 -> x27, Pallas kernels: 114 us -> 121 us  [tile_kernel_call(): pl.pallas_call(kernel, grid=(steps,), cost_estimate=pl.CostEstimate(flops...]
    unnamed x460 -> x478, local copies, waits for them, and re-layouts: 66.7 us -> 70.7 us
    ppermute x23 -> x27, starting transfers between devices: 22.7 us -> 26.7 us  [seq_swap(): return lax.ppermute(value, 'seq', [(i, i ^ flip) for i in range(size)])]
  transfers between devices with their start and end apart: 74 -> 79, of which waited for: 39 -> 40; matrix products, arithmetic and copies ran while one was open for 17% -> 21% of each run, Pallas kernels for 8% -> 8%
where the time goes in v11:
time: 1220 us; the launch traced here: 1210 us
  waiting for transfers between devices  482 us (40%)
  Pallas kernels  171 us (14%)
  local copies, waits for them, and re-layouts  163 us (13%)
  starting transfers between devices  128 us (10%)
  other arithmetic  116 us (10%)
  matrix products  102 us (8%)
  between operations  41.3 us (3%)
    ppermute x27, waiting for transfers between devices, seq_swap(): return lax.ppermute(value, 'seq', [(i, i ^ flip) for i in range(size)])  170 us
    ppermute x18, waiting for transfers between devices, chip_shift(): lax.ppermute(value, 'fsdp', [(i, (i // 2 + offset) % chips * 2 + i % 2) f...  169 us
    pallas_call x27, Pallas kernels, tile_kernel_call(): pl.pallas_call(kernel, grid=(steps,), cost_estimate=pl.CostEstimate(flops...  121 us
    ppermute x26, starting transfers between devices, core_swap(): return lax.ppermute(value, 'fsdp', [(i, i ^ 1) for i in range(size)])  79.8 us
    unnamed x478, local copies, waits for them, and re-layouts  70.7 us
    reduce_scatter x1, waiting for transfers between devices, on_device(): lax.psum_scatter(matmul_flip(hidden_low, w_down).astype(bf16), 'fsdp', sc...  48.2 us
    pallas_call x2, Pallas kernels, rotate_update(): pl.pallas_call(kernel, grid=(count // each,), out_shape=(shape, shape, sh...  47.4 us
    all_gather x1, waiting for transfers between devices, on_device(): feed_low = lax.all_gather(feed_own, 'fsdp', axis=0, tiled=True)  36.6 us
  transfers between devices with their start and end apart: 79, of which 40 were waited for; matrix products, arithmetic and copies ran while one was open for 21% of the time, Pallas kernels for 8%

profile of v11, /device:TPU:9, one launch (start us, length us, event | category | flops | bytes accessed | tf_op | source)
XLA Modules:
  0.0 1205.1 jit_solution(13164528803197242809)
XLA Ops:
  94.5 8.6 collective-permute-done.6.refs_3_
  104.8 24.5 %collective-permute-done.5.refs_2_ = bf16[40,128,128]{2,1,0:T(8,128)(2,1)} collective-permute-done((bf16[40,128,128]{2,1,0:T(8,128)(2,1)}, bf16[40,128,128]{2,1,0:T(8,128)(2,1)}, u32[]{:S(2)}, u32[]{:S(2)}) %collective-permute-start.5) | collective-permute-done | bytes 1310752 | tf_op jit(solution)/shard_map/ppermute | solution.py:382
  183.8 8.5 shard_map.264
  211.9 61.5 %collective-permute-done.13 = bf16[33,128,128]{2,1,0:T(8,128)(2,1)S(1)} collective-permute-done((bf16[33,128,128]{2,1,0:T(8,128)(2,1)S(1)}, bf16[33,128,128]{2,1,0:T(8,128)(2,1)S(1)}, u32[]{:S(2)}, u32[]{:S(2)}) %collective-permute-start.13) | collective-permute-done | bytes 1081376 | tf_op jit(solution)/shard_map/ppermute | solution.py:399
  273.9 21.2 %collective-permute-done.11 = bf16[33,128,128]{2,1,0:T(8,128)(2,1)S(1)} collective-permute-done((bf16[33,128,128]{2,1,0:T(8,128)(2,1)S(1)}, bf16[33,128,128]{2,1,0:T(8,128)(2,1)S(1)}, u32[]{:S(2)}, u32[]{:S(2)}) %collective-permute-start.11) | collective-permute-done | bytes 1081376 | tf_op jit(solution)/shard_map/ppermute | solution.py:399
  301.9 10.9 conditional.4
  301.9 10.7 branch_1_fun.3
  350.7 9.0 conditional.5
  351.7 7.6 branch_1_fun.4
  362.5 23.5 %collective-permute-done.21 = bf16[128,2048]{1,0:T(8,128)(2,1)} collective-permute-done((bf16[128,2048]{1,0:T(8,128)(2,1)}, bf16[128,2048]{1,0:T(8,128)(2,1)}, u32[]{:S(2)}, u32[]{:S(2)}) %collective-permute-start.21) | collective-permute-done | bytes 524320 | tf_op jit(solution)/shard_map/ppermute | solution.py:382
  394.2 24.3 %all-gather.9.cloned.1.call-done = bf16[368,128,128]{2,1,0:T(8,128)(2,1)} async-done(((bf16[92,128,128]{2,1,0:T(8,128)(2,1)}), bf16[368,128,128]{2,1,0:T(8,128)(2,1)}) %all-gather.9.cloned.1.call-update) | async-done | bytes 12058640 | tf_op jit(solution)/shard_map/all_gather | solution.py:815
  418.5 10.7 conditional.6
  418.5 10.7 branch_1_fun.5
  429.2 36.6 %all-gather.7.cloned.1.call-done = bf16[1024,2048]{1,0:T(8,128)(2,1)} async-done(((bf16[128,2048]{1,0:T(8,128)(2,1)}), bf16[1024,2048]{1,0:T(8,128)(2,1)}) %all-gather.7.cloned.1.call-update) | async-done | bytes 4194320 | tf_op jit(solution)/shard_map/all_gather | solution.py:908
  465.8 12.5 %fusion.282 = f32[1024,2048]{1,0:T(8,128)S(1)} fusion(bf16[1024,2048]{1,0:T(8,128)(2,1)} %all-gather.7.cloned.1.call-done, bf16[2048,2048]{1,0:T(8,128)(2,1)} %get-tuple-element.647), kind=kOutput, calls=%fused_computation.770 | convolution fusion | flops 8589934592 | bytes 20971520 | tf_op jit(solution)/shard_map/dot_general | solution.py:61
  490.8 48.2 %reduce-scatter.5.cloned.1.call-done = bf16[128,2048]{1,0:T(8,128)(2,1)} async-done(((bf16[1024,2048]{1,0:T(8,128)(2,1)}), bf16[128,2048]{1,0:T(8,128)(2,1)}) %reduce-scatter.5.cloned.1.call-update) | async-done | bytes 524304 | tf_op jit(solution)/shard_map/reduce_scatter | solution.py:915
  576.8 17.9 %all-gather.11.cloned.1.call-done = bf16[1024,2048]{1,0:T(8,128)(2,1)} async-done(((bf16[128,2048]{1,0:T(8,128)(2,1)}), bf16[1024,2048]{1,0:T(8,128)(2,1)}) %all-gather.11.cloned.1.call-update) | async-done | bytes 4194320 | tf_op jit(solution)/shard_map/all_gather | solution.py:936
  594.7 12.1 %fusion.13 = (bf16[1024,1024]{1,0:T(8,128)(2,1)S(1)}, bf16[1024,1024]{1,0:T(8,128)(2,1)S(1)}) fusion(f32[1024,2048]{1,0:T(8,128)} %copy-done.59, bf16[1024,2048]{1,0:T(8,128)(2,1)} %all-gather.11.cloned.1.call-done, bf16[2048,1024]{1,0:T(8,128)(2,1)} %get-tuple-element.646), kind=kOutput, calls=%fused_computation.43 | convolution fusion | flops 4320133120 | bytes 20971520 | tf_op jit(solution)/shard_map/dot_general | solution.py:61
  608.8 12.6 %convolution_convert_fusion.1 = bf16[1024,2048]{1,0:T(8,128)(2,1)} fusion(bf16[2048,2048]{1,0:T(8,128)(2,1)} %get-tuple-element.647, bf16[1024,1024]{1,0:T(8,128)(2,1)S(1)} %get-tuple-element.471, bf16[1024,1024]{1,0:T(8,128)(2,1)S(1)} %get-tuple-element.470), kind=kOutput, calls=%fused_computation.53 | convolution fusion | flops 8600420352 | bytes 16777216 | tf_op jit(solution)/shard_map/dot_general | solution.py:65
  664.5 10.1 convolution_convert_fusion.refs_0_
  685.1 13.3 %shard_map.270 = bf16[224,128,128]{2,1,0:T(8,128)(2,1)S(1)} custom-call(s32[224]{0:T(256)S(1)} %min.269.index_ref, bf16[2048,2048]{1,0:T(8,128)(2,1)} %copy-done.36), custom_call_target="tpu_custom_call" | custom-call | bytes 14680064 | tf_op jit(solution)/shard_map/pallas_call | solution.py:151
  745.6 8.7 collective-permute-done.31
  754.3 12.6 %collective-permute-done.30 = bf16[128,2048]{1,0:T(8,128)(2,1)S(1)} collective-permute-done((bf16[128,2048]{1,0:T(8,128)(2,1)S(1)}, bf16[128,2048]{1,0:T(8,128)(2,1)S(1)}, u32[]{:S(2)}, u32[]{:S(2)}) %collective-permute-start.30) | collective-permute-done | bytes 524320 | tf_op jit(solution)/shard_map/ppermute | solution.py:382
  784.6 21.9 %collective-permute-done.32 = bf16[512,256]{1,0:T(8,128)(2,1)S(1)} collective-permute-done((bf16[512,256]{1,0:T(8,128)(2,1)S(1)}, bf16[512,256]{1,0:T(8,128)(2,1)S(1)}, u32[]{:S(2)}, u32[]{:S(2)}) %collective-permute-start.32) | collective-permute-done | bytes 262176 | tf_op jit(solution)/shard_map/ppermute | solution.py:382
  843.8 8.7 fusion.257
  866.9 18.6 %collective-permute-done.46 = bf16[128,2048]{1,0:T(8,128)(2,1)S(1)} collective-permute-done((bf16[128,2048]{1,0:T(8,128)(2,1)S(1)}, bf16[128,2048]{1,0:T(8,128)(2,1)S(1)}, u32[]{:S(2)}, u32[]{:S(2)}) %collective-permute-start.46) | collective-permute-done | bytes 524320 | tf_op jit(solution)/shard_map/ppermute | solution.py:382
  892.5 15.1 %collective-permute-done.48 = bf16[128,2048]{1,0:T(8,128)(2,1)} collective-permute-done((bf16[128,2048]{1,0:T(8,128)(2,1)}, bf16[128,2048]{1,0:T(8,128)(2,1)}, u32[]{:S(2)}, u32[]{:S(2)}) %collective-permute-start.48) | collective-permute-done | bytes 524320 | tf_op jit(solution)/shard_map/ppermute | solution.py:382
  911.1 44.4 %collective-permute-done.44 = bf16[33,128,128]{2,1,0:T(8,128)(2,1)} collective-permute-done((bf16[33,128,128]{2,1,0:T(8,128)(2,1)}, bf16[33,128,128]{2,1,0:T(8,128)(2,1)}, u32[]{:S(2)}, u32[]{:S(2)}) %collective-permute-start.44) | collective-permute-done | bytes 1081376 | tf_op jit(solution)/shard_map/ppermute | solution.py:399
  1030.6 12.5 %collective-permute-done.56.refs_1_ = bf16[40,128,128]{2,1,0:T(8,128)(2,1)S(1)} collective-permute-done((bf16[40,128,128]{2,1,0:T(8,128)(2,1)S(1)}, bf16[40,128,128]{2,1,0:T(8,128)(2,1)S(1)}, u32[]{:S(2)}, u32[]{:S(2)}) %collective-permute-start.56) | collective-permute-done | bytes 1310752 | tf_op jit(solution)/shard_map/ppermute | solution.py:399
  1043.1 60.0 %collective-permute-start.66 = (bf16[13,128,128]{2,1,0:T(8,128)(2,1)}, bf16[13,128,128]{2,1,0:T(8,128)(2,1)}, u32[]{:S(2)}, u32[]{:S(2)}) collective-permute-start(bf16[13,128,128]{2,1,0:T(8,128)(2,1)} %shard_map.279.refs_8_), channel_id=1, source_target_pairs={{0,1},{1,0},{2,3},{3,2},{4,5},{5,4},{6,7},{7,6},{8,9},{9,8},{10,11... | collective-permute-start | bytes 1277960 | tf_op jit(solution)/shard_map/ppermute | solution.py:393
  1103.1 22.2 %collective-permute-done.57.refs_2_ = bf16[40,128,128]{2,1,0:T(8,128)(2,1)S(1)} collective-permute-done((bf16[40,128,128]{2,1,0:T(8,128)(2,1)S(1)}, bf16[40,128,128]{2,1,0:T(8,128)(2,1)S(1)}, u32[]{:S(2)}, u32[]{:S(2)}) %collective-permute-start.57) | collective-permute-done | bytes 1310752 | tf_op jit(solution)/shard_map/ppermute | solution.py:399
  1157.6 40.4 %shard_map.283 = (f32[116,128,128]{2,1,0:T(8,128)}, f32[116,128,128]{2,1,0:T(8,128)}, f32[116,128,128]{2,1,0:T(8,128)}) custom-call(s32[116]{0:T(128)S(1)} %fusion.221.index_ref, bf16[40,128,128]{2,1,0:T(8,128)(2,1)S(1)} %copy-done.11, bf16[40,128,128]{2,1,0:T(8,128)(2,1)S(1)} %copy-done.23, bf16[40,128,128]{2,1,0:T(8,128)(2,1)S(1)} %copy-done.25, ...), custom_call_target="tpu_custom_call" | custom-call | tf_op jit(solution)/shard_map/pallas_call | solution.py:364
  (999 shorter events, 536.5 us)
Async XLA Ops:
  7.2 294.7 %all-gather.5.cloned.1.call-start = ((), (), s32[]{:S(2)}) async-start(), calls=%async_computation.8 | async-start | bytes 9175040 | tf_op jit(solution)/shard_map/all_gather | solution.py:814
  54.9 101.2 %collective-permute-start.1 = (bf16[37,128,128]{2,1,0:T(8,128)(2,1)}, bf16[37,128,128]{2,1,0:T(8,128)(2,1)}, u32[]{:S(2)}, u32[]{:S(2)}) collective-permute-start(bf16[37,128,128]{2,1,0:T(8,128)(2,1)} %copy-done.32), channel_id=1, source_target_pairs={{0,2},{1,3},{2,4},{3,5},{4,6},{5,7},{6,0},{7,1},{8,10},{9,11},{10,... | collective-permute-start | bytes 3637256 | tf_op jit(solution)/shard_map/ppermute | solution.py:399
  56.2 102.9 %collective-permute-start.2 = (bf16[37,128,128]{2,1,0:T(8,128)(2,1)}, bf16[37,128,128]{2,1,0:T(8,128)(2,1)}, u32[]{:S(2)}, u32[]{:S(2)}) collective-permute-start(bf16[37,128,128]{2,1,0:T(8,128)(2,1)} %copy-done.31), channel_id=1, source_target_pairs={{0,4},{1,5},{2,6},{3,7},{4,0},{5,1},{6,2},{7,3},{8,12},{9,13},{10,... | collective-permute-start | bytes 3637256 | tf_op jit(solution)/shard_map/ppermute | solution.py:399
  73.3 56.0 %collective-permute-start.5 = (bf16[40,128,128]{2,1,0:T(8,128)(2,1)}, bf16[40,128,128]{2,1,0:T(8,128)(2,1)}, u32[]{:S(2)}, u32[]{:S(2)}) collective-permute-start(bf16[40,128,128]{2,1,0:T(8,128)(2,1)} %get-tuple-element.512), channel_id=1, source_target_pairs={{0,16},{8,24},{16,0},{24,8},{1,17},{9,25},{17,1},{25,9},{2,18},{10... | collective-permute-start | bytes 3932168 | tf_op jit(solution)/shard_map/ppermute | solution.py:382
  73.4 56.6 %collective-permute-start.4 = (bf16[40,128,128]{2,1,0:T(8,128)(2,1)}, bf16[40,128,128]{2,1,0:T(8,128)(2,1)}, u32[]{:S(2)}, u32[]{:S(2)}) collective-permute-start(bf16[40,128,128]{2,1,0:T(8,128)(2,1)} %get-tuple-element.513), channel_id=1, source_target_pairs={{0,8},{8,0},{16,24},{24,16},{1,9},{9,1},{17,25},{25,17},{2,10},{10... | collective-permute-start | bytes 3932168 | tf_op jit(solution)/shard_map/ppermute | solution.py:382
  103.1 57.4 %collective-permute-start.3 = (bf16[37,128,128]{2,1,0:T(8,128)(2,1)}, bf16[37,128,128]{2,1,0:T(8,128)(2,1)}, u32[]{:S(2)}, u32[]{:S(2)}) collective-permute-start(bf16[37,128,128]{2,1,0:T(8,128)(2,1)} %copy-done.30), channel_id=1, source_target_pairs={{0,6},{1,7},{2,0},{3,1},{4,2},{5,3},{6,4},{7,5},{8,14},{9,15},{10,... | collective-permute-start | bytes 3637256 | tf_op jit(solution)/shard_map/ppermute | solution.py:399
  192.4 226.1 %all-gather.9.cloned.1.call-start = ((), (), s32[]{:S(2)}) async-start(), calls=%async_computation.10 | async-start | bytes 15073280 | tf_op jit(solution)/shard_map/all_gather | solution.py:815
  193.2 272.6 %all-gather.7.cloned.1.call-start = ((), (), s32[]{:S(2)}) async-start(), calls=%async_computation.9 | async-start | bytes 4718592 | tf_op jit(solution)/shard_map/all_gather | solution.py:908
  201.5 71.9 %collective-permute-start.13 = (bf16[33,128,128]{2,1,0:T(8,128)(2,1)S(1)}, bf16[33,128,128]{2,1,0:T(8,128)(2,1)S(1)}, u32[]{:S(2)}, u32[]{:S(2)}) collective-permute-start(bf16[33,128,128]{2,1,0:T(8,128)(2,1)S(1)} %copy-done.76), channel_id=1, source_target_pairs={{0,6},{1,7},{2,0},{3,1},{4,2},{5,3},{6,4},{7,5},{8,14},{9,15},{10,... | collective-permute-start | bytes 3244040 | tf_op jit(solution)/shard_map/ppermute | solution.py:399
  201.5 71.9 %collective-permute-start.12 = (bf16[33,128,128]{2,1,0:T(8,128)(2,1)S(1)}, bf16[33,128,128]{2,1,0:T(8,128)(2,1)S(1)}, u32[]{:S(2)}, u32[]{:S(2)}) collective-permute-start(bf16[33,128,128]{2,1,0:T(8,128)(2,1)S(1)} %copy-done.76), channel_id=1, source_target_pairs={{0,4},{1,5},{2,6},{3,7},{4,0},{5,1},{6,2},{7,3},{8,12},{9,13},{10,... | collective-permute-start | bytes 3244040 | tf_op jit(solution)/shard_map/ppermute | solution.py:399
  202.8 92.2 %collective-permute-start.11 = (bf16[33,128,128]{2,1,0:T(8,128)(2,1)S(1)}, bf16[33,128,128]{2,1,0:T(8,128)(2,1)S(1)}, u32[]{:S(2)}, u32[]{:S(2)}) collective-permute-start(bf16[33,128,128]{2,1,0:T(8,128)(2,1)S(1)} %copy-done.76), channel_id=1, source_target_pairs={{0,2},{1,3},{2,4},{3,5},{4,6},{5,7},{6,0},{7,1},{8,10},{9,11},{10,... | collective-permute-start | bytes 3244040 | tf_op jit(solution)/shard_map/ppermute | solution.py:399
  211.8 87.6 %collective-permute-start.14 = (bf16[33,128,128]{2,1,0:T(8,128)(2,1)S(1)}, bf16[33,128,128]{2,1,0:T(8,128)(2,1)S(1)}, u32[]{:S(2)}, u32[]{:S(2)}) collective-permute-start(bf16[33,128,128]{2,1,0:T(8,128)(2,1)S(1)} %copy-done.76), channel_id=1, source_target_pairs={{0,1},{1,0},{2,3},{3,2},{4,5},{5,4},{6,7},{7,6},{8,9},{9,8},{10,11... | collective-permute-start | bytes 3244040 | tf_op jit(solution)/shard_map/ppermute | solution.py:393
  298.4 42.5 %collective-permute-start.22 = (bf16[4,10,128,128]{3,2,1,0:T(8,128)(2,1)}, bf16[4,10,128,128]{3,2,1,0:T(8,128)(2,1)}, u32[]{:S(2)}, u32[]{:S(2)}) collective-permute-start(bf16[4,10,128,128]{3,2,1,0:T(8,128)(2,1)} %get-tuple-element.495), channel_id=1, source_target_pairs={{0,1},{1,0},{2,3},{3,2},{4,5},{5,4},{6,7},{7,6},{8,9},{9,8},{10,11... | collective-permute-start | bytes 3932168 | tf_op jit(solution)/shard_map/ppermute | solution.py:393
  338.7 47.3 %collective-permute-start.21 = (bf16[128,2048]{1,0:T(8,128)(2,1)}, bf16[128,2048]{1,0:T(8,128)(2,1)}, u32[]{:S(2)}, u32[]{:S(2)}) collective-permute-start(bf16[128,2048]{1,0:T(8,128)(2,1)} %get-tuple-element.484), channel_id=1, source_target_pairs={{0,24},{8,16},{16,8},{24,0},{1,25},{9,17},{17,9},{25,1},{2,26},{10... | collective-permute-start | bytes 1572872 | tf_op jit(solution)/shard_map/ppermute | solution.py:382
  340.1 46.0 %collective-permute-start.20 = (bf16[128,2048]{1,0:T(8,128)(2,1)}, bf16[128,2048]{1,0:T(8,128)(2,1)}, u32[]{:S(2)}, u32[]{:S(2)}) collective-permute-start(bf16[128,2048]{1,0:T(8,128)(2,1)} %get-tuple-element.485), channel_id=1, source_target_pairs={{0,16},{8,24},{16,0},{24,8},{1,17},{9,25},{17,1},{25,9},{2,18},{10... | collective-permute-start | bytes 1572872 | tf_op jit(solution)/shard_map/ppermute | solution.py:382
  394.1 144.9 %reduce-scatter.5.cloned.1.call-start = ((), (), s32[]{:S(2)}) async-start(), calls=%async_computation.11 | async-start | bytes 4718592 | tf_op jit(solution)/shard_map/reduce_scatter | solution.py:915
  490.6 104.2 %all-gather.11.cloned.1.call-start = ((), (), s32[]{:S(2)}) async-start(), calls=%async_computation.12 | async-start | bytes 4718592 | tf_op jit(solution)/shard_map/all_gather | solution.py:936
  548.9 163.6 %reduce-scatter.7.cloned.1.call-start = ((), (), s32[]{:S(2)}) async-start(), calls=%async_computation.13 | async-start | bytes 4718592 | tf_op jit(solution)/shard_map/reduce_scatter | solution.py:946
  621.4 211.3 %reduce-scatter.9.cloned.1.call-start = ((), (), s32[]{:S(2)}) async-start(), calls=%async_computation.14 | async-start | bytes 5898240 | tf_op jit(solution)/shard_map/reduce_scatter | solution.py:969
  663.3 45.1 %collective-permute-start.24 = (bf16[56,128,128]{2,1,0:T(8,128)(2,1)}, bf16[56,128,128]{2,1,0:T(8,128)(2,1)}, u32[]{:S(2)}, u32[]{:S(2)}) collective-permute-start(bf16[56,128,128]{2,1,0:T(8,128)(2,1)} %shard_map.268), channel_id=1, source_target_pairs={{0,16},{8,24},{16,0},{24,8},{1,17},{9,25},{17,1},{25,9},{2,18},{10... | collective-permute-start | bytes 5505032 | tf_op jit(solution)/shard_map/ppermute | solution.py:382
  714.7 278.2 %reduce-scatter.11.cloned.1.call-start = ((), (), s32[]{:S(2)}) async-start(), calls=%async_computation.15 | async-start | bytes 9175040 | tf_op jit(solution)/shard_map/reduce_scatter | solution.py:969
  742.3 84.9 %collective-permute-start.41 = (bf16[28,128,128]{2,1,0:T(8,128)(2,1)}, bf16[28,128,128]{2,1,0:T(8,128)(2,1)}, u32[]{:S(2)}, u32[]{:S(2)}) collective-permute-start(bf16[28,128,128]{2,1,0:T(8,128)(2,1)} %slice.722), channel_id=1, source_target_pairs={{0,8},{8,0},{16,24},{24,16},{1,9},{9,1},{17,25},{25,17},{2,10},{10... | collective-permute-start | bytes 2752520 | tf_op jit(solution)/shard_map/ppermute | solution.py:382
  743.5 86.0 %collective-permute-start.40 = (bf16[28,128,128]{2,1,0:T(8,128)(2,1)}, bf16[28,128,128]{2,1,0:T(8,128)(2,1)}, u32[]{:S(2)}, u32[]{:S(2)}) collective-permute-start(bf16[28,128,128]{2,1,0:T(8,128)(2,1)} %slice.723), channel_id=1, source_target_pairs={{0,16},{8,24},{16,0},{24,8},{1,17},{9,25},{17,1},{25,9},{2,18},{10... | collective-permute-start | bytes 2752520 | tf_op jit(solution)/shard_map/ppermute | solution.py:382
  861.8 49.3 %collective-permute-start.43 = (bf16[33,128,128]{2,1,0:T(8,128)(2,1)}, bf16[33,128,128]{2,1,0:T(8,128)(2,1)}, u32[]{:S(2)}, u32[]{:S(2)}) collective-permute-start(bf16[33,128,128]{2,1,0:T(8,128)(2,1)} %get-tuple-element.326), channel_id=1, source_target_pairs={{0,2},{1,3},{2,4},{3,5},{4,6},{5,7},{6,0},{7,1},{8,10},{9,11},{10,... | collective-permute-start | bytes 3244040 | tf_op jit(solution)/shard_map/ppermute | solution.py:399
  863.0 92.4 %collective-permute-start.44 = (bf16[33,128,128]{2,1,0:T(8,128)(2,1)}, bf16[33,128,128]{2,1,0:T(8,128)(2,1)}, u32[]{:S(2)}, u32[]{:S(2)}) collective-permute-start(bf16[33,128,128]{2,1,0:T(8,128)(2,1)} %get-tuple-element.327), channel_id=1, source_target_pairs={{0,4},{1,5},{2,6},{3,7},{4,0},{5,1},{6,2},{7,3},{8,12},{9,13},{10,... | collective-permute-start | bytes 3244040 | tf_op jit(solution)/shard_map/ppermute | solution.py:399
  864.1 94.2 %collective-permute-start.45 = (bf16[33,128,128]{2,1,0:T(8,128)(2,1)}, bf16[33,128,128]{2,1,0:T(8,128)(2,1)}, u32[]{:S(2)}, u32[]{:S(2)}) collective-permute-start(bf16[33,128,128]{2,1,0:T(8,128)(2,1)} %get-tuple-element.328), channel_id=1, source_target_pairs={{0,6},{1,7},{2,0},{3,1},{4,2},{5,3},{6,4},{7,5},{8,14},{9,15},{10,... | collective-permute-start | bytes 3244040 | tf_op jit(solution)/shard_map/ppermute | solution.py:399
  907.6 88.1 %collective-permute-start.55 = (bf16[56,128,128]{2,1,0:T(8,128)(2,1)S(1)}, bf16[56,128,128]{2,1,0:T(8,128)(2,1)}, u32[]{:S(2)}, u32[]{:S(2)}) collective-permute-start(bf16[56,128,128]{2,1,0:T(8,128)(2,1)S(1)} %pad_maximum_fusion.11.refs_4_), channel_id=1, source_target_pairs={{0,1},{1,0},{2,3},{3,2},{4,5},{5,4},{6,7},{7,6},{8,9},{9,8},{10,11... | collective-permute-start | bytes 5505032 | tf_op jit(solution)/shard_map/ppermute | solution.py:393
  1015.2 110.1 %collective-permute-start.57 = (bf16[40,128,128]{2,1,0:T(8,128)(2,1)S(1)}, bf16[40,128,128]{2,1,0:T(8,128)(2,1)S(1)}, u32[]{:S(2)}, u32[]{:S(2)}) collective-permute-start(bf16[40,128,128]{2,1,0:T(8,128)(2,1)S(1)} %shard_map.277), channel_id=1, source_target_pairs={{0,4},{1,5},{2,6},{3,7},{4,0},{5,1},{6,2},{7,3},{8,12},{9,13},{10,... | collective-permute-start | bytes 3932168 | tf_op jit(solution)/shard_map/ppermute | solution.py:399
  1015.9 115.6 %collective-permute-start.58 = (bf16[40,128,128]{2,1,0:T(8,128)(2,1)}, bf16[40,128,128]{2,1,0:T(8,128)(2,1)}, u32[]{:S(2)}, u32[]{:S(2)}) collective-permute-start(bf16[40,128,128]{2,1,0:T(8,128)(2,1)} %shard_map.278), channel_id=1, source_target_pairs={{0,6},{1,7},{2,0},{3,1},{4,2},{5,3},{6,4},{7,5},{8,14},{9,15},{10,... | collective-permute-start | bytes 3932168 | tf_op jit(solution)/shard_map/ppermute | solution.py:399
  1023.9 108.7 %collective-permute-start.64 = (bf16[13,128,128]{2,1,0:T(8,128)(2,1)}, bf16[13,128,128]{2,1,0:T(8,128)(2,1)}, u32[]{:S(2)}, u32[]{:S(2)}) collective-permute-start(bf16[13,128,128]{2,1,0:T(8,128)(2,1)} %shard_map.281), channel_id=1, source_target_pairs={{0,16},{8,24},{16,0},{24,8},{1,17},{9,25},{17,1},{25,9},{2,18},{10... | collective-permute-start | bytes 1277960 | tf_op jit(solution)/shard_map/ppermute | solution.py:382
  1027.2 105.6 %collective-permute-start.65 = (bf16[13,128,128]{2,1,0:T(8,128)(2,1)}, bf16[13,128,128]{2,1,0:T(8,128)(2,1)}, u32[]{:S(2)}, u32[]{:S(2)}) collective-permute-start(bf16[13,128,128]{2,1,0:T(8,128)(2,1)} %shard_map.282), channel_id=1, source_target_pairs={{0,24},{8,16},{16,8},{24,0},{1,25},{9,17},{17,9},{25,1},{2,26},{10... | collective-permute-start | bytes 1277960 | tf_op jit(solution)/shard_map/ppermute | solution.py:382
  1043.1 90.1 %collective-permute-start.66 = (bf16[13,128,128]{2,1,0:T(8,128)(2,1)}, bf16[13,128,128]{2,1,0:T(8,128)(2,1)}, u32[]{:S(2)}, u32[]{:S(2)}) collective-permute-start(bf16[13,128,128]{2,1,0:T(8,128)(2,1)} %shard_map.279.refs_8_), channel_id=1, source_target_pairs={{0,1},{1,0},{2,3},{3,2},{4,5},{5,4},{6,7},{7,6},{8,9},{9,8},{10,11... | collective-permute-start | bytes 1277960 | tf_op jit(solution)/shard_map/ppermute | solution.py:393
  (278 other events, 4146.4 us)
Sparse Core Ops, SparseCore 0:
  192.5 78.2 all-gather.4
  272.6 145.8 all-gather.8
  420.6 45.0 all-gather.6
  490.7 48.2 reduce-scatter.4
  549.0 45.6 all-gather.10
  621.6 48.5 reduce-scatter.6
  714.7 96.3 reduce-scatter.8
  836.7 99.3 reduce-scatter.10

commit v12 on v10

--- a/solution.py
+++ b/solution.py
@@ -28,7 +28,8 @@
 RATE_GAIN = 0.3
 DECAY = 0.01
 NEGATIVE = -1e30
-VMEM_BYTES = 32 * 1024 * 1024
+TILE = 128
+VMEM_BYTES = 4 * 1024 * 1024
 
 
 def rms_norm(value, gain):
@@ -131,7 +132,7 @@
         ],
         out_specs=pl.BlockSpec((1, 1, size), lambda i: (i, 0, 0)),
         cost_estimate=pl.CostEstimate(flops=0, transcendentals=0, bytes_accessed=0),
-        compiler_params=pltpu.CompilerParams(vmem_limit_bytes=VMEM_BYTES),
+        compiler_params=pltpu.CompilerParams(vmem_limit_bytes=4 * VMEM_BYTES),
     )(keys[:, None, :], keys[:, :, None]).reshape(groups, size)
 
 
@@ -139,11 +140,11 @@
     return jnp.sum(jnp.where(match, value, 0), axis=-1)
 
 
-def steps_of(count):
-    for steps in range(4, 129):
-        if count % steps == 0 and 16 <= count // steps <= 66:
+def steps_of(counts):
+    for steps in (8, 4, 2):
+        if all(count % steps == 0 for count in counts) and sum(counts) // steps >= 24:
             return steps
-    return 2 if count % 2 == 0 else 1
+    return 1
 
 
 def tile_kernel_call(kernel, index, arrays, out_shape, out_specs, steps):
@@ -157,7 +158,7 @@
         + [pl.BlockSpec(memory_space=pl.ANY)] * len(arrays),
         out_specs=out_specs,
         scratch_shapes=[pltpu.SemaphoreType.DMA],
-        compiler_params=pltpu.CompilerParams(vmem_limit_bytes=VMEM_BYTES),
+        compiler_params=pltpu.CompilerParams(vmem_limit_bytes=2 * moved // steps + VMEM_BYTES),
     )(index, *arrays)
 
 
@@ -177,32 +178,63 @@
         start_copy(sources[half:], place, target, sem, middle)
 
 
-def gather_tiles(arrays, index):
-    tile = arrays[0].shape[-1]
-    count = index.shape[0]
-    steps = steps_of(count)
-    each = count // steps
+def fill_tiles(arrays, indices, total, start):
+    tile = arrays[0].shape[-1] if arrays[0].ndim == 3 else TILE
+    counts = [index.shape[0] for index in indices]
+    steps = steps_of(counts)
 
     def kernel(index_ref, *refs):
-        sources, out, sem = refs[:-2], refs[-2], refs[-1]
-        base = pl.program_id(0) * each
-
-        def step(i, carry):
-            start_copy(sources, index_ref[base + i], out.at[i], sem)
-            return carry
-
-        lax.fori_loop(0, each, step, 0)
-        pltpu.make_async_copy(out, out, sem).wait()
-
-    total = sum(array.shape[0] for array in arrays)
+        sources, outs, sem = refs[: len(arrays)], refs[len(arrays) : -1], refs[-1]
+        first = 0
+        for out, count in zip(outs, counts):
+            each = count // steps
+            base = first + pl.program_id(0) * each
+
+            def step(i, carry, out=out, base=base):
+                start(sources, index_ref[base + i], out.at[i], sem)
+                return carry
+
+            lax.fori_loop(0, each, step, 0)
+            first = first + count
+        for out in outs:
+            pltpu.make_async_copy(out, out, sem).wait()
+
     return tile_kernel_call(
         kernel,
-        jnp.clip(index, 0, total - 1),
+        jnp.clip(jnp.concatenate(indices), 0, total - 1),
         arrays,
-        jax.ShapeDtypeStruct((count, tile, tile), arrays[0].dtype),
-        pl.BlockSpec((each, tile, tile), lambda i: (i, 0, 0)),
+        [jax.ShapeDtypeStruct((count, tile, tile), arrays[0].dtype) for count in counts],
+        [pl.BlockSpec((count // steps, tile, tile), lambda i: (i, 0, 0)) for count in counts],
         steps,
     )
+
+
+def gather_tiles(arrays, indices):
+    return fill_tiles(arrays, indices, sum(array.shape[0] for array in arrays), start_copy)
+
+
+def cut_tiles(matrices, indices):
+    row_blocks = matrices[0].shape[0] // TILE
+    widths = [matrix.shape[1] // TILE for matrix in matrices]
+
+    def start(sources, place, target, sem):
+        first = 0
+        for ref, width in zip(sources, widths):
+            size = row_blocks * width
+
+            @pl.when((place >= first) & (place < first + size))
+            def _(ref=ref, first=first, width=width):
+                row = (place - first) // width
+                column = place - first - row * width
+                source = ref.at[
+                    pl.ds(pl.multiple_of(row * TILE, TILE), TILE),
+                    pl.ds(pl.multiple_of(column * TILE, TILE), TILE),
+                ]
+                pltpu.make_async_copy(source, target, sem).start()
+
+            first = first + size
+
+    return fill_tiles(matrices, indices, row_blocks * sum(widths), start)
 
 
 def join_tiles(arrays, index, row_blocks, columns):
@@ -239,49 +271,6 @@
     out_specs = tuple(pl.BlockSpec((each * tile, width * tile), lambda i: (i, 0)) for width in columns)
     return tile_kernel_call(
         kernel, jnp.clip(index, 0, total - 1), arrays, out_shape, out_specs, steps
-    )
-
-
-def cut_tiles(matrices, index, tile):
-    row_blocks = matrices[0].shape[0] // tile
-    widths = [matrix.shape[1] // tile for matrix in matrices]
-    count = index.shape[0]
-    steps = steps_of(count)
-    each = count // steps
-
-    def kernel(index_ref, *refs):
-        sources, out, sem = refs[:-2], refs[-2], refs[-1]
-        base = pl.program_id(0) * each
-
-        def step(i, carry):
-            place = index_ref[base + i]
-            start = 0
-            for ref, width in zip(sources, widths):
-                size = row_blocks * width
-
-                @pl.when((place >= start) & (place < start + size))
-                def _(ref=ref, start=start, width=width):
-                    row = (place - start) // width
-                    column = place - start - row * width
-                    source = ref.at[
-                        pl.ds(pl.multiple_of(row * tile, tile), tile),
-                        pl.ds(pl.multiple_of(column * tile, tile), tile),
-                    ]
-                    pltpu.make_async_copy(source, out.at[i], sem).start()
-
-                start = start + size
-            return carry
-
-        lax.fori_loop(0, each, step, 0)
-        pltpu.make_async_copy(out, out, sem).wait()
-
-    return tile_kernel_call(
-        kernel,
-        jnp.clip(index, 0, row_blocks * sum(widths) - 1),
-        matrices,
-        jax.ShapeDtypeStruct((count, tile, tile), matrices[0].dtype),
-        pl.BlockSpec((each, tile, tile), lambda i: (i, 0, 0)),
-        steps,
     )
 
 
@@ -373,7 +362,7 @@
             pltpu.VMEM((count, tile, tile), jnp.bfloat16),
             pltpu.SemaphoreType.DMA((count // each,)),
         ],
-        compiler_params=pltpu.CompilerParams(vmem_limit_bytes=VMEM_BYTES),
+        compiler_params=pltpu.CompilerParams(vmem_limit_bytes=4 * VMEM_BYTES),
     )(jnp.clip(index, 0, total - 1), *grads, master, first, second, left, right)
 
 
@@ -601,7 +590,7 @@
     )
     master_low = tile_master.astype(bf16)
     masters = [master_low, core_swap(master_low)]
-    ffn_sent = [gather_tiles(masters, ffn_pack[i]) for i in range(chips)]
+    ffn_sent = gather_tiles(masters, [ffn_pack[i] for i in range(chips)])
     small_rows = small_master.shape[0] // 2
     small_half = lax.dynamic_slice_in_dim(small_master, my_core * small_rows, small_rows)
     masters, ffn_sent, chip_rank, owners, own_tokens, own_gains, small_half = (
@@ -636,8 +625,7 @@
         & (chip_slots[1] == jnp.arange(attn_room)[None, :, None]),
         both_slots,
     )
-    attn_sent = gather_tiles(masters, attn_pack.reshape(-1))
-    attn_sent = attn_sent.reshape(seq_size, attn_room, tile, tile)
+    attn_sent = gather_tiles(masters, [attn_pack[i] for i in range(seq_size)])
     seq_view = ffn_to.reshape(seq_size, fsdp_size * mine)
     ffn_rank = count_long(seq_view).reshape(owners.shape)
     def by_chip(value):
@@ -797,12 +785,9 @@
     small_got = core_pair(seq_order(jnp.stack([part[token_end:small_end] for part in parts])))
     small_got = small_got.transpose(1, 0, 2, 3, 4)
     small_table = assemble(small_got.reshape((-1,) + small_master.shape[1:]), row_blocks)
-    attn_kept = gather_tiles(attn_got, attn_keep)
+    (attn_kept,) = gather_tiles(attn_got, [attn_keep])
     ffn_got = ffn_got + [core_swap(value) for value in ffn_got]
-    ffn_kept = [
-        gather_tiles(ffn_got, ffn_keep[:ffn_half]),
-        gather_tiles(ffn_got, ffn_keep[ffn_half:]),
-    ]
+    ffn_kept = gather_tiles(ffn_got, [ffn_keep[:ffn_half], ffn_keep[ffn_half:]])
     ffn_kept, attn_kept = lax.optimization_barrier((ffn_kept, attn_kept))
     ffn_all = [lax.all_gather(value, "seq", axis=0, tiled=True) for value in ffn_kept]
     attn_all = [attn_kept] + [chip_shift(attn_kept, offset) for offset in range(1, chips)]
@@ -937,10 +922,10 @@
     grad_feed = lax.psum_scatter(feed_part, "fsdp", scatter_dimension=0, tiled=True).astype(f32)
     both_grad_w = matmul_outer(feed_low, both_grad_low).astype(bf16)
     down_grad_w = matmul_outer(down_grad_low, hidden_low).astype(bf16)
-    ffn_parts = [
-        cut_tiles([both_grad_w, down_grad_w], index.reshape(-1), tile)
-        for index in (ffn_cut[:, :ffn_half], ffn_cut[:, ffn_half:])
-    ]
+    ffn_parts = cut_tiles(
+        [both_grad_w, down_grad_w],
+        [ffn_cut[:, :ffn_half].reshape(-1), ffn_cut[:, ffn_half:].reshape(-1)],
+    )
     ffn_parts, grad_feed = lax.optimization_barrier((ffn_parts, grad_feed))
     ffn_sums = [
         lax.psum_scatter(value, "seq", scatter_dimension=0, tiled=True) for value in ffn_parts
@@ -986,25 +971,28 @@
     near_place = take_blocks(by_chip(attn_place), near)[:, None, :]
 
     def attn_cut(core):
-        index = pick(
+        return pick(
             (near_key == 2 * my_seq + core)
             & (near_order == jnp.arange(attn_hold)[None, :, None]),
             near_place,
-        )
-        return cut_tiles([first_grad_w, out_grad_w], index.reshape(-1), tile)
-
-    attn_given, attn_own = attn_cut(1 - my_core), attn_cut(my_core)
+        ).reshape(-1)
+
+    attn_given, attn_own = cut_tiles(
+        [first_grad_w, out_grad_w], [attn_cut(1 - my_core), attn_cut(my_core)]
+    )
     attn_given, attn_own, ffn_sums[0] = lax.optimization_barrier(
         (attn_given, attn_own, ffn_sums[0])
     )
     attn_parts = added(attn_own, core_swap(attn_given)).reshape(chips, attn_hold, tile, tile)
     attn_sum = attn_parts[0]
     attn_parts = [attn_parts[offset].astype(bf16) for offset in range(1, chips)]
-    normed_sum = seq_sum(matmul_flip(first_grad_low, w_first), bf16)
-    attn_sum, attn_parts, normed_sum = lax.optimization_barrier((attn_sum, attn_parts, normed_sum))
+    normed_pre = matmul_flip(first_grad_low, w_first)
+    attn_sum, attn_parts, normed_pre = lax.optimization_barrier((attn_sum, attn_parts, normed_pre))
+    normed_sum = seq_sum(normed_pre, bf16)
     for offset in range(1, chips):
         attn_sum = attn_sum + chip_shift(attn_parts[offset - 1], offset).astype(f32)
     attn_sum = attn_sum.astype(bf16)
+    attn_sum, normed_sum = lax.optimization_barrier((attn_sum, normed_sum))
     attn_back = pick(
         (column_slots[3][None, None, :] == (my_seq ^ flips)[:, None, None])
         & (column_slots[0][None, None, :] == my_key)
@@ -1045,13 +1033,12 @@
     late = late.reshape(2, late_count, tile, tile)
     late = lax.dynamic_index_in_dim(late, my_core, 0, False)
     late_index = 2 * ffn_hold + jnp.arange(late_count)
-    ffn_return = [
-        gather_tiles(ffn_sums + [late], jnp.concatenate([ffn_back[i], late_index]))
-        for i in range(chips)
-    ]
+    ffn_return = gather_tiles(
+        ffn_sums + [late], [jnp.concatenate([ffn_back[i], late_index]) for i in range(chips)]
+    )
     ffn_return, attn_sum = lax.optimization_barrier((ffn_return, attn_sum))
     ffn_returned = chip_exchange(ffn_return)
-    attn_returned = seq_exchange([gather_tiles([attn_sum], attn_back[i]) for i in range(seq_size)])
+    attn_returned = seq_exchange(gather_tiles([attn_sum], [attn_back[i] for i in range(seq_size)]))
     attn_returned = attn_returned + [core_swap(value) for value in attn_returned]
     back_size = 2 * chips * return_size
     slot_grad = jnp.where(my_slots[0] >= 0, my_slots[1], back_size + my_slots[2])
@@ -1065,7 +1052,9 @@
             ffn_place,
             jnp.where(attn_to == my_seq, ffn_count + attn_place, ffn_count + attn_count),
         )
-        spread = gather_tiles([parts], index.reshape(-1))
+        spread = jnp.concatenate(
+            [gather_tiles([parts], [rows_of])[0] for rows_of in index.reshape(8, -1)]
+        )
         spread = lax.all_to_all(
             spread.reshape((seq_size * fsdp_size, mine, tile, tile)),
             ("seq", "fsdp"),

time: 1190 us -> 1130 us (0.950)
  starting transfers between devices: 113 us -> 58.4 us
  waiting for transfers between devices: 526 us -> 559 us
  Pallas kernels: 164 us -> 144 us
    ppermute x25, starting transfers between devices: 67 us -> 11.9 us  [core_swap(): return lax.ppermute(value, 'fsdp', [(i, i ^ 1) for i in range(size)])]
    pallas_call x22 -> x10, Pallas kernels: 114 us -> 96 us  [tile_kernel_call(): pl.pallas_call(kernel, grid=(steps,), cost_estimate=pl.CostEstimate(flops...]
    ppermute x18, waiting for transfers between devices: 224 us -> 240 us  [chip_shift(): lax.ppermute(value, 'fsdp', [(i, (i // 2 + offset) % chips * 2 + i % 2) f...]
    ppermute x23, waiting for transfers between devices: 183 us -> 198 us  [seq_swap(): return lax.ppermute(value, 'seq', [(i, i ^ flip) for i in range(size)])]
    unnamed x460 -> x409, local copies, waits for them, and re-layouts: 66.7 us -> 62.6 us
  transfers between devices with their start and end apart: 74 -> 74, of which waited for: 39 -> 41; matrix products, arithmetic and copies ran while one was open for 17% -> 17% of each run, Pallas kernels for 8% -> 7%
where the time goes in v12:
time: 1130 us; the launch traced here: 1110 us
  waiting for transfers between devices  559 us (49%)
  Pallas kernels  144 us (13%)
  local copies, waits for them, and re-layouts  126 us (11%)
  matrix products  98.5 us (9%)
  other arithmetic  86.6 us (8%)
  starting transfers between devices  58.4 us (5%)
  between operations  41.3 us (4%)
    ppermute x18, waiting for transfers between devices, chip_shift(): lax.ppermute(value, 'fsdp', [(i, (i // 2 + offset) % chips * 2 + i % 2) f...  240 us
    ppermute x23, waiting for transfers between devices, seq_swap(): return lax.ppermute(value, 'seq', [(i, i ^ flip) for i in range(size)])  198 us
    pallas_call x10, Pallas kernels, tile_kernel_call(): pl.pallas_call(kernel, grid=(steps,), cost_estimate=pl.CostEstimate(flops...  96 us
    unnamed x409, local copies, waits for them, and re-layouts  62.6 us
    reduce_scatter x1, waiting for transfers between devices, on_device(): lax.psum_scatter(matmul_flip(hidden_low, w_down).astype(bf16), 'fsdp', sc...  48.4 us
    pallas_call x2, Pallas kernels, rotate_update(): pl.pallas_call(kernel, grid=(count // each,), out_shape=(shape, shape, sh...  44.9 us
    dot_general x8, matrix products, matmul(): return jnp.dot(left, right, preferred_element_type=jnp.float32)  34.6 us
    dot_general x8, matrix products, matmul_flip(): lax.dot_general(left, right, (((1,), (1,)), ((), ())), preferred_element_...  33.8 us
  transfers between devices with their start and end apart: 74, of which 41 were waited for; matrix products, arithmetic and copies ran while one was open for 17% of the time, Pallas kernels for 7%

profile of v12, /device:TPU:9, one launch (start us, length us, event | category | flops | bytes accessed | tf_op | source)
XLA Modules:
  0.0 1114.1 jit_solution(3124248058577471449)
XLA Ops:
  72.4 46.0 %collective-permute-done.6.refs_3_ = bf16[40,128,128]{2,1,0:T(8,128)(2,1)} collective-permute-done((bf16[40,128,128]{2,1,0:T(8,128)(2,1)}, bf16[40,128,128]{2,1,0:T(8,128)(2,1)}, u32[]{:S(2)}, u32[]{:S(2)}) %collective-permute-start.6) | collective-permute-done | bytes 1310752 | tf_op jit(solution)/shard_map/ppermute | solution.py:371
  159.3 11.5 %shard_map.261 = (bf16[56,128,128]{2,1,0:T(8,128)(2,1)}, bf16[76,128,128]{2,1,0:T(8,128)(2,1)}) custom-call(s32[132]{0:T(256)S(1)} %broadcast_clamp_fusion.5.index_ref, bf16[37,128,128]{2,1,0:T(8,128)(2,1)S(1)} %copy-done.30, bf16[37,128,128]{2,1,0:T(8,128)(2,1)} %collective-permute-done.1.refs_1_, bf16[37,128,128]{2,1,0:T(8,128)(2,1)} %collective-permute-done.2.refs_2_, ...), custom_call_target="tpu_custom_call" | custom-call | bytes 8650752 | tf_op jit(solution)/shard_map/pallas_call | solution.py:152
  184.1 17.5 %collective-permute-done.11 = bf16[33,128,128]{2,1,0:T(8,128)(2,1)S(1)} collective-permute-done((bf16[33,128,128]{2,1,0:T(8,128)(2,1)S(1)}, bf16[33,128,128]{2,1,0:T(8,128)(2,1)S(1)}, u32[]{:S(2)}, u32[]{:S(2)}) %collective-permute-start.11) | collective-permute-done | bytes 1081376 | tf_op jit(solution)/shard_map/ppermute | solution.py:388
  201.6 66.7 %collective-permute-done.12 = bf16[33,128,128]{2,1,0:T(8,128)(2,1)S(1)} collective-permute-done((bf16[33,128,128]{2,1,0:T(8,128)(2,1)S(1)}, bf16[33,128,128]{2,1,0:T(8,128)(2,1)S(1)}, u32[]{:S(2)}, u32[]{:S(2)}) %collective-permute-start.12) | collective-permute-done | bytes 1081376 | tf_op jit(solution)/shard_map/ppermute | solution.py:388
  278.4 11.2 %conditional.3 = ((bf16[2048,768]{1,0:T(8,128)(2,1)}, bf16[2048,512]{1,0:T(8,128)(2,1)})) conditional(s32[]{:T(128)} %convert_element_type.377, (s32[]{:T(128)}, s32[4,8,116]{2,1,0:T(8,128)S(1)}, s32[4,8,116]{2,1,0:T(8,128)S(1)}, bf16[116,128,128]{2,1,0:T(8,128)(2,1)}) %tuple.42, (s32[160]{0:T(256)S(1)}, bf16[33,128,128]{2,1,0:T(8,128)(2,1)S(1)}, ...), branch_computations={%region_12.14_spmd, %region_14.15_spmd} | conditional | flops 2379392 | bytes 500902304 | solution.py:817
  278.4 10.8 branch_1_fun.2
  328.0 13.8 %collective-permute-done.21 = bf16[128,2048]{1,0:T(8,128)(2,1)S(1)} collective-permute-done((bf16[128,2048]{1,0:T(8,128)(2,1)}, bf16[128,2048]{1,0:T(8,128)(2,1)S(1)}, u32[]{:S(2)}, u32[]{:S(2)}) %collective-permute-start.21) | collective-permute-done | bytes 524320 | tf_op jit(solution)/shard_map/ppermute | solution.py:371
  341.8 12.6 %collective-permute-done.20 = bf16[128,2048]{1,0:T(8,128)(2,1)} collective-permute-done((bf16[128,2048]{1,0:T(8,128)(2,1)}, bf16[128,2048]{1,0:T(8,128)(2,1)}, u32[]{:S(2)}, u32[]{:S(2)}) %collective-permute-start.20) | collective-permute-done | bytes 524320 | tf_op jit(solution)/shard_map/ppermute | solution.py:371
  369.5 10.5 all-gather.9.cloned.1.call-done
  380.1 14.2 %conditional.4 = ((bf16[2048,2048]{1,0:T(8,128)(2,1)}, bf16[2048,1024]{1,0:T(8,128)(2,1)})) conditional(s32[]{:T(128)} %convert_element_type.377, (s32[]{:T(128)}, s32[4,8,116]{2,1,0:T(8,128)S(1)}, s32[4,8,116]{2,1,0:T(8,128)S(1)}, bf16[116,128,128]{2,1,0:T(8,128)(2,1)}) %tuple.245, (s32[384]{0:T(512)S(1)}, bf16[224,128,128]{2,1,0:T(8,128)(2,1)}, ...), branch_computations={%region_24.26_spmd, %region_26.27_spmd} | conditional | flops 5705344 | bytes 515585056 | solution.py:817
  380.3 14.0 %branch_1_fun.3 = (bf16[2048,2048]{1,0:T(8,128)(2,1)}, bf16[2048,1024]{1,0:T(8,128)(2,1)}) custom-call(s32[384]{0:T(512)S(1)} %broadcast_clamp_fusion.3.index_ref, bf16[224,128,128]{2,1,0:T(8,128)(2,1)} %get-tuple-element.81.refs_0_, bf16[304,128,128]{2,1,0:T(8,128)(2,1)} %get-tuple-element.82.refs_1_), custom_call_target="tpu_custom_call" | custom-call | bytes 25165824 | tf_op jit(solution)/shard_map/cond/branch_1_fun/pallas_call | solution.py:152
  394.3 33.1 %all-gather.7.cloned.1.call-done = bf16[1024,2048]{1,0:T(8,128)(2,1)} async-done(((bf16[128,2048]{1,0:T(8,128)(2,1)}), bf16[1024,2048]{1,0:T(8,128)(2,1)}) %all-gather.7.cloned.1.call-update) | async-done | bytes 4194320 | tf_op jit(solution)/shard_map/all_gather | solution.py:882
  427.3 12.5 %fusion.265 = f32[1024,2048]{1,0:T(8,128)S(1)} fusion(bf16[1024,2048]{1,0:T(8,128)(2,1)} %all-gather.7.cloned.1.call-done, bf16[2048,2048]{1,0:T(8,128)(2,1)} %get-tuple-element.274), kind=kOutput, calls=%fused_computation.730 | convolution fusion | flops 8589934592 | bytes 20971520 | tf_op jit(solution)/shard_map/dot_general | solution.py:62
  451.5 48.4 %reduce-scatter.5.cloned.1.call-done = bf16[128,2048]{1,0:T(8,128)(2,1)} async-done(((bf16[1024,2048]{1,0:T(8,128)(2,1)}), bf16[128,2048]{1,0:T(8,128)(2,1)}) %reduce-scatter.5.cloned.1.call-update) | async-done | bytes 524304 | tf_op jit(solution)/shard_map/reduce_scatter | solution.py:891
  567.2 12.1 %fusion.13 = (bf16[1024,1024]{1,0:T(8,128)(2,1)S(1)}, bf16[1024,1024]{1,0:T(8,128)(2,1)S(1)}) fusion(f32[1024,2048]{1,0:T(8,128)} %copy-done.61, bf16[1024,2048]{1,0:T(8,128)(2,1)} %all-gather.11.cloned.1.call-done, bf16[2048,1024]{1,0:T(8,128)(2,1)} %get-tuple-element.275), kind=kOutput, calls=%fused_computation.53 | convolution fusion | flops 4320133120 | bytes 20971520 | tf_op jit(solution)/shard_map/dot_general | solution.py:62
  581.3 12.6 %convolution_convert_fusion.1 = bf16[1024,2048]{1,0:T(8,128)(2,1)} fusion(bf16[2048,2048]{1,0:T(8,128)(2,1)} %get-tuple-element.274, bf16[1024,1024]{1,0:T(8,128)(2,1)S(1)} %get-tuple-element.443, bf16[1024,1024]{1,0:T(8,128)(2,1)S(1)} %get-tuple-element.442), kind=kOutput, calls=%fused_computation.60 | convolution fusion | flops 8600420352 | bytes 16777216 | tf_op jit(solution)/shard_map/dot_general | solution.py:66
  604.7 9.4 convolution_convert_fusion.refs_0_
  617.3 20.0 %shard_map.263 = (bf16[224,128,128]{2,1,0:T(8,128)(2,1)S(1)}, bf16[304,128,128]{2,1,0:T(8,128)(2,1)S(1)}) custom-call(s32[528]{0:T(1024)S(1)} %add_clamp_fusion.index_ref, bf16[2048,2048]{1,0:T(8,128)(2,1)S(1)} %convolution_convert_fusion.refs_0_, bf16[2048,1024]{1,0:T(8,128)(2,1)S(1)} %convolution_convert_fusion.2.refs_1_), custom_call_target="tpu_custom_call" | custom-call | bytes 34603008 | tf_op jit(solution)/shard_map/pallas_call | solution.py:152
  657.2 21.2 %collective-permute-done.36 = bf16[128,2048]{1,0:T(8,128)(2,1)S(1)} collective-permute-done((bf16[128,2048]{1,0:T(8,128)(2,1)S(1)}, bf16[128,2048]{1,0:T(8,128)(2,1)S(1)}, u32[]{:S(2)}, u32[]{:S(2)}) %collective-permute-start.36) | collective-permute-done | bytes 524320 | tf_op jit(solution)/shard_map/ppermute | solution.py:371
  678.4 11.6 %collective-permute-done.35 = bf16[128,2048]{1,0:T(8,128)(2,1)S(1)} collective-permute-done((bf16[128,2048]{1,0:T(8,128)(2,1)S(1)}, bf16[128,2048]{1,0:T(8,128)(2,1)S(1)}, u32[]{:S(2)}, u32[]{:S(2)}) %collective-permute-start.35) | collective-permute-done | bytes 524320 | tf_op jit(solution)/shard_map/ppermute | solution.py:371
  690.0 10.4 collective-permute-done.34
  729.7 10.2 shard_map.264
  783.5 18.7 %collective-permute-done.44 = bf16[128,2048]{1,0:T(8,128)(2,1)S(1)} collective-permute-done((bf16[128,2048]{1,0:T(8,128)(2,1)S(1)}, bf16[128,2048]{1,0:T(8,128)(2,1)S(1)}, u32[]{:S(2)}, u32[]{:S(2)}) %collective-permute-start.44) | collective-permute-done | bytes 524320 | tf_op jit(solution)/shard_map/ppermute | solution.py:371
  806.8 9.6 collective-permute-done.43
  816.4 10.7 collective-permute-done.42
  828.9 21.0 %collective-permute-done.40 = bf16[33,128,128]{2,1,0:T(8,128)(2,1)} collective-permute-done((bf16[33,128,128]{2,1,0:T(8,128)(2,1)}, bf16[33,128,128]{2,1,0:T(8,128)(2,1)}, u32[]{:S(2)}, u32[]{:S(2)}) %collective-permute-start.40) | collective-permute-done | bytes 1081376 | tf_op jit(solution)/shard_map/ppermute | solution.py:388
  849.9 23.2 %collective-permute-done.39 = bf16[33,128,128]{2,1,0:T(8,128)(2,1)} collective-permute-done((bf16[33,128,128]{2,1,0:T(8,128)(2,1)}, bf16[33,128,128]{2,1,0:T(8,128)(2,1)}, u32[]{:S(2)}, u32[]{:S(2)}) %collective-permute-start.39) | collective-permute-done | bytes 1081376 | tf_op jit(solution)/shard_map/ppermute | solution.py:388
  906.3 12.0 %shard_map.265 = (bf16[40,128,128]{2,1,0:T(8,128)(2,1)S(1)}, bf16[40,128,128]{2,1,0:T(8,128)(2,1)S(1)}, bf16[40,128,128]{2,1,0:T(8,128)(2,1)S(1)}, bf16[40,128,128]{2,1,0:T(8,128)(2,1)}) custom-call(s32[160]{0:T(256)S(1)} %broadcast_clamp_fusion.4.index_ref, bf16[56,128,128]{2,1,0:T(8,128)(2,1)S(1)} %copy-done.18, bf16[76,128,128]{2,1,0:T(8,128)(2,1)S(1)} %copy-done.16, ...), custom_call_target="tpu_custom_call" | custom-call | bytes 10485760 | tf_op jit(solution)/shard_map/pallas_call | solution.py:152
  929.2 9.6 collective-permute-done.58.refs_9_
  940.0 65.7 %collective-permute-done.51.refs_1_ = bf16[40,128,128]{2,1,0:T(8,128)(2,1)S(1)} collective-permute-done((bf16[40,128,128]{2,1,0:T(8,128)(2,1)S(1)}, bf16[40,128,128]{2,1,0:T(8,128)(2,1)S(1)}, u32[]{:S(2)}, u32[]{:S(2)}) %collective-permute-start.51) | collective-permute-done | bytes 1310752 | tf_op jit(solution)/shard_map/ppermute | solution.py:388
  1006.9 27.0 %collective-permute-done.52.refs_2_ = bf16[40,128,128]{2,1,0:T(8,128)(2,1)S(1)} collective-permute-done((bf16[40,128,128]{2,1,0:T(8,128)(2,1)S(1)}, bf16[40,128,128]{2,1,0:T(8,128)(2,1)S(1)}, u32[]{:S(2)}, u32[]{:S(2)}) %collective-permute-start.52) | collective-permute-done | bytes 1310752 | tf_op jit(solution)/shard_map/ppermute | solution.py:388
  1069.1 37.9 %shard_map.267 = (f32[116,128,128]{2,1,0:T(8,128)}, f32[116,128,128]{2,1,0:T(8,128)}, f32[116,128,128]{2,1,0:T(8,128)}) custom-call(s32[116]{0:T(128)S(1)} %fusion.206.index_ref, bf16[40,128,128]{2,1,0:T(8,128)(2,1)S(1)} %copy-done.20, bf16[40,128,128]{2,1,0:T(8,128)(2,1)S(1)} %copy-done.22, bf16[40,128,128]{2,1,0:T(8,128)(2,1)S(1)} %copy-done.24, ...), custom_call_target="tpu_custom_call" | custom-call | tf_op jit(solution)/shard_map/pallas_call | solution.py:353
  (880 shorter events, 434.7 us)
Async XLA Ops:
  7.2 271.2 %all-gather.5.cloned.1.call-start = ((), (), s32[]{:S(2)}) async-start(), calls=%async_computation.7 | async-start | bytes 9175040 | tf_op jit(solution)/shard_map/all_gather | solution.py:792
  45.7 99.9 %collective-permute-start.1 = (bf16[37,128,128]{2,1,0:T(8,128)(2,1)}, bf16[37,128,128]{2,1,0:T(8,128)(2,1)}, u32[]{:S(2)}, u32[]{:S(2)}) collective-permute-start(bf16[37,128,128]{2,1,0:T(8,128)(2,1)} %get-tuple-element.220), channel_id=1, source_target_pairs={{0,2},{1,3},{2,4},{3,5},{4,6},{5,7},{6,0},{7,1},{8,10},{9,11},{10,... | collective-permute-start | bytes 3637256 | tf_op jit(solution)/shard_map/ppermute | solution.py:388
  46.8 102.8 %collective-permute-start.2 = (bf16[37,128,128]{2,1,0:T(8,128)(2,1)}, bf16[37,128,128]{2,1,0:T(8,128)(2,1)}, u32[]{:S(2)}, u32[]{:S(2)}) collective-permute-start(bf16[37,128,128]{2,1,0:T(8,128)(2,1)} %get-tuple-element.221), channel_id=1, source_target_pairs={{0,4},{1,5},{2,6},{3,7},{4,0},{5,1},{6,2},{7,3},{8,12},{9,13},{10,... | collective-permute-start | bytes 3637256 | tf_op jit(solution)/shard_map/ppermute | solution.py:388
  60.2 61.5 %collective-permute-start.4 = (bf16[40,128,128]{2,1,0:T(8,128)(2,1)}, bf16[40,128,128]{2,1,0:T(8,128)(2,1)S(1)}, u32[]{:S(2)}, u32[]{:S(2)}) collective-permute-start(bf16[40,128,128]{2,1,0:T(8,128)(2,1)} %get-tuple-element.481), channel_id=1, source_target_pairs={{0,8},{8,0},{16,24},{24,16},{1,9},{9,1},{17,25},{25,17},{2,10},{10... | collective-permute-start | bytes 3932168 | tf_op jit(solution)/shard_map/ppermute | solution.py:371
  61.0 59.9 %collective-permute-start.5 = (bf16[40,128,128]{2,1,0:T(8,128)(2,1)}, bf16[40,128,128]{2,1,0:T(8,128)(2,1)}, u32[]{:S(2)}, u32[]{:S(2)}) collective-permute-start(bf16[40,128,128]{2,1,0:T(8,128)(2,1)} %get-tuple-element.480), channel_id=1, source_target_pairs={{0,16},{8,24},{16,0},{24,8},{1,17},{9,25},{17,1},{25,9},{2,18},{10... | collective-permute-start | bytes 3932168 | tf_op jit(solution)/shard_map/ppermute | solution.py:371
  62.4 56.0 %collective-permute-start.6 = (bf16[40,128,128]{2,1,0:T(8,128)(2,1)}, bf16[40,128,128]{2,1,0:T(8,128)(2,1)}, u32[]{:S(2)}, u32[]{:S(2)}) collective-permute-start(bf16[40,128,128]{2,1,0:T(8,128)(2,1)} %get-tuple-element.479), channel_id=1, source_target_pairs={{0,24},{8,16},{16,8},{24,0},{1,25},{9,17},{17,9},{25,1},{2,26},{10... | collective-permute-start | bytes 3932168 | tf_op jit(solution)/shard_map/ppermute | solution.py:371
  170.8 209.2 %all-gather.9.cloned.1.call-start = ((), (), s32[]{:S(2)}) async-start(), calls=%async_computation.9 | async-start | bytes 12451840 | tf_op jit(solution)/shard_map/all_gather | solution.py:792
  171.6 255.7 %all-gather.7.cloned.1.call-start = ((), (), s32[]{:S(2)}) async-start(), calls=%async_computation.8 | async-start | bytes 4718592 | tf_op jit(solution)/shard_map/all_gather | solution.py:882
  175.6 92.6 %collective-permute-start.12 = (bf16[33,128,128]{2,1,0:T(8,128)(2,1)S(1)}, bf16[33,128,128]{2,1,0:T(8,128)(2,1)S(1)}, u32[]{:S(2)}, u32[]{:S(2)}) collective-permute-start(bf16[33,128,128]{2,1,0:T(8,128)(2,1)S(1)} %copy-done.80), channel_id=1, source_target_pairs={{0,4},{1,5},{2,6},{3,7},{4,0},{5,1},{6,2},{7,3},{8,12},{9,13},{10,... | collective-permute-start | bytes 3244040 | tf_op jit(solution)/shard_map/ppermute | solution.py:388
  178.1 94.1 %collective-permute-start.13 = (bf16[33,128,128]{2,1,0:T(8,128)(2,1)S(1)}, bf16[33,128,128]{2,1,0:T(8,128)(2,1)S(1)}, u32[]{:S(2)}, u32[]{:S(2)}) collective-permute-start(bf16[33,128,128]{2,1,0:T(8,128)(2,1)S(1)} %copy-done.80), channel_id=1, source_target_pairs={{0,6},{1,7},{2,0},{3,1},{4,2},{5,3},{6,4},{7,5},{8,14},{9,15},{10,... | collective-permute-start | bytes 3244040 | tf_op jit(solution)/shard_map/ppermute | solution.py:388
  183.3 92.7 %collective-permute-start.14 = (bf16[33,128,128]{2,1,0:T(8,128)(2,1)S(1)}, bf16[33,128,128]{2,1,0:T(8,128)(2,1)S(1)}, u32[]{:S(2)}, u32[]{:S(2)}) collective-permute-start(bf16[33,128,128]{2,1,0:T(8,128)(2,1)S(1)} %copy-done.80), channel_id=1, source_target_pairs={{0,1},{1,0},{2,3},{3,2},{4,5},{5,4},{6,7},{7,6},{8,9},{9,8},{10,11... | collective-permute-start | bytes 3244040 | tf_op jit(solution)/shard_map/ppermute | solution.py:382
  201.6 74.4 %collective-permute-start.15 = (bf16[33,128,128]{2,1,0:T(8,128)(2,1)S(1)}, bf16[33,128,128]{2,1,0:T(8,128)(2,1)S(1)}, u32[]{:S(2)}, u32[]{:S(2)}) collective-permute-start(bf16[33,128,128]{2,1,0:T(8,128)(2,1)S(1)} %collective-permute-done.11), channel_id=1, source_target_pairs={{0,1},{1,0},{2,3},{3,2},{4,5},{5,4},{6,7},{7,6},{8,9},{9,8},{10,11... | collective-permute-start | bytes 3244040 | tf_op jit(solution)/shard_map/ppermute | solution.py:382
  275.7 44.3 %collective-permute-start.22 = (bf16[4,10,128,128]{3,2,1,0:T(8,128)(2,1)}, bf16[4,10,128,128]{3,2,1,0:T(8,128)(2,1)}, u32[]{:S(2)}, u32[]{:S(2)}) collective-permute-start(bf16[4,10,128,128]{3,2,1,0:T(8,128)(2,1)} %get-tuple-element.463), channel_id=1, source_target_pairs={{0,1},{1,0},{2,3},{3,2},{4,5},{5,4},{6,7},{7,6},{8,9},{9,8},{10,11... | collective-permute-start | bytes 3932168 | tf_op jit(solution)/shard_map/ppermute | solution.py:382
  318.9 35.5 %collective-permute-start.20 = (bf16[128,2048]{1,0:T(8,128)(2,1)}, bf16[128,2048]{1,0:T(8,128)(2,1)}, u32[]{:S(2)}, u32[]{:S(2)}) collective-permute-start(bf16[128,2048]{1,0:T(8,128)(2,1)} %get-tuple-element.457), channel_id=1, source_target_pairs={{0,16},{8,24},{16,0},{24,8},{1,17},{9,25},{17,1},{25,9},{2,18},{10... | collective-permute-start | bytes 1572872 | tf_op jit(solution)/shard_map/ppermute | solution.py:371
  319.3 44.3 %collective-permute-start.19 = (bf16[128,2048]{1,0:T(8,128)(2,1)}, bf16[128,2048]{1,0:T(8,128)(2,1)}, u32[]{:S(2)}, u32[]{:S(2)}) collective-permute-start(bf16[128,2048]{1,0:T(8,128)(2,1)} %get-tuple-element.455), channel_id=1, source_target_pairs={{0,8},{8,0},{16,24},{24,16},{1,9},{9,1},{17,25},{25,17},{2,10},{10... | collective-permute-start | bytes 1572872 | tf_op jit(solution)/shard_map/ppermute | solution.py:371
  369.5 130.4 %reduce-scatter.5.cloned.1.call-start = ((), (), s32[]{:S(2)}) async-start(), calls=%async_computation.10 | async-start | bytes 4718592 | tf_op jit(solution)/shard_map/reduce_scatter | solution.py:891
  451.5 115.7 %all-gather.11.cloned.1.call-start = ((), (), s32[]{:S(2)}) async-start(), calls=%async_computation.11 | async-start | bytes 4718592 | tf_op jit(solution)/shard_map/all_gather | solution.py:912
  508.7 135.4 %reduce-scatter.7.cloned.1.call-start = ((), (), s32[]{:S(2)}) async-start(), calls=%async_computation.12 | async-start | bytes 4718592 | tf_op jit(solution)/shard_map/reduce_scatter | solution.py:922
  593.9 159.4 %reduce-scatter.9.cloned.1.call-start = ((), (), s32[]{:S(2)}) async-start(), calls=%async_computation.13 | async-start | bytes 9175040 | tf_op jit(solution)/shard_map/reduce_scatter | solution.py:931
  646.4 250.5 %reduce-scatter.11.cloned.1.call-start = ((), (), s32[]{:S(2)}) async-start(), calls=%async_computation.14 | async-start | bytes 12451840 | tf_op jit(solution)/shard_map/reduce_scatter | solution.py:931
  654.1 35.9 %collective-permute-start.35 = (bf16[128,2048]{1,0:T(8,128)(2,1)S(1)}, bf16[128,2048]{1,0:T(8,128)(2,1)S(1)}, u32[]{:S(2)}, u32[]{:S(2)}) collective-permute-start(bf16[128,2048]{1,0:T(8,128)(2,1)S(1)} %get-tuple-element.474), channel_id=1, source_target_pairs={{0,16},{8,24},{16,0},{24,8},{1,17},{9,25},{17,1},{25,9},{2,18},{10... | collective-permute-start | bytes 1572872 | tf_op jit(solution)/shard_map/ppermute | solution.py:371
  655.0 45.4 %collective-permute-start.34 = (bf16[128,2048]{1,0:T(8,128)(2,1)S(1)}, bf16[128,2048]{1,0:T(8,128)(2,1)S(1)}, u32[]{:S(2)}, u32[]{:S(2)}) collective-permute-start(bf16[128,2048]{1,0:T(8,128)(2,1)S(1)} %get-tuple-element.474), channel_id=1, source_target_pairs={{0,8},{8,0},{16,24},{24,16},{1,9},{9,1},{17,25},{25,17},{2,10},{10... | collective-permute-start | bytes 1572872 | tf_op jit(solution)/shard_map/ppermute | solution.py:371
  777.9 51.0 %collective-permute-start.41 = (bf16[33,128,128]{2,1,0:T(8,128)(2,1)}, bf16[33,128,128]{2,1,0:T(8,128)(2,1)}, u32[]{:S(2)}, u32[]{:S(2)}) collective-permute-start(bf16[33,128,128]{2,1,0:T(8,128)(2,1)} %get-tuple-element.290), channel_id=1, source_target_pairs={{0,6},{1,7},{2,0},{3,1},{4,2},{5,3},{6,4},{7,5},{8,14},{9,15},{10,... | collective-permute-start | bytes 3244040 | tf_op jit(solution)/shard_map/ppermute | solution.py:388
  778.2 71.7 %collective-permute-start.40 = (bf16[33,128,128]{2,1,0:T(8,128)(2,1)}, bf16[33,128,128]{2,1,0:T(8,128)(2,1)}, u32[]{:S(2)}, u32[]{:S(2)}) collective-permute-start(bf16[33,128,128]{2,1,0:T(8,128)(2,1)} %get-tuple-element.289), channel_id=1, source_target_pairs={{0,4},{1,5},{2,6},{3,7},{4,0},{5,1},{6,2},{7,3},{8,12},{9,13},{10,... | collective-permute-start | bytes 3244040 | tf_op jit(solution)/shard_map/ppermute | solution.py:388
  780.4 92.7 %collective-permute-start.39 = (bf16[33,128,128]{2,1,0:T(8,128)(2,1)}, bf16[33,128,128]{2,1,0:T(8,128)(2,1)}, u32[]{:S(2)}, u32[]{:S(2)}) collective-permute-start(bf16[33,128,128]{2,1,0:T(8,128)(2,1)} %get-tuple-element.288), channel_id=1, source_target_pairs={{0,2},{1,3},{2,4},{3,5},{4,6},{5,7},{6,0},{7,1},{8,10},{9,11},{10,... | collective-permute-start | bytes 3244040 | tf_op jit(solution)/shard_map/ppermute | solution.py:388
  782.5 33.9 %collective-permute-start.43 = (bf16[128,2048]{1,0:T(8,128)(2,1)}, bf16[128,2048]{1,0:T(8,128)(2,1)}, u32[]{:S(2)}, u32[]{:S(2)}) collective-permute-start(bf16[128,2048]{1,0:T(8,128)(2,1)} %get-tuple-element.451), channel_id=1, source_target_pairs={{0,16},{8,24},{16,0},{24,8},{1,17},{9,25},{17,1},{25,9},{2,18},{10... | collective-permute-start | bytes 1572872 | tf_op jit(solution)/shard_map/ppermute | solution.py:371
  919.4 86.3 %collective-permute-start.51 = (bf16[40,128,128]{2,1,0:T(8,128)(2,1)S(1)}, bf16[40,128,128]{2,1,0:T(8,128)(2,1)S(1)}, u32[]{:S(2)}, u32[]{:S(2)}) collective-permute-start(bf16[40,128,128]{2,1,0:T(8,128)(2,1)S(1)} %get-tuple-element.304), channel_id=1, source_target_pairs={{0,2},{1,3},{2,4},{3,5},{4,6},{5,7},{6,0},{7,1},{8,10},{9,11},{10,... | collective-permute-start | bytes 3932168 | tf_op jit(solution)/shard_map/ppermute | solution.py:388
  921.4 112.5 %collective-permute-start.52 = (bf16[40,128,128]{2,1,0:T(8,128)(2,1)S(1)}, bf16[40,128,128]{2,1,0:T(8,128)(2,1)S(1)}, u32[]{:S(2)}, u32[]{:S(2)}) collective-permute-start(bf16[40,128,128]{2,1,0:T(8,128)(2,1)S(1)} %get-tuple-element.305), channel_id=1, source_target_pairs={{0,4},{1,5},{2,6},{3,7},{4,0},{5,1},{6,2},{7,3},{8,12},{9,13},{10,... | collective-permute-start | bytes 3932168 | tf_op jit(solution)/shard_map/ppermute | solution.py:388
  922.2 116.0 %collective-permute-start.53 = (bf16[40,128,128]{2,1,0:T(8,128)(2,1)}, bf16[40,128,128]{2,1,0:T(8,128)(2,1)}, u32[]{:S(2)}, u32[]{:S(2)}) collective-permute-start(bf16[40,128,128]{2,1,0:T(8,128)(2,1)} %get-tuple-element.306), channel_id=1, source_target_pairs={{0,6},{1,7},{2,0},{3,1},{4,2},{5,3},{6,4},{7,5},{8,14},{9,15},{10,... | collective-permute-start | bytes 3932168 | tf_op jit(solution)/shard_map/ppermute | solution.py:388
  929.2 109.7 %collective-permute-start.59 = (bf16[13,128,128]{2,1,0:T(8,128)(2,1)}, bf16[13,128,128]{2,1,0:T(8,128)(2,1)}, u32[]{:S(2)}, u32[]{:S(2)}) collective-permute-start(bf16[13,128,128]{2,1,0:T(8,128)(2,1)} %get-tuple-element.314), channel_id=1, source_target_pairs={{0,16},{8,24},{16,0},{24,8},{1,17},{9,25},{17,1},{25,9},{2,18},{10... | collective-permute-start | bytes 1277960 | tf_op jit(solution)/shard_map/ppermute | solution.py:371
  938.9 100.2 %collective-permute-start.60 = (bf16[13,128,128]{2,1,0:T(8,128)(2,1)}, bf16[13,128,128]{2,1,0:T(8,128)(2,1)}, u32[]{:S(2)}, u32[]{:S(2)}) collective-permute-start(bf16[13,128,128]{2,1,0:T(8,128)(2,1)} %get-tuple-element.315), channel_id=1, source_target_pairs={{0,24},{8,16},{16,8},{24,0},{1,25},{9,17},{17,9},{25,1},{2,26},{10... | collective-permute-start | bytes 1277960 | tf_op jit(solution)/shard_map/ppermute | solution.py:371
  1005.7 33.8 %collective-permute-start.61 = (bf16[13,128,128]{2,1,0:T(8,128)(2,1)}, bf16[13,128,128]{2,1,0:T(8,128)(2,1)}, u32[]{:S(2)}, u32[]{:S(2)}) collective-permute-start(bf16[13,128,128]{2,1,0:T(8,128)(2,1)} %get-tuple-element.312.refs_8_), channel_id=1, source_target_pairs={{0,1},{1,0},{2,3},{3,2},{4,5},{5,4},{6,7},{7,6},{8,9},{9,8},{10,11... | collective-permute-start | bytes 1277960 | tf_op jit(solution)/shard_map/ppermute | solution.py:382
  (242 other events, 4097.3 us)
Sparse Core Ops, SparseCore 0:
  171.0 78.0 all-gather.4
  250.9 129.0 all-gather.8
  382.2 45.0 all-gather.6
  451.6 48.2 reduce-scatter.4
  508.8 52.9 all-gather.10
  594.0 48.3 reduce-scatter.6
  646.5 106.7 reduce-scatter.8
  756.4 121.6 reduce-scatter.10

commit v13 on v12

--- a/solution.py
+++ b/solution.py
@@ -354,6 +354,9 @@
         kernel,
         grid=(count // each,),
         out_shape=(shape, shape, shape),
+        cost_estimate=pl.CostEstimate(
+            flops=count * 22 * tile**3, transcendentals=0, bytes_accessed=count * tile**2 * 34
+        ),
         in_specs=[pl.BlockSpec(memory_space=pltpu.SMEM)]
         + [pl.BlockSpec(memory_space=pl.ANY)] * len(grads)
         + [spec] * 5,
@@ -520,9 +523,10 @@
     attn_hold = (room(attn_count, 1.0 / chips) + 1) // 2 + 1
     ffn_room = (room(2 * mine, ffn_share / chips) + 1) // 2
     both_count = row_blocks * ffn_first
-    ffn_hold = (room(ffn_count, 1.0 / seq_size) + 3) // 4 * 4
-    ffn_half = ffn_hold * 3 // 7 // 4 * 4
-    ffn_rest = ffn_hold - ffn_half
+    near_hold = (room(2 * mine, ffn_share / fsdp_size) + 3) // 4 * 4
+    far_hold = (room(ffn_count * (1.0 - 1.0 / chips), 1.0 / seq_size) + 3) // 4 * 4
+    far_half = far_hold * 3 // 7 // 4 * 4
+    far_rest = far_hold - far_half
 
     def tile_places(owner):
         row = owner // columns
@@ -580,9 +584,17 @@
     ffn_chip = jnp.where(ffn_to < 0, -1, ffn_to // 2)
     chip_view = ffn_chip.reshape(seq_size, chips, 2 * mine)
     chip_rank = count_earlier(chip_view, chip_view >= 0).reshape(owners.shape)
+    near_view = jnp.where(slot_chip == ffn_chip, ffn_to, -1).reshape(chip_view.shape)
+    near_rank = count_earlier(near_view, near_view >= 0).reshape(owners.shape)
     ffn_slots = lax.dynamic_slice(
-        jnp.stack([ffn_chip, chip_rank]), (0, my_seq, 2 * my_chip, 0), (2, 1, 2, mine)
-    ).reshape(2, 1, 1, 2 * mine)
+        jnp.stack([ffn_chip, chip_rank, near_view.reshape(owners.shape), near_rank]),
+        (0, my_seq, 2 * my_chip, 0),
+        (4, 1, 2, mine),
+    ).reshape(4, 1, 1, 2 * mine)
+    near_keep = pick(
+        (ffn_slots[2][0] == my_fsdp) & (ffn_slots[3][0] == jnp.arange(near_hold)[:, None]),
+        both_slots,
+    )
     ffn_pack = pick(
         (ffn_slots[0] == ((my_chip + shifts) % chips)[:, None, None])
         & (ffn_slots[1] == (my_core * ffn_room + jnp.arange(ffn_room))[None, :, None]),
@@ -590,15 +602,19 @@
     )
     master_low = tile_master.astype(bf16)
     masters = [master_low, core_swap(master_low)]
-    ffn_sent = gather_tiles(masters, [ffn_pack[i] for i in range(chips)])
+    *ffn_sent, near_kept = gather_tiles(
+        masters, [ffn_pack[i] for i in range(1, chips)] + [near_keep]
+    )
     small_rows = small_master.shape[0] // 2
     small_half = lax.dynamic_slice_in_dim(small_master, my_core * small_rows, small_rows)
-    masters, ffn_sent, chip_rank, owners, own_tokens, own_gains, small_half = (
+    masters, ffn_sent, near_kept, chip_rank, near_rank, owners, own_tokens, own_gains, small_half = (
         lax.optimization_barrier(
             (
                 masters,
                 ffn_sent,
+                near_kept,
                 chip_rank,
+                near_rank,
                 owners,
                 tokens[0],
                 gains.astype(bf16),
@@ -606,7 +622,8 @@
             )
         )
     )
-    ffn_got = chip_exchange(ffn_sent)
+    ffn_got = [chip_shift(value, i + 1) for i, value in enumerate(ffn_sent)]
+    near_all = lax.all_gather(near_kept, "seq", axis=0, tiled=True)
 
     ffn_to, ffn_place, attn_to, attn_place = tile_places(owners)
     ffn_chip = jnp.where(ffn_to < 0, -1, ffn_to // 2)
@@ -626,8 +643,10 @@
         both_slots,
     )
     attn_sent = gather_tiles(masters, [attn_pack[i] for i in range(seq_size)])
-    seq_view = ffn_to.reshape(seq_size, fsdp_size * mine)
-    ffn_rank = count_long(seq_view).reshape(owners.shape)
+    is_near = slot_chip == ffn_chip
+    near_key = jnp.where(is_near, ffn_to, -1)
+    far_key = jnp.where(is_near, -1, ffn_to)
+    far_rank = count_long(far_key.reshape(seq_size, fsdp_size * mine)).reshape(owners.shape)
     def by_chip(value):
         value = value.reshape(seq_size, chips, 2 * mine).transpose(1, 0, 2)
         return value.reshape(chips, seq_size * 2 * mine)
@@ -641,24 +660,26 @@
         jnp.where(
             ffn_to < 0,
             (attn_rank < attn_room) & (attn_order < attn_hold),
-            (chip_rank < 2 * ffn_room) & (ffn_rank < ffn_hold),
+            jnp.where(
+                is_near, near_rank < near_hold, (chip_rank < 2 * ffn_room) & (far_rank < far_hold)
+            ),
         )
     )
-    half = chips * ffn_room
-    rows_late = 2 * RANK * row_blocks // seq_size
     rank_core = chip_rank // ffn_room
     rank_local = chip_rank % ffn_room
     out_place = (
-        jnp.where(rank_core == my_core, 0, half)
-        + (my_chip - slot_chip) % chips * ffn_room
+        jnp.where(rank_core == my_core, 0, (chips - 1) * ffn_room)
+        + ((my_chip - slot_chip) % chips - 1) * ffn_room
         + rank_local
     )
-    late_count = -(-(rows_late + own_gains.shape[0] // tile) // (2 * tile))
-    return_size = ffn_room + late_count
-    back_place = (
-        jnp.where(rank_core == my_core, 0, chips * return_size)
-        + (my_chip - ffn_chip) % chips * return_size
-        + rank_local
+    near_start = 2 * (chips - 1) * ffn_room
+    back_size = near_start + 2 * near_hold
+    back_place = jnp.where(
+        is_near,
+        near_start + jnp.where(ffn_to == my_fsdp, 0, near_hold) + near_rank,
+        jnp.where(rank_core == my_core, 0, (chips - 1) * ffn_room)
+        + ((my_chip - ffn_chip) % chips - 1) * ffn_room
+        + rank_local,
     )
     attn_back_place = (
         jnp.where(attn_core == my_core, 0, seq_size * attn_room)
@@ -671,8 +692,8 @@
     seq_slots = lax.dynamic_slice(
         jnp.stack(
             [
-                ffn_to,
-                ffn_rank,
+                far_key,
+                far_rank,
                 ffn_chip,
                 out_place,
                 chip_rank,
@@ -709,30 +730,38 @@
         ).reshape(1, -1),
     )
     ffn_keep = pick(
-        (seq_slots[0][None, :] == my_fsdp) & (seq_slots[1][None, :] == jnp.arange(ffn_hold)[:, None]),
+        (seq_slots[0][None, :] == my_fsdp) & (seq_slots[1][None, :] == jnp.arange(far_hold)[:, None]),
         seq_slots[3][None, :],
     )
     ffn_join = pick(
         (ffn_to.reshape(1, -1) == my_fsdp)
         & (ffn_place.reshape(1, -1) == jnp.arange(ffn_count)[:, None]),
-        (
-            jnp.where(
-                ffn_rank < ffn_half,
-                slot_seq * ffn_half + ffn_rank,
-                seq_size * ffn_half + slot_seq * ffn_rest + ffn_rank - ffn_half,
-            )
+        jnp.where(
+            is_near,
+            slot_seq * near_hold + near_rank,
+            seq_size * near_hold
+            + jnp.where(
+                far_rank < far_half,
+                slot_seq * far_half + far_rank,
+                seq_size * far_half + slot_seq * far_rest + far_rank - far_half,
+            ),
         ).reshape(1, -1),
     )
-    ffn_cut = pick(
-        (ffn_to.reshape(seq_size, 1, -1) == my_fsdp)
-        & (ffn_rank.reshape(seq_size, 1, -1) == jnp.arange(ffn_hold)[None, :, None]),
-        ffn_place.reshape(seq_size, 1, -1),
-    )
+
+    def cut_index(key, rank, hold):
+        return pick(
+            (key.reshape(seq_size, 1, -1) == my_fsdp)
+            & (rank.reshape(seq_size, 1, -1) == jnp.arange(hold)[None, :, None]),
+            ffn_place.reshape(seq_size, 1, -1),
+        )
+
+    far_cut = cut_index(far_key, far_rank, far_hold)
+    near_cut = cut_index(near_key, near_rank, near_hold)
     ffn_back = pick(
         (seq_slots[5][None, None, :] == ((my_chip + shifts) % chips)[:, None, None])
         & (seq_slots[2][None, None, :] == my_chip)
         & (seq_slots[4][None, None, :] == (my_core * ffn_room + jnp.arange(ffn_room))[None, :, None]),
-        jnp.where(seq_slots[0] == my_fsdp, 0, ffn_hold) + seq_slots[1],
+        jnp.where(seq_slots[0] == my_fsdp, 0, far_hold) + seq_slots[1],
     )
 
     token_tiles = own_tokens.reshape(rows, row_blocks, tile).transpose(1, 0, 2)
@@ -779,7 +808,9 @@
     gain_in = gain_full[0:width]
     pack_normed = rms_norm(pack_tokens.astype(f32), gain_in).astype(bf16)
     ready = (allow, cosine, sine, ffn_keep, attn_keep, pack_normed, gain_full)
-    ffn_got, attn_got, parts, ready = lax.optimization_barrier((ffn_got, attn_got, parts, ready))
+    ffn_got, attn_got, parts, ready, near_all = lax.optimization_barrier(
+        (ffn_got, attn_got, parts, ready, near_all)
+    )
     allow, cosine, sine, ffn_keep, attn_keep, pack_normed, gain_full = ready
     gain_in = gain_full[0:width]
     small_got = core_pair(seq_order(jnp.stack([part[token_end:small_end] for part in parts])))
@@ -787,7 +818,7 @@
     small_table = assemble(small_got.reshape((-1,) + small_master.shape[1:]), row_blocks)
     (attn_kept,) = gather_tiles(attn_got, [attn_keep])
     ffn_got = ffn_got + [core_swap(value) for value in ffn_got]
-    ffn_kept = gather_tiles(ffn_got, [ffn_keep[:ffn_half], ffn_keep[ffn_half:]])
+    ffn_kept = gather_tiles(ffn_got, [ffn_keep[:far_half], ffn_keep[far_half:]])
     ffn_kept, attn_kept = lax.optimization_barrier((ffn_kept, attn_kept))
     ffn_all = [lax.all_gather(value, "seq", axis=0, tiled=True) for value in ffn_kept]
     attn_all = [attn_kept] + [chip_shift(attn_kept, offset) for offset in range(1, chips)]
@@ -882,7 +913,7 @@
     feed_low = lax.all_gather(feed_own, "fsdp", axis=0, tiled=True)
     ffn_all, _ = lax.optimization_barrier((ffn_all, feed_own))
     w_both, w_down = fetch(
-        ffn_all, ffn_join, ffn_to, my_fsdp, ffn_place, (ffn_first, ffn_each)
+        [near_all] + ffn_all, ffn_join, ffn_to, my_fsdp, ffn_place, (ffn_first, ffn_each)
     )
     both_pre = matmul(feed_low, w_both)
     ffn_width = w_down.shape[1]
@@ -924,10 +955,10 @@
     down_grad_w = matmul_outer(down_grad_low, hidden_low).astype(bf16)
     ffn_parts = cut_tiles(
         [both_grad_w, down_grad_w],
-        [ffn_cut[:, :ffn_half].reshape(-1), ffn_cut[:, ffn_half:].reshape(-1)],
+        [index.reshape(-1) for index in (far_cut[:, :far_half], far_cut[:, far_half:], near_cut)],
     )
     ffn_parts, grad_feed = lax.optimization_barrier((ffn_parts, grad_feed))
-    ffn_sums = [
+    *ffn_sums, near_sum = [
         lax.psum_scatter(value, "seq", scatter_dimension=0, tiled=True) for value in ffn_parts
     ]
 
@@ -992,7 +1023,6 @@
     for offset in range(1, chips):
         attn_sum = attn_sum + chip_shift(attn_parts[offset - 1], offset).astype(f32)
     attn_sum = attn_sum.astype(bf16)
-    attn_sum, normed_sum = lax.optimization_barrier((attn_sum, normed_sum))
     attn_back = pick(
         (column_slots[3][None, None, :] == (my_seq ^ flips)[:, None, None])
         & (column_slots[0][None, None, :] == my_key)
@@ -1003,6 +1033,15 @@
     grad_normed = half_grad + matmul_flip(left_grad_low, laurel_left) + normed_sum
     grad_stream_norm, grad_gain_in = normed_pull(grad_normed)
     input_grad = (half_grad + grad_stream_norm)[None]
+    ffn_sums, attn_sum, grad_gain_in, input_grad = lax.optimization_barrier(
+        (ffn_sums, attn_sum, grad_gain_in, input_grad)
+    )
+    ffn_sums = ffn_sums + [core_swap(value) for value in ffn_sums]
+    ffn_return = gather_tiles(ffn_sums, [ffn_back[i] for i in range(1, chips)])
+    ffn_return, attn_sum, grad_gain_in = lax.optimization_barrier(
+        (ffn_return, attn_sum, grad_gain_in)
+    )
+    ffn_returned = [chip_shift(value, i + 1) for i, value in enumerate(ffn_return)]
     gain_grad = jnp.concatenate(
         [
             grad_gain_in,
@@ -1025,22 +1064,8 @@
 
     late = late.astype(bf16)
     late = added(late, core_swap(late)).astype(bf16)
-    ffn_sums, attn_sum, late, input_grad = lax.optimization_barrier(
-        (ffn_sums, attn_sum, late, input_grad)
-    )
-    ffn_sums = ffn_sums + [core_swap(value) for value in ffn_sums]
-    late = jnp.pad(late, ((0, 2 * late_count * tile - late.shape[0]), (0, 0)))
-    late = late.reshape(2, late_count, tile, tile)
-    late = lax.dynamic_index_in_dim(late, my_core, 0, False)
-    late_index = 2 * ffn_hold + jnp.arange(late_count)
-    ffn_return = gather_tiles(
-        ffn_sums + [late], [jnp.concatenate([ffn_back[i], late_index]) for i in range(chips)]
-    )
-    ffn_return, attn_sum = lax.optimization_barrier((ffn_return, attn_sum))
-    ffn_returned = chip_exchange(ffn_return)
     attn_returned = seq_exchange(gather_tiles([attn_sum], [attn_back[i] for i in range(seq_size)]))
     attn_returned = attn_returned + [core_swap(value) for value in attn_returned]
-    back_size = 2 * chips * return_size
     slot_grad = jnp.where(my_slots[0] >= 0, my_slots[1], back_size + my_slots[2])
 
     def slow_return():
@@ -1066,11 +1091,16 @@
 
     slow_start = back_size + 2 * seq_size * attn_room
     slow_grads = lax.cond(fits, lambda: jnp.zeros((mine, tile, tile), bf16), slow_return)
-    ffn_returned, slow_grads = lax.optimization_barrier((ffn_returned, slow_grads))
-    late = sum(value[ffn_room:].astype(f32) for value in ffn_returned).astype(bf16)
-    late = core_pair(late).reshape(-1, tile).astype(f32)
+    ffn_returned, slow_grads, near_sum, late = lax.optimization_barrier(
+        (ffn_returned, slow_grads, near_sum, late)
+    )
+    late_sum = late.astype(f32)
+    for offset in range(1, chips):
+        late_sum = late_sum + chip_shift(late, offset).astype(f32)
+    late = late_sum
     ffn_returned = ffn_returned + [core_swap(value) for value in ffn_returned]
-    tile_grads = ffn_returned + attn_returned + [slow_grads]
+    near_sums = [near_sum, core_swap(near_sum)]
+    tile_grads = ffn_returned + near_sums + attn_returned + [slow_grads]
     slot_grad = jnp.where(fits, slot_grad, slow_start + local_slots)
 
     tile_new, tile_first_new, tile_second_new = rotate_update(

time: 1130 us -> 1100 us (0.973)
  waiting for transfers between devices: 559 us -> 527 us
    ppermute x18 -> x21, waiting for transfers between devices: 240 us -> 233 us  [chip_shift(): lax.ppermute(value, 'fsdp', [(i, (i // 2 + offset) % chips * 2 + i % 2) f...]
    ppermute x18 -> x21, starting transfers between devices: 23.6 us -> 29 us  [chip_shift(): lax.ppermute(value, 'fsdp', [(i, (i // 2 + offset) % chips * 2 + i % 2) f...]
    unnamed x409 -> x415, local copies, waits for them, and re-layouts: 62.6 us -> 64.2 us
  transfers between devices with their start and end apart: 74 -> 77, of which waited for: 41 -> 40; matrix products, arithmetic and copies ran while one was open for 17% -> 18% of each run, Pallas kernels for 7% -> 8%
where the time goes in v13:
time: 1100 us; the launch traced here: 1090 us
  waiting for transfers between devices  527 us (48%)
  Pallas kernels  139 us (13%)
  local copies, waits for them, and re-layouts  130 us (12%)
  matrix products  98.6 us (9%)
  other arithmetic  86.8 us (8%)
  starting transfers between devices  64.9 us (6%)
  between operations  40.9 us (4%)
    ppermute x21, waiting for transfers between devices, chip_shift(): lax.ppermute(value, 'fsdp', [(i, (i // 2 + offset) % chips * 2 + i % 2) f...  233 us
    ppermute x23, waiting for transfers between devices, seq_swap(): return lax.ppermute(value, 'seq', [(i, i ^ flip) for i in range(size)])  205 us
    pallas_call x10, Pallas kernels, tile_kernel_call(): pl.pallas_call(kernel, grid=(steps,), cost_estimate=pl.CostEstimate(flops...  91.2 us
    unnamed x415, local copies, waits for them, and re-layouts  64.2 us
    reduce_scatter x1, waiting for transfers between devices, on_device(): lax.psum_scatter(matmul_flip(hidden_low, w_down).astype(bf16), 'fsdp', sc...  48.4 us
    pallas_call x2, Pallas kernels, rotate_update(): pl.pallas_call(kernel, grid=(count // each,), out_shape=(shape, shape, sh...  44.4 us
    dot_general x8, matrix products, matmul(): return jnp.dot(left, right, preferred_element_type=jnp.float32)  34.5 us
    dot_general x8, matrix products, matmul_flip(): lax.dot_general(left, right, (((1,), (1,)), ((), ())), preferred_element_...  33.5 us
  transfers between devices with their start and end apart: 77, of which 40 were waited for; matrix products, arithmetic and copies ran while one was open for 18% of the time, Pallas kernels for 8%

profile of v13, /device:TPU:9, one launch (start us, length us, event | category | flops | bytes accessed | tf_op | source)
XLA Modules:
  0.0 1087.6 jit_solution(13684513304036542930)
XLA Ops:
  75.4 41.6 %collective-permute-done.4.refs_1_ = bf16[40,128,128]{2,1,0:T(8,128)(2,1)S(1)} collective-permute-done((bf16[40,128,128]{2,1,0:T(8,128)(2,1)}, bf16[40,128,128]{2,1,0:T(8,128)(2,1)S(1)}, u32[]{:S(2)}, u32[]{:S(2)}) %collective-permute-start.4) | collective-permute-done | bytes 1310752 | tf_op jit(solution)/shard_map/ppermute | solution.py:374
  123.1 26.9 %collective-permute-done.6.refs_3_ = bf16[40,128,128]{2,1,0:T(8,128)(2,1)} collective-permute-done((bf16[40,128,128]{2,1,0:T(8,128)(2,1)}, bf16[40,128,128]{2,1,0:T(8,128)(2,1)}, u32[]{:S(2)}, u32[]{:S(2)}) %collective-permute-start.6) | collective-permute-done | bytes 1310752 | tf_op jit(solution)/shard_map/ppermute | solution.py:374
  184.1 9.1 shard_map.261
  204.6 18.0 %collective-permute-done.10 = bf16[33,128,128]{2,1,0:T(8,128)(2,1)S(1)} collective-permute-done((bf16[33,128,128]{2,1,0:T(8,128)(2,1)S(1)}, bf16[33,128,128]{2,1,0:T(8,128)(2,1)S(1)}, u32[]{:S(2)}, u32[]{:S(2)}) %collective-permute-start.10) | collective-permute-done | bytes 1081376 | tf_op jit(solution)/shard_map/ppermute | solution.py:391
  222.8 66.8 %collective-permute-done.11 = bf16[33,128,128]{2,1,0:T(8,128)(2,1)S(1)} collective-permute-done((bf16[33,128,128]{2,1,0:T(8,128)(2,1)S(1)}, bf16[33,128,128]{2,1,0:T(8,128)(2,1)S(1)}, u32[]{:S(2)}, u32[]{:S(2)}) %collective-permute-start.11) | collective-permute-done | bytes 1081376 | tf_op jit(solution)/shard_map/ppermute | solution.py:391
  296.6 11.2 %conditional.3 = ((bf16[2048,768]{1,0:T(8,128)(2,1)}, bf16[2048,512]{1,0:T(8,128)(2,1)})) conditional(s32[]{:T(128)} %convert_element_type.372, (s32[]{:T(128)}, s32[4,8,116]{2,1,0:T(8,128)S(1)}, s32[4,8,116]{2,1,0:T(8,128)S(1)}, bf16[116,128,128]{2,1,0:T(8,128)(2,1)}) %tuple.41, (s32[160]{0:T(256)S(1)}, bf16[33,128,128]{2,1,0:T(8,128)(2,1)S(1)}, ...), branch_computations={%region_14.16_spmd, %region_16.17_spmd} | conditional | flops 2379392 | bytes 500902304 | solution.py:848
  296.6 10.8 branch_1_fun.2
  320.4 10.9 %collective-permute-done.17 = bf16[512,256]{1,0:T(8,128)(2,1)S(1)} collective-permute-done((bf16[512,256]{1,0:T(8,128)(2,1)S(1)}, bf16[512,256]{1,0:T(8,128)(2,1)S(1)}, u32[]{:S(2)}, u32[]{:S(2)}) %collective-permute-start.17) | collective-permute-done | bytes 262176 | tf_op jit(solution)/shard_map/ppermute | solution.py:374
  359.7 12.2 %collective-permute-done.20 = bf16[128,2048]{1,0:T(8,128)(2,1)} collective-permute-done((bf16[128,2048]{1,0:T(8,128)(2,1)}, bf16[128,2048]{1,0:T(8,128)(2,1)}, u32[]{:S(2)}, u32[]{:S(2)}) %collective-permute-start.20) | collective-permute-done | bytes 524320 | tf_op jit(solution)/shard_map/ppermute | solution.py:374
  378.0 14.4 %conditional.4 = ((bf16[2048,2048]{1,0:T(8,128)(2,1)}, bf16[2048,1024]{1,0:T(8,128)(2,1)})) conditional(s32[]{:T(128)} %convert_element_type.372, (s32[]{:T(128)}, s32[4,8,116]{2,1,0:T(8,128)S(1)}, s32[4,8,116]{2,1,0:T(8,128)S(1)}, bf16[116,128,128]{2,1,0:T(8,128)(2,1)}) %tuple.252, (s32[384]{0:T(512)S(1)}, bf16[176,128,128]{2,1,0:T(8,128)(2,1)}, ...), branch_computations={%region_26.28_spmd, %region_28.29_spmd} | conditional | flops 5705344 | bytes 515585056 | solution.py:848
  378.2 14.2 %branch_1_fun.3 = (bf16[2048,2048]{1,0:T(8,128)(2,1)}, bf16[2048,1024]{1,0:T(8,128)(2,1)}) custom-call(s32[384]{0:T(512)S(1)} %broadcast_clamp_fusion.3.index_ref, bf16[176,128,128]{2,1,0:T(8,128)(2,1)} %get-tuple-element.83.refs_0_, bf16[176,128,128]{2,1,0:T(8,128)(2,1)} %get-tuple-element.84.refs_1_, bf16[240,128,128]{2,1,0:T(8,128)(2,1)} %get-tuple-element.85.refs_2_), custom_call_target="tpu_custom_call" | custom-call | bytes 25165824 | tf_op jit(solution)/shard_map/cond/branch_1_fun/pallas_call | solution.py:152
  392.4 30.9 %all-gather.10.cloned.1.call-done = bf16[1024,2048]{1,0:T(8,128)(2,1)} async-done(((bf16[128,2048]{1,0:T(8,128)(2,1)}), bf16[1024,2048]{1,0:T(8,128)(2,1)}) %all-gather.10.cloned.1.call-update) | async-done | bytes 4194320 | tf_op jit(solution)/shard_map/all_gather | solution.py:913
  423.3 12.5 %fusion.271 = f32[1024,2048]{1,0:T(8,128)S(1)} fusion(bf16[1024,2048]{1,0:T(8,128)(2,1)} %all-gather.10.cloned.1.call-done, bf16[2048,2048]{1,0:T(8,128)(2,1)} %get-tuple-element.279), kind=kOutput, calls=%fused_computation.753 | convolution fusion | flops 8589934592 | bytes 20971520 | tf_op jit(solution)/shard_map/dot_general | solution.py:62
  447.5 48.4 %reduce-scatter.6.cloned.1.call-done = bf16[128,2048]{1,0:T(8,128)(2,1)} async-done(((bf16[1024,2048]{1,0:T(8,128)(2,1)}), bf16[128,2048]{1,0:T(8,128)(2,1)}) %reduce-scatter.6.cloned.1.call-update) | async-done | bytes 524304 | tf_op jit(solution)/shard_map/reduce_scatter | solution.py:922
  537.6 7.9 collective-permute-done.27
  563.5 12.1 %fusion.13 = (bf16[1024,1024]{1,0:T(8,128)(2,1)S(1)}, bf16[1024,1024]{1,0:T(8,128)(2,1)S(1)}) fusion(f32[1024,2048]{1,0:T(8,128)} %copy-done.59, bf16[1024,2048]{1,0:T(8,128)(2,1)} %all-gather.14.cloned.1.call-done, bf16[2048,1024]{1,0:T(8,128)(2,1)} %get-tuple-element.280), kind=kOutput, calls=%fused_computation.53 | convolution fusion | flops 4320133120 | bytes 20971520 | tf_op jit(solution)/shard_map/dot_general | solution.py:62
  577.6 12.6 %convolution_convert_fusion.1 = bf16[1024,2048]{1,0:T(8,128)(2,1)} fusion(bf16[2048,2048]{1,0:T(8,128)(2,1)} %get-tuple-element.279, bf16[1024,1024]{1,0:T(8,128)(2,1)S(1)} %get-tuple-element.452, bf16[1024,1024]{1,0:T(8,128)(2,1)S(1)} %get-tuple-element.451), kind=kOutput, calls=%fused_computation.61 | convolution fusion | flops 8600420352 | bytes 16777216 | tf_op jit(solution)/shard_map/dot_general | solution.py:66
  600.3 9.4 convolution_convert_fusion.refs_0_
  612.9 22.4 %shard_map.263 = (bf16[176,128,128]{2,1,0:T(8,128)(2,1)S(1)}, bf16[240,128,128]{2,1,0:T(8,128)(2,1)S(1)}, bf16[176,128,128]{2,1,0:T(8,128)(2,1)S(1)}) custom-call(s32[592]{0:T(1024)S(1)} %add_clamp_fusion.index_ref, bf16[2048,2048]{1,0:T(8,128)(2,1)S(1)} %convolution_convert_fusion.refs_0_, bf16[2048,1024]{1,0:T(8,128)(2,1)S(1)} %convolution_convert_fusion.2.refs_1_), custom_call_target="tpu_custom_call" | custom-call | bytes 38797312 | tf_op jit(solution)/shard_map/pallas_call | solution.py:152
  657.3 20.2 %collective-permute-done.33 = bf16[128,2048]{1,0:T(8,128)(2,1)S(1)} collective-permute-done((bf16[128,2048]{1,0:T(8,128)(2,1)S(1)}, bf16[128,2048]{1,0:T(8,128)(2,1)S(1)}, u32[]{:S(2)}, u32[]{:S(2)}) %collective-permute-start.33) | collective-permute-done | bytes 524320 | tf_op jit(solution)/shard_map/ppermute | solution.py:374
  678.7 21.9 %collective-permute-done.35 = bf16[128,2048]{1,0:T(8,128)(2,1)S(1)} collective-permute-done((bf16[128,2048]{1,0:T(8,128)(2,1)S(1)}, bf16[128,2048]{1,0:T(8,128)(2,1)S(1)}, u32[]{:S(2)}, u32[]{:S(2)}) %collective-permute-start.35) | collective-permute-done | bytes 524320 | tf_op jit(solution)/shard_map/ppermute | solution.py:374
  715.1 7.6 collective-permute-done.36
  732.2 10.2 shard_map.264
  758.0 7.3 fusion.248
  783.1 15.2 %collective-permute-done.41 = bf16[128,2048]{1,0:T(8,128)(2,1)} collective-permute-done((bf16[128,2048]{1,0:T(8,128)(2,1)}, bf16[128,2048]{1,0:T(8,128)(2,1)}, u32[]{:S(2)}, u32[]{:S(2)}) %collective-permute-start.41) | collective-permute-done | bytes 524320 | tf_op jit(solution)/shard_map/ppermute | solution.py:374
  801.9 13.1 %collective-permute-done.43 = bf16[128,2048]{1,0:T(8,128)(2,1)} collective-permute-done((bf16[128,2048]{1,0:T(8,128)(2,1)}, bf16[128,2048]{1,0:T(8,128)(2,1)}, u32[]{:S(2)}, u32[]{:S(2)}) %collective-permute-start.43) | collective-permute-done | bytes 524320 | tf_op jit(solution)/shard_map/ppermute | solution.py:374
  819.0 51.3 %collective-permute-done.39 = bf16[33,128,128]{2,1,0:T(8,128)(2,1)S(1)} collective-permute-done((bf16[33,128,128]{2,1,0:T(8,128)(2,1)}, bf16[33,128,128]{2,1,0:T(8,128)(2,1)S(1)}, u32[]{:S(2)}, u32[]{:S(2)}) %collective-permute-start.39) | collective-permute-done | bytes 1081376 | tf_op jit(solution)/shard_map/ppermute | solution.py:391
  886.6 7.9 shard_map.265
  919.3 10.9 collective-permute-done.57.refs_9_
  934.7 40.8 %collective-permute-done.46.refs_0_ = bf16[37,128,128]{2,1,0:T(8,128)(2,1)} collective-permute-done((bf16[37,128,128]{2,1,0:T(8,128)(2,1)}, bf16[37,128,128]{2,1,0:T(8,128)(2,1)}, u32[]{:S(2)}, u32[]{:S(2)}) %collective-permute-start.46) | collective-permute-done | bytes 1212448 | tf_op jit(solution)/shard_map/ppermute | solution.py:391
  975.6 23.6 %collective-permute-done.47.refs_1_ = bf16[37,128,128]{2,1,0:T(8,128)(2,1)} collective-permute-done((bf16[37,128,128]{2,1,0:T(8,128)(2,1)}, bf16[37,128,128]{2,1,0:T(8,128)(2,1)}, u32[]{:S(2)}, u32[]{:S(2)}) %collective-permute-start.47) | collective-permute-done | bytes 1212448 | tf_op jit(solution)/shard_map/ppermute | solution.py:391
  1043.1 37.5 %shard_map.267 = (f32[116,128,128]{2,1,0:T(8,128)}, f32[116,128,128]{2,1,0:T(8,128)}, f32[116,128,128]{2,1,0:T(8,128)}) custom-call(s32[116]{0:T(128)S(1)} %fusion.212.index_ref, bf16[37,128,128]{2,1,0:T(8,128)(2,1)} %collective-permute-done.46.refs_0_, bf16[37,128,128]{2,1,0:T(8,128)(2,1)} %collective-permute-done.47.refs_1_, ...), custom_call_target="tpu_custom_call" | custom-call | flops 5351931904 | bytes 64618496 | tf_op jit(solution)/shard_map/pallas_call | solution.py:353
  (895 shorter events, 415.2 us)
Async XLA Ops:
  7.2 170.3 %all-gather.6.cloned.1.call-start = ((), (), s32[]{:S(2)}) async-start(), calls=%async_computation.8 | async-start | bytes 7208960 | tf_op jit(solution)/shard_map/all_gather | solution.py:626
  31.5 265.1 %all-gather.8.cloned.1.call-start = ((), (), s32[]{:S(2)}) async-start(), calls=%async_computation.9 | async-start | bytes 7208960 | tf_op jit(solution)/shard_map/all_gather | solution.py:823
  60.9 56.2 %collective-permute-start.4 = (bf16[40,128,128]{2,1,0:T(8,128)(2,1)}, bf16[40,128,128]{2,1,0:T(8,128)(2,1)S(1)}, u32[]{:S(2)}, u32[]{:S(2)}) collective-permute-start(bf16[40,128,128]{2,1,0:T(8,128)(2,1)} %get-tuple-element.490), channel_id=1, source_target_pairs={{0,8},{8,0},{16,24},{24,16},{1,9},{9,1},{17,25},{25,17},{2,10},{10... | collective-permute-start | bytes 3932168 | tf_op jit(solution)/shard_map/ppermute | solution.py:374
  62.2 60.2 %collective-permute-start.5 = (bf16[40,128,128]{2,1,0:T(8,128)(2,1)}, bf16[40,128,128]{2,1,0:T(8,128)(2,1)}, u32[]{:S(2)}, u32[]{:S(2)}) collective-permute-start(bf16[40,128,128]{2,1,0:T(8,128)(2,1)} %get-tuple-element.489), channel_id=1, source_target_pairs={{0,16},{8,24},{16,0},{24,8},{1,17},{9,25},{17,1},{25,9},{2,18},{10... | collective-permute-start | bytes 3932168 | tf_op jit(solution)/shard_map/ppermute | solution.py:374
  63.1 86.9 %collective-permute-start.6 = (bf16[40,128,128]{2,1,0:T(8,128)(2,1)}, bf16[40,128,128]{2,1,0:T(8,128)(2,1)}, u32[]{:S(2)}, u32[]{:S(2)}) collective-permute-start(bf16[40,128,128]{2,1,0:T(8,128)(2,1)} %get-tuple-element.488), channel_id=1, source_target_pairs={{0,24},{8,16},{16,8},{24,0},{1,25},{9,17},{17,9},{25,1},{2,26},{10... | collective-permute-start | bytes 3932168 | tf_op jit(solution)/shard_map/ppermute | solution.py:374
  70.5 102.8 %collective-permute-start.1 = (bf16[37,128,128]{2,1,0:T(8,128)(2,1)}, bf16[37,128,128]{2,1,0:T(8,128)(2,1)S(1)}, u32[]{:S(2)}, u32[]{:S(2)}) collective-permute-start(bf16[37,128,128]{2,1,0:T(8,128)(2,1)} %copy-done.33), channel_id=1, source_target_pairs={{0,2},{1,3},{2,4},{3,5},{4,6},{5,7},{6,0},{7,1},{8,10},{9,11},{10,... | collective-permute-start | bytes 3637256 | tf_op jit(solution)/shard_map/ppermute | solution.py:391
  71.9 103.9 %collective-permute-start.2 = (bf16[37,128,128]{2,1,0:T(8,128)(2,1)}, bf16[37,128,128]{2,1,0:T(8,128)(2,1)}, u32[]{:S(2)}, u32[]{:S(2)}) collective-permute-start(bf16[37,128,128]{2,1,0:T(8,128)(2,1)} %copy-done.32), channel_id=1, source_target_pairs={{0,4},{1,5},{2,6},{3,7},{4,0},{5,1},{6,2},{7,3},{8,12},{9,13},{10,... | collective-permute-start | bytes 3637256 | tf_op jit(solution)/shard_map/ppermute | solution.py:391
  117.1 60.4 %collective-permute-start.3 = (bf16[37,128,128]{2,1,0:T(8,128)(2,1)}, bf16[37,128,128]{2,1,0:T(8,128)(2,1)}, u32[]{:S(2)}, u32[]{:S(2)}) collective-permute-start(bf16[37,128,128]{2,1,0:T(8,128)(2,1)} %copy-done.31), channel_id=1, source_target_pairs={{0,6},{1,7},{2,0},{3,1},{4,2},{5,3},{6,4},{7,5},{8,14},{9,15},{10,... | collective-permute-start | bytes 3637256 | tf_op jit(solution)/shard_map/ppermute | solution.py:391
  193.2 184.7 %all-gather.12.cloned.1.call-start = ((), (), s32[]{:S(2)}) async-start(), calls=%async_computation.11 | async-start | bytes 9830400 | tf_op jit(solution)/shard_map/all_gather | solution.py:823
  194.0 229.3 %all-gather.10.cloned.1.call-start = ((), (), s32[]{:S(2)}) async-start(), calls=%async_computation.10 | async-start | bytes 4718592 | tf_op jit(solution)/shard_map/all_gather | solution.py:913
  196.8 92.8 %collective-permute-start.11 = (bf16[33,128,128]{2,1,0:T(8,128)(2,1)S(1)}, bf16[33,128,128]{2,1,0:T(8,128)(2,1)S(1)}, u32[]{:S(2)}, u32[]{:S(2)}) collective-permute-start(bf16[33,128,128]{2,1,0:T(8,128)(2,1)S(1)} %copy-done.79), channel_id=1, source_target_pairs={{0,4},{1,5},{2,6},{3,7},{4,0},{5,1},{6,2},{7,3},{8,12},{9,13},{10,... | collective-permute-start | bytes 3244040 | tf_op jit(solution)/shard_map/ppermute | solution.py:391
  197.3 93.1 %collective-permute-start.12 = (bf16[33,128,128]{2,1,0:T(8,128)(2,1)S(1)}, bf16[33,128,128]{2,1,0:T(8,128)(2,1)S(1)}, u32[]{:S(2)}, u32[]{:S(2)}) collective-permute-start(bf16[33,128,128]{2,1,0:T(8,128)(2,1)S(1)} %copy-done.79), channel_id=1, source_target_pairs={{0,6},{1,7},{2,0},{3,1},{4,2},{5,3},{6,4},{7,5},{8,14},{9,15},{10,... | collective-permute-start | bytes 3244040 | tf_op jit(solution)/shard_map/ppermute | solution.py:391
  204.5 89.7 %collective-permute-start.13 = (bf16[33,128,128]{2,1,0:T(8,128)(2,1)S(1)}, bf16[33,128,128]{2,1,0:T(8,128)(2,1)S(1)}, u32[]{:S(2)}, u32[]{:S(2)}) collective-permute-start(bf16[33,128,128]{2,1,0:T(8,128)(2,1)S(1)} %copy-done.79), channel_id=1, source_target_pairs={{0,1},{1,0},{2,3},{3,2},{4,5},{5,4},{6,7},{7,6},{8,9},{9,8},{10,11... | collective-permute-start | bytes 3244040 | tf_op jit(solution)/shard_map/ppermute | solution.py:385
  222.6 71.6 %collective-permute-start.14 = (bf16[33,128,128]{2,1,0:T(8,128)(2,1)S(1)}, bf16[33,128,128]{2,1,0:T(8,128)(2,1)S(1)}, u32[]{:S(2)}, u32[]{:S(2)}) collective-permute-start(bf16[33,128,128]{2,1,0:T(8,128)(2,1)S(1)} %collective-permute-done.10), channel_id=1, source_target_pairs={{0,1},{1,0},{2,3},{3,2},{4,5},{5,4},{6,7},{7,6},{8,9},{9,8},{10,11... | collective-permute-start | bytes 3244040 | tf_op jit(solution)/shard_map/ppermute | solution.py:385
  293.9 50.6 %collective-permute-start.21 = (bf16[4,10,128,128]{3,2,1,0:T(8,128)(2,1)}, bf16[4,10,128,128]{3,2,1,0:T(8,128)(2,1)}, u32[]{:S(2)}, u32[]{:S(2)}) collective-permute-start(bf16[4,10,128,128]{3,2,1,0:T(8,128)(2,1)} %get-tuple-element.472), channel_id=1, source_target_pairs={{0,1},{1,0},{2,3},{3,2},{4,5},{5,4},{6,7},{7,6},{8,9},{9,8},{10,11... | collective-permute-start | bytes 3932168 | tf_op jit(solution)/shard_map/ppermute | solution.py:385
  377.8 118.1 %reduce-scatter.6.cloned.1.call-start = ((), (), s32[]{:S(2)}) async-start(), calls=%async_computation.12 | async-start | bytes 4718592 | tf_op jit(solution)/shard_map/reduce_scatter | solution.py:922
  447.5 116.1 %all-gather.14.cloned.1.call-start = ((), (), s32[]{:S(2)}) async-start(), calls=%async_computation.13 | async-start | bytes 4718592 | tf_op jit(solution)/shard_map/all_gather | solution.py:943
  504.7 138.9 %reduce-scatter.8.cloned.1.call-start = ((), (), s32[]{:S(2)}) async-start(), calls=%async_computation.14 | async-start | bytes 4718592 | tf_op jit(solution)/shard_map/reduce_scatter | solution.py:953
  590.3 156.2 %reduce-scatter.10.cloned.1.call-start = ((), (), s32[]{:S(2)}) async-start(), calls=%async_computation.15 | async-start | bytes 7208960 | tf_op jit(solution)/shard_map/reduce_scatter | solution.py:962
  645.7 230.4 %reduce-scatter.12.cloned.1.call-start = ((), (), s32[]{:S(2)}) async-start(), calls=%async_computation.16 | async-start | bytes 9830400 | tf_op jit(solution)/shard_map/reduce_scatter | solution.py:962
  646.9 353.3 %reduce-scatter.14.cloned.1.call-start = ((), (), s32[]{:S(2)}) async-start(), calls=%async_computation.17 | async-start | bytes 7208960 | tf_op jit(solution)/shard_map/reduce_scatter | solution.py:962
  655.0 45.7 %collective-permute-start.35 = (bf16[128,2048]{1,0:T(8,128)(2,1)S(1)}, bf16[128,2048]{1,0:T(8,128)(2,1)S(1)}, u32[]{:S(2)}, u32[]{:S(2)}) collective-permute-start(bf16[128,2048]{1,0:T(8,128)(2,1)S(1)} %get-tuple-element.483), channel_id=1, source_target_pairs={{0,24},{8,16},{16,8},{24,0},{1,25},{9,17},{17,9},{25,1},{2,26},{10... | collective-permute-start | bytes 1572872 | tf_op jit(solution)/shard_map/ppermute | solution.py:374
  775.0 40.1 %collective-permute-start.43 = (bf16[128,2048]{1,0:T(8,128)(2,1)}, bf16[128,2048]{1,0:T(8,128)(2,1)}, u32[]{:S(2)}, u32[]{:S(2)}) collective-permute-start(bf16[128,2048]{1,0:T(8,128)(2,1)} %get-tuple-element.459), channel_id=1, source_target_pairs={{0,24},{8,16},{16,8},{24,0},{1,25},{9,17},{17,9},{25,1},{2,26},{10... | collective-permute-start | bytes 1572872 | tf_op jit(solution)/shard_map/ppermute | solution.py:374
  777.3 41.7 %collective-permute-start.38 = (bf16[33,128,128]{2,1,0:T(8,128)(2,1)}, bf16[33,128,128]{2,1,0:T(8,128)(2,1)S(1)}, u32[]{:S(2)}, u32[]{:S(2)}) collective-permute-start(bf16[33,128,128]{2,1,0:T(8,128)(2,1)} %get-tuple-element.294), channel_id=1, source_target_pairs={{0,2},{1,3},{2,4},{3,5},{4,6},{5,7},{6,0},{7,1},{8,10},{9,11},{10,... | collective-permute-start | bytes 3244040 | tf_op jit(solution)/shard_map/ppermute | solution.py:391
  778.3 92.0 %collective-permute-start.39 = (bf16[33,128,128]{2,1,0:T(8,128)(2,1)}, bf16[33,128,128]{2,1,0:T(8,128)(2,1)S(1)}, u32[]{:S(2)}, u32[]{:S(2)}) collective-permute-start(bf16[33,128,128]{2,1,0:T(8,128)(2,1)} %get-tuple-element.295), channel_id=1, source_target_pairs={{0,4},{1,5},{2,6},{3,7},{4,0},{5,1},{6,2},{7,3},{8,12},{9,13},{10,... | collective-permute-start | bytes 3244040 | tf_op jit(solution)/shard_map/ppermute | solution.py:391
  798.3 77.1 %collective-permute-start.40 = (bf16[33,128,128]{2,1,0:T(8,128)(2,1)S(1)}, bf16[33,128,128]{2,1,0:T(8,128)(2,1)S(1)}, u32[]{:S(2)}, u32[]{:S(2)}) collective-permute-start(bf16[33,128,128]{2,1,0:T(8,128)(2,1)S(1)} %get-tuple-element.296), channel_id=1, source_target_pairs={{0,6},{1,7},{2,0},{3,1},{4,2},{5,3},{6,4},{7,5},{8,14},{9,15},{10,... | collective-permute-start | bytes 3244040 | tf_op jit(solution)/shard_map/ppermute | solution.py:391
  896.7 78.9 %collective-permute-start.46 = (bf16[37,128,128]{2,1,0:T(8,128)(2,1)}, bf16[37,128,128]{2,1,0:T(8,128)(2,1)}, u32[]{:S(2)}, u32[]{:S(2)}) collective-permute-start(bf16[37,128,128]{2,1,0:T(8,128)(2,1)} %copy-done.35), channel_id=1, source_target_pairs={{0,2},{1,3},{2,4},{3,5},{4,6},{5,7},{6,0},{7,1},{8,10},{9,11},{10,... | collective-permute-start | bytes 3637256 | tf_op jit(solution)/shard_map/ppermute | solution.py:391
  896.7 102.4 %collective-permute-start.47 = (bf16[37,128,128]{2,1,0:T(8,128)(2,1)}, bf16[37,128,128]{2,1,0:T(8,128)(2,1)}, u32[]{:S(2)}, u32[]{:S(2)}) collective-permute-start(bf16[37,128,128]{2,1,0:T(8,128)(2,1)} %copy-done.34), channel_id=1, source_target_pairs={{0,4},{1,5},{2,6},{3,7},{4,0},{5,1},{6,2},{7,3},{8,12},{9,13},{10,... | collective-permute-start | bytes 3637256 | tf_op jit(solution)/shard_map/ppermute | solution.py:391
  900.5 99.7 %collective-permute-start.48 = (bf16[37,128,128]{2,1,0:T(8,128)(2,1)}, bf16[37,128,128]{2,1,0:T(8,128)(2,1)}, u32[]{:S(2)}, u32[]{:S(2)}) collective-permute-start(bf16[37,128,128]{2,1,0:T(8,128)(2,1)} %get-tuple-element.308), channel_id=1, source_target_pairs={{0,6},{1,7},{2,0},{3,1},{4,2},{5,3},{6,4},{7,5},{8,14},{9,15},{10,... | collective-permute-start | bytes 3637256 | tf_op jit(solution)/shard_map/ppermute | solution.py:391
  919.1 81.7 %collective-permute-start.58 = (bf16[13,128,128]{2,1,0:T(8,128)(2,1)}, bf16[13,128,128]{2,1,0:T(8,128)(2,1)}, u32[]{:S(2)}, u32[]{:S(2)}) collective-permute-start(bf16[13,128,128]{2,1,0:T(8,128)(2,1)} %get-tuple-element.318), channel_id=1, source_target_pairs={{0,16},{8,24},{16,0},{24,8},{1,17},{9,25},{17,1},{25,9},{2,18},{10... | collective-permute-start | bytes 1277960 | tf_op jit(solution)/shard_map/ppermute | solution.py:374
  930.1 70.7 %collective-permute-start.59 = (bf16[13,128,128]{2,1,0:T(8,128)(2,1)}, bf16[13,128,128]{2,1,0:T(8,128)(2,1)}, u32[]{:S(2)}, u32[]{:S(2)}) collective-permute-start(bf16[13,128,128]{2,1,0:T(8,128)(2,1)} %get-tuple-element.319), channel_id=1, source_target_pairs={{0,24},{8,16},{16,8},{24,0},{1,25},{9,17},{17,9},{25,1},{2,26},{10... | collective-permute-start | bytes 1277960 | tf_op jit(solution)/shard_map/ppermute | solution.py:374
  1000.2 35.1 %collective-permute-start.56 = (bf16[44,128,128]{2,1,0:T(8,128)(2,1)}, bf16[44,128,128]{2,1,0:T(8,128)(2,1)S(1)}, u32[]{:S(2)}, u32[]{:S(2)}) collective-permute-start(bf16[44,128,128]{2,1,0:T(8,128)(2,1)} %reduce-scatter.14.cloned.1.call-done.refs_6_), channel_id=1, source_target_pairs={{0,1},{1,0},{2,3},{3,2},{4,5},{5,4},{6,7},{7,6},{8,9},{9,8},{10,11... | collective-permute-start | bytes 4325384 | tf_op jit(solution)/shard_map/ppermute | solution.py:385
  (247 other events, 4320.9 us)
Sparse Core Ops, SparseCore 0:
  31.6 119.1 all-gather.5
  193.4 64.6 all-gather.7
  260.0 92.9 all-gather.11
  378.0 45.2 all-gather.9
  447.6 48.2 reduce-scatter.5
  504.8 52.9 all-gather.13
  590.4 48.2 reduce-scatter.7
  645.9 91.9 reduce-scatter.9
  740.9 102.7 reduce-scatter.11
  877.9 82.3 reduce-scatter.13

commit v14 on v13

--- a/solution.py
+++ b/solution.py
@@ -1091,13 +1091,11 @@
 
     slow_start = back_size + 2 * seq_size * attn_room
     slow_grads = lax.cond(fits, lambda: jnp.zeros((mine, tile, tile), bf16), slow_return)
-    ffn_returned, slow_grads, near_sum, late = lax.optimization_barrier(
-        (ffn_returned, slow_grads, near_sum, late)
-    )
-    late_sum = late.astype(f32)
-    for offset in range(1, chips):
-        late_sum = late_sum + chip_shift(late, offset).astype(f32)
-    late = late_sum
+    late_parts = [late] + [chip_shift(late, offset) for offset in range(1, chips)]
+    ffn_returned, slow_grads, near_sum, late_parts = lax.optimization_barrier(
+        (ffn_returned, slow_grads, near_sum, late_parts)
+    )
+    late = sum(value.astype(f32) for value in late_parts)
     ffn_returned = ffn_returned + [core_swap(value) for value in ffn_returned]
     near_sums = [near_sum, core_swap(near_sum)]
     tile_grads = ffn_returned + near_sums + attn_returned + [slow_grads]

time: 1100 us -> 1130 us (1.027)
  waiting for transfers between devices: 527 us -> 541 us
    ppermute x23, starting transfers between devices: 12.9 us -> 32.1 us  [core_swap(): return lax.ppermute(value, 'fsdp', [(i, i ^ 1) for i in range(size)])]
    ppermute x21, waiting for transfers between devices: 233 us -> 252 us  [chip_shift(): lax.ppermute(value, 'fsdp', [(i, (i // 2 + offset) % chips * 2 + i % 2) f...]
    unnamed x415 -> x413, local copies, waits for them, and re-layouts: 64.2 us -> 65.9 us
  transfers between devices with their start and end apart: 77 -> 77, of which waited for: 40 -> 37; matrix products, arithmetic and copies ran while one was open for 18% -> 18% of each run, Pallas kernels for 8% -> 8%
where the time goes in v14:
time: 1130 us; the launch traced here: 1110 us
  waiting for transfers between devices  541 us (48%)
  Pallas kernels  136 us (12%)
  local copies, waits for them, and re-layouts  131 us (12%)
  matrix products  98.4 us (9%)
  other arithmetic  88.9 us (8%)
  starting transfers between devices  74.2 us (7%)
  between operations  41.4 us (4%)
    ppermute x21, waiting for transfers between devices, chip_shift(): lax.ppermute(value, 'fsdp', [(i, (i // 2 + offset) % chips * 2 + i % 2) f...  252 us
    ppermute x23, waiting for transfers between devices, seq_swap(): return lax.ppermute(value, 'seq', [(i, i ^ flip) for i in range(size)])  200 us
    pallas_call x10, Pallas kernels, tile_kernel_call(): pl.pallas_call(kernel, grid=(steps,), cost_estimate=pl.CostEstimate(flops...  89 us
    unnamed x413, local copies, waits for them, and re-layouts  65.9 us
    reduce_scatter x1, waiting for transfers between devices, on_device(): lax.psum_scatter(matmul_flip(hidden_low, w_down).astype(bf16), 'fsdp', sc...  48.4 us
    pallas_call x2, Pallas kernels, rotate_update(): pl.pallas_call(kernel, grid=(count // each,), out_shape=(shape, shape, sh...  43.9 us
    dot_general x8, matrix products, matmul(): return jnp.dot(left, right, preferred_element_type=jnp.float32)  34.6 us
    dot_general x8, matrix products, matmul_flip(): lax.dot_general(left, right, (((1,), (1,)), ((), ())), preferred_element_...  33.3 us
  transfers between devices with their start and end apart: 77, of which 37 were waited for; matrix products, arithmetic and copies ran while one was open for 18% of the time, Pallas kernels for 8%

profile of v14, /device:TPU:9, one launch (start us, length us, event | category | flops | bytes accessed | tf_op | source)
XLA Modules:
  0.0 1112.4 jit_solution(16321045964777576752)
XLA Ops:
  75.4 40.8 %collective-permute-done.4.refs_1_ = bf16[40,128,128]{2,1,0:T(8,128)(2,1)S(1)} collective-permute-done((bf16[40,128,128]{2,1,0:T(8,128)(2,1)}, bf16[40,128,128]{2,1,0:T(8,128)(2,1)S(1)}, u32[]{:S(2)}, u32[]{:S(2)}) %collective-permute-start.4) | collective-permute-done | bytes 1310752 | tf_op jit(solution)/shard_map/ppermute | solution.py:374
  122.1 28.1 %collective-permute-done.6.refs_3_ = bf16[40,128,128]{2,1,0:T(8,128)(2,1)} collective-permute-done((bf16[40,128,128]{2,1,0:T(8,128)(2,1)}, bf16[40,128,128]{2,1,0:T(8,128)(2,1)}, u32[]{:S(2)}, u32[]{:S(2)}) %collective-permute-start.6) | collective-permute-done | bytes 1310752 | tf_op jit(solution)/shard_map/ppermute | solution.py:374
  183.9 9.1 shard_map.261
  204.9 17.3 %collective-permute-done.10 = bf16[33,128,128]{2,1,0:T(8,128)(2,1)S(1)} collective-permute-done((bf16[33,128,128]{2,1,0:T(8,128)(2,1)S(1)}, bf16[33,128,128]{2,1,0:T(8,128)(2,1)S(1)}, u32[]{:S(2)}, u32[]{:S(2)}) %collective-permute-start.10) | collective-permute-done | bytes 1081376 | tf_op jit(solution)/shard_map/ppermute | solution.py:391
  223.5 66.2 %collective-permute-done.11 = bf16[33,128,128]{2,1,0:T(8,128)(2,1)S(1)} collective-permute-done((bf16[33,128,128]{2,1,0:T(8,128)(2,1)S(1)}, bf16[33,128,128]{2,1,0:T(8,128)(2,1)S(1)}, u32[]{:S(2)}, u32[]{:S(2)}) %collective-permute-start.11) | collective-permute-done | bytes 1081376 | tf_op jit(solution)/shard_map/ppermute | solution.py:391
  297.0 11.1 conditional.3
  297.0 10.7 branch_1_fun.2
  320.1 10.8 collective-permute-done.17
  352.5 7.0 collective-permute-done.18
  359.5 12.3 %collective-permute-done.20 = bf16[128,2048]{1,0:T(8,128)(2,1)} collective-permute-done((bf16[128,2048]{1,0:T(8,128)(2,1)}, bf16[128,2048]{1,0:T(8,128)(2,1)}, u32[]{:S(2)}, u32[]{:S(2)}) %collective-permute-start.20) | collective-permute-done | bytes 524320 | tf_op jit(solution)/shard_map/ppermute | solution.py:374
  377.8 14.4 %conditional.4 = ((bf16[2048,2048]{1,0:T(8,128)(2,1)}, bf16[2048,1024]{1,0:T(8,128)(2,1)})) conditional(s32[]{:T(128)} %convert_element_type.372, (s32[]{:T(128)}, s32[4,8,116]{2,1,0:T(8,128)S(1)}, s32[4,8,116]{2,1,0:T(8,128)S(1)}, bf16[116,128,128]{2,1,0:T(8,128)(2,1)}) %tuple.252, (s32[384]{0:T(512)S(1)}, bf16[176,128,128]{2,1,0:T(8,128)(2,1)}, ...), branch_computations={%region_26.28_spmd, %region_28.29_spmd} | conditional | flops 5705344 | bytes 515585056 | solution.py:848
  378.0 14.2 %branch_1_fun.3 = (bf16[2048,2048]{1,0:T(8,128)(2,1)}, bf16[2048,1024]{1,0:T(8,128)(2,1)}) custom-call(s32[384]{0:T(512)S(1)} %broadcast_clamp_fusion.3.index_ref, bf16[176,128,128]{2,1,0:T(8,128)(2,1)} %get-tuple-element.83.refs_0_, bf16[176,128,128]{2,1,0:T(8,128)(2,1)} %get-tuple-element.84.refs_1_, bf16[240,128,128]{2,1,0:T(8,128)(2,1)} %get-tuple-element.85.refs_2_), custom_call_target="tpu_custom_call" | custom-call | bytes 25165824 | tf_op jit(solution)/shard_map/cond/branch_1_fun/pallas_call | solution.py:152
  392.2 30.9 %all-gather.10.cloned.1.call-done = bf16[1024,2048]{1,0:T(8,128)(2,1)} async-done(((bf16[128,2048]{1,0:T(8,128)(2,1)}), bf16[1024,2048]{1,0:T(8,128)(2,1)}) %all-gather.10.cloned.1.call-update) | async-done | bytes 4194320 | tf_op jit(solution)/shard_map/all_gather | solution.py:913
  423.1 12.5 %fusion.271 = f32[1024,2048]{1,0:T(8,128)S(1)} fusion(bf16[1024,2048]{1,0:T(8,128)(2,1)} %all-gather.10.cloned.1.call-done, bf16[2048,2048]{1,0:T(8,128)(2,1)} %get-tuple-element.282), kind=kOutput, calls=%fused_computation.753 | convolution fusion | flops 8589934592 | bytes 20971520 | tf_op jit(solution)/shard_map/dot_general | solution.py:62
  447.4 48.4 %reduce-scatter.6.cloned.1.call-done = bf16[128,2048]{1,0:T(8,128)(2,1)} async-done(((bf16[1024,2048]{1,0:T(8,128)(2,1)}), bf16[128,2048]{1,0:T(8,128)(2,1)}) %reduce-scatter.6.cloned.1.call-update) | async-done | bytes 524304 | tf_op jit(solution)/shard_map/reduce_scatter | solution.py:922
  538.0 7.9 collective-permute-done.27
  564.1 12.1 %fusion.13 = (bf16[1024,1024]{1,0:T(8,128)(2,1)S(1)}, bf16[1024,1024]{1,0:T(8,128)(2,1)S(1)}) fusion(f32[1024,2048]{1,0:T(8,128)} %copy-done.60, bf16[1024,2048]{1,0:T(8,128)(2,1)} %all-gather.14.cloned.1.call-done, bf16[2048,1024]{1,0:T(8,128)(2,1)} %get-tuple-element.283), kind=kOutput, calls=%fused_computation.53 | convolution fusion | flops 4320133120 | bytes 20971520 | tf_op jit(solution)/shard_map/dot_general | solution.py:62
  578.2 12.6 %convolution_convert_fusion.1 = bf16[1024,2048]{1,0:T(8,128)(2,1)} fusion(bf16[2048,2048]{1,0:T(8,128)(2,1)} %get-tuple-element.282, bf16[1024,1024]{1,0:T(8,128)(2,1)S(1)} %get-tuple-element.458, bf16[1024,1024]{1,0:T(8,128)(2,1)S(1)} %get-tuple-element.457), kind=kOutput, calls=%fused_computation.61 | convolution fusion | flops 8600420352 | bytes 16777216 | tf_op jit(solution)/shard_map/dot_general | solution.py:66
  593.7 7.2 convolution_convert_fusion.2.refs_1_
  600.9 9.4 convolution_convert_fusion.refs_0_
  613.5 22.4 %shard_map.263 = (bf16[176,128,128]{2,1,0:T(8,128)(2,1)S(1)}, bf16[240,128,128]{2,1,0:T(8,128)(2,1)S(1)}, bf16[176,128,128]{2,1,0:T(8,128)(2,1)S(1)}) custom-call(s32[592]{0:T(1024)S(1)} %add_clamp_fusion.index_ref, bf16[2048,2048]{1,0:T(8,128)(2,1)S(1)} %convolution_convert_fusion.refs_0_, bf16[2048,1024]{1,0:T(8,128)(2,1)S(1)} %convolution_convert_fusion.2.refs_1_), custom_call_target="tpu_custom_call" | custom-call | bytes 38797312 | tf_op jit(solution)/shard_map/pallas_call | solution.py:152
  657.9 20.3 %collective-permute-done.33 = bf16[128,2048]{1,0:T(8,128)(2,1)S(1)} collective-permute-done((bf16[128,2048]{1,0:T(8,128)(2,1)S(1)}, bf16[128,2048]{1,0:T(8,128)(2,1)S(1)}, u32[]{:S(2)}, u32[]{:S(2)}) %collective-permute-start.33) | collective-permute-done | bytes 524320 | tf_op jit(solution)/shard_map/ppermute | solution.py:374
  679.4 21.9 %collective-permute-done.35 = bf16[128,2048]{1,0:T(8,128)(2,1)S(1)} collective-permute-done((bf16[128,2048]{1,0:T(8,128)(2,1)S(1)}, bf16[128,2048]{1,0:T(8,128)(2,1)S(1)}, u32[]{:S(2)}, u32[]{:S(2)}) %collective-permute-start.35) | collective-permute-done | bytes 524320 | tf_op jit(solution)/shard_map/ppermute | solution.py:374
  715.4 6.9 collective-permute-done.36
  732.2 10.2 shard_map.264
  759.6 7.3 fusion.248
  781.4 15.9 %collective-permute-done.41 = bf16[128,2048]{1,0:T(8,128)(2,1)S(1)} collective-permute-done((bf16[128,2048]{1,0:T(8,128)(2,1)S(1)}, bf16[128,2048]{1,0:T(8,128)(2,1)S(1)}, u32[]{:S(2)}, u32[]{:S(2)}) %collective-permute-start.41) | collective-permute-done | bytes 524320 | tf_op jit(solution)/shard_map/ppermute | solution.py:374
  800.2 15.2 %collective-permute-done.43 = bf16[128,2048]{1,0:T(8,128)(2,1)S(1)} collective-permute-done((bf16[128,2048]{1,0:T(8,128)(2,1)S(1)}, bf16[128,2048]{1,0:T(8,128)(2,1)S(1)}, u32[]{:S(2)}, u32[]{:S(2)}) %collective-permute-start.43) | collective-permute-done | bytes 524320 | tf_op jit(solution)/shard_map/ppermute | solution.py:374
  818.7 49.1 %collective-permute-done.39 = bf16[33,128,128]{2,1,0:T(8,128)(2,1)S(1)} collective-permute-done((bf16[33,128,128]{2,1,0:T(8,128)(2,1)S(1)}, bf16[33,128,128]{2,1,0:T(8,128)(2,1)S(1)}, u32[]{:S(2)}, u32[]{:S(2)}) %collective-permute-start.39) | collective-permute-done | bytes 1081376 | tf_op jit(solution)/shard_map/ppermute | solution.py:391
  919.7 95.3 %collective-permute-done.53 = bf16[537,128]{1,0:T(8,128)(2,1)S(1)} collective-permute-done((bf16[537,128]{1,0:T(8,128)(2,1)S(1)}, bf16[537,128]{1,0:T(8,128)(2,1)S(1)}, u32[]{:S(2)}, u32[]{:S(2)}) %collective-permute-start.53) | collective-permute-done | bytes 137504 | tf_op jit(solution)/shard_map/ppermute | solution.py:391
  1053.0 7.0 shard_map.268
  1068.4 36.9 %shard_map.267 = (f32[116,128,128]{2,1,0:T(8,128)}, f32[116,128,128]{2,1,0:T(8,128)}, f32[116,128,128]{2,1,0:T(8,128)}) custom-call(s32[116]{0:T(128)S(1)} %fusion.212.index_ref, bf16[37,128,128]{2,1,0:T(8,128)(2,1)} %collective-permute-done.46.refs_0_, bf16[37,128,128]{2,1,0:T(8,128)(2,1)} %collective-permute-done.47.refs_1_, ...), custom_call_target="tpu_custom_call" | custom-call | flops 5351931904 | bytes 64618496 | tf_op jit(solution)/shard_map/pallas_call | solution.py:353
  (893 shorter events, 407.6 us)
Async XLA Ops:
  7.2 170.1 %all-gather.6.cloned.1.call-start = ((), (), s32[]{:S(2)}) async-start(), calls=%async_computation.8 | async-start | bytes 7208960 | tf_op jit(solution)/shard_map/all_gather | solution.py:626
  31.4 265.6 %all-gather.8.cloned.1.call-start = ((), (), s32[]{:S(2)}) async-start(), calls=%async_computation.9 | async-start | bytes 7208960 | tf_op jit(solution)/shard_map/all_gather | solution.py:823
  60.8 55.4 %collective-permute-start.4 = (bf16[40,128,128]{2,1,0:T(8,128)(2,1)}, bf16[40,128,128]{2,1,0:T(8,128)(2,1)S(1)}, u32[]{:S(2)}, u32[]{:S(2)}) collective-permute-start(bf16[40,128,128]{2,1,0:T(8,128)(2,1)} %get-tuple-element.496), channel_id=1, source_target_pairs={{0,8},{8,0},{16,24},{24,16},{1,9},{9,1},{17,25},{25,17},{2,10},{10... | collective-permute-start | bytes 3932168 | tf_op jit(solution)/shard_map/ppermute | solution.py:374
  62.0 59.5 %collective-permute-start.5 = (bf16[40,128,128]{2,1,0:T(8,128)(2,1)}, bf16[40,128,128]{2,1,0:T(8,128)(2,1)}, u32[]{:S(2)}, u32[]{:S(2)}) collective-permute-start(bf16[40,128,128]{2,1,0:T(8,128)(2,1)} %get-tuple-element.495), channel_id=1, source_target_pairs={{0,16},{8,24},{16,0},{24,8},{1,17},{9,25},{17,1},{25,9},{2,18},{10... | collective-permute-start | bytes 3932168 | tf_op jit(solution)/shard_map/ppermute | solution.py:374
  63.2 87.0 %collective-permute-start.6 = (bf16[40,128,128]{2,1,0:T(8,128)(2,1)}, bf16[40,128,128]{2,1,0:T(8,128)(2,1)}, u32[]{:S(2)}, u32[]{:S(2)}) collective-permute-start(bf16[40,128,128]{2,1,0:T(8,128)(2,1)} %get-tuple-element.494), channel_id=1, source_target_pairs={{0,24},{8,16},{16,8},{24,0},{1,25},{9,17},{17,9},{25,1},{2,26},{10... | collective-permute-start | bytes 3932168 | tf_op jit(solution)/shard_map/ppermute | solution.py:374
  70.4 103.1 %collective-permute-start.1 = (bf16[37,128,128]{2,1,0:T(8,128)(2,1)}, bf16[37,128,128]{2,1,0:T(8,128)(2,1)S(1)}, u32[]{:S(2)}, u32[]{:S(2)}) collective-permute-start(bf16[37,128,128]{2,1,0:T(8,128)(2,1)} %copy-done.33), channel_id=1, source_target_pairs={{0,2},{1,3},{2,4},{3,5},{4,6},{5,7},{6,0},{7,1},{8,10},{9,11},{10,... | collective-permute-start | bytes 3637256 | tf_op jit(solution)/shard_map/ppermute | solution.py:391
  71.7 104.2 %collective-permute-start.2 = (bf16[37,128,128]{2,1,0:T(8,128)(2,1)}, bf16[37,128,128]{2,1,0:T(8,128)(2,1)}, u32[]{:S(2)}, u32[]{:S(2)}) collective-permute-start(bf16[37,128,128]{2,1,0:T(8,128)(2,1)} %copy-done.32), channel_id=1, source_target_pairs={{0,4},{1,5},{2,6},{3,7},{4,0},{5,1},{6,2},{7,3},{8,12},{9,13},{10,... | collective-permute-start | bytes 3637256 | tf_op jit(solution)/shard_map/ppermute | solution.py:391
  116.2 61.1 %collective-permute-start.3 = (bf16[37,128,128]{2,1,0:T(8,128)(2,1)}, bf16[37,128,128]{2,1,0:T(8,128)(2,1)}, u32[]{:S(2)}, u32[]{:S(2)}) collective-permute-start(bf16[37,128,128]{2,1,0:T(8,128)(2,1)} %copy-done.31), channel_id=1, source_target_pairs={{0,6},{1,7},{2,0},{3,1},{4,2},{5,3},{6,4},{7,5},{8,14},{9,15},{10,... | collective-permute-start | bytes 3637256 | tf_op jit(solution)/shard_map/ppermute | solution.py:391
  193.1 184.6 %all-gather.12.cloned.1.call-start = ((), (), s32[]{:S(2)}) async-start(), calls=%async_computation.11 | async-start | bytes 9830400 | tf_op jit(solution)/shard_map/all_gather | solution.py:823
  193.8 229.3 %all-gather.10.cloned.1.call-start = ((), (), s32[]{:S(2)}) async-start(), calls=%async_computation.10 | async-start | bytes 4718592 | tf_op jit(solution)/shard_map/all_gather | solution.py:913
  196.8 92.9 %collective-permute-start.11 = (bf16[33,128,128]{2,1,0:T(8,128)(2,1)S(1)}, bf16[33,128,128]{2,1,0:T(8,128)(2,1)S(1)}, u32[]{:S(2)}, u32[]{:S(2)}) collective-permute-start(bf16[33,128,128]{2,1,0:T(8,128)(2,1)S(1)} %copy-done.79), channel_id=1, source_target_pairs={{0,4},{1,5},{2,6},{3,7},{4,0},{5,1},{6,2},{7,3},{8,12},{9,13},{10,... | collective-permute-start | bytes 3244040 | tf_op jit(solution)/shard_map/ppermute | solution.py:391
  197.4 93.3 %collective-permute-start.12 = (bf16[33,128,128]{2,1,0:T(8,128)(2,1)S(1)}, bf16[33,128,128]{2,1,0:T(8,128)(2,1)S(1)}, u32[]{:S(2)}, u32[]{:S(2)}) collective-permute-start(bf16[33,128,128]{2,1,0:T(8,128)(2,1)S(1)} %copy-done.79), channel_id=1, source_target_pairs={{0,6},{1,7},{2,0},{3,1},{4,2},{5,3},{6,4},{7,5},{8,14},{9,15},{10,... | collective-permute-start | bytes 3244040 | tf_op jit(solution)/shard_map/ppermute | solution.py:391
  204.7 89.9 %collective-permute-start.13 = (bf16[33,128,128]{2,1,0:T(8,128)(2,1)S(1)}, bf16[33,128,128]{2,1,0:T(8,128)(2,1)S(1)}, u32[]{:S(2)}, u32[]{:S(2)}) collective-permute-start(bf16[33,128,128]{2,1,0:T(8,128)(2,1)S(1)} %copy-done.79), channel_id=1, source_target_pairs={{0,1},{1,0},{2,3},{3,2},{4,5},{5,4},{6,7},{7,6},{8,9},{9,8},{10,11... | collective-permute-start | bytes 3244040 | tf_op jit(solution)/shard_map/ppermute | solution.py:385
  222.2 72.4 %collective-permute-start.14 = (bf16[33,128,128]{2,1,0:T(8,128)(2,1)S(1)}, bf16[33,128,128]{2,1,0:T(8,128)(2,1)S(1)}, u32[]{:S(2)}, u32[]{:S(2)}) collective-permute-start(bf16[33,128,128]{2,1,0:T(8,128)(2,1)S(1)} %collective-permute-done.10), channel_id=1, source_target_pairs={{0,1},{1,0},{2,3},{3,2},{4,5},{5,4},{6,7},{7,6},{8,9},{9,8},{10,11... | collective-permute-start | bytes 3244040 | tf_op jit(solution)/shard_map/ppermute | solution.py:385
  294.2 49.9 %collective-permute-start.21 = (bf16[4,10,128,128]{3,2,1,0:T(8,128)(2,1)}, bf16[4,10,128,128]{3,2,1,0:T(8,128)(2,1)}, u32[]{:S(2)}, u32[]{:S(2)}) collective-permute-start(bf16[4,10,128,128]{3,2,1,0:T(8,128)(2,1)} %get-tuple-element.478), channel_id=1, source_target_pairs={{0,1},{1,0},{2,3},{3,2},{4,5},{5,4},{6,7},{7,6},{8,9},{9,8},{10,11... | collective-permute-start | bytes 3932168 | tf_op jit(solution)/shard_map/ppermute | solution.py:385
  377.6 118.1 %reduce-scatter.6.cloned.1.call-start = ((), (), s32[]{:S(2)}) async-start(), calls=%async_computation.12 | async-start | bytes 4718592 | tf_op jit(solution)/shard_map/reduce_scatter | solution.py:922
  447.3 116.8 %all-gather.14.cloned.1.call-start = ((), (), s32[]{:S(2)}) async-start(), calls=%async_computation.13 | async-start | bytes 4718592 | tf_op jit(solution)/shard_map/all_gather | solution.py:943
  505.1 139.1 %reduce-scatter.8.cloned.1.call-start = ((), (), s32[]{:S(2)}) async-start(), calls=%async_computation.14 | async-start | bytes 4718592 | tf_op jit(solution)/shard_map/reduce_scatter | solution.py:953
  590.9 155.6 %reduce-scatter.10.cloned.1.call-start = ((), (), s32[]{:S(2)}) async-start(), calls=%async_computation.15 | async-start | bytes 7208960 | tf_op jit(solution)/shard_map/reduce_scatter | solution.py:962
  646.3 227.9 %reduce-scatter.12.cloned.1.call-start = ((), (), s32[]{:S(2)}) async-start(), calls=%async_computation.16 | async-start | bytes 9830400 | tf_op jit(solution)/shard_map/reduce_scatter | solution.py:962
  647.5 382.0 %reduce-scatter.14.cloned.1.call-start = ((), (), s32[]{:S(2)}) async-start(), calls=%async_computation.17 | async-start | bytes 7208960 | tf_op jit(solution)/shard_map/reduce_scatter | solution.py:962
  655.3 46.0 %collective-permute-start.35 = (bf16[128,2048]{1,0:T(8,128)(2,1)S(1)}, bf16[128,2048]{1,0:T(8,128)(2,1)S(1)}, u32[]{:S(2)}, u32[]{:S(2)}) collective-permute-start(bf16[128,2048]{1,0:T(8,128)(2,1)S(1)} %get-tuple-element.489), channel_id=1, source_target_pairs={{0,24},{8,16},{16,8},{24,0},{1,25},{9,17},{17,9},{25,1},{2,26},{10... | collective-permute-start | bytes 1572872 | tf_op jit(solution)/shard_map/ppermute | solution.py:374
  773.4 42.1 %collective-permute-start.43 = (bf16[128,2048]{1,0:T(8,128)(2,1)S(1)}, bf16[128,2048]{1,0:T(8,128)(2,1)S(1)}, u32[]{:S(2)}, u32[]{:S(2)}) collective-permute-start(bf16[128,2048]{1,0:T(8,128)(2,1)S(1)} %get-tuple-element.465), channel_id=1, source_target_pairs={{0,24},{8,16},{16,8},{24,0},{1,25},{9,17},{17,9},{25,1},{2,26},{10... | collective-permute-start | bytes 1572872 | tf_op jit(solution)/shard_map/ppermute | solution.py:374
  776.2 42.6 %collective-permute-start.38 = (bf16[33,128,128]{2,1,0:T(8,128)(2,1)S(1)}, bf16[33,128,128]{2,1,0:T(8,128)(2,1)S(1)}, u32[]{:S(2)}, u32[]{:S(2)}) collective-permute-start(bf16[33,128,128]{2,1,0:T(8,128)(2,1)S(1)} %get-tuple-element.297), channel_id=1, source_target_pairs={{0,2},{1,3},{2,4},{3,5},{4,6},{5,7},{6,0},{7,1},{8,10},{9,11},{10,... | collective-permute-start | bytes 3244040 | tf_op jit(solution)/shard_map/ppermute | solution.py:391
  776.2 91.6 %collective-permute-start.39 = (bf16[33,128,128]{2,1,0:T(8,128)(2,1)S(1)}, bf16[33,128,128]{2,1,0:T(8,128)(2,1)S(1)}, u32[]{:S(2)}, u32[]{:S(2)}) collective-permute-start(bf16[33,128,128]{2,1,0:T(8,128)(2,1)S(1)} %get-tuple-element.298), channel_id=1, source_target_pairs={{0,4},{1,5},{2,6},{3,7},{4,0},{5,1},{6,2},{7,3},{8,12},{9,13},{10,... | collective-permute-start | bytes 3244040 | tf_op jit(solution)/shard_map/ppermute | solution.py:391
  797.2 76.3 %collective-permute-start.40 = (bf16[33,128,128]{2,1,0:T(8,128)(2,1)S(1)}, bf16[33,128,128]{2,1,0:T(8,128)(2,1)S(1)}, u32[]{:S(2)}, u32[]{:S(2)}) collective-permute-start(bf16[33,128,128]{2,1,0:T(8,128)(2,1)S(1)} %get-tuple-element.299), channel_id=1, source_target_pairs={{0,6},{1,7},{2,0},{3,1},{4,2},{5,3},{6,4},{7,5},{8,14},{9,15},{10,... | collective-permute-start | bytes 3244040 | tf_op jit(solution)/shard_map/ppermute | solution.py:391
  903.1 118.0 %collective-permute-start.46 = (bf16[37,128,128]{2,1,0:T(8,128)(2,1)S(1)}, bf16[37,128,128]{2,1,0:T(8,128)(2,1)}, u32[]{:S(2)}, u32[]{:S(2)}) collective-permute-start(bf16[37,128,128]{2,1,0:T(8,128)(2,1)S(1)} %copy-done.37), channel_id=1, source_target_pairs={{0,2},{1,3},{2,4},{3,5},{4,6},{5,7},{6,0},{7,1},{8,10},{9,11},{10,... | collective-permute-start | bytes 3637256 | tf_op jit(solution)/shard_map/ppermute | solution.py:391
  903.1 119.1 %collective-permute-start.47 = (bf16[37,128,128]{2,1,0:T(8,128)(2,1)S(1)}, bf16[37,128,128]{2,1,0:T(8,128)(2,1)}, u32[]{:S(2)}, u32[]{:S(2)}) collective-permute-start(bf16[37,128,128]{2,1,0:T(8,128)(2,1)S(1)} %copy-done.35), channel_id=1, source_target_pairs={{0,4},{1,5},{2,6},{3,7},{4,0},{5,1},{6,2},{7,3},{8,12},{9,13},{10,... | collective-permute-start | bytes 3637256 | tf_op jit(solution)/shard_map/ppermute | solution.py:391
  908.9 120.6 %collective-permute-start.48 = (bf16[37,128,128]{2,1,0:T(8,128)(2,1)}, bf16[37,128,128]{2,1,0:T(8,128)(2,1)}, u32[]{:S(2)}, u32[]{:S(2)}) collective-permute-start(bf16[37,128,128]{2,1,0:T(8,128)(2,1)} %get-tuple-element.311), channel_id=1, source_target_pairs={{0,6},{1,7},{2,0},{3,1},{4,2},{5,3},{6,4},{7,5},{8,14},{9,15},{10,... | collective-permute-start | bytes 3637256 | tf_op jit(solution)/shard_map/ppermute | solution.py:391
  918.1 96.8 %collective-permute-start.53 = (bf16[537,128]{1,0:T(8,128)(2,1)S(1)}, bf16[537,128]{1,0:T(8,128)(2,1)S(1)}, u32[]{:S(2)}, u32[]{:S(2)}) collective-permute-start(bf16[537,128]{1,0:T(8,128)(2,1)S(1)} %add_convert_fusion.3), channel_id=1, source_target_pairs={{0,2},{1,3},{2,4},{3,5},{4,6},{5,7},{6,0},{7,1},{8,10},{9,11},{10,... | collective-permute-start | bytes 412424 | tf_op jit(solution)/shard_map/ppermute | solution.py:391
  919.4 100.0 %collective-permute-start.54 = (bf16[537,128]{1,0:T(8,128)(2,1)S(1)}, bf16[537,128]{1,0:T(8,128)(2,1)S(1)}, u32[]{:S(2)}, u32[]{:S(2)}) collective-permute-start(bf16[537,128]{1,0:T(8,128)(2,1)S(1)} %add_convert_fusion.3), channel_id=1, source_target_pairs={{0,4},{1,5},{2,6},{3,7},{4,0},{5,1},{6,2},{7,3},{8,12},{9,13},{10,... | collective-permute-start | bytes 412424 | tf_op jit(solution)/shard_map/ppermute | solution.py:391
  1029.5 31.2 %collective-permute-start.59 = (bf16[44,128,128]{2,1,0:T(8,128)(2,1)}, bf16[44,128,128]{2,1,0:T(8,128)(2,1)S(1)}, u32[]{:S(2)}, u32[]{:S(2)}) collective-permute-start(bf16[44,128,128]{2,1,0:T(8,128)(2,1)} %reduce-scatter.14.cloned.1.call-done.refs_6_), channel_id=1, source_target_pairs={{0,1},{1,0},{2,3},{3,2},{4,5},{5,4},{6,7},{7,6},{8,9},{9,8},{10,11... | collective-permute-start | bytes 4325384 | tf_op jit(solution)/shard_map/ppermute | solution.py:385
  (246 other events, 4389.5 us)
Sparse Core Ops, SparseCore 0:
  31.5 119.4 all-gather.5
  193.2 64.7 all-gather.7
  259.9 93.0 all-gather.11
  377.8 45.3 all-gather.9
  447.4 48.2 reduce-scatter.5
  505.2 52.9 all-gather.13
  591.0 48.2 reduce-scatter.7
  646.4 92.0 reduce-scatter.9
  741.5 102.7 reduce-scatter.11
  876.3 69.2 reduce-scatter.13

commit v15 on v13

--- a/solution.py
+++ b/solution.py
@@ -1094,10 +1094,7 @@
     ffn_returned, slow_grads, near_sum, late = lax.optimization_barrier(
         (ffn_returned, slow_grads, near_sum, late)
     )
-    late_sum = late.astype(f32)
-    for offset in range(1, chips):
-        late_sum = late_sum + chip_shift(late, offset).astype(f32)
-    late = late_sum
+    late_parts = [late] + [chip_shift(late, offset) for offset in range(1, chips)]
     ffn_returned = ffn_returned + [core_swap(value) for value in ffn_returned]
     near_sums = [near_sum, core_swap(near_sum)]
     tile_grads = ffn_returned + near_sums + attn_returned + [slow_grads]
@@ -1106,6 +1103,10 @@
     tile_new, tile_first_new, tile_second_new = rotate_update(
         tile_grads, slot_grad, tile_master, tile_first, tile_second, left_basis, right_basis, RATE_TILE
     )
+    late_parts, tile_new, tile_first_new, tile_second_new = lax.optimization_barrier(
+        (late_parts, tile_new, tile_first_new, tile_second_new)
+    )
+    late = sum(value.astype(f32) for value in late_parts)
     late_rows = late_full.shape[0] // seq_size
     late_tiles = late[:late_rows].reshape(-1, 1, tile, tile)
     gain_grad_mine = late[late_rows : late_rows + own_gains.shape[0] // tile].reshape(-1)

time: 1100 us -> 1090 us (level)
    ppermute x21, waiting for transfers between devices: 233 us -> 215 us  [chip_shift(): lax.ppermute(value, 'fsdp', [(i, (i // 2 + offset) % chips * 2 + i % 2) f...]
    unnamed x415 -> x405, local copies, waits for them, and re-layouts: 64.2 us -> 58.7 us
  transfers between devices with their start and end apart: 77 -> 77, of which waited for: 40 -> 36; matrix products, arithmetic and copies ran while one was open for 18% -> 18% of each run, Pallas kernels for 8% -> 11%
where the time goes in v15:
time: 1090 us; the launch traced here: 1080 us
  waiting for transfers between devices  518 us (48%)
  Pallas kernels  140 us (13%)
  local copies, waits for them, and re-layouts  123 us (11%)
  matrix products  98.9 us (9%)
  other arithmetic  84.1 us (8%)
  starting transfers between devices  68.8 us (6%)
  between operations  41 us (4%)
    ppermute x21, waiting for transfers between devices, chip_shift(): lax.ppermute(value, 'fsdp', [(i, (i // 2 + offset) % chips * 2 + i % 2) f...  215 us
    ppermute x23, waiting for transfers between devices, seq_swap(): return lax.ppermute(value, 'seq', [(i, i ^ flip) for i in range(size)])  207 us
    pallas_call x10, Pallas kernels, tile_kernel_call(): pl.pallas_call(kernel, grid=(steps,), cost_estimate=pl.CostEstimate(flops...  91.6 us
    unnamed x405, local copies, waits for them, and re-layouts  58.7 us
    reduce_scatter x1, waiting for transfers between devices, on_device(): lax.psum_scatter(matmul_flip(hidden_low, w_down).astype(bf16), 'fsdp', sc...  48.4 us
    pallas_call x2, Pallas kernels, rotate_update(): pl.pallas_call(kernel, grid=(count // each,), out_shape=(shape, shape, sh...  45.2 us
    dot_general x8, matrix products, matmul(): return jnp.dot(left, right, preferred_element_type=jnp.float32)  34.6 us
    dot_general x8, matrix products, matmul_flip(): lax.dot_general(left, right, (((1,), (1,)), ((), ())), preferred_element_...  34.2 us
  transfers between devices with their start and end apart: 77, of which 36 were waited for; matrix products, arithmetic and copies ran while one was open for 18% of the time, Pallas kernels for 11%

profile of v15, /device:TPU:9, one launch (start us, length us, event | category | flops | bytes accessed | tf_op | source)
XLA Modules:
  0.0 1075.1 jit_solution(6300063475895400250)
XLA Ops:
  21.4 7.5 shard_map.257
  73.7 77.4 %collective-permute-done.6.refs_3_ = bf16[40,128,128]{2,1,0:T(8,128)(2,1)} collective-permute-done((bf16[40,128,128]{2,1,0:T(8,128)(2,1)}, bf16[40,128,128]{2,1,0:T(8,128)(2,1)}, u32[]{:S(2)}, u32[]{:S(2)}) %collective-permute-start.6) | collective-permute-done | bytes 1310752 | tf_op jit(solution)/shard_map/ppermute | solution.py:374
  186.4 9.7 shard_map.261
  212.0 13.4 %collective-permute-done.10 = bf16[33,128,128]{2,1,0:T(8,128)(2,1)S(1)} collective-permute-done((bf16[33,128,128]{2,1,0:T(8,128)(2,1)S(1)}, bf16[33,128,128]{2,1,0:T(8,128)(2,1)S(1)}, u32[]{:S(2)}, u32[]{:S(2)}) %collective-permute-start.10) | collective-permute-done | bytes 1081376 | tf_op jit(solution)/shard_map/ppermute | solution.py:391
  226.9 66.5 %collective-permute-done.11 = bf16[33,128,128]{2,1,0:T(8,128)(2,1)S(1)} collective-permute-done((bf16[33,128,128]{2,1,0:T(8,128)(2,1)S(1)}, bf16[33,128,128]{2,1,0:T(8,128)(2,1)S(1)}, u32[]{:S(2)}, u32[]{:S(2)}) %collective-permute-start.11) | collective-permute-done | bytes 1081376 | tf_op jit(solution)/shard_map/ppermute | solution.py:391
  304.0 11.3 %conditional.3 = ((bf16[2048,768]{1,0:T(8,128)(2,1)}, bf16[2048,512]{1,0:T(8,128)(2,1)})) conditional(s32[]{:T(128)} %convert_element_type.372, (s32[]{:T(128)}, s32[4,8,116]{2,1,0:T(8,128)S(1)}, s32[4,8,116]{2,1,0:T(8,128)S(1)}, bf16[116,128,128]{2,1,0:T(8,128)(2,1)}) %tuple.42, (s32[160]{0:T(256)S(1)}, bf16[33,128,128]{2,1,0:T(8,128)(2,1)S(1)}, ...), branch_computations={%region_14.16_spmd, %region_16.17_spmd} | conditional | flops 2379392 | bytes 500902304 | solution.py:848
  304.0 10.9 %branch_1_fun.2 = (bf16[2048,768]{1,0:T(8,128)(2,1)}, bf16[2048,512]{1,0:T(8,128)(2,1)}) custom-call(s32[160]{0:T(256)S(1)} %broadcast_clamp_fusion.1.index_ref, bf16[33,128,128]{2,1,0:T(8,128)(2,1)S(1)} %get-tuple-element.70.refs_0_, bf16[33,128,128]{2,1,0:T(8,128)(2,1)S(1)} %get-tuple-element.71.refs_1_, bf16[33,128,128]{2,1,0:T(8,128)(2,1)} %get-tuple-element.72.refs_2_, ...), custom_call_target="tpu_custom_call" | custom-call | bytes 10485760 | tf_op jit(solution)/shard_map/cond/branch_1_fun/pallas_call | solution.py:152
  324.9 10.2 collective-permute-done.17
  356.6 9.1 collective-permute-done.20
  382.1 14.4 %conditional.4 = ((bf16[2048,2048]{1,0:T(8,128)(2,1)}, bf16[2048,1024]{1,0:T(8,128)(2,1)})) conditional(s32[]{:T(128)} %convert_element_type.372, (s32[]{:T(128)}, s32[4,8,116]{2,1,0:T(8,128)S(1)}, s32[4,8,116]{2,1,0:T(8,128)S(1)}, bf16[116,128,128]{2,1,0:T(8,128)(2,1)}) %tuple.255, (s32[384]{0:T(512)S(1)}, bf16[176,128,128]{2,1,0:T(8,128)(2,1)}, ...), branch_computations={%region_26.28_spmd, %region_28.29_spmd} | conditional | flops 5705344 | bytes 515585056 | solution.py:848
  382.3 14.1 %branch_1_fun.3 = (bf16[2048,2048]{1,0:T(8,128)(2,1)}, bf16[2048,1024]{1,0:T(8,128)(2,1)}) custom-call(s32[384]{0:T(512)S(1)} %broadcast_clamp_fusion.3.index_ref, bf16[176,128,128]{2,1,0:T(8,128)(2,1)} %get-tuple-element.83.refs_0_, bf16[176,128,128]{2,1,0:T(8,128)(2,1)} %get-tuple-element.84.refs_1_, bf16[240,128,128]{2,1,0:T(8,128)(2,1)} %get-tuple-element.85.refs_2_), custom_call_target="tpu_custom_call" | custom-call | bytes 25165824 | tf_op jit(solution)/shard_map/cond/branch_1_fun/pallas_call | solution.py:152
  396.5 31.9 %all-gather.10.cloned.1.call-done = bf16[1024,2048]{1,0:T(8,128)(2,1)} async-done(((bf16[128,2048]{1,0:T(8,128)(2,1)}), bf16[1024,2048]{1,0:T(8,128)(2,1)}) %all-gather.10.cloned.1.call-update) | async-done | bytes 4194320 | tf_op jit(solution)/shard_map/all_gather | solution.py:913
  428.4 12.5 %fusion.271 = f32[1024,2048]{1,0:T(8,128)S(1)} fusion(bf16[1024,2048]{1,0:T(8,128)(2,1)} %all-gather.10.cloned.1.call-done, bf16[2048,2048]{1,0:T(8,128)(2,1)} %get-tuple-element.286), kind=kOutput, calls=%fused_computation.753 | convolution fusion | flops 8589934592 | bytes 20971520 | tf_op jit(solution)/shard_map/dot_general | solution.py:62
  452.6 48.4 %reduce-scatter.6.cloned.1.call-done = bf16[128,2048]{1,0:T(8,128)(2,1)} async-done(((bf16[1024,2048]{1,0:T(8,128)(2,1)}), bf16[128,2048]{1,0:T(8,128)(2,1)}) %reduce-scatter.6.cloned.1.call-update) | async-done | bytes 524304 | tf_op jit(solution)/shard_map/reduce_scatter | solution.py:922
  568.1 12.1 %fusion.13 = (bf16[1024,1024]{1,0:T(8,128)(2,1)S(1)}, bf16[1024,1024]{1,0:T(8,128)(2,1)S(1)}) fusion(f32[1024,2048]{1,0:T(8,128)} %copy-done.56, bf16[1024,2048]{1,0:T(8,128)(2,1)} %all-gather.14.cloned.1.call-done, bf16[2048,1024]{1,0:T(8,128)(2,1)} %get-tuple-element.287), kind=kOutput, calls=%fused_computation.53 | convolution fusion | flops 4320133120 | bytes 20971520 | tf_op jit(solution)/shard_map/dot_general | solution.py:62
  582.2 12.6 %convolution_convert_fusion.1 = bf16[1024,2048]{1,0:T(8,128)(2,1)} fusion(bf16[2048,2048]{1,0:T(8,128)(2,1)} %get-tuple-element.286, bf16[1024,1024]{1,0:T(8,128)(2,1)S(1)} %get-tuple-element.466, bf16[1024,1024]{1,0:T(8,128)(2,1)S(1)} %get-tuple-element.465), kind=kOutput, calls=%fused_computation.61 | convolution fusion | flops 8600420352 | bytes 16777216 | tf_op jit(solution)/shard_map/dot_general | solution.py:66
  597.6 7.2 convolution_convert_fusion.2.refs_1_
  604.8 9.4 convolution_convert_fusion.refs_0_
  617.4 22.4 %shard_map.263 = (bf16[176,128,128]{2,1,0:T(8,128)(2,1)S(1)}, bf16[240,128,128]{2,1,0:T(8,128)(2,1)S(1)}, bf16[176,128,128]{2,1,0:T(8,128)(2,1)S(1)}) custom-call(s32[592]{0:T(1024)S(1)} %add_clamp_fusion.index_ref, bf16[2048,2048]{1,0:T(8,128)(2,1)S(1)} %convolution_convert_fusion.refs_0_, bf16[2048,1024]{1,0:T(8,128)(2,1)S(1)} %convolution_convert_fusion.2.refs_1_), custom_call_target="tpu_custom_call" | custom-call | bytes 38797312 | tf_op jit(solution)/shard_map/pallas_call | solution.py:152
  661.8 21.1 %collective-permute-done.35 = bf16[128,2048]{1,0:T(8,128)(2,1)S(1)} collective-permute-done((bf16[128,2048]{1,0:T(8,128)(2,1)S(1)}, bf16[128,2048]{1,0:T(8,128)(2,1)S(1)}, u32[]{:S(2)}, u32[]{:S(2)}) %collective-permute-start.35) | collective-permute-done | bytes 524320 | tf_op jit(solution)/shard_map/ppermute | solution.py:374
  682.8 11.9 %collective-permute-done.34 = bf16[128,2048]{1,0:T(8,128)(2,1)S(1)} collective-permute-done((bf16[128,2048]{1,0:T(8,128)(2,1)S(1)}, bf16[128,2048]{1,0:T(8,128)(2,1)S(1)}, u32[]{:S(2)}, u32[]{:S(2)}) %collective-permute-start.34) | collective-permute-done | bytes 524320 | tf_op jit(solution)/shard_map/ppermute | solution.py:374
  694.7 10.9 %collective-permute-done.33 = bf16[128,2048]{1,0:T(8,128)(2,1)S(1)} collective-permute-done((bf16[128,2048]{1,0:T(8,128)(2,1)S(1)}, bf16[128,2048]{1,0:T(8,128)(2,1)S(1)}, u32[]{:S(2)}, u32[]{:S(2)}) %collective-permute-start.33) | collective-permute-done | bytes 524320 | tf_op jit(solution)/shard_map/ppermute | solution.py:374
  727.9 10.2 shard_map.264
  751.4 7.3 fusion.248
  775.1 17.4 %collective-permute-done.43 = bf16[128,2048]{1,0:T(8,128)(2,1)} collective-permute-done((bf16[128,2048]{1,0:T(8,128)(2,1)}, bf16[128,2048]{1,0:T(8,128)(2,1)}, u32[]{:S(2)}, u32[]{:S(2)}) %collective-permute-start.43) | collective-permute-done | bytes 524320 | tf_op jit(solution)/shard_map/ppermute | solution.py:374
  793.3 10.9 %collective-permute-done.42 = bf16[128,2048]{1,0:T(8,128)(2,1)} collective-permute-done((bf16[128,2048]{1,0:T(8,128)(2,1)}, bf16[128,2048]{1,0:T(8,128)(2,1)}, u32[]{:S(2)}, u32[]{:S(2)}) %collective-permute-start.42) | collective-permute-done | bytes 524320 | tf_op jit(solution)/shard_map/ppermute | solution.py:374
  804.2 9.9 collective-permute-done.41
  818.1 27.0 %collective-permute-done.39 = bf16[33,128,128]{2,1,0:T(8,128)(2,1)S(1)} collective-permute-done((bf16[33,128,128]{2,1,0:T(8,128)(2,1)}, bf16[33,128,128]{2,1,0:T(8,128)(2,1)S(1)}, u32[]{:S(2)}, u32[]{:S(2)}) %collective-permute-start.39) | collective-permute-done | bytes 1081376 | tf_op jit(solution)/shard_map/ppermute | solution.py:391
  845.1 23.1 %collective-permute-done.38 = bf16[33,128,128]{2,1,0:T(8,128)(2,1)S(1)} collective-permute-done((bf16[33,128,128]{2,1,0:T(8,128)(2,1)S(1)}, bf16[33,128,128]{2,1,0:T(8,128)(2,1)S(1)}, u32[]{:S(2)}, u32[]{:S(2)}) %collective-permute-start.38) | collective-permute-done | bytes 1081376 | tf_op jit(solution)/shard_map/ppermute | solution.py:391
  920.2 45.1 %collective-permute-done.46.refs_0_ = bf16[37,128,128]{2,1,0:T(8,128)(2,1)} collective-permute-done((bf16[37,128,128]{2,1,0:T(8,128)(2,1)}, bf16[37,128,128]{2,1,0:T(8,128)(2,1)}, u32[]{:S(2)}, u32[]{:S(2)}) %collective-permute-start.46) | collective-permute-done | bytes 1212448 | tf_op jit(solution)/shard_map/ppermute | solution.py:391
  966.7 24.8 %collective-permute-done.47.refs_1_ = bf16[37,128,128]{2,1,0:T(8,128)(2,1)} collective-permute-done((bf16[37,128,128]{2,1,0:T(8,128)(2,1)}, bf16[37,128,128]{2,1,0:T(8,128)(2,1)}, u32[]{:S(2)}, u32[]{:S(2)}) %collective-permute-start.47) | collective-permute-done | bytes 1212448 | tf_op jit(solution)/shard_map/ppermute | solution.py:391
  1021.4 38.3 %shard_map.267 = (f32[116,128,128]{2,1,0:T(8,128)}, f32[116,128,128]{2,1,0:T(8,128)}, f32[116,128,128]{2,1,0:T(8,128)}) custom-call(s32[116]{0:T(128)S(1)} %fusion.212.index_ref, bf16[37,128,128]{2,1,0:T(8,128)(2,1)} %collective-permute-done.46.refs_0_, bf16[37,128,128]{2,1,0:T(8,128)(2,1)} %collective-permute-done.47.refs_1_, ...), custom_call_target="tpu_custom_call" | custom-call | flops 5351931904 | bytes 64618496 | tf_op jit(solution)/shard_map/pallas_call | solution.py:353
  (886 shorter events, 403.4 us)
Async XLA Ops:
  7.2 172.3 %all-gather.6.cloned.1.call-start = ((), (), s32[]{:S(2)}) async-start(), calls=%async_computation.8 | async-start | bytes 7208960 | tf_op jit(solution)/shard_map/all_gather | solution.py:626
  30.1 273.9 %all-gather.8.cloned.1.call-start = ((), (), s32[]{:S(2)}) async-start(), calls=%async_computation.9 | async-start | bytes 7208960 | tf_op jit(solution)/shard_map/all_gather | solution.py:823
  47.3 131.1 %collective-permute-start.1 = (bf16[37,128,128]{2,1,0:T(8,128)(2,1)}, bf16[37,128,128]{2,1,0:T(8,128)(2,1)}, u32[]{:S(2)}, u32[]{:S(2)}) collective-permute-start(bf16[37,128,128]{2,1,0:T(8,128)(2,1)} %get-tuple-element.230), channel_id=1, source_target_pairs={{0,2},{1,3},{2,4},{3,5},{4,6},{5,7},{6,0},{7,1},{8,10},{9,11},{10,... | collective-permute-start | bytes 3637256 | tf_op jit(solution)/shard_map/ppermute | solution.py:391
  48.1 130.2 %collective-permute-start.2 = (bf16[37,128,128]{2,1,0:T(8,128)(2,1)}, bf16[37,128,128]{2,1,0:T(8,128)(2,1)}, u32[]{:S(2)}, u32[]{:S(2)}) collective-permute-start(bf16[37,128,128]{2,1,0:T(8,128)(2,1)} %get-tuple-element.231), channel_id=1, source_target_pairs={{0,4},{1,5},{2,6},{3,7},{4,0},{5,1},{6,2},{7,3},{8,12},{9,13},{10,... | collective-permute-start | bytes 3637256 | tf_op jit(solution)/shard_map/ppermute | solution.py:391
  61.3 93.1 %collective-permute-start.4 = (bf16[40,128,128]{2,1,0:T(8,128)(2,1)}, bf16[40,128,128]{2,1,0:T(8,128)(2,1)S(1)}, u32[]{:S(2)}, u32[]{:S(2)}) collective-permute-start(bf16[40,128,128]{2,1,0:T(8,128)(2,1)} %get-tuple-element.504), channel_id=1, source_target_pairs={{0,8},{8,0},{16,24},{24,16},{1,9},{9,1},{17,25},{25,17},{2,10},{10... | collective-permute-start | bytes 3932168 | tf_op jit(solution)/shard_map/ppermute | solution.py:374
  62.9 90.7 %collective-permute-start.5 = (bf16[40,128,128]{2,1,0:T(8,128)(2,1)}, bf16[40,128,128]{2,1,0:T(8,128)(2,1)}, u32[]{:S(2)}, u32[]{:S(2)}) collective-permute-start(bf16[40,128,128]{2,1,0:T(8,128)(2,1)} %get-tuple-element.503), channel_id=1, source_target_pairs={{0,16},{8,24},{16,0},{24,8},{1,17},{9,25},{17,1},{25,9},{2,18},{10... | collective-permute-start | bytes 3932168 | tf_op jit(solution)/shard_map/ppermute | solution.py:374
  63.8 87.3 %collective-permute-start.6 = (bf16[40,128,128]{2,1,0:T(8,128)(2,1)}, bf16[40,128,128]{2,1,0:T(8,128)(2,1)}, u32[]{:S(2)}, u32[]{:S(2)}) collective-permute-start(bf16[40,128,128]{2,1,0:T(8,128)(2,1)} %get-tuple-element.502), channel_id=1, source_target_pairs={{0,24},{8,16},{16,8},{24,0},{1,25},{9,17},{17,9},{25,1},{2,26},{10... | collective-permute-start | bytes 3932168 | tf_op jit(solution)/shard_map/ppermute | solution.py:374
  196.1 186.0 %all-gather.12.cloned.1.call-start = ((), (), s32[]{:S(2)}) async-start(), calls=%async_computation.11 | async-start | bytes 9830400 | tf_op jit(solution)/shard_map/all_gather | solution.py:823
  196.8 231.5 %all-gather.10.cloned.1.call-start = ((), (), s32[]{:S(2)}) async-start(), calls=%async_computation.10 | async-start | bytes 4718592 | tf_op jit(solution)/shard_map/all_gather | solution.py:913
  200.7 92.7 %collective-permute-start.11 = (bf16[33,128,128]{2,1,0:T(8,128)(2,1)S(1)}, bf16[33,128,128]{2,1,0:T(8,128)(2,1)S(1)}, u32[]{:S(2)}, u32[]{:S(2)}) collective-permute-start(bf16[33,128,128]{2,1,0:T(8,128)(2,1)S(1)} %copy-done.75), channel_id=1, source_target_pairs={{0,4},{1,5},{2,6},{3,7},{4,0},{5,1},{6,2},{7,3},{8,12},{9,13},{10,... | collective-permute-start | bytes 3244040 | tf_op jit(solution)/shard_map/ppermute | solution.py:391
  203.8 94.0 %collective-permute-start.12 = (bf16[33,128,128]{2,1,0:T(8,128)(2,1)S(1)}, bf16[33,128,128]{2,1,0:T(8,128)(2,1)S(1)}, u32[]{:S(2)}, u32[]{:S(2)}) collective-permute-start(bf16[33,128,128]{2,1,0:T(8,128)(2,1)S(1)} %copy-done.75), channel_id=1, source_target_pairs={{0,6},{1,7},{2,0},{3,1},{4,2},{5,3},{6,4},{7,5},{8,14},{9,15},{10,... | collective-permute-start | bytes 3244040 | tf_op jit(solution)/shard_map/ppermute | solution.py:391
  211.1 90.6 %collective-permute-start.13 = (bf16[33,128,128]{2,1,0:T(8,128)(2,1)S(1)}, bf16[33,128,128]{2,1,0:T(8,128)(2,1)S(1)}, u32[]{:S(2)}, u32[]{:S(2)}) collective-permute-start(bf16[33,128,128]{2,1,0:T(8,128)(2,1)S(1)} %copy-done.75), channel_id=1, source_target_pairs={{0,1},{1,0},{2,3},{3,2},{4,5},{5,4},{6,7},{7,6},{8,9},{9,8},{10,11... | collective-permute-start | bytes 3244040 | tf_op jit(solution)/shard_map/ppermute | solution.py:385
  225.4 76.2 %collective-permute-start.14 = (bf16[33,128,128]{2,1,0:T(8,128)(2,1)S(1)}, bf16[33,128,128]{2,1,0:T(8,128)(2,1)S(1)}, u32[]{:S(2)}, u32[]{:S(2)}) collective-permute-start(bf16[33,128,128]{2,1,0:T(8,128)(2,1)S(1)} %collective-permute-done.10), channel_id=1, source_target_pairs={{0,1},{1,0},{2,3},{3,2},{4,5},{5,4},{6,7},{7,6},{8,9},{9,8},{10,11... | collective-permute-start | bytes 3244040 | tf_op jit(solution)/shard_map/ppermute | solution.py:385
  301.2 47.2 %collective-permute-start.21 = (bf16[4,10,128,128]{3,2,1,0:T(8,128)(2,1)}, bf16[4,10,128,128]{3,2,1,0:T(8,128)(2,1)}, u32[]{:S(2)}, u32[]{:S(2)}) collective-permute-start(bf16[4,10,128,128]{3,2,1,0:T(8,128)(2,1)} %get-tuple-element.486), channel_id=1, source_target_pairs={{0,1},{1,0},{2,3},{3,2},{4,5},{5,4},{6,7},{7,6},{8,9},{9,8},{10,11... | collective-permute-start | bytes 3932168 | tf_op jit(solution)/shard_map/ppermute | solution.py:385
  382.0 119.0 %reduce-scatter.6.cloned.1.call-start = ((), (), s32[]{:S(2)}) async-start(), calls=%async_computation.12 | async-start | bytes 4718592 | tf_op jit(solution)/shard_map/reduce_scatter | solution.py:922
  452.5 115.6 %all-gather.14.cloned.1.call-start = ((), (), s32[]{:S(2)}) async-start(), calls=%async_computation.13 | async-start | bytes 4718592 | tf_op jit(solution)/shard_map/all_gather | solution.py:943
  509.8 138.3 %reduce-scatter.8.cloned.1.call-start = ((), (), s32[]{:S(2)}) async-start(), calls=%async_computation.14 | async-start | bytes 4718592 | tf_op jit(solution)/shard_map/reduce_scatter | solution.py:953
  594.8 147.4 %reduce-scatter.10.cloned.1.call-start = ((), (), s32[]{:S(2)}) async-start(), calls=%async_computation.15 | async-start | bytes 7208960 | tf_op jit(solution)/shard_map/reduce_scatter | solution.py:962
  650.2 218.6 %reduce-scatter.12.cloned.1.call-start = ((), (), s32[]{:S(2)}) async-start(), calls=%async_computation.16 | async-start | bytes 9830400 | tf_op jit(solution)/shard_map/reduce_scatter | solution.py:962
  651.4 342.7 %reduce-scatter.14.cloned.1.call-start = ((), (), s32[]{:S(2)}) async-start(), calls=%async_computation.17 | async-start | bytes 7208960 | tf_op jit(solution)/shard_map/reduce_scatter | solution.py:962
  659.7 45.9 %collective-permute-start.33 = (bf16[128,2048]{1,0:T(8,128)(2,1)S(1)}, bf16[128,2048]{1,0:T(8,128)(2,1)S(1)}, u32[]{:S(2)}, u32[]{:S(2)}) collective-permute-start(bf16[128,2048]{1,0:T(8,128)(2,1)S(1)} %get-tuple-element.497), channel_id=1, source_target_pairs={{0,8},{8,0},{16,24},{24,16},{1,9},{9,1},{17,25},{25,17},{2,10},{10... | collective-permute-start | bytes 1572872 | tf_op jit(solution)/shard_map/ppermute | solution.py:374
  770.6 47.5 %collective-permute-start.40 = (bf16[33,128,128]{2,1,0:T(8,128)(2,1)}, bf16[33,128,128]{2,1,0:T(8,128)(2,1)S(1)}, u32[]{:S(2)}, u32[]{:S(2)}) collective-permute-start(bf16[33,128,128]{2,1,0:T(8,128)(2,1)} %get-tuple-element.303), channel_id=1, source_target_pairs={{0,6},{1,7},{2,0},{3,1},{4,2},{5,3},{6,4},{7,5},{8,14},{9,15},{10,... | collective-permute-start | bytes 3244040 | tf_op jit(solution)/shard_map/ppermute | solution.py:391
  775.1 70.0 %collective-permute-start.39 = (bf16[33,128,128]{2,1,0:T(8,128)(2,1)}, bf16[33,128,128]{2,1,0:T(8,128)(2,1)S(1)}, u32[]{:S(2)}, u32[]{:S(2)}) collective-permute-start(bf16[33,128,128]{2,1,0:T(8,128)(2,1)} %get-tuple-element.302), channel_id=1, source_target_pairs={{0,4},{1,5},{2,6},{3,7},{4,0},{5,1},{6,2},{7,3},{8,12},{9,13},{10,... | collective-permute-start | bytes 3244040 | tf_op jit(solution)/shard_map/ppermute | solution.py:391
  792.6 75.6 %collective-permute-start.38 = (bf16[33,128,128]{2,1,0:T(8,128)(2,1)S(1)}, bf16[33,128,128]{2,1,0:T(8,128)(2,1)S(1)}, u32[]{:S(2)}, u32[]{:S(2)}) collective-permute-start(bf16[33,128,128]{2,1,0:T(8,128)(2,1)S(1)} %get-tuple-element.301), channel_id=1, source_target_pairs={{0,2},{1,3},{2,4},{3,5},{4,6},{5,7},{6,0},{7,1},{8,10},{9,11},{10,... | collective-permute-start | bytes 3244040 | tf_op jit(solution)/shard_map/ppermute | solution.py:391
  885.0 80.4 %collective-permute-start.46 = (bf16[37,128,128]{2,1,0:T(8,128)(2,1)}, bf16[37,128,128]{2,1,0:T(8,128)(2,1)}, u32[]{:S(2)}, u32[]{:S(2)}) collective-permute-start(bf16[37,128,128]{2,1,0:T(8,128)(2,1)} %get-tuple-element.313), channel_id=1, source_target_pairs={{0,2},{1,3},{2,4},{3,5},{4,6},{5,7},{6,0},{7,1},{8,10},{9,11},{10,... | collective-permute-start | bytes 3637256 | tf_op jit(solution)/shard_map/ppermute | solution.py:391
  887.3 104.2 %collective-permute-start.47 = (bf16[37,128,128]{2,1,0:T(8,128)(2,1)}, bf16[37,128,128]{2,1,0:T(8,128)(2,1)}, u32[]{:S(2)}, u32[]{:S(2)}) collective-permute-start(bf16[37,128,128]{2,1,0:T(8,128)(2,1)} %get-tuple-element.314), channel_id=1, source_target_pairs={{0,4},{1,5},{2,6},{3,7},{4,0},{5,1},{6,2},{7,3},{8,12},{9,13},{10,... | collective-permute-start | bytes 3637256 | tf_op jit(solution)/shard_map/ppermute | solution.py:391
  887.3 106.8 %collective-permute-start.48 = (bf16[37,128,128]{2,1,0:T(8,128)(2,1)}, bf16[37,128,128]{2,1,0:T(8,128)(2,1)}, u32[]{:S(2)}, u32[]{:S(2)}) collective-permute-start(bf16[37,128,128]{2,1,0:T(8,128)(2,1)} %get-tuple-element.315), channel_id=1, source_target_pairs={{0,6},{1,7},{2,0},{3,1},{4,2},{5,3},{6,4},{7,5},{8,14},{9,15},{10,... | collective-permute-start | bytes 3637256 | tf_op jit(solution)/shard_map/ppermute | solution.py:391
  915.7 78.4 %collective-permute-start.60 = (bf16[13,128,128]{2,1,0:T(8,128)(2,1)}, bf16[13,128,128]{2,1,0:T(8,128)(2,1)}, u32[]{:S(2)}, u32[]{:S(2)}) collective-permute-start(bf16[13,128,128]{2,1,0:T(8,128)(2,1)} %get-tuple-element.325), channel_id=1, source_target_pairs={{0,8},{8,0},{16,24},{24,16},{1,9},{9,1},{17,25},{25,17},{2,10},{10... | collective-permute-start | bytes 1277960 | tf_op jit(solution)/shard_map/ppermute | solution.py:374
  920.2 74.4 %collective-permute-start.61 = (bf16[13,128,128]{2,1,0:T(8,128)(2,1)S(1)}, bf16[13,128,128]{2,1,0:T(8,128)(2,1)S(1)}, u32[]{:S(2)}, u32[]{:S(2)}) collective-permute-start(bf16[13,128,128]{2,1,0:T(8,128)(2,1)S(1)} %get-tuple-element.326), channel_id=1, source_target_pairs={{0,16},{8,24},{16,0},{24,8},{1,17},{9,25},{17,1},{25,9},{2,18},{10... | collective-permute-start | bytes 1277960 | tf_op jit(solution)/shard_map/ppermute | solution.py:374
  1005.0 54.8 %collective-permute-start.53 = (bf16[537,128]{1,0:T(8,128)(2,1)}, bf16[537,128]{1,0:T(8,128)(2,1)S(1)}, u32[]{:S(2)}, u32[]{:S(2)}) collective-permute-start(bf16[537,128]{1,0:T(8,128)(2,1)} %add_convert_fusion.3), channel_id=1, source_target_pairs={{0,2},{1,3},{2,4},{3,5},{4,6},{5,7},{6,0},{7,1},{8,10},{9,11},{10,... | collective-permute-start | bytes 412424 | tf_op jit(solution)/shard_map/ppermute | solution.py:391
  1005.0 54.8 %collective-permute-start.54 = (bf16[537,128]{1,0:T(8,128)(2,1)}, bf16[537,128]{1,0:T(8,128)(2,1)S(1)}, u32[]{:S(2)}, u32[]{:S(2)}) collective-permute-start(bf16[537,128]{1,0:T(8,128)(2,1)} %add_convert_fusion.3), channel_id=1, source_target_pairs={{0,4},{1,5},{2,6},{3,7},{4,0},{5,1},{6,2},{7,3},{8,12},{9,13},{10,... | collective-permute-start | bytes 412424 | tf_op jit(solution)/shard_map/ppermute | solution.py:391
  1008.1 51.7 %collective-permute-start.55 = (bf16[537,128]{1,0:T(8,128)(2,1)}, bf16[537,128]{1,0:T(8,128)(2,1)S(1)}, u32[]{:S(2)}, u32[]{:S(2)}) collective-permute-start(bf16[537,128]{1,0:T(8,128)(2,1)} %add_convert_fusion.3), channel_id=1, source_target_pairs={{0,6},{1,7},{2,0},{3,1},{4,2},{5,3},{6,4},{7,5},{8,14},{9,15},{10,... | collective-permute-start | bytes 412424 | tf_op jit(solution)/shard_map/ppermute | solution.py:391
  (243 other events, 4625.9 us)
Sparse Core Ops, SparseCore 0:
  30.2 121.9 all-gather.5
  196.2 66.9 all-gather.7
  265.1 94.3 all-gather.11
  382.1 46.1 all-gather.9
  452.7 48.2 reduce-scatter.5
  509.9 52.9 all-gather.13
  594.9 48.2 reduce-scatter.7
  650.3 88.0 reduce-scatter.9
  741.4 105.6 reduce-scatter.11
  869.7 79.3 reduce-scatter.13

commit v16 on v15

--- a/solution.py
+++ b/solution.py
@@ -365,7 +365,7 @@
             pltpu.VMEM((count, tile, tile), jnp.bfloat16),
             pltpu.SemaphoreType.DMA((count // each,)),
         ],
-        compiler_params=pltpu.CompilerParams(vmem_limit_bytes=4 * VMEM_BYTES),
+        compiler_params=pltpu.CompilerParams(vmem_limit_bytes=(4 if count < 64 else 10) * VMEM_BYTES),
     )(jnp.clip(index, 0, total - 1), *grads, master, first, second, left, right)
 
 

time: 1090 us -> 1080 us (level)
    unnamed x405 -> x399, local copies, waits for them, and re-layouts: 58.7 us -> 49.3 us
where the time goes in v16:
time: 1080 us; the launch traced here: 1070 us
  waiting for transfers between devices  518 us (48%)
  Pallas kernels  147 us (14%)
  local copies, waits for them, and re-layouts  114 us (11%)
  matrix products  98.9 us (9%)
  other arithmetic  84.1 us (8%)
  starting transfers between devices  65.3 us (6%)
  between operations  41.1 us (4%)
    ppermute x21, waiting for transfers between devices, chip_shift(): lax.ppermute(value, 'fsdp', [(i, (i // 2 + offset) % chips * 2 + i % 2) f...  215 us
    ppermute x23, waiting for transfers between devices, seq_swap(): return lax.ppermute(value, 'seq', [(i, i ^ flip) for i in range(size)])  207 us
    pallas_call x10, Pallas kernels, tile_kernel_call(): pl.pallas_call(kernel, grid=(steps,), cost_estimate=pl.CostEstimate(flops...  95.2 us
    unnamed x399, local copies, waits for them, and re-layouts  49.3 us
    pallas_call x2, Pallas kernels, rotate_update(): pl.pallas_call(kernel, grid=(count // each,), out_shape=(shape, shape, sh...  49.2 us
    reduce_scatter x1, waiting for transfers between devices, on_device(): lax.psum_scatter(matmul_flip(hidden_low, w_down).astype(bf16), 'fsdp', sc...  48.4 us
    dot_general x8, matrix products, matmul(): return jnp.dot(left, right, preferred_element_type=jnp.float32)  34.6 us
    dot_general x8, matrix products, matmul_flip(): lax.dot_general(left, right, (((1,), (1,)), ((), ())), preferred_element_...  34.2 us
  transfers between devices with their start and end apart: 77, of which 36 were waited for; matrix products, arithmetic and copies ran while one was open for 18% of the time, Pallas kernels for 11%

profile of v16, /device:TPU:9, one launch (start us, length us, event | category | flops | bytes accessed | tf_op | source)
XLA Modules:
  0.0 1069.9 jit_solution(16998016533126061498)
XLA Ops:
  21.4 7.3 shard_map.257
  73.7 77.5 %collective-permute-done.6.refs_3_ = bf16[40,128,128]{2,1,0:T(8,128)(2,1)} collective-permute-done((bf16[40,128,128]{2,1,0:T(8,128)(2,1)}, bf16[40,128,128]{2,1,0:T(8,128)(2,1)}, u32[]{:S(2)}, u32[]{:S(2)}) %collective-permute-start.6) | collective-permute-done | bytes 1310752 | tf_op jit(solution)/shard_map/ppermute | solution.py:374
  186.9 10.5 shard_map.261
  212.7 14.3 %collective-permute-done.10 = bf16[33,128,128]{2,1,0:T(8,128)(2,1)S(1)} collective-permute-done((bf16[33,128,128]{2,1,0:T(8,128)(2,1)S(1)}, bf16[33,128,128]{2,1,0:T(8,128)(2,1)S(1)}, u32[]{:S(2)}, u32[]{:S(2)}) %collective-permute-start.10) | collective-permute-done | bytes 1081376 | tf_op jit(solution)/shard_map/ppermute | solution.py:391
  227.6 66.6 %collective-permute-done.11 = bf16[33,128,128]{2,1,0:T(8,128)(2,1)S(1)} collective-permute-done((bf16[33,128,128]{2,1,0:T(8,128)(2,1)S(1)}, bf16[33,128,128]{2,1,0:T(8,128)(2,1)S(1)}, u32[]{:S(2)}, u32[]{:S(2)}) %collective-permute-start.11) | collective-permute-done | bytes 1081376 | tf_op jit(solution)/shard_map/ppermute | solution.py:391
  304.9 11.3 %conditional.3 = ((bf16[2048,768]{1,0:T(8,128)(2,1)}, bf16[2048,512]{1,0:T(8,128)(2,1)})) conditional(s32[]{:T(128)} %convert_element_type.372, (s32[]{:T(128)}, s32[4,8,116]{2,1,0:T(8,128)S(1)}, s32[4,8,116]{2,1,0:T(8,128)S(1)}, bf16[116,128,128]{2,1,0:T(8,128)(2,1)}) %tuple.42, (s32[160]{0:T(256)S(1)}, bf16[33,128,128]{2,1,0:T(8,128)(2,1)S(1)}, ...), branch_computations={%region_14.16_spmd, %region_16.17_spmd} | conditional | flops 2379392 | bytes 500902304 | solution.py:848
  304.9 10.9 %branch_1_fun.2 = (bf16[2048,768]{1,0:T(8,128)(2,1)}, bf16[2048,512]{1,0:T(8,128)(2,1)}) custom-call(s32[160]{0:T(256)S(1)} %broadcast_clamp_fusion.1.index_ref, bf16[33,128,128]{2,1,0:T(8,128)(2,1)S(1)} %get-tuple-element.70.refs_0_, bf16[33,128,128]{2,1,0:T(8,128)(2,1)S(1)} %get-tuple-element.71.refs_1_, bf16[33,128,128]{2,1,0:T(8,128)(2,1)} %get-tuple-element.72.refs_2_, ...), custom_call_target="tpu_custom_call" | custom-call | bytes 10485760 | tf_op jit(solution)/shard_map/cond/branch_1_fun/pallas_call | solution.py:152
  325.8 10.3 collective-permute-done.17
  357.6 9.0 collective-permute-done.20
  382.9 14.3 %conditional.4 = ((bf16[2048,2048]{1,0:T(8,128)(2,1)}, bf16[2048,1024]{1,0:T(8,128)(2,1)})) conditional(s32[]{:T(128)} %convert_element_type.372, (s32[]{:T(128)}, s32[4,8,116]{2,1,0:T(8,128)S(1)}, s32[4,8,116]{2,1,0:T(8,128)S(1)}, bf16[116,128,128]{2,1,0:T(8,128)(2,1)}) %tuple.255, (s32[384]{0:T(512)S(1)}, bf16[176,128,128]{2,1,0:T(8,128)(2,1)}, ...), branch_computations={%region_26.28_spmd, %region_28.29_spmd} | conditional | flops 5705344 | bytes 515585056 | solution.py:848
  383.2 14.1 %branch_1_fun.3 = (bf16[2048,2048]{1,0:T(8,128)(2,1)}, bf16[2048,1024]{1,0:T(8,128)(2,1)}) custom-call(s32[384]{0:T(512)S(1)} %broadcast_clamp_fusion.3.index_ref, bf16[176,128,128]{2,1,0:T(8,128)(2,1)} %get-tuple-element.83.refs_0_, bf16[176,128,128]{2,1,0:T(8,128)(2,1)} %get-tuple-element.84.refs_1_, bf16[240,128,128]{2,1,0:T(8,128)(2,1)} %get-tuple-element.85.refs_2_), custom_call_target="tpu_custom_call" | custom-call | bytes 25165824 | tf_op jit(solution)/shard_map/cond/branch_1_fun/pallas_call | solution.py:152
  397.3 31.9 %all-gather.10.cloned.1.call-done = bf16[1024,2048]{1,0:T(8,128)(2,1)} async-done(((bf16[128,2048]{1,0:T(8,128)(2,1)}), bf16[1024,2048]{1,0:T(8,128)(2,1)}) %all-gather.10.cloned.1.call-update) | async-done | bytes 4194320 | tf_op jit(solution)/shard_map/all_gather | solution.py:913
  429.2 12.5 %fusion.271 = f32[1024,2048]{1,0:T(8,128)S(1)} fusion(bf16[1024,2048]{1,0:T(8,128)(2,1)} %all-gather.10.cloned.1.call-done, bf16[2048,2048]{1,0:T(8,128)(2,1)} %get-tuple-element.286), kind=kOutput, calls=%fused_computation.753 | convolution fusion | flops 8589934592 | bytes 20971520 | tf_op jit(solution)/shard_map/dot_general | solution.py:62
  453.4 48.4 %reduce-scatter.6.cloned.1.call-done = bf16[128,2048]{1,0:T(8,128)(2,1)} async-done(((bf16[1024,2048]{1,0:T(8,128)(2,1)}), bf16[128,2048]{1,0:T(8,128)(2,1)}) %reduce-scatter.6.cloned.1.call-update) | async-done | bytes 524304 | tf_op jit(solution)/shard_map/reduce_scatter | solution.py:922
  569.1 12.1 %fusion.13 = (bf16[1024,1024]{1,0:T(8,128)(2,1)S(1)}, bf16[1024,1024]{1,0:T(8,128)(2,1)S(1)}) fusion(f32[1024,2048]{1,0:T(8,128)} %copy-done.53, bf16[1024,2048]{1,0:T(8,128)(2,1)} %all-gather.14.cloned.1.call-done, bf16[2048,1024]{1,0:T(8,128)(2,1)} %get-tuple-element.287), kind=kOutput, calls=%fused_computation.53 | convolution fusion | flops 4320133120 | bytes 20971520 | tf_op jit(solution)/shard_map/dot_general | solution.py:62
  583.1 12.6 %convolution_convert_fusion.1 = bf16[1024,2048]{1,0:T(8,128)(2,1)} fusion(bf16[2048,2048]{1,0:T(8,128)(2,1)} %get-tuple-element.286, bf16[1024,1024]{1,0:T(8,128)(2,1)S(1)} %get-tuple-element.466, bf16[1024,1024]{1,0:T(8,128)(2,1)S(1)} %get-tuple-element.465), kind=kOutput, calls=%fused_computation.61 | convolution fusion | flops 8600420352 | bytes 16777216 | tf_op jit(solution)/shard_map/dot_general | solution.py:66
  605.8 9.4 convolution_convert_fusion.refs_0_
  618.4 22.4 %shard_map.263 = (bf16[176,128,128]{2,1,0:T(8,128)(2,1)S(1)}, bf16[240,128,128]{2,1,0:T(8,128)(2,1)S(1)}, bf16[176,128,128]{2,1,0:T(8,128)(2,1)S(1)}) custom-call(s32[592]{0:T(1024)S(1)} %add_clamp_fusion.index_ref, bf16[2048,2048]{1,0:T(8,128)(2,1)S(1)} %convolution_convert_fusion.refs_0_, bf16[2048,1024]{1,0:T(8,128)(2,1)S(1)} %convolution_convert_fusion.2.refs_1_), custom_call_target="tpu_custom_call" | custom-call | bytes 38797312 | tf_op jit(solution)/shard_map/pallas_call | solution.py:152
  662.7 21.0 %collective-permute-done.35 = bf16[128,2048]{1,0:T(8,128)(2,1)S(1)} collective-permute-done((bf16[128,2048]{1,0:T(8,128)(2,1)S(1)}, bf16[128,2048]{1,0:T(8,128)(2,1)S(1)}, u32[]{:S(2)}, u32[]{:S(2)}) %collective-permute-start.35) | collective-permute-done | bytes 524320 | tf_op jit(solution)/shard_map/ppermute | solution.py:374
  683.8 12.0 %collective-permute-done.34 = bf16[128,2048]{1,0:T(8,128)(2,1)S(1)} collective-permute-done((bf16[128,2048]{1,0:T(8,128)(2,1)S(1)}, bf16[128,2048]{1,0:T(8,128)(2,1)S(1)}, u32[]{:S(2)}, u32[]{:S(2)}) %collective-permute-start.34) | collective-permute-done | bytes 524320 | tf_op jit(solution)/shard_map/ppermute | solution.py:374
  695.7 10.7 %collective-permute-done.33 = bf16[128,2048]{1,0:T(8,128)(2,1)S(1)} collective-permute-done((bf16[128,2048]{1,0:T(8,128)(2,1)S(1)}, bf16[128,2048]{1,0:T(8,128)(2,1)S(1)}, u32[]{:S(2)}, u32[]{:S(2)}) %collective-permute-start.33) | collective-permute-done | bytes 524320 | tf_op jit(solution)/shard_map/ppermute | solution.py:374
  728.9 10.2 shard_map.264
  752.3 7.3 fusion.248
  775.6 17.8 %collective-permute-done.43 = bf16[128,2048]{1,0:T(8,128)(2,1)} collective-permute-done((bf16[128,2048]{1,0:T(8,128)(2,1)}, bf16[128,2048]{1,0:T(8,128)(2,1)}, u32[]{:S(2)}, u32[]{:S(2)}) %collective-permute-start.43) | collective-permute-done | bytes 524320 | tf_op jit(solution)/shard_map/ppermute | solution.py:374
  794.1 10.9 %collective-permute-done.42 = bf16[128,2048]{1,0:T(8,128)(2,1)} collective-permute-done((bf16[128,2048]{1,0:T(8,128)(2,1)}, bf16[128,2048]{1,0:T(8,128)(2,1)}, u32[]{:S(2)}, u32[]{:S(2)}) %collective-permute-start.42) | collective-permute-done | bytes 524320 | tf_op jit(solution)/shard_map/ppermute | solution.py:374
  805.1 10.0 collective-permute-done.41
  819.1 26.5 %collective-permute-done.39 = bf16[33,128,128]{2,1,0:T(8,128)(2,1)S(1)} collective-permute-done((bf16[33,128,128]{2,1,0:T(8,128)(2,1)}, bf16[33,128,128]{2,1,0:T(8,128)(2,1)S(1)}, u32[]{:S(2)}, u32[]{:S(2)}) %collective-permute-start.39) | collective-permute-done | bytes 1081376 | tf_op jit(solution)/shard_map/ppermute | solution.py:391
  845.6 23.1 %collective-permute-done.38 = bf16[33,128,128]{2,1,0:T(8,128)(2,1)S(1)} collective-permute-done((bf16[33,128,128]{2,1,0:T(8,128)(2,1)S(1)}, bf16[33,128,128]{2,1,0:T(8,128)(2,1)S(1)}, u32[]{:S(2)}, u32[]{:S(2)}) %collective-permute-start.38) | collective-permute-done | bytes 1081376 | tf_op jit(solution)/shard_map/ppermute | solution.py:391
  878.9 9.7 shard_map.265
  921.2 47.9 %collective-permute-done.46.refs_0_ = bf16[37,128,128]{2,1,0:T(8,128)(2,1)} collective-permute-done((bf16[37,128,128]{2,1,0:T(8,128)(2,1)}, bf16[37,128,128]{2,1,0:T(8,128)(2,1)}, u32[]{:S(2)}, u32[]{:S(2)}) %collective-permute-start.46) | collective-permute-done | bytes 1212448 | tf_op jit(solution)/shard_map/ppermute | solution.py:391
  971.0 21.6 %collective-permute-done.47.refs_1_ = bf16[37,128,128]{2,1,0:T(8,128)(2,1)} collective-permute-done((bf16[37,128,128]{2,1,0:T(8,128)(2,1)}, bf16[37,128,128]{2,1,0:T(8,128)(2,1)}, u32[]{:S(2)}, u32[]{:S(2)}) %collective-permute-start.47) | collective-permute-done | bytes 1212448 | tf_op jit(solution)/shard_map/ppermute | solution.py:391
  1012.3 42.2 %shard_map.267 = (f32[116,128,128]{2,1,0:T(8,128)}, f32[116,128,128]{2,1,0:T(8,128)}, f32[116,128,128]{2,1,0:T(8,128)}) custom-call(s32[116]{0:T(128)S(1)} %fusion.212.index_ref, bf16[37,128,128]{2,1,0:T(8,128)(2,1)} %collective-permute-done.46.refs_0_, bf16[37,128,128]{2,1,0:T(8,128)(2,1)} %collective-permute-done.47.refs_1_, ...), custom_call_target="tpu_custom_call" | custom-call | flops 5351931904 | bytes 64618496 | tf_op jit(solution)/shard_map/pallas_call | solution.py:353
  (880 shorter events, 390.4 us)
Async XLA Ops:
  7.2 173.0 %all-gather.6.cloned.1.call-start = ((), (), s32[]{:S(2)}) async-start(), calls=%async_computation.8 | async-start | bytes 7208960 | tf_op jit(solution)/shard_map/all_gather | solution.py:626
  29.8 275.1 %all-gather.8.cloned.1.call-start = ((), (), s32[]{:S(2)}) async-start(), calls=%async_computation.9 | async-start | bytes 7208960 | tf_op jit(solution)/shard_map/all_gather | solution.py:823
  47.0 131.6 %collective-permute-start.1 = (bf16[37,128,128]{2,1,0:T(8,128)(2,1)}, bf16[37,128,128]{2,1,0:T(8,128)(2,1)}, u32[]{:S(2)}, u32[]{:S(2)}) collective-permute-start(bf16[37,128,128]{2,1,0:T(8,128)(2,1)} %get-tuple-element.230), channel_id=1, source_target_pairs={{0,2},{1,3},{2,4},{3,5},{4,6},{5,7},{6,0},{7,1},{8,10},{9,11},{10,... | collective-permute-start | bytes 3637256 | tf_op jit(solution)/shard_map/ppermute | solution.py:391
  48.6 129.9 %collective-permute-start.2 = (bf16[37,128,128]{2,1,0:T(8,128)(2,1)}, bf16[37,128,128]{2,1,0:T(8,128)(2,1)}, u32[]{:S(2)}, u32[]{:S(2)}) collective-permute-start(bf16[37,128,128]{2,1,0:T(8,128)(2,1)} %get-tuple-element.231), channel_id=1, source_target_pairs={{0,4},{1,5},{2,6},{3,7},{4,0},{5,1},{6,2},{7,3},{8,12},{9,13},{10,... | collective-permute-start | bytes 3637256 | tf_op jit(solution)/shard_map/ppermute | solution.py:391
  61.5 93.1 %collective-permute-start.4 = (bf16[40,128,128]{2,1,0:T(8,128)(2,1)}, bf16[40,128,128]{2,1,0:T(8,128)(2,1)S(1)}, u32[]{:S(2)}, u32[]{:S(2)}) collective-permute-start(bf16[40,128,128]{2,1,0:T(8,128)(2,1)} %get-tuple-element.504), channel_id=1, source_target_pairs={{0,8},{8,0},{16,24},{24,16},{1,9},{9,1},{17,25},{25,17},{2,10},{10... | collective-permute-start | bytes 3932168 | tf_op jit(solution)/shard_map/ppermute | solution.py:374
  62.9 91.0 %collective-permute-start.5 = (bf16[40,128,128]{2,1,0:T(8,128)(2,1)}, bf16[40,128,128]{2,1,0:T(8,128)(2,1)}, u32[]{:S(2)}, u32[]{:S(2)}) collective-permute-start(bf16[40,128,128]{2,1,0:T(8,128)(2,1)} %get-tuple-element.503), channel_id=1, source_target_pairs={{0,16},{8,24},{16,0},{24,8},{1,17},{9,25},{17,1},{25,9},{2,18},{10... | collective-permute-start | bytes 3932168 | tf_op jit(solution)/shard_map/ppermute | solution.py:374
  64.0 87.2 %collective-permute-start.6 = (bf16[40,128,128]{2,1,0:T(8,128)(2,1)}, bf16[40,128,128]{2,1,0:T(8,128)(2,1)}, u32[]{:S(2)}, u32[]{:S(2)}) collective-permute-start(bf16[40,128,128]{2,1,0:T(8,128)(2,1)} %get-tuple-element.502), channel_id=1, source_target_pairs={{0,24},{8,16},{16,8},{24,0},{1,25},{9,17},{17,9},{25,1},{2,26},{10... | collective-permute-start | bytes 3932168 | tf_op jit(solution)/shard_map/ppermute | solution.py:374
  197.4 185.5 %all-gather.12.cloned.1.call-start = ((), (), s32[]{:S(2)}) async-start(), calls=%async_computation.11 | async-start | bytes 9830400 | tf_op jit(solution)/shard_map/all_gather | solution.py:823
  198.2 231.0 %all-gather.10.cloned.1.call-start = ((), (), s32[]{:S(2)}) async-start(), calls=%async_computation.10 | async-start | bytes 4718592 | tf_op jit(solution)/shard_map/all_gather | solution.py:913
  201.2 93.0 %collective-permute-start.11 = (bf16[33,128,128]{2,1,0:T(8,128)(2,1)S(1)}, bf16[33,128,128]{2,1,0:T(8,128)(2,1)S(1)}, u32[]{:S(2)}, u32[]{:S(2)}) collective-permute-start(bf16[33,128,128]{2,1,0:T(8,128)(2,1)S(1)} %copy-done.72), channel_id=1, source_target_pairs={{0,4},{1,5},{2,6},{3,7},{4,0},{5,1},{6,2},{7,3},{8,12},{9,13},{10,... | collective-permute-start | bytes 3244040 | tf_op jit(solution)/shard_map/ppermute | solution.py:391
  205.0 93.7 %collective-permute-start.12 = (bf16[33,128,128]{2,1,0:T(8,128)(2,1)S(1)}, bf16[33,128,128]{2,1,0:T(8,128)(2,1)S(1)}, u32[]{:S(2)}, u32[]{:S(2)}) collective-permute-start(bf16[33,128,128]{2,1,0:T(8,128)(2,1)S(1)} %copy-done.72), channel_id=1, source_target_pairs={{0,6},{1,7},{2,0},{3,1},{4,2},{5,3},{6,4},{7,5},{8,14},{9,15},{10,... | collective-permute-start | bytes 3244040 | tf_op jit(solution)/shard_map/ppermute | solution.py:391
  212.3 90.3 %collective-permute-start.13 = (bf16[33,128,128]{2,1,0:T(8,128)(2,1)S(1)}, bf16[33,128,128]{2,1,0:T(8,128)(2,1)S(1)}, u32[]{:S(2)}, u32[]{:S(2)}) collective-permute-start(bf16[33,128,128]{2,1,0:T(8,128)(2,1)S(1)} %copy-done.72), channel_id=1, source_target_pairs={{0,1},{1,0},{2,3},{3,2},{4,5},{5,4},{6,7},{7,6},{8,9},{9,8},{10,11... | collective-permute-start | bytes 3244040 | tf_op jit(solution)/shard_map/ppermute | solution.py:385
  227.0 75.6 %collective-permute-start.14 = (bf16[33,128,128]{2,1,0:T(8,128)(2,1)S(1)}, bf16[33,128,128]{2,1,0:T(8,128)(2,1)S(1)}, u32[]{:S(2)}, u32[]{:S(2)}) collective-permute-start(bf16[33,128,128]{2,1,0:T(8,128)(2,1)S(1)} %collective-permute-done.10), channel_id=1, source_target_pairs={{0,1},{1,0},{2,3},{3,2},{4,5},{5,4},{6,7},{7,6},{8,9},{9,8},{10,11... | collective-permute-start | bytes 3244040 | tf_op jit(solution)/shard_map/ppermute | solution.py:385
  302.2 47.1 %collective-permute-start.21 = (bf16[4,10,128,128]{3,2,1,0:T(8,128)(2,1)}, bf16[4,10,128,128]{3,2,1,0:T(8,128)(2,1)}, u32[]{:S(2)}, u32[]{:S(2)}) collective-permute-start(bf16[4,10,128,128]{3,2,1,0:T(8,128)(2,1)} %get-tuple-element.486), channel_id=1, source_target_pairs={{0,1},{1,0},{2,3},{3,2},{4,5},{5,4},{6,7},{7,6},{8,9},{9,8},{10,11... | collective-permute-start | bytes 3932168 | tf_op jit(solution)/shard_map/ppermute | solution.py:385
  382.8 119.0 %reduce-scatter.6.cloned.1.call-start = ((), (), s32[]{:S(2)}) async-start(), calls=%async_computation.12 | async-start | bytes 4718592 | tf_op jit(solution)/shard_map/reduce_scatter | solution.py:922
  453.4 115.7 %all-gather.14.cloned.1.call-start = ((), (), s32[]{:S(2)}) async-start(), calls=%async_computation.13 | async-start | bytes 4718592 | tf_op jit(solution)/shard_map/all_gather | solution.py:943
  510.7 138.4 %reduce-scatter.8.cloned.1.call-start = ((), (), s32[]{:S(2)}) async-start(), calls=%async_computation.14 | async-start | bytes 4718592 | tf_op jit(solution)/shard_map/reduce_scatter | solution.py:953
  595.8 147.4 %reduce-scatter.10.cloned.1.call-start = ((), (), s32[]{:S(2)}) async-start(), calls=%async_computation.15 | async-start | bytes 7208960 | tf_op jit(solution)/shard_map/reduce_scatter | solution.py:962
  651.2 218.2 %reduce-scatter.12.cloned.1.call-start = ((), (), s32[]{:S(2)}) async-start(), calls=%async_computation.16 | async-start | bytes 9830400 | tf_op jit(solution)/shard_map/reduce_scatter | solution.py:962
  652.3 342.0 %reduce-scatter.14.cloned.1.call-start = ((), (), s32[]{:S(2)}) async-start(), calls=%async_computation.17 | async-start | bytes 7208960 | tf_op jit(solution)/shard_map/reduce_scatter | solution.py:962
  660.6 45.8 %collective-permute-start.33 = (bf16[128,2048]{1,0:T(8,128)(2,1)S(1)}, bf16[128,2048]{1,0:T(8,128)(2,1)S(1)}, u32[]{:S(2)}, u32[]{:S(2)}) collective-permute-start(bf16[128,2048]{1,0:T(8,128)(2,1)S(1)} %get-tuple-element.497), channel_id=1, source_target_pairs={{0,8},{8,0},{16,24},{24,16},{1,9},{9,1},{17,25},{25,17},{2,10},{10... | collective-permute-start | bytes 1572872 | tf_op jit(solution)/shard_map/ppermute | solution.py:374
  771.5 47.6 %collective-permute-start.40 = (bf16[33,128,128]{2,1,0:T(8,128)(2,1)}, bf16[33,128,128]{2,1,0:T(8,128)(2,1)S(1)}, u32[]{:S(2)}, u32[]{:S(2)}) collective-permute-start(bf16[33,128,128]{2,1,0:T(8,128)(2,1)} %get-tuple-element.303), channel_id=1, source_target_pairs={{0,6},{1,7},{2,0},{3,1},{4,2},{5,3},{6,4},{7,5},{8,14},{9,15},{10,... | collective-permute-start | bytes 3244040 | tf_op jit(solution)/shard_map/ppermute | solution.py:391
  775.6 70.0 %collective-permute-start.39 = (bf16[33,128,128]{2,1,0:T(8,128)(2,1)}, bf16[33,128,128]{2,1,0:T(8,128)(2,1)S(1)}, u32[]{:S(2)}, u32[]{:S(2)}) collective-permute-start(bf16[33,128,128]{2,1,0:T(8,128)(2,1)} %get-tuple-element.302), channel_id=1, source_target_pairs={{0,4},{1,5},{2,6},{3,7},{4,0},{5,1},{6,2},{7,3},{8,12},{9,13},{10,... | collective-permute-start | bytes 3244040 | tf_op jit(solution)/shard_map/ppermute | solution.py:391
  793.4 75.3 %collective-permute-start.38 = (bf16[33,128,128]{2,1,0:T(8,128)(2,1)S(1)}, bf16[33,128,128]{2,1,0:T(8,128)(2,1)S(1)}, u32[]{:S(2)}, u32[]{:S(2)}) collective-permute-start(bf16[33,128,128]{2,1,0:T(8,128)(2,1)S(1)} %get-tuple-element.301), channel_id=1, source_target_pairs={{0,2},{1,3},{2,4},{3,5},{4,6},{5,7},{6,0},{7,1},{8,10},{9,11},{10,... | collective-permute-start | bytes 3244040 | tf_op jit(solution)/shard_map/ppermute | solution.py:391
  888.6 80.5 %collective-permute-start.46 = (bf16[37,128,128]{2,1,0:T(8,128)(2,1)}, bf16[37,128,128]{2,1,0:T(8,128)(2,1)}, u32[]{:S(2)}, u32[]{:S(2)}) collective-permute-start(bf16[37,128,128]{2,1,0:T(8,128)(2,1)} %get-tuple-element.313), channel_id=1, source_target_pairs={{0,2},{1,3},{2,4},{3,5},{4,6},{5,7},{6,0},{7,1},{8,10},{9,11},{10,... | collective-permute-start | bytes 3637256 | tf_op jit(solution)/shard_map/ppermute | solution.py:391
  890.3 102.4 %collective-permute-start.47 = (bf16[37,128,128]{2,1,0:T(8,128)(2,1)}, bf16[37,128,128]{2,1,0:T(8,128)(2,1)}, u32[]{:S(2)}, u32[]{:S(2)}) collective-permute-start(bf16[37,128,128]{2,1,0:T(8,128)(2,1)} %get-tuple-element.314), channel_id=1, source_target_pairs={{0,4},{1,5},{2,6},{3,7},{4,0},{5,1},{6,2},{7,3},{8,12},{9,13},{10,... | collective-permute-start | bytes 3637256 | tf_op jit(solution)/shard_map/ppermute | solution.py:391
  890.3 104.0 %collective-permute-start.48 = (bf16[37,128,128]{2,1,0:T(8,128)(2,1)}, bf16[37,128,128]{2,1,0:T(8,128)(2,1)}, u32[]{:S(2)}, u32[]{:S(2)}) collective-permute-start(bf16[37,128,128]{2,1,0:T(8,128)(2,1)} %get-tuple-element.315), channel_id=1, source_target_pairs={{0,6},{1,7},{2,0},{3,1},{4,2},{5,3},{6,4},{7,5},{8,14},{9,15},{10,... | collective-permute-start | bytes 3637256 | tf_op jit(solution)/shard_map/ppermute | solution.py:391
  916.6 78.3 %collective-permute-start.60 = (bf16[13,128,128]{2,1,0:T(8,128)(2,1)}, bf16[13,128,128]{2,1,0:T(8,128)(2,1)}, u32[]{:S(2)}, u32[]{:S(2)}) collective-permute-start(bf16[13,128,128]{2,1,0:T(8,128)(2,1)} %get-tuple-element.325), channel_id=1, source_target_pairs={{0,8},{8,0},{16,24},{24,16},{1,9},{9,1},{17,25},{25,17},{2,10},{10... | collective-permute-start | bytes 1277960 | tf_op jit(solution)/shard_map/ppermute | solution.py:374
  921.2 73.7 %collective-permute-start.61 = (bf16[13,128,128]{2,1,0:T(8,128)(2,1)S(1)}, bf16[13,128,128]{2,1,0:T(8,128)(2,1)S(1)}, u32[]{:S(2)}, u32[]{:S(2)}) collective-permute-start(bf16[13,128,128]{2,1,0:T(8,128)(2,1)S(1)} %get-tuple-element.326), channel_id=1, source_target_pairs={{0,16},{8,24},{16,0},{24,8},{1,17},{9,25},{17,1},{25,9},{2,18},{10... | collective-permute-start | bytes 1277960 | tf_op jit(solution)/shard_map/ppermute | solution.py:374
  1005.6 49.0 %collective-permute-start.53 = (bf16[537,128]{1,0:T(8,128)(2,1)}, bf16[537,128]{1,0:T(8,128)(2,1)S(1)}, u32[]{:S(2)}, u32[]{:S(2)}) collective-permute-start(bf16[537,128]{1,0:T(8,128)(2,1)} %add_convert_fusion.3), channel_id=1, source_target_pairs={{0,2},{1,3},{2,4},{3,5},{4,6},{5,7},{6,0},{7,1},{8,10},{9,11},{10,... | collective-permute-start | bytes 412424 | tf_op jit(solution)/shard_map/ppermute | solution.py:391
  1005.6 49.0 %collective-permute-start.54 = (bf16[537,128]{1,0:T(8,128)(2,1)}, bf16[537,128]{1,0:T(8,128)(2,1)S(1)}, u32[]{:S(2)}, u32[]{:S(2)}) collective-permute-start(bf16[537,128]{1,0:T(8,128)(2,1)} %add_convert_fusion.3), channel_id=1, source_target_pairs={{0,4},{1,5},{2,6},{3,7},{4,0},{5,1},{6,2},{7,3},{8,12},{9,13},{10,... | collective-permute-start | bytes 412424 | tf_op jit(solution)/shard_map/ppermute | solution.py:391
  1008.4 46.2 %collective-permute-start.55 = (bf16[537,128]{1,0:T(8,128)(2,1)}, bf16[537,128]{1,0:T(8,128)(2,1)S(1)}, u32[]{:S(2)}, u32[]{:S(2)}) collective-permute-start(bf16[537,128]{1,0:T(8,128)(2,1)} %add_convert_fusion.3), channel_id=1, source_target_pairs={{0,6},{1,7},{2,0},{3,1},{4,2},{5,3},{6,4},{7,5},{8,14},{9,15},{10,... | collective-permute-start | bytes 412424 | tf_op jit(solution)/shard_map/ppermute | solution.py:391
  (240 other events, 4620.0 us)
Sparse Core Ops, SparseCore 0:
  29.9 122.2 all-gather.5
  197.6 66.5 all-gather.7
  266.0 94.6 all-gather.11
  382.9 46.2 all-gather.9
  453.5 48.3 reduce-scatter.5
  510.8 52.9 all-gather.13
  595.9 48.3 reduce-scatter.7
  651.3 88.1 reduce-scatter.9
  742.5 105.7 reduce-scatter.11
  870.2 84.4 reduce-scatter.13
